TPU v7x, 32 devices: a whole 2x2x4 slice. The times are simulated.
32 devices in a mesh: load: 2 (over core), sy: 4 (over y, x), sz: 4 (over z).
Axes of the slice: x: 2, y: 2, z: 4, core: 2. Of those that a mesh axis runs over, the one named last changes fastest.
Arguments:
- displacements: float32 [4, 3, 16, 64, 512], P('load', None, 'sz', 'sy'), may hold values from -2.4 to 2.4
- density: float32 [16, 64, 512], P('sz', 'sy'), may hold values from 0.05 to 1
- solid: int32 [16, 64, 512], P('sz', 'sy'), may hold values 0 or 1
- fixed: int32 [16, 64, 512], P('sz', 'sy'), may hold values 0 or 1
Outputs:
- sensitivity: float32 [16, 64, 512], P('sz', 'sy')
All inputs are finite; a program needn't handle non-finite values. No bound on the sum of `solid` or of `fixed` on one device may be relied on, other than what follows from the above.
Results may differ from a plain program's by a relative error of at most 0.0001.
Values sent between devices are 32-bit elements; how exact they have to be, the bound alone decides.
No kernel may reach another device: no remote copies, remote signals or barrier semaphores. Data moves between devices by JAX's collectives and lax.ppermute only.
A program may use at most 64 MiB of HBM per device.

v0:
```python
import jax
import jax.numpy as jnp
import numpy as np
from jax import lax
from jax.sharding import PartitionSpec as P

OFFSETS = [(0, 0, 0), (1, 0, 0), (1, 1, 0), (0, 1, 0), (0, 0, 1), (1, 0, 1), (1, 1, 1), (0, 1, 1)]


def shifted(value, axis, by):
    size = lax.axis_size(axis)
    pairs = [(i, i + by) for i in range(size) if 0 <= i + by < size]
    return lax.ppermute(value, axis, pairs)


def extended_2(cells, sides, width):
    for axis, dim in sides:
        count = lax.axis_size(axis)
        ends = count - 1
        head = lax.slice_in_dim(cells, 0, width, axis=dim)
        tail = lax.slice_in_dim(cells, cells.shape[dim] - width, cells.shape[dim], axis=dim)
        cells = jnp.concatenate(
            [
                lax.ppermute(tail, axis, [(i, (i + 1) % count) for i in range(ends)]),
                cells,
                lax.ppermute(head, axis, [((i + 1) % count, i) for i in range(ends)]),
            ],
            axis=dim,
        )
    return cells


def element_matrix():
    corners = np.array(
        [
            [-1.0, -1.0, -1.0],
            [1.0, -1.0, -1.0],
            [1.0, 1.0, -1.0],
            [-1.0, 1.0, -1.0],
            [-1.0, -1.0, 1.0],
            [1.0, -1.0, 1.0],
            [1.0, 1.0, 1.0],
            [-1.0, 1.0, 1.0],
        ]
    )
    poisson = 0.3
    lame = poisson / ((1.0 + poisson) * (1.0 - 2.0 * poisson))
    shear = 1.0 / (2.0 * (1.0 + poisson))
    elastic = np.zeros((6, 6))
    elastic[:3, :3] = lame
    for k in range(3):
        elastic[k, k] += 2.0 * shear
        elastic[3 + k, 3 + k] = shear
    gauss = 1.0 / np.sqrt(3.0)
    stiffness = np.zeros((24, 24))
    for gi in range(2):
        for gj in range(2):
            for gk in range(2):
                point = np.array([(2 * gi - 1) * gauss, (2 * gj - 1) * gauss, (2 * gk - 1) * gauss])
                strain = np.zeros((6, 24))
                for node in range(8):
                    grads = np.zeros(3)
                    for k in range(3):
                        value = corners[node, k] / 8.0
                        for m in range(3):
                            if m != k:
                                value = value * (1.0 + point[m] * corners[node, m])
                        grads[k] = 2.0 * value
                    col = 3 * node
                    strain[0, col] = grads[0]
                    strain[1, col + 1] = grads[1]
                    strain[2, col + 2] = grads[2]
                    strain[3, col] = grads[1]
                    strain[3, col + 1] = grads[0]
                    strain[4, col + 1] = grads[2]
                    strain[4, col + 2] = grads[1]
                    strain[5, col] = grads[2]
                    strain[5, col + 2] = grads[0]
                stiffness += strain.T @ elastic @ strain / 8.0
    return stiffness


def weight_line(coord, count):
    total = jnp.zeros(coord.shape, jnp.float32)
    for step in range(-3, 4):
        inside = (coord + step >= 0) & (coord + step < count)
        total = total + jnp.where(inside, 4.0 - abs(step), 0.0).astype(jnp.float32)
    return total


def spread_axis(padded, axis, length):
    total = None
    for k in range(7):
        piece = (4.0 - abs(k - 3)) * lax.slice_in_dim(padded, k, k + length, axis=axis)
        total = piece if total is None else total + piece
    return total


def body(displacements, density, solid, fixed):
    stiffness = jnp.asarray(element_matrix(), jnp.float32)
    load_dev, _, zlen, ylen, xlen = displacements.shape
    held = displacements * (1 - fixed).astype(jnp.float32)[None, None]
    upper_z = shifted(held[:, :, :1], "sz", -1)
    extended = jnp.concatenate([held, upper_z], axis=2)
    upper_y = shifted(extended[:, :, :, :1], "sy", -1)
    extended = jnp.concatenate([extended, upper_y], axis=3)
    extended = jnp.pad(extended, ((0, 0), (0, 0), (0, 0), (0, 0), (0, 1)))
    partial_energy = jnp.zeros((zlen, ylen, xlen), jnp.float32)
    for case in range(load_dev):
        nodes = [extended[case, :, c : c + zlen, b : b + ylen, a : a + xlen] for a, b, c in OFFSETS]
        local = jnp.stack(nodes, axis=0).reshape(24, zlen * ylen * xlen)
        image = jnp.dot(
            stiffness, local, precision=lax.Precision.HIGHEST, preferred_element_type=jnp.float32
        )
        partial_energy = partial_energy + jnp.sum(local * image, axis=0).reshape(zlen, ylen, xlen)
    total_z = zlen * lax.axis_size("sz")
    total_y = ylen * lax.axis_size("sy")
    hz = weight_line(lax.axis_index("sz") * zlen + jnp.arange(zlen, dtype=jnp.int32), total_z)
    hy = weight_line(lax.axis_index("sy") * ylen + jnp.arange(ylen, dtype=jnp.int32), total_y)
    width = xlen // lax.axis_size("load")
    start = lax.axis_index("load") * width
    energy = lax.psum_scatter(partial_energy, "load", scatter_dimension=2, tiled=True)
    own_density = lax.dynamic_slice_in_dim(density, start, width, 2)
    own_solid = lax.dynamic_slice_in_dim(solid, start, width, 2)
    hx = weight_line(start + jnp.arange(width, dtype=jnp.int32), xlen)
    term = own_solid.astype(jnp.float32) * (-3.0 * own_density * own_density) * energy
    quotient = term / (hz[:, None, None] * hy[None, :, None] * hx[None, None, :])
    padded_x = extended_2(quotient, (("load", 2),), 3)
    filtered = spread_axis(padded_x, 2, width)
    padded = extended_2(filtered, (("sy", 1), ("sz", 0)), 3)
    filtered = spread_axis(padded, 1, ylen)
    filtered = spread_axis(filtered, 0, zlen)
    filtered = lax.all_gather(filtered, "load", axis=2, tiled=True)
    return filtered


def solution(mesh):
    return jax.shard_map(
        body,
        mesh=mesh,
        in_specs=(
            P("load", None, "sz", "sy", None),
            P("sz", "sy", None),
            P("sz", "sy", None),
            P("sz", "sy", None),
        ),
        out_specs=P("sz", "sy", None),
        check_vma=False,
    )
```

profile of v0, /device:TPU:0, one launch (start us, length us, event | category | flops | bytes accessed | tf_op | source)
XLA Modules:
  0.0 90.3 jit_solution(300191165203236750)
XLA Ops:
  6.5 0.9 %subtract_convert_fusion = f32[4,16,512]{2,1,0:T(8,128)S(1)} fusion(s32[4,16,512]{2,1,0:T(8,128)} %param.8), kind=kLoop, calls=%fused_computation.43 | loop fusion | flops 65536 | bytes 262144 | tf_op jit(solution)/shard_map/convert_element_type | solution.py:102
  7.5 1.2 %broadcast_multiply_fusion = f32[2,3,4,16,512]{4,3,2,1,0:T(8,128)S(1)} fusion(f32[2,3,4,16,512]{4,3,2,1,0:T(8,128)} %param.5, f32[4,16,512]{2,1,0:T(8,128)S(1)} %subtract_convert_fusion), kind=kLoop, calls=%fused_computation.30 | loop fusion | flops 196608 | bytes 1703936 | tf_op jit(solution)/shard_map/mul | solution.py:102
  8.7 1.3 %collective-permute-start = (f32[2,3,1,16,512]{4,3,2,1,0:T(8,128)S(1)}, f32[2,3,1,16,512]{4,3,2,1,0:T(8,128)S(1)}, u32[]{:S(2)}, u32[]{:S(2)}) collective-permute-start(f32[2,3,1,16,512]{4,3,2,1,0:T(8,128)S(1)} %slice.197), channel_id=1, source_target_pairs={{1,0},{2,1},{3,2},{5,4},{6,5},{7,6},{9,8},{10,9},{11,10},{13,12},{... | collective-permute-start | bytes 589832 | tf_op jit(solution)/shard_map/ppermute | solution.py:13
  10.1 8.5 %collective-permute-done = f32[2,3,1,16,512]{4,3,2,1,0:T(8,128)S(1)} collective-permute-done((f32[2,3,1,16,512]{4,3,2,1,0:T(8,128)S(1)}, f32[2,3,1,16,512]{4,3,2,1,0:T(8,128)S(1)}, u32[]{:S(2)}, u32[]{:S(2)}) %collective-permute-start) | collective-permute-done | bytes 196640 | tf_op jit(solution)/shard_map/ppermute | solution.py:13
  18.6 1.3 %collective-permute-start.1 = (f32[2,3,5,1,512]{4,3,2,1,0:T(1,128)S(1)}, f32[2,3,5,1,512]{4,3,2,1,0:T(1,128)S(1)}, u32[]{:S(2)}, u32[]{:S(2)}) collective-permute-start(f32[2,3,5,1,512]{4,3,2,1,0:T(1,128)S(1)} %pad_maximum_fusion.6), channel_id=1, source_target_pairs={{4,0},{8,4},{12,8},{5,1},{9,5},{13,9},{6,2},{10,6},{14,10},{7,3},{... | collective-permute-start | bytes 184328 | tf_op jit(solution)/shard_map/ppermute | solution.py:13
  19.9 4.8 %collective-permute-done.1 = f32[2,3,5,1,512]{4,3,2,1,0:T(1,128)S(1)} collective-permute-done((f32[2,3,5,1,512]{4,3,2,1,0:T(1,128)S(1)}, f32[2,3,5,1,512]{4,3,2,1,0:T(1,128)S(1)}, u32[]{:S(2)}, u32[]{:S(2)}) %collective-permute-start.1) | collective-permute-done | bytes 61472 | tf_op jit(solution)/shard_map/ppermute | solution.py:13
  25.3 0.8 fusion.10
  26.3 1.0 %fusion.9 = (f32[8,3,4,16,512]{4,3,2,1,0:T(8,128)S(1)}, f32[8,3,4,16,512]{4,3,2,1,0:T(8,128)}) fusion(f32[8,3,4,16,512]{4,3,2,1,0:T(8,128)S(1)} %fusion.8, f32[2,3,5,17,512]{4,3,2,1,0:T(8,128)S(1)} %pad_maximum_fusion, f32[8,3,4,16,512]{4,3,2,1,0:T(8,128)} %get-tuple-element.10), kind=kLoop, calls=%fused_computation.20 | loop fusion | bytes 2260992
  27.3 0.9 %slice_dynamic-update-slice_fusion = (f32[8,3,4,16,512]{4,3,2,1,0:T(8,128)S(1)}, f32[8,3,4,16,512]{4,3,2,1,0:T(8,128)}) fusion(f32[8,3,4,16,512]{4,3,2,1,0:T(8,128)S(1)} %get-tuple-element.7, f32[2,3,5,17,512]{4,3,2,1,0:T(8,128)S(1)} %pad_maximum_fusion, f32[8,3,4,16,512]{4,3,2,1,0:T(8,128)} %get-tuple-element.8), kind=kLoop, calls=%fused_computation.21 | loop fusion | bytes 2654208 | tf_op jit(solution)/shard_map/stack | solution.py:111
  28.2 0.8 slice_dynamic-update-slice_fusion.4
  29.1 1.1 %maximum_dynamic-update-slice_fusion = f32[8,3,4,16,512]{4,3,2,1,0:T(8,128)} fusion(f32[8,3,4,16,512]{4,3,2,1,0:T(8,128)} %slice_dynamic-update-slice_fusion.4, f32[2,3,1,16,512]{4,3,2,1,0:T(8,128)S(1)} %collective-permute-done, f32[2,3,4,16,512]{4,3,2,1,0:T(8,128)S(1)} %broadcast_multiply_fusion), kind=kLoop, calls=%fused_computation.27 | loop fusion | flops 98304 | bytes 1376256
  30.2 0.9 %fusion.4 = f32[8,3,4,16,512]{4,3,2,1,0:T(8,128)} fusion(f32[8,3,4,16,512]{4,3,2,1,0:T(8,128)} %maximum_dynamic-update-slice_fusion, f32[2,3,5,17,512]{4,3,2,1,0:T(8,128)S(1)} %pad_maximum_fusion), kind=kLoop, calls=%fused_computation.15 | loop fusion | bytes 1437696
  31.1 0.9 %fusion.5 = f32[8,3,4,16,512]{4,3,2,1,0:T(8,128)} fusion(f32[8,3,4,16,512]{4,3,2,1,0:T(8,128)} %fusion.4, f32[2,3,5,17,512]{4,3,2,1,0:T(8,128)S(1)} %pad_maximum_fusion), kind=kLoop, calls=%fused_computation.16 | loop fusion | bytes 1437696
  32.0 0.8 slice_dynamic-update-slice_fusion.3
  32.8 2.9 %reshape.174 = f32[24,32768]{1,0:T(8,128)S(1)} reshape(f32[8,3,4,16,512]{4,3,2,1,0:T(8,128)} %slice_dynamic-update-slice_fusion.3) | data formatting | bytes 6291456 | tf_op jit(solution)/shard_map/reshape | solution.py:111
  35.7 4.6 %reshape.175 = f32[24,32768]{1,0:T(8,128)} reshape(f32[8,3,4,16,512]{4,3,2,1,0:T(8,128)} %copy-done.1) | data formatting | bytes 6291456 | tf_op jit(solution)/shard_map/reshape | solution.py:111
  40.3 3.0 %fusion = f32[32768]{0:T(1024)S(1)} fusion(f32[24,32768]{1,0:T(8,128)S(1)} %reshape.174, f32[24,24]{1,0:T(8,128)S(1)} %copy-done.2), kind=kOutput, calls=%fused_computation.10 | convolution fusion | flops 228032512 | bytes 3279104 | tf_op jit(solution)/shard_map/dot_general | solution.py:112
  43.3 3.1 %fusion.1 = f32[32768]{0:T(1024)S(1)} fusion(f32[24,32768]{1,0:T(8,128)S(1)} %copy-done, f32[24,24]{1,0:T(8,128)S(1)} %copy-done.2), kind=kOutput, calls=%fused_computation.11 | convolution fusion | flops 228032512 | bytes 3279104 | tf_op jit(solution)/shard_map/dot_general | solution.py:112
  46.5 0.7 add.370
  47.3 7.9 %reduce-scatter.2.cloned.1.call-done = f32[4,16,256]{2,1,0:T(8,128)} async-done(((f32[4,16,512]{2,1,0:T(8,128)}), f32[4,16,256]{2,1,0:T(8,128)}) %reduce-scatter.2.cloned.1.call-update) | async-done | bytes 65552 | tf_op jit(solution)/shard_map/reduce_scatter | solution.py:122
  55.2 0.9 %fusion.18 = f32[4,16,256]{2,1,0:T(8,128)S(1)} fusion(f32[4,16,256]{2,1,0:T(8,128)} %reduce-scatter.2.cloned.1.call-done, f32[4,16,512]{2,1,0:T(8,128)S(1)} %copy-done.3, s32[]{:T(128)S(6)} %select_n.154, s32[4,16,512]{2,1,0:T(8,128)S(1)} %copy-done.4, f32[256]{0:T(256)S(1)} %fusion.43, f32[4,16]{1,0:T(4,128)S(1)} %broadcast_multiply_fusion.1), kind=kLoop, calls=%fused_computation.56 | loop fusion | flops 114688 | bytes 263428 | tf_op jit(solution)/shard_map/div | solution.py:127
  56.2 2.1 %collective-permute-start.2 = (f32[4,16,3]{2,1,0:T(8,128)S(1)}, f32[4,16,3]{2,1,0:T(8,128)S(1)}, u32[]{:S(2)}, u32[]{:S(2)}) collective-permute-start(f32[4,16,3]{2,1,0:T(8,128)S(1)} %get-tuple-element.15), channel_id=1, source_target_pairs={{0,16},{1,17},{2,18},{3,19},{4,20},{5,21},{6,22},{7,23},{8,24},{9,... | collective-permute-start | bytes 2312 | tf_op jit(solution)/shard_map/ppermute | solution.py:24
  58.3 1.3 %collective-permute-start.3 = (f32[4,16,3]{2,1,0:T(8,128)S(1)}, f32[4,16,3]{2,1,0:T(8,128)S(1)}, u32[]{:S(2)}, u32[]{:S(2)}) collective-permute-start(f32[4,16,3]{2,1,0:T(8,128)S(1)} %get-tuple-element.16), channel_id=1, source_target_pairs={{16,0},{17,1},{18,2},{19,3},{20,4},{21,5},{22,6},{23,7},{24,8},{25... | collective-permute-start | bytes 2312 | tf_op jit(solution)/shard_map/ppermute | solution.py:26
  59.6 1.8 %collective-permute-done.3 = f32[4,16,3]{2,1,0:T(8,128)S(1)} collective-permute-done((f32[4,16,3]{2,1,0:T(8,128)S(1)}, f32[4,16,3]{2,1,0:T(8,128)S(1)}, u32[]{:S(2)}, u32[]{:S(2)}) %collective-permute-start.3) | collective-permute-done | bytes 800 | tf_op jit(solution)/shard_map/ppermute | solution.py:26
  61.6 3.8 %collective-permute-start.4 = (f32[4,3,256]{2,1,0:T(4,128)S(1)}, f32[4,3,256]{2,1,0:T(4,128)S(1)}, u32[]{:S(2)}, u32[]{:S(2)}) collective-permute-start(f32[4,3,256]{2,1,0:T(4,128)S(1)} %get-tuple-element.13), channel_id=1, source_target_pairs={{0,4},{4,8},{8,12},{1,5},{5,9},{9,13},{2,6},{6,10},{10,14},{3,7},{... | collective-permute-start | bytes 36872 | tf_op jit(solution)/shard_map/ppermute | solution.py:24
  65.4 1.3 %collective-permute-start.5 = (f32[4,3,256]{2,1,0:T(4,128)S(1)}, f32[4,3,256]{2,1,0:T(4,128)S(1)}, u32[]{:S(2)}, u32[]{:S(2)}) collective-permute-start(f32[4,3,256]{2,1,0:T(4,128)S(1)} %get-tuple-element.14), channel_id=1, source_target_pairs={{4,0},{8,4},{12,8},{5,1},{9,5},{13,9},{6,2},{10,6},{14,10},{7,3},{... | collective-permute-start | bytes 36872 | tf_op jit(solution)/shard_map/ppermute | solution.py:26
  66.8 4.2 %collective-permute-done.5 = f32[4,3,256]{2,1,0:T(4,128)S(1)} collective-permute-done((f32[4,3,256]{2,1,0:T(4,128)S(1)}, f32[4,3,256]{2,1,0:T(4,128)S(1)}, u32[]{:S(2)}, u32[]{:S(2)}) %collective-permute-start.5) | collective-permute-done | bytes 12320 | tf_op jit(solution)/shard_map/ppermute | solution.py:26
  71.1 3.4 %collective-permute-start.6 = (f32[3,22,256]{2,1,0:T(8,128)S(1)}, f32[3,22,256]{2,1,0:T(8,128)S(1)}, u32[]{:S(2)}, u32[]{:S(2)}) collective-permute-start(f32[3,22,256]{2,1,0:T(8,128)S(1)} %get-tuple-element.11), channel_id=1, source_target_pairs={{0,1},{1,2},{2,3},{4,5},{5,6},{6,7},{8,9},{9,10},{10,11},{12,13},{... | collective-permute-start | bytes 202760 | tf_op jit(solution)/shard_map/ppermute | solution.py:24
  74.4 1.3 %collective-permute-start.7 = (f32[3,22,256]{2,1,0:T(8,128)S(1)}, f32[3,22,256]{2,1,0:T(8,128)S(1)}, u32[]{:S(2)}, u32[]{:S(2)}) collective-permute-start(f32[3,22,256]{2,1,0:T(8,128)S(1)} %get-tuple-element.12), channel_id=1, source_target_pairs={{1,0},{2,1},{3,2},{5,4},{6,5},{7,6},{9,8},{10,9},{11,10},{13,12},{... | collective-permute-start | bytes 202760 | tf_op jit(solution)/shard_map/ppermute | solution.py:26
  75.7 0.7 collective-permute-done.6
  76.4 4.3 %collective-permute-done.7 = f32[3,22,256]{2,1,0:T(8,128)S(1)} collective-permute-done((f32[3,22,256]{2,1,0:T(8,128)S(1)}, f32[3,22,256]{2,1,0:T(8,128)S(1)}, u32[]{:S(2)}, u32[]{:S(2)}) %collective-permute-start.7) | collective-permute-done | bytes 67616 | tf_op jit(solution)/shard_map/ppermute | solution.py:26
  80.9 1.9 %all_gather.3 = f32[4,16,512]{2,1,0:T(8,128)S(1)} all-gather(f32[4,16,256]{2,1,0:T(8,128)S(1)} %slice_add_fusion.1), channel_id=1, replica_groups=mesh['load'=2,'sy'=4,'sz'=4] {'load'}, dimensions={2}, use_global_device_ids=true | all-gather | bytes 196608 | tf_op jit(solution)/shard_map/all_gather | solution.py:133
  (36 shorter events, 2.3 us)
Async XLA Ops:
  6.5 48.6 %reduce-scatter.2.cloned.1.call-start = ((), (), s32[]{:S(2)}) async-start(), calls=%async_computation.1 | async-start | bytes 196608 | tf_op jit(solution)/shard_map/reduce_scatter | solution.py:122
  8.7 9.8 %collective-permute-start = (f32[2,3,1,16,512]{4,3,2,1,0:T(8,128)S(1)}, f32[2,3,1,16,512]{4,3,2,1,0:T(8,128)S(1)}, u32[]{:S(2)}, u32[]{:S(2)}) collective-permute-start(f32[2,3,1,16,512]{4,3,2,1,0:T(8,128)S(1)} %slice.197), channel_id=1, source_target_pairs={{1,0},{2,1},{3,2},{5,4},{6,5},{7,6},{9,8},{10,9},{11,10},{13,12},{... | collective-permute-start | bytes 589832 | tf_op jit(solution)/shard_map/ppermute | solution.py:13
  18.6 6.1 %collective-permute-start.1 = (f32[2,3,5,1,512]{4,3,2,1,0:T(1,128)S(1)}, f32[2,3,5,1,512]{4,3,2,1,0:T(1,128)S(1)}, u32[]{:S(2)}, u32[]{:S(2)}) collective-permute-start(f32[2,3,5,1,512]{4,3,2,1,0:T(1,128)S(1)} %pad_maximum_fusion.6), channel_id=1, source_target_pairs={{4,0},{8,4},{12,8},{5,1},{9,5},{13,9},{6,2},{10,6},{14,10},{7,3},{... | collective-permute-start | bytes 184328 | tf_op jit(solution)/shard_map/ppermute | solution.py:13
  28.2 3.8 %copy-start.1 = (f32[8,3,4,16,512]{4,3,2,1,0:T(8,128)}, f32[8,3,4,16,512]{4,3,2,1,0:T(8,128)S(1)}, u32[]{:S(2)}) copy-start(f32[8,3,4,16,512]{4,3,2,1,0:T(8,128)S(1)} %get-tuple-element.5) | copy-start | bytes 9437188
  35.7 4.6 %copy-start.2 = (f32[24,24]{1,0:T(8,128)S(1)}, f32[24,24]{1,0:T(8,128)}, u32[]{:S(2)}) copy-start(f32[24,24]{1,0:T(8,128)} %constant.45.clone) | copy-start | bytes 6916
  40.3 3.0 %copy-start = (f32[24,32768]{1,0:T(8,128)S(1)}, f32[24,32768]{1,0:T(8,128)}, u32[]{:S(2)}) copy-start(f32[24,32768]{1,0:T(8,128)} %reshape.175) | copy-start | bytes 9437188
  40.3 14.8 %copy-start.3 = (f32[4,16,512]{2,1,0:T(8,128)S(1)}, f32[4,16,512]{2,1,0:T(8,128)}, u32[]{:S(2)}) copy-start(f32[4,16,512]{2,1,0:T(8,128)} %param.6) | copy-start | bytes 393220
  40.3 14.8 %copy-start.4 = (s32[4,16,512]{2,1,0:T(8,128)S(1)}, s32[4,16,512]{2,1,0:T(8,128)}, u32[]{:S(2)}) copy-start(s32[4,16,512]{2,1,0:T(8,128)} %param.7) | copy-start | bytes 393220
  56.2 3.4 %collective-permute-start.2 = (f32[4,16,3]{2,1,0:T(8,128)S(1)}, f32[4,16,3]{2,1,0:T(8,128)S(1)}, u32[]{:S(2)}, u32[]{:S(2)}) collective-permute-start(f32[4,16,3]{2,1,0:T(8,128)S(1)} %get-tuple-element.15), channel_id=1, source_target_pairs={{0,16},{1,17},{2,18},{3,19},{4,20},{5,21},{6,22},{7,23},{8,24},{9,... | collective-permute-start | bytes 2312 | tf_op jit(solution)/shard_map/ppermute | solution.py:24
  58.3 3.1 %collective-permute-start.3 = (f32[4,16,3]{2,1,0:T(8,128)S(1)}, f32[4,16,3]{2,1,0:T(8,128)S(1)}, u32[]{:S(2)}, u32[]{:S(2)}) collective-permute-start(f32[4,16,3]{2,1,0:T(8,128)S(1)} %get-tuple-element.16), channel_id=1, source_target_pairs={{16,0},{17,1},{18,2},{19,3},{20,4},{21,5},{22,6},{23,7},{24,8},{25... | collective-permute-start | bytes 2312 | tf_op jit(solution)/shard_map/ppermute | solution.py:26
  61.6 5.2 %collective-permute-start.4 = (f32[4,3,256]{2,1,0:T(4,128)S(1)}, f32[4,3,256]{2,1,0:T(4,128)S(1)}, u32[]{:S(2)}, u32[]{:S(2)}) collective-permute-start(f32[4,3,256]{2,1,0:T(4,128)S(1)} %get-tuple-element.13), channel_id=1, source_target_pairs={{0,4},{4,8},{8,12},{1,5},{5,9},{9,13},{2,6},{6,10},{10,14},{3,7},{... | collective-permute-start | bytes 36872 | tf_op jit(solution)/shard_map/ppermute | solution.py:24
  65.4 5.6 %collective-permute-start.5 = (f32[4,3,256]{2,1,0:T(4,128)S(1)}, f32[4,3,256]{2,1,0:T(4,128)S(1)}, u32[]{:S(2)}, u32[]{:S(2)}) collective-permute-start(f32[4,3,256]{2,1,0:T(4,128)S(1)} %get-tuple-element.14), channel_id=1, source_target_pairs={{4,0},{8,4},{12,8},{5,1},{9,5},{13,9},{6,2},{10,6},{14,10},{7,3},{... | collective-permute-start | bytes 36872 | tf_op jit(solution)/shard_map/ppermute | solution.py:26
  71.1 5.3 %collective-permute-start.6 = (f32[3,22,256]{2,1,0:T(8,128)S(1)}, f32[3,22,256]{2,1,0:T(8,128)S(1)}, u32[]{:S(2)}, u32[]{:S(2)}) collective-permute-start(f32[3,22,256]{2,1,0:T(8,128)S(1)} %get-tuple-element.11), channel_id=1, source_target_pairs={{0,1},{1,2},{2,3},{4,5},{5,6},{6,7},{8,9},{9,10},{10,11},{12,13},{... | collective-permute-start | bytes 202760 | tf_op jit(solution)/shard_map/ppermute | solution.py:24
  74.4 6.2 %collective-permute-start.7 = (f32[3,22,256]{2,1,0:T(8,128)S(1)}, f32[3,22,256]{2,1,0:T(8,128)S(1)}, u32[]{:S(2)}, u32[]{:S(2)}) collective-permute-start(f32[3,22,256]{2,1,0:T(8,128)S(1)} %get-tuple-element.12), channel_id=1, source_target_pairs={{1,0},{2,1},{3,2},{5,4},{6,5},{7,6},{9,8},{10,9},{11,10},{13,12},{... | collective-permute-start | bytes 202760 | tf_op jit(solution)/shard_map/ppermute | solution.py:26
Sparse Core Ops, SparseCore 0:
  47.3 7.8 reduce-scatter.1
where the time goes:
time: 90.8 us; the launch traced here: 90.3 us
  waiting for transfers between devices  32.2 us (35%)
  starting transfers between devices  15.7 us (17%)
  local copies, waits for them, and re-layouts  15 us (17%)
  between operations  13.7 us (15%)
  matrix products  6.1 us (7%)
  other arithmetic  5.72 us (6%)
  blocking collectives  1.9 us (2%)
    ppermute x2, waiting for transfers between devices, shifted(): return lax.ppermute(value, axis, pairs)  13.3 us
    ppermute x3, waiting for transfers between devices, extended_2(): lax.ppermute(head, axis, [((i + 1) % count, i) for i in range(ends)])  10.3 us
    ppermute x3, starting transfers between devices, extended_2(): lax.ppermute(tail, axis, [(i, (i + 1) % count) for i in range(ends)])  9.22 us
    reduce_scatter x1, waiting for transfers between devices, body(): lax.psum_scatter(partial_energy, 'load', scatter_dimension=2, tiled=True)  7.91 us
    reshape x2, local copies, waits for them, and re-layouts, body(): local = jnp.stack(nodes, axis=0).reshape(24, zlen * ylen * xlen)  7.51 us
    dot_general x2, matrix products, body(): jnp.dot(stiffness, local, precision=lax.Precision.HIGHEST, preferred_elem...  6.1 us
    unnamed x20, local copies, waits for them, and re-layouts  4.96 us
    ppermute x3, starting transfers between devices, extended_2(): lax.ppermute(head, axis, [((i + 1) % count, i) for i in range(ends)])  3.88 us
  transfers between devices with their start and end apart: 9, of which 8 were waited for; matrix products, arithmetic and copies ran while one was open for 0% of the time, Pallas kernels for 0%

commit v1 on v0

v1 whole, which is shorter than its diff:
```python
import jax
import jax.numpy as jnp
import numpy as np
from jax import lax
from jax.experimental import pallas as pl
from jax.experimental.pallas import tpu as pltpu
from jax.sharding import PartitionSpec as P

OFFSETS = [(0, 0, 0), (1, 0, 0), (1, 1, 0), (0, 1, 0), (0, 0, 1), (1, 0, 1), (1, 1, 1), (0, 1, 1)]
REACH = 3
ROWS = REACH + 1
TILE = 8
LANES = 128


def element_matrix():
    corners = np.array(
        [
            [-1.0, -1.0, -1.0],
            [1.0, -1.0, -1.0],
            [1.0, 1.0, -1.0],
            [-1.0, 1.0, -1.0],
            [-1.0, -1.0, 1.0],
            [1.0, -1.0, 1.0],
            [1.0, 1.0, 1.0],
            [-1.0, 1.0, 1.0],
        ]
    )
    poisson = 0.3
    lame = poisson / ((1.0 + poisson) * (1.0 - 2.0 * poisson))
    shear = 1.0 / (2.0 * (1.0 + poisson))
    elastic = np.zeros((6, 6))
    elastic[:3, :3] = lame
    for k in range(3):
        elastic[k, k] += 2.0 * shear
        elastic[3 + k, 3 + k] = shear
    gauss = 1.0 / np.sqrt(3.0)
    stiffness = np.zeros((24, 24))
    for gi in range(2):
        for gj in range(2):
            for gk in range(2):
                point = np.array([(2 * gi - 1) * gauss, (2 * gj - 1) * gauss, (2 * gk - 1) * gauss])
                strain = np.zeros((6, 24))
                for node in range(8):
                    grads = np.zeros(3)
                    for k in range(3):
                        value = corners[node, k] / 8.0
                        for m in range(3):
                            if m != k:
                                value = value * (1.0 + point[m] * corners[node, m])
                        grads[k] = 2.0 * value
                    col = 3 * node
                    strain[0, col] = grads[0]
                    strain[1, col + 1] = grads[1]
                    strain[2, col + 2] = grads[2]
                    strain[3, col] = grads[1]
                    strain[3, col + 1] = grads[0]
                    strain[4, col + 1] = grads[2]
                    strain[4, col + 2] = grads[1]
                    strain[5, col] = grads[2]
                    strain[5, col + 2] = grads[0]
                stiffness += strain.T @ elastic @ strain / 8.0
    return stiffness


def mode_weights():
    modes = [(i, j, k) for k in (0, 1) for j in (0, 1) for i in (0, 1)]
    sums = np.zeros((24, 24))
    for m, mode in enumerate(modes):
        for n, corner in enumerate(OFFSETS):
            sign = np.prod([(1 if corner[d] else -1) if mode[d] else 1 for d in range(3)])
            for comp in range(3):
                sums[3 * m + comp, 3 * n + comp] = sign
    form = sums @ element_matrix() @ sums.T / 64.0

    def at(first, second):
        return form[3 * modes.index(first[1]) + first[0], 3 * modes.index(second[1]) + second[0]]

    ux, vy, uy = (0, (1, 0, 0)), (1, (0, 1, 0)), (0, (0, 1, 0))
    uxy, wyz = (0, (1, 1, 0)), (2, (0, 1, 1))
    wxy, vxz, uxyz = (2, (1, 1, 0)), (1, (1, 0, 1)), (0, (1, 1, 1))
    return dict(
        normal=at(ux, ux) - at(ux, vy),
        trace=at(ux, vy),
        shear=at(uy, uy),
        plus=(at(uxy, uxy) + at(uxy, wyz)) / 2,
        minus=(at(uxy, uxy) - at(uxy, wyz)) / 2,
        twist=at(wxy, wxy) - at(wxy, vxz),
        twist_sum=at(wxy, vxz),
        corner=at(uxyz, uxyz),
    )


def square(value):
    return value * value


def quadratic(low, high, weights):
    x = [low[c][1] + high[c][1] for c in range(3)]
    y = [low[c][2] + high[c][2] for c in range(3)]
    z = [high[c][0] - low[c][0] for c in range(3)]
    xy = [low[c][3] + high[c][3] for c in range(3)]
    xz = [high[c][1] - low[c][1] for c in range(3)]
    yz = [high[c][2] - low[c][2] for c in range(3)]
    xyz = [high[c][3] - low[c][3] for c in range(3)]
    normal = square(x[0]) + square(y[1]) + square(z[2])
    trace = square(x[0] + y[1] + z[2])
    shear = square(y[0] + x[1]) + square(z[0] + x[2]) + square(z[1] + y[2])
    pairs = ((xy[0], yz[2]), (xy[1], xz[2]), (xz[0], yz[1]))
    plus = sum(square(p + q) for p, q in pairs)
    minus = sum(square(p - q) for p, q in pairs)
    twist = square(xy[2]) + square(xz[1]) + square(yz[0])
    twist_sum = square(xy[2] + xz[1] + yz[0])
    corner = square(xyz[0]) + square(xyz[1]) + square(xyz[2])
    groups = dict(
        normal=normal, trace=trace, shear=shear, plus=plus, minus=minus, twist=twist, twist_sum=twist_sum, corner=corner
    )
    return sum(np.float32(weights[name]) * group for name, group in groups.items())


def line_weight(coord, count):
    def outside(distance):
        missing = jnp.maximum(REACH - distance, 0)
        return missing * (missing + 1) // 2

    whole = (REACH + 1) * (REACH + 1)
    return (whole - outside(coord) - outside(count - 1 - coord)).astype(jnp.float32)


def voxel_factor(density, solid, plane, first_row, total_z, total_y):
    rows, length = density.shape
    row = lax.broadcasted_iota(jnp.int32, (rows, length), 0) + first_row
    column = lax.broadcasted_iota(jnp.int32, (rows, length), 1)
    weight = line_weight(row, total_y) * line_weight(column, length)
    weight = weight * line_weight(jnp.full((rows, length), plane, jnp.int32), total_z)
    return solid.astype(jnp.float32) * (-3.0 * density * density) / weight


def spread_x(value):
    rows, length = value.shape
    wide = jnp.concatenate([value, jnp.zeros((rows, LANES), jnp.float32)], axis=1)
    span = length + LANES
    wide = wide + pltpu.roll(wide, span - 1, 1)
    wide = wide + pltpu.roll(wide, span - 2, 1)
    wide = wide + pltpu.roll(wide, 1, 1)
    wide = wide + pltpu.roll(wide, 2, 1)
    return wide[:, :length]


def spread_layers(layers):
    for step in (1, 2, 1, 2):
        layers = [layers[k] + layers[k + step] for k in range(len(layers) - step)]
    return layers


def lead_kernel(totals, disp, fixed, density, solid, z_out, y_out, d_out):
    loads, comps, zlen, ylen, _ = disp.shape
    total_z, total_y = totals
    base_z = lax.axis_index("sz") * zlen
    base_y = lax.axis_index("sy") * ylen
    free = [1.0 - fixed[z].astype(jnp.float32) for z in range(zlen)]
    for case in range(loads):
        for comp in range(comps):
            k = case * comps + comp
            layer = disp[case, comp, 0] * free[0]
            z_out[k] = layer
            d_out[ROWS * k : ROWS * (k + 1)] = layer[:ROWS]
            y_out[k, :ROWS] = layer[:ROWS]
            for z in range(1, zlen):
                y_out[k, ROWS * z : ROWS * (z + 1)] = disp[case, comp, z, :ROWS] * free[z][:ROWS]
    for z in range(zlen):
        factor = voxel_factor(density[z, :TILE], solid[z, :TILE], base_z + z, base_y, total_z, total_y)
        y_out[loads * comps, ROWS * z : ROWS * (z + 1)] = factor[:ROWS]


def energy_kernel(totals, disp, fixed, density, solid, z_in, y_in, d_in, own_out, up_out, plus, diff, factor, quotient):
    loads, comps, zlen, ylen, xlen = disp.shape
    total_z, total_y = totals
    base_z = lax.axis_index("sz") * zlen
    base_y = lax.axis_index("sy") * ylen
    weights = mode_weights()

    def split_x(value):
        column = lax.broadcasted_iota(jnp.int32, value.shape, 1)
        ahead = jnp.where(column == xlen - 1, 0.0, pltpu.roll(value, xlen - 1, 1))
        return value + ahead, ahead - value

    @pl.loop(0, loads * comps)
    def _(k):
        case, comp = k // comps, k % comps
        for z in range(zlen):
            whole, change = split_x(disp[case, comp, z] * (1.0 - fixed[z].astype(jnp.float32)))
            plus[k, z, :ylen] = whole
            diff[k, z, :ylen] = change
        whole, change = split_x(z_in[k])
        plus[k, zlen, :ylen] = whole
        diff[k, zlen, :ylen] = change
        whole, change = split_x(y_in[k])
        for z in range(zlen):
            plus[k, z, ylen : ylen + ROWS] = whole[ROWS * z : ROWS * (z + 1)]
            diff[k, z, ylen : ylen + ROWS] = change[ROWS * z : ROWS * (z + 1)]

    whole, change = split_x(d_in[...])
    for k in range(loads * comps):
        plus[k, zlen, ylen : ylen + ROWS] = whole[ROWS * k : ROWS * (k + 1)]
        diff[k, zlen, ylen : ylen + ROWS] = change[ROWS * k : ROWS * (k + 1)]

    for z in range(zlen):
        factor[z, :ylen] = voxel_factor(density[z], solid[z], base_z + z, base_y, total_z, total_y)
        factor[z, ylen : ylen + ROWS] = y_in[loads * comps, ROWS * z : ROWS * (z + 1)]

    for first in range(0, ylen + REACH, TILE):

        @pl.loop(0, xlen // LANES)
        def _(chunk):
            lanes = pl.ds(pl.multiple_of(chunk * LANES, LANES), LANES)

            def faces(k, z):
                whole, whole_next = plus[k, z, first : first + TILE, lanes], plus[k, z, first + 1 : first + TILE + 1, lanes]
                change, change_next = diff[k, z, first : first + TILE, lanes], diff[k, z, first + 1 : first + TILE + 1, lanes]
                return whole + whole_next, change + change_next, whole_next - whole, change_next - change

            energy = [None] * zlen
            for case in range(loads):
                low = None
                for z in range(zlen + 1):
                    high = [faces(case * comps + comp, z) for comp in range(comps)]
                    if low is not None:
                        part = quadratic(low, high, weights)
                        energy[z - 1] = part if energy[z - 1] is None else energy[z - 1] + part
                    low = high
            for z in range(zlen):
                quotient[z, first + TILE : first + 2 * TILE, lanes] = energy[z] * factor[z, first : first + TILE, lanes]

    for z in range(zlen):
        quotient[z, :TILE] = jnp.zeros((TILE, xlen), jnp.float32)
        rows = [quotient[z, TILE + step : TILE + step + ylen] for step in range(-REACH, REACH + 1)]
        own_out[z] = sum((ROWS - abs(k - REACH)) * rows[k] for k in range(2 * REACH + 1))
        top = quotient[z, ylen : ylen + TILE]
        last = [top[TILE - 1 - k : TILE - k] for k in range(REACH)]
        up = [
            sum(float(REACH - row - k) * last[k] for k in range(REACH - row)) for row in range(REACH)
        ]
        up_out[ROWS * z : ROWS * (z + 1)] = jnp.concatenate(up + [jnp.zeros((1, xlen), jnp.float32)], axis=0)


def rows_kernel(own, up_in, h_out, down_out, up_out):
    zlen = own.shape[0]
    for z in range(zlen):
        h_out[z] = own[z]
        h_out[z, :ROWS] = own[z, :ROWS] + up_in[ROWS * z : ROWS * (z + 1)]
    down_out[...] = h_out[:REACH]
    up_out[...] = h_out[zlen - REACH :]


def layers_kernel(h, below, above, out):
    zlen = h.shape[0]
    layers = [below[k] for k in range(REACH)] + [h[z] for z in range(zlen)] + [above[k] for k in range(REACH)]
    for z, layer in enumerate(spread_layers(layers)):
        out[z] = spread_x(layer)


def sum_kernel(parts, out):
    out[...] = parts[0] + parts[1]


def vmem(count):
    return [pl.BlockSpec(memory_space=pltpu.VMEM)] * count


def call(kernel, outs, args, scratch=(), **kwargs):
    shapes = [jax.ShapeDtypeStruct(shape, jnp.float32) for shape in outs]
    result = pl.pallas_call(
        kernel,
        out_shape=shapes,
        in_specs=vmem(len(args)),
        out_specs=vmem(len(outs)),
        scratch_shapes=list(scratch),
        compiler_params=pltpu.CompilerParams(vmem_limit_bytes=32 * 1024 * 1024),
        **kwargs,
    )(*args)
    return result


def moved(value, axes, steps):
    sizes = [lax.axis_size(axis) for axis in axes]
    pairs = []
    for flat in range(int(np.prod(sizes))):
        place = np.unravel_index(flat, sizes)
        source = [int(p) + s for p, s in zip(place, steps)]
        if all(0 <= s < size for s, size in zip(source, sizes)):
            pairs.append((int(np.ravel_multi_index(source, sizes)), flat))
    return lax.ppermute(value, axes if len(axes) > 1 else axes[0], pairs)


def body(displacements, density, solid, fixed):
    loads, comps, zlen, ylen, xlen = displacements.shape
    planes = loads * comps
    totals = (zlen * lax.axis_size("sz"), ylen * lax.axis_size("sy"))

    def bound(kernel):
        def run(*refs):
            kernel(totals, *refs)

        return run

    z_send, y_send, d_send = call(
        bound(lead_kernel),
        [(planes, ylen, xlen), (planes + 1, ROWS * zlen, xlen), (ROWS * planes, xlen)],
        (displacements, fixed, density, solid),
    )
    z_in = moved(z_send, ("sz",), (1,))
    y_in = moved(y_send, ("sy",), (1,))
    d_in = moved(d_send, ("sy", "sz"), (1, 1))
    high = ylen + 2 * TILE
    own, up_send = call(
        bound(energy_kernel),
        [(zlen, ylen, xlen), (ROWS * zlen, xlen)],
        (displacements, fixed, density, solid, z_in, y_in, d_in),
        scratch=[
            pltpu.VMEM((planes, zlen + 1, high, xlen), jnp.float32),
            pltpu.VMEM((planes, zlen + 1, high, xlen), jnp.float32),
            pltpu.VMEM((zlen, ylen + TILE, xlen), jnp.float32),
            pltpu.VMEM((zlen, ylen + 2 * TILE, xlen), jnp.float32),
        ],
    )
    up_in = moved(up_send, ("sy",), (-1,))
    h, down_send, over_send = call(
        rows_kernel, [(zlen, ylen, xlen), (REACH, ylen, xlen), (REACH, ylen, xlen)], (own, up_in)
    )
    above = moved(down_send, ("sz",), (1,))
    below = moved(over_send, ("sz",), (-1,))
    (part,) = call(layers_kernel, [(zlen, ylen, xlen)], (h, below, above))
    parts = lax.all_gather(part, "load", axis=0)
    (out,) = call(sum_kernel, [(zlen, ylen, xlen)], (parts,))
    return out


def solution(mesh):
    return jax.shard_map(
        body,
        mesh=mesh,
        in_specs=(
            P("load", None, "sz", "sy", None),
            P("sz", "sy", None),
            P("sz", "sy", None),
            P("sz", "sy", None),
        ),
        out_specs=P("sz", "sy", None),
        check_vma=False,
    )
```

time: 90.8 us -> 41.3 us (0.45)
  waiting for transfers between devices: 32.2 us -> 16.9 us
  between operations: 13.7 us -> 0.07 us
  local copies, waits for them, and re-layouts: 15 us -> 3.84 us
  matrix products: 6.1 us -> 0 us
  other arithmetic: 5.72 us -> 0 us
  Pallas kernels: 0 us -> 5.12 us
  starting transfers between devices: 15.7 us -> 13.1 us
    reduce_scatter x1 -> x0, waiting for transfers between devices: 7.91 us -> none  [body(): lax.psum_scatter(partial_energy, 'load', scatter_dimension=2, tiled=True)]
    reshape x2 -> x0, local copies, waits for them, and re-layouts: 7.51 us -> none  [body(): local = jnp.stack(nodes, axis=0).reshape(24, zlen * ylen * xlen)]
    ppermute x8 -> x6, waiting for transfers between devices: 24.3 us -> 16.9 us  [moved(): return lax.ppermute(value, axes if len(axes) > 1 else axes[0], pairs)]
    dot_general x2 -> x0, matrix products: 6.1 us -> none  [body(): jnp.dot(stiffness, local, precision=lax.Precision.HIGHEST, preferred_elem...]
    pallas_call x0 -> x5, Pallas kernels: none -> 5.12 us  [call(): pl.pallas_call(kernel, out_shape=shapes, in_specs=vmem(len(args)), out_sp...]
    ppermute x8 -> x6, starting transfers between devices: 15.7 us -> 13.1 us  [moved(): return lax.ppermute(value, axes if len(axes) > 1 else axes[0], pairs)]
    unnamed x2 -> x0, other arithmetic: 1.9 us -> none
    another operation x2 -> x0, local copies, waits for them, and re-layouts: 1.73 us -> none  [body(): local = jnp.stack(nodes, axis=0).reshape(24, zlen * ylen * xlen)]
  transfers between devices with their start and end apart: 9 -> 6, of which waited for: 8 -> 4; matrix products, arithmetic and copies ran while one was open for 0% -> 0% of each run, Pallas kernels for 0% -> 0%
where the time goes in v1:
time: 41.3 us; the launch traced here: 41 us
  waiting for transfers between devices  16.9 us (41%)
  starting transfers between devices  13.1 us (32%)
  Pallas kernels  5.12 us (12%)
  local copies, waits for them, and re-layouts  3.84 us (9%)
  blocking collectives  1.99 us (5%)
    ppermute x6, waiting for transfers between devices, moved(): return lax.ppermute(value, axes if len(axes) > 1 else axes[0], pairs)  16.9 us
    ppermute x6, starting transfers between devices, moved(): return lax.ppermute(value, axes if len(axes) > 1 else axes[0], pairs)  13.1 us
    pallas_call x5, Pallas kernels, call(): pl.pallas_call(kernel, out_shape=shapes, in_specs=vmem(len(args)), out_sp...  5.12 us
    unnamed x8, local copies, waits for them, and re-layouts  3.84 us
    all_gather x1, blocking collectives, body(): parts = lax.all_gather(part, 'load', axis=0)  1.99 us
  transfers between devices with their start and end apart: 6, of which 4 were waited for; matrix products, arithmetic and copies ran while one was open for 0% of the time, Pallas kernels for 0%

profile of v1, /device:TPU:0, one launch (start us, length us, event | category | flops | bytes accessed | tf_op | source)
XLA Modules:
  0.0 41.0 jit_solution(4035246303884938093)
XLA Ops:
  0.0 0.0 copy-start
  0.0 1.1 %copy-done = f32[2,3,4,16,512]{4,3,2,1,0:T(8,128)S(1)} copy-done((f32[2,3,4,16,512]{4,3,2,1,0:T(8,128)S(1)}, f32[2,3,4,16,512]{4,3,2,1,0:T(8,128)}, u32[]{:S(2)}) %copy-start) | copy-done | bytes 786456
  1.1 0.0 copy-start.1
  1.1 0.9 %copy-done.1 = s32[4,16,512]{2,1,0:T(8,128)S(1)} copy-done((s32[4,16,512]{2,1,0:T(8,128)S(1)}, s32[4,16,512]{2,1,0:T(8,128)}, u32[]{:S(2)}) %copy-start.1) | copy-done | bytes 131096
  2.0 0.0 copy-start.2
  2.0 0.9 %copy-done.2 = f32[4,16,512]{2,1,0:T(8,128)S(1)} copy-done((f32[4,16,512]{2,1,0:T(8,128)S(1)}, f32[4,16,512]{2,1,0:T(8,128)}, u32[]{:S(2)}) %copy-start.2) | copy-done | bytes 131096
  2.9 0.0 copy-start.3
  2.9 0.9 %copy-done.3 = s32[4,16,512]{2,1,0:T(8,128)S(1)} copy-done((s32[4,16,512]{2,1,0:T(8,128)S(1)}, s32[4,16,512]{2,1,0:T(8,128)}, u32[]{:S(2)}) %copy-start.3) | copy-done | bytes 131096
  3.8 0.1 shard_map.46
  4.0 1.3 %collective-permute-start.1 = (f32[7,16,512]{2,1,0:T(8,128)S(1)}, f32[7,16,512]{2,1,0:T(8,128)S(1)}, u32[]{:S(2)}, u32[]{:S(2)}) collective-permute-start(f32[7,16,512]{2,1,0:T(8,128)S(1)} %get-tuple-element.14), channel_id=1, source_target_pairs={{4,0},{8,4},{12,8},{5,1},{9,5},{13,9},{6,2},{10,6},{14,10},{7,3},{... | collective-permute-start | bytes 688136 | tf_op jit(solution)/shard_map/ppermute | solution.py:293
  5.3 1.3 %collective-permute-start = (f32[6,16,512]{2,1,0:T(8,128)S(1)}, f32[6,16,512]{2,1,0:T(8,128)S(1)}, u32[]{:S(2)}, u32[]{:S(2)}) collective-permute-start(f32[6,16,512]{2,1,0:T(8,128)S(1)} %get-tuple-element.13), channel_id=1, source_target_pairs={{1,0},{2,1},{3,2},{5,4},{6,5},{7,6},{9,8},{10,9},{11,10},{13,12},{... | collective-permute-start | bytes 589832 | tf_op jit(solution)/shard_map/ppermute | solution.py:293
  6.6 1.3 %collective-permute-start.2 = (f32[24,512]{1,0:T(8,128)S(1)}, f32[24,512]{1,0:T(8,128)S(1)}, u32[]{:S(2)}, u32[]{:S(2)}) collective-permute-start(f32[24,512]{1,0:T(8,128)S(1)} %get-tuple-element.15), channel_id=1, source_target_pairs={{5,0},{6,1},{7,2},{9,4},{10,5},{11,6},{13,8},{14,9},{15,10},{21,16... | collective-permute-start | bytes 147464 | tf_op jit(solution)/shard_map/ppermute | solution.py:293
  7.9 10.1 %collective-permute-done.2.refs_6_ = f32[24,512]{1,0:T(8,128)S(1)} collective-permute-done((f32[24,512]{1,0:T(8,128)S(1)}, f32[24,512]{1,0:T(8,128)S(1)}, u32[]{:S(2)}, u32[]{:S(2)}) %collective-permute-start.2) | collective-permute-done | bytes 49184 | tf_op jit(solution)/shard_map/ppermute | solution.py:293
  17.9 0.0 collective-permute-done.refs_4_
  17.9 0.0 collective-permute-done.1.refs_5_
  17.9 3.9 %shard_map.47 = (f32[4,16,512]{2,1,0:T(8,128)S(1)}, f32[16,512]{1,0:T(8,128)S(1)}) custom-call(f32[2,3,4,16,512]{4,3,2,1,0:T(8,128)S(1)} %copy-done, s32[4,16,512]{2,1,0:T(8,128)S(1)} %copy-done.1, f32[4,16,512]{2,1,0:T(8,128)S(1)} %copy-done.2, s32[4,16,512]{2,1,0:T(8,128)S(1)} %copy-done.3, f32[6,16,512]{2,1,0:T(8,128)S(1)} %collective-permute-done.refs_4_, ...), custom_call_target="tpu_custom_call" | custom-call | tf_op jit(solution)/shard_map/pallas_call | solution.py:273
  21.9 4.5 %collective-permute-start.3 = (f32[16,512]{1,0:T(8,128)S(1)}, f32[16,512]{1,0:T(8,128)S(1)}, u32[]{:S(2)}, u32[]{:S(2)}) collective-permute-start(f32[16,512]{1,0:T(8,128)S(1)} %get-tuple-element.17), channel_id=1, source_target_pairs={{0,4},{4,8},{8,12},{1,5},{5,9},{9,13},{2,6},{6,10},{10,14},{3,7},{... | collective-permute-start | bytes 98312 | tf_op jit(solution)/shard_map/ppermute | solution.py:293
  26.4 1.6 %collective-permute-done.3.up_in = f32[16,512]{1,0:T(8,128)S(1)} collective-permute-done((f32[16,512]{1,0:T(8,128)S(1)}, f32[16,512]{1,0:T(8,128)S(1)}, u32[]{:S(2)}, u32[]{:S(2)}) %collective-permute-start.3) | collective-permute-done | bytes 32800 | tf_op jit(solution)/shard_map/ppermute | solution.py:293
  28.0 3.5 %collective-permute-start.4 = (f32[3,16,512]{2,1,0:T(8,128)S(1)}, f32[3,16,512]{2,1,0:T(8,128)S(1)}, u32[]{:S(2)}, u32[]{:S(2)}) collective-permute-start(f32[3,16,512]{2,1,0:T(8,128)S(1)} %get-tuple-element.19), channel_id=1, source_target_pairs={{0,1},{1,2},{2,3},{4,5},{5,6},{6,7},{8,9},{9,10},{10,11},{12,13},{... | collective-permute-start | bytes 294920 | tf_op jit(solution)/shard_map/ppermute | solution.py:293
  31.5 1.3 %collective-permute-start.5 = (f32[3,16,512]{2,1,0:T(8,128)S(1)}, f32[3,16,512]{2,1,0:T(8,128)S(1)}, u32[]{:S(2)}, u32[]{:S(2)}) collective-permute-start(f32[3,16,512]{2,1,0:T(8,128)S(1)} %get-tuple-element.20), channel_id=1, source_target_pairs={{1,0},{2,1},{3,2},{5,4},{6,5},{7,6},{9,8},{10,9},{11,10},{13,12},{... | collective-permute-start | bytes 294920 | tf_op jit(solution)/shard_map/ppermute | solution.py:293
  32.8 0.9 %collective-permute-done.4.below = f32[3,16,512]{2,1,0:T(8,128)S(1)} collective-permute-done((f32[3,16,512]{2,1,0:T(8,128)S(1)}, f32[3,16,512]{2,1,0:T(8,128)S(1)}, u32[]{:S(2)}, u32[]{:S(2)}) %collective-permute-start.4) | collective-permute-done | bytes 98336 | tf_op jit(solution)/shard_map/ppermute | solution.py:293
  33.7 4.3 %collective-permute-done.5.above = f32[3,16,512]{2,1,0:T(8,128)S(1)} collective-permute-done((f32[3,16,512]{2,1,0:T(8,128)S(1)}, f32[3,16,512]{2,1,0:T(8,128)S(1)}, u32[]{:S(2)}, u32[]{:S(2)}) %collective-permute-start.5) | collective-permute-done | bytes 98336 | tf_op jit(solution)/shard_map/ppermute | solution.py:293
  38.0 0.4 shard_map.49
  38.3 2.0 %all-gather = f32[8,16,512]{2,1,0:T(8,128)S(1)} all-gather(f32[4,16,512]{2,1,0:T(8,128)S(1)} %shard_map.49), channel_id=2, replica_groups=mesh['load'=2,'sy'=4,'sz'=4] {'load'}, dimensions={0}, use_global_device_ids=true | all-gather | bytes 393216 | tf_op jit(solution)/shard_map/all_gather | solution.py:334
  40.3 0.7 %shard_map.50 = f32[4,16,512]{2,1,0:T(8,128)} custom-call(f32[2,4,16,512]{3,2,1,0:T(8,128)S(1)} %bitcast.1), custom_call_target="tpu_custom_call" | custom-call | tf_op jit(solution)/shard_map/pallas_call | solution.py:273
  (1 shorter events, 0.0 us)
Async XLA Ops:
  0.0 1.1 %copy-start = (f32[2,3,4,16,512]{4,3,2,1,0:T(8,128)S(1)}, f32[2,3,4,16,512]{4,3,2,1,0:T(8,128)}, u32[]{:S(2)}) copy-start(f32[2,3,4,16,512]{4,3,2,1,0:T(8,128)} %refs_0_.3) | copy-start | bytes 2359300
  1.1 0.9 %copy-start.1 = (s32[4,16,512]{2,1,0:T(8,128)S(1)}, s32[4,16,512]{2,1,0:T(8,128)}, u32[]{:S(2)}) copy-start(s32[4,16,512]{2,1,0:T(8,128)} %refs_1_.3) | copy-start | bytes 393220
  2.0 0.9 %copy-start.2 = (f32[4,16,512]{2,1,0:T(8,128)S(1)}, f32[4,16,512]{2,1,0:T(8,128)}, u32[]{:S(2)}) copy-start(f32[4,16,512]{2,1,0:T(8,128)} %refs_2_.3) | copy-start | bytes 393220
  2.9 0.9 %copy-start.3 = (s32[4,16,512]{2,1,0:T(8,128)S(1)}, s32[4,16,512]{2,1,0:T(8,128)}, u32[]{:S(2)}) copy-start(s32[4,16,512]{2,1,0:T(8,128)} %refs_3_.3) | copy-start | bytes 393220
  4.0 14.0 %collective-permute-start.1 = (f32[7,16,512]{2,1,0:T(8,128)S(1)}, f32[7,16,512]{2,1,0:T(8,128)S(1)}, u32[]{:S(2)}, u32[]{:S(2)}) collective-permute-start(f32[7,16,512]{2,1,0:T(8,128)S(1)} %get-tuple-element.14), channel_id=1, source_target_pairs={{4,0},{8,4},{12,8},{5,1},{9,5},{13,9},{6,2},{10,6},{14,10},{7,3},{... | collective-permute-start | bytes 688136 | tf_op jit(solution)/shard_map/ppermute | solution.py:293
  5.3 12.7 %collective-permute-start = (f32[6,16,512]{2,1,0:T(8,128)S(1)}, f32[6,16,512]{2,1,0:T(8,128)S(1)}, u32[]{:S(2)}, u32[]{:S(2)}) collective-permute-start(f32[6,16,512]{2,1,0:T(8,128)S(1)} %get-tuple-element.13), channel_id=1, source_target_pairs={{1,0},{2,1},{3,2},{5,4},{6,5},{7,6},{9,8},{10,9},{11,10},{13,12},{... | collective-permute-start | bytes 589832 | tf_op jit(solution)/shard_map/ppermute | solution.py:293
  6.6 11.4 %collective-permute-start.2 = (f32[24,512]{1,0:T(8,128)S(1)}, f32[24,512]{1,0:T(8,128)S(1)}, u32[]{:S(2)}, u32[]{:S(2)}) collective-permute-start(f32[24,512]{1,0:T(8,128)S(1)} %get-tuple-element.15), channel_id=1, source_target_pairs={{5,0},{6,1},{7,2},{9,4},{10,5},{11,6},{13,8},{14,9},{15,10},{21,16... | collective-permute-start | bytes 147464 | tf_op jit(solution)/shard_map/ppermute | solution.py:293
  21.9 6.0 %collective-permute-start.3 = (f32[16,512]{1,0:T(8,128)S(1)}, f32[16,512]{1,0:T(8,128)S(1)}, u32[]{:S(2)}, u32[]{:S(2)}) collective-permute-start(f32[16,512]{1,0:T(8,128)S(1)} %get-tuple-element.17), channel_id=1, source_target_pairs={{0,4},{4,8},{8,12},{1,5},{5,9},{9,13},{2,6},{6,10},{10,14},{3,7},{... | collective-permute-start | bytes 98312 | tf_op jit(solution)/shard_map/ppermute | solution.py:293
  28.0 5.7 %collective-permute-start.4 = (f32[3,16,512]{2,1,0:T(8,128)S(1)}, f32[3,16,512]{2,1,0:T(8,128)S(1)}, u32[]{:S(2)}, u32[]{:S(2)}) collective-permute-start(f32[3,16,512]{2,1,0:T(8,128)S(1)} %get-tuple-element.19), channel_id=1, source_target_pairs={{0,1},{1,2},{2,3},{4,5},{5,6},{6,7},{8,9},{9,10},{10,11},{12,13},{... | collective-permute-start | bytes 294920 | tf_op jit(solution)/shard_map/ppermute | solution.py:293
  31.5 6.5 %collective-permute-start.5 = (f32[3,16,512]{2,1,0:T(8,128)S(1)}, f32[3,16,512]{2,1,0:T(8,128)S(1)}, u32[]{:S(2)}, u32[]{:S(2)}) collective-permute-start(f32[3,16,512]{2,1,0:T(8,128)S(1)} %get-tuple-element.20), channel_id=1, source_target_pairs={{1,0},{2,1},{3,2},{5,4},{6,5},{7,6},{9,8},{10,9},{11,10},{13,12},{... | collective-permute-start | bytes 294920 | tf_op jit(solution)/shard_map/ppermute | solution.py:293

commit v2 on v1

--- a/solution.py
+++ b/solution.py
@@ -153,31 +153,37 @@
     return layers
 
 
-def lead_kernel(totals, disp, fixed, density, solid, z_out, y_out, d_out):
-    loads, comps, zlen, ylen, _ = disp.shape
-    total_z, total_y = totals
-    base_z = lax.axis_index("sz") * zlen
-    base_y = lax.axis_index("sy") * ylen
+def lead_kernel(disp_hbm, fixed_hbm, density_hbm, solid_hbm, disp, fixed, density, solid, z_out, y_out, d_out, sems):
+    loads, comps, zlen, _, _ = disp.shape
+    copies = [
+        pltpu.make_async_copy(source, target, sems.at[k])
+        for k, (source, target) in enumerate(
+            ((disp_hbm, disp), (fixed_hbm, fixed), (density_hbm, density), (solid_hbm, solid))
+        )
+    ]
+    for copy in copies:
+        copy.start()
+    for copy in copies:
+        copy.wait()
     free = [1.0 - fixed[z].astype(jnp.float32) for z in range(zlen)]
+    d_out[...] = jnp.zeros(d_out.shape, jnp.float32)
     for case in range(loads):
         for comp in range(comps):
             k = case * comps + comp
             layer = disp[case, comp, 0] * free[0]
             z_out[k] = layer
-            d_out[ROWS * k : ROWS * (k + 1)] = layer[:ROWS]
-            y_out[k, :ROWS] = layer[:ROWS]
+            d_out[k : k + 1] = layer[:1]
+            y_out[zlen * k : zlen * k + 1] = layer[:1]
             for z in range(1, zlen):
-                y_out[k, ROWS * z : ROWS * (z + 1)] = disp[case, comp, z, :ROWS] * free[z][:ROWS]
-    for z in range(zlen):
-        factor = voxel_factor(density[z, :TILE], solid[z, :TILE], base_z + z, base_y, total_z, total_y)
-        y_out[loads * comps, ROWS * z : ROWS * (z + 1)] = factor[:ROWS]
-
-
-def energy_kernel(totals, disp, fixed, density, solid, z_in, y_in, d_in, own_out, up_out, plus, diff, factor, quotient):
+                y_out[zlen * k + z : zlen * k + z + 1] = disp[case, comp, z, :1] * free[z][:1]
+
+
+def energy_kernel(totals, disp, fixed, density, solid, z_in, y_in, d_in, own_out, a_out, b_out, plus, diff, quotient):
     loads, comps, zlen, ylen, xlen = disp.shape
     total_z, total_y = totals
+    index_y = lax.axis_index("sy")
     base_z = lax.axis_index("sz") * zlen
-    base_y = lax.axis_index("sy") * ylen
+    base_y = index_y * ylen
     weights = mode_weights()
 
     def split_x(value):
@@ -195,21 +201,24 @@
         whole, change = split_x(z_in[k])
         plus[k, zlen, :ylen] = whole
         diff[k, zlen, :ylen] = change
-        whole, change = split_x(y_in[k])
+
+    whole, change = split_x(y_in[...])
+    for k in range(loads * comps):
         for z in range(zlen):
-            plus[k, z, ylen : ylen + ROWS] = whole[ROWS * z : ROWS * (z + 1)]
-            diff[k, z, ylen : ylen + ROWS] = change[ROWS * z : ROWS * (z + 1)]
-
+            plus[k, z, ylen : ylen + 1] = whole[zlen * k + z : zlen * k + z + 1]
+            diff[k, z, ylen : ylen + 1] = change[zlen * k + z : zlen * k + z + 1]
     whole, change = split_x(d_in[...])
     for k in range(loads * comps):
-        plus[k, zlen, ylen : ylen + ROWS] = whole[ROWS * k : ROWS * (k + 1)]
-        diff[k, zlen, ylen : ylen + ROWS] = change[ROWS * k : ROWS * (k + 1)]
-
+        plus[k, zlen, ylen : ylen + 1] = whole[k : k + 1]
+        diff[k, zlen, ylen : ylen + 1] = change[k : k + 1]
+
+    zeros = jnp.zeros((TILE, xlen), jnp.float32)
     for z in range(zlen):
-        factor[z, :ylen] = voxel_factor(density[z], solid[z], base_z + z, base_y, total_z, total_y)
-        factor[z, ylen : ylen + ROWS] = y_in[loads * comps, ROWS * z : ROWS * (z + 1)]
-
-    for first in range(0, ylen + REACH, TILE):
+        quotient[z, :TILE] = zeros
+        quotient[z, TILE : TILE + ylen] = voxel_factor(density[z], solid[z], base_z + z, base_y, total_z, total_y)
+        quotient[z, TILE + ylen :] = zeros
+
+    for first in range(0, ylen, TILE):
 
         @pl.loop(0, xlen // LANES)
         def _(chunk):
@@ -230,32 +239,47 @@
                         energy[z - 1] = part if energy[z - 1] is None else energy[z - 1] + part
                     low = high
             for z in range(zlen):
-                quotient[z, first + TILE : first + 2 * TILE, lanes] = energy[z] * factor[z, first : first + TILE, lanes]
-
+                here = quotient[z, first + TILE : first + 2 * TILE, lanes]
+                quotient[z, first + TILE : first + 2 * TILE, lanes] = energy[z] * here
+
+    even = index_y % 2 == 0
     for z in range(zlen):
-        quotient[z, :TILE] = jnp.zeros((TILE, xlen), jnp.float32)
         rows = [quotient[z, TILE + step : TILE + step + ylen] for step in range(-REACH, REACH + 1)]
         own_out[z] = sum((ROWS - abs(k - REACH)) * rows[k] for k in range(2 * REACH + 1))
         top = quotient[z, ylen : ylen + TILE]
-        last = [top[TILE - 1 - k : TILE - k] for k in range(REACH)]
-        up = [
-            sum(float(REACH - row - k) * last[k] for k in range(REACH - row)) for row in range(REACH)
-        ]
-        up_out[ROWS * z : ROWS * (z + 1)] = jnp.concatenate(up + [jnp.zeros((1, xlen), jnp.float32)], axis=0)
-
-
-def rows_kernel(own, up_in, h_out, down_out, up_out):
-    zlen = own.shape[0]
+        base = quotient[z, TILE : 2 * TILE]
+        ahead, back = [], []
+        for row in range(REACH):
+            ahead.append(sum(float(REACH - row - k) * top[TILE - 1 - k : TILE - k] for k in range(REACH - row)))
+            back.append(sum(float(row + 1 - k) * base[k : k + 1] for k in range(row + 1)))
+        blank = jnp.zeros((1, xlen), jnp.float32)
+        ahead = jnp.concatenate(ahead + [blank], axis=0)
+        back = jnp.concatenate([blank] + back, axis=0)
+        a_out[ROWS * z : ROWS * (z + 1)] = jnp.where(even, ahead, back)
+        b_out[ROWS * z : ROWS * (z + 1)] = jnp.where(even, back, ahead)
+
+
+def rows_kernel(own, a_in, b_in, h_out, a_out, b_out):
+    zlen, ylen, _ = own.shape
+    even = lax.axis_index("sy") % 2 == 0
     for z in range(zlen):
+        part = slice(ROWS * z, ROWS * (z + 1))
+        from_low = jnp.where(even, b_in[part], a_in[part])
+        from_high = jnp.where(even, a_in[part], b_in[part])
         h_out[z] = own[z]
-        h_out[z, :ROWS] = own[z, :ROWS] + up_in[ROWS * z : ROWS * (z + 1)]
-    down_out[...] = h_out[:REACH]
-    up_out[...] = h_out[zlen - REACH :]
-
-
-def layers_kernel(h, below, above, out):
+        h_out[z, :ROWS] = own[z, :ROWS] + from_low
+        h_out[z, ylen - ROWS :] = own[z, ylen - ROWS :] + from_high
+    top = (zlen - REACH) * (lax.axis_index("sz") % 2 == 0).astype(jnp.int32)
+    a_out[...] = h_out[pl.ds(top, REACH)]
+    b_out[...] = h_out[pl.ds(zlen - REACH - top, REACH)]
+
+
+def layers_kernel(h, a_in, b_in, out):
     zlen = h.shape[0]
-    layers = [below[k] for k in range(REACH)] + [h[z] for z in range(zlen)] + [above[k] for k in range(REACH)]
+    even = lax.axis_index("sz") % 2 == 0
+    below = [jnp.where(even, b_in[k], a_in[k]) for k in range(REACH)]
+    above = [jnp.where(even, a_in[k], b_in[k]) for k in range(REACH)]
+    layers = below + [h[z] for z in range(zlen)] + above
     for z, layer in enumerate(spread_layers(layers)):
         out[z] = spread_x(layer)
 
@@ -264,22 +288,16 @@
     out[...] = parts[0] + parts[1]
 
 
-def vmem(count):
-    return [pl.BlockSpec(memory_space=pltpu.VMEM)] * count
-
-
-def call(kernel, outs, args, scratch=(), **kwargs):
-    shapes = [jax.ShapeDtypeStruct(shape, jnp.float32) for shape in outs]
-    result = pl.pallas_call(
+def call(kernel, outs, args, scratch=(), space=pltpu.VMEM):
+    shapes = [jax.ShapeDtypeStruct(out, jnp.float32) if isinstance(out, tuple) else out for out in outs]
+    return pl.pallas_call(
         kernel,
         out_shape=shapes,
-        in_specs=vmem(len(args)),
-        out_specs=vmem(len(outs)),
+        in_specs=[pl.BlockSpec(memory_space=space)] * len(args),
+        out_specs=[pl.BlockSpec(memory_space=pltpu.VMEM)] * len(outs),
         scratch_shapes=list(scratch),
         compiler_params=pltpu.CompilerParams(vmem_limit_bytes=32 * 1024 * 1024),
-        **kwargs,
     )(*args)
-    return result
 
 
 def moved(value, axes, steps):
@@ -293,44 +311,50 @@
     return lax.ppermute(value, axes if len(axes) > 1 else axes[0], pairs)
 
 
+def swapped(value, axis, first):
+    pairs = []
+    for low in range(first, lax.axis_size(axis) - 1, 2):
+        pairs += [(low, low + 1), (low + 1, low)]
+    return lax.ppermute(value, axis, pairs)
+
+
 def body(displacements, density, solid, fixed):
     loads, comps, zlen, ylen, xlen = displacements.shape
     planes = loads * comps
     totals = (zlen * lax.axis_size("sz"), ylen * lax.axis_size("sy"))
-
-    def bound(kernel):
-        def run(*refs):
-            kernel(totals, *refs)
-
-        return run
-
-    z_send, y_send, d_send = call(
-        bound(lead_kernel),
-        [(planes, ylen, xlen), (planes + 1, ROWS * zlen, xlen), (ROWS * planes, xlen)],
-        (displacements, fixed, density, solid),
+    args = [
+        pltpu.with_memory_space_constraint(arg, pltpu.HBM) for arg in (displacements, fixed, density, solid)
+    ]
+
+    disp, fixed, density, solid, z_send, y_send, d_send = call(
+        lead_kernel,
+        [jax.ShapeDtypeStruct(arg.shape, arg.dtype) for arg in args]
+        + [(planes, ylen, xlen), (planes * zlen, xlen), (TILE, xlen)],
+        args,
+        scratch=[pltpu.SemaphoreType.DMA((len(args),))],
+        space=pltpu.HBM,
     )
     z_in = moved(z_send, ("sz",), (1,))
     y_in = moved(y_send, ("sy",), (1,))
     d_in = moved(d_send, ("sy", "sz"), (1, 1))
-    high = ylen + 2 * TILE
-    own, up_send = call(
-        bound(energy_kernel),
-        [(zlen, ylen, xlen), (ROWS * zlen, xlen)],
-        (displacements, fixed, density, solid, z_in, y_in, d_in),
+    own, a_send, b_send = call(
+        lambda *refs: energy_kernel(totals, *refs),
+        [(zlen, ylen, xlen), (ROWS * zlen, xlen), (ROWS * zlen, xlen)],
+        (disp, fixed, density, solid, z_in, y_in, d_in),
         scratch=[
-            pltpu.VMEM((planes, zlen + 1, high, xlen), jnp.float32),
-            pltpu.VMEM((planes, zlen + 1, high, xlen), jnp.float32),
-            pltpu.VMEM((zlen, ylen + TILE, xlen), jnp.float32),
+            pltpu.VMEM((planes, zlen + 1, ylen + TILE, xlen), jnp.float32),
+            pltpu.VMEM((planes, zlen + 1, ylen + TILE, xlen), jnp.float32),
             pltpu.VMEM((zlen, ylen + 2 * TILE, xlen), jnp.float32),
         ],
     )
-    up_in = moved(up_send, ("sy",), (-1,))
-    h, down_send, over_send = call(
-        rows_kernel, [(zlen, ylen, xlen), (REACH, ylen, xlen), (REACH, ylen, xlen)], (own, up_in)
-    )
-    above = moved(down_send, ("sz",), (1,))
-    below = moved(over_send, ("sz",), (-1,))
-    (part,) = call(layers_kernel, [(zlen, ylen, xlen)], (h, below, above))
+    a_in = swapped(a_send, "sy", 0)
+    b_in = swapped(b_send, "sy", 1)
+    h, a_send, b_send = call(
+        rows_kernel, [(zlen, ylen, xlen), (REACH, ylen, xlen), (REACH, ylen, xlen)], (own, a_in, b_in)
+    )
+    a_in = swapped(a_send, "sz", 0)
+    b_in = swapped(b_send, "sz", 1)
+    (part,) = call(layers_kernel, [(zlen, ylen, xlen)], (h, a_in, b_in))
     parts = lax.all_gather(part, "load", axis=0)
     (out,) = call(sum_kernel, [(zlen, ylen, xlen)], (parts,))
     return out

time: 41.3 us -> 33.8 us (0.82)
  the two profiles are of different devices: /device:TPU:0 before, /device:TPU:21 now
where the time goes in v2:
time: 33.8 us; the launch traced here: 33.6 us
  starting transfers between devices  12.3 us (36%)
  waiting for transfers between devices  9.21 us (27%)
  blocking collectives  6.56 us (19%)
  Pallas kernels  5.38 us (16%)
    ppermute x3, starting transfers between devices, moved(): return lax.ppermute(value, axes if len(axes) > 1 else axes[0], pairs)  7.06 us
    all_gather x1, blocking collectives, body(): parts = lax.all_gather(part, 'load', axis=0)  6.56 us
    ppermute x4, waiting for transfers between devices, swapped(): return lax.ppermute(value, axis, pairs)  5.75 us
    pallas_call x5, Pallas kernels, call(): pl.pallas_call(kernel, out_shape=shapes, in_specs=[pl.BlockSpec(memory_sp...  5.38 us
    ppermute x4, starting transfers between devices, swapped(): return lax.ppermute(value, axis, pairs)  5.28 us
    ppermute x3, waiting for transfers between devices, moved(): return lax.ppermute(value, axes if len(axes) > 1 else axes[0], pairs)  3.46 us
  transfers between devices with their start and end apart: 7, of which 4 were waited for; matrix products, arithmetic and copies ran while one was open for 0% of the time, Pallas kernels for 0%

profile of v2, /device:TPU:21, one launch (start us, length us, event | category | flops | bytes accessed | tf_op | source)
XLA Modules:
  0.0 33.6 jit_solution(7340722955978090754)
XLA Ops:
  0.0 1.3 %shard_map.46 = (f32[2,3,4,16,512]{4,3,2,1,0:T(8,128)S(1)}, s32[4,16,512]{2,1,0:T(8,128)S(1)}, f32[4,16,512]{2,1,0:T(8,128)S(1)}, s32[4,16,512]{2,1,0:T(8,128)S(...) custom-call(f32[2,3,4,16,512]{4,3,2,1,0:T(8,128)} %disp_hbm.1, ...), custom_call_target="tpu_custom_call" | custom-call | tf_op jit(solution)/shard_map/pallas_call | solution.py:293
  1.3 2.1 %collective-permute-start = (f32[6,16,512]{2,1,0:T(8,128)S(1)}, f32[6,16,512]{2,1,0:T(8,128)S(1)}, u32[]{:S(2)}, u32[]{:S(2)}) collective-permute-start(f32[6,16,512]{2,1,0:T(8,128)S(1)} %get-tuple-element.22), channel_id=1, source_target_pairs={{1,0},{2,1},{3,2},{5,4},{6,5},{7,6},{9,8},{10,9},{11,10},{13,12},{... | collective-permute-start | bytes 589832 | tf_op jit(solution)/shard_map/ppermute | solution.py:311
  3.4 3.1 %collective-permute-start.1 = (f32[24,512]{1,0:T(8,128)S(1)}, f32[24,512]{1,0:T(8,128)S(1)}, u32[]{:S(2)}, u32[]{:S(2)}) collective-permute-start(f32[24,512]{1,0:T(8,128)S(1)} %get-tuple-element.23), channel_id=1, source_target_pairs={{4,0},{8,4},{12,8},{5,1},{9,5},{13,9},{6,2},{10,6},{14,10},{7,3},{... | collective-permute-start | bytes 147464 | tf_op jit(solution)/shard_map/ppermute | solution.py:311
  6.4 1.9 %collective-permute-start.2 = (f32[8,512]{1,0:T(8,128)S(1)}, f32[8,512]{1,0:T(8,128)S(1)}, u32[]{:S(2)}, u32[]{:S(2)}) collective-permute-start(f32[8,512]{1,0:T(8,128)S(1)} %get-tuple-element.24), channel_id=1, source_target_pairs={{5,0},{6,1},{7,2},{9,4},{10,5},{11,6},{13,8},{14,9},{15,10},{21,16... | collective-permute-start | bytes 49160 | tf_op jit(solution)/shard_map/ppermute | solution.py:311
  8.4 3.5 %collective-permute-done.2.refs_6_ = f32[8,512]{1,0:T(8,128)S(1)} collective-permute-done((f32[8,512]{1,0:T(8,128)S(1)}, f32[8,512]{1,0:T(8,128)S(1)}, u32[]{:S(2)}, u32[]{:S(2)}) %collective-permute-start.2) | collective-permute-done | bytes 16416 | tf_op jit(solution)/shard_map/ppermute | solution.py:311
  11.8 0.0 collective-permute-done.1.refs_5_
  11.8 0.0 collective-permute-done.refs_4_
  11.8 3.0 %shard_map.47 = (f32[4,16,512]{2,1,0:T(8,128)S(1)}, f32[16,512]{1,0:T(8,128)S(1)}, f32[16,512]{1,0:T(8,128)S(1)}) custom-call(f32[2,3,4,16,512]{4,3,2,1,0:T(8,128)S(1)} %get-tuple-element.18.refs_0_, s32[4,16,512]{2,1,0:T(8,128)S(1)} %get-tuple-element.19.refs_1_, f32[4,16,512]{2,1,0:T(8,128)S(1)} %get-tuple-element.20.refs_2_, ...), custom_call_target="tpu_custom_call" | custom-call | tf_op jit(solution)/shard_map/pallas_call | solution.py:293
  14.9 0.1 collective-permute-start.3
  14.9 3.1 %collective-permute-start.4 = (f32[16,512]{1,0:T(8,128)S(1)}, f32[16,512]{1,0:T(8,128)S(1)}, u32[]{:S(2)}, u32[]{:S(2)}) collective-permute-start(f32[16,512]{1,0:T(8,128)S(1)} %get-tuple-element.27), channel_id=1, source_target_pairs={{4,8},{8,4},{5,9},{9,5},{6,10},{10,6},{7,11},{11,7},{20,24},{24,20... | collective-permute-start | bytes 98312 | tf_op jit(solution)/shard_map/ppermute | solution.py:318
  18.0 0.0 collective-permute-done.3.a_in
  18.0 2.5 %collective-permute-done.4.b_in = f32[16,512]{1,0:T(8,128)S(1)} collective-permute-done((f32[16,512]{1,0:T(8,128)S(1)}, f32[16,512]{1,0:T(8,128)S(1)}, u32[]{:S(2)}, u32[]{:S(2)}) %collective-permute-start.4) | collective-permute-done | bytes 32800 | tf_op jit(solution)/shard_map/ppermute | solution.py:318
  20.5 0.1 collective-permute-start.5
  20.6 2.1 %collective-permute-start.6 = (f32[3,16,512]{2,1,0:T(8,128)S(1)}, f32[3,16,512]{2,1,0:T(8,128)S(1)}, u32[]{:S(2)}, u32[]{:S(2)}) collective-permute-start(f32[3,16,512]{2,1,0:T(8,128)S(1)} %get-tuple-element.30), channel_id=1, source_target_pairs={{1,2},{2,1},{5,6},{6,5},{9,10},{10,9},{13,14},{14,13},{17,18},{18,... | collective-permute-start | bytes 294920 | tf_op jit(solution)/shard_map/ppermute | solution.py:318
  22.7 1.4 %collective-permute-done.5.a_in = f32[3,16,512]{2,1,0:T(8,128)S(1)} collective-permute-done((f32[3,16,512]{2,1,0:T(8,128)S(1)}, f32[3,16,512]{2,1,0:T(8,128)S(1)}, u32[]{:S(2)}, u32[]{:S(2)}) %collective-permute-start.5) | collective-permute-done | bytes 98336 | tf_op jit(solution)/shard_map/ppermute | solution.py:318
  24.1 1.9 %collective-permute-done.6.b_in = f32[3,16,512]{2,1,0:T(8,128)S(1)} collective-permute-done((f32[3,16,512]{2,1,0:T(8,128)S(1)}, f32[3,16,512]{2,1,0:T(8,128)S(1)}, u32[]{:S(2)}, u32[]{:S(2)}) %collective-permute-start.6) | collective-permute-done | bytes 98336 | tf_op jit(solution)/shard_map/ppermute | solution.py:318
  26.0 0.4 %shard_map.49 = f32[4,16,512]{2,1,0:T(8,128)S(1)} custom-call(f32[4,16,512]{2,1,0:T(8,128)S(1)} %get-tuple-element.28.h, f32[3,16,512]{2,1,0:T(8,128)S(1)} %collective-permute-done.5.a_in, f32[3,16,512]{2,1,0:T(8,128)S(1)} %collective-permute-done.6.b_in), custom_call_target="tpu_custom_call" | custom-call | tf_op jit(solution)/shard_map/pallas_call | solution.py:293
  26.4 6.6 %all-gather = f32[8,16,512]{2,1,0:T(8,128)S(1)} all-gather(f32[4,16,512]{2,1,0:T(8,128)S(1)} %shard_map.49), channel_id=2, replica_groups=mesh['load'=2,'sy'=4,'sz'=4] {'load'}, dimensions={0}, use_global_device_ids=true | all-gather | bytes 393216 | tf_op jit(solution)/shard_map/all_gather | solution.py:358
  32.9 0.7 %shard_map.50 = f32[4,16,512]{2,1,0:T(8,128)} custom-call(f32[2,4,16,512]{3,2,1,0:T(8,128)S(1)} %bitcast.1), custom_call_target="tpu_custom_call" | custom-call | tf_op jit(solution)/shard_map/pallas_call | solution.py:293
  (1 shorter events, 0.0 us)
Async XLA Ops:
  1.3 10.5 %collective-permute-start = (f32[6,16,512]{2,1,0:T(8,128)S(1)}, f32[6,16,512]{2,1,0:T(8,128)S(1)}, u32[]{:S(2)}, u32[]{:S(2)}) collective-permute-start(f32[6,16,512]{2,1,0:T(8,128)S(1)} %get-tuple-element.22), channel_id=1, source_target_pairs={{1,0},{2,1},{3,2},{5,4},{6,5},{7,6},{9,8},{10,9},{11,10},{13,12},{... | collective-permute-start | bytes 589832 | tf_op jit(solution)/shard_map/ppermute | solution.py:311
  3.4 8.5 %collective-permute-start.1 = (f32[24,512]{1,0:T(8,128)S(1)}, f32[24,512]{1,0:T(8,128)S(1)}, u32[]{:S(2)}, u32[]{:S(2)}) collective-permute-start(f32[24,512]{1,0:T(8,128)S(1)} %get-tuple-element.23), channel_id=1, source_target_pairs={{4,0},{8,4},{12,8},{5,1},{9,5},{13,9},{6,2},{10,6},{14,10},{7,3},{... | collective-permute-start | bytes 147464 | tf_op jit(solution)/shard_map/ppermute | solution.py:311
  6.4 5.4 %collective-permute-start.2 = (f32[8,512]{1,0:T(8,128)S(1)}, f32[8,512]{1,0:T(8,128)S(1)}, u32[]{:S(2)}, u32[]{:S(2)}) collective-permute-start(f32[8,512]{1,0:T(8,128)S(1)} %get-tuple-element.24), channel_id=1, source_target_pairs={{5,0},{6,1},{7,2},{9,4},{10,5},{11,6},{13,8},{14,9},{15,10},{21,16... | collective-permute-start | bytes 49160 | tf_op jit(solution)/shard_map/ppermute | solution.py:311
  14.9 3.2 %collective-permute-start.3 = (f32[16,512]{1,0:T(8,128)S(1)}, f32[16,512]{1,0:T(8,128)S(1)}, u32[]{:S(2)}, u32[]{:S(2)}) collective-permute-start(f32[16,512]{1,0:T(8,128)S(1)} %get-tuple-element.26), channel_id=1, source_target_pairs={{0,4},{4,0},{8,12},{12,8},{1,5},{5,1},{9,13},{13,9},{2,6},{6,2},{1... | collective-permute-start | bytes 98312 | tf_op jit(solution)/shard_map/ppermute | solution.py:318
  14.9 5.6 %collective-permute-start.4 = (f32[16,512]{1,0:T(8,128)S(1)}, f32[16,512]{1,0:T(8,128)S(1)}, u32[]{:S(2)}, u32[]{:S(2)}) collective-permute-start(f32[16,512]{1,0:T(8,128)S(1)} %get-tuple-element.27), channel_id=1, source_target_pairs={{4,8},{8,4},{5,9},{9,5},{6,10},{10,6},{7,11},{11,7},{20,24},{24,20... | collective-permute-start | bytes 98312 | tf_op jit(solution)/shard_map/ppermute | solution.py:318
  20.5 3.5 %collective-permute-start.5 = (f32[3,16,512]{2,1,0:T(8,128)S(1)}, f32[3,16,512]{2,1,0:T(8,128)S(1)}, u32[]{:S(2)}, u32[]{:S(2)}) collective-permute-start(f32[3,16,512]{2,1,0:T(8,128)S(1)} %get-tuple-element.29), channel_id=1, source_target_pairs={{0,1},{1,0},{2,3},{3,2},{4,5},{5,4},{6,7},{7,6},{8,9},{9,8},{10,11... | collective-permute-start | bytes 294920 | tf_op jit(solution)/shard_map/ppermute | solution.py:318
  20.6 5.4 %collective-permute-start.6 = (f32[3,16,512]{2,1,0:T(8,128)S(1)}, f32[3,16,512]{2,1,0:T(8,128)S(1)}, u32[]{:S(2)}, u32[]{:S(2)}) collective-permute-start(f32[3,16,512]{2,1,0:T(8,128)S(1)} %get-tuple-element.30), channel_id=1, source_target_pairs={{1,2},{2,1},{5,6},{6,5},{9,10},{10,9},{13,14},{14,13},{17,18},{18,... | collective-permute-start | bytes 294920 | tf_op jit(solution)/shard_map/ppermute | solution.py:318

commit v3 on v2

--- a/solution.py
+++ b/solution.py
@@ -178,7 +178,7 @@
                 y_out[zlen * k + z : zlen * k + z + 1] = disp[case, comp, z, :1] * free[z][:1]
 
 
-def energy_kernel(totals, disp, fixed, density, solid, z_in, y_in, d_in, own_out, a_out, b_out, plus, diff, quotient):
+def energy_kernel(totals, disp, fixed, density, solid, z_in, y_in, d_in, own_out, ends_out, plus, diff, quotient):
     loads, comps, zlen, ylen, xlen = disp.shape
     total_z, total_y = totals
     index_y = lax.axis_index("sy")
@@ -242,7 +242,6 @@
                 here = quotient[z, first + TILE : first + 2 * TILE, lanes]
                 quotient[z, first + TILE : first + 2 * TILE, lanes] = energy[z] * here
 
-    even = index_y % 2 == 0
     for z in range(zlen):
         rows = [quotient[z, TILE + step : TILE + step + ylen] for step in range(-REACH, REACH + 1)]
         own_out[z] = sum((ROWS - abs(k - REACH)) * rows[k] for k in range(2 * REACH + 1))
@@ -253,19 +252,19 @@
             ahead.append(sum(float(REACH - row - k) * top[TILE - 1 - k : TILE - k] for k in range(REACH - row)))
             back.append(sum(float(row + 1 - k) * base[k : k + 1] for k in range(row + 1)))
         blank = jnp.zeros((1, xlen), jnp.float32)
-        ahead = jnp.concatenate(ahead + [blank], axis=0)
-        back = jnp.concatenate([blank] + back, axis=0)
-        a_out[ROWS * z : ROWS * (z + 1)] = jnp.where(even, ahead, back)
-        b_out[ROWS * z : ROWS * (z + 1)] = jnp.where(even, back, ahead)
-
-
-def rows_kernel(own, a_in, b_in, h_out, a_out, b_out):
+        ends_out[0, ROWS * z : ROWS * (z + 1)] = jnp.concatenate(ahead + [blank], axis=0)
+        ends_out[1, ROWS * z : ROWS * (z + 1)] = jnp.concatenate([blank] + back, axis=0)
+
+
+def rows_kernel(own, ends, h_out, a_out, b_out):
     zlen, ylen, _ = own.shape
-    even = lax.axis_index("sy") % 2 == 0
+    index = lax.axis_index("sy")
+    last = ends.shape[0] - 1
+    low, high = jnp.maximum(index - 1, 0), jnp.minimum(index + 1, last)
     for z in range(zlen):
         part = slice(ROWS * z, ROWS * (z + 1))
-        from_low = jnp.where(even, b_in[part], a_in[part])
-        from_high = jnp.where(even, a_in[part], b_in[part])
+        from_low = jnp.where(index > 0, ends[low, 0, part], 0.0)
+        from_high = jnp.where(index < last, ends[high, 1, part], 0.0)
         h_out[z] = own[z]
         h_out[z, :ROWS] = own[z, :ROWS] + from_low
         h_out[z, ylen - ROWS :] = own[z, ylen - ROWS :] + from_high
@@ -337,9 +336,9 @@
     z_in = moved(z_send, ("sz",), (1,))
     y_in = moved(y_send, ("sy",), (1,))
     d_in = moved(d_send, ("sy", "sz"), (1, 1))
-    own, a_send, b_send = call(
+    own, ends = call(
         lambda *refs: energy_kernel(totals, *refs),
-        [(zlen, ylen, xlen), (ROWS * zlen, xlen), (ROWS * zlen, xlen)],
+        [(zlen, ylen, xlen), (2, ROWS * zlen, xlen)],
         (disp, fixed, density, solid, z_in, y_in, d_in),
         scratch=[
             pltpu.VMEM((planes, zlen + 1, ylen + TILE, xlen), jnp.float32),
@@ -347,11 +346,8 @@
             pltpu.VMEM((zlen, ylen + 2 * TILE, xlen), jnp.float32),
         ],
     )
-    a_in = swapped(a_send, "sy", 0)
-    b_in = swapped(b_send, "sy", 1)
-    h, a_send, b_send = call(
-        rows_kernel, [(zlen, ylen, xlen), (REACH, ylen, xlen), (REACH, ylen, xlen)], (own, a_in, b_in)
-    )
+    ends = lax.all_gather(ends, "sy", axis=0)
+    h, a_send, b_send = call(rows_kernel, [(zlen, ylen, xlen), (REACH, ylen, xlen), (REACH, ylen, xlen)], (own, ends))
     a_in = swapped(a_send, "sz", 0)
     b_in = swapped(b_send, "sz", 1)
     (part,) = call(layers_kernel, [(zlen, ylen, xlen)], (h, a_in, b_in))

time: 33.8 us -> 35.8 us (1.059)
  the two profiles are of different devices: /device:TPU:21 before, /device:TPU:9 now
where the time goes in v3:
time: 35.8 us; the launch traced here: 35.6 us
  blocking collectives  15.1 us (42%)
  starting transfers between devices  7.78 us (22%)
  waiting for transfers between devices  7.25 us (20%)
  Pallas kernels  5.38 us (15%)
    all_gather x1, blocking collectives, body(): ends = lax.all_gather(ends, 'sy', axis=0)  8.03 us
    all_gather x1, blocking collectives, body(): parts = lax.all_gather(part, 'load', axis=0)  7.05 us
    pallas_call x5, Pallas kernels, call(): pl.pallas_call(kernel, out_shape=shapes, in_specs=[pl.BlockSpec(memory_sp...  5.38 us
    ppermute x3, waiting for transfers between devices, moved(): return lax.ppermute(value, axes if len(axes) > 1 else axes[0], pairs)  5.1 us
    ppermute x3, starting transfers between devices, moved(): return lax.ppermute(value, axes if len(axes) > 1 else axes[0], pairs)  4.5 us
    ppermute x2, starting transfers between devices, swapped(): return lax.ppermute(value, axis, pairs)  3.28 us
    ppermute x2, waiting for transfers between devices, swapped(): return lax.ppermute(value, axis, pairs)  2.15 us
  transfers between devices with their start and end apart: 5, of which 3 were waited for; matrix products, arithmetic and copies ran while one was open for 0% of the time, Pallas kernels for 0%

profile of v3, /device:TPU:9, one launch (start us, length us, event | category | flops | bytes accessed | tf_op | source)
XLA Modules:
  0.0 35.6 jit_solution(1769427597567072466)
XLA Ops:
  0.0 1.3 %shard_map.46 = (f32[2,3,4,16,512]{4,3,2,1,0:T(8,128)S(1)}, s32[4,16,512]{2,1,0:T(8,128)S(1)}, f32[4,16,512]{2,1,0:T(8,128)S(1)}, s32[4,16,512]{2,1,0:T(8,128)S(...) custom-call(f32[2,3,4,16,512]{4,3,2,1,0:T(8,128)} %disp_hbm.1, ...), custom_call_target="tpu_custom_call" | custom-call | tf_op jit(solution)/shard_map/pallas_call | solution.py:292
  1.3 1.9 %collective-permute-start = (f32[6,16,512]{2,1,0:T(8,128)S(1)}, f32[6,16,512]{2,1,0:T(8,128)S(1)}, u32[]{:S(2)}, u32[]{:S(2)}) collective-permute-start(f32[6,16,512]{2,1,0:T(8,128)S(1)} %get-tuple-element.21), channel_id=1, source_target_pairs={{1,0},{2,1},{3,2},{5,4},{6,5},{7,6},{9,8},{10,9},{11,10},{13,12},{... | collective-permute-start | bytes 589832 | tf_op jit(solution)/shard_map/ppermute | solution.py:310
  3.2 1.3 %collective-permute-start.1 = (f32[24,512]{1,0:T(8,128)S(1)}, f32[24,512]{1,0:T(8,128)S(1)}, u32[]{:S(2)}, u32[]{:S(2)}) collective-permute-start(f32[24,512]{1,0:T(8,128)S(1)} %get-tuple-element.22), channel_id=1, source_target_pairs={{4,0},{8,4},{12,8},{5,1},{9,5},{13,9},{6,2},{10,6},{14,10},{7,3},{... | collective-permute-start | bytes 147464 | tf_op jit(solution)/shard_map/ppermute | solution.py:310
  4.5 1.3 %collective-permute-start.2 = (f32[8,512]{1,0:T(8,128)S(1)}, f32[8,512]{1,0:T(8,128)S(1)}, u32[]{:S(2)}, u32[]{:S(2)}) collective-permute-start(f32[8,512]{1,0:T(8,128)S(1)} %get-tuple-element.23), channel_id=1, source_target_pairs={{5,0},{6,1},{7,2},{9,4},{10,5},{11,6},{13,8},{14,9},{15,10},{21,16... | collective-permute-start | bytes 49160 | tf_op jit(solution)/shard_map/ppermute | solution.py:310
  5.8 5.1 %collective-permute-done.2.refs_6_ = f32[8,512]{1,0:T(8,128)S(1)} collective-permute-done((f32[8,512]{1,0:T(8,128)S(1)}, f32[8,512]{1,0:T(8,128)S(1)}, u32[]{:S(2)}, u32[]{:S(2)}) %collective-permute-start.2) | collective-permute-done | bytes 16416 | tf_op jit(solution)/shard_map/ppermute | solution.py:310
  10.9 0.0 collective-permute-done.1.refs_5_
  10.9 0.0 collective-permute-done.refs_4_
  10.9 3.0 %shard_map.47 = (f32[4,16,512]{2,1,0:T(8,128)S(1)}, f32[2,16,512]{2,1,0:T(8,128)S(1)}) custom-call(f32[2,3,4,16,512]{4,3,2,1,0:T(8,128)S(1)} %get-tuple-element.17.refs_0_, s32[4,16,512]{2,1,0:T(8,128)S(1)} %get-tuple-element.18.refs_1_, f32[4,16,512]{2,1,0:T(8,128)S(1)} %get-tuple-element.19.refs_2_, s32[4,16,512]{2,1,0:T(8,128)S(1)} %get-tuple-element.20.refs_3_, ...), custom_call_target="tpu_custom_call" | custom-call | tf_op jit(solution)/shard_map/pallas_call | solution.py:292
  13.9 8.0 %all-gather = f32[8,16,512]{2,1,0:T(8,128)S(1)} all-gather(f32[2,16,512]{2,1,0:T(8,128)S(1)} %get-tuple-element.25), channel_id=2, replica_groups=mesh['load'=2,'sy'=4,'sz'=4] {'sy'}, dimensions={0}, use_global_device_ids=true | all-gather | bytes 327680 | tf_op jit(solution)/shard_map/all_gather | solution.py:349
  22.0 0.1 collective-permute-start.3
  22.1 3.2 %collective-permute-start.4 = (f32[3,16,512]{2,1,0:T(8,128)S(1)}, f32[3,16,512]{2,1,0:T(8,128)S(1)}, u32[]{:S(2)}, u32[]{:S(2)}) collective-permute-start(f32[3,16,512]{2,1,0:T(8,128)S(1)} %get-tuple-element.28), channel_id=1, source_target_pairs={{1,2},{2,1},{5,6},{6,5},{9,10},{10,9},{13,14},{14,13},{17,18},{18,... | collective-permute-start | bytes 294920 | tf_op jit(solution)/shard_map/ppermute | solution.py:317
  25.3 0.5 %collective-permute-done.3.a_in = f32[3,16,512]{2,1,0:T(8,128)S(1)} collective-permute-done((f32[3,16,512]{2,1,0:T(8,128)S(1)}, f32[3,16,512]{2,1,0:T(8,128)S(1)}, u32[]{:S(2)}, u32[]{:S(2)}) %collective-permute-start.3) | collective-permute-done | bytes 98336 | tf_op jit(solution)/shard_map/ppermute | solution.py:317
  25.8 1.6 %collective-permute-done.4.b_in = f32[3,16,512]{2,1,0:T(8,128)S(1)} collective-permute-done((f32[3,16,512]{2,1,0:T(8,128)S(1)}, f32[3,16,512]{2,1,0:T(8,128)S(1)}, u32[]{:S(2)}, u32[]{:S(2)}) %collective-permute-start.4) | collective-permute-done | bytes 98336 | tf_op jit(solution)/shard_map/ppermute | solution.py:317
  27.5 0.4 %shard_map.49 = f32[4,16,512]{2,1,0:T(8,128)S(1)} custom-call(f32[4,16,512]{2,1,0:T(8,128)S(1)} %get-tuple-element.26.h, f32[3,16,512]{2,1,0:T(8,128)S(1)} %collective-permute-done.3.a_in, f32[3,16,512]{2,1,0:T(8,128)S(1)} %collective-permute-done.4.b_in), custom_call_target="tpu_custom_call" | custom-call | tf_op jit(solution)/shard_map/pallas_call | solution.py:292
  27.8 7.1 %all-gather.1 = f32[8,16,512]{2,1,0:T(8,128)S(1)} all-gather(f32[4,16,512]{2,1,0:T(8,128)S(1)} %shard_map.49), channel_id=3, replica_groups=mesh['load'=2,'sy'=4,'sz'=4] {'load'}, dimensions={0}, use_global_device_ids=true | all-gather | bytes 393216 | tf_op jit(solution)/shard_map/all_gather | solution.py:354
  34.9 0.7 %shard_map.50 = f32[4,16,512]{2,1,0:T(8,128)} custom-call(f32[2,4,16,512]{3,2,1,0:T(8,128)S(1)} %bitcast.3), custom_call_target="tpu_custom_call" | custom-call | tf_op jit(solution)/shard_map/pallas_call | solution.py:292
  (1 shorter events, 0.0 us)
Async XLA Ops:
  1.3 9.6 %collective-permute-start = (f32[6,16,512]{2,1,0:T(8,128)S(1)}, f32[6,16,512]{2,1,0:T(8,128)S(1)}, u32[]{:S(2)}, u32[]{:S(2)}) collective-permute-start(f32[6,16,512]{2,1,0:T(8,128)S(1)} %get-tuple-element.21), channel_id=1, source_target_pairs={{1,0},{2,1},{3,2},{5,4},{6,5},{7,6},{9,8},{10,9},{11,10},{13,12},{... | collective-permute-start | bytes 589832 | tf_op jit(solution)/shard_map/ppermute | solution.py:310
  3.2 7.7 %collective-permute-start.1 = (f32[24,512]{1,0:T(8,128)S(1)}, f32[24,512]{1,0:T(8,128)S(1)}, u32[]{:S(2)}, u32[]{:S(2)}) collective-permute-start(f32[24,512]{1,0:T(8,128)S(1)} %get-tuple-element.22), channel_id=1, source_target_pairs={{4,0},{8,4},{12,8},{5,1},{9,5},{13,9},{6,2},{10,6},{14,10},{7,3},{... | collective-permute-start | bytes 147464 | tf_op jit(solution)/shard_map/ppermute | solution.py:310
  4.5 6.4 %collective-permute-start.2 = (f32[8,512]{1,0:T(8,128)S(1)}, f32[8,512]{1,0:T(8,128)S(1)}, u32[]{:S(2)}, u32[]{:S(2)}) collective-permute-start(f32[8,512]{1,0:T(8,128)S(1)} %get-tuple-element.23), channel_id=1, source_target_pairs={{5,0},{6,1},{7,2},{9,4},{10,5},{11,6},{13,8},{14,9},{15,10},{21,16... | collective-permute-start | bytes 49160 | tf_op jit(solution)/shard_map/ppermute | solution.py:310
  22.0 3.8 %collective-permute-start.3 = (f32[3,16,512]{2,1,0:T(8,128)S(1)}, f32[3,16,512]{2,1,0:T(8,128)S(1)}, u32[]{:S(2)}, u32[]{:S(2)}) collective-permute-start(f32[3,16,512]{2,1,0:T(8,128)S(1)} %get-tuple-element.27), channel_id=1, source_target_pairs={{0,1},{1,0},{2,3},{3,2},{4,5},{5,4},{6,7},{7,6},{8,9},{9,8},{10,11... | collective-permute-start | bytes 294920 | tf_op jit(solution)/shard_map/ppermute | solution.py:317
  22.1 5.4 %collective-permute-start.4 = (f32[3,16,512]{2,1,0:T(8,128)S(1)}, f32[3,16,512]{2,1,0:T(8,128)S(1)}, u32[]{:S(2)}, u32[]{:S(2)}) collective-permute-start(f32[3,16,512]{2,1,0:T(8,128)S(1)} %get-tuple-element.28), channel_id=1, source_target_pairs={{1,2},{2,1},{5,6},{6,5},{9,10},{10,9},{13,14},{14,13},{17,18},{18,... | collective-permute-start | bytes 294920 | tf_op jit(solution)/shard_map/ppermute | solution.py:317

commit v4 on v2

--- a/solution.py
+++ b/solution.py
@@ -153,8 +153,34 @@
     return layers
 
 
-def lead_kernel(disp_hbm, fixed_hbm, density_hbm, solid_hbm, disp, fixed, density, solid, z_out, y_out, d_out, sems):
-    loads, comps, zlen, _, _ = disp.shape
+def held(disp, fixed, case, comp, z, rows):
+    return disp[case, comp, z, rows] * (1.0 - fixed[z, rows].astype(jnp.float32))
+
+
+def split_x(value):
+    length = value.shape[1]
+    column = lax.broadcasted_iota(jnp.int32, value.shape, 1)
+    ahead = jnp.where(column == length - 1, 0.0, pltpu.roll(value, length - 1, 1))
+    return value + ahead, ahead - value
+
+
+def spread_y(quotient, ylen):
+    rows = [quotient[TILE + step : TILE + step + ylen] for step in range(-REACH, REACH + 1)]
+    return sum((ROWS - abs(k - REACH)) * rows[k] for k in range(2 * REACH + 1))
+
+
+def to_neighbours(quotient, ylen):
+    top = quotient[ylen : ylen + TILE]
+    base = quotient[TILE : 2 * TILE]
+    ahead, back = [], []
+    for row in range(REACH):
+        ahead.append(sum(float(REACH - row - k) * top[TILE - 1 - k : TILE - k] for k in range(REACH - row)))
+        back.append(sum(float(row + 1 - k) * base[k : k + 1] for k in range(row + 1)))
+    return ahead, back
+
+
+def lead_kernel(disp_hbm, fixed_hbm, density_hbm, solid_hbm, disp, fixed, density, solid, z_out, sems):
+    loads, comps, _, _, _ = disp.shape
     copies = [
         pltpu.make_async_copy(source, target, sems.at[k])
         for k, (source, target) in enumerate(
@@ -165,110 +191,185 @@
         copy.start()
     for copy in copies:
         copy.wait()
-    free = [1.0 - fixed[z].astype(jnp.float32) for z in range(zlen)]
-    d_out[...] = jnp.zeros(d_out.shape, jnp.float32)
     for case in range(loads):
         for comp in range(comps):
-            k = case * comps + comp
-            layer = disp[case, comp, 0] * free[0]
-            z_out[k] = layer
-            d_out[k : k + 1] = layer[:1]
-            y_out[zlen * k : zlen * k + 1] = layer[:1]
-            for z in range(1, zlen):
-                y_out[zlen * k + z : zlen * k + z + 1] = disp[case, comp, z, :1] * free[z][:1]
-
-
-def energy_kernel(totals, disp, fixed, density, solid, z_in, y_in, d_in, own_out, a_out, b_out, plus, diff, quotient):
+            z_out[case * comps + comp] = held(disp, fixed, case, comp, 0, slice(None))
+
+
+def tile_energies(plus, diff, first, lanes, layers, loads, comps):
+    weights = mode_weights()
+
+    def faces(k, z):
+        near, far = slice(first, first + TILE), slice(first + 1, first + TILE + 1)
+        whole, whole_next = plus[k, z, near, lanes], plus[k, z, far, lanes]
+        change, change_next = diff[k, z, near, lanes], diff[k, z, far, lanes]
+        return whole + whole_next, change + change_next, whole_next - whole, change_next - change
+
+    energy = [None] * layers
+    for case in range(loads):
+        low = None
+        for z in range(layers + 1):
+            high = [faces(case * comps + comp, z) for comp in range(comps)]
+            if low is not None:
+                part = quadratic(low, high, weights)
+                energy[z - 1] = part if energy[z - 1] is None else energy[z - 1] + part
+            low = high
+    return energy
+
+
+def blank_last(value, first, ylen):
+    row = lax.broadcasted_iota(jnp.int32, value.shape, 0) + first
+    return jnp.where(row == ylen - 1, 0.0, value)
+
+
+def inner_kernel(totals, disp, fixed, density, solid, own, lines, sends, last_plus, last_diff, last_factor, plus, diff, quotient):
     loads, comps, zlen, ylen, xlen = disp.shape
     total_z, total_y = totals
-    index_y = lax.axis_index("sy")
     base_z = lax.axis_index("sz") * zlen
-    base_y = index_y * ylen
-    weights = mode_weights()
-
-    def split_x(value):
-        column = lax.broadcasted_iota(jnp.int32, value.shape, 1)
-        ahead = jnp.where(column == xlen - 1, 0.0, pltpu.roll(value, xlen - 1, 1))
-        return value + ahead, ahead - value
+    base_y = lax.axis_index("sy") * ylen
+    inner = zlen - 1
 
     @pl.loop(0, loads * comps)
     def _(k):
         case, comp = k // comps, k % comps
         for z in range(zlen):
-            whole, change = split_x(disp[case, comp, z] * (1.0 - fixed[z].astype(jnp.float32)))
+            whole, change = split_x(held(disp, fixed, case, comp, z, slice(None)))
             plus[k, z, :ylen] = whole
             diff[k, z, :ylen] = change
-        whole, change = split_x(z_in[k])
-        plus[k, zlen, :ylen] = whole
-        diff[k, zlen, :ylen] = change
-
-    whole, change = split_x(y_in[...])
-    for k in range(loads * comps):
-        for z in range(zlen):
-            plus[k, z, ylen : ylen + 1] = whole[zlen * k + z : zlen * k + z + 1]
-            diff[k, z, ylen : ylen + 1] = change[zlen * k + z : zlen * k + z + 1]
-    whole, change = split_x(d_in[...])
-    for k in range(loads * comps):
-        plus[k, zlen, ylen : ylen + 1] = whole[k : k + 1]
-        diff[k, zlen, ylen : ylen + 1] = change[k : k + 1]
+        last_plus[k] = whole
+        last_diff[k] = change
+
+    for comp in range(comps):
+        for case in range(loads):
+            for z in range(zlen):
+                at = (comp * loads + case) * zlen + z
+                lines[0, at : at + 1] = held(disp, fixed, case, comp, z, slice(0, 1))
+                lines[1, at : at + 1] = held(disp, fixed, case, comp, z, slice(ylen - 1, ylen))
 
     zeros = jnp.zeros((TILE, xlen), jnp.float32)
     for z in range(zlen):
-        quotient[z, :TILE] = zeros
-        quotient[z, TILE : TILE + ylen] = voxel_factor(density[z], solid[z], base_z + z, base_y, total_z, total_y)
-        quotient[z, TILE + ylen :] = zeros
+        factor = voxel_factor(density[z], solid[z], base_z + z, base_y, total_z, total_y)
+        sends[0, ROWS * z + REACH : ROWS * (z + 1)] = factor[ylen - 1 :]
+        sends[1, ROWS * z : ROWS * z + 1] = zeros[:1]
+        if z == inner:
+            last_factor[...] = factor
+        else:
+            quotient[z, :TILE] = zeros
+            quotient[z, TILE : TILE + ylen] = factor
+            quotient[z, TILE + ylen :] = zeros
 
     for first in range(0, ylen, TILE):
 
         @pl.loop(0, xlen // LANES)
         def _(chunk):
             lanes = pl.ds(pl.multiple_of(chunk * LANES, LANES), LANES)
-
-            def faces(k, z):
-                whole, whole_next = plus[k, z, first : first + TILE, lanes], plus[k, z, first + 1 : first + TILE + 1, lanes]
-                change, change_next = diff[k, z, first : first + TILE, lanes], diff[k, z, first + 1 : first + TILE + 1, lanes]
-                return whole + whole_next, change + change_next, whole_next - whole, change_next - change
-
-            energy = [None] * zlen
+            energy = tile_energies(plus, diff, first, lanes, inner, loads, comps)
+            for z in range(inner):
+                here = quotient[z, first + TILE : first + 2 * TILE, lanes]
+                quotient[z, first + TILE : first + 2 * TILE, lanes] = blank_last(energy[z] * here, first, ylen)
+
+    for z in range(inner):
+        own[z] = spread_x(spread_y(quotient.at[z], ylen))
+        ahead, back = to_neighbours(quotient.at[z], ylen)
+        ends = spread_x(jnp.concatenate(ahead + back + [zeros[:2]], axis=0))
+        sends[0, ROWS * z : ROWS * z + REACH] = ends[:REACH]
+        sends[1, ROWS * z + 1 : ROWS * (z + 1)] = ends[REACH : 2 * REACH]
+
+
+def outer_kernel(
+    shape, z_in, own_in, lines_in, sends_in, last_plus, last_diff, last_factor, own, lines, a_out, b_out, plus, diff, quotient
+):
+    loads, comps, zlen, ylen, xlen = shape
+    planes = loads * comps
+    for k in range(planes):
+        plus[k, 0, :ylen] = last_plus[k]
+        diff[k, 0, :ylen] = last_diff[k]
+        whole, change = split_x(z_in[k])
+        plus[k, 1, :ylen] = whole
+        diff[k, 1, :ylen] = change
+
+    zeros = jnp.zeros((TILE, xlen), jnp.float32)
+    quotient[:TILE] = zeros
+    quotient[TILE + ylen :] = zeros
+    for first in range(0, ylen, TILE):
+
+        @pl.loop(0, xlen // LANES)
+        def _(chunk):
+            lanes = pl.ds(pl.multiple_of(chunk * LANES, LANES), LANES)
+            (energy,) = tile_energies(plus, diff, first, lanes, 1, loads, comps)
+            here = energy * last_factor[first : first + TILE, lanes]
+            quotient[first + TILE : first + 2 * TILE, lanes] = blank_last(here, first, ylen)
+
+    own[: zlen - 1] = own_in[: zlen - 1]
+    own[zlen - 1] = spread_x(spread_y(quotient, ylen))
+    ahead, back = to_neighbours(quotient, ylen)
+    ends = spread_x(jnp.concatenate(ahead + back + [zeros[:2]], axis=0))
+
+    stored = planes * zlen
+    for end, row in ((0, 0), (1, ylen - 1)):
+        lines[end, :stored] = lines_in[end]
+        for comp in range(comps):
             for case in range(loads):
-                low = None
-                for z in range(zlen + 1):
-                    high = [faces(case * comps + comp, z) for comp in range(comps)]
-                    if low is not None:
-                        part = quadratic(low, high, weights)
-                        energy[z - 1] = part if energy[z - 1] is None else energy[z - 1] + part
-                    low = high
-            for z in range(zlen):
-                here = quotient[z, first + TILE : first + 2 * TILE, lanes]
-                quotient[z, first + TILE : first + 2 * TILE, lanes] = energy[z] * here
-
-    even = index_y % 2 == 0
-    for z in range(zlen):
-        rows = [quotient[z, TILE + step : TILE + step + ylen] for step in range(-REACH, REACH + 1)]
-        own_out[z] = sum((ROWS - abs(k - REACH)) * rows[k] for k in range(2 * REACH + 1))
-        top = quotient[z, ylen : ylen + TILE]
-        base = quotient[z, TILE : 2 * TILE]
-        ahead, back = [], []
-        for row in range(REACH):
-            ahead.append(sum(float(REACH - row - k) * top[TILE - 1 - k : TILE - k] for k in range(REACH - row)))
-            back.append(sum(float(row + 1 - k) * base[k : k + 1] for k in range(row + 1)))
-        blank = jnp.zeros((1, xlen), jnp.float32)
-        ahead = jnp.concatenate(ahead + [blank], axis=0)
-        back = jnp.concatenate([blank] + back, axis=0)
-        a_out[ROWS * z : ROWS * (z + 1)] = jnp.where(even, ahead, back)
-        b_out[ROWS * z : ROWS * (z + 1)] = jnp.where(even, back, ahead)
-
-
-def rows_kernel(own, a_in, b_in, h_out, a_out, b_out):
+                at = stored + comp * loads + case
+                lines[end, at : at + 1] = z_in[case * comps + comp, row : row + 1]
+        lines[end, stored + planes :] = jnp.zeros((lines.shape[1] - stored - planes, xlen), jnp.float32)
+    even = lax.axis_index("sy") % 2 == 0
+    size = lines.shape[1]
+    last = ROWS * (zlen - 1)
+    up = jnp.concatenate([sends_in[0, :last], ends[:REACH], sends_in[0, last + REACH :]], axis=0)
+    down = jnp.concatenate([sends_in[1, : last + 1], ends[REACH : 2 * REACH]], axis=0)
+    a_out[:size] = jnp.where(even, lines[1], lines[0])
+    b_out[:size] = jnp.where(even, lines[0], lines[1])
+    a_out[size:] = jnp.where(even, up, down)
+    b_out[size:] = jnp.where(even, down, up)
+
+
+def line_quotients(near, far, factor, loads, comps, zlen):
+    count = loads * zlen
+    stored = comps * count
+
+    def face(rows, comp):
+        low = rows[comp * count : (comp + 1) * count]
+        end = rows[stored + comp * loads : stored + (comp + 1) * loads]
+        parts = []
+        for case in range(loads):
+            parts += [low[case * zlen + 1 : (case + 1) * zlen], end[case : case + 1]]
+        return low, jnp.concatenate(parts, axis=0)
+
+    low, high = [], []
+    for comp in range(comps):
+        for rows_near, rows_far, into in zip(face(near, comp), face(far, comp), (low, high)):
+            (whole, change), (whole_next, change_next) = split_x(rows_near), split_x(rows_far)
+            into.append((whole + whole_next, change + change_next, whole_next - whole, change_next - change))
+    energy = quadratic(low, high, mode_weights())
+    return sum(energy[case * zlen : (case + 1) * zlen] for case in range(loads)) * factor
+
+
+def rows_kernel(loads, comps, own, lines, factors, a_in, b_in, h_out, a_out, b_out):
     zlen, ylen, _ = own.shape
     even = lax.axis_index("sy") % 2 == 0
+    size = lines.shape[1]
+    from_low = jnp.where(even, b_in[...], a_in[...])
+    from_high = jnp.where(even, a_in[...], b_in[...])
+    rows = [ROWS * z + REACH for z in range(zlen)]
+    own_factor = jnp.concatenate([factors[0, r : r + 1] for r in rows], axis=0)
+    low_factor = jnp.concatenate([from_low[size + r : size + r + 1] for r in rows], axis=0)
+    first = line_quotients(from_low, lines[0], low_factor, loads, comps, zlen)
+    last = line_quotients(lines[1], from_high, own_factor, loads, comps, zlen)
+    both = spread_x(jnp.concatenate([first, last], axis=0))
+    row = lax.broadcasted_iota(jnp.int32, (TILE, own.shape[2]), 0)
+    rising = jnp.maximum(row - (TILE - 1 - ROWS), 0).astype(jnp.float32)
+    falling = jnp.maximum(REACH - row, 0).astype(jnp.float32)
+    blank = jnp.zeros((TILE - ROWS, own.shape[2]), jnp.float32)
     for z in range(zlen):
-        part = slice(ROWS * z, ROWS * (z + 1))
-        from_low = jnp.where(even, b_in[part], a_in[part])
-        from_high = jnp.where(even, a_in[part], b_in[part])
+        part = slice(size + ROWS * z, size + ROWS * (z + 1))
+        head = jnp.concatenate([from_low[part], blank], axis=0)
+        head = jnp.where(row < REACH, head, 0.0) + falling * both[z : z + 1]
+        tail = jnp.concatenate([blank, from_high[part]], axis=0)
+        tail = jnp.where(row >= TILE - REACH, tail, 0.0) + rising * both[zlen + z : zlen + z + 1]
         h_out[z] = own[z]
-        h_out[z, :ROWS] = own[z, :ROWS] + from_low
-        h_out[z, ylen - ROWS :] = own[z, ylen - ROWS :] + from_high
+        h_out[z, :TILE] += head
+        h_out[z, ylen - TILE :] += tail
     top = (zlen - REACH) * (lax.axis_index("sz") % 2 == 0).astype(jnp.int32)
     a_out[...] = h_out[pl.ds(top, REACH)]
     b_out[...] = h_out[pl.ds(zlen - REACH - top, REACH)]
@@ -281,7 +382,7 @@
     above = [jnp.where(even, a_in[k], b_in[k]) for k in range(REACH)]
     layers = below + [h[z] for z in range(zlen)] + above
     for z, layer in enumerate(spread_layers(layers)):
-        out[z] = spread_x(layer)
+        out[z] = layer
 
 
 def sum_kernel(parts, out):
@@ -326,31 +427,42 @@
         pltpu.with_memory_space_constraint(arg, pltpu.HBM) for arg in (displacements, fixed, density, solid)
     ]
 
-    disp, fixed, density, solid, z_send, y_send, d_send = call(
+    rows = planes * zlen
+    size = rows + -(-planes // TILE) * TILE
+    disp, fixed, density, solid, z_send = call(
         lead_kernel,
-        [jax.ShapeDtypeStruct(arg.shape, arg.dtype) for arg in args]
-        + [(planes, ylen, xlen), (planes * zlen, xlen), (TILE, xlen)],
+        [jax.ShapeDtypeStruct(arg.shape, arg.dtype) for arg in args] + [(planes, ylen, xlen)],
         args,
         scratch=[pltpu.SemaphoreType.DMA((len(args),))],
         space=pltpu.HBM,
     )
     z_in = moved(z_send, ("sz",), (1,))
-    y_in = moved(y_send, ("sy",), (1,))
-    d_in = moved(d_send, ("sy", "sz"), (1, 1))
-    own, a_send, b_send = call(
-        lambda *refs: energy_kernel(totals, *refs),
-        [(zlen, ylen, xlen), (ROWS * zlen, xlen), (ROWS * zlen, xlen)],
-        (disp, fixed, density, solid, z_in, y_in, d_in),
-        scratch=[
-            pltpu.VMEM((planes, zlen + 1, ylen + TILE, xlen), jnp.float32),
-            pltpu.VMEM((planes, zlen + 1, ylen + TILE, xlen), jnp.float32),
-            pltpu.VMEM((zlen, ylen + 2 * TILE, xlen), jnp.float32),
+    nodes = lambda layers: pltpu.VMEM((planes, layers, ylen + TILE, xlen), jnp.float32)
+    inner = call(
+        lambda *refs: inner_kernel(totals, *refs),
+        [
+            (zlen, ylen, xlen),
+            (2, rows, xlen),
+            (2, ROWS * zlen, xlen),
+            (planes, ylen, xlen),
+            (planes, ylen, xlen),
+            (ylen, xlen),
         ],
+        (disp, fixed, density, solid),
+        scratch=[nodes(zlen), nodes(zlen), pltpu.VMEM((zlen - 1, ylen + 2 * TILE, xlen), jnp.float32)],
+    )
+    own, lines, a_send, b_send = call(
+        lambda *refs: outer_kernel(displacements.shape, *refs),
+        [(zlen, ylen, xlen), (2, size, xlen), (size + ROWS * zlen, xlen), (size + ROWS * zlen, xlen)],
+        (z_in, *inner),
+        scratch=[nodes(2), nodes(2), pltpu.VMEM((ylen + 2 * TILE, xlen), jnp.float32)],
     )
     a_in = swapped(a_send, "sy", 0)
     b_in = swapped(b_send, "sy", 1)
     h, a_send, b_send = call(
-        rows_kernel, [(zlen, ylen, xlen), (REACH, ylen, xlen), (REACH, ylen, xlen)], (own, a_in, b_in)
+        lambda *refs: rows_kernel(loads, comps, *refs),
+        [(zlen, ylen, xlen), (REACH, ylen, xlen), (REACH, ylen, xlen)],
+        (own, lines, inner[2], a_in, b_in),
     )
     a_in = swapped(a_send, "sz", 0)
     b_in = swapped(b_send, "sz", 1)

time: 33.8 us -> 30.7 us (0.908)
  the two profiles are of different devices: /device:TPU:21 before, /device:TPU:13 now
where the time goes in v4:
time: 30.7 us; the launch traced here: 30.5 us
  waiting for transfers between devices  9.18 us (30%)
  starting transfers between devices  8.73 us (28%)
  Pallas kernels  6.49 us (21%)
  blocking collectives  6.04 us (20%)
    ppermute x4, starting transfers between devices, swapped(): return lax.ppermute(value, axis, pairs)  6.65 us
    pallas_call x6, Pallas kernels, call(): pl.pallas_call(kernel, out_shape=shapes, in_specs=[pl.BlockSpec(memory_sp...  6.49 us
    ppermute x4, waiting for transfers between devices, swapped(): return lax.ppermute(value, axis, pairs)  6.44 us
    all_gather x1, blocking collectives, body(): parts = lax.all_gather(part, 'load', axis=0)  6.04 us
    ppermute x1, waiting for transfers between devices, moved(): return lax.ppermute(value, axes if len(axes) > 1 else axes[0], pairs)  2.74 us
    ppermute x1, starting transfers between devices, moved(): return lax.ppermute(value, axes if len(axes) > 1 else axes[0], pairs)  2.08 us
  transfers between devices with their start and end apart: 5, of which 5 were waited for; matrix products, arithmetic and copies ran while one was open for 0% of the time, Pallas kernels for 9%

profile of v4, /device:TPU:13, one launch (start us, length us, event | category | flops | bytes accessed | tf_op | source)
XLA Modules:
  0.0 30.5 jit_solution(3507303102841441634)
XLA Ops:
  0.0 1.3 %shard_map.46 = (f32[2,3,4,16,512]{4,3,2,1,0:T(8,128)S(1)}, s32[4,16,512]{2,1,0:T(8,128)S(1)}, f32[4,16,512]{2,1,0:T(8,128)S(1)}, s32[4,16,512]{2,1,0:T(8,128)S(1)}, f32[6,16,512]{2,1,0:T(8,128)S(1)}) custom-call(f32[2,3,4,16,512]{4,3,2,1,0:T(8,128)} %disp_hbm.1, s32[4,16,512]{2,1,0:T(8,128)} %fixed_hbm.1, f32[4,16,512]{2,1,0:T(8,128)} %density_hbm.1, ...), custom_call_target="tpu_custom_call" | custom-call | tf_op jit(solution)/shard_map/pallas_call | solution.py:394
  1.3 2.1 %collective-permute-start = (f32[6,16,512]{2,1,0:T(8,128)S(1)}, f32[6,16,512]{2,1,0:T(8,128)S(1)}, u32[]{:S(2)}, u32[]{:S(2)}) collective-permute-start(f32[6,16,512]{2,1,0:T(8,128)S(1)} %get-tuple-element.23), channel_id=1, source_target_pairs={{1,0},{2,1},{3,2},{5,4},{6,5},{7,6},{9,8},{10,9},{11,10},{13,12},{... | collective-permute-start | bytes 589832 | tf_op jit(solution)/shard_map/ppermute | solution.py:412
  3.4 2.8 %shard_map.47 = (f32[4,16,512]{2,1,0:T(8,128)S(1)}, f32[2,24,512]{2,1,0:T(8,128)S(1)}, f32[2,16,512]{2,1,0:T(8,128)S(1)}, f32[6,16,512]{2,1,0:T(8,128)S(1)}, f32...) custom-call(f32[2,3,4,16,512]{4,3,2,1,0:T(8,128)S(1)} %get-tuple-element.24.refs_0_, ...), custom_call_target="tpu_custom_call" | custom-call | tf_op jit(solution)/shard_map/pallas_call | solution.py:394
  6.2 2.7 %collective-permute-done.refs_0_ = f32[6,16,512]{2,1,0:T(8,128)S(1)} collective-permute-done((f32[6,16,512]{2,1,0:T(8,128)S(1)}, f32[6,16,512]{2,1,0:T(8,128)S(1)}, u32[]{:S(2)}, u32[]{:S(2)}) %collective-permute-start) | collective-permute-done | bytes 196640 | tf_op jit(solution)/shard_map/ppermute | solution.py:412
  8.9 1.1 %shard_map.48 = (f32[4,16,512]{2,1,0:T(8,128)S(1)}, f32[2,32,512]{2,1,0:T(8,128)S(1)}, f32[48,512]{1,0:T(8,128)S(1)}, f32[48,512]{1,0:T(8,128)S(1)}) custom-call(f32[6,16,512]{2,1,0:T(8,128)S(1)} %collective-permute-done.refs_0_, f32[4,16,512]{2,1,0:T(8,128)S(1)} %get-tuple-element.28.refs_1_, f32[2,24,512]{2,1,0:T(8,128)S(1)} %get-tuple-element.29.refs_2_, ...), custom_call_target="tpu_custom_call" | custom-call | tf_op jit(solution)/shard_map/pallas_call | solution.py:394
  10.0 1.3 %collective-permute-start.1 = (f32[48,512]{1,0:T(8,128)S(1)}, f32[48,512]{1,0:T(8,128)S(1)}, u32[]{:S(2)}, u32[]{:S(2)}) collective-permute-start(f32[48,512]{1,0:T(8,128)S(1)} %get-tuple-element.36), channel_id=1, source_target_pairs={{0,4},{4,0},{8,12},{12,8},{1,5},{5,1},{9,13},{13,9},{2,6},{6,2},{1... | collective-permute-start | bytes 294920 | tf_op jit(solution)/shard_map/ppermute | solution.py:419
  11.3 2.1 %collective-permute-start.2 = (f32[48,512]{1,0:T(8,128)S(1)}, f32[48,512]{1,0:T(8,128)S(1)}, u32[]{:S(2)}, u32[]{:S(2)}) collective-permute-start(f32[48,512]{1,0:T(8,128)S(1)} %get-tuple-element.37), channel_id=1, source_target_pairs={{4,8},{8,4},{5,9},{9,5},{6,10},{10,6},{7,11},{11,7},{20,24},{24,20... | collective-permute-start | bytes 294920 | tf_op jit(solution)/shard_map/ppermute | solution.py:419
  13.4 0.2 collective-permute-done.1.refs_3_
  13.6 4.0 %collective-permute-done.2.refs_4_ = f32[48,512]{1,0:T(8,128)S(1)} collective-permute-done((f32[48,512]{1,0:T(8,128)S(1)}, f32[48,512]{1,0:T(8,128)S(1)}, u32[]{:S(2)}, u32[]{:S(2)}) %collective-permute-start.2) | collective-permute-done | bytes 98336 | tf_op jit(solution)/shard_map/ppermute | solution.py:419
  17.6 0.6 %shard_map.49 = (f32[4,16,512]{2,1,0:T(8,128)S(1)}, f32[3,16,512]{2,1,0:T(8,128)S(1)}, f32[3,16,512]{2,1,0:T(8,128)S(1)}) custom-call(f32[4,16,512]{2,1,0:T(8,128)S(1)} %get-tuple-element.34.refs_0_, f32[2,32,512]{2,1,0:T(8,128)S(1)} %get-tuple-element.35.refs_1_, f32[2,16,512]{2,1,0:T(8,128)S(1)} %get-tuple-element.30.refs_3_.refs_2_, ...), custom_call_target="tpu_custom_call" | custom-call | tf_op jit(solution)/shard_map/pallas_call | solution.py:394
  18.2 0.2 collective-permute-start.3
  18.4 3.0 %collective-permute-start.4 = (f32[3,16,512]{2,1,0:T(8,128)S(1)}, f32[3,16,512]{2,1,0:T(8,128)S(1)}, u32[]{:S(2)}, u32[]{:S(2)}) collective-permute-start(f32[3,16,512]{2,1,0:T(8,128)S(1)} %get-tuple-element.40), channel_id=1, source_target_pairs={{1,2},{2,1},{5,6},{6,5},{9,10},{10,9},{13,14},{14,13},{17,18},{18,... | collective-permute-start | bytes 294920 | tf_op jit(solution)/shard_map/ppermute | solution.py:419
  21.4 0.2 collective-permute-done.3.a_in
  21.7 2.1 %collective-permute-done.4.b_in = f32[3,16,512]{2,1,0:T(8,128)S(1)} collective-permute-done((f32[3,16,512]{2,1,0:T(8,128)S(1)}, f32[3,16,512]{2,1,0:T(8,128)S(1)}, u32[]{:S(2)}, u32[]{:S(2)}) %collective-permute-start.4) | collective-permute-done | bytes 98336 | tf_op jit(solution)/shard_map/ppermute | solution.py:419
  23.8 6.0 %all-gather = f32[8,16,512]{2,1,0:T(8,128)S(1)} all-gather(f32[4,16,512]{2,1,0:T(8,128)S(1)} %shard_map.50), channel_id=2, replica_groups=mesh['load'=2,'sy'=4,'sz'=4] {'load'}, dimensions={0}, use_global_device_ids=true | all-gather | bytes 393216 | tf_op jit(solution)/shard_map/all_gather | solution.py:470
  29.8 0.7 %shard_map.51 = f32[4,16,512]{2,1,0:T(8,128)} custom-call(f32[2,4,16,512]{3,2,1,0:T(8,128)S(1)} %bitcast.1), custom_call_target="tpu_custom_call" | custom-call | tf_op jit(solution)/shard_map/pallas_call | solution.py:394
  (1 shorter events, 0.0 us)
Async XLA Ops:
  1.3 7.7 %collective-permute-start = (f32[6,16,512]{2,1,0:T(8,128)S(1)}, f32[6,16,512]{2,1,0:T(8,128)S(1)}, u32[]{:S(2)}, u32[]{:S(2)}) collective-permute-start(f32[6,16,512]{2,1,0:T(8,128)S(1)} %get-tuple-element.23), channel_id=1, source_target_pairs={{1,0},{2,1},{3,2},{5,4},{6,5},{7,6},{9,8},{10,9},{11,10},{13,12},{... | collective-permute-start | bytes 589832 | tf_op jit(solution)/shard_map/ppermute | solution.py:412
  10.0 3.5 %collective-permute-start.1 = (f32[48,512]{1,0:T(8,128)S(1)}, f32[48,512]{1,0:T(8,128)S(1)}, u32[]{:S(2)}, u32[]{:S(2)}) collective-permute-start(f32[48,512]{1,0:T(8,128)S(1)} %get-tuple-element.36), channel_id=1, source_target_pairs={{0,4},{4,0},{8,12},{12,8},{1,5},{5,1},{9,13},{13,9},{2,6},{6,2},{1... | collective-permute-start | bytes 294920 | tf_op jit(solution)/shard_map/ppermute | solution.py:419
  11.3 6.2 %collective-permute-start.2 = (f32[48,512]{1,0:T(8,128)S(1)}, f32[48,512]{1,0:T(8,128)S(1)}, u32[]{:S(2)}, u32[]{:S(2)}) collective-permute-start(f32[48,512]{1,0:T(8,128)S(1)} %get-tuple-element.37), channel_id=1, source_target_pairs={{4,8},{8,4},{5,9},{9,5},{6,10},{10,6},{7,11},{11,7},{20,24},{24,20... | collective-permute-start | bytes 294920 | tf_op jit(solution)/shard_map/ppermute | solution.py:419
  18.2 3.5 %collective-permute-start.3 = (f32[3,16,512]{2,1,0:T(8,128)S(1)}, f32[3,16,512]{2,1,0:T(8,128)S(1)}, u32[]{:S(2)}, u32[]{:S(2)}) collective-permute-start(f32[3,16,512]{2,1,0:T(8,128)S(1)} %get-tuple-element.39), channel_id=1, source_target_pairs={{0,1},{1,0},{2,3},{3,2},{4,5},{5,4},{6,7},{7,6},{8,9},{9,8},{10,11... | collective-permute-start | bytes 294920 | tf_op jit(solution)/shard_map/ppermute | solution.py:419
  18.4 5.3 %collective-permute-start.4 = (f32[3,16,512]{2,1,0:T(8,128)S(1)}, f32[3,16,512]{2,1,0:T(8,128)S(1)}, u32[]{:S(2)}, u32[]{:S(2)}) collective-permute-start(f32[3,16,512]{2,1,0:T(8,128)S(1)} %get-tuple-element.40), channel_id=1, source_target_pairs={{1,2},{2,1},{5,6},{6,5},{9,10},{10,9},{13,14},{14,13},{17,18},{18,... | collective-permute-start | bytes 294920 | tf_op jit(solution)/shard_map/ppermute | solution.py:419

commit v5 on v4

--- a/solution.py
+++ b/solution.py
@@ -179,8 +179,8 @@
     return ahead, back
 
 
-def lead_kernel(disp_hbm, fixed_hbm, density_hbm, solid_hbm, disp, fixed, density, solid, z_out, sems):
-    loads, comps, _, _, _ = disp.shape
+def lead_kernel(disp_hbm, fixed_hbm, density_hbm, solid_hbm, disp, fixed, density, solid, z_out, y_out, sems):
+    loads, comps, zlen, _, _ = disp.shape
     copies = [
         pltpu.make_async_copy(source, target, sems.at[k])
         for k, (source, target) in enumerate(
@@ -194,6 +194,9 @@
     for case in range(loads):
         for comp in range(comps):
             z_out[case * comps + comp] = held(disp, fixed, case, comp, 0, slice(None))
+            for z in range(zlen):
+                at = (comp * loads + case) * zlen + z
+                y_out[at : at + 1] = held(disp, fixed, case, comp, z, slice(0, 1))
 
 
 def tile_energies(plus, diff, first, lanes, layers, loads, comps):
@@ -222,7 +225,7 @@
     return jnp.where(row == ylen - 1, 0.0, value)
 
 
-def inner_kernel(totals, disp, fixed, density, solid, own, lines, sends, last_plus, last_diff, last_factor, plus, diff, quotient):
+def inner_kernel(totals, disp, fixed, density, solid, own, line, sends, last_plus, last_diff, last_factor, edge, plus, diff, quotient):
     loads, comps, zlen, ylen, xlen = disp.shape
     total_z, total_y = totals
     base_z = lax.axis_index("sz") * zlen
@@ -243,14 +246,14 @@
         for case in range(loads):
             for z in range(zlen):
                 at = (comp * loads + case) * zlen + z
-                lines[0, at : at + 1] = held(disp, fixed, case, comp, z, slice(0, 1))
-                lines[1, at : at + 1] = held(disp, fixed, case, comp, z, slice(ylen - 1, ylen))
+                line[0, at : at + 1] = plus[case * comps + comp, z, ylen - 1 : ylen]
+                line[1, at : at + 1] = diff[case * comps + comp, z, ylen - 1 : ylen]
 
     zeros = jnp.zeros((TILE, xlen), jnp.float32)
+    edge[...] = jnp.zeros(edge.shape, jnp.float32)
     for z in range(zlen):
         factor = voxel_factor(density[z], solid[z], base_z + z, base_y, total_z, total_y)
-        sends[0, ROWS * z + REACH : ROWS * (z + 1)] = factor[ylen - 1 :]
-        sends[1, ROWS * z : ROWS * z + 1] = zeros[:1]
+        edge[z : z + 1] = factor[ylen - 1 :]
         if z == inner:
             last_factor[...] = factor
         else:
@@ -272,15 +275,16 @@
         own[z] = spread_x(spread_y(quotient.at[z], ylen))
         ahead, back = to_neighbours(quotient.at[z], ylen)
         ends = spread_x(jnp.concatenate(ahead + back + [zeros[:2]], axis=0))
-        sends[0, ROWS * z : ROWS * z + REACH] = ends[:REACH]
-        sends[1, ROWS * z + 1 : ROWS * (z + 1)] = ends[REACH : 2 * REACH]
+        sends[0, REACH * z : REACH * (z + 1)] = ends[:REACH]
+        sends[1, REACH * z : REACH * (z + 1)] = ends[REACH : 2 * REACH]
 
 
 def outer_kernel(
-    shape, z_in, own_in, lines_in, sends_in, last_plus, last_diff, last_factor, own, lines, a_out, b_out, plus, diff, quotient
+    shape, z_in, y_in, disp, fixed, own_in, line, sends, last_plus, last_diff, last_factor, edge, own, known, a_out, b_out, plus, diff, quotient
 ):
     loads, comps, zlen, ylen, xlen = shape
     planes = loads * comps
+    inner = zlen - 1
     for k in range(planes):
         plus[k, 0, :ylen] = last_plus[k]
         diff[k, 0, :ylen] = last_diff[k]
@@ -300,73 +304,89 @@
             here = energy * last_factor[first : first + TILE, lanes]
             quotient[first + TILE : first + 2 * TILE, lanes] = blank_last(here, first, ylen)
 
-    own[: zlen - 1] = own_in[: zlen - 1]
-    own[zlen - 1] = spread_x(spread_y(quotient, ylen))
+    count = loads * zlen
+    low, high = [], []
+    for comp in range(comps):
+        part = slice(comp * count, (comp + 1) * count)
+        whole, change = line[0, part], line[1, part]
+        whole_next, change_next = split_x(y_in[part])
+        face = (whole + whole_next, change + change_next, whole_next - whole, change_next - change)
+        low.append(face)
+        high.append([pltpu.roll(value, count - 1, 0) for value in face])
+    energy = quadratic(low, high, mode_weights())
+    energy = sum(energy[case * zlen : case * zlen + inner] for case in range(loads)) * edge[:inner]
+    last = spread_x(jnp.concatenate([energy, jnp.zeros((TILE - inner, xlen), jnp.float32)], axis=0))
+
+    row = lax.broadcasted_iota(jnp.int32, (TILE, xlen), 0)
+    rising = jnp.maximum(row - (TILE - 1 - ROWS), 0).astype(jnp.float32)
+    ups, downs = [], []
+    for z in range(inner):
+        own[z] = own_in[z]
+        own[z, ylen - TILE :] += rising * last[z : z + 1]
+        here = sends[0, REACH * z : REACH * (z + 1)]
+        ups += [here[r : r + 1] + float(REACH - r) * last[z : z + 1] for r in range(REACH)]
+        downs.append(sends[1, REACH * z : REACH * (z + 1)])
+    own[inner] = spread_x(spread_y(quotient, ylen))
     ahead, back = to_neighbours(quotient, ylen)
     ends = spread_x(jnp.concatenate(ahead + back + [zeros[:2]], axis=0))
-
-    stored = planes * zlen
-    for end, row in ((0, 0), (1, ylen - 1)):
-        lines[end, :stored] = lines_in[end]
-        for comp in range(comps):
-            for case in range(loads):
-                at = stored + comp * loads + case
-                lines[end, at : at + 1] = z_in[case * comps + comp, row : row + 1]
-        lines[end, stored + planes :] = jnp.zeros((lines.shape[1] - stored - planes, xlen), jnp.float32)
+    ups += [ends[: REACH - 1], edge[inner:zlen]]
+    downs.append(ends[REACH : 2 * REACH])
+
+    pairs = [(case, comp) for comp in range(comps) for case in range(loads)]
+    here_last = [held(disp, fixed, case, comp, inner, slice(ylen - 1, ylen)) for case, comp in pairs]
+    here_first = [held(disp, fixed, case, comp, inner, slice(0, 1)) for case, comp in pairs]
+    next_row = [y_in[(k + 1) * zlen - 1 : (k + 1) * zlen] for k in range(planes)]
+    over_last = [z_in[case * comps + comp, ylen - 1 : ylen] for case, comp in pairs]
+    over_first = [z_in[case * comps + comp, 0:1] for case, comp in pairs]
+    rows = here_last + over_last + next_row + here_first + over_first
+    known[: len(rows)] = jnp.concatenate(rows, axis=0)
+    known[len(rows) :] = jnp.zeros((known.shape[0] - len(rows), xlen), jnp.float32)
+    up = jnp.concatenate(ups + here_last + over_last, axis=0)
+    down = jnp.concatenate(downs + over_first + [jnp.zeros((planes, xlen), jnp.float32)], axis=0)
     even = lax.axis_index("sy") % 2 == 0
-    size = lines.shape[1]
-    last = ROWS * (zlen - 1)
-    up = jnp.concatenate([sends_in[0, :last], ends[:REACH], sends_in[0, last + REACH :]], axis=0)
-    down = jnp.concatenate([sends_in[1, : last + 1], ends[REACH : 2 * REACH]], axis=0)
-    a_out[:size] = jnp.where(even, lines[1], lines[0])
-    b_out[:size] = jnp.where(even, lines[0], lines[1])
-    a_out[size:] = jnp.where(even, up, down)
-    b_out[size:] = jnp.where(even, down, up)
-
-
-def line_quotients(near, far, factor, loads, comps, zlen):
-    count = loads * zlen
-    stored = comps * count
-
-    def face(rows, comp):
-        low = rows[comp * count : (comp + 1) * count]
-        end = rows[stored + comp * loads : stored + (comp + 1) * loads]
-        parts = []
-        for case in range(loads):
-            parts += [low[case * zlen + 1 : (case + 1) * zlen], end[case : case + 1]]
-        return low, jnp.concatenate(parts, axis=0)
-
-    low, high = [], []
-    for comp in range(comps):
-        for rows_near, rows_far, into in zip(face(near, comp), face(far, comp), (low, high)):
-            (whole, change), (whole_next, change_next) = split_x(rows_near), split_x(rows_far)
-            into.append((whole + whole_next, change + change_next, whole_next - whole, change_next - change))
-    energy = quadratic(low, high, mode_weights())
-    return sum(energy[case * zlen : (case + 1) * zlen] for case in range(loads)) * factor
-
-
-def rows_kernel(loads, comps, own, lines, factors, a_in, b_in, h_out, a_out, b_out):
-    zlen, ylen, _ = own.shape
+    a_out[...] = jnp.where(even, up, down)
+    b_out[...] = jnp.where(even, down, up)
+
+
+def rows_kernel(loads, comps, own, known, edge, a_in, b_in, h_out, a_out, b_out):
+    zlen, ylen, xlen = own.shape
+    planes = loads * comps
     even = lax.axis_index("sy") % 2 == 0
-    size = lines.shape[1]
     from_low = jnp.where(even, b_in[...], a_in[...])
     from_high = jnp.where(even, a_in[...], b_in[...])
-    rows = [ROWS * z + REACH for z in range(zlen)]
-    own_factor = jnp.concatenate([factors[0, r : r + 1] for r in rows], axis=0)
-    low_factor = jnp.concatenate([from_low[size + r : size + r + 1] for r in rows], axis=0)
-    first = line_quotients(from_low, lines[0], low_factor, loads, comps, zlen)
-    last = line_quotients(lines[1], from_high, own_factor, loads, comps, zlen)
-    both = spread_x(jnp.concatenate([first, last], axis=0))
-    row = lax.broadcasted_iota(jnp.int32, (TILE, own.shape[2]), 0)
+    ends = REACH * zlen
+
+    def nodes(first, second, comp):
+        part = slice(comp * loads, (comp + 1) * loads)
+        rows = jnp.concatenate([first[part], second[part]], axis=0)
+        return split_x(jnp.concatenate([rows, rows], axis=0))
+
+    def face(near_own, near_in, far_own, far_in, comp):
+        whole, change = nodes(near_own, near_in, comp)
+        whole_next, change_next = nodes(far_own, far_in, comp)
+        return whole + whole_next, change + change_next, whole_next - whole, change_next - change
+
+    here_last, over_last, next_row, here_first, over_first = (known[planes * k : planes * (k + 1)] for k in range(5))
+    low_last, low_over = from_low[ends : ends + planes], from_low[ends + planes : ends + 2 * planes]
+    next_over = from_high[ends : ends + planes]
+    low = [face(here_last, low_last, next_row, here_first, comp) for comp in range(comps)]
+    high = [face(over_last, low_over, next_over, over_first, comp) for comp in range(comps)]
+    energy = quadratic(low, high, mode_weights())
+    lines = [sum(energy[loads * k + case : loads * k + case + 1] for case in range(loads)) for k in range(2)]
+    lines = [lines[0] * edge[zlen - 1 : zlen], lines[1] * from_low[ends - 1 : ends]]
+    lines = spread_x(jnp.concatenate(lines + [jnp.zeros((TILE - 2, xlen), jnp.float32)], axis=0))
+
+    row = lax.broadcasted_iota(jnp.int32, (TILE, xlen), 0)
     rising = jnp.maximum(row - (TILE - 1 - ROWS), 0).astype(jnp.float32)
     falling = jnp.maximum(REACH - row, 0).astype(jnp.float32)
-    blank = jnp.zeros((TILE - ROWS, own.shape[2]), jnp.float32)
+    blank = jnp.zeros((TILE - REACH, xlen), jnp.float32)
     for z in range(zlen):
-        part = slice(size + ROWS * z, size + ROWS * (z + 1))
+        part = slice(REACH * z, REACH * (z + 1))
         head = jnp.concatenate([from_low[part], blank], axis=0)
-        head = jnp.where(row < REACH, head, 0.0) + falling * both[z : z + 1]
         tail = jnp.concatenate([blank, from_high[part]], axis=0)
-        tail = jnp.where(row >= TILE - REACH, tail, 0.0) + rising * both[zlen + z : zlen + z + 1]
+        if z == zlen - 1:
+            head = jnp.where(row == REACH - 1, 0.0, head) + falling * lines[1:2]
+            tail = tail + rising * lines[0:1]
         h_out[z] = own[z]
         h_out[z, :TILE] += head
         h_out[z, ylen - TILE :] += tail
@@ -427,34 +447,35 @@
         pltpu.with_memory_space_constraint(arg, pltpu.HBM) for arg in (displacements, fixed, density, solid)
     ]
 
-    rows = planes * zlen
-    size = rows + -(-planes // TILE) * TILE
-    disp, fixed, density, solid, z_send = call(
+    disp, fixed, density, solid, z_send, y_send = call(
         lead_kernel,
-        [jax.ShapeDtypeStruct(arg.shape, arg.dtype) for arg in args] + [(planes, ylen, xlen)],
+        [jax.ShapeDtypeStruct(arg.shape, arg.dtype) for arg in args] + [(planes, ylen, xlen), (planes * zlen, xlen)],
         args,
         scratch=[pltpu.SemaphoreType.DMA((len(args),))],
         space=pltpu.HBM,
     )
     z_in = moved(z_send, ("sz",), (1,))
+    y_in = moved(y_send, ("sy",), (1,))
     nodes = lambda layers: pltpu.VMEM((planes, layers, ylen + TILE, xlen), jnp.float32)
     inner = call(
         lambda *refs: inner_kernel(totals, *refs),
         [
             (zlen, ylen, xlen),
-            (2, rows, xlen),
-            (2, ROWS * zlen, xlen),
+            (2, planes * zlen, xlen),
+            (2, REACH * (zlen - 1), xlen),
             (planes, ylen, xlen),
             (planes, ylen, xlen),
             (ylen, xlen),
+            (TILE, xlen),
         ],
         (disp, fixed, density, solid),
         scratch=[nodes(zlen), nodes(zlen), pltpu.VMEM((zlen - 1, ylen + 2 * TILE, xlen), jnp.float32)],
     )
-    own, lines, a_send, b_send = call(
+    size = REACH * zlen + 2 * planes
+    own, known, a_send, b_send = call(
         lambda *refs: outer_kernel(displacements.shape, *refs),
-        [(zlen, ylen, xlen), (2, size, xlen), (size + ROWS * zlen, xlen), (size + ROWS * zlen, xlen)],
-        (z_in, *inner),
+        [(zlen, ylen, xlen), (-(-5 * planes // TILE) * TILE, xlen), (size, xlen), (size, xlen)],
+        (z_in, y_in, disp, fixed, *inner),
         scratch=[nodes(2), nodes(2), pltpu.VMEM((ylen + 2 * TILE, xlen), jnp.float32)],
     )
     a_in = swapped(a_send, "sy", 0)
@@ -462,7 +483,7 @@
     h, a_send, b_send = call(
         lambda *refs: rows_kernel(loads, comps, *refs),
         [(zlen, ylen, xlen), (REACH, ylen, xlen), (REACH, ylen, xlen)],
-        (own, lines, inner[2], a_in, b_in),
+        (own, known, inner[-1], a_in, b_in),
     )
     a_in = swapped(a_send, "sz", 0)
     b_in = swapped(b_send, "sz", 1)

time: 30.7 us -> 30.6 us (level)
  the two profiles are of different devices: /device:TPU:13 before, /device:TPU:19 now
where the time goes in v5:
time: 30.6 us; the launch traced here: 30.4 us
  starting transfers between devices  11.2 us (37%)
  waiting for transfers between devices  6.55 us (21%)
  Pallas kernels  6.52 us (21%)
  blocking collectives  6.02 us (20%)
    ppermute x4, starting transfers between devices, swapped(): return lax.ppermute(value, axis, pairs)  6.98 us
    pallas_call x6, Pallas kernels, call(): pl.pallas_call(kernel, out_shape=shapes, in_specs=[pl.BlockSpec(memory_sp...  6.52 us
    all_gather x1, blocking collectives, body(): parts = lax.all_gather(part, 'load', axis=0)  6.02 us
    ppermute x4, waiting for transfers between devices, swapped(): return lax.ppermute(value, axis, pairs)  5.82 us
    ppermute x2, starting transfers between devices, moved(): return lax.ppermute(value, axes if len(axes) > 1 else axes[0], pairs)  4.24 us
    ppermute x2, waiting for transfers between devices, moved(): return lax.ppermute(value, axes if len(axes) > 1 else axes[0], pairs)  0.72 us
  transfers between devices with their start and end apart: 6, of which 4 were waited for; matrix products, arithmetic and copies ran while one was open for 0% of the time, Pallas kernels for 9%

profile of v5, /device:TPU:19, one launch (start us, length us, event | category | flops | bytes accessed | tf_op | source)
XLA Modules:
  0.0 30.4 jit_solution(7599153619308676280)
XLA Ops:
  0.0 1.3 %shard_map.46 = (f32[2,3,4,16,512]{4,3,2,1,0:T(8,128)S(1)}, s32[4,16,512]{2,1,0:T(8,128)S(1)}, f32[4,16,512]{2,1,0:T(8,128)S(1)}, s32[4,16,512]{2,1,0:T(8,128)S(...) custom-call(f32[2,3,4,16,512]{4,3,2,1,0:T(8,128)} %disp_hbm.1, s32[4,16,512]{2,1,0:T(8,128)} %fixed_hbm.1, ...), custom_call_target="tpu_custom_call" | custom-call | tf_op jit(solution)/shard_map/pallas_call | solution.py:414
  1.3 2.1 %collective-permute-start = (f32[6,16,512]{2,1,0:T(8,128)S(1)}, f32[6,16,512]{2,1,0:T(8,128)S(1)}, u32[]{:S(2)}, u32[]{:S(2)}) collective-permute-start(f32[6,16,512]{2,1,0:T(8,128)S(1)} %get-tuple-element.25), channel_id=1, source_target_pairs={{1,0},{2,1},{3,2},{5,4},{6,5},{7,6},{9,8},{10,9},{11,10},{13,12},{... | collective-permute-start | bytes 589832 | tf_op jit(solution)/shard_map/ppermute | solution.py:432
  3.4 2.2 %collective-permute-start.1 = (f32[24,512]{1,0:T(8,128)S(1)}, f32[24,512]{1,0:T(8,128)S(1)}, u32[]{:S(2)}, u32[]{:S(2)}) collective-permute-start(f32[24,512]{1,0:T(8,128)S(1)} %get-tuple-element.26), channel_id=1, source_target_pairs={{4,0},{8,4},{12,8},{5,1},{9,5},{13,9},{6,2},{10,6},{14,10},{7,3},{... | collective-permute-start | bytes 147464 | tf_op jit(solution)/shard_map/ppermute | solution.py:432
  5.5 2.8 %shard_map.47 = (f32[4,16,512]{2,1,0:T(8,128)S(1)}, f32[2,24,512]{2,1,0:T(8,128)S(1)}, f32[2,9,512]{2,1,0:T(8,128)S(1)}, f32[6,16,512]{2,1,0:T(8,128)S(1)}, f32[...) custom-call(f32[2,3,4,16,512]{4,3,2,1,0:T(8,128)S(1)} %get-tuple-element.27.refs_0_.refs_2_, ...), custom_call_target="tpu_custom_call" | custom-call | tf_op jit(solution)/shard_map/pallas_call | solution.py:414
  8.4 0.7 %collective-permute-done.1.refs_1_ = f32[24,512]{1,0:T(8,128)S(1)} collective-permute-done((f32[24,512]{1,0:T(8,128)S(1)}, f32[24,512]{1,0:T(8,128)S(1)}, u32[]{:S(2)}, u32[]{:S(2)}) %collective-permute-start.1) | collective-permute-done | bytes 49184 | tf_op jit(solution)/shard_map/ppermute | solution.py:432
  9.1 0.0 collective-permute-done.refs_0_
  9.1 1.2 %shard_map.48 = (f32[4,16,512]{2,1,0:T(8,128)S(1)}, f32[32,512]{1,0:T(8,128)S(1)}, f32[24,512]{1,0:T(8,128)S(1)}, f32[24,512]{1,0:T(8,128)S(1)}) custom-call(f32[6,16,512]{2,1,0:T(8,128)S(1)} %collective-permute-done.refs_0_, f32[24,512]{1,0:T(8,128)S(1)} %collective-permute-done.1.refs_1_, f32[2,3,4,16,512]{4,3,2,1,0:T(8,128)S(1)} %get-tuple-element.27.refs_0_.refs_2_, ...), custom_call_target="tpu_custom_call" | custom-call | tf_op jit(solution)/shard_map/pallas_call | solution.py:414
  10.3 0.2 collective-permute-start.2
  10.5 4.1 %collective-permute-start.3 = (f32[24,512]{1,0:T(8,128)S(1)}, f32[24,512]{1,0:T(8,128)S(1)}, u32[]{:S(2)}, u32[]{:S(2)}) collective-permute-start(f32[24,512]{1,0:T(8,128)S(1)} %get-tuple-element.41), channel_id=1, source_target_pairs={{4,8},{8,4},{5,9},{9,5},{6,10},{10,6},{7,11},{11,7},{20,24},{24,20... | collective-permute-start | bytes 147464 | tf_op jit(solution)/shard_map/ppermute | solution.py:439
  14.5 0.0 collective-permute-done.2.refs_3_
  14.6 2.1 %collective-permute-done.3.refs_4_ = f32[24,512]{1,0:T(8,128)S(1)} collective-permute-done((f32[24,512]{1,0:T(8,128)S(1)}, f32[24,512]{1,0:T(8,128)S(1)}, u32[]{:S(2)}, u32[]{:S(2)}) %collective-permute-start.3) | collective-permute-done | bytes 49184 | tf_op jit(solution)/shard_map/ppermute | solution.py:439
  16.6 0.5 %shard_map.49 = (f32[4,16,512]{2,1,0:T(8,128)S(1)}, f32[3,16,512]{2,1,0:T(8,128)S(1)}, f32[3,16,512]{2,1,0:T(8,128)S(1)}) custom-call(f32[4,16,512]{2,1,0:T(8,128)S(1)} %get-tuple-element.38.refs_0_, f32[32,512]{1,0:T(8,128)S(1)} %get-tuple-element.39.refs_1_, f32[8,512]{1,0:T(8,128)S(1)} %get-tuple-element.37.refs_10_.refs_2_, ...), custom_call_target="tpu_custom_call" | custom-call | tf_op jit(solution)/shard_map/pallas_call | solution.py:414
  17.1 0.8 %collective-permute-start.4 = (f32[3,16,512]{2,1,0:T(8,128)S(1)}, f32[3,16,512]{2,1,0:T(8,128)S(1)}, u32[]{:S(2)}, u32[]{:S(2)}) collective-permute-start(f32[3,16,512]{2,1,0:T(8,128)S(1)} %get-tuple-element.43), channel_id=1, source_target_pairs={{0,1},{1,0},{2,3},{3,2},{4,5},{5,4},{6,7},{7,6},{8,9},{9,8},{10,11... | collective-permute-start | bytes 294920 | tf_op jit(solution)/shard_map/ppermute | solution.py:439
  18.0 1.9 %collective-permute-start.5 = (f32[3,16,512]{2,1,0:T(8,128)S(1)}, f32[3,16,512]{2,1,0:T(8,128)S(1)}, u32[]{:S(2)}, u32[]{:S(2)}) collective-permute-start(f32[3,16,512]{2,1,0:T(8,128)S(1)} %get-tuple-element.44), channel_id=1, source_target_pairs={{1,2},{2,1},{5,6},{6,5},{9,10},{10,9},{13,14},{14,13},{17,18},{18,... | collective-permute-start | bytes 294920 | tf_op jit(solution)/shard_map/ppermute | solution.py:439
  19.9 0.8 %collective-permute-done.4.a_in = f32[3,16,512]{2,1,0:T(8,128)S(1)} collective-permute-done((f32[3,16,512]{2,1,0:T(8,128)S(1)}, f32[3,16,512]{2,1,0:T(8,128)S(1)}, u32[]{:S(2)}, u32[]{:S(2)}) %collective-permute-start.4) | collective-permute-done | bytes 98336 | tf_op jit(solution)/shard_map/ppermute | solution.py:439
  20.7 3.0 %collective-permute-done.5.b_in = f32[3,16,512]{2,1,0:T(8,128)S(1)} collective-permute-done((f32[3,16,512]{2,1,0:T(8,128)S(1)}, f32[3,16,512]{2,1,0:T(8,128)S(1)}, u32[]{:S(2)}, u32[]{:S(2)}) %collective-permute-start.5) | collective-permute-done | bytes 98336 | tf_op jit(solution)/shard_map/ppermute | solution.py:439
  23.7 6.0 %all-gather = f32[8,16,512]{2,1,0:T(8,128)S(1)} all-gather(f32[4,16,512]{2,1,0:T(8,128)S(1)} %shard_map.50), channel_id=2, replica_groups=mesh['load'=2,'sy'=4,'sz'=4] {'load'}, dimensions={0}, use_global_device_ids=true | all-gather | bytes 393216 | tf_op jit(solution)/shard_map/all_gather | solution.py:491
  29.7 0.7 %shard_map.51 = f32[4,16,512]{2,1,0:T(8,128)} custom-call(f32[2,4,16,512]{3,2,1,0:T(8,128)S(1)} %bitcast.1), custom_call_target="tpu_custom_call" | custom-call | tf_op jit(solution)/shard_map/pallas_call | solution.py:414
  (1 shorter events, 0.0 us)
Async XLA Ops:
  1.3 7.8 %collective-permute-start = (f32[6,16,512]{2,1,0:T(8,128)S(1)}, f32[6,16,512]{2,1,0:T(8,128)S(1)}, u32[]{:S(2)}, u32[]{:S(2)}) collective-permute-start(f32[6,16,512]{2,1,0:T(8,128)S(1)} %get-tuple-element.25), channel_id=1, source_target_pairs={{1,0},{2,1},{3,2},{5,4},{6,5},{7,6},{9,8},{10,9},{11,10},{13,12},{... | collective-permute-start | bytes 589832 | tf_op jit(solution)/shard_map/ppermute | solution.py:432
  3.4 5.7 %collective-permute-start.1 = (f32[24,512]{1,0:T(8,128)S(1)}, f32[24,512]{1,0:T(8,128)S(1)}, u32[]{:S(2)}, u32[]{:S(2)}) collective-permute-start(f32[24,512]{1,0:T(8,128)S(1)} %get-tuple-element.26), channel_id=1, source_target_pairs={{4,0},{8,4},{12,8},{5,1},{9,5},{13,9},{6,2},{10,6},{14,10},{7,3},{... | collective-permute-start | bytes 147464 | tf_op jit(solution)/shard_map/ppermute | solution.py:432
  10.3 4.2 %collective-permute-start.2 = (f32[24,512]{1,0:T(8,128)S(1)}, f32[24,512]{1,0:T(8,128)S(1)}, u32[]{:S(2)}, u32[]{:S(2)}) collective-permute-start(f32[24,512]{1,0:T(8,128)S(1)} %get-tuple-element.40), channel_id=1, source_target_pairs={{0,4},{4,0},{8,12},{12,8},{1,5},{5,1},{9,13},{13,9},{2,6},{6,2},{1... | collective-permute-start | bytes 147464 | tf_op jit(solution)/shard_map/ppermute | solution.py:439
  10.5 6.2 %collective-permute-start.3 = (f32[24,512]{1,0:T(8,128)S(1)}, f32[24,512]{1,0:T(8,128)S(1)}, u32[]{:S(2)}, u32[]{:S(2)}) collective-permute-start(f32[24,512]{1,0:T(8,128)S(1)} %get-tuple-element.41), channel_id=1, source_target_pairs={{4,8},{8,4},{5,9},{9,5},{6,10},{10,6},{7,11},{11,7},{20,24},{24,20... | collective-permute-start | bytes 147464 | tf_op jit(solution)/shard_map/ppermute | solution.py:439
  17.1 3.5 %collective-permute-start.4 = (f32[3,16,512]{2,1,0:T(8,128)S(1)}, f32[3,16,512]{2,1,0:T(8,128)S(1)}, u32[]{:S(2)}, u32[]{:S(2)}) collective-permute-start(f32[3,16,512]{2,1,0:T(8,128)S(1)} %get-tuple-element.43), channel_id=1, source_target_pairs={{0,1},{1,0},{2,3},{3,2},{4,5},{5,4},{6,7},{7,6},{8,9},{9,8},{10,11... | collective-permute-start | bytes 294920 | tf_op jit(solution)/shard_map/ppermute | solution.py:439
  18.0 5.6 %collective-permute-start.5 = (f32[3,16,512]{2,1,0:T(8,128)S(1)}, f32[3,16,512]{2,1,0:T(8,128)S(1)}, u32[]{:S(2)}, u32[]{:S(2)}) collective-permute-start(f32[3,16,512]{2,1,0:T(8,128)S(1)} %get-tuple-element.44), channel_id=1, source_target_pairs={{1,2},{2,1},{5,6},{6,5},{9,10},{10,9},{13,14},{14,13},{17,18},{18,... | collective-permute-start | bytes 294920 | tf_op jit(solution)/shard_map/ppermute | solution.py:439

commit v6 on v5

--- a/solution.py
+++ b/solution.py
@@ -348,7 +348,7 @@
     b_out[...] = jnp.where(even, down, up)
 
 
-def rows_kernel(loads, comps, own, known, edge, a_in, b_in, h_out, a_out, b_out):
+def rows_kernel(loads, comps, own, known, edge, b_in, a_in, h_out):
     zlen, ylen, xlen = own.shape
     planes = loads * comps
     even = lax.axis_index("sy") % 2 == 0
@@ -390,17 +390,28 @@
         h_out[z] = own[z]
         h_out[z, :TILE] += head
         h_out[z, ylen - TILE :] += tail
-    top = (zlen - REACH) * (lax.axis_index("sz") % 2 == 0).astype(jnp.int32)
-    a_out[...] = h_out[pl.ds(top, REACH)]
-    b_out[...] = h_out[pl.ds(zlen - REACH - top, REACH)]
-
-
-def layers_kernel(h, a_in, b_in, out):
+
+
+def upper_side():
+    return (lax.axis_index("sz") + lax.axis_index("load")) % 2 == 0
+
+
+def total_kernel(parts, h_out, z_out):
+    zlen = h_out.shape[0]
+    for z in range(zlen):
+        h_out[z] = parts[0, z] + parts[1, z]
+    top = (zlen - REACH) * upper_side().astype(jnp.int32)
+    z_out[...] = h_out[pl.ds(top, REACH)]
+
+
+def layers_kernel(h, z_in, out):
     zlen = h.shape[0]
-    even = lax.axis_index("sz") % 2 == 0
-    below = [jnp.where(even, b_in[k], a_in[k]) for k in range(REACH)]
-    above = [jnp.where(even, a_in[k], b_in[k]) for k in range(REACH)]
-    layers = below + [h[z] for z in range(zlen)] + above
+    upper = upper_side()
+    first = lax.axis_index("load") == 0
+    zero = jnp.zeros(h.shape[1:], jnp.float32)
+    below = [jnp.where(upper, zero, z_in[k]) for k in range(REACH)]
+    above = [jnp.where(upper, z_in[k], zero) for k in range(REACH)]
+    layers = below + [jnp.where(first, h[z], zero) for z in range(zlen)] + above
     for z, layer in enumerate(spread_layers(layers)):
         out[z] = layer
 
@@ -437,6 +448,16 @@
     for low in range(first, lax.axis_size(axis) - 1, 2):
         pairs += [(low, low + 1), (low + 1, low)]
     return lax.ppermute(value, axis, pairs)
+
+
+def shared(value):
+    cores, size = lax.axis_size("load"), lax.axis_size("sz")
+    pairs = []
+    for core in range(cores):
+        for low in range(core % 2, size - 1, 2):
+            ends = core * size + low, core * size + low + 1
+            pairs += [ends, ends[::-1]]
+    return lax.ppermute(value, ("load", "sz"), pairs)
 
 
 def body(displacements, density, solid, fixed):
@@ -478,16 +499,14 @@
         (z_in, y_in, disp, fixed, *inner),
         scratch=[nodes(2), nodes(2), pltpu.VMEM((ylen + 2 * TILE, xlen), jnp.float32)],
     )
+    b_in = swapped(b_send, "sy", 1)
     a_in = swapped(a_send, "sy", 0)
-    b_in = swapped(b_send, "sy", 1)
-    h, a_send, b_send = call(
-        lambda *refs: rows_kernel(loads, comps, *refs),
-        [(zlen, ylen, xlen), (REACH, ylen, xlen), (REACH, ylen, xlen)],
-        (own, known, inner[-1], a_in, b_in),
-    )
-    a_in = swapped(a_send, "sz", 0)
-    b_in = swapped(b_send, "sz", 1)
-    (part,) = call(layers_kernel, [(zlen, ylen, xlen)], (h, a_in, b_in))
+    (h,) = call(
+        lambda *refs: rows_kernel(loads, comps, *refs), [(zlen, ylen, xlen)], (own, known, inner[-1], b_in, a_in)
+    )
+    parts = lax.all_gather(h, "load", axis=0)
+    h, z_send = call(total_kernel, [(zlen, ylen, xlen), (REACH, ylen, xlen)], (parts,))
+    (part,) = call(layers_kernel, [(zlen, ylen, xlen)], (h, shared(z_send)))
     parts = lax.all_gather(part, "load", axis=0)
     (out,) = call(sum_kernel, [(zlen, ylen, xlen)], (parts,))
     return out

time: 30.6 us -> 31.9 us (1.042)
  the two profiles are of different devices: /device:TPU:19 before, /device:TPU:0 now
where the time goes in v6:
time: 31.9 us; the launch traced here: 31.7 us
  starting transfers between devices  11.2 us (35%)
  waiting for transfers between devices  9.86 us (31%)
  Pallas kernels  6.5 us (20%)
  blocking collectives  3.99 us (13%)
    pallas_call x7, Pallas kernels, call(): pl.pallas_call(kernel, out_shape=shapes, in_specs=[pl.BlockSpec(memory_sp...  6.5 us
    ppermute x2, starting transfers between devices, swapped(): return lax.ppermute(value, axis, pairs)  5.11 us
    ppermute x2, waiting for transfers between devices, moved(): return lax.ppermute(value, axes if len(axes) > 1 else axes[0], pairs)  4.38 us
    ppermute x1, starting transfers between devices, shared(): return lax.ppermute(value, ('load', 'sz'), pairs)  3.53 us
    ppermute x1, waiting for transfers between devices, shared(): return lax.ppermute(value, ('load', 'sz'), pairs)  2.97 us
    ppermute x2, starting transfers between devices, moved(): return lax.ppermute(value, axes if len(axes) > 1 else axes[0], pairs)  2.58 us
    ppermute x2, waiting for transfers between devices, swapped(): return lax.ppermute(value, axis, pairs)  2.5 us
    all_gather x1, blocking collectives, body(): parts = lax.all_gather(part, 'load', axis=0)  1.99 us
  transfers between devices with their start and end apart: 5, of which 4 were waited for; matrix products, arithmetic and copies ran while one was open for 0% of the time, Pallas kernels for 9%

profile of v6, /device:TPU:0, one launch (start us, length us, event | category | flops | bytes accessed | tf_op | source)
XLA Modules:
  0.0 31.7 jit_solution(14830165282320693341)
XLA Ops:
  0.0 1.3 %shard_map.46 = (f32[2,3,4,16,512]{4,3,2,1,0:T(8,128)S(1)}, s32[4,16,512]{2,1,0:T(8,128)S(1)}, f32[4,16,512]{2,1,0:T(8,128)S(1)}, s32[4,16,512]{2,1,0:T(8,128)S(...) custom-call(f32[2,3,4,16,512]{4,3,2,1,0:T(8,128)} %disp_hbm.1, s32[4,16,512]{2,1,0:T(8,128)} %fixed_hbm.1, ...), custom_call_target="tpu_custom_call" | custom-call | tf_op jit(solution)/shard_map/pallas_call | solution.py:425
  1.3 1.3 %collective-permute-start = (f32[6,16,512]{2,1,0:T(8,128)S(1)}, f32[6,16,512]{2,1,0:T(8,128)S(1)}, u32[]{:S(2)}, u32[]{:S(2)}) collective-permute-start(f32[6,16,512]{2,1,0:T(8,128)S(1)} %get-tuple-element.24), channel_id=1, source_target_pairs={{1,0},{2,1},{3,2},{5,4},{6,5},{7,6},{9,8},{10,9},{11,10},{13,12},{... | collective-permute-start | bytes 589832 | tf_op jit(solution)/shard_map/ppermute | solution.py:443
  2.6 1.3 %collective-permute-start.1 = (f32[24,512]{1,0:T(8,128)S(1)}, f32[24,512]{1,0:T(8,128)S(1)}, u32[]{:S(2)}, u32[]{:S(2)}) collective-permute-start(f32[24,512]{1,0:T(8,128)S(1)} %get-tuple-element.25), channel_id=1, source_target_pairs={{4,0},{8,4},{12,8},{5,1},{9,5},{13,9},{6,2},{10,6},{14,10},{7,3},{... | collective-permute-start | bytes 147464 | tf_op jit(solution)/shard_map/ppermute | solution.py:443
  3.9 2.8 %shard_map.47 = (f32[4,16,512]{2,1,0:T(8,128)S(1)}, f32[2,24,512]{2,1,0:T(8,128)S(1)}, f32[2,9,512]{2,1,0:T(8,128)S(1)}, f32[6,16,512]{2,1,0:T(8,128)S(1)}, f32[...) custom-call(f32[2,3,4,16,512]{4,3,2,1,0:T(8,128)S(1)} %get-tuple-element.26.refs_0_.refs_2_, ...), custom_call_target="tpu_custom_call" | custom-call | tf_op jit(solution)/shard_map/pallas_call | solution.py:425
  6.7 2.8 %collective-permute-done.1.refs_1_ = f32[24,512]{1,0:T(8,128)S(1)} collective-permute-done((f32[24,512]{1,0:T(8,128)S(1)}, f32[24,512]{1,0:T(8,128)S(1)}, u32[]{:S(2)}, u32[]{:S(2)}) %collective-permute-start.1) | collective-permute-done | bytes 49184 | tf_op jit(solution)/shard_map/ppermute | solution.py:443
  9.5 1.6 %collective-permute-done.refs_0_ = f32[6,16,512]{2,1,0:T(8,128)S(1)} collective-permute-done((f32[6,16,512]{2,1,0:T(8,128)S(1)}, f32[6,16,512]{2,1,0:T(8,128)S(1)}, u32[]{:S(2)}, u32[]{:S(2)}) %collective-permute-start) | collective-permute-done | bytes 196640 | tf_op jit(solution)/shard_map/ppermute | solution.py:443
  11.1 1.2 %shard_map.48 = (f32[4,16,512]{2,1,0:T(8,128)S(1)}, f32[32,512]{1,0:T(8,128)S(1)}, f32[24,512]{1,0:T(8,128)S(1)}, f32[24,512]{1,0:T(8,128)S(1)}) custom-call(f32[6,16,512]{2,1,0:T(8,128)S(1)} %collective-permute-done.refs_0_, f32[24,512]{1,0:T(8,128)S(1)} %collective-permute-done.1.refs_1_, f32[2,3,4,16,512]{4,3,2,1,0:T(8,128)S(1)} %get-tuple-element.26.refs_0_.refs_2_, ...), custom_call_target="tpu_custom_call" | custom-call | tf_op jit(solution)/shard_map/pallas_call | solution.py:425
  12.3 0.7 %collective-permute-start.2 = (f32[24,512]{1,0:T(8,128)S(1)}, f32[24,512]{1,0:T(8,128)S(1)}, u32[]{:S(2)}, u32[]{:S(2)}) collective-permute-start(f32[24,512]{1,0:T(8,128)S(1)} %get-tuple-element.39), channel_id=1, source_target_pairs={{4,8},{8,4},{5,9},{9,5},{6,10},{10,6},{7,11},{11,7},{20,24},{24,20... | collective-permute-start | bytes 147464 | tf_op jit(solution)/shard_map/ppermute | solution.py:450
  13.0 4.4 %collective-permute-start.3 = (f32[24,512]{1,0:T(8,128)S(1)}, f32[24,512]{1,0:T(8,128)S(1)}, u32[]{:S(2)}, u32[]{:S(2)}) collective-permute-start(f32[24,512]{1,0:T(8,128)S(1)} %get-tuple-element.40), channel_id=1, source_target_pairs={{0,4},{4,0},{8,12},{12,8},{1,5},{5,1},{9,13},{13,9},{2,6},{6,2},{1... | collective-permute-start | bytes 147464 | tf_op jit(solution)/shard_map/ppermute | solution.py:450
  17.4 0.0 collective-permute-done.2.refs_3_
  17.4 2.5 %collective-permute-done.3.refs_4_ = f32[24,512]{1,0:T(8,128)S(1)} collective-permute-done((f32[24,512]{1,0:T(8,128)S(1)}, f32[24,512]{1,0:T(8,128)S(1)}, u32[]{:S(2)}, u32[]{:S(2)}) %collective-permute-start.3) | collective-permute-done | bytes 49184 | tf_op jit(solution)/shard_map/ppermute | solution.py:450
  19.9 0.5 %shard_map.49 = f32[4,16,512]{2,1,0:T(8,128)S(1)} custom-call(f32[4,16,512]{2,1,0:T(8,128)S(1)} %get-tuple-element.37.refs_0_, f32[32,512]{1,0:T(8,128)S(1)} %get-tuple-element.38.refs_1_, f32[8,512]{1,0:T(8,128)S(1)} %get-tuple-element.36.refs_10_.refs_2_, f32[24,512]{1,0:T(8,128)S(1)} %collective-permute-done.2.refs_3_, ...), custom_call_target="tpu_custom_call" | custom-call | tf_op jit(solution)/shard_map/pallas_call | solution.py:425
  20.4 2.0 %all-gather = f32[8,16,512]{2,1,0:T(8,128)S(1)} all-gather(f32[4,16,512]{2,1,0:T(8,128)S(1)} %shard_map.49), channel_id=2, replica_groups=mesh['load'=2,'sy'=4,'sz'=4] {'load'}, dimensions={0}, use_global_device_ids=true | all-gather | bytes 393216 | tf_op jit(solution)/shard_map/all_gather | solution.py:507
  22.4 3.5 %collective-permute-start.4 = (f32[3,16,512]{2,1,0:T(8,128)S(1)}, f32[3,16,512]{2,1,0:T(8,128)S(1)}, u32[]{:S(2)}, u32[]{:S(2)}) collective-permute-start(f32[3,16,512]{2,1,0:T(8,128)S(1)} %get-tuple-element.42), channel_id=1, source_target_pairs={{0,1},{1,0},{2,3},{3,2},{17,18},{18,17},{4,5},{5,4},{6,7},{7,6},{2... | collective-permute-start | bytes 294920 | tf_op jit(solution)/shard_map/ppermute | solution.py:460
  26.0 3.0 %collective-permute-done.4.z_in = f32[3,16,512]{2,1,0:T(8,128)S(1)} collective-permute-done((f32[3,16,512]{2,1,0:T(8,128)S(1)}, f32[3,16,512]{2,1,0:T(8,128)S(1)}, u32[]{:S(2)}, u32[]{:S(2)}) %collective-permute-start.4) | collective-permute-done | bytes 98336 | tf_op jit(solution)/shard_map/ppermute | solution.py:460
  29.0 2.0 %all-gather.1 = f32[8,16,512]{2,1,0:T(8,128)S(1)} all-gather(f32[4,16,512]{2,1,0:T(8,128)S(1)} %shard_map.51), channel_id=3, replica_groups=mesh['load'=2,'sy'=4,'sz'=4] {'load'}, dimensions={0}, use_global_device_ids=true | all-gather | bytes 393216 | tf_op jit(solution)/shard_map/all_gather | solution.py:510
  31.0 0.7 %shard_map.52 = f32[4,16,512]{2,1,0:T(8,128)} custom-call(f32[2,4,16,512]{3,2,1,0:T(8,128)S(1)} %bitcast.2), custom_call_target="tpu_custom_call" | custom-call | tf_op jit(solution)/shard_map/pallas_call | solution.py:425
  (2 shorter events, 0.1 us)
Async XLA Ops:
  1.3 9.8 %collective-permute-start = (f32[6,16,512]{2,1,0:T(8,128)S(1)}, f32[6,16,512]{2,1,0:T(8,128)S(1)}, u32[]{:S(2)}, u32[]{:S(2)}) collective-permute-start(f32[6,16,512]{2,1,0:T(8,128)S(1)} %get-tuple-element.24), channel_id=1, source_target_pairs={{1,0},{2,1},{3,2},{5,4},{6,5},{7,6},{9,8},{10,9},{11,10},{13,12},{... | collective-permute-start | bytes 589832 | tf_op jit(solution)/shard_map/ppermute | solution.py:443
  2.6 6.9 %collective-permute-start.1 = (f32[24,512]{1,0:T(8,128)S(1)}, f32[24,512]{1,0:T(8,128)S(1)}, u32[]{:S(2)}, u32[]{:S(2)}) collective-permute-start(f32[24,512]{1,0:T(8,128)S(1)} %get-tuple-element.25), channel_id=1, source_target_pairs={{4,0},{8,4},{12,8},{5,1},{9,5},{13,9},{6,2},{10,6},{14,10},{7,3},{... | collective-permute-start | bytes 147464 | tf_op jit(solution)/shard_map/ppermute | solution.py:443
  12.3 5.1 %collective-permute-start.2 = (f32[24,512]{1,0:T(8,128)S(1)}, f32[24,512]{1,0:T(8,128)S(1)}, u32[]{:S(2)}, u32[]{:S(2)}) collective-permute-start(f32[24,512]{1,0:T(8,128)S(1)} %get-tuple-element.39), channel_id=1, source_target_pairs={{4,8},{8,4},{5,9},{9,5},{6,10},{10,6},{7,11},{11,7},{20,24},{24,20... | collective-permute-start | bytes 147464 | tf_op jit(solution)/shard_map/ppermute | solution.py:450
  13.0 7.0 %collective-permute-start.3 = (f32[24,512]{1,0:T(8,128)S(1)}, f32[24,512]{1,0:T(8,128)S(1)}, u32[]{:S(2)}, u32[]{:S(2)}) collective-permute-start(f32[24,512]{1,0:T(8,128)S(1)} %get-tuple-element.40), channel_id=1, source_target_pairs={{0,4},{4,0},{8,12},{12,8},{1,5},{5,1},{9,13},{13,9},{2,6},{6,2},{1... | collective-permute-start | bytes 147464 | tf_op jit(solution)/shard_map/ppermute | solution.py:450
  22.4 6.5 %collective-permute-start.4 = (f32[3,16,512]{2,1,0:T(8,128)S(1)}, f32[3,16,512]{2,1,0:T(8,128)S(1)}, u32[]{:S(2)}, u32[]{:S(2)}) collective-permute-start(f32[3,16,512]{2,1,0:T(8,128)S(1)} %get-tuple-element.42), channel_id=1, source_target_pairs={{0,1},{1,0},{2,3},{3,2},{17,18},{18,17},{4,5},{5,4},{6,7},{7,6},{2... | collective-permute-start | bytes 294920 | tf_op jit(solution)/shard_map/ppermute | solution.py:460

commit v7 on v5

--- a/solution.py
+++ b/solution.py
@@ -280,7 +280,7 @@
 
 
 def outer_kernel(
-    shape, z_in, y_in, disp, fixed, own_in, line, sends, last_plus, last_diff, last_factor, edge, own, known, a_out, b_out, plus, diff, quotient
+    shape, z_in, y_in, disp, fixed, own_in, line, sends, last_plus, last_diff, last_factor, edge, share, plus, diff, quotient
 ):
     loads, comps, zlen, ylen, xlen = shape
     planes = loads * comps
@@ -321,12 +321,12 @@
     rising = jnp.maximum(row - (TILE - 1 - ROWS), 0).astype(jnp.float32)
     ups, downs = [], []
     for z in range(inner):
-        own[z] = own_in[z]
-        own[z, ylen - TILE :] += rising * last[z : z + 1]
+        share[ylen * z : ylen * (z + 1)] = own_in[z]
+        share[ylen * (z + 1) - TILE : ylen * (z + 1)] += rising * last[z : z + 1]
         here = sends[0, REACH * z : REACH * (z + 1)]
         ups += [here[r : r + 1] + float(REACH - r) * last[z : z + 1] for r in range(REACH)]
         downs.append(sends[1, REACH * z : REACH * (z + 1)])
-    own[inner] = spread_x(spread_y(quotient, ylen))
+    share[ylen * inner : ylen * zlen] = spread_x(spread_y(quotient, ylen))
     ahead, back = to_neighbours(quotient, ylen)
     ends = spread_x(jnp.concatenate(ahead + back + [zeros[:2]], axis=0))
     ups += [ends[: REACH - 1], edge[inner:zlen]]
@@ -338,41 +338,71 @@
     next_row = [y_in[(k + 1) * zlen - 1 : (k + 1) * zlen] for k in range(planes)]
     over_last = [z_in[case * comps + comp, ylen - 1 : ylen] for case, comp in pairs]
     over_first = [z_in[case * comps + comp, 0:1] for case, comp in pairs]
-    rows = here_last + over_last + next_row + here_first + over_first
-    known[: len(rows)] = jnp.concatenate(rows, axis=0)
-    known[len(rows) :] = jnp.zeros((known.shape[0] - len(rows), xlen), jnp.float32)
-    up = jnp.concatenate(ups + here_last + over_last, axis=0)
-    down = jnp.concatenate(downs + over_first + [jnp.zeros((planes, xlen), jnp.float32)], axis=0)
+    rows = ups + downs + here_last + over_last + next_row + here_first + over_first
+    rows.append(jnp.zeros((share.shape[0] - ylen * zlen - 2 * REACH * zlen - 5 * planes, xlen), jnp.float32))
+    share[ylen * zlen :] = jnp.concatenate(rows, axis=0)
+
+
+class Shared:
+    def __init__(self, shape):
+        self.loads, self.comps, self.zlen, self.ylen, self.xlen = shape
+        self.planes = self.loads * self.comps
+        self.reach = REACH * self.zlen
+        self.ups = self.ylen * self.zlen
+        self.downs = self.ups + self.reach
+        self.nodes = self.downs + self.reach
+        self.rows = -(-(self.nodes + 5 * self.planes) // TILE) * TILE
+
+    def group(self, parts, core, k):
+        return parts[core, self.nodes + k * self.planes : self.nodes + (k + 1) * self.planes]
+
+    def payload(self, cores):
+        return -(-(self.reach + 2 * self.planes * cores) // TILE) * TILE
+
+
+def meet_kernel(at, parts, b_out, a_out):
+    cores = parts.shape[0]
+    size = a_out.shape[0]
+    ups = sum(parts[core, at.ups : at.downs - 1] for core in range(cores))
+    downs = sum(parts[core, at.downs : at.nodes] for core in range(cores))
+    up = [ups, parts[0, at.downs - 1 : at.downs]] + [at.group(parts, core, k) for k in range(2) for core in range(cores)]
+    down = [downs] + [at.group(parts, core, 4) for core in range(cores)]
+    up.append(jnp.zeros((size - at.reach - 2 * cores * at.planes, at.xlen), jnp.float32))
+    down.append(jnp.zeros((size - at.reach - cores * at.planes, at.xlen), jnp.float32))
+    up, down = (jnp.concatenate([piece for piece in rows if piece.shape[0]], axis=0) for rows in (up, down))
     even = lax.axis_index("sy") % 2 == 0
     a_out[...] = jnp.where(even, up, down)
     b_out[...] = jnp.where(even, down, up)
 
 
-def rows_kernel(loads, comps, own, known, edge, a_in, b_in, h_out, a_out, b_out):
-    zlen, ylen, xlen = own.shape
-    planes = loads * comps
+def rows_kernel(at, parts, edge, b_in, a_in, h_out, a_out, b_out):
+    zlen, ylen, xlen = h_out.shape
+    cores, loads, comps, ends = parts.shape[0], at.loads, at.comps, at.reach
+    cases = cores * loads
     even = lax.axis_index("sy") % 2 == 0
     from_low = jnp.where(even, b_in[...], a_in[...])
     from_high = jnp.where(even, a_in[...], b_in[...])
-    ends = REACH * zlen
+
+    def here(k):
+        return [at.group(parts, core, k) for core in range(cores)]
+
+    def there(rows, k):
+        first = ends + k * cores * at.planes
+        return [rows[first + core * at.planes : first + (core + 1) * at.planes] for core in range(cores)]
 
     def nodes(first, second, comp):
         part = slice(comp * loads, (comp + 1) * loads)
-        rows = jnp.concatenate([first[part], second[part]], axis=0)
-        return split_x(jnp.concatenate([rows, rows], axis=0))
+        return split_x(jnp.concatenate([value[part] for value in first + second], axis=0))
 
     def face(near_own, near_in, far_own, far_in, comp):
         whole, change = nodes(near_own, near_in, comp)
         whole_next, change_next = nodes(far_own, far_in, comp)
         return whole + whole_next, change + change_next, whole_next - whole, change_next - change
 
-    here_last, over_last, next_row, here_first, over_first = (known[planes * k : planes * (k + 1)] for k in range(5))
-    low_last, low_over = from_low[ends : ends + planes], from_low[ends + planes : ends + 2 * planes]
-    next_over = from_high[ends : ends + planes]
-    low = [face(here_last, low_last, next_row, here_first, comp) for comp in range(comps)]
-    high = [face(over_last, low_over, next_over, over_first, comp) for comp in range(comps)]
+    low = [face(here(0), there(from_low, 0), here(2), here(3), comp) for comp in range(comps)]
+    high = [face(here(1), there(from_low, 1), there(from_high, 0), here(4), comp) for comp in range(comps)]
     energy = quadratic(low, high, mode_weights())
-    lines = [sum(energy[loads * k + case : loads * k + case + 1] for case in range(loads)) for k in range(2)]
+    lines = [sum(energy[cases * k + case : cases * k + case + 1] for case in range(cases)) for k in range(2)]
     lines = [lines[0] * edge[zlen - 1 : zlen], lines[1] * from_low[ends - 1 : ends]]
     lines = spread_x(jnp.concatenate(lines + [jnp.zeros((TILE - 2, xlen), jnp.float32)], axis=0))
 
@@ -387,7 +417,7 @@
         if z == zlen - 1:
             head = jnp.where(row == REACH - 1, 0.0, head) + falling * lines[1:2]
             tail = tail + rising * lines[0:1]
-        h_out[z] = own[z]
+        h_out[z] = sum(parts[core, ylen * z : ylen * (z + 1)] for core in range(cores))
         h_out[z, :TILE] += head
         h_out[z, ylen - TILE :] += tail
     top = (zlen - REACH) * (lax.axis_index("sz") % 2 == 0).astype(jnp.int32)
@@ -405,8 +435,8 @@
         out[z] = layer
 
 
-def sum_kernel(parts, out):
-    out[...] = parts[0] + parts[1]
+def pick_kernel(parts, out):
+    out[...] = parts[parts.shape[0] - 1]
 
 
 def call(kernel, outs, args, scratch=(), space=pltpu.VMEM):
@@ -433,10 +463,11 @@
 
 
 def swapped(value, axis, first):
+    cores, size = lax.axis_size("load"), lax.axis_size(axis)
     pairs = []
-    for low in range(first, lax.axis_size(axis) - 1, 2):
+    for low in range((cores - 1) * size + first, cores * size - 1, 2):
         pairs += [(low, low + 1), (low + 1, low)]
-    return lax.ppermute(value, axis, pairs)
+    return lax.ppermute(value, ("load", axis), pairs)
 
 
 def body(displacements, density, solid, fixed):
@@ -471,25 +502,28 @@
         (disp, fixed, density, solid),
         scratch=[nodes(zlen), nodes(zlen), pltpu.VMEM((zlen - 1, ylen + 2 * TILE, xlen), jnp.float32)],
     )
-    size = REACH * zlen + 2 * planes
-    own, known, a_send, b_send = call(
+    at = Shared(displacements.shape)
+    (share,) = call(
         lambda *refs: outer_kernel(displacements.shape, *refs),
-        [(zlen, ylen, xlen), (-(-5 * planes // TILE) * TILE, xlen), (size, xlen), (size, xlen)],
+        [(at.rows, xlen)],
         (z_in, y_in, disp, fixed, *inner),
         scratch=[nodes(2), nodes(2), pltpu.VMEM((ylen + 2 * TILE, xlen), jnp.float32)],
     )
+    parts = lax.all_gather(share, "load", axis=0)
+    size = at.payload(parts.shape[0])
+    b_send, a_send = call(lambda *refs: meet_kernel(at, *refs), [(size, xlen), (size, xlen)], (parts,))
+    b_in = swapped(b_send, "sy", 1)
     a_in = swapped(a_send, "sy", 0)
-    b_in = swapped(b_send, "sy", 1)
     h, a_send, b_send = call(
-        lambda *refs: rows_kernel(loads, comps, *refs),
+        lambda *refs: rows_kernel(at, *refs),
         [(zlen, ylen, xlen), (REACH, ylen, xlen), (REACH, ylen, xlen)],
-        (own, known, inner[-1], a_in, b_in),
+        (parts, inner[-1], b_in, a_in),
     )
     a_in = swapped(a_send, "sz", 0)
     b_in = swapped(b_send, "sz", 1)
     (part,) = call(layers_kernel, [(zlen, ylen, xlen)], (h, a_in, b_in))
     parts = lax.all_gather(part, "load", axis=0)
-    (out,) = call(sum_kernel, [(zlen, ylen, xlen)], (parts,))
+    (out,) = call(pick_kernel, [(zlen, ylen, xlen)], (parts,))
     return out
 
 

time: 30.6 us -> 34.6 us (1.13)
  the two profiles are of different devices: /device:TPU:19 before, /device:TPU:21 now
where the time goes in v7:
time: 34.6 us; the launch traced here: 34.3 us
  starting transfers between devices  15.9 us (46%)
  waiting for transfers between devices  6.69 us (19%)
  Pallas kernels  6.56 us (19%)
  blocking collectives  5.01 us (14%)
    ppermute x4, starting transfers between devices, swapped(): return lax.ppermute(value, ('load', axis), pairs)  10.8 us
    ppermute x4, waiting for transfers between devices, swapped(): return lax.ppermute(value, ('load', axis), pairs)  6.69 us
    pallas_call x7, Pallas kernels, call(): pl.pallas_call(kernel, out_shape=shapes, in_specs=[pl.BlockSpec(memory_sp...  6.56 us
    ppermute x2, starting transfers between devices, moved(): return lax.ppermute(value, axes if len(axes) > 1 else axes[0], pairs)  5.14 us
    all_gather x1, blocking collectives, body(): parts = lax.all_gather(share, 'load', axis=0)  3.02 us
    all_gather x1, blocking collectives, body(): parts = lax.all_gather(part, 'load', axis=0)  1.99 us
  transfers between devices with their start and end apart: 6, of which 4 were waited for; matrix products, arithmetic and copies ran while one was open for 0% of the time, Pallas kernels for 8%

profile of v7, /device:TPU:21, one launch (start us, length us, event | category | flops | bytes accessed | tf_op | source)
XLA Modules:
  0.0 34.3 jit_solution(5503776299055361246)
XLA Ops:
  0.0 1.3 %shard_map.46 = (f32[2,3,4,16,512]{4,3,2,1,0:T(8,128)S(1)}, s32[4,16,512]{2,1,0:T(8,128)S(1)}, f32[4,16,512]{2,1,0:T(8,128)S(1)}, s32[4,16,512]{2,1,0:T(8,128)S(...) custom-call(f32[2,3,4,16,512]{4,3,2,1,0:T(8,128)} %disp_hbm.1, s32[4,16,512]{2,1,0:T(8,128)} %fixed_hbm.1, ...), custom_call_target="tpu_custom_call" | custom-call | tf_op jit(solution)/shard_map/pallas_call | solution.py:444
  1.3 2.1 %collective-permute-start = (f32[6,16,512]{2,1,0:T(8,128)S(1)}, f32[6,16,512]{2,1,0:T(8,128)S(1)}, u32[]{:S(2)}, u32[]{:S(2)}) collective-permute-start(f32[6,16,512]{2,1,0:T(8,128)S(1)} %get-tuple-element.23), channel_id=1, source_target_pairs={{1,0},{2,1},{3,2},{5,4},{6,5},{7,6},{9,8},{10,9},{11,10},{13,12},{... | collective-permute-start | bytes 589832 | tf_op jit(solution)/shard_map/ppermute | solution.py:462
  3.4 3.1 %collective-permute-start.1 = (f32[24,512]{1,0:T(8,128)S(1)}, f32[24,512]{1,0:T(8,128)S(1)}, u32[]{:S(2)}, u32[]{:S(2)}) collective-permute-start(f32[24,512]{1,0:T(8,128)S(1)} %get-tuple-element.24), channel_id=1, source_target_pairs={{4,0},{8,4},{12,8},{5,1},{9,5},{13,9},{6,2},{10,6},{14,10},{7,3},{... | collective-permute-start | bytes 147464 | tf_op jit(solution)/shard_map/ppermute | solution.py:462
  6.4 2.8 %shard_map.47 = (f32[4,16,512]{2,1,0:T(8,128)S(1)}, f32[2,24,512]{2,1,0:T(8,128)S(1)}, f32[2,9,512]{2,1,0:T(8,128)S(1)}, f32[6,16,512]{2,1,0:T(8,128)S(1)}, f32[...) custom-call(f32[2,3,4,16,512]{4,3,2,1,0:T(8,128)S(1)} %get-tuple-element.25.refs_0_.refs_2_, ...), custom_call_target="tpu_custom_call" | custom-call | tf_op jit(solution)/shard_map/pallas_call | solution.py:444
  9.3 0.0 collective-permute-done.1.refs_1_
  9.3 0.0 collective-permute-done.refs_0_
  9.3 1.2 %shard_map.48 = f32[120,512]{1,0:T(8,128)S(1)} custom-call(f32[6,16,512]{2,1,0:T(8,128)S(1)} %collective-permute-done.refs_0_, f32[24,512]{1,0:T(8,128)S(1)} %collective-permute-done.1.refs_1_, f32[2,3,4,16,512]{4,3,2,1,0:T(8,128)S(1)} %get-tuple-element.25.refs_0_.refs_2_, s32[4,16,512]{2,1,0:T(8,128)S(1)} %get-tuple-element.26.refs_1_.refs_3_, ...), custom_call_target="tpu_custom_call" | custom-call | tf_op jit(solution)/shard_map/pallas_call | solution.py:444
  10.5 3.0 %all-gather = f32[240,512]{1,0:T(8,128)S(1)} all-gather(f32[120,512]{1,0:T(8,128)S(1)} %shard_map.48), channel_id=2, replica_groups=mesh['load'=2,'sy'=4,'sz'=4] {'load'}, dimensions={0}, use_global_device_ids=true | all-gather | bytes 737280 | tf_op jit(solution)/shard_map/all_gather | solution.py:512
  13.6 3.7 %collective-permute-start.2 = (f32[40,512]{1,0:T(8,128)S(1)}, f32[40,512]{1,0:T(8,128)S(1)}, u32[]{:S(2)}, u32[]{:S(2)}) collective-permute-start(f32[40,512]{1,0:T(8,128)S(1)} %get-tuple-element.36), channel_id=1, source_target_pairs={{20,24},{24,20},{21,25},{25,21},{22,26},{26,22},{23,27},{27,23}} | collective-permute-start | bytes 245768 | tf_op jit(solution)/shard_map/ppermute | solution.py:470
  17.3 1.9 %collective-permute-start.3 = (f32[40,512]{1,0:T(8,128)S(1)}, f32[40,512]{1,0:T(8,128)S(1)}, u32[]{:S(2)}, u32[]{:S(2)}) collective-permute-start(f32[40,512]{1,0:T(8,128)S(1)} %get-tuple-element.37), channel_id=1, source_target_pairs={{16,20},{20,16},{24,28},{28,24},{17,21},{21,17},{25,29},{29,25},{1... | collective-permute-start | bytes 245768 | tf_op jit(solution)/shard_map/ppermute | solution.py:470
  19.2 0.4 %collective-permute-done.2.refs_2_ = f32[40,512]{1,0:T(8,128)S(1)} collective-permute-done((f32[40,512]{1,0:T(8,128)S(1)}, f32[40,512]{1,0:T(8,128)S(1)}, u32[]{:S(2)}, u32[]{:S(2)}) %collective-permute-start.2) | collective-permute-done | bytes 81952 | tf_op jit(solution)/shard_map/ppermute | solution.py:470
  19.7 2.8 %collective-permute-done.3.refs_3_ = f32[40,512]{1,0:T(8,128)S(1)} collective-permute-done((f32[40,512]{1,0:T(8,128)S(1)}, f32[40,512]{1,0:T(8,128)S(1)}, u32[]{:S(2)}, u32[]{:S(2)}) %collective-permute-start.3) | collective-permute-done | bytes 81952 | tf_op jit(solution)/shard_map/ppermute | solution.py:470
  22.5 0.5 %shard_map.50 = (f32[4,16,512]{2,1,0:T(8,128)S(1)}, f32[3,16,512]{2,1,0:T(8,128)S(1)}, f32[3,16,512]{2,1,0:T(8,128)S(1)}) custom-call(f32[2,120,512]{2,1,0:T(8,128)S(1)} %bitcast.3, f32[8,512]{1,0:T(8,128)S(1)} %get-tuple-element.35.refs_10_.refs_1_, f32[40,512]{1,0:T(8,128)S(1)} %collective-permute-done.2.refs_2_, f32[40,512]{1,0:T(8,128)S(1)} %collective-permute-done.3.refs_3_), custom_call_target="tpu_custom_call" | custom-call | tf_op jit(solution)/shard_map/pallas_call | solution.py:444
  23.0 3.2 %collective-permute-start.4 = (f32[3,16,512]{2,1,0:T(8,128)S(1)}, f32[3,16,512]{2,1,0:T(8,128)S(1)}, u32[]{:S(2)}, u32[]{:S(2)}) collective-permute-start(f32[3,16,512]{2,1,0:T(8,128)S(1)} %get-tuple-element.39), channel_id=1, source_target_pairs={{16,17},{17,16},{18,19},{19,18},{20,21},{21,20},{22,23},{23,22},{2... | collective-permute-start | bytes 294920 | tf_op jit(solution)/shard_map/ppermute | solution.py:470
  26.2 1.9 %collective-permute-start.5 = (f32[3,16,512]{2,1,0:T(8,128)S(1)}, f32[3,16,512]{2,1,0:T(8,128)S(1)}, u32[]{:S(2)}, u32[]{:S(2)}) collective-permute-start(f32[3,16,512]{2,1,0:T(8,128)S(1)} %get-tuple-element.40), channel_id=1, source_target_pairs={{17,18},{18,17},{21,22},{22,21},{25,26},{26,25},{29,30},{30,29}} | collective-permute-start | bytes 294920 | tf_op jit(solution)/shard_map/ppermute | solution.py:470
  28.2 0.2 collective-permute-done.4.a_in
  28.4 3.2 %collective-permute-done.5.b_in = f32[3,16,512]{2,1,0:T(8,128)S(1)} collective-permute-done((f32[3,16,512]{2,1,0:T(8,128)S(1)}, f32[3,16,512]{2,1,0:T(8,128)S(1)}, u32[]{:S(2)}, u32[]{:S(2)}) %collective-permute-start.5) | collective-permute-done | bytes 98336 | tf_op jit(solution)/shard_map/ppermute | solution.py:470
  31.6 2.0 %all-gather.1 = f32[8,16,512]{2,1,0:T(8,128)S(1)} all-gather(f32[4,16,512]{2,1,0:T(8,128)S(1)} %shard_map.51), channel_id=3, replica_groups=mesh['load'=2,'sy'=4,'sz'=4] {'load'}, dimensions={0}, use_global_device_ids=true | all-gather | bytes 393216 | tf_op jit(solution)/shard_map/all_gather | solution.py:525
  33.6 0.7 %shard_map.52 = f32[4,16,512]{2,1,0:T(8,128)} custom-call(f32[2,4,16,512]{3,2,1,0:T(8,128)S(1)} %bitcast.4), custom_call_target="tpu_custom_call" | custom-call | tf_op jit(solution)/shard_map/pallas_call | solution.py:444
  (2 shorter events, 0.1 us)
Async XLA Ops:
  1.3 8.0 %collective-permute-start = (f32[6,16,512]{2,1,0:T(8,128)S(1)}, f32[6,16,512]{2,1,0:T(8,128)S(1)}, u32[]{:S(2)}, u32[]{:S(2)}) collective-permute-start(f32[6,16,512]{2,1,0:T(8,128)S(1)} %get-tuple-element.23), channel_id=1, source_target_pairs={{1,0},{2,1},{3,2},{5,4},{6,5},{7,6},{9,8},{10,9},{11,10},{13,12},{... | collective-permute-start | bytes 589832 | tf_op jit(solution)/shard_map/ppermute | solution.py:462
  3.4 5.9 %collective-permute-start.1 = (f32[24,512]{1,0:T(8,128)S(1)}, f32[24,512]{1,0:T(8,128)S(1)}, u32[]{:S(2)}, u32[]{:S(2)}) collective-permute-start(f32[24,512]{1,0:T(8,128)S(1)} %get-tuple-element.24), channel_id=1, source_target_pairs={{4,0},{8,4},{12,8},{5,1},{9,5},{13,9},{6,2},{10,6},{14,10},{7,3},{... | collective-permute-start | bytes 147464 | tf_op jit(solution)/shard_map/ppermute | solution.py:462
  13.6 6.1 %collective-permute-start.2 = (f32[40,512]{1,0:T(8,128)S(1)}, f32[40,512]{1,0:T(8,128)S(1)}, u32[]{:S(2)}, u32[]{:S(2)}) collective-permute-start(f32[40,512]{1,0:T(8,128)S(1)} %get-tuple-element.36), channel_id=1, source_target_pairs={{20,24},{24,20},{21,25},{25,21},{22,26},{26,22},{23,27},{27,23}} | collective-permute-start | bytes 245768 | tf_op jit(solution)/shard_map/ppermute | solution.py:470
  17.3 5.2 %collective-permute-start.3 = (f32[40,512]{1,0:T(8,128)S(1)}, f32[40,512]{1,0:T(8,128)S(1)}, u32[]{:S(2)}, u32[]{:S(2)}) collective-permute-start(f32[40,512]{1,0:T(8,128)S(1)} %get-tuple-element.37), channel_id=1, source_target_pairs={{16,20},{20,16},{24,28},{28,24},{17,21},{21,17},{25,29},{29,25},{1... | collective-permute-start | bytes 245768 | tf_op jit(solution)/shard_map/ppermute | solution.py:470
  23.0 5.4 %collective-permute-start.4 = (f32[3,16,512]{2,1,0:T(8,128)S(1)}, f32[3,16,512]{2,1,0:T(8,128)S(1)}, u32[]{:S(2)}, u32[]{:S(2)}) collective-permute-start(f32[3,16,512]{2,1,0:T(8,128)S(1)} %get-tuple-element.39), channel_id=1, source_target_pairs={{16,17},{17,16},{18,19},{19,18},{20,21},{21,20},{22,23},{23,22},{2... | collective-permute-start | bytes 294920 | tf_op jit(solution)/shard_map/ppermute | solution.py:470
  26.2 5.4 %collective-permute-start.5 = (f32[3,16,512]{2,1,0:T(8,128)S(1)}, f32[3,16,512]{2,1,0:T(8,128)S(1)}, u32[]{:S(2)}, u32[]{:S(2)}) collective-permute-start(f32[3,16,512]{2,1,0:T(8,128)S(1)} %get-tuple-element.40), channel_id=1, source_target_pairs={{17,18},{18,17},{21,22},{22,21},{25,26},{26,25},{29,30},{30,29}} | collective-permute-start | bytes 294920 | tf_op jit(solution)/shard_map/ppermute | solution.py:470

commit v8 on v5

--- a/solution.py
+++ b/solution.py
@@ -351,9 +351,10 @@
 def rows_kernel(loads, comps, own, known, edge, a_in, b_in, h_out, a_out, b_out):
     zlen, ylen, xlen = own.shape
     planes = loads * comps
-    even = lax.axis_index("sy") % 2 == 0
-    from_low = jnp.where(even, b_in[...], a_in[...])
-    from_high = jnp.where(even, a_in[...], b_in[...])
+    index, last = lax.axis_index("sy"), lax.axis_size("sy") - 1
+    even = index % 2 == 0
+    from_low = jnp.where(index > 0, jnp.where(even, b_in[...], a_in[...]), 0.0)
+    from_high = jnp.where(index < last, jnp.where(even, a_in[...], b_in[...]), 0.0)
     ends = REACH * zlen
 
     def nodes(first, second, comp):
@@ -397,9 +398,10 @@
 
 def layers_kernel(h, a_in, b_in, out):
     zlen = h.shape[0]
-    even = lax.axis_index("sz") % 2 == 0
-    below = [jnp.where(even, b_in[k], a_in[k]) for k in range(REACH)]
-    above = [jnp.where(even, a_in[k], b_in[k]) for k in range(REACH)]
+    index, last = lax.axis_index("sz"), lax.axis_size("sz") - 1
+    even = index % 2 == 0
+    below = [jnp.where(index > 0, jnp.where(even, b_in[k], a_in[k]), 0.0) for k in range(REACH)]
+    above = [jnp.where(index < last, jnp.where(even, a_in[k], b_in[k]), 0.0) for k in range(REACH)]
     layers = below + [h[z] for z in range(zlen)] + above
     for z, layer in enumerate(spread_layers(layers)):
         out[z] = layer
@@ -433,10 +435,11 @@
 
 
 def swapped(value, axis, first):
-    pairs = []
-    for low in range(first, lax.axis_size(axis) - 1, 2):
-        pairs += [(low, low + 1), (low + 1, low)]
-    return lax.ppermute(value, axis, pairs)
+    size = lax.axis_size(axis)
+    pairs = {k: k for k in range(size)}
+    for low in range(first, size - 1, 2):
+        pairs[low], pairs[low + 1] = low + 1, low
+    return lax.ppermute(value, axis, list(pairs.items()))
 
 
 def body(displacements, density, solid, fixed):

time: 30.6 us -> 30.6 us (level)
  no operation moved by 1% of the time
where the time goes in v8:
time: 30.6 us; the launch traced here: 30.4 us
  starting transfers between devices  11.2 us (37%)
  waiting for transfers between devices  6.55 us (21%)
  Pallas kernels  6.53 us (21%)
  blocking collectives  6.02 us (20%)
    ppermute x4, starting transfers between devices, swapped(): return lax.ppermute(value, axis, list(pairs.items()))  6.97 us
    pallas_call x6, Pallas kernels, call(): pl.pallas_call(kernel, out_shape=shapes, in_specs=[pl.BlockSpec(memory_sp...  6.53 us
    all_gather x1, blocking collectives, body(): parts = lax.all_gather(part, 'load', axis=0)  6.02 us
    ppermute x4, waiting for transfers between devices, swapped(): return lax.ppermute(value, axis, list(pairs.items()))  5.82 us
    ppermute x2, starting transfers between devices, moved(): return lax.ppermute(value, axes if len(axes) > 1 else axes[0], pairs)  4.24 us
    ppermute x2, waiting for transfers between devices, moved(): return lax.ppermute(value, axes if len(axes) > 1 else axes[0], pairs)  0.72 us
  transfers between devices with their start and end apart: 6, of which 4 were waited for; matrix products, arithmetic and copies ran while one was open for 0% of the time, Pallas kernels for 9%

profile of v8, /device:TPU:19, one launch (start us, length us, event | category | flops | bytes accessed | tf_op | source)
XLA Modules:
  0.0 30.4 jit_solution(16597281874216970640)
XLA Ops:
  0.0 1.3 %shard_map.46 = (f32[2,3,4,16,512]{4,3,2,1,0:T(8,128)S(1)}, s32[4,16,512]{2,1,0:T(8,128)S(1)}, f32[4,16,512]{2,1,0:T(8,128)S(1)}, s32[4,16,512]{2,1,0:T(8,128)S(...) custom-call(f32[2,3,4,16,512]{4,3,2,1,0:T(8,128)} %disp_hbm.1, s32[4,16,512]{2,1,0:T(8,128)} %fixed_hbm.1, ...), custom_call_target="tpu_custom_call" | custom-call | tf_op jit(solution)/shard_map/pallas_call | solution.py:416
  1.3 2.1 %collective-permute-start = (f32[6,16,512]{2,1,0:T(8,128)S(1)}, f32[6,16,512]{2,1,0:T(8,128)S(1)}, u32[]{:S(2)}, u32[]{:S(2)}) collective-permute-start(f32[6,16,512]{2,1,0:T(8,128)S(1)} %get-tuple-element.25), channel_id=1, source_target_pairs={{1,0},{2,1},{3,2},{5,4},{6,5},{7,6},{9,8},{10,9},{11,10},{13,12},{... | collective-permute-start | bytes 589832 | tf_op jit(solution)/shard_map/ppermute | solution.py:434
  3.4 2.2 %collective-permute-start.1 = (f32[24,512]{1,0:T(8,128)S(1)}, f32[24,512]{1,0:T(8,128)S(1)}, u32[]{:S(2)}, u32[]{:S(2)}) collective-permute-start(f32[24,512]{1,0:T(8,128)S(1)} %get-tuple-element.26), channel_id=1, source_target_pairs={{4,0},{8,4},{12,8},{5,1},{9,5},{13,9},{6,2},{10,6},{14,10},{7,3},{... | collective-permute-start | bytes 147464 | tf_op jit(solution)/shard_map/ppermute | solution.py:434
  5.5 2.8 %shard_map.47 = (f32[4,16,512]{2,1,0:T(8,128)S(1)}, f32[2,24,512]{2,1,0:T(8,128)S(1)}, f32[2,9,512]{2,1,0:T(8,128)S(1)}, f32[6,16,512]{2,1,0:T(8,128)S(1)}, f32[...) custom-call(f32[2,3,4,16,512]{4,3,2,1,0:T(8,128)S(1)} %get-tuple-element.27.refs_0_.refs_2_, ...), custom_call_target="tpu_custom_call" | custom-call | tf_op jit(solution)/shard_map/pallas_call | solution.py:416
  8.4 0.7 %collective-permute-done.1.refs_1_ = f32[24,512]{1,0:T(8,128)S(1)} collective-permute-done((f32[24,512]{1,0:T(8,128)S(1)}, f32[24,512]{1,0:T(8,128)S(1)}, u32[]{:S(2)}, u32[]{:S(2)}) %collective-permute-start.1) | collective-permute-done | bytes 49184 | tf_op jit(solution)/shard_map/ppermute | solution.py:434
  9.1 0.0 collective-permute-done.refs_0_
  9.1 1.2 %shard_map.48 = (f32[4,16,512]{2,1,0:T(8,128)S(1)}, f32[32,512]{1,0:T(8,128)S(1)}, f32[24,512]{1,0:T(8,128)S(1)}, f32[24,512]{1,0:T(8,128)S(1)}) custom-call(f32[6,16,512]{2,1,0:T(8,128)S(1)} %collective-permute-done.refs_0_, f32[24,512]{1,0:T(8,128)S(1)} %collective-permute-done.1.refs_1_, f32[2,3,4,16,512]{4,3,2,1,0:T(8,128)S(1)} %get-tuple-element.27.refs_0_.refs_2_, ...), custom_call_target="tpu_custom_call" | custom-call | tf_op jit(solution)/shard_map/pallas_call | solution.py:416
  10.3 0.2 collective-permute-start.2
  10.5 4.1 %collective-permute-start.3 = (f32[24,512]{1,0:T(8,128)S(1)}, f32[24,512]{1,0:T(8,128)S(1)}, u32[]{:S(2)}, u32[]{:S(2)}) collective-permute-start(f32[24,512]{1,0:T(8,128)S(1)} %get-tuple-element.41), channel_id=1, source_target_pairs={{0,0},{4,8},{8,4},{12,12},{1,1},{5,9},{9,5},{13,13},{2,2},{6,10},{... | collective-permute-start | bytes 147464 | tf_op jit(solution)/shard_map/ppermute | solution.py:442
  14.5 0.0 collective-permute-done.2.refs_3_
  14.6 2.1 %collective-permute-done.3.refs_4_ = f32[24,512]{1,0:T(8,128)S(1)} collective-permute-done((f32[24,512]{1,0:T(8,128)S(1)}, f32[24,512]{1,0:T(8,128)S(1)}, u32[]{:S(2)}, u32[]{:S(2)}) %collective-permute-start.3) | collective-permute-done | bytes 49184 | tf_op jit(solution)/shard_map/ppermute | solution.py:442
  16.6 0.5 %shard_map.49 = (f32[4,16,512]{2,1,0:T(8,128)S(1)}, f32[3,16,512]{2,1,0:T(8,128)S(1)}, f32[3,16,512]{2,1,0:T(8,128)S(1)}) custom-call(f32[4,16,512]{2,1,0:T(8,128)S(1)} %get-tuple-element.38.refs_0_, f32[32,512]{1,0:T(8,128)S(1)} %get-tuple-element.39.refs_1_, f32[8,512]{1,0:T(8,128)S(1)} %get-tuple-element.37.refs_10_.refs_2_, ...), custom_call_target="tpu_custom_call" | custom-call | tf_op jit(solution)/shard_map/pallas_call | solution.py:416
  17.1 0.8 %collective-permute-start.4 = (f32[3,16,512]{2,1,0:T(8,128)S(1)}, f32[3,16,512]{2,1,0:T(8,128)S(1)}, u32[]{:S(2)}, u32[]{:S(2)}) collective-permute-start(f32[3,16,512]{2,1,0:T(8,128)S(1)} %get-tuple-element.43), channel_id=1, source_target_pairs={{0,1},{1,0},{2,3},{3,2},{4,5},{5,4},{6,7},{7,6},{8,9},{9,8},{10,11... | collective-permute-start | bytes 294920 | tf_op jit(solution)/shard_map/ppermute | solution.py:442
  18.0 1.9 %collective-permute-start.5 = (f32[3,16,512]{2,1,0:T(8,128)S(1)}, f32[3,16,512]{2,1,0:T(8,128)S(1)}, u32[]{:S(2)}, u32[]{:S(2)}) collective-permute-start(f32[3,16,512]{2,1,0:T(8,128)S(1)} %get-tuple-element.44), channel_id=1, source_target_pairs={{0,0},{1,2},{2,1},{3,3},{4,4},{5,6},{6,5},{7,7},{8,8},{9,10},{10,9... | collective-permute-start | bytes 294920 | tf_op jit(solution)/shard_map/ppermute | solution.py:442
  19.9 0.8 %collective-permute-done.4.a_in = f32[3,16,512]{2,1,0:T(8,128)S(1)} collective-permute-done((f32[3,16,512]{2,1,0:T(8,128)S(1)}, f32[3,16,512]{2,1,0:T(8,128)S(1)}, u32[]{:S(2)}, u32[]{:S(2)}) %collective-permute-start.4) | collective-permute-done | bytes 98336 | tf_op jit(solution)/shard_map/ppermute | solution.py:442
  20.7 3.0 %collective-permute-done.5.b_in = f32[3,16,512]{2,1,0:T(8,128)S(1)} collective-permute-done((f32[3,16,512]{2,1,0:T(8,128)S(1)}, f32[3,16,512]{2,1,0:T(8,128)S(1)}, u32[]{:S(2)}, u32[]{:S(2)}) %collective-permute-start.5) | collective-permute-done | bytes 98336 | tf_op jit(solution)/shard_map/ppermute | solution.py:442
  23.6 0.1 shard_map.50
  23.7 6.0 %all-gather = f32[8,16,512]{2,1,0:T(8,128)S(1)} all-gather(f32[4,16,512]{2,1,0:T(8,128)S(1)} %shard_map.50), channel_id=2, replica_groups=mesh['load'=2,'sy'=4,'sz'=4] {'load'}, dimensions={0}, use_global_device_ids=true | all-gather | bytes 393216 | tf_op jit(solution)/shard_map/all_gather | solution.py:494
  29.7 0.7 %shard_map.51 = f32[4,16,512]{2,1,0:T(8,128)} custom-call(f32[2,4,16,512]{3,2,1,0:T(8,128)S(1)} %bitcast.1), custom_call_target="tpu_custom_call" | custom-call | tf_op jit(solution)/shard_map/pallas_call | solution.py:416
Async XLA Ops:
  1.3 7.8 %collective-permute-start = (f32[6,16,512]{2,1,0:T(8,128)S(1)}, f32[6,16,512]{2,1,0:T(8,128)S(1)}, u32[]{:S(2)}, u32[]{:S(2)}) collective-permute-start(f32[6,16,512]{2,1,0:T(8,128)S(1)} %get-tuple-element.25), channel_id=1, source_target_pairs={{1,0},{2,1},{3,2},{5,4},{6,5},{7,6},{9,8},{10,9},{11,10},{13,12},{... | collective-permute-start | bytes 589832 | tf_op jit(solution)/shard_map/ppermute | solution.py:434
  3.4 5.7 %collective-permute-start.1 = (f32[24,512]{1,0:T(8,128)S(1)}, f32[24,512]{1,0:T(8,128)S(1)}, u32[]{:S(2)}, u32[]{:S(2)}) collective-permute-start(f32[24,512]{1,0:T(8,128)S(1)} %get-tuple-element.26), channel_id=1, source_target_pairs={{4,0},{8,4},{12,8},{5,1},{9,5},{13,9},{6,2},{10,6},{14,10},{7,3},{... | collective-permute-start | bytes 147464 | tf_op jit(solution)/shard_map/ppermute | solution.py:434
  10.3 4.2 %collective-permute-start.2 = (f32[24,512]{1,0:T(8,128)S(1)}, f32[24,512]{1,0:T(8,128)S(1)}, u32[]{:S(2)}, u32[]{:S(2)}) collective-permute-start(f32[24,512]{1,0:T(8,128)S(1)} %get-tuple-element.40), channel_id=1, source_target_pairs={{0,4},{4,0},{8,12},{12,8},{1,5},{5,1},{9,13},{13,9},{2,6},{6,2},{1... | collective-permute-start | bytes 147464 | tf_op jit(solution)/shard_map/ppermute | solution.py:442
  10.5 6.2 %collective-permute-start.3 = (f32[24,512]{1,0:T(8,128)S(1)}, f32[24,512]{1,0:T(8,128)S(1)}, u32[]{:S(2)}, u32[]{:S(2)}) collective-permute-start(f32[24,512]{1,0:T(8,128)S(1)} %get-tuple-element.41), channel_id=1, source_target_pairs={{0,0},{4,8},{8,4},{12,12},{1,1},{5,9},{9,5},{13,13},{2,2},{6,10},{... | collective-permute-start | bytes 147464 | tf_op jit(solution)/shard_map/ppermute | solution.py:442
  17.1 3.5 %collective-permute-start.4 = (f32[3,16,512]{2,1,0:T(8,128)S(1)}, f32[3,16,512]{2,1,0:T(8,128)S(1)}, u32[]{:S(2)}, u32[]{:S(2)}) collective-permute-start(f32[3,16,512]{2,1,0:T(8,128)S(1)} %get-tuple-element.43), channel_id=1, source_target_pairs={{0,1},{1,0},{2,3},{3,2},{4,5},{5,4},{6,7},{7,6},{8,9},{9,8},{10,11... | collective-permute-start | bytes 294920 | tf_op jit(solution)/shard_map/ppermute | solution.py:442
  18.0 5.6 %collective-permute-start.5 = (f32[3,16,512]{2,1,0:T(8,128)S(1)}, f32[3,16,512]{2,1,0:T(8,128)S(1)}, u32[]{:S(2)}, u32[]{:S(2)}) collective-permute-start(f32[3,16,512]{2,1,0:T(8,128)S(1)} %get-tuple-element.44), channel_id=1, source_target_pairs={{0,0},{1,2},{2,1},{3,3},{4,4},{5,6},{6,5},{7,7},{8,8},{9,10},{10,9... | collective-permute-start | bytes 294920 | tf_op jit(solution)/shard_map/ppermute | solution.py:442

commit v9 on v8

--- a/solution.py
+++ b/solution.py
@@ -305,11 +305,12 @@
             quotient[first + TILE : first + 2 * TILE, lanes] = blank_last(here, first, ylen)
 
     count = loads * zlen
+    more = lax.axis_index("sy") < lax.axis_size("sy") - 1
     low, high = [], []
     for comp in range(comps):
         part = slice(comp * count, (comp + 1) * count)
         whole, change = line[0, part], line[1, part]
-        whole_next, change_next = split_x(y_in[part])
+        whole_next, change_next = split_x(jnp.where(more, y_in[part], 0.0))
         face = (whole + whole_next, change + change_next, whole_next - whole, change_next - change)
         low.append(face)
         high.append([pltpu.roll(value, count - 1, 0) for value in face])
@@ -335,7 +336,7 @@
     pairs = [(case, comp) for comp in range(comps) for case in range(loads)]
     here_last = [held(disp, fixed, case, comp, inner, slice(ylen - 1, ylen)) for case, comp in pairs]
     here_first = [held(disp, fixed, case, comp, inner, slice(0, 1)) for case, comp in pairs]
-    next_row = [y_in[(k + 1) * zlen - 1 : (k + 1) * zlen] for k in range(planes)]
+    next_row = [jnp.where(more, y_in[(k + 1) * zlen - 1 : (k + 1) * zlen], 0.0) for k in range(planes)]
     over_last = [z_in[case * comps + comp, ylen - 1 : ylen] for case, comp in pairs]
     over_first = [z_in[case * comps + comp, 0:1] for case, comp in pairs]
     rows = here_last + over_last + next_row + here_first + over_first
@@ -423,23 +424,35 @@
     )(*args)
 
 
-def moved(value, axes, steps):
-    sizes = [lax.axis_size(axis) for axis in axes]
-    pairs = []
-    for flat in range(int(np.prod(sizes))):
-        place = np.unravel_index(flat, sizes)
-        source = [int(p) + s for p, s in zip(place, steps)]
-        if all(0 <= s < size for s, size in zip(source, sizes)):
-            pairs.append((int(np.ravel_multi_index(source, sizes)), flat))
-    return lax.ppermute(value, axes if len(axes) > 1 else axes[0], pairs)
+def moved(value, axis):
+    size = lax.axis_size(axis)
+    return lax.ppermute(value, axis, [(k + 1, k) for k in range(size - 1)])
+
+
+def ring_moved(value, axis):
+    size = lax.axis_size(axis)
+    return lax.ppermute(value, axis, [((k + 1) % size, k) for k in range(size)])
 
 
 def swapped(value, axis, first):
     size = lax.axis_size(axis)
     pairs = {k: k for k in range(size)}
-    for low in range(first, size - 1, 2):
-        pairs[low], pairs[low + 1] = low + 1, low
+    for low in range(first, size + first - 1, 2):
+        high = (low + 1) % size
+        pairs[low], pairs[high] = high, low
     return lax.ppermute(value, axis, list(pairs.items()))
+
+
+def swapped_inside(value, axis, other):
+    size, rows = lax.axis_size(axis), lax.axis_size(other)
+    pairs = []
+    for row in range(rows):
+        beside = row ^ 1 if (row ^ 1) < rows else row
+        for k in range(size):
+            inside = k + 1 if k % 2 else k - 1
+            target = (row, inside) if 0 <= inside < size else (beside, k)
+            pairs.append((row * size + k, target[0] * size + target[1]))
+    return lax.ppermute(value, (other, axis), pairs)
 
 
 def body(displacements, density, solid, fixed):
@@ -457,8 +470,8 @@
         scratch=[pltpu.SemaphoreType.DMA((len(args),))],
         space=pltpu.HBM,
     )
-    z_in = moved(z_send, ("sz",), (1,))
-    y_in = moved(y_send, ("sy",), (1,))
+    z_in = moved(z_send, "sz")
+    y_in = ring_moved(y_send, "sy")
     nodes = lambda layers: pltpu.VMEM((planes, layers, ylen + TILE, xlen), jnp.float32)
     inner = call(
         lambda *refs: inner_kernel(totals, *refs),
@@ -489,7 +502,7 @@
         (own, known, inner[-1], a_in, b_in),
     )
     a_in = swapped(a_send, "sz", 0)
-    b_in = swapped(b_send, "sz", 1)
+    b_in = swapped_inside(b_send, "sz", "sy")
     (part,) = call(layers_kernel, [(zlen, ylen, xlen)], (h, a_in, b_in))
     parts = lax.all_gather(part, "load", axis=0)
     (out,) = call(sum_kernel, [(zlen, ylen, xlen)], (parts,))

time: 30.6 us -> 28.7 us (0.938)
  the two profiles are of different devices: /device:TPU:19 before, /device:TPU:0 now
where the time goes in v9:
time: 28.7 us; the launch traced here: 28.5 us
  starting transfers between devices  10.7 us (37%)
  waiting for transfers between devices  9.28 us (32%)
  Pallas kernels  6.53 us (23%)
  blocking collectives  1.99 us (7%)
    pallas_call x6, Pallas kernels, call(): pl.pallas_call(kernel, out_shape=shapes, in_specs=[pl.BlockSpec(memory_sp...  6.53 us
    ppermute x3, waiting for transfers between devices, swapped(): return lax.ppermute(value, axis, list(pairs.items()))  5.96 us
    ppermute x3, starting transfers between devices, swapped(): return lax.ppermute(value, axis, list(pairs.items()))  4.84 us
    ppermute x1, starting transfers between devices, ring_moved(): return lax.ppermute(value, axis, [((k + 1) % size, k) for k in range(size)])  3.95 us
    all_gather x1, blocking collectives, body(): parts = lax.all_gather(part, 'load', axis=0)  1.99 us
    ppermute x1, waiting for transfers between devices, moved(): return lax.ppermute(value, axis, [(k + 1, k) for k in range(size - 1)])  1.75 us
    ppermute x1, waiting for transfers between devices, swapped_inside(): return lax.ppermute(value, (other, axis), pairs)  1.57 us
    ppermute x1, starting transfers between devices, moved(): return lax.ppermute(value, axis, [(k + 1, k) for k in range(size - 1)])  1.29 us
  transfers between devices with their start and end apart: 6, of which 5 were waited for; matrix products, arithmetic and copies ran while one was open for 0% of the time, Pallas kernels for 10%

profile of v9, /device:TPU:0, one launch (start us, length us, event | category | flops | bytes accessed | tf_op | source)
XLA Modules:
  0.0 28.5 jit_solution(12294573876989658550)
XLA Ops:
  0.0 1.3 %shard_map.46 = (f32[2,3,4,16,512]{4,3,2,1,0:T(8,128)S(1)}, s32[4,16,512]{2,1,0:T(8,128)S(1)}, f32[4,16,512]{2,1,0:T(8,128)S(1)}, s32[4,16,512]{2,1,0:T(8,128)S(...) custom-call(f32[2,3,4,16,512]{4,3,2,1,0:T(8,128)} %disp_hbm.1, s32[4,16,512]{2,1,0:T(8,128)} %fixed_hbm.1, ...), custom_call_target="tpu_custom_call" | custom-call | tf_op jit(solution)/shard_map/pallas_call | solution.py:417
  1.3 1.3 %collective-permute-start = (f32[6,16,512]{2,1,0:T(8,128)S(1)}, f32[6,16,512]{2,1,0:T(8,128)S(1)}, u32[]{:S(2)}, u32[]{:S(2)}) collective-permute-start(f32[6,16,512]{2,1,0:T(8,128)S(1)} %get-tuple-element.25), channel_id=1, source_target_pairs={{1,0},{2,1},{3,2},{5,4},{6,5},{7,6},{9,8},{10,9},{11,10},{13,12},{... | collective-permute-start | bytes 589832 | tf_op jit(solution)/shard_map/ppermute | solution.py:429
  2.6 3.9 %collective-permute-start.1 = (f32[24,512]{1,0:T(8,128)S(1)}, f32[24,512]{1,0:T(8,128)S(1)}, u32[]{:S(2)}, u32[]{:S(2)}) collective-permute-start(f32[24,512]{1,0:T(8,128)S(1)} %get-tuple-element.26), channel_id=1, source_target_pairs={{4,0},{8,4},{12,8},{0,12},{5,1},{9,5},{13,9},{1,13},{6,2},{10,6},{... | collective-permute-start | bytes 147464 | tf_op jit(solution)/shard_map/ppermute | solution.py:434
  6.5 2.8 %shard_map.47 = (f32[4,16,512]{2,1,0:T(8,128)S(1)}, f32[2,24,512]{2,1,0:T(8,128)S(1)}, f32[2,9,512]{2,1,0:T(8,128)S(1)}, f32[6,16,512]{2,1,0:T(8,128)S(1)}, f32[...) custom-call(f32[2,3,4,16,512]{4,3,2,1,0:T(8,128)S(1)} %get-tuple-element.27.refs_0_.refs_2_, ...), custom_call_target="tpu_custom_call" | custom-call | tf_op jit(solution)/shard_map/pallas_call | solution.py:417
  9.4 0.0 collective-permute-done.1.refs_1_
  9.4 1.7 %collective-permute-done.refs_0_ = f32[6,16,512]{2,1,0:T(8,128)S(1)} collective-permute-done((f32[6,16,512]{2,1,0:T(8,128)S(1)}, f32[6,16,512]{2,1,0:T(8,128)S(1)}, u32[]{:S(2)}, u32[]{:S(2)}) %collective-permute-start) | collective-permute-done | bytes 196640 | tf_op jit(solution)/shard_map/ppermute | solution.py:429
  11.1 1.2 %shard_map.48 = (f32[4,16,512]{2,1,0:T(8,128)S(1)}, f32[32,512]{1,0:T(8,128)S(1)}, f32[24,512]{1,0:T(8,128)S(1)}, f32[24,512]{1,0:T(8,128)S(1)}) custom-call(f32[6,16,512]{2,1,0:T(8,128)S(1)} %collective-permute-done.refs_0_, f32[24,512]{1,0:T(8,128)S(1)} %collective-permute-done.1.refs_1_, f32[2,3,4,16,512]{4,3,2,1,0:T(8,128)S(1)} %get-tuple-element.27.refs_0_.refs_2_, ...), custom_call_target="tpu_custom_call" | custom-call | tf_op jit(solution)/shard_map/pallas_call | solution.py:417
  12.3 1.7 %collective-permute-start.2 = (f32[24,512]{1,0:T(8,128)S(1)}, f32[24,512]{1,0:T(8,128)S(1)}, u32[]{:S(2)}, u32[]{:S(2)}) collective-permute-start(f32[24,512]{1,0:T(8,128)S(1)} %get-tuple-element.40), channel_id=1, source_target_pairs={{0,4},{4,0},{8,12},{12,8},{1,5},{5,1},{9,13},{13,9},{2,6},{6,2},{1... | collective-permute-start | bytes 147464 | tf_op jit(solution)/shard_map/ppermute | solution.py:443
  14.1 1.5 %collective-permute-start.3 = (f32[24,512]{1,0:T(8,128)S(1)}, f32[24,512]{1,0:T(8,128)S(1)}, u32[]{:S(2)}, u32[]{:S(2)}) collective-permute-start(f32[24,512]{1,0:T(8,128)S(1)} %get-tuple-element.41), channel_id=1, source_target_pairs={{0,12},{4,8},{8,4},{12,0},{1,13},{5,9},{9,5},{13,1},{2,14},{6,10},... | collective-permute-start | bytes 147464 | tf_op jit(solution)/shard_map/ppermute | solution.py:443
  15.5 1.2 %collective-permute-done.2.refs_3_ = f32[24,512]{1,0:T(8,128)S(1)} collective-permute-done((f32[24,512]{1,0:T(8,128)S(1)}, f32[24,512]{1,0:T(8,128)S(1)}, u32[]{:S(2)}, u32[]{:S(2)}) %collective-permute-start.2) | collective-permute-done | bytes 49184 | tf_op jit(solution)/shard_map/ppermute | solution.py:443
  16.7 2.3 %collective-permute-done.3.refs_4_ = f32[24,512]{1,0:T(8,128)S(1)} collective-permute-done((f32[24,512]{1,0:T(8,128)S(1)}, f32[24,512]{1,0:T(8,128)S(1)}, u32[]{:S(2)}, u32[]{:S(2)}) %collective-permute-start.3) | collective-permute-done | bytes 49184 | tf_op jit(solution)/shard_map/ppermute | solution.py:443
  19.0 0.5 %shard_map.49 = (f32[4,16,512]{2,1,0:T(8,128)S(1)}, f32[3,16,512]{2,1,0:T(8,128)S(1)}, f32[3,16,512]{2,1,0:T(8,128)S(1)}) custom-call(f32[4,16,512]{2,1,0:T(8,128)S(1)} %get-tuple-element.38.refs_0_, f32[32,512]{1,0:T(8,128)S(1)} %get-tuple-element.39.refs_1_, f32[8,512]{1,0:T(8,128)S(1)} %get-tuple-element.37.refs_10_.refs_2_, ...), custom_call_target="tpu_custom_call" | custom-call | tf_op jit(solution)/shard_map/pallas_call | solution.py:417
  19.5 1.6 %collective-permute-start.4 = (f32[3,16,512]{2,1,0:T(8,128)S(1)}, f32[3,16,512]{2,1,0:T(8,128)S(1)}, u32[]{:S(2)}, u32[]{:S(2)}) collective-permute-start(f32[3,16,512]{2,1,0:T(8,128)S(1)} %get-tuple-element.43), channel_id=1, source_target_pairs={{0,1},{1,0},{2,3},{3,2},{4,5},{5,4},{6,7},{7,6},{8,9},{9,8},{10,11... | collective-permute-start | bytes 294920 | tf_op jit(solution)/shard_map/ppermute | solution.py:443
  21.2 0.6 %collective-permute-start.5 = (f32[3,16,512]{2,1,0:T(8,128)S(1)}, f32[3,16,512]{2,1,0:T(8,128)S(1)}, u32[]{:S(2)}, u32[]{:S(2)}) collective-permute-start(f32[3,16,512]{2,1,0:T(8,128)S(1)} %get-tuple-element.44), channel_id=1, source_target_pairs={{0,4},{1,2},{2,1},{3,7},{4,0},{5,6},{6,5},{7,3},{8,12},{9,10},{10,... | collective-permute-start | bytes 294920 | tf_op jit(solution)/shard_map/ppermute | solution.py:455
  21.8 2.5 %collective-permute-done.4.a_in = f32[3,16,512]{2,1,0:T(8,128)S(1)} collective-permute-done((f32[3,16,512]{2,1,0:T(8,128)S(1)}, f32[3,16,512]{2,1,0:T(8,128)S(1)}, u32[]{:S(2)}, u32[]{:S(2)}) %collective-permute-start.4) | collective-permute-done | bytes 98336 | tf_op jit(solution)/shard_map/ppermute | solution.py:443
  24.2 1.6 %collective-permute-done.5.b_in = f32[3,16,512]{2,1,0:T(8,128)S(1)} collective-permute-done((f32[3,16,512]{2,1,0:T(8,128)S(1)}, f32[3,16,512]{2,1,0:T(8,128)S(1)}, u32[]{:S(2)}, u32[]{:S(2)}) %collective-permute-start.5) | collective-permute-done | bytes 98336 | tf_op jit(solution)/shard_map/ppermute | solution.py:455
  25.8 0.1 shard_map.50
  25.9 2.0 %all-gather = f32[8,16,512]{2,1,0:T(8,128)S(1)} all-gather(f32[4,16,512]{2,1,0:T(8,128)S(1)} %shard_map.50), channel_id=2, replica_groups=mesh['load'=2,'sy'=4,'sz'=4] {'load'}, dimensions={0}, use_global_device_ids=true | all-gather | bytes 393216 | tf_op jit(solution)/shard_map/all_gather | solution.py:507
  27.9 0.7 %shard_map.51 = f32[4,16,512]{2,1,0:T(8,128)} custom-call(f32[2,4,16,512]{3,2,1,0:T(8,128)S(1)} %bitcast.1), custom_call_target="tpu_custom_call" | custom-call | tf_op jit(solution)/shard_map/pallas_call | solution.py:417
Async XLA Ops:
  1.3 9.8 %collective-permute-start = (f32[6,16,512]{2,1,0:T(8,128)S(1)}, f32[6,16,512]{2,1,0:T(8,128)S(1)}, u32[]{:S(2)}, u32[]{:S(2)}) collective-permute-start(f32[6,16,512]{2,1,0:T(8,128)S(1)} %get-tuple-element.25), channel_id=1, source_target_pairs={{1,0},{2,1},{3,2},{5,4},{6,5},{7,6},{9,8},{10,9},{11,10},{13,12},{... | collective-permute-start | bytes 589832 | tf_op jit(solution)/shard_map/ppermute | solution.py:429
  2.6 6.8 %collective-permute-start.1 = (f32[24,512]{1,0:T(8,128)S(1)}, f32[24,512]{1,0:T(8,128)S(1)}, u32[]{:S(2)}, u32[]{:S(2)}) collective-permute-start(f32[24,512]{1,0:T(8,128)S(1)} %get-tuple-element.26), channel_id=1, source_target_pairs={{4,0},{8,4},{12,8},{0,12},{5,1},{9,5},{13,9},{1,13},{6,2},{10,6},{... | collective-permute-start | bytes 147464 | tf_op jit(solution)/shard_map/ppermute | solution.py:434
  12.3 4.4 %collective-permute-start.2 = (f32[24,512]{1,0:T(8,128)S(1)}, f32[24,512]{1,0:T(8,128)S(1)}, u32[]{:S(2)}, u32[]{:S(2)}) collective-permute-start(f32[24,512]{1,0:T(8,128)S(1)} %get-tuple-element.40), channel_id=1, source_target_pairs={{0,4},{4,0},{8,12},{12,8},{1,5},{5,1},{9,13},{13,9},{2,6},{6,2},{1... | collective-permute-start | bytes 147464 | tf_op jit(solution)/shard_map/ppermute | solution.py:443
  14.1 5.0 %collective-permute-start.3 = (f32[24,512]{1,0:T(8,128)S(1)}, f32[24,512]{1,0:T(8,128)S(1)}, u32[]{:S(2)}, u32[]{:S(2)}) collective-permute-start(f32[24,512]{1,0:T(8,128)S(1)} %get-tuple-element.41), channel_id=1, source_target_pairs={{0,12},{4,8},{8,4},{12,0},{1,13},{5,9},{9,5},{13,1},{2,14},{6,10},... | collective-permute-start | bytes 147464 | tf_op jit(solution)/shard_map/ppermute | solution.py:443
  19.5 4.7 %collective-permute-start.4 = (f32[3,16,512]{2,1,0:T(8,128)S(1)}, f32[3,16,512]{2,1,0:T(8,128)S(1)}, u32[]{:S(2)}, u32[]{:S(2)}) collective-permute-start(f32[3,16,512]{2,1,0:T(8,128)S(1)} %get-tuple-element.43), channel_id=1, source_target_pairs={{0,1},{1,0},{2,3},{3,2},{4,5},{5,4},{6,7},{7,6},{8,9},{9,8},{10,11... | collective-permute-start | bytes 294920 | tf_op jit(solution)/shard_map/ppermute | solution.py:443
  21.2 4.6 %collective-permute-start.5 = (f32[3,16,512]{2,1,0:T(8,128)S(1)}, f32[3,16,512]{2,1,0:T(8,128)S(1)}, u32[]{:S(2)}, u32[]{:S(2)}) collective-permute-start(f32[3,16,512]{2,1,0:T(8,128)S(1)} %get-tuple-element.44), channel_id=1, source_target_pairs={{0,4},{1,2},{2,1},{3,7},{4,0},{5,6},{6,5},{7,3},{8,12},{9,10},{10,... | collective-permute-start | bytes 294920 | tf_op jit(solution)/shard_map/ppermute | solution.py:455

commit v10 on v9

--- a/solution.py
+++ b/solution.py
@@ -179,8 +179,12 @@
     return ahead, back
 
 
-def lead_kernel(disp_hbm, fixed_hbm, density_hbm, solid_hbm, disp, fixed, density, solid, z_out, y_out, sems):
-    loads, comps, zlen, _, _ = disp.shape
+def on_first():
+    return lax.axis_index("load") == 0
+
+
+def lead_kernel(totals, disp_hbm, fixed_hbm, density_hbm, solid_hbm, disp, fixed, density, solid, z_out, y_out, sems):
+    loads, comps, zlen, ylen, _ = disp.shape
     copies = [
         pltpu.make_async_copy(source, target, sems.at[k])
         for k, (source, target) in enumerate(
@@ -191,15 +195,19 @@
         copy.start()
     for copy in copies:
         copy.wait()
+    gives = jnp.where(on_first(), 0, zlen - 1)
+    plane = lax.axis_index("sz") * zlen + gives
+    base_y = lax.axis_index("sy") * ylen
+    z_out[loads * comps] = voxel_factor(density[gives], solid[gives], plane, base_y, *totals)
     for case in range(loads):
         for comp in range(comps):
-            z_out[case * comps + comp] = held(disp, fixed, case, comp, 0, slice(None))
+            z_out[case * comps + comp] = held(disp, fixed, case, comp, gives, slice(None))
             for z in range(zlen):
                 at = (comp * loads + case) * zlen + z
                 y_out[at : at + 1] = held(disp, fixed, case, comp, z, slice(0, 1))
 
 
-def tile_energies(plus, diff, first, lanes, layers, loads, comps):
+def tile_energies(plus, diff, first, lanes, layers, loads, comps, base=0):
     weights = mode_weights()
 
     def faces(k, z):
@@ -212,7 +220,7 @@
     for case in range(loads):
         low = None
         for z in range(layers + 1):
-            high = [faces(case * comps + comp, z) for comp in range(comps)]
+            high = [faces(case * comps + comp, base + z) for comp in range(comps)]
             if low is not None:
                 part = quadratic(low, high, weights)
                 energy[z - 1] = part if energy[z - 1] is None else energy[z - 1] + part
@@ -231,6 +239,7 @@
     base_z = lax.axis_index("sz") * zlen
     base_y = lax.axis_index("sy") * ylen
     inner = zlen - 1
+    keeps = jnp.where(on_first(), inner, 0)
 
     @pl.loop(0, loads * comps)
     def _(k):
@@ -239,8 +248,8 @@
             whole, change = split_x(held(disp, fixed, case, comp, z, slice(None)))
             plus[k, z, :ylen] = whole
             diff[k, z, :ylen] = change
-        last_plus[k] = whole
-        last_diff[k] = change
+        last_plus[k] = plus[k, keeps, :ylen]
+        last_diff[k] = diff[k, keeps, :ylen]
 
     for comp in range(comps):
         for case in range(loads):
@@ -280,17 +289,31 @@
 
 
 def outer_kernel(
-    shape, z_in, y_in, disp, fixed, own_in, line, sends, last_plus, last_diff, last_factor, edge, own, known, a_out, b_out, plus, diff, quotient
+    shape, z_in, y_in, disp, fixed, own_in, line, sends, last_plus, last_diff, last_factor, edge, own, known, a_out, b_out, plus, diff, quotient, factor
 ):
     loads, comps, zlen, ylen, xlen = shape
     planes = loads * comps
     inner = zlen - 1
+    first_core, index = on_first(), lax.axis_index("sz")
+    top = first_core & (index == lax.axis_size("sz") - 1)
+    keeps = jnp.where(first_core, inner, 0)
+    stays, comes = jnp.where(first_core, 0, 1), jnp.where(first_core, jnp.where(top, 2, 1), 0)
     for k in range(planes):
-        plus[k, 0, :ylen] = last_plus[k]
-        diff[k, 0, :ylen] = last_diff[k]
+        plus[k, stays, :ylen] = last_plus[k]
+        diff[k, stays, :ylen] = last_diff[k]
         whole, change = split_x(z_in[k])
-        plus[k, 1, :ylen] = whole
-        diff[k, 1, :ylen] = change
+        plus[k, comes, :ylen] = whole
+        diff[k, comes, :ylen] = change
+    below = jnp.where(index > 0, z_in[planes], 0.0)
+    factor[...] = jnp.where(first_core, last_factor[...], below)
+
+    @pl.when(top)
+    def _():
+        clamped = jnp.zeros((ylen + TILE, xlen), jnp.float32)
+        for k in range(planes):
+            for slot in (1, 3):
+                plus[k, slot] = clamped
+                diff[k, slot] = clamped
 
     zeros = jnp.zeros((TILE, xlen), jnp.float32)
     quotient[:TILE] = zeros
@@ -301,8 +324,19 @@
         def _(chunk):
             lanes = pl.ds(pl.multiple_of(chunk * LANES, LANES), LANES)
             (energy,) = tile_energies(plus, diff, first, lanes, 1, loads, comps)
-            here = energy * last_factor[first : first + TILE, lanes]
+            here = energy * factor[first : first + TILE, lanes]
             quotient[first + TILE : first + 2 * TILE, lanes] = blank_last(here, first, ylen)
+
+    @pl.when(top)
+    def _():
+        for first in range(0, ylen, TILE):
+
+            @pl.loop(0, xlen // LANES)
+            def _(chunk):
+                lanes = pl.ds(pl.multiple_of(chunk * LANES, LANES), LANES)
+                (energy,) = tile_energies(plus, diff, first, lanes, 1, loads, comps, base=2)
+                here = energy * factor[first : first + TILE, lanes]
+                quotient[first + TILE : first + 2 * TILE, lanes] += blank_last(here, first, ylen)
 
     count = loads * zlen
     more = lax.axis_index("sy") < lax.axis_size("sy") - 1
@@ -330,26 +364,27 @@
     own[inner] = spread_x(spread_y(quotient, ylen))
     ahead, back = to_neighbours(quotient, ylen)
     ends = spread_x(jnp.concatenate(ahead + back + [zeros[:2]], axis=0))
-    ups += [ends[: REACH - 1], edge[inner:zlen]]
+    ups += [ends[: REACH - 1], factor[ylen - 1 :]]
     downs.append(ends[REACH : 2 * REACH])
 
     pairs = [(case, comp) for comp in range(comps) for case in range(loads)]
-    here_last = [held(disp, fixed, case, comp, inner, slice(ylen - 1, ylen)) for case, comp in pairs]
-    here_first = [held(disp, fixed, case, comp, inner, slice(0, 1)) for case, comp in pairs]
-    next_row = [jnp.where(more, y_in[(k + 1) * zlen - 1 : (k + 1) * zlen], 0.0) for k in range(planes)]
-    over_last = [z_in[case * comps + comp, ylen - 1 : ylen] for case, comp in pairs]
-    over_first = [z_in[case * comps + comp, 0:1] for case, comp in pairs]
-    rows = here_last + over_last + next_row + here_first + over_first
+    here_last = [held(disp, fixed, case, comp, keeps, slice(ylen - 1, ylen)) for case, comp in pairs]
+    here_first = [held(disp, fixed, case, comp, keeps, slice(0, 1)) for case, comp in pairs]
+    next_row = [jnp.where(first_core, y_in[k * zlen + inner : (k + 1) * zlen], y_in[k * zlen : k * zlen + 1]) for k in range(planes)]
+    next_row = [jnp.where(more, row, 0.0) for row in next_row]
+    come_last = [z_in[case * comps + comp, ylen - 1 : ylen] for case, comp in pairs]
+    come_first = [z_in[case * comps + comp, 0:1] for case, comp in pairs]
+    rows = here_last + come_last + next_row + here_first + come_first + [factor[ylen - 1 :]]
     known[: len(rows)] = jnp.concatenate(rows, axis=0)
     known[len(rows) :] = jnp.zeros((known.shape[0] - len(rows), xlen), jnp.float32)
-    up = jnp.concatenate(ups + here_last + over_last, axis=0)
-    down = jnp.concatenate(downs + over_first + [jnp.zeros((planes, xlen), jnp.float32)], axis=0)
+    up = jnp.concatenate(ups + here_last + come_last, axis=0)
+    down = jnp.concatenate(downs + come_first + [jnp.zeros((planes, xlen), jnp.float32)], axis=0)
     even = lax.axis_index("sy") % 2 == 0
     a_out[...] = jnp.where(even, up, down)
     b_out[...] = jnp.where(even, down, up)
 
 
-def rows_kernel(loads, comps, own, known, edge, a_in, b_in, h_out, a_out, b_out):
+def rows_kernel(loads, comps, own, known, a_in, b_in, h_out, a_out, b_out):
     zlen, ylen, xlen = own.shape
     planes = loads * comps
     index, last = lax.axis_index("sy"), lax.axis_size("sy") - 1
@@ -357,53 +392,69 @@
     from_low = jnp.where(index > 0, jnp.where(even, b_in[...], a_in[...]), 0.0)
     from_high = jnp.where(index < last, jnp.where(even, a_in[...], b_in[...]), 0.0)
     ends = REACH * zlen
+    first_core = on_first()
+    top = first_core & (lax.axis_index("sz") == lax.axis_size("sz") - 1)
 
     def nodes(first, second, comp):
         part = slice(comp * loads, (comp + 1) * loads)
-        rows = jnp.concatenate([first[part], second[part]], axis=0)
-        return split_x(jnp.concatenate([rows, rows], axis=0))
+        zero = jnp.zeros((loads, xlen), jnp.float32)
+        (first, first_more), (second, second_more) = first, second
+        pieces = [first, first_more, second, second_more]
+        return split_x(jnp.concatenate([zero if piece is None else piece[part] for piece in pieces], axis=0))
+
+    def under(stays, comes):
+        return jnp.where(first_core, stays, comes), jnp.where(top, comes, 0.0)
+
+    def over(stays, comes):
+        return jnp.where(first_core, jnp.where(top, 0.0, comes), stays), None
 
     def face(near_own, near_in, far_own, far_in, comp):
         whole, change = nodes(near_own, near_in, comp)
         whole_next, change_next = nodes(far_own, far_in, comp)
         return whole + whole_next, change + change_next, whole_next - whole, change_next - change
 
-    here_last, over_last, next_row, here_first, over_first = (known[planes * k : planes * (k + 1)] for k in range(5))
-    low_last, low_over = from_low[ends : ends + planes], from_low[ends + planes : ends + 2 * planes]
-    next_over = from_high[ends : ends + planes]
-    low = [face(here_last, low_last, next_row, here_first, comp) for comp in range(comps)]
-    high = [face(over_last, low_over, next_over, over_first, comp) for comp in range(comps)]
+    here_last, come_last, next_row, here_first, come_first = (known[planes * k : planes * (k + 1)] for k in range(5))
+    low_last, low_come = from_low[ends : ends + planes], from_low[ends + planes : ends + 2 * planes]
+    next_come = from_high[ends : ends + planes]
+    corners = [(here_last, come_last), (low_last, low_come), (next_row, next_come), (here_first, come_first)]
+    low = [face(*(under(*corner) for corner in corners), comp) for comp in range(comps)]
+    high = [face(*(over(*corner) for corner in corners), comp) for comp in range(comps)]
     energy = quadratic(low, high, mode_weights())
-    lines = [sum(energy[loads * k + case : loads * k + case + 1] for case in range(loads)) for k in range(2)]
-    lines = [lines[0] * edge[zlen - 1 : zlen], lines[1] * from_low[ends - 1 : ends]]
+    cases = 2 * loads
+    lines = [sum(energy[cases * k + case : cases * k + case + 1] for case in range(cases)) for k in range(2)]
+    lines = [lines[0] * known[5 * planes : 5 * planes + 1], lines[1] * from_low[ends - 1 : ends]]
     lines = spread_x(jnp.concatenate(lines + [jnp.zeros((TILE - 2, xlen), jnp.float32)], axis=0))
 
     row = lax.broadcasted_iota(jnp.int32, (TILE, xlen), 0)
     rising = jnp.maximum(row - (TILE - 1 - ROWS), 0).astype(jnp.float32)
     falling = jnp.maximum(REACH - row, 0).astype(jnp.float32)
     blank = jnp.zeros((TILE - REACH, xlen), jnp.float32)
+    between = jnp.where(first_core, zlen, 0)
+    h_out[zlen - between] = jnp.zeros((ylen, xlen), jnp.float32)
     for z in range(zlen):
         part = slice(REACH * z, REACH * (z + 1))
         head = jnp.concatenate([from_low[part], blank], axis=0)
         tail = jnp.concatenate([blank, from_high[part]], axis=0)
+        at = z + 1
         if z == zlen - 1:
             head = jnp.where(row == REACH - 1, 0.0, head) + falling * lines[1:2]
             tail = tail + rising * lines[0:1]
-        h_out[z] = own[z]
-        h_out[z, :TILE] += head
-        h_out[z, ylen - TILE :] += tail
-    top = (zlen - REACH) * (lax.axis_index("sz") % 2 == 0).astype(jnp.int32)
-    a_out[...] = h_out[pl.ds(top, REACH)]
-    b_out[...] = h_out[pl.ds(zlen - REACH - top, REACH)]
+            at = between
+        h_out[at] = own[z]
+        h_out[at, :TILE] += head
+        h_out[at, ylen - TILE :] += tail
+    high = (lax.axis_index("sz") % 2 == 0).astype(jnp.int32)
+    a_out[...] = h_out[pl.ds(high, zlen)]
+    b_out[...] = h_out[pl.ds(1 - high, zlen)]
 
 
 def layers_kernel(h, a_in, b_in, out):
-    zlen = h.shape[0]
+    zlen = out.shape[0]
     index, last = lax.axis_index("sz"), lax.axis_size("sz") - 1
     even = index % 2 == 0
-    below = [jnp.where(index > 0, jnp.where(even, b_in[k], a_in[k]), 0.0) for k in range(REACH)]
-    above = [jnp.where(index < last, jnp.where(even, a_in[k], b_in[k]), 0.0) for k in range(REACH)]
-    layers = below + [h[z] for z in range(zlen)] + above
+    below = [jnp.where(index > 0, jnp.where(even, b_in[k], a_in[k]), 0.0) for k in range(zlen - REACH, zlen)]
+    above = [jnp.where(index < last, jnp.where(even, a_in[k], b_in[k]), 0.0) for k in range(zlen)]
+    layers = below[:-1] + [below[-1] + h[0]] + [h[z] for z in range(1, zlen)] + [h[zlen] + above[0]] + above[1:]
     for z, layer in enumerate(spread_layers(layers)):
         out[z] = layer
 
@@ -424,9 +475,10 @@
     )(*args)
 
 
-def moved(value, axis):
-    size = lax.axis_size(axis)
-    return lax.ppermute(value, axis, [(k + 1, k) for k in range(size - 1)])
+def column_moved(value):
+    size = lax.axis_size("sz")
+    ring = list(range(size - 1, -1, -1)) + [size + k for k in range(size)]
+    return lax.ppermute(value, ("load", "sz"), [(ring[k - 1], ring[k]) for k in range(len(ring))])
 
 
 def ring_moved(value, axis):
@@ -435,24 +487,14 @@
 
 
 def swapped(value, axis, first):
-    size = lax.axis_size(axis)
-    pairs = {k: k for k in range(size)}
-    for low in range(first, size + first - 1, 2):
-        high = (low + 1) % size
-        pairs[low], pairs[high] = high, low
-    return lax.ppermute(value, axis, list(pairs.items()))
-
-
-def swapped_inside(value, axis, other):
-    size, rows = lax.axis_size(axis), lax.axis_size(other)
+    cores, size = lax.axis_size("load"), lax.axis_size(axis)
     pairs = []
-    for row in range(rows):
-        beside = row ^ 1 if (row ^ 1) < rows else row
+    for core in range(cores):
         for k in range(size):
-            inside = k + 1 if k % 2 else k - 1
-            target = (row, inside) if 0 <= inside < size else (beside, k)
-            pairs.append((row * size + k, target[0] * size + target[1]))
-    return lax.ppermute(value, (other, axis), pairs)
+            other = k + 1 if (k - first) % 2 == 0 else k - 1
+            target = core * size + other if 0 <= other < size else (cores - 1 - core) * size + k
+            pairs.append((core * size + k, target))
+    return lax.ppermute(value, ("load", axis), pairs)
 
 
 def body(displacements, density, solid, fixed):
@@ -464,13 +506,14 @@
     ]
 
     disp, fixed, density, solid, z_send, y_send = call(
-        lead_kernel,
-        [jax.ShapeDtypeStruct(arg.shape, arg.dtype) for arg in args] + [(planes, ylen, xlen), (planes * zlen, xlen)],
+        lambda *refs: lead_kernel(totals, *refs),
+        [jax.ShapeDtypeStruct(arg.shape, arg.dtype) for arg in args]
+        + [(planes + 1, ylen, xlen), (planes * zlen, xlen)],
         args,
         scratch=[pltpu.SemaphoreType.DMA((len(args),))],
         space=pltpu.HBM,
     )
-    z_in = moved(z_send, "sz")
+    z_in = column_moved(z_send)
     y_in = ring_moved(y_send, "sy")
     nodes = lambda layers: pltpu.VMEM((planes, layers, ylen + TILE, xlen), jnp.float32)
     inner = call(
@@ -490,19 +533,24 @@
     size = REACH * zlen + 2 * planes
     own, known, a_send, b_send = call(
         lambda *refs: outer_kernel(displacements.shape, *refs),
-        [(zlen, ylen, xlen), (-(-5 * planes // TILE) * TILE, xlen), (size, xlen), (size, xlen)],
+        [(zlen, ylen, xlen), (-(-(5 * planes + 1) // TILE) * TILE, xlen), (size, xlen), (size, xlen)],
         (z_in, y_in, disp, fixed, *inner),
-        scratch=[nodes(2), nodes(2), pltpu.VMEM((ylen + 2 * TILE, xlen), jnp.float32)],
+        scratch=[
+            nodes(4),
+            nodes(4),
+            pltpu.VMEM((ylen + 2 * TILE, xlen), jnp.float32),
+            pltpu.VMEM((ylen, xlen), jnp.float32),
+        ],
     )
     a_in = swapped(a_send, "sy", 0)
     b_in = swapped(b_send, "sy", 1)
     h, a_send, b_send = call(
         lambda *refs: rows_kernel(loads, comps, *refs),
-        [(zlen, ylen, xlen), (REACH, ylen, xlen), (REACH, ylen, xlen)],
-        (own, known, inner[-1], a_in, b_in),
+        [(zlen + 1, ylen, xlen), (zlen, ylen, xlen), (zlen, ylen, xlen)],
+        (own, known, a_in, b_in),
     )
     a_in = swapped(a_send, "sz", 0)
-    b_in = swapped_inside(b_send, "sz", "sy")
+    b_in = swapped(b_send, "sz", 1)
     (part,) = call(layers_kernel, [(zlen, ylen, xlen)], (h, a_in, b_in))
     parts = lax.all_gather(part, "load", axis=0)
     (out,) = call(sum_kernel, [(zlen, ylen, xlen)], (parts,))

time: 28.7 us -> 25.6 us (0.89)
  the two profiles are of different devices: /device:TPU:0 before, /device:TPU:21 now
where the time goes in v10:
time: 25.6 us; the launch traced here: 25.4 us
  waiting for transfers between devices  6.79 us (27%)
  Pallas kernels  6.64 us (26%)
  blocking collectives  6.42 us (25%)
  starting transfers between devices  5.52 us (22%)
    ppermute x4, waiting for transfers between devices, swapped(): return lax.ppermute(value, ('load', axis), pairs)  6.79 us
    pallas_call x6, Pallas kernels, call(): pl.pallas_call(kernel, out_shape=shapes, in_specs=[pl.BlockSpec(memory_sp...  6.64 us
    all_gather x1, blocking collectives, body(): parts = lax.all_gather(part, 'load', axis=0)  6.42 us
    ppermute x4, starting transfers between devices, swapped(): return lax.ppermute(value, ('load', axis), pairs)  3.05 us
    ppermute x1, starting transfers between devices, column_moved(): lax.ppermute(value, ('load', 'sz'), [(ring[k - 1], ring[k]) for k in rang...  1.31 us
    ppermute x1, starting transfers between devices, ring_moved(): return lax.ppermute(value, axis, [((k + 1) % size, k) for k in range(size)])  1.15 us
  transfers between devices with their start and end apart: 6, of which 4 were waited for; matrix products, arithmetic and copies ran while one was open for 0% of the time, Pallas kernels for 11%

profile of v10, /device:TPU:21, one launch (start us, length us, event | category | flops | bytes accessed | tf_op | source)
XLA Modules:
  0.0 25.4 jit_solution(6406421435214617882)
XLA Ops:
  0.0 1.3 %shard_map.46 = (f32[2,3,4,16,512]{4,3,2,1,0:T(8,128)S(1)}, s32[4,16,512]{2,1,0:T(8,128)S(1)}, f32[4,16,512]{2,1,0:T(8,128)S(1)}, s32[4,16,512]{2,1,0:T(8,128)S(...) custom-call(f32[2,3,4,16,512]{4,3,2,1,0:T(8,128)} %refs_0_.1, s32[4,16,512]{2,1,0:T(8,128)} %refs_1_.1, ...), custom_call_target="tpu_custom_call" | custom-call | tf_op jit(solution)/shard_map/pallas_call | solution.py:468
  1.3 1.3 %collective-permute-start = (f32[7,16,512]{2,1,0:T(8,128)S(1)}, f32[7,16,512]{2,1,0:T(8,128)S(1)}, u32[]{:S(2)}, u32[]{:S(2)}) collective-permute-start(f32[7,16,512]{2,1,0:T(8,128)S(1)} %get-tuple-element.25), channel_id=1, source_target_pairs={{19,3},{3,2},{2,1},{1,0},{0,16},{16,17},{17,18},{18,19},{23,7},{7,... | collective-permute-start | bytes 688136 | tf_op jit(solution)/shard_map/ppermute | solution.py:481
  2.6 1.2 %collective-permute-start.1 = (f32[24,512]{1,0:T(8,128)S(1)}, f32[24,512]{1,0:T(8,128)S(1)}, u32[]{:S(2)}, u32[]{:S(2)}) collective-permute-start(f32[24,512]{1,0:T(8,128)S(1)} %get-tuple-element.26), channel_id=1, source_target_pairs={{4,0},{8,4},{12,8},{0,12},{5,1},{9,5},{13,9},{1,13},{6,2},{10,6},{... | collective-permute-start | bytes 147464 | tf_op jit(solution)/shard_map/ppermute | solution.py:486
  3.8 2.8 %shard_map.47 = (f32[4,16,512]{2,1,0:T(8,128)S(1)}, f32[2,24,512]{2,1,0:T(8,128)S(1)}, f32[2,9,512]{2,1,0:T(8,128)S(1)}, f32[6,16,512]{2,1,0:T(8,128)S(1)}, f32[...) custom-call(f32[2,3,4,16,512]{4,3,2,1,0:T(8,128)S(1)} %get-tuple-element.27.refs_0_.refs_2_, ...), custom_call_target="tpu_custom_call" | custom-call | tf_op jit(solution)/shard_map/pallas_call | solution.py:468
  6.6 0.0 collective-permute-done.1.refs_1_
  6.7 0.0 collective-permute-done.refs_0_
  6.7 1.2 %shard_map.48 = (f32[4,16,512]{2,1,0:T(8,128)S(1)}, f32[32,512]{1,0:T(8,128)S(1)}, f32[24,512]{1,0:T(8,128)S(1)}, f32[24,512]{1,0:T(8,128)S(1)}) custom-call(f32[7,16,512]{2,1,0:T(8,128)S(1)} %collective-permute-done.refs_0_, f32[24,512]{1,0:T(8,128)S(1)} %collective-permute-done.1.refs_1_, f32[2,3,4,16,512]{4,3,2,1,0:T(8,128)S(1)} %get-tuple-element.27.refs_0_.refs_2_, ...), custom_call_target="tpu_custom_call" | custom-call | tf_op jit(solution)/shard_map/pallas_call | solution.py:468
  7.9 1.6 %collective-permute-start.2 = (f32[24,512]{1,0:T(8,128)S(1)}, f32[24,512]{1,0:T(8,128)S(1)}, u32[]{:S(2)}, u32[]{:S(2)}) collective-permute-start(f32[24,512]{1,0:T(8,128)S(1)} %get-tuple-element.40), channel_id=1, source_target_pairs={{0,4},{4,0},{8,12},{12,8},{16,20},{20,16},{24,28},{28,24},{1,5},{5... | collective-permute-start | bytes 147464 | tf_op jit(solution)/shard_map/ppermute | solution.py:497
  9.5 0.9 %collective-permute-start.3 = (f32[24,512]{1,0:T(8,128)S(1)}, f32[24,512]{1,0:T(8,128)S(1)}, u32[]{:S(2)}, u32[]{:S(2)}) collective-permute-start(f32[24,512]{1,0:T(8,128)S(1)} %get-tuple-element.41), channel_id=1, source_target_pairs={{0,16},{4,8},{8,4},{12,28},{16,0},{20,24},{24,20},{28,12},{1,17},{... | collective-permute-start | bytes 147464 | tf_op jit(solution)/shard_map/ppermute | solution.py:497
  10.4 0.6 %collective-permute-done.2.refs_2_ = f32[24,512]{1,0:T(8,128)S(1)} collective-permute-done((f32[24,512]{1,0:T(8,128)S(1)}, f32[24,512]{1,0:T(8,128)S(1)}, u32[]{:S(2)}, u32[]{:S(2)}) %collective-permute-start.2) | collective-permute-done | bytes 49184 | tf_op jit(solution)/shard_map/ppermute | solution.py:497
  11.0 2.4 %collective-permute-done.3.refs_3_ = f32[24,512]{1,0:T(8,128)S(1)} collective-permute-done((f32[24,512]{1,0:T(8,128)S(1)}, f32[24,512]{1,0:T(8,128)S(1)}, u32[]{:S(2)}, u32[]{:S(2)}) %collective-permute-start.3) | collective-permute-done | bytes 49184 | tf_op jit(solution)/shard_map/ppermute | solution.py:497
  13.4 0.5 %shard_map.49 = (f32[5,16,512]{2,1,0:T(8,128)S(1)}, f32[4,16,512]{2,1,0:T(8,128)S(1)}, f32[4,16,512]{2,1,0:T(8,128)S(1)}) custom-call(f32[4,16,512]{2,1,0:T(8,128)S(1)} %get-tuple-element.38.refs_0_, f32[32,512]{1,0:T(8,128)S(1)} %get-tuple-element.39.refs_1_, f32[24,512]{1,0:T(8,128)S(1)} %collective-permute-done.2.refs_2_, ...), custom_call_target="tpu_custom_call" | custom-call | tf_op jit(solution)/shard_map/pallas_call | solution.py:468
  13.9 0.6 %collective-permute-start.4 = (f32[4,16,512]{2,1,0:T(8,128)S(1)}, f32[4,16,512]{2,1,0:T(8,128)S(1)}, u32[]{:S(2)}, u32[]{:S(2)}) collective-permute-start(f32[4,16,512]{2,1,0:T(8,128)S(1)} %get-tuple-element.43), channel_id=1, source_target_pairs={{0,1},{1,0},{2,3},{3,2},{16,17},{17,16},{18,19},{19,18},{4,5},{5,4... | collective-permute-start | bytes 393224 | tf_op jit(solution)/shard_map/ppermute | solution.py:497
  14.5 0.0 collective-permute-start.5
  14.5 3.3 %collective-permute-done.4.a_in = f32[4,16,512]{2,1,0:T(8,128)S(1)} collective-permute-done((f32[4,16,512]{2,1,0:T(8,128)S(1)}, f32[4,16,512]{2,1,0:T(8,128)S(1)}, u32[]{:S(2)}, u32[]{:S(2)}) %collective-permute-start.4) | collective-permute-done | bytes 131104 | tf_op jit(solution)/shard_map/ppermute | solution.py:497
  17.8 0.5 %collective-permute-done.5.b_in = f32[4,16,512]{2,1,0:T(8,128)S(1)} collective-permute-done((f32[4,16,512]{2,1,0:T(8,128)S(1)}, f32[4,16,512]{2,1,0:T(8,128)S(1)}, u32[]{:S(2)}, u32[]{:S(2)}) %collective-permute-start.5) | collective-permute-done | bytes 131104 | tf_op jit(solution)/shard_map/ppermute | solution.py:497
  18.3 0.1 shard_map.50
  18.3 6.4 %all-gather = f32[8,16,512]{2,1,0:T(8,128)S(1)} all-gather(f32[4,16,512]{2,1,0:T(8,128)S(1)} %shard_map.50), channel_id=2, replica_groups=mesh['load'=2,'sy'=4,'sz'=4] {'load'}, dimensions={0}, use_global_device_ids=true | all-gather | bytes 393216 | tf_op jit(solution)/shard_map/all_gather | solution.py:555
  24.8 0.7 %shard_map.51 = f32[4,16,512]{2,1,0:T(8,128)} custom-call(f32[2,4,16,512]{3,2,1,0:T(8,128)S(1)} %bitcast.1), custom_call_target="tpu_custom_call" | custom-call | tf_op jit(solution)/shard_map/pallas_call | solution.py:468
Async XLA Ops:
  1.3 5.3 %collective-permute-start = (f32[7,16,512]{2,1,0:T(8,128)S(1)}, f32[7,16,512]{2,1,0:T(8,128)S(1)}, u32[]{:S(2)}, u32[]{:S(2)}) collective-permute-start(f32[7,16,512]{2,1,0:T(8,128)S(1)} %get-tuple-element.25), channel_id=1, source_target_pairs={{19,3},{3,2},{2,1},{1,0},{0,16},{16,17},{17,18},{18,19},{23,7},{7,... | collective-permute-start | bytes 688136 | tf_op jit(solution)/shard_map/ppermute | solution.py:481
  2.6 4.0 %collective-permute-start.1 = (f32[24,512]{1,0:T(8,128)S(1)}, f32[24,512]{1,0:T(8,128)S(1)}, u32[]{:S(2)}, u32[]{:S(2)}) collective-permute-start(f32[24,512]{1,0:T(8,128)S(1)} %get-tuple-element.26), channel_id=1, source_target_pairs={{4,0},{8,4},{12,8},{0,12},{5,1},{9,5},{13,9},{1,13},{6,2},{10,6},{... | collective-permute-start | bytes 147464 | tf_op jit(solution)/shard_map/ppermute | solution.py:486
  7.9 3.1 %collective-permute-start.2 = (f32[24,512]{1,0:T(8,128)S(1)}, f32[24,512]{1,0:T(8,128)S(1)}, u32[]{:S(2)}, u32[]{:S(2)}) collective-permute-start(f32[24,512]{1,0:T(8,128)S(1)} %get-tuple-element.40), channel_id=1, source_target_pairs={{0,4},{4,0},{8,12},{12,8},{16,20},{20,16},{24,28},{28,24},{1,5},{5... | collective-permute-start | bytes 147464 | tf_op jit(solution)/shard_map/ppermute | solution.py:497
  9.5 3.8 %collective-permute-start.3 = (f32[24,512]{1,0:T(8,128)S(1)}, f32[24,512]{1,0:T(8,128)S(1)}, u32[]{:S(2)}, u32[]{:S(2)}) collective-permute-start(f32[24,512]{1,0:T(8,128)S(1)} %get-tuple-element.41), channel_id=1, source_target_pairs={{0,16},{4,8},{8,4},{12,28},{16,0},{20,24},{24,20},{28,12},{1,17},{... | collective-permute-start | bytes 147464 | tf_op jit(solution)/shard_map/ppermute | solution.py:497
  13.9 3.9 %collective-permute-start.4 = (f32[4,16,512]{2,1,0:T(8,128)S(1)}, f32[4,16,512]{2,1,0:T(8,128)S(1)}, u32[]{:S(2)}, u32[]{:S(2)}) collective-permute-start(f32[4,16,512]{2,1,0:T(8,128)S(1)} %get-tuple-element.43), channel_id=1, source_target_pairs={{0,1},{1,0},{2,3},{3,2},{16,17},{17,16},{18,19},{19,18},{4,5},{5,4... | collective-permute-start | bytes 393224 | tf_op jit(solution)/shard_map/ppermute | solution.py:497
  14.5 3.8 %collective-permute-start.5 = (f32[4,16,512]{2,1,0:T(8,128)S(1)}, f32[4,16,512]{2,1,0:T(8,128)S(1)}, u32[]{:S(2)}, u32[]{:S(2)}) collective-permute-start(f32[4,16,512]{2,1,0:T(8,128)S(1)} %get-tuple-element.44), channel_id=1, source_target_pairs={{0,16},{1,2},{2,1},{3,19},{16,0},{17,18},{18,17},{19,3},{4,20},{5,... | collective-permute-start | bytes 393224 | tf_op jit(solution)/shard_map/ppermute | solution.py:497

commit v11 on v10

--- a/solution.py
+++ b/solution.py
@@ -384,7 +384,7 @@
     b_out[...] = jnp.where(even, down, up)
 
 
-def rows_kernel(loads, comps, own, known, a_in, b_in, h_out, a_out, b_out):
+def rows_kernel(loads, comps, own, known, b_in, a_in, h_out, p_out, q_out):
     zlen, ylen, xlen = own.shape
     planes = loads * comps
     index, last = lax.axis_index("sy"), lax.axis_size("sy") - 1
@@ -443,17 +443,18 @@
         h_out[at] = own[z]
         h_out[at, :TILE] += head
         h_out[at, ylen - TILE :] += tail
-    high = (lax.axis_index("sz") % 2 == 0).astype(jnp.int32)
-    a_out[...] = h_out[pl.ds(high, zlen)]
-    b_out[...] = h_out[pl.ds(1 - high, zlen)]
-
-
-def layers_kernel(h, a_in, b_in, out):
+    p_out[...] = h_out[pl.ds(jnp.where(first_core, 1, zlen + 1 - REACH), REACH)]
+    q_out[...] = h_out[pl.ds(jnp.where(first_core, 1, 0), zlen)]
+
+
+def layers_kernel(h, p_in, q_in, out):
     zlen = out.shape[0]
     index, last = lax.axis_index("sz"), lax.axis_size("sz") - 1
-    even = index % 2 == 0
-    below = [jnp.where(index > 0, jnp.where(even, b_in[k], a_in[k]), 0.0) for k in range(zlen - REACH, zlen)]
-    above = [jnp.where(index < last, jnp.where(even, a_in[k], b_in[k]), 0.0) for k in range(zlen)]
+    first_core = on_first()
+    below = [jnp.where(first_core, q_in[zlen - REACH + k], p_in[k]) for k in range(REACH)]
+    above = [jnp.where(first_core, p_in[k - 1] if k else 0.0, q_in[k]) for k in range(zlen)]
+    below = [jnp.where(index > 0, layer, 0.0) for layer in below]
+    above = [jnp.where(index < last, layer, 0.0) for layer in above]
     layers = below[:-1] + [below[-1] + h[0]] + [h[z] for z in range(1, zlen)] + [h[zlen] + above[0]] + above[1:]
     for z, layer in enumerate(spread_layers(layers)):
         out[z] = layer
@@ -475,9 +476,11 @@
     )(*args)
 
 
-def column_moved(value):
+def column_moved(value, back=False):
     size = lax.axis_size("sz")
     ring = list(range(size - 1, -1, -1)) + [size + k for k in range(size)]
+    if back:
+        ring.reverse()
     return lax.ppermute(value, ("load", "sz"), [(ring[k - 1], ring[k]) for k in range(len(ring))])
 
 
@@ -542,16 +545,16 @@
             pltpu.VMEM((ylen, xlen), jnp.float32),
         ],
     )
+    b_in = swapped(b_send, "sy", 1)
     a_in = swapped(a_send, "sy", 0)
-    b_in = swapped(b_send, "sy", 1)
-    h, a_send, b_send = call(
+    h, p_send, q_send = call(
         lambda *refs: rows_kernel(loads, comps, *refs),
-        [(zlen + 1, ylen, xlen), (zlen, ylen, xlen), (zlen, ylen, xlen)],
-        (own, known, a_in, b_in),
-    )
-    a_in = swapped(a_send, "sz", 0)
-    b_in = swapped(b_send, "sz", 1)
-    (part,) = call(layers_kernel, [(zlen, ylen, xlen)], (h, a_in, b_in))
+        [(zlen + 1, ylen, xlen), (REACH, ylen, xlen), (zlen, ylen, xlen)],
+        (own, known, b_in, a_in),
+    )
+    p_in = column_moved(p_send)
+    q_in = column_moved(q_send, back=True)
+    (part,) = call(layers_kernel, [(zlen, ylen, xlen)], (h, p_in, q_in))
     parts = lax.all_gather(part, "load", axis=0)
     (out,) = call(sum_kernel, [(zlen, ylen, xlen)], (parts,))
     return out

time: 25.6 us -> 25.3 us (0.988)
  the two profiles are of different devices: /device:TPU:21 before, /device:TPU:0 now
where the time goes in v11:
time: 25.3 us; the launch traced here: 25.1 us
  starting transfers between devices  9.06 us (36%)
  waiting for transfers between devices  7.4 us (29%)
  Pallas kernels  6.64 us (26%)
  blocking collectives  1.99 us (8%)
    pallas_call x6, Pallas kernels, call(): pl.pallas_call(kernel, out_shape=shapes, in_specs=[pl.BlockSpec(memory_sp...  6.64 us
    ppermute x3, waiting for transfers between devices, column_moved(): lax.ppermute(value, ('load', 'sz'), [(ring[k - 1], ring[k]) for k in rang...  4.81 us
    ppermute x1, starting transfers between devices, ring_moved(): return lax.ppermute(value, axis, [((k + 1) % size, k) for k in range(size)])  3.51 us
    ppermute x2, starting transfers between devices, swapped(): return lax.ppermute(value, ('load', axis), pairs)  3.49 us
    ppermute x2, waiting for transfers between devices, swapped(): return lax.ppermute(value, ('load', axis), pairs)  2.59 us
    ppermute x3, starting transfers between devices, column_moved(): lax.ppermute(value, ('load', 'sz'), [(ring[k - 1], ring[k]) for k in rang...  2.06 us
    all_gather x1, blocking collectives, body(): parts = lax.all_gather(part, 'load', axis=0)  1.99 us
  transfers between devices with their start and end apart: 6, of which 3 were waited for; matrix products, arithmetic and copies ran while one was open for 0% of the time, Pallas kernels for 11%

profile of v11, /device:TPU:0, one launch (start us, length us, event | category | flops | bytes accessed | tf_op | source)
XLA Modules:
  0.0 25.1 jit_solution(9563925642595183668)
XLA Ops:
  0.0 1.3 %shard_map.46 = (f32[2,3,4,16,512]{4,3,2,1,0:T(8,128)S(1)}, s32[4,16,512]{2,1,0:T(8,128)S(1)}, f32[4,16,512]{2,1,0:T(8,128)S(1)}, s32[4,16,512]{2,1,0:T(8,128)S(...) custom-call(f32[2,3,4,16,512]{4,3,2,1,0:T(8,128)} %refs_0_.1, s32[4,16,512]{2,1,0:T(8,128)} %refs_1_.1, ...), custom_call_target="tpu_custom_call" | custom-call | tf_op jit(solution)/shard_map/pallas_call | solution.py:469
  1.3 0.5 %collective-permute-start = (f32[7,16,512]{2,1,0:T(8,128)S(1)}, f32[7,16,512]{2,1,0:T(8,128)S(1)}, u32[]{:S(2)}, u32[]{:S(2)}) collective-permute-start(f32[7,16,512]{2,1,0:T(8,128)S(1)} %get-tuple-element.25), channel_id=1, source_target_pairs={{19,3},{3,2},{2,1},{1,0},{0,16},{16,17},{17,18},{18,19},{23,7},{7,... | collective-permute-start | bytes 688136 | tf_op jit(solution)/shard_map/ppermute | solution.py:484
  1.8 3.5 %collective-permute-start.1 = (f32[24,512]{1,0:T(8,128)S(1)}, f32[24,512]{1,0:T(8,128)S(1)}, u32[]{:S(2)}, u32[]{:S(2)}) collective-permute-start(f32[24,512]{1,0:T(8,128)S(1)} %get-tuple-element.26), channel_id=1, source_target_pairs={{4,0},{8,4},{12,8},{0,12},{5,1},{9,5},{13,9},{1,13},{6,2},{10,6},{... | collective-permute-start | bytes 147464 | tf_op jit(solution)/shard_map/ppermute | solution.py:489
  5.3 2.9 %shard_map.47 = (f32[4,16,512]{2,1,0:T(8,128)S(1)}, f32[2,24,512]{2,1,0:T(8,128)S(1)}, f32[2,9,512]{2,1,0:T(8,128)S(1)}, f32[6,16,512]{2,1,0:T(8,128)S(1)}, f32[...) custom-call(f32[2,3,4,16,512]{4,3,2,1,0:T(8,128)S(1)} %get-tuple-element.27.refs_0_.refs_2_, ...), custom_call_target="tpu_custom_call" | custom-call | tf_op jit(solution)/shard_map/pallas_call | solution.py:469
  8.2 0.0 collective-permute-done.1.refs_1_
  8.2 0.2 collective-permute-done.refs_0_
  8.4 1.2 %shard_map.48 = (f32[4,16,512]{2,1,0:T(8,128)S(1)}, f32[32,512]{1,0:T(8,128)S(1)}, f32[24,512]{1,0:T(8,128)S(1)}, f32[24,512]{1,0:T(8,128)S(1)}) custom-call(f32[7,16,512]{2,1,0:T(8,128)S(1)} %collective-permute-done.refs_0_, f32[24,512]{1,0:T(8,128)S(1)} %collective-permute-done.1.refs_1_, f32[2,3,4,16,512]{4,3,2,1,0:T(8,128)S(1)} %get-tuple-element.27.refs_0_.refs_2_, ...), custom_call_target="tpu_custom_call" | custom-call | tf_op jit(solution)/shard_map/pallas_call | solution.py:469
  9.6 0.7 %collective-permute-start.2 = (f32[24,512]{1,0:T(8,128)S(1)}, f32[24,512]{1,0:T(8,128)S(1)}, u32[]{:S(2)}, u32[]{:S(2)}) collective-permute-start(f32[24,512]{1,0:T(8,128)S(1)} %get-tuple-element.40), channel_id=1, source_target_pairs={{0,16},{4,8},{8,4},{12,28},{16,0},{20,24},{24,20},{28,12},{1,17},{... | collective-permute-start | bytes 147464 | tf_op jit(solution)/shard_map/ppermute | solution.py:500
  10.3 2.8 %collective-permute-start.3 = (f32[24,512]{1,0:T(8,128)S(1)}, f32[24,512]{1,0:T(8,128)S(1)}, u32[]{:S(2)}, u32[]{:S(2)}) collective-permute-start(f32[24,512]{1,0:T(8,128)S(1)} %get-tuple-element.41), channel_id=1, source_target_pairs={{0,4},{4,0},{8,12},{12,8},{16,20},{20,16},{24,28},{28,24},{1,5},{5... | collective-permute-start | bytes 147464 | tf_op jit(solution)/shard_map/ppermute | solution.py:500
  13.1 0.0 collective-permute-done.2.refs_2_
  13.1 2.6 %collective-permute-done.3.refs_3_ = f32[24,512]{1,0:T(8,128)S(1)} collective-permute-done((f32[24,512]{1,0:T(8,128)S(1)}, f32[24,512]{1,0:T(8,128)S(1)}, u32[]{:S(2)}, u32[]{:S(2)}) %collective-permute-start.3) | collective-permute-done | bytes 49184 | tf_op jit(solution)/shard_map/ppermute | solution.py:500
  15.7 0.5 %shard_map.49 = (f32[5,16,512]{2,1,0:T(8,128)S(1)}, f32[3,16,512]{2,1,0:T(8,128)S(1)}, f32[4,16,512]{2,1,0:T(8,128)S(1)}) custom-call(f32[4,16,512]{2,1,0:T(8,128)S(1)} %get-tuple-element.38.refs_0_, f32[32,512]{1,0:T(8,128)S(1)} %get-tuple-element.39.refs_1_, f32[24,512]{1,0:T(8,128)S(1)} %collective-permute-done.2.refs_2_, ...), custom_call_target="tpu_custom_call" | custom-call | tf_op jit(solution)/shard_map/pallas_call | solution.py:469
  16.2 1.6 %collective-permute-start.5 = (f32[4,16,512]{2,1,0:T(8,128)S(1)}, f32[4,16,512]{2,1,0:T(8,128)S(1)}, u32[]{:S(2)}, u32[]{:S(2)}) collective-permute-start(f32[4,16,512]{2,1,0:T(8,128)S(1)} %get-tuple-element.44), channel_id=1, source_target_pairs={{3,19},{19,18},{18,17},{17,16},{16,0},{0,1},{1,2},{2,3},{7,23},{23... | collective-permute-start | bytes 393224 | tf_op jit(solution)/shard_map/ppermute | solution.py:484
  17.8 0.0 collective-permute-start.4
  17.8 4.6 %collective-permute-done.4.p_in = f32[3,16,512]{2,1,0:T(8,128)S(1)} collective-permute-done((f32[3,16,512]{2,1,0:T(8,128)S(1)}, f32[3,16,512]{2,1,0:T(8,128)S(1)}, u32[]{:S(2)}, u32[]{:S(2)}) %collective-permute-start.4) | collective-permute-done | bytes 98336 | tf_op jit(solution)/shard_map/ppermute | solution.py:484
  22.4 0.0 collective-permute-done.5.q_in
  22.4 0.1 shard_map.50
  22.5 2.0 %all-gather = f32[8,16,512]{2,1,0:T(8,128)S(1)} all-gather(f32[4,16,512]{2,1,0:T(8,128)S(1)} %shard_map.50), channel_id=2, replica_groups=mesh['load'=2,'sy'=4,'sz'=4] {'load'}, dimensions={0}, use_global_device_ids=true | all-gather | bytes 393216 | tf_op jit(solution)/shard_map/all_gather | solution.py:558
  24.5 0.7 %shard_map.51 = f32[4,16,512]{2,1,0:T(8,128)} custom-call(f32[2,4,16,512]{3,2,1,0:T(8,128)S(1)} %bitcast.1), custom_call_target="tpu_custom_call" | custom-call | tf_op jit(solution)/shard_map/pallas_call | solution.py:469
Async XLA Ops:
  1.3 7.0 %collective-permute-start = (f32[7,16,512]{2,1,0:T(8,128)S(1)}, f32[7,16,512]{2,1,0:T(8,128)S(1)}, u32[]{:S(2)}, u32[]{:S(2)}) collective-permute-start(f32[7,16,512]{2,1,0:T(8,128)S(1)} %get-tuple-element.25), channel_id=1, source_target_pairs={{19,3},{3,2},{2,1},{1,0},{0,16},{16,17},{17,18},{18,19},{23,7},{7,... | collective-permute-start | bytes 688136 | tf_op jit(solution)/shard_map/ppermute | solution.py:484
  1.8 6.4 %collective-permute-start.1 = (f32[24,512]{1,0:T(8,128)S(1)}, f32[24,512]{1,0:T(8,128)S(1)}, u32[]{:S(2)}, u32[]{:S(2)}) collective-permute-start(f32[24,512]{1,0:T(8,128)S(1)} %get-tuple-element.26), channel_id=1, source_target_pairs={{4,0},{8,4},{12,8},{0,12},{5,1},{9,5},{13,9},{1,13},{6,2},{10,6},{... | collective-permute-start | bytes 147464 | tf_op jit(solution)/shard_map/ppermute | solution.py:489
  9.6 3.5 %collective-permute-start.2 = (f32[24,512]{1,0:T(8,128)S(1)}, f32[24,512]{1,0:T(8,128)S(1)}, u32[]{:S(2)}, u32[]{:S(2)}) collective-permute-start(f32[24,512]{1,0:T(8,128)S(1)} %get-tuple-element.40), channel_id=1, source_target_pairs={{0,16},{4,8},{8,4},{12,28},{16,0},{20,24},{24,20},{28,12},{1,17},{... | collective-permute-start | bytes 147464 | tf_op jit(solution)/shard_map/ppermute | solution.py:500
  10.3 5.4 %collective-permute-start.3 = (f32[24,512]{1,0:T(8,128)S(1)}, f32[24,512]{1,0:T(8,128)S(1)}, u32[]{:S(2)}, u32[]{:S(2)}) collective-permute-start(f32[24,512]{1,0:T(8,128)S(1)} %get-tuple-element.41), channel_id=1, source_target_pairs={{0,4},{4,0},{8,12},{12,8},{16,20},{20,16},{24,28},{28,24},{1,5},{5... | collective-permute-start | bytes 147464 | tf_op jit(solution)/shard_map/ppermute | solution.py:500
  16.2 6.2 %collective-permute-start.5 = (f32[4,16,512]{2,1,0:T(8,128)S(1)}, f32[4,16,512]{2,1,0:T(8,128)S(1)}, u32[]{:S(2)}, u32[]{:S(2)}) collective-permute-start(f32[4,16,512]{2,1,0:T(8,128)S(1)} %get-tuple-element.44), channel_id=1, source_target_pairs={{3,19},{19,18},{18,17},{17,16},{16,0},{0,1},{1,2},{2,3},{7,23},{23... | collective-permute-start | bytes 393224 | tf_op jit(solution)/shard_map/ppermute | solution.py:484
  17.8 4.6 %collective-permute-start.4 = (f32[3,16,512]{2,1,0:T(8,128)S(1)}, f32[3,16,512]{2,1,0:T(8,128)S(1)}, u32[]{:S(2)}, u32[]{:S(2)}) collective-permute-start(f32[3,16,512]{2,1,0:T(8,128)S(1)} %get-tuple-element.43), channel_id=1, source_target_pairs={{19,3},{3,2},{2,1},{1,0},{0,16},{16,17},{17,18},{18,19},{23,7},{7,... | collective-permute-start | bytes 294920 | tf_op jit(solution)/shard_map/ppermute | solution.py:484

commit v12 on v11

--- a/solution.py
+++ b/solution.py
@@ -140,11 +140,11 @@
     rows, length = value.shape
     wide = jnp.concatenate([value, jnp.zeros((rows, LANES), jnp.float32)], axis=1)
     span = length + LANES
-    wide = wide + pltpu.roll(wide, span - 1, 1)
-    wide = wide + pltpu.roll(wide, span - 2, 1)
-    wide = wide + pltpu.roll(wide, 1, 1)
-    wide = wide + pltpu.roll(wide, 2, 1)
-    return wide[:, :length]
+    total = float(ROWS) * value
+    for step in range(1, ROWS):
+        both = pltpu.roll(wide, span - step, 1) + pltpu.roll(wide, step, 1)
+        total = total + float(ROWS - step) * both[:, :length]
+    return total
 
 
 def spread_layers(layers):
@@ -460,8 +460,8 @@
         out[z] = layer
 
 
-def sum_kernel(parts, out):
-    out[...] = parts[0] + parts[1]
+def sum_kernel(part, other, out):
+    out[...] = part[...] + other[...]
 
 
 def call(kernel, outs, args, scratch=(), space=pltpu.VMEM):
@@ -555,8 +555,9 @@
     p_in = column_moved(p_send)
     q_in = column_moved(q_send, back=True)
     (part,) = call(layers_kernel, [(zlen, ylen, xlen)], (h, p_in, q_in))
-    parts = lax.all_gather(part, "load", axis=0)
-    (out,) = call(sum_kernel, [(zlen, ylen, xlen)], (parts,))
+    cores = lax.axis_size("load")
+    other = lax.ppermute(part, "load", [(core, cores - 1 - core) for core in range(cores)])
+    (out,) = call(sum_kernel, [(zlen, ylen, xlen)], (part, other))
     return out
 
 

time: 25.3 us -> 24.3 us (0.960)
  blocking collectives: 1.99 us -> 0 us
  waiting for transfers between devices: 7.4 us -> 8.91 us
  Pallas kernels: 6.64 us -> 6.06 us
    all_gather x1 -> x0, blocking collectives: 1.99 us -> none  [body(): parts = lax.all_gather(part, 'load', axis=0)]
    ppermute x0 -> x1, waiting for transfers between devices: none -> 1.33 us  [body(): lax.ppermute(part, 'load', [(core, cores - 1 - core) for core in range(co...]
    pallas_call x6, Pallas kernels: 6.64 us -> 6.06 us  [call(): pl.pallas_call(kernel, out_shape=shapes, in_specs=[pl.BlockSpec(memory_sp...]
  transfers between devices with their start and end apart: 6 -> 7, of which waited for: 3 -> 4; matrix products, arithmetic and copies ran while one was open for 0% -> 0% of each run, Pallas kernels for 11% -> 11%
where the time goes in v12:
time: 24.3 us; the launch traced here: 24.2 us
  starting transfers between devices  9.13 us (38%)
  waiting for transfers between devices  8.91 us (37%)
  Pallas kernels  6.06 us (25%)
    pallas_call x6, Pallas kernels, call(): pl.pallas_call(kernel, out_shape=shapes, in_specs=[pl.BlockSpec(memory_sp...  6.06 us
    ppermute x3, waiting for transfers between devices, column_moved(): lax.ppermute(value, ('load', 'sz'), [(ring[k - 1], ring[k]) for k in rang...  4.98 us
    ppermute x1, starting transfers between devices, ring_moved(): return lax.ppermute(value, axis, [((k + 1) % size, k) for k in range(size)])  3.51 us
    ppermute x2, starting transfers between devices, swapped(): return lax.ppermute(value, ('load', axis), pairs)  3.49 us
    ppermute x2, waiting for transfers between devices, swapped(): return lax.ppermute(value, ('load', axis), pairs)  2.59 us
    ppermute x3, starting transfers between devices, column_moved(): lax.ppermute(value, ('load', 'sz'), [(ring[k - 1], ring[k]) for k in rang...  2.06 us
    ppermute x1, waiting for transfers between devices, body(): lax.ppermute(part, 'load', [(core, cores - 1 - core) for core in range(co...  1.33 us
  transfers between devices with their start and end apart: 7, of which 4 were waited for; matrix products, arithmetic and copies ran while one was open for 0% of the time, Pallas kernels for 11%

profile of v12, /device:TPU:0, one launch (start us, length us, event | category | flops | bytes accessed | tf_op | source)
XLA Modules:
  0.0 24.2 jit_solution(16950660800485284445)
XLA Ops:
  0.0 1.3 %shard_map.46 = (f32[2,3,4,16,512]{4,3,2,1,0:T(8,128)S(1)}, s32[4,16,512]{2,1,0:T(8,128)S(1)}, f32[4,16,512]{2,1,0:T(8,128)S(1)}, s32[4,16,512]{2,1,0:T(8,128)S(...) custom-call(f32[2,3,4,16,512]{4,3,2,1,0:T(8,128)} %refs_0_.1, s32[4,16,512]{2,1,0:T(8,128)} %refs_1_.1, ...), custom_call_target="tpu_custom_call" | custom-call | tf_op jit(solution)/shard_map/pallas_call | solution.py:469
  1.3 0.5 %collective-permute-start = (f32[7,16,512]{2,1,0:T(8,128)S(1)}, f32[7,16,512]{2,1,0:T(8,128)S(1)}, u32[]{:S(2)}, u32[]{:S(2)}) collective-permute-start(f32[7,16,512]{2,1,0:T(8,128)S(1)} %get-tuple-element.25), channel_id=1, source_target_pairs={{19,3},{3,2},{2,1},{1,0},{0,16},{16,17},{17,18},{18,19},{23,7},{7,... | collective-permute-start | bytes 688136 | tf_op jit(solution)/shard_map/ppermute | solution.py:484
  1.8 3.5 %collective-permute-start.1 = (f32[24,512]{1,0:T(8,128)S(1)}, f32[24,512]{1,0:T(8,128)S(1)}, u32[]{:S(2)}, u32[]{:S(2)}) collective-permute-start(f32[24,512]{1,0:T(8,128)S(1)} %get-tuple-element.26), channel_id=1, source_target_pairs={{4,0},{8,4},{12,8},{0,12},{5,1},{9,5},{13,9},{1,13},{6,2},{10,6},{... | collective-permute-start | bytes 147464 | tf_op jit(solution)/shard_map/ppermute | solution.py:489
  5.3 2.7 %shard_map.47 = (f32[4,16,512]{2,1,0:T(8,128)S(1)}, f32[2,24,512]{2,1,0:T(8,128)S(1)}, f32[2,9,512]{2,1,0:T(8,128)S(1)}, f32[6,16,512]{2,1,0:T(8,128)S(1)}, f32[...) custom-call(f32[2,3,4,16,512]{4,3,2,1,0:T(8,128)S(1)} %get-tuple-element.27.refs_0_.refs_2_, ...), custom_call_target="tpu_custom_call" | custom-call | tf_op jit(solution)/shard_map/pallas_call | solution.py:469
  8.0 0.0 collective-permute-done.1.refs_1_
  8.0 0.4 %collective-permute-done.refs_0_ = f32[7,16,512]{2,1,0:T(8,128)S(1)} collective-permute-done((f32[7,16,512]{2,1,0:T(8,128)S(1)}, f32[7,16,512]{2,1,0:T(8,128)S(1)}, u32[]{:S(2)}, u32[]{:S(2)}) %collective-permute-start) | collective-permute-done | bytes 229408 | tf_op jit(solution)/shard_map/ppermute | solution.py:484
  8.4 1.0 %shard_map.48 = (f32[4,16,512]{2,1,0:T(8,128)S(1)}, f32[32,512]{1,0:T(8,128)S(1)}, f32[24,512]{1,0:T(8,128)S(1)}, f32[24,512]{1,0:T(8,128)S(1)}) custom-call(f32[7,16,512]{2,1,0:T(8,128)S(1)} %collective-permute-done.refs_0_, f32[24,512]{1,0:T(8,128)S(1)} %collective-permute-done.1.refs_1_, f32[2,3,4,16,512]{4,3,2,1,0:T(8,128)S(1)} %get-tuple-element.27.refs_0_.refs_2_, ...), custom_call_target="tpu_custom_call" | custom-call | tf_op jit(solution)/shard_map/pallas_call | solution.py:469
  9.4 0.5 %collective-permute-start.2 = (f32[24,512]{1,0:T(8,128)S(1)}, f32[24,512]{1,0:T(8,128)S(1)}, u32[]{:S(2)}, u32[]{:S(2)}) collective-permute-start(f32[24,512]{1,0:T(8,128)S(1)} %get-tuple-element.40), channel_id=1, source_target_pairs={{0,16},{4,8},{8,4},{12,28},{16,0},{20,24},{24,20},{28,12},{1,17},{... | collective-permute-start | bytes 147464 | tf_op jit(solution)/shard_map/ppermute | solution.py:500
  9.9 3.0 %collective-permute-start.3 = (f32[24,512]{1,0:T(8,128)S(1)}, f32[24,512]{1,0:T(8,128)S(1)}, u32[]{:S(2)}, u32[]{:S(2)}) collective-permute-start(f32[24,512]{1,0:T(8,128)S(1)} %get-tuple-element.41), channel_id=1, source_target_pairs={{0,4},{4,0},{8,12},{12,8},{16,20},{20,16},{24,28},{28,24},{1,5},{5... | collective-permute-start | bytes 147464 | tf_op jit(solution)/shard_map/ppermute | solution.py:500
  12.9 0.0 collective-permute-done.2.refs_2_
  12.9 2.6 %collective-permute-done.3.refs_3_ = f32[24,512]{1,0:T(8,128)S(1)} collective-permute-done((f32[24,512]{1,0:T(8,128)S(1)}, f32[24,512]{1,0:T(8,128)S(1)}, u32[]{:S(2)}, u32[]{:S(2)}) %collective-permute-start.3) | collective-permute-done | bytes 49184 | tf_op jit(solution)/shard_map/ppermute | solution.py:500
  15.5 0.3 %shard_map.49 = (f32[5,16,512]{2,1,0:T(8,128)S(1)}, f32[3,16,512]{2,1,0:T(8,128)S(1)}, f32[4,16,512]{2,1,0:T(8,128)S(1)}) custom-call(f32[4,16,512]{2,1,0:T(8,128)S(1)} %get-tuple-element.38.refs_0_, f32[32,512]{1,0:T(8,128)S(1)} %get-tuple-element.39.refs_1_, f32[24,512]{1,0:T(8,128)S(1)} %collective-permute-done.2.refs_2_, ...), custom_call_target="tpu_custom_call" | custom-call | tf_op jit(solution)/shard_map/pallas_call | solution.py:469
  15.8 1.6 %collective-permute-start.5 = (f32[4,16,512]{2,1,0:T(8,128)S(1)}, f32[4,16,512]{2,1,0:T(8,128)S(1)}, u32[]{:S(2)}, u32[]{:S(2)}) collective-permute-start(f32[4,16,512]{2,1,0:T(8,128)S(1)} %get-tuple-element.44), channel_id=1, source_target_pairs={{3,19},{19,18},{18,17},{17,16},{16,0},{0,1},{1,2},{2,3},{7,23},{23... | collective-permute-start | bytes 393224 | tf_op jit(solution)/shard_map/ppermute | solution.py:484
  17.4 0.0 collective-permute-start.4
  17.4 4.6 %collective-permute-done.4.p_in = f32[3,16,512]{2,1,0:T(8,128)S(1)} collective-permute-done((f32[3,16,512]{2,1,0:T(8,128)S(1)}, f32[3,16,512]{2,1,0:T(8,128)S(1)}, u32[]{:S(2)}, u32[]{:S(2)}) %collective-permute-start.4) | collective-permute-done | bytes 98336 | tf_op jit(solution)/shard_map/ppermute | solution.py:484
  22.0 0.0 collective-permute-done.5.q_in
  22.0 0.1 shard_map.50.part
  22.1 0.1 collective-permute-start.6
  22.2 1.3 %collective-permute-done.6.other = f32[4,16,512]{2,1,0:T(8,128)S(1)} collective-permute-done((f32[4,16,512]{2,1,0:T(8,128)S(1)}, f32[4,16,512]{2,1,0:T(8,128)S(1)}, u32[]{:S(2)}, u32[]{:S(2)}) %collective-permute-start.6) | collective-permute-done | bytes 131104 | tf_op jit(solution)/shard_map/ppermute | solution.py:559
  23.5 0.7 %shard_map.51 = f32[4,16,512]{2,1,0:T(8,128)} custom-call(f32[4,16,512]{2,1,0:T(8,128)S(1)} %shard_map.50.part, f32[4,16,512]{2,1,0:T(8,128)S(1)} %collective-permute-done.6.other), custom_call_target="tpu_custom_call" | custom-call | tf_op jit(solution)/shard_map/pallas_call | solution.py:469
Async XLA Ops:
  1.3 7.0 %collective-permute-start = (f32[7,16,512]{2,1,0:T(8,128)S(1)}, f32[7,16,512]{2,1,0:T(8,128)S(1)}, u32[]{:S(2)}, u32[]{:S(2)}) collective-permute-start(f32[7,16,512]{2,1,0:T(8,128)S(1)} %get-tuple-element.25), channel_id=1, source_target_pairs={{19,3},{3,2},{2,1},{1,0},{0,16},{16,17},{17,18},{18,19},{23,7},{7,... | collective-permute-start | bytes 688136 | tf_op jit(solution)/shard_map/ppermute | solution.py:484
  1.8 6.2 %collective-permute-start.1 = (f32[24,512]{1,0:T(8,128)S(1)}, f32[24,512]{1,0:T(8,128)S(1)}, u32[]{:S(2)}, u32[]{:S(2)}) collective-permute-start(f32[24,512]{1,0:T(8,128)S(1)} %get-tuple-element.26), channel_id=1, source_target_pairs={{4,0},{8,4},{12,8},{0,12},{5,1},{9,5},{13,9},{1,13},{6,2},{10,6},{... | collective-permute-start | bytes 147464 | tf_op jit(solution)/shard_map/ppermute | solution.py:489
  9.4 3.5 %collective-permute-start.2 = (f32[24,512]{1,0:T(8,128)S(1)}, f32[24,512]{1,0:T(8,128)S(1)}, u32[]{:S(2)}, u32[]{:S(2)}) collective-permute-start(f32[24,512]{1,0:T(8,128)S(1)} %get-tuple-element.40), channel_id=1, source_target_pairs={{0,16},{4,8},{8,4},{12,28},{16,0},{20,24},{24,20},{28,12},{1,17},{... | collective-permute-start | bytes 147464 | tf_op jit(solution)/shard_map/ppermute | solution.py:500
  9.9 5.6 %collective-permute-start.3 = (f32[24,512]{1,0:T(8,128)S(1)}, f32[24,512]{1,0:T(8,128)S(1)}, u32[]{:S(2)}, u32[]{:S(2)}) collective-permute-start(f32[24,512]{1,0:T(8,128)S(1)} %get-tuple-element.41), channel_id=1, source_target_pairs={{0,4},{4,0},{8,12},{12,8},{16,20},{20,16},{24,28},{28,24},{1,5},{5... | collective-permute-start | bytes 147464 | tf_op jit(solution)/shard_map/ppermute | solution.py:500
  15.8 6.2 %collective-permute-start.5 = (f32[4,16,512]{2,1,0:T(8,128)S(1)}, f32[4,16,512]{2,1,0:T(8,128)S(1)}, u32[]{:S(2)}, u32[]{:S(2)}) collective-permute-start(f32[4,16,512]{2,1,0:T(8,128)S(1)} %get-tuple-element.44), channel_id=1, source_target_pairs={{3,19},{19,18},{18,17},{17,16},{16,0},{0,1},{1,2},{2,3},{7,23},{23... | collective-permute-start | bytes 393224 | tf_op jit(solution)/shard_map/ppermute | solution.py:484
  17.4 4.6 %collective-permute-start.4 = (f32[3,16,512]{2,1,0:T(8,128)S(1)}, f32[3,16,512]{2,1,0:T(8,128)S(1)}, u32[]{:S(2)}, u32[]{:S(2)}) collective-permute-start(f32[3,16,512]{2,1,0:T(8,128)S(1)} %get-tuple-element.43), channel_id=1, source_target_pairs={{19,3},{3,2},{2,1},{1,0},{0,16},{16,17},{17,18},{18,19},{23,7},{7,... | collective-permute-start | bytes 294920 | tf_op jit(solution)/shard_map/ppermute | solution.py:484
  22.1 1.4 %collective-permute-start.6 = (f32[4,16,512]{2,1,0:T(8,128)S(1)}, f32[4,16,512]{2,1,0:T(8,128)S(1)}, u32[]{:S(2)}, u32[]{:S(2)}) collective-permute-start(f32[4,16,512]{2,1,0:T(8,128)S(1)} %shard_map.50.part), channel_id=1, source_target_pairs={{0,16},{16,0},{1,17},{17,1},{2,18},{18,2},{3,19},{19,3},{4,20},{20... | collective-permute-start | bytes 393224 | tf_op jit(solution)/shard_map/ppermute | solution.py:559

commit v13 on v10

--- a/solution.py
+++ b/solution.py
@@ -140,11 +140,11 @@
     rows, length = value.shape
     wide = jnp.concatenate([value, jnp.zeros((rows, LANES), jnp.float32)], axis=1)
     span = length + LANES
-    wide = wide + pltpu.roll(wide, span - 1, 1)
-    wide = wide + pltpu.roll(wide, span - 2, 1)
-    wide = wide + pltpu.roll(wide, 1, 1)
-    wide = wide + pltpu.roll(wide, 2, 1)
-    return wide[:, :length]
+    total = float(ROWS) * value
+    for step in range(1, ROWS):
+        both = pltpu.roll(wide, span - step, 1) + pltpu.roll(wide, step, 1)
+        total = total + float(ROWS - step) * both[:, :length]
+    return total
 
 
 def spread_layers(layers):
@@ -384,7 +384,7 @@
     b_out[...] = jnp.where(even, down, up)
 
 
-def rows_kernel(loads, comps, own, known, a_in, b_in, h_out, a_out, b_out):
+def rows_kernel(loads, comps, own, known, b_in, a_in, h_out, a_out, b_out):
     zlen, ylen, xlen = own.shape
     planes = loads * comps
     index, last = lax.axis_index("sy"), lax.axis_size("sy") - 1
@@ -459,8 +459,8 @@
         out[z] = layer
 
 
-def sum_kernel(parts, out):
-    out[...] = parts[0] + parts[1]
+def sum_kernel(part, other, out):
+    out[...] = part[...] + other[...]
 
 
 def call(kernel, outs, args, scratch=(), space=pltpu.VMEM):
@@ -486,14 +486,15 @@
     return lax.ppermute(value, axis, [((k + 1) % size, k) for k in range(size)])
 
 
-def swapped(value, axis, first):
+def swapped(value, axis, first, crossed=False):
     cores, size = lax.axis_size("load"), lax.axis_size(axis)
     pairs = []
     for core in range(cores):
         for k in range(size):
             other = k + 1 if (k - first) % 2 == 0 else k - 1
-            target = core * size + other if 0 <= other < size else (cores - 1 - core) * size + k
-            pairs.append((core * size + k, target))
+            inside = 0 <= other < size
+            side = cores - 1 - core if crossed or not inside else core
+            pairs.append((core * size + k, side * size + (other if inside else k)))
     return lax.ppermute(value, ("load", axis), pairs)
 
 
@@ -542,18 +543,19 @@
             pltpu.VMEM((ylen, xlen), jnp.float32),
         ],
     )
+    b_in = swapped(b_send, "sy", 1)
     a_in = swapped(a_send, "sy", 0)
-    b_in = swapped(b_send, "sy", 1)
     h, a_send, b_send = call(
         lambda *refs: rows_kernel(loads, comps, *refs),
         [(zlen + 1, ylen, xlen), (zlen, ylen, xlen), (zlen, ylen, xlen)],
-        (own, known, a_in, b_in),
-    )
-    a_in = swapped(a_send, "sz", 0)
-    b_in = swapped(b_send, "sz", 1)
+        (own, known, b_in, a_in),
+    )
+    a_in = swapped(a_send, "sz", 0, crossed=True)
+    b_in = swapped(b_send, "sz", 1, crossed=True)
     (part,) = call(layers_kernel, [(zlen, ylen, xlen)], (h, a_in, b_in))
-    parts = lax.all_gather(part, "load", axis=0)
-    (out,) = call(sum_kernel, [(zlen, ylen, xlen)], (parts,))
+    cores = lax.axis_size("load")
+    other = lax.ppermute(part, "load", [(core, cores - 1 - core) for core in range(cores)])
+    (out,) = call(sum_kernel, [(zlen, ylen, xlen)], (part, other))
     return out
 
 

time: 25.6 us -> 23.8 us (0.930)
  the two profiles are of different devices: /device:TPU:21 before, /device:TPU:0 now
where the time goes in v13:
time: 23.8 us; the launch traced here: 23.7 us
  starting transfers between devices  9.4 us (39%)
  waiting for transfers between devices  8.17 us (34%)
  Pallas kernels  6.07 us (26%)
    ppermute x4, waiting for transfers between devices, swapped(): return lax.ppermute(value, ('load', axis), pairs)  6.57 us
    pallas_call x6, Pallas kernels, call(): pl.pallas_call(kernel, out_shape=shapes, in_specs=[pl.BlockSpec(memory_sp...  6.07 us
    ppermute x4, starting transfers between devices, swapped(): return lax.ppermute(value, ('load', axis), pairs)  5.24 us
    ppermute x1, starting transfers between devices, ring_moved(): return lax.ppermute(value, axis, [((k + 1) % size, k) for k in range(size)])  3.51 us
    ppermute x1, waiting for transfers between devices, body(): lax.ppermute(part, 'load', [(core, cores - 1 - core) for core in range(co...  1.23 us
  transfers between devices with their start and end apart: 7, of which 4 were waited for; matrix products, arithmetic and copies ran while one was open for 0% of the time, Pallas kernels for 11%

profile of v13, /device:TPU:0, one launch (start us, length us, event | category | flops | bytes accessed | tf_op | source)
XLA Modules:
  0.0 23.7 jit_solution(16818305498856305343)
XLA Ops:
  0.0 1.3 %shard_map.46 = (f32[2,3,4,16,512]{4,3,2,1,0:T(8,128)S(1)}, s32[4,16,512]{2,1,0:T(8,128)S(1)}, f32[4,16,512]{2,1,0:T(8,128)S(1)}, s32[4,16,512]{2,1,0:T(8,128)S(...) custom-call(f32[2,3,4,16,512]{4,3,2,1,0:T(8,128)} %refs_0_.1, s32[4,16,512]{2,1,0:T(8,128)} %refs_1_.1, ...), custom_call_target="tpu_custom_call" | custom-call | tf_op jit(solution)/shard_map/pallas_call | solution.py:468
  1.3 0.5 %collective-permute-start = (f32[7,16,512]{2,1,0:T(8,128)S(1)}, f32[7,16,512]{2,1,0:T(8,128)S(1)}, u32[]{:S(2)}, u32[]{:S(2)}) collective-permute-start(f32[7,16,512]{2,1,0:T(8,128)S(1)} %get-tuple-element.25), channel_id=1, source_target_pairs={{19,3},{3,2},{2,1},{1,0},{0,16},{16,17},{17,18},{18,19},{23,7},{7,... | collective-permute-start | bytes 688136 | tf_op jit(solution)/shard_map/ppermute | solution.py:481
  1.8 3.5 %collective-permute-start.1 = (f32[24,512]{1,0:T(8,128)S(1)}, f32[24,512]{1,0:T(8,128)S(1)}, u32[]{:S(2)}, u32[]{:S(2)}) collective-permute-start(f32[24,512]{1,0:T(8,128)S(1)} %get-tuple-element.26), channel_id=1, source_target_pairs={{4,0},{8,4},{12,8},{0,12},{5,1},{9,5},{13,9},{1,13},{6,2},{10,6},{... | collective-permute-start | bytes 147464 | tf_op jit(solution)/shard_map/ppermute | solution.py:486
  5.3 2.7 %shard_map.47 = (f32[4,16,512]{2,1,0:T(8,128)S(1)}, f32[2,24,512]{2,1,0:T(8,128)S(1)}, f32[2,9,512]{2,1,0:T(8,128)S(1)}, f32[6,16,512]{2,1,0:T(8,128)S(1)}, f32[...) custom-call(f32[2,3,4,16,512]{4,3,2,1,0:T(8,128)S(1)} %get-tuple-element.27.refs_0_.refs_2_, ...), custom_call_target="tpu_custom_call" | custom-call | tf_op jit(solution)/shard_map/pallas_call | solution.py:468
  8.0 0.0 collective-permute-done.1.refs_1_
  8.0 0.4 %collective-permute-done.refs_0_ = f32[7,16,512]{2,1,0:T(8,128)S(1)} collective-permute-done((f32[7,16,512]{2,1,0:T(8,128)S(1)}, f32[7,16,512]{2,1,0:T(8,128)S(1)}, u32[]{:S(2)}, u32[]{:S(2)}) %collective-permute-start) | collective-permute-done | bytes 229408 | tf_op jit(solution)/shard_map/ppermute | solution.py:481
  8.4 1.0 %shard_map.48 = (f32[4,16,512]{2,1,0:T(8,128)S(1)}, f32[32,512]{1,0:T(8,128)S(1)}, f32[24,512]{1,0:T(8,128)S(1)}, f32[24,512]{1,0:T(8,128)S(1)}) custom-call(f32[7,16,512]{2,1,0:T(8,128)S(1)} %collective-permute-done.refs_0_, f32[24,512]{1,0:T(8,128)S(1)} %collective-permute-done.1.refs_1_, f32[2,3,4,16,512]{4,3,2,1,0:T(8,128)S(1)} %get-tuple-element.27.refs_0_.refs_2_, ...), custom_call_target="tpu_custom_call" | custom-call | tf_op jit(solution)/shard_map/pallas_call | solution.py:468
  9.4 0.5 %collective-permute-start.2 = (f32[24,512]{1,0:T(8,128)S(1)}, f32[24,512]{1,0:T(8,128)S(1)}, u32[]{:S(2)}, u32[]{:S(2)}) collective-permute-start(f32[24,512]{1,0:T(8,128)S(1)} %get-tuple-element.40), channel_id=1, source_target_pairs={{0,16},{4,8},{8,4},{12,28},{16,0},{20,24},{24,20},{28,12},{1,17},{... | collective-permute-start | bytes 147464 | tf_op jit(solution)/shard_map/ppermute | solution.py:498
  9.9 3.0 %collective-permute-start.3 = (f32[24,512]{1,0:T(8,128)S(1)}, f32[24,512]{1,0:T(8,128)S(1)}, u32[]{:S(2)}, u32[]{:S(2)}) collective-permute-start(f32[24,512]{1,0:T(8,128)S(1)} %get-tuple-element.41), channel_id=1, source_target_pairs={{0,4},{4,0},{8,12},{12,8},{16,20},{20,16},{24,28},{28,24},{1,5},{5... | collective-permute-start | bytes 147464 | tf_op jit(solution)/shard_map/ppermute | solution.py:498
  12.9 0.0 collective-permute-done.2.refs_2_
  12.9 2.6 %collective-permute-done.3.refs_3_ = f32[24,512]{1,0:T(8,128)S(1)} collective-permute-done((f32[24,512]{1,0:T(8,128)S(1)}, f32[24,512]{1,0:T(8,128)S(1)}, u32[]{:S(2)}, u32[]{:S(2)}) %collective-permute-start.3) | collective-permute-done | bytes 49184 | tf_op jit(solution)/shard_map/ppermute | solution.py:498
  15.5 0.3 %shard_map.49 = (f32[5,16,512]{2,1,0:T(8,128)S(1)}, f32[4,16,512]{2,1,0:T(8,128)S(1)}, f32[4,16,512]{2,1,0:T(8,128)S(1)}) custom-call(f32[4,16,512]{2,1,0:T(8,128)S(1)} %get-tuple-element.38.refs_0_, f32[32,512]{1,0:T(8,128)S(1)} %get-tuple-element.39.refs_1_, f32[24,512]{1,0:T(8,128)S(1)} %collective-permute-done.2.refs_2_, ...), custom_call_target="tpu_custom_call" | custom-call | tf_op jit(solution)/shard_map/pallas_call | solution.py:468
  15.8 0.1 collective-permute-start.4
  15.9 1.7 %collective-permute-start.5 = (f32[4,16,512]{2,1,0:T(8,128)S(1)}, f32[4,16,512]{2,1,0:T(8,128)S(1)}, u32[]{:S(2)}, u32[]{:S(2)}) collective-permute-start(f32[4,16,512]{2,1,0:T(8,128)S(1)} %get-tuple-element.44), channel_id=1, source_target_pairs={{0,16},{1,18},{2,17},{3,19},{16,0},{17,2},{18,1},{19,3},{4,20},{5,... | collective-permute-start | bytes 393224 | tf_op jit(solution)/shard_map/ppermute | solution.py:498
  17.6 4.0 %collective-permute-done.4.a_in = f32[4,16,512]{2,1,0:T(8,128)S(1)} collective-permute-done((f32[4,16,512]{2,1,0:T(8,128)S(1)}, f32[4,16,512]{2,1,0:T(8,128)S(1)}, u32[]{:S(2)}, u32[]{:S(2)}) %collective-permute-start.4) | collective-permute-done | bytes 131104 | tf_op jit(solution)/shard_map/ppermute | solution.py:498
  21.5 0.0 collective-permute-done.5.b_in
  21.5 0.1 shard_map.50.part
  21.6 0.2 collective-permute-start.6
  21.8 1.2 %collective-permute-done.6.other = f32[4,16,512]{2,1,0:T(8,128)S(1)} collective-permute-done((f32[4,16,512]{2,1,0:T(8,128)S(1)}, f32[4,16,512]{2,1,0:T(8,128)S(1)}, u32[]{:S(2)}, u32[]{:S(2)}) %collective-permute-start.6) | collective-permute-done | bytes 131104 | tf_op jit(solution)/shard_map/ppermute | solution.py:557
  23.0 0.7 %shard_map.51 = f32[4,16,512]{2,1,0:T(8,128)} custom-call(f32[4,16,512]{2,1,0:T(8,128)S(1)} %shard_map.50.part, f32[4,16,512]{2,1,0:T(8,128)S(1)} %collective-permute-done.6.other), custom_call_target="tpu_custom_call" | custom-call | tf_op jit(solution)/shard_map/pallas_call | solution.py:468
Async XLA Ops:
  1.3 7.0 %collective-permute-start = (f32[7,16,512]{2,1,0:T(8,128)S(1)}, f32[7,16,512]{2,1,0:T(8,128)S(1)}, u32[]{:S(2)}, u32[]{:S(2)}) collective-permute-start(f32[7,16,512]{2,1,0:T(8,128)S(1)} %get-tuple-element.25), channel_id=1, source_target_pairs={{19,3},{3,2},{2,1},{1,0},{0,16},{16,17},{17,18},{18,19},{23,7},{7,... | collective-permute-start | bytes 688136 | tf_op jit(solution)/shard_map/ppermute | solution.py:481
  1.8 6.2 %collective-permute-start.1 = (f32[24,512]{1,0:T(8,128)S(1)}, f32[24,512]{1,0:T(8,128)S(1)}, u32[]{:S(2)}, u32[]{:S(2)}) collective-permute-start(f32[24,512]{1,0:T(8,128)S(1)} %get-tuple-element.26), channel_id=1, source_target_pairs={{4,0},{8,4},{12,8},{0,12},{5,1},{9,5},{13,9},{1,13},{6,2},{10,6},{... | collective-permute-start | bytes 147464 | tf_op jit(solution)/shard_map/ppermute | solution.py:486
  9.4 3.5 %collective-permute-start.2 = (f32[24,512]{1,0:T(8,128)S(1)}, f32[24,512]{1,0:T(8,128)S(1)}, u32[]{:S(2)}, u32[]{:S(2)}) collective-permute-start(f32[24,512]{1,0:T(8,128)S(1)} %get-tuple-element.40), channel_id=1, source_target_pairs={{0,16},{4,8},{8,4},{12,28},{16,0},{20,24},{24,20},{28,12},{1,17},{... | collective-permute-start | bytes 147464 | tf_op jit(solution)/shard_map/ppermute | solution.py:498
  9.9 5.6 %collective-permute-start.3 = (f32[24,512]{1,0:T(8,128)S(1)}, f32[24,512]{1,0:T(8,128)S(1)}, u32[]{:S(2)}, u32[]{:S(2)}) collective-permute-start(f32[24,512]{1,0:T(8,128)S(1)} %get-tuple-element.41), channel_id=1, source_target_pairs={{0,4},{4,0},{8,12},{12,8},{16,20},{20,16},{24,28},{28,24},{1,5},{5... | collective-permute-start | bytes 147464 | tf_op jit(solution)/shard_map/ppermute | solution.py:498
  15.8 5.7 %collective-permute-start.4 = (f32[4,16,512]{2,1,0:T(8,128)S(1)}, f32[4,16,512]{2,1,0:T(8,128)S(1)}, u32[]{:S(2)}, u32[]{:S(2)}) collective-permute-start(f32[4,16,512]{2,1,0:T(8,128)S(1)} %get-tuple-element.43), channel_id=1, source_target_pairs={{0,17},{1,16},{2,19},{3,18},{16,1},{17,0},{18,3},{19,2},{4,21},{5,... | collective-permute-start | bytes 393224 | tf_op jit(solution)/shard_map/ppermute | solution.py:498
  15.9 5.7 %collective-permute-start.5 = (f32[4,16,512]{2,1,0:T(8,128)S(1)}, f32[4,16,512]{2,1,0:T(8,128)S(1)}, u32[]{:S(2)}, u32[]{:S(2)}) collective-permute-start(f32[4,16,512]{2,1,0:T(8,128)S(1)} %get-tuple-element.44), channel_id=1, source_target_pairs={{0,16},{1,18},{2,17},{3,19},{16,0},{17,2},{18,1},{19,3},{4,20},{5,... | collective-permute-start | bytes 393224 | tf_op jit(solution)/shard_map/ppermute | solution.py:498
  21.6 1.4 %collective-permute-start.6 = (f32[4,16,512]{2,1,0:T(8,128)S(1)}, f32[4,16,512]{2,1,0:T(8,128)S(1)}, u32[]{:S(2)}, u32[]{:S(2)}) collective-permute-start(f32[4,16,512]{2,1,0:T(8,128)S(1)} %shard_map.50.part), channel_id=1, source_target_pairs={{0,16},{16,0},{1,17},{17,1},{2,18},{18,2},{3,19},{19,3},{4,20},{20... | collective-permute-start | bytes 393224 | tf_op jit(solution)/shard_map/ppermute | solution.py:557

commit v14 on v13

--- a/solution.py
+++ b/solution.py
@@ -185,23 +185,32 @@
 
 def lead_kernel(totals, disp_hbm, fixed_hbm, density_hbm, solid_hbm, disp, fixed, density, solid, z_out, y_out, sems):
     loads, comps, zlen, ylen, _ = disp.shape
-    copies = [
-        pltpu.make_async_copy(source, target, sems.at[k])
-        for k, (source, target) in enumerate(
-            ((disp_hbm, disp), (fixed_hbm, fixed), (density_hbm, density), (solid_hbm, solid))
-        )
-    ]
-    for copy in copies:
-        copy.start()
-    for copy in copies:
+    gives = jnp.where(on_first(), 0, zlen - 1)
+    arrays = ((disp_hbm, disp), (fixed_hbm, fixed), (density_hbm, density), (solid_hbm, solid))
+
+    def copies(layer, sem):
+        layer = lax.rem(layer, zlen)
+        parts = [(source.at[:, :, layer], target.at[:, :, layer]) for source, target in arrays[:1]]
+        parts += [(source.at[layer], target.at[layer]) for source, target in arrays[1:]]
+        return [pltpu.make_async_copy(source, target, sems.at[sem, k]) for k, (source, target) in enumerate(parts)]
+
+    started = [copies(gives + step, step) for step in range(zlen)]
+    for group in started:
+        for copy in group:
+            copy.start()
+    for copy in started[0]:
         copy.wait()
-    gives = jnp.where(on_first(), 0, zlen - 1)
     plane = lax.axis_index("sz") * zlen + gives
     base_y = lax.axis_index("sy") * ylen
     z_out[loads * comps] = voxel_factor(density[gives], solid[gives], plane, base_y, *totals)
     for case in range(loads):
         for comp in range(comps):
             z_out[case * comps + comp] = held(disp, fixed, case, comp, gives, slice(None))
+    for group in started[1:]:
+        for copy in group:
+            copy.wait()
+    for case in range(loads):
+        for comp in range(comps):
             for z in range(zlen):
                 at = (comp * loads + case) * zlen + z
                 y_out[at : at + 1] = held(disp, fixed, case, comp, z, slice(0, 1))
@@ -384,7 +393,7 @@
     b_out[...] = jnp.where(even, down, up)
 
 
-def rows_kernel(loads, comps, own, known, b_in, a_in, h_out, a_out, b_out):
+def rows_kernel(loads, comps, own, b_in, a_in, known, h_out, a_out, b_out):
     zlen, ylen, xlen = own.shape
     planes = loads * comps
     index, last = lax.axis_index("sy"), lax.axis_size("sy") - 1
@@ -392,7 +401,7 @@
     from_low = jnp.where(index > 0, jnp.where(even, b_in[...], a_in[...]), 0.0)
     from_high = jnp.where(index < last, jnp.where(even, a_in[...], b_in[...]), 0.0)
     ends = REACH * zlen
-    first_core = on_first()
+    first_core = jnp.logical_not(on_first())
     top = first_core & (lax.axis_index("sz") == lax.axis_size("sz") - 1)
 
     def nodes(first, second, comp):
@@ -429,8 +438,9 @@
     rising = jnp.maximum(row - (TILE - 1 - ROWS), 0).astype(jnp.float32)
     falling = jnp.maximum(REACH - row, 0).astype(jnp.float32)
     blank = jnp.zeros((TILE - REACH, xlen), jnp.float32)
-    between = jnp.where(first_core, zlen, 0)
-    h_out[zlen - between] = jnp.zeros((ylen, xlen), jnp.float32)
+    theirs = jnp.where(first_core, zlen, 0)
+    h_out[zlen - theirs] = own[zlen - 1]
+    h_out[theirs] = jnp.zeros((ylen, xlen), jnp.float32)
     for z in range(zlen):
         part = slice(REACH * z, REACH * (z + 1))
         head = jnp.concatenate([from_low[part], blank], axis=0)
@@ -439,8 +449,9 @@
         if z == zlen - 1:
             head = jnp.where(row == REACH - 1, 0.0, head) + falling * lines[1:2]
             tail = tail + rising * lines[0:1]
-            at = between
-        h_out[at] = own[z]
+            at = theirs
+        else:
+            h_out[at] = own[z]
         h_out[at, :TILE] += head
         h_out[at, ylen - TILE :] += tail
     high = (lax.axis_index("sz") % 2 == 0).astype(jnp.int32)
@@ -498,6 +509,11 @@
     return lax.ppermute(value, ("load", axis), pairs)
 
 
+def chip_swapped(value):
+    cores = lax.axis_size("load")
+    return lax.ppermute(value, "load", [(core, cores - 1 - core) for core in range(cores)])
+
+
 def body(displacements, density, solid, fixed):
     loads, comps, zlen, ylen, xlen = displacements.shape
     planes = loads * comps
@@ -511,7 +527,7 @@
         [jax.ShapeDtypeStruct(arg.shape, arg.dtype) for arg in args]
         + [(planes + 1, ylen, xlen), (planes * zlen, xlen)],
         args,
-        scratch=[pltpu.SemaphoreType.DMA((len(args),))],
+        scratch=[pltpu.SemaphoreType.DMA((zlen, len(args)))],
         space=pltpu.HBM,
     )
     z_in = column_moved(z_send)
@@ -543,19 +559,17 @@
             pltpu.VMEM((ylen, xlen), jnp.float32),
         ],
     )
-    b_in = swapped(b_send, "sy", 1)
-    a_in = swapped(a_send, "sy", 0)
+    b_in = swapped(b_send, "sy", 1, crossed=True)
+    a_in = swapped(a_send, "sy", 0, crossed=True)
     h, a_send, b_send = call(
         lambda *refs: rows_kernel(loads, comps, *refs),
         [(zlen + 1, ylen, xlen), (zlen, ylen, xlen), (zlen, ylen, xlen)],
-        (own, known, b_in, a_in),
+        (own, b_in, a_in, chip_swapped(known)),
     )
     a_in = swapped(a_send, "sz", 0, crossed=True)
     b_in = swapped(b_send, "sz", 1, crossed=True)
     (part,) = call(layers_kernel, [(zlen, ylen, xlen)], (h, a_in, b_in))
-    cores = lax.axis_size("load")
-    other = lax.ppermute(part, "load", [(core, cores - 1 - core) for core in range(cores)])
-    (out,) = call(sum_kernel, [(zlen, ylen, xlen)], (part, other))
+    (out,) = call(sum_kernel, [(zlen, ylen, xlen)], (part, chip_swapped(part)))
     return out
 
 

time: 23.8 us -> 24 us (level); the launches traced: 23.7 us -> 23.5 us
  waiting for transfers between devices: 8.17 us -> 7.83 us
    ppermute x1 -> x2, starting transfers between devices: 0.18 us -> 0.85 us  [chip_swapped(): lax.ppermute(value, 'load', [(core, cores - 1 - core) for core in range(c...]
    ppermute x4, starting transfers between devices: 5.24 us -> 4.59 us  [swapped(): return lax.ppermute(value, ('load', axis), pairs)]
    ppermute x1 -> x2, waiting for transfers between devices: 1.23 us -> 1.05 us  [chip_swapped(): lax.ppermute(value, 'load', [(core, cores - 1 - core) for core in range(c...]
  transfers between devices with their start and end apart: 7 -> 8, of which waited for: 4 -> 4; matrix products, arithmetic and copies ran while one was open for 0% -> 0% of each run, Pallas kernels for 11% -> 11%
where the time goes in v14:
time: 24 us; the launch traced here: 23.5 us
  starting transfers between devices  9.42 us (39%)
  waiting for transfers between devices  7.83 us (33%)
  Pallas kernels  6.24 us (26%)
    ppermute x4, waiting for transfers between devices, swapped(): return lax.ppermute(value, ('load', axis), pairs)  6.41 us
    pallas_call x6, Pallas kernels, call(): pl.pallas_call(kernel, out_shape=shapes, in_specs=[pl.BlockSpec(memory_sp...  6.24 us
    ppermute x4, starting transfers between devices, swapped(): return lax.ppermute(value, ('load', axis), pairs)  4.59 us
    ppermute x1, starting transfers between devices, ring_moved(): return lax.ppermute(value, axis, [((k + 1) % size, k) for k in range(size)])  3.51 us
    ppermute x2, waiting for transfers between devices, chip_swapped(): lax.ppermute(value, 'load', [(core, cores - 1 - core) for core in range(c...  1.05 us
    ppermute x2, starting transfers between devices, chip_swapped(): lax.ppermute(value, 'load', [(core, cores - 1 - core) for core in range(c...  0.85 us
  transfers between devices with their start and end apart: 8, of which 4 were waited for; matrix products, arithmetic and copies ran while one was open for 0% of the time, Pallas kernels for 11%

profile of v14, /device:TPU:0, one launch (start us, length us, event | category | flops | bytes accessed | tf_op | source)
XLA Modules:
  0.0 23.5 jit_solution(16234515162155899113)
XLA Ops:
  0.0 1.5 %shard_map.46 = (f32[2,3,4,16,512]{4,3,2,1,0:T(8,128)S(1)}, s32[4,16,512]{2,1,0:T(8,128)S(1)}, f32[4,16,512]{2,1,0:T(8,128)S(1)}, s32[4,16,512]{2,1,0:T(8,128)S(...) custom-call(f32[2,3,4,16,512]{4,3,2,1,0:T(8,128)} %refs_0_.1, s32[4,16,512]{2,1,0:T(8,128)} %refs_1_.1, ...), custom_call_target="tpu_custom_call" | custom-call | tf_op jit(solution)/shard_map/pallas_call | solution.py:479
  1.5 0.5 %collective-permute-start = (f32[7,16,512]{2,1,0:T(8,128)S(1)}, f32[7,16,512]{2,1,0:T(8,128)S(1)}, u32[]{:S(2)}, u32[]{:S(2)}) collective-permute-start(f32[7,16,512]{2,1,0:T(8,128)S(1)} %get-tuple-element.25), channel_id=1, source_target_pairs={{19,3},{3,2},{2,1},{1,0},{0,16},{16,17},{17,18},{18,19},{23,7},{7,... | collective-permute-start | bytes 688136 | tf_op jit(solution)/shard_map/ppermute | solution.py:492
  2.0 3.5 %collective-permute-start.1 = (f32[24,512]{1,0:T(8,128)S(1)}, f32[24,512]{1,0:T(8,128)S(1)}, u32[]{:S(2)}, u32[]{:S(2)}) collective-permute-start(f32[24,512]{1,0:T(8,128)S(1)} %get-tuple-element.26), channel_id=1, source_target_pairs={{4,0},{8,4},{12,8},{0,12},{5,1},{9,5},{13,9},{1,13},{6,2},{10,6},{... | collective-permute-start | bytes 147464 | tf_op jit(solution)/shard_map/ppermute | solution.py:497
  5.5 2.7 %shard_map.47 = (f32[4,16,512]{2,1,0:T(8,128)S(1)}, f32[2,24,512]{2,1,0:T(8,128)S(1)}, f32[2,9,512]{2,1,0:T(8,128)S(1)}, f32[6,16,512]{2,1,0:T(8,128)S(1)}, f32[...) custom-call(f32[2,3,4,16,512]{4,3,2,1,0:T(8,128)S(1)} %get-tuple-element.27.refs_0_.refs_2_, ...), custom_call_target="tpu_custom_call" | custom-call | tf_op jit(solution)/shard_map/pallas_call | solution.py:479
  8.2 0.0 collective-permute-done.1.refs_1_
  8.2 0.4 %collective-permute-done.refs_0_ = f32[7,16,512]{2,1,0:T(8,128)S(1)} collective-permute-done((f32[7,16,512]{2,1,0:T(8,128)S(1)}, f32[7,16,512]{2,1,0:T(8,128)S(1)}, u32[]{:S(2)}, u32[]{:S(2)}) %collective-permute-start) | collective-permute-done | bytes 229408 | tf_op jit(solution)/shard_map/ppermute | solution.py:492
  8.5 1.0 %shard_map.48 = (f32[4,16,512]{2,1,0:T(8,128)S(1)}, f32[32,512]{1,0:T(8,128)S(1)}, f32[24,512]{1,0:T(8,128)S(1)}, f32[24,512]{1,0:T(8,128)S(1)}) custom-call(f32[7,16,512]{2,1,0:T(8,128)S(1)} %collective-permute-done.refs_0_, f32[24,512]{1,0:T(8,128)S(1)} %collective-permute-done.1.refs_1_, f32[2,3,4,16,512]{4,3,2,1,0:T(8,128)S(1)} %get-tuple-element.27.refs_0_.refs_2_, ...), custom_call_target="tpu_custom_call" | custom-call | tf_op jit(solution)/shard_map/pallas_call | solution.py:479
  9.5 0.5 %collective-permute-start.4 = (f32[32,512]{1,0:T(8,128)S(1)}, f32[32,512]{1,0:T(8,128)S(1)}, u32[]{:S(2)}, u32[]{:S(2)}) collective-permute-start(f32[32,512]{1,0:T(8,128)S(1)} %get-tuple-element.41), channel_id=1, source_target_pairs={{0,16},{16,0},{1,17},{17,1},{2,18},{18,2},{3,19},{19,3},{4,20},{20... | collective-permute-start | bytes 196616 | tf_op jit(solution)/shard_map/ppermute | solution.py:514
  10.0 0.1 collective-permute-start.2
  10.1 2.7 %collective-permute-start.3 = (f32[24,512]{1,0:T(8,128)S(1)}, f32[24,512]{1,0:T(8,128)S(1)}, u32[]{:S(2)}, u32[]{:S(2)}) collective-permute-start(f32[24,512]{1,0:T(8,128)S(1)} %get-tuple-element.40), channel_id=1, source_target_pairs={{0,20},{4,16},{8,28},{12,24},{16,4},{20,0},{24,12},{28,8},{1,21},{... | collective-permute-start | bytes 147464 | tf_op jit(solution)/shard_map/ppermute | solution.py:509
  12.8 0.0 collective-permute-done.2.refs_1_
  12.8 2.8 %collective-permute-done.3.refs_2_ = f32[24,512]{1,0:T(8,128)S(1)} collective-permute-done((f32[24,512]{1,0:T(8,128)S(1)}, f32[24,512]{1,0:T(8,128)S(1)}, u32[]{:S(2)}, u32[]{:S(2)}) %collective-permute-start.3) | collective-permute-done | bytes 49184 | tf_op jit(solution)/shard_map/ppermute | solution.py:509
  15.6 0.0 collective-permute-done.4.refs_3_
  15.6 0.3 %shard_map.49 = (f32[5,16,512]{2,1,0:T(8,128)S(1)}, f32[4,16,512]{2,1,0:T(8,128)S(1)}, f32[4,16,512]{2,1,0:T(8,128)S(1)}) custom-call(f32[4,16,512]{2,1,0:T(8,128)S(1)} %get-tuple-element.38.refs_0_, f32[24,512]{1,0:T(8,128)S(1)} %collective-permute-done.2.refs_1_, f32[24,512]{1,0:T(8,128)S(1)} %collective-permute-done.3.refs_2_, ...), custom_call_target="tpu_custom_call" | custom-call | tf_op jit(solution)/shard_map/pallas_call | solution.py:479
  16.0 1.6 %collective-permute-start.5 = (f32[4,16,512]{2,1,0:T(8,128)S(1)}, f32[4,16,512]{2,1,0:T(8,128)S(1)}, u32[]{:S(2)}, u32[]{:S(2)}) collective-permute-start(f32[4,16,512]{2,1,0:T(8,128)S(1)} %get-tuple-element.43), channel_id=1, source_target_pairs={{0,17},{1,16},{2,19},{3,18},{16,1},{17,0},{18,3},{19,2},{4,21},{5,... | collective-permute-start | bytes 393224 | tf_op jit(solution)/shard_map/ppermute | solution.py:509
  17.6 0.1 collective-permute-start.6
  17.7 3.6 %collective-permute-done.5.a_in = f32[4,16,512]{2,1,0:T(8,128)S(1)} collective-permute-done((f32[4,16,512]{2,1,0:T(8,128)S(1)}, f32[4,16,512]{2,1,0:T(8,128)S(1)}, u32[]{:S(2)}, u32[]{:S(2)}) %collective-permute-start.5) | collective-permute-done | bytes 131104 | tf_op jit(solution)/shard_map/ppermute | solution.py:509
  21.4 0.0 collective-permute-done.6.b_in
  21.4 0.1 shard_map.50.part
  21.4 0.4 %collective-permute-start.7 = (f32[4,16,512]{2,1,0:T(8,128)S(1)}, f32[4,16,512]{2,1,0:T(8,128)S(1)}, u32[]{:S(2)}, u32[]{:S(2)}) collective-permute-start(f32[4,16,512]{2,1,0:T(8,128)S(1)} %shard_map.50.part), channel_id=1, source_target_pairs={{0,16},{16,0},{1,17},{17,1},{2,18},{18,2},{3,19},{19,3},{4,20},{20... | collective-permute-start | bytes 393224 | tf_op jit(solution)/shard_map/ppermute | solution.py:514
  21.8 1.1 %collective-permute-done.7.other = f32[4,16,512]{2,1,0:T(8,128)S(1)} collective-permute-done((f32[4,16,512]{2,1,0:T(8,128)S(1)}, f32[4,16,512]{2,1,0:T(8,128)S(1)}, u32[]{:S(2)}, u32[]{:S(2)}) %collective-permute-start.7) | collective-permute-done | bytes 131104 | tf_op jit(solution)/shard_map/ppermute | solution.py:514
  22.9 0.7 %shard_map.51 = f32[4,16,512]{2,1,0:T(8,128)} custom-call(f32[4,16,512]{2,1,0:T(8,128)S(1)} %shard_map.50.part, f32[4,16,512]{2,1,0:T(8,128)S(1)} %collective-permute-done.7.other), custom_call_target="tpu_custom_call" | custom-call | tf_op jit(solution)/shard_map/pallas_call | solution.py:479
Async XLA Ops:
  1.5 7.0 %collective-permute-start = (f32[7,16,512]{2,1,0:T(8,128)S(1)}, f32[7,16,512]{2,1,0:T(8,128)S(1)}, u32[]{:S(2)}, u32[]{:S(2)}) collective-permute-start(f32[7,16,512]{2,1,0:T(8,128)S(1)} %get-tuple-element.25), channel_id=1, source_target_pairs={{19,3},{3,2},{2,1},{1,0},{0,16},{16,17},{17,18},{18,19},{23,7},{7,... | collective-permute-start | bytes 688136 | tf_op jit(solution)/shard_map/ppermute | solution.py:492
  2.0 6.2 %collective-permute-start.1 = (f32[24,512]{1,0:T(8,128)S(1)}, f32[24,512]{1,0:T(8,128)S(1)}, u32[]{:S(2)}, u32[]{:S(2)}) collective-permute-start(f32[24,512]{1,0:T(8,128)S(1)} %get-tuple-element.26), channel_id=1, source_target_pairs={{4,0},{8,4},{12,8},{0,12},{5,1},{9,5},{13,9},{1,13},{6,2},{10,6},{... | collective-permute-start | bytes 147464 | tf_op jit(solution)/shard_map/ppermute | solution.py:497
  9.5 6.1 %collective-permute-start.4 = (f32[32,512]{1,0:T(8,128)S(1)}, f32[32,512]{1,0:T(8,128)S(1)}, u32[]{:S(2)}, u32[]{:S(2)}) collective-permute-start(f32[32,512]{1,0:T(8,128)S(1)} %get-tuple-element.41), channel_id=1, source_target_pairs={{0,16},{16,0},{1,17},{17,1},{2,18},{18,2},{3,19},{19,3},{4,20},{20... | collective-permute-start | bytes 196616 | tf_op jit(solution)/shard_map/ppermute | solution.py:514
  10.0 2.8 %collective-permute-start.2 = (f32[24,512]{1,0:T(8,128)S(1)}, f32[24,512]{1,0:T(8,128)S(1)}, u32[]{:S(2)}, u32[]{:S(2)}) collective-permute-start(f32[24,512]{1,0:T(8,128)S(1)} %get-tuple-element.39), channel_id=1, source_target_pairs={{0,16},{4,24},{8,20},{12,28},{16,0},{20,8},{24,4},{28,12},{1,17},{... | collective-permute-start | bytes 147464 | tf_op jit(solution)/shard_map/ppermute | solution.py:509
  10.1 5.5 %collective-permute-start.3 = (f32[24,512]{1,0:T(8,128)S(1)}, f32[24,512]{1,0:T(8,128)S(1)}, u32[]{:S(2)}, u32[]{:S(2)}) collective-permute-start(f32[24,512]{1,0:T(8,128)S(1)} %get-tuple-element.40), channel_id=1, source_target_pairs={{0,20},{4,16},{8,28},{12,24},{16,4},{20,0},{24,12},{28,8},{1,21},{... | collective-permute-start | bytes 147464 | tf_op jit(solution)/shard_map/ppermute | solution.py:509
  16.0 5.4 %collective-permute-start.5 = (f32[4,16,512]{2,1,0:T(8,128)S(1)}, f32[4,16,512]{2,1,0:T(8,128)S(1)}, u32[]{:S(2)}, u32[]{:S(2)}) collective-permute-start(f32[4,16,512]{2,1,0:T(8,128)S(1)} %get-tuple-element.43), channel_id=1, source_target_pairs={{0,17},{1,16},{2,19},{3,18},{16,1},{17,0},{18,3},{19,2},{4,21},{5,... | collective-permute-start | bytes 393224 | tf_op jit(solution)/shard_map/ppermute | solution.py:509
  17.6 3.8 %collective-permute-start.6 = (f32[4,16,512]{2,1,0:T(8,128)S(1)}, f32[4,16,512]{2,1,0:T(8,128)S(1)}, u32[]{:S(2)}, u32[]{:S(2)}) collective-permute-start(f32[4,16,512]{2,1,0:T(8,128)S(1)} %get-tuple-element.44), channel_id=1, source_target_pairs={{0,16},{1,18},{2,17},{3,19},{16,0},{17,2},{18,1},{19,3},{4,20},{5,... | collective-permute-start | bytes 393224 | tf_op jit(solution)/shard_map/ppermute | solution.py:509
  21.4 1.4 %collective-permute-start.7 = (f32[4,16,512]{2,1,0:T(8,128)S(1)}, f32[4,16,512]{2,1,0:T(8,128)S(1)}, u32[]{:S(2)}, u32[]{:S(2)}) collective-permute-start(f32[4,16,512]{2,1,0:T(8,128)S(1)} %shard_map.50.part), channel_id=1, source_target_pairs={{0,16},{16,0},{1,17},{17,1},{2,18},{18,2},{3,19},{19,3},{4,20},{20... | collective-permute-start | bytes 393224 | tf_op jit(solution)/shard_map/ppermute | solution.py:514

commit v15 on v13

--- a/solution.py
+++ b/solution.py
@@ -384,7 +384,7 @@
     b_out[...] = jnp.where(even, down, up)
 
 
-def rows_kernel(loads, comps, own, known, b_in, a_in, h_out, a_out, b_out):
+def rows_kernel(loads, comps, own, known, b_in, a_in, h_out):
     zlen, ylen, xlen = own.shape
     planes = loads * comps
     index, last = lax.axis_index("sy"), lax.axis_size("sy") - 1
@@ -443,18 +443,23 @@
         h_out[at] = own[z]
         h_out[at, :TILE] += head
         h_out[at, ylen - TILE :] += tail
-    high = (lax.axis_index("sz") % 2 == 0).astype(jnp.int32)
-    a_out[...] = h_out[pl.ds(high, zlen)]
-    b_out[...] = h_out[pl.ds(1 - high, zlen)]
-
-
-def layers_kernel(h, a_in, b_in, out):
+
+
+def total_kernel(h, other, h_out, z_out):
+    for k in range(h.shape[0]):
+        h_out[k] = h[k] + other[k]
+    z_out[...] = h_out[pl.ds(jnp.where(on_first(), 0, 1), z_out.shape[0])]
+
+
+def layers_kernel(h, z_in, out):
     zlen = out.shape[0]
-    index, last = lax.axis_index("sz"), lax.axis_size("sz") - 1
-    even = index % 2 == 0
-    below = [jnp.where(index > 0, jnp.where(even, b_in[k], a_in[k]), 0.0) for k in range(zlen - REACH, zlen)]
-    above = [jnp.where(index < last, jnp.where(even, a_in[k], b_in[k]), 0.0) for k in range(zlen)]
-    layers = below[:-1] + [below[-1] + h[0]] + [h[z] for z in range(1, zlen)] + [h[zlen] + above[0]] + above[1:]
+    first_core = on_first()
+    inside = lax.axis_index("sz") > 0, lax.axis_index("sz") < lax.axis_size("sz") - 1
+    under, over = jnp.logical_not(first_core) & inside[0], first_core & inside[1]
+    below = [jnp.where(under, z_in[k], 0.0) for k in range(zlen - REACH, zlen)]
+    above = [jnp.where(over, z_in[k], 0.0) for k in range(zlen)]
+    own = [jnp.where(first_core, h[k], 0.0) for k in range(zlen + 1)]
+    layers = below[:-1] + [below[-1] + own[0]] + own[1:-1] + [own[-1] + above[0]] + above[1:]
     for z, layer in enumerate(spread_layers(layers)):
         out[z] = layer
 
@@ -486,16 +491,21 @@
     return lax.ppermute(value, axis, [((k + 1) % size, k) for k in range(size)])
 
 
-def swapped(value, axis, first, crossed=False):
+def swapped(value, axis, first):
     cores, size = lax.axis_size("load"), lax.axis_size(axis)
     pairs = []
     for core in range(cores):
         for k in range(size):
             other = k + 1 if (k - first) % 2 == 0 else k - 1
             inside = 0 <= other < size
-            side = cores - 1 - core if crossed or not inside else core
+            side = core if inside else cores - 1 - core
             pairs.append((core * size + k, side * size + (other if inside else k)))
     return lax.ppermute(value, ("load", axis), pairs)
+
+
+def chip_swapped(value):
+    cores = lax.axis_size("load")
+    return lax.ppermute(value, "load", [(core, cores - 1 - core) for core in range(cores)])
 
 
 def body(displacements, density, solid, fixed):
@@ -545,17 +555,12 @@
     )
     b_in = swapped(b_send, "sy", 1)
     a_in = swapped(a_send, "sy", 0)
-    h, a_send, b_send = call(
-        lambda *refs: rows_kernel(loads, comps, *refs),
-        [(zlen + 1, ylen, xlen), (zlen, ylen, xlen), (zlen, ylen, xlen)],
-        (own, known, b_in, a_in),
-    )
-    a_in = swapped(a_send, "sz", 0, crossed=True)
-    b_in = swapped(b_send, "sz", 1, crossed=True)
-    (part,) = call(layers_kernel, [(zlen, ylen, xlen)], (h, a_in, b_in))
-    cores = lax.axis_size("load")
-    other = lax.ppermute(part, "load", [(core, cores - 1 - core) for core in range(cores)])
-    (out,) = call(sum_kernel, [(zlen, ylen, xlen)], (part, other))
+    (h,) = call(
+        lambda *refs: rows_kernel(loads, comps, *refs), [(zlen + 1, ylen, xlen)], (own, known, b_in, a_in)
+    )
+    h, z_send = call(total_kernel, [(zlen + 1, ylen, xlen), (zlen, ylen, xlen)], (h, chip_swapped(h)))
+    (part,) = call(layers_kernel, [(zlen, ylen, xlen)], (h, column_moved(z_send)))
+    (out,) = call(sum_kernel, [(zlen, ylen, xlen)], (part, chip_swapped(part)))
     return out
 
 

time: 23.8 us -> 24.5 us (1.029)
  waiting for transfers between devices: 8.17 us -> 10.5 us
  starting transfers between devices: 9.4 us -> 7.77 us
    ppermute x1 -> x2, waiting for transfers between devices: 0.37 us -> 5.19 us  [column_moved(): lax.ppermute(value, ('load', 'sz'), [(ring[k - 1], ring[k]) for k in rang...]
    ppermute x4 -> x2, waiting for transfers between devices: 6.57 us -> 2.59 us  [swapped(): return lax.ppermute(value, ('load', axis), pairs)]
    ppermute x4 -> x2, starting transfers between devices: 5.24 us -> 3.49 us  [swapped(): return lax.ppermute(value, ('load', axis), pairs)]
    ppermute x1 -> x2, waiting for transfers between devices: 1.23 us -> 2.72 us  [chip_swapped(): lax.ppermute(value, 'load', [(core, cores - 1 - core) for core in range(c...]
    ppermute x1 -> x2, starting transfers between devices: 0.47 us -> 0.63 us  [column_moved(): lax.ppermute(value, ('load', 'sz'), [(ring[k - 1], ring[k]) for k in rang...]
    pallas_call x6 -> x7, Pallas kernels: 6.07 us -> 6.05 us  [call(): pl.pallas_call(kernel, out_shape=shapes, in_specs=[pl.BlockSpec(memory_sp...]
  transfers between devices with their start and end apart: 7 -> 7, of which waited for: 4 -> 5; matrix products, arithmetic and copies ran while one was open for 0% -> 0% of each run, Pallas kernels for 11% -> 11%
where the time goes in v15:
time: 24.5 us; the launch traced here: 24.4 us
  waiting for transfers between devices  10.5 us (43%)
  starting transfers between devices  7.77 us (32%)
  Pallas kernels  6.05 us (25%)
    pallas_call x7, Pallas kernels, call(): pl.pallas_call(kernel, out_shape=shapes, in_specs=[pl.BlockSpec(memory_sp...  6.05 us
    ppermute x2, waiting for transfers between devices, column_moved(): lax.ppermute(value, ('load', 'sz'), [(ring[k - 1], ring[k]) for k in rang...  5.19 us
    ppermute x1, starting transfers between devices, ring_moved(): return lax.ppermute(value, axis, [((k + 1) % size, k) for k in range(size)])  3.51 us
    ppermute x2, starting transfers between devices, swapped(): return lax.ppermute(value, ('load', axis), pairs)  3.49 us
    ppermute x2, waiting for transfers between devices, chip_swapped(): lax.ppermute(value, 'load', [(core, cores - 1 - core) for core in range(c...  2.72 us
    ppermute x2, waiting for transfers between devices, swapped(): return lax.ppermute(value, ('load', axis), pairs)  2.59 us
    ppermute x2, starting transfers between devices, column_moved(): lax.ppermute(value, ('load', 'sz'), [(ring[k - 1], ring[k]) for k in rang...  0.63 us
  transfers between devices with their start and end apart: 7, of which 5 were waited for; matrix products, arithmetic and copies ran while one was open for 0% of the time, Pallas kernels for 11%

profile of v15, /device:TPU:0, one launch (start us, length us, event | category | flops | bytes accessed | tf_op | source)
XLA Modules:
  0.0 24.4 jit_solution(5718355967446065116)
XLA Ops:
  0.0 1.3 %shard_map.46 = (f32[2,3,4,16,512]{4,3,2,1,0:T(8,128)S(1)}, s32[4,16,512]{2,1,0:T(8,128)S(1)}, f32[4,16,512]{2,1,0:T(8,128)S(1)}, s32[4,16,512]{2,1,0:T(8,128)S(...) custom-call(f32[2,3,4,16,512]{4,3,2,1,0:T(8,128)} %refs_0_.1, s32[4,16,512]{2,1,0:T(8,128)} %refs_1_.1, ...), custom_call_target="tpu_custom_call" | custom-call | tf_op jit(solution)/shard_map/pallas_call | solution.py:473
  1.3 0.5 %collective-permute-start = (f32[7,16,512]{2,1,0:T(8,128)S(1)}, f32[7,16,512]{2,1,0:T(8,128)S(1)}, u32[]{:S(2)}, u32[]{:S(2)}) collective-permute-start(f32[7,16,512]{2,1,0:T(8,128)S(1)} %get-tuple-element.24), channel_id=1, source_target_pairs={{19,3},{3,2},{2,1},{1,0},{0,16},{16,17},{17,18},{18,19},{23,7},{7,... | collective-permute-start | bytes 688136 | tf_op jit(solution)/shard_map/ppermute | solution.py:486
  1.8 3.5 %collective-permute-start.1 = (f32[24,512]{1,0:T(8,128)S(1)}, f32[24,512]{1,0:T(8,128)S(1)}, u32[]{:S(2)}, u32[]{:S(2)}) collective-permute-start(f32[24,512]{1,0:T(8,128)S(1)} %get-tuple-element.25), channel_id=1, source_target_pairs={{4,0},{8,4},{12,8},{0,12},{5,1},{9,5},{13,9},{1,13},{6,2},{10,6},{... | collective-permute-start | bytes 147464 | tf_op jit(solution)/shard_map/ppermute | solution.py:491
  5.3 2.7 %shard_map.47 = (f32[4,16,512]{2,1,0:T(8,128)S(1)}, f32[2,24,512]{2,1,0:T(8,128)S(1)}, f32[2,9,512]{2,1,0:T(8,128)S(1)}, f32[6,16,512]{2,1,0:T(8,128)S(1)}, f32[...) custom-call(f32[2,3,4,16,512]{4,3,2,1,0:T(8,128)S(1)} %get-tuple-element.26.refs_0_.refs_2_, ...), custom_call_target="tpu_custom_call" | custom-call | tf_op jit(solution)/shard_map/pallas_call | solution.py:473
  8.0 0.0 collective-permute-done.1.refs_1_
  8.0 0.4 %collective-permute-done.refs_0_ = f32[7,16,512]{2,1,0:T(8,128)S(1)} collective-permute-done((f32[7,16,512]{2,1,0:T(8,128)S(1)}, f32[7,16,512]{2,1,0:T(8,128)S(1)}, u32[]{:S(2)}, u32[]{:S(2)}) %collective-permute-start) | collective-permute-done | bytes 229408 | tf_op jit(solution)/shard_map/ppermute | solution.py:486
  8.4 1.0 %shard_map.48 = (f32[4,16,512]{2,1,0:T(8,128)S(1)}, f32[32,512]{1,0:T(8,128)S(1)}, f32[24,512]{1,0:T(8,128)S(1)}, f32[24,512]{1,0:T(8,128)S(1)}) custom-call(f32[7,16,512]{2,1,0:T(8,128)S(1)} %collective-permute-done.refs_0_, f32[24,512]{1,0:T(8,128)S(1)} %collective-permute-done.1.refs_1_, f32[2,3,4,16,512]{4,3,2,1,0:T(8,128)S(1)} %get-tuple-element.26.refs_0_.refs_2_, ...), custom_call_target="tpu_custom_call" | custom-call | tf_op jit(solution)/shard_map/pallas_call | solution.py:473
  9.4 0.5 %collective-permute-start.2 = (f32[24,512]{1,0:T(8,128)S(1)}, f32[24,512]{1,0:T(8,128)S(1)}, u32[]{:S(2)}, u32[]{:S(2)}) collective-permute-start(f32[24,512]{1,0:T(8,128)S(1)} %get-tuple-element.39), channel_id=1, source_target_pairs={{0,16},{4,8},{8,4},{12,28},{16,0},{20,24},{24,20},{28,12},{1,17},{... | collective-permute-start | bytes 147464 | tf_op jit(solution)/shard_map/ppermute | solution.py:503
  9.9 3.0 %collective-permute-start.3 = (f32[24,512]{1,0:T(8,128)S(1)}, f32[24,512]{1,0:T(8,128)S(1)}, u32[]{:S(2)}, u32[]{:S(2)}) collective-permute-start(f32[24,512]{1,0:T(8,128)S(1)} %get-tuple-element.40), channel_id=1, source_target_pairs={{0,4},{4,0},{8,12},{12,8},{16,20},{20,16},{24,28},{28,24},{1,5},{5... | collective-permute-start | bytes 147464 | tf_op jit(solution)/shard_map/ppermute | solution.py:503
  12.9 0.0 collective-permute-done.2.refs_2_
  12.9 2.6 %collective-permute-done.3.refs_3_ = f32[24,512]{1,0:T(8,128)S(1)} collective-permute-done((f32[24,512]{1,0:T(8,128)S(1)}, f32[24,512]{1,0:T(8,128)S(1)}, u32[]{:S(2)}, u32[]{:S(2)}) %collective-permute-start.3) | collective-permute-done | bytes 49184 | tf_op jit(solution)/shard_map/ppermute | solution.py:503
  15.5 0.3 %shard_map.49.h = f32[5,16,512]{2,1,0:T(8,128)S(1)} custom-call(f32[4,16,512]{2,1,0:T(8,128)S(1)} %get-tuple-element.37.refs_0_, f32[32,512]{1,0:T(8,128)S(1)} %get-tuple-element.38.refs_1_, f32[24,512]{1,0:T(8,128)S(1)} %collective-permute-done.2.refs_2_, f32[24,512]{1,0:T(8,128)S(1)} %collective-permute-done.3.refs_3_), custom_call_target="tpu_custom_call" | custom-call | tf_op jit(solution)/shard_map/pallas_call | solution.py:473
  15.8 0.1 collective-permute-start.4
  15.8 1.4 %collective-permute-done.4.other = f32[5,16,512]{2,1,0:T(8,128)S(1)} collective-permute-done((f32[5,16,512]{2,1,0:T(8,128)S(1)}, f32[5,16,512]{2,1,0:T(8,128)S(1)}, u32[]{:S(2)}, u32[]{:S(2)}) %collective-permute-start.4) | collective-permute-done | bytes 163872 | tf_op jit(solution)/shard_map/ppermute | solution.py:508
  17.3 0.2 collective-permute-start.5
  17.4 4.8 %collective-permute-done.5.z_in = f32[4,16,512]{2,1,0:T(8,128)S(1)} collective-permute-done((f32[4,16,512]{2,1,0:T(8,128)S(1)}, f32[4,16,512]{2,1,0:T(8,128)S(1)}, u32[]{:S(2)}, u32[]{:S(2)}) %collective-permute-start.5) | collective-permute-done | bytes 131104 | tf_op jit(solution)/shard_map/ppermute | solution.py:486
  22.3 0.1 collective-permute-start.6
  22.4 1.3 %collective-permute-done.6.other = f32[4,16,512]{2,1,0:T(8,128)S(1)} collective-permute-done((f32[4,16,512]{2,1,0:T(8,128)S(1)}, f32[4,16,512]{2,1,0:T(8,128)S(1)}, u32[]{:S(2)}, u32[]{:S(2)}) %collective-permute-start.6) | collective-permute-done | bytes 131104 | tf_op jit(solution)/shard_map/ppermute | solution.py:508
  23.7 0.7 %shard_map.52 = f32[4,16,512]{2,1,0:T(8,128)} custom-call(f32[4,16,512]{2,1,0:T(8,128)S(1)} %shard_map.51.part, f32[4,16,512]{2,1,0:T(8,128)S(1)} %collective-permute-done.6.other), custom_call_target="tpu_custom_call" | custom-call | tf_op jit(solution)/shard_map/pallas_call | solution.py:473
  (2 shorter events, 0.1 us)
Async XLA Ops:
  1.3 7.0 %collective-permute-start = (f32[7,16,512]{2,1,0:T(8,128)S(1)}, f32[7,16,512]{2,1,0:T(8,128)S(1)}, u32[]{:S(2)}, u32[]{:S(2)}) collective-permute-start(f32[7,16,512]{2,1,0:T(8,128)S(1)} %get-tuple-element.24), channel_id=1, source_target_pairs={{19,3},{3,2},{2,1},{1,0},{0,16},{16,17},{17,18},{18,19},{23,7},{7,... | collective-permute-start | bytes 688136 | tf_op jit(solution)/shard_map/ppermute | solution.py:486
  1.8 6.2 %collective-permute-start.1 = (f32[24,512]{1,0:T(8,128)S(1)}, f32[24,512]{1,0:T(8,128)S(1)}, u32[]{:S(2)}, u32[]{:S(2)}) collective-permute-start(f32[24,512]{1,0:T(8,128)S(1)} %get-tuple-element.25), channel_id=1, source_target_pairs={{4,0},{8,4},{12,8},{0,12},{5,1},{9,5},{13,9},{1,13},{6,2},{10,6},{... | collective-permute-start | bytes 147464 | tf_op jit(solution)/shard_map/ppermute | solution.py:491
  9.4 3.5 %collective-permute-start.2 = (f32[24,512]{1,0:T(8,128)S(1)}, f32[24,512]{1,0:T(8,128)S(1)}, u32[]{:S(2)}, u32[]{:S(2)}) collective-permute-start(f32[24,512]{1,0:T(8,128)S(1)} %get-tuple-element.39), channel_id=1, source_target_pairs={{0,16},{4,8},{8,4},{12,28},{16,0},{20,24},{24,20},{28,12},{1,17},{... | collective-permute-start | bytes 147464 | tf_op jit(solution)/shard_map/ppermute | solution.py:503
  9.9 5.6 %collective-permute-start.3 = (f32[24,512]{1,0:T(8,128)S(1)}, f32[24,512]{1,0:T(8,128)S(1)}, u32[]{:S(2)}, u32[]{:S(2)}) collective-permute-start(f32[24,512]{1,0:T(8,128)S(1)} %get-tuple-element.40), channel_id=1, source_target_pairs={{0,4},{4,0},{8,12},{12,8},{16,20},{20,16},{24,28},{28,24},{1,5},{5... | collective-permute-start | bytes 147464 | tf_op jit(solution)/shard_map/ppermute | solution.py:503
  15.8 1.5 %collective-permute-start.4 = (f32[5,16,512]{2,1,0:T(8,128)S(1)}, f32[5,16,512]{2,1,0:T(8,128)S(1)}, u32[]{:S(2)}, u32[]{:S(2)}) collective-permute-start(f32[5,16,512]{2,1,0:T(8,128)S(1)} %shard_map.49.h), channel_id=1, source_target_pairs={{0,16},{16,0},{1,17},{17,1},{2,18},{18,2},{3,19},{19,3},{4,20},{20... | collective-permute-start | bytes 491528 | tf_op jit(solution)/shard_map/ppermute | solution.py:508
  17.3 5.0 %collective-permute-start.5 = (f32[4,16,512]{2,1,0:T(8,128)S(1)}, f32[4,16,512]{2,1,0:T(8,128)S(1)}, u32[]{:S(2)}, u32[]{:S(2)}) collective-permute-start(f32[4,16,512]{2,1,0:T(8,128)S(1)} %get-tuple-element.42), channel_id=1, source_target_pairs={{19,3},{3,2},{2,1},{1,0},{0,16},{16,17},{17,18},{18,19},{23,7},{7,... | collective-permute-start | bytes 393224 | tf_op jit(solution)/shard_map/ppermute | solution.py:486
  22.3 1.4 %collective-permute-start.6 = (f32[4,16,512]{2,1,0:T(8,128)S(1)}, f32[4,16,512]{2,1,0:T(8,128)S(1)}, u32[]{:S(2)}, u32[]{:S(2)}) collective-permute-start(f32[4,16,512]{2,1,0:T(8,128)S(1)} %shard_map.51.part), channel_id=1, source_target_pairs={{0,16},{16,0},{1,17},{17,1},{2,18},{18,2},{3,19},{19,3},{4,20},{20... | collective-permute-start | bytes 393224 | tf_op jit(solution)/shard_map/ppermute | solution.py:508

commit v16 on v15

--- a/solution.py
+++ b/solution.py
@@ -183,7 +183,7 @@
     return lax.axis_index("load") == 0
 
 
-def lead_kernel(totals, disp_hbm, fixed_hbm, density_hbm, solid_hbm, disp, fixed, density, solid, z_out, y_out, sems):
+def lead_kernel(totals, disp_hbm, fixed_hbm, density_hbm, solid_hbm, disp, fixed, density, solid, d_out, z_out, y_out, sems):
     loads, comps, zlen, ylen, _ = disp.shape
     copies = [
         pltpu.make_async_copy(source, target, sems.at[k])
@@ -198,10 +198,13 @@
     gives = jnp.where(on_first(), 0, zlen - 1)
     plane = lax.axis_index("sz") * zlen + gives
     base_y = lax.axis_index("sy") * ylen
+    d_out[...] = jnp.zeros(d_out.shape, jnp.float32)
     z_out[loads * comps] = voxel_factor(density[gives], solid[gives], plane, base_y, *totals)
     for case in range(loads):
         for comp in range(comps):
-            z_out[case * comps + comp] = held(disp, fixed, case, comp, gives, slice(None))
+            k = case * comps + comp
+            z_out[k] = held(disp, fixed, case, comp, gives, slice(None))
+            d_out[k : k + 1] = z_out[k, :1]
             for z in range(zlen):
                 at = (comp * loads + case) * zlen + z
                 y_out[at : at + 1] = held(disp, fixed, case, comp, z, slice(0, 1))
@@ -289,21 +292,32 @@
 
 
 def outer_kernel(
-    shape, z_in, y_in, disp, fixed, own_in, line, sends, last_plus, last_diff, last_factor, edge, own, known, a_out, b_out, plus, diff, quotient, factor
+    shape, d_in, z_in, y_in, own_in, line, sends, last_plus, last_diff, last_factor, edge, share, plus, diff, quotient, factor
 ):
     loads, comps, zlen, ylen, xlen = shape
     planes = loads * comps
     inner = zlen - 1
     first_core, index = on_first(), lax.axis_index("sz")
     top = first_core & (index == lax.axis_size("sz") - 1)
-    keeps = jnp.where(first_core, inner, 0)
+    more = lax.axis_index("sy") < lax.axis_size("sy") - 1
     stays, comes = jnp.where(first_core, 0, 1), jnp.where(first_core, jnp.where(top, 2, 1), 0)
+    y_rows = jnp.where(more, y_in[...], 0.0)
+    y_plus, y_diff = split_x(y_rows)
+    d_plus, d_diff = split_x(jnp.where(more, d_in[...], 0.0))
     for k in range(planes):
+        case, comp = k // comps, k % comps
+        at = (comp * loads + case) * zlen
+        beside = jnp.where(first_core, y_plus[at + inner : at + zlen], y_plus[at : at + 1])
+        beside_diff = jnp.where(first_core, y_diff[at + inner : at + zlen], y_diff[at : at + 1])
         plus[k, stays, :ylen] = last_plus[k]
         diff[k, stays, :ylen] = last_diff[k]
+        plus[k, stays, ylen : ylen + 1] = beside
+        diff[k, stays, ylen : ylen + 1] = beside_diff
         whole, change = split_x(z_in[k])
         plus[k, comes, :ylen] = whole
         diff[k, comes, :ylen] = change
+        plus[k, comes, ylen : ylen + 1] = d_plus[k : k + 1]
+        diff[k, comes, ylen : ylen + 1] = d_diff[k : k + 1]
     below = jnp.where(index > 0, z_in[planes], 0.0)
     factor[...] = jnp.where(first_core, last_factor[...], below)
 
@@ -324,8 +338,7 @@
         def _(chunk):
             lanes = pl.ds(pl.multiple_of(chunk * LANES, LANES), LANES)
             (energy,) = tile_energies(plus, diff, first, lanes, 1, loads, comps)
-            here = energy * factor[first : first + TILE, lanes]
-            quotient[first + TILE : first + 2 * TILE, lanes] = blank_last(here, first, ylen)
+            quotient[first + TILE : first + 2 * TILE, lanes] = energy * factor[first : first + TILE, lanes]
 
     @pl.when(top)
     def _():
@@ -335,16 +348,14 @@
             def _(chunk):
                 lanes = pl.ds(pl.multiple_of(chunk * LANES, LANES), LANES)
                 (energy,) = tile_energies(plus, diff, first, lanes, 1, loads, comps, base=2)
-                here = energy * factor[first : first + TILE, lanes]
-                quotient[first + TILE : first + 2 * TILE, lanes] += blank_last(here, first, ylen)
+                quotient[first + TILE : first + 2 * TILE, lanes] += energy * factor[first : first + TILE, lanes]
 
     count = loads * zlen
-    more = lax.axis_index("sy") < lax.axis_size("sy") - 1
     low, high = [], []
     for comp in range(comps):
         part = slice(comp * count, (comp + 1) * count)
         whole, change = line[0, part], line[1, part]
-        whole_next, change_next = split_x(jnp.where(more, y_in[part], 0.0))
+        whole_next, change_next = y_plus[part], y_diff[part]
         face = (whole + whole_next, change + change_next, whole_next - whole, change_next - change)
         low.append(face)
         high.append([pltpu.roll(value, count - 1, 0) for value in face])
@@ -356,109 +367,82 @@
     rising = jnp.maximum(row - (TILE - 1 - ROWS), 0).astype(jnp.float32)
     ups, downs = [], []
     for z in range(inner):
-        own[z] = own_in[z]
-        own[z, ylen - TILE :] += rising * last[z : z + 1]
+        share[ylen * z : ylen * (z + 1)] = own_in[z]
+        share[ylen * (z + 1) - TILE : ylen * (z + 1)] += rising * last[z : z + 1]
         here = sends[0, REACH * z : REACH * (z + 1)]
         ups += [here[r : r + 1] + float(REACH - r) * last[z : z + 1] for r in range(REACH)]
         downs.append(sends[1, REACH * z : REACH * (z + 1)])
-    own[inner] = spread_x(spread_y(quotient, ylen))
+    share[ylen * inner : ylen * zlen] = spread_x(spread_y(quotient, ylen))
     ahead, back = to_neighbours(quotient, ylen)
     ends = spread_x(jnp.concatenate(ahead + back + [zeros[:2]], axis=0))
-    ups += [ends[: REACH - 1], factor[ylen - 1 :]]
-    downs.append(ends[REACH : 2 * REACH])
-
-    pairs = [(case, comp) for comp in range(comps) for case in range(loads)]
-    here_last = [held(disp, fixed, case, comp, keeps, slice(ylen - 1, ylen)) for case, comp in pairs]
-    here_first = [held(disp, fixed, case, comp, keeps, slice(0, 1)) for case, comp in pairs]
-    next_row = [jnp.where(first_core, y_in[k * zlen + inner : (k + 1) * zlen], y_in[k * zlen : k * zlen + 1]) for k in range(planes)]
-    next_row = [jnp.where(more, row, 0.0) for row in next_row]
-    come_last = [z_in[case * comps + comp, ylen - 1 : ylen] for case, comp in pairs]
-    come_first = [z_in[case * comps + comp, 0:1] for case, comp in pairs]
-    rows = here_last + come_last + next_row + here_first + come_first + [factor[ylen - 1 :]]
-    known[: len(rows)] = jnp.concatenate(rows, axis=0)
-    known[len(rows) :] = jnp.zeros((known.shape[0] - len(rows), xlen), jnp.float32)
-    up = jnp.concatenate(ups + here_last + come_last, axis=0)
-    down = jnp.concatenate(downs + come_first + [jnp.zeros((planes, xlen), jnp.float32)], axis=0)
-    even = lax.axis_index("sy") % 2 == 0
-    a_out[...] = jnp.where(even, up, down)
-    b_out[...] = jnp.where(even, down, up)
-
-
-def rows_kernel(loads, comps, own, known, b_in, a_in, h_out):
-    zlen, ylen, xlen = own.shape
-    planes = loads * comps
-    index, last = lax.axis_index("sy"), lax.axis_size("sy") - 1
-    even = index % 2 == 0
-    from_low = jnp.where(index > 0, jnp.where(even, b_in[...], a_in[...]), 0.0)
-    from_high = jnp.where(index < last, jnp.where(even, a_in[...], b_in[...]), 0.0)
-    ends = REACH * zlen
+    share[ylen * zlen :] = jnp.concatenate(ups + [ends[:REACH]] + downs + [ends[REACH : 2 * REACH]], axis=0)
+
+
+def total_kernel(shape, share, other, h_out, z_out, y_out, d_out, e_out):
+    _, _, zlen, ylen, xlen = shape
     first_core = on_first()
-    top = first_core & (lax.axis_index("sz") == lax.axis_size("sz") - 1)
-
-    def nodes(first, second, comp):
-        part = slice(comp * loads, (comp + 1) * loads)
-        zero = jnp.zeros((loads, xlen), jnp.float32)
-        (first, first_more), (second, second_more) = first, second
-        pieces = [first, first_more, second, second_more]
-        return split_x(jnp.concatenate([zero if piece is None else piece[part] for piece in pieces], axis=0))
-
-    def under(stays, comes):
-        return jnp.where(first_core, stays, comes), jnp.where(top, comes, 0.0)
-
-    def over(stays, comes):
-        return jnp.where(first_core, jnp.where(top, 0.0, comes), stays), None
-
-    def face(near_own, near_in, far_own, far_in, comp):
-        whole, change = nodes(near_own, near_in, comp)
-        whole_next, change_next = nodes(far_own, far_in, comp)
-        return whole + whole_next, change + change_next, whole_next - whole, change_next - change
-
-    here_last, come_last, next_row, here_first, come_first = (known[planes * k : planes * (k + 1)] for k in range(5))
-    low_last, low_come = from_low[ends : ends + planes], from_low[ends + planes : ends + 2 * planes]
-    next_come = from_high[ends : ends + planes]
-    corners = [(here_last, come_last), (low_last, low_come), (next_row, next_come), (here_first, come_first)]
-    low = [face(*(under(*corner) for corner in corners), comp) for comp in range(comps)]
-    high = [face(*(over(*corner) for corner in corners), comp) for comp in range(comps)]
-    energy = quadratic(low, high, mode_weights())
-    cases = 2 * loads
-    lines = [sum(energy[cases * k + case : cases * k + case + 1] for case in range(cases)) for k in range(2)]
-    lines = [lines[0] * known[5 * planes : 5 * planes + 1], lines[1] * from_low[ends - 1 : ends]]
-    lines = spread_x(jnp.concatenate(lines + [jnp.zeros((TILE - 2, xlen), jnp.float32)], axis=0))
-
-    row = lax.broadcasted_iota(jnp.int32, (TILE, xlen), 0)
-    rising = jnp.maximum(row - (TILE - 1 - ROWS), 0).astype(jnp.float32)
-    falling = jnp.maximum(REACH - row, 0).astype(jnp.float32)
+    inner, rows = zlen - 1, ylen * zlen
+    reach = REACH * zlen
+
+    def layers(first, count):
+        mine, theirs = share[first + inner * count : first + zlen * count], other[first + inner * count : first + zlen * count]
+        middle = share[first : first + inner * count] + other[first : first + inner * count]
+        return jnp.where(first_core, theirs, mine), middle, jnp.where(first_core, mine, theirs)
+
+    lowest, middle, highest = layers(0, ylen)
+    h_out[0] = lowest
+    for z in range(inner):
+        h_out[z + 1] = middle[ylen * z : ylen * (z + 1)]
+    h_out[zlen] = highest
+    z_out[...] = h_out[pl.ds(jnp.where(first_core, 0, 1), zlen)]
+    ups = jnp.concatenate(layers(rows, REACH), axis=0)
+    downs = jnp.concatenate(layers(rows + reach, REACH), axis=0)
+    blank = jnp.zeros((y_out.shape[0] - reach - REACH, xlen), jnp.float32)
+    y_out[...] = jnp.concatenate([jnp.where(first_core, downs, ups), blank], axis=0)
+    d_out[...] = jnp.where(first_core, downs[:reach], ups[REACH:])
+    e_out[...] = jnp.where(first_core, ups[:reach], downs[REACH:])
+
+
+def layers_kernel(h, z_in, y_in, d_in, e_in, out):
+    zlen, ylen, xlen = out.shape
+    reach = REACH * zlen
+    first_core = on_first()
+    z_index, z_last = lax.axis_index("sz"), lax.axis_size("sz") - 1
+    y_index, y_last = lax.axis_index("sy"), lax.axis_size("sy") - 1
+    z_side = jnp.where(first_core, z_index < z_last, z_index > 0)
+    y_side = jnp.where(first_core, y_index < y_last, y_index > 0)
+    y_other = jnp.where(first_core, y_index > 0, y_index < y_last)
     blank = jnp.zeros((TILE - REACH, xlen), jnp.float32)
-    between = jnp.where(first_core, zlen, 0)
-    h_out[zlen - between] = jnp.zeros((ylen, xlen), jnp.float32)
-    for z in range(zlen):
-        part = slice(REACH * z, REACH * (z + 1))
-        head = jnp.concatenate([from_low[part], blank], axis=0)
-        tail = jnp.concatenate([blank, from_high[part]], axis=0)
-        at = z + 1
-        if z == zlen - 1:
-            head = jnp.where(row == REACH - 1, 0.0, head) + falling * lines[1:2]
-            tail = tail + rising * lines[0:1]
-            at = between
-        h_out[at] = own[z]
-        h_out[at, :TILE] += head
-        h_out[at, ylen - TILE :] += tail
-
-
-def total_kernel(h, other, h_out, z_out):
-    for k in range(h.shape[0]):
-        h_out[k] = h[k] + other[k]
-    z_out[...] = h_out[pl.ds(jnp.where(on_first(), 0, 1), z_out.shape[0])]
-
-
-def layers_kernel(h, z_in, out):
-    zlen = out.shape[0]
-    first_core = on_first()
-    inside = lax.axis_index("sz") > 0, lax.axis_index("sz") < lax.axis_size("sz") - 1
-    under, over = jnp.logical_not(first_core) & inside[0], first_core & inside[1]
-    below = [jnp.where(under, z_in[k], 0.0) for k in range(zlen - REACH, zlen)]
-    above = [jnp.where(over, z_in[k], 0.0) for k in range(zlen)]
-    own = [jnp.where(first_core, h[k], 0.0) for k in range(zlen + 1)]
+
+    def at_start(rows):
+        return jnp.concatenate([rows, blank], axis=0)
+
+    def at_end(rows):
+        return jnp.concatenate([blank, rows], axis=0)
+
+    def ends(rows, keep, at_last):
+        rows = jnp.where(keep, rows, 0.0)
+        return at_start(jnp.where(at_last, 0.0, rows)), at_end(jnp.where(at_last, rows, 0.0))
+
+    def with_ends(layer, *pairs):
+        head, tail = layer[:TILE], layer[ylen - TILE :]
+        for first, last in pairs:
+            head, tail = head + first, tail + last
+        return jnp.concatenate([head, layer[TILE : ylen - TILE], tail] if ylen > 2 * TILE else [head, tail], axis=0)
+
+    own = []
+    for k in range(zlen + 1):
+        layer = jnp.where(first_core, h[k], 0.0)
+        own.append(with_ends(layer, ends(y_in[REACH * k : REACH * (k + 1)], y_side, first_core)))
+    come = []
+    for k in range(zlen):
+        part = slice(REACH * k, REACH * (k + 1))
+        layer = jnp.where(z_side, z_in[k], 0.0)
+        straight = ends(d_in[part], z_side & y_side, first_core)
+        across = ends(e_in[part], z_side & y_other, jnp.logical_not(first_core))
+        come.append(with_ends(layer, straight, across))
+    below = [jnp.where(first_core, 0.0, layer) for layer in come[zlen - REACH :]]
+    above = [jnp.where(first_core, layer, 0.0) for layer in come]
     layers = below[:-1] + [below[-1] + own[0]] + own[1:-1] + [own[-1] + above[0]] + above[1:]
     for z, layer in enumerate(spread_layers(layers)):
         out[z] = layer
@@ -480,32 +464,29 @@
     )(*args)
 
 
-def column_moved(value):
-    size = lax.axis_size("sz")
-    ring = list(range(size - 1, -1, -1)) + [size + k for k in range(size)]
-    return lax.ppermute(value, ("load", "sz"), [(ring[k - 1], ring[k]) for k in range(len(ring))])
-
-
 def ring_moved(value, axis):
     size = lax.axis_size(axis)
     return lax.ppermute(value, axis, [((k + 1) % size, k) for k in range(size)])
 
 
-def swapped(value, axis, first):
-    cores, size = lax.axis_size("load"), lax.axis_size(axis)
-    pairs = []
-    for core in range(cores):
-        for k in range(size):
-            other = k + 1 if (k - first) % 2 == 0 else k - 1
-            inside = 0 <= other < size
-            side = core if inside else cores - 1 - core
-            pairs.append((core * size + k, side * size + (other if inside else k)))
-    return lax.ppermute(value, ("load", axis), pairs)
-
-
 def chip_swapped(value):
     cores = lax.axis_size("load")
     return lax.ppermute(value, "load", [(core, cores - 1 - core) for core in range(cores)])
+
+
+def opposed(value, z_step, y_step, y_shift=0):
+    cores, rows, size = lax.axis_size("load"), lax.axis_size("sy"), lax.axis_size("sz")
+    pairs = []
+    for core in range(cores):
+        sign = -1 if core else 1
+        for y in range(rows):
+            for z in range(size):
+                to_y, to_z, side = y + sign * y_step, z + sign * z_step, core
+                if not (0 <= to_y < rows and 0 <= to_z < size):
+                    to_y, to_z, side = y, z, cores - 1 - core
+                to_y = (to_y + y_shift) % rows
+                pairs.append(((core * rows + y) * size + z, (side * rows + to_y) * size + to_z))
+    return lax.ppermute(value, ("load", "sy", "sz"), pairs)
 
 
 def body(displacements, density, solid, fixed):
@@ -516,15 +497,16 @@
         pltpu.with_memory_space_constraint(arg, pltpu.HBM) for arg in (displacements, fixed, density, solid)
     ]
 
-    disp, fixed, density, solid, z_send, y_send = call(
+    disp, fixed, density, solid, d_send, z_send, y_send = call(
         lambda *refs: lead_kernel(totals, *refs),
         [jax.ShapeDtypeStruct(arg.shape, arg.dtype) for arg in args]
-        + [(planes + 1, ylen, xlen), (planes * zlen, xlen)],
+        + [(-(-planes // TILE) * TILE, xlen), (planes + 1, ylen, xlen), (planes * zlen, xlen)],
         args,
         scratch=[pltpu.SemaphoreType.DMA((len(args),))],
         space=pltpu.HBM,
     )
-    z_in = column_moved(z_send)
+    d_in = opposed(d_send, -1, 0, y_shift=-1)
+    z_in = opposed(z_send, -1, 0)
     y_in = ring_moved(y_send, "sy")
     nodes = lambda layers: pltpu.VMEM((planes, layers, ylen + TILE, xlen), jnp.float32)
     inner = call(
@@ -541,11 +523,11 @@
         (disp, fixed, density, solid),
         scratch=[nodes(zlen), nodes(zlen), pltpu.VMEM((zlen - 1, ylen + 2 * TILE, xlen), jnp.float32)],
     )
-    size = REACH * zlen + 2 * planes
-    own, known, a_send, b_send = call(
+    reach = REACH * zlen
+    (share,) = call(
         lambda *refs: outer_kernel(displacements.shape, *refs),
-        [(zlen, ylen, xlen), (-(-(5 * planes + 1) // TILE) * TILE, xlen), (size, xlen), (size, xlen)],
-        (z_in, y_in, disp, fixed, *inner),
+        [(ylen * zlen + 2 * reach, xlen)],
+        (d_in, z_in, y_in, *inner),
         scratch=[
             nodes(4),
             nodes(4),
@@ -553,13 +535,22 @@
             pltpu.VMEM((ylen, xlen), jnp.float32),
         ],
     )
-    b_in = swapped(b_send, "sy", 1)
-    a_in = swapped(a_send, "sy", 0)
-    (h,) = call(
-        lambda *refs: rows_kernel(loads, comps, *refs), [(zlen + 1, ylen, xlen)], (own, known, b_in, a_in)
-    )
-    h, z_send = call(total_kernel, [(zlen + 1, ylen, xlen), (zlen, ylen, xlen)], (h, chip_swapped(h)))
-    (part,) = call(layers_kernel, [(zlen, ylen, xlen)], (h, column_moved(z_send)))
+    h, z_send, y_send, d_send, e_send = call(
+        lambda *refs: total_kernel(displacements.shape, *refs),
+        [
+            (zlen + 1, ylen, xlen),
+            (zlen, ylen, xlen),
+            (-(-(reach + REACH) // TILE) * TILE, xlen),
+            (reach, xlen),
+            (reach, xlen),
+        ],
+        (share, chip_swapped(share)),
+    )
+    d_in = opposed(d_send, -1, -1)
+    e_in = opposed(e_send, -1, 1)
+    y_in = opposed(y_send, 0, -1)
+    z_in = opposed(z_send, -1, 0)
+    (part,) = call(layers_kernel, [(zlen, ylen, xlen)], (h, z_in, y_in, d_in, e_in))
     (out,) = call(sum_kernel, [(zlen, ylen, xlen)], (part, chip_swapped(part)))
     return out
 

time: 24.5 us -> 22.3 us (0.910)
  the two profiles are of different devices: /device:TPU:0 before, /device:TPU:11 now
where the time goes in v16:
time: 22.3 us; the launch traced here: 22.2 us
  starting transfers between devices  9.28 us (42%)
  waiting for transfers between devices  6.97 us (31%)
  Pallas kernels  5.85 us (26%)
    ppermute x6, starting transfers between devices, opposed(): return lax.ppermute(value, ('load', 'sy', 'sz'), pairs)  8.53 us
    pallas_call x6, Pallas kernels, call(): pl.pallas_call(kernel, out_shape=shapes, in_specs=[pl.BlockSpec(memory_sp...  5.85 us
    ppermute x6, waiting for transfers between devices, opposed(): return lax.ppermute(value, ('load', 'sy', 'sz'), pairs)  4.57 us
    ppermute x2, waiting for transfers between devices, chip_swapped(): lax.ppermute(value, 'load', [(core, cores - 1 - core) for core in range(c...  2.39 us
    ppermute x2, starting transfers between devices, chip_swapped(): lax.ppermute(value, 'load', [(core, cores - 1 - core) for core in range(c...  0.5 us
  transfers between devices with their start and end apart: 9, of which 4 were waited for; matrix products, arithmetic and copies ran while one was open for 0% of the time, Pallas kernels for 12%

profile of v16, /device:TPU:11, one launch (start us, length us, event | category | flops | bytes accessed | tf_op | source)
XLA Modules:
  0.0 22.2 jit_solution(10330965231871989987)
XLA Ops:
  0.0 1.3 %shard_map.46 = (f32[2,3,4,16,512]{4,3,2,1,0:T(8,128)S(1)}, s32[4,16,512]{2,1,0:T(8,128)S(1)}, f32[4,16,512]{2,1,0:T(8,128)S(1)}, s32[4,16,512]{2,1,0:T(8,128)S(...) custom-call(f32[2,3,4,16,512]{4,3,2,1,0:T(8,128)} %refs_0_.1, s32[4,16,512]{2,1,0:T(8,128)} %refs_1_.1, ...), custom_call_target="tpu_custom_call" | custom-call | tf_op jit(solution)/shard_map/pallas_call | solution.py:457
  1.3 1.3 %collective-permute-start.1 = (f32[7,16,512]{2,1,0:T(8,128)S(1)}, f32[7,16,512]{2,1,0:T(8,128)S(1)}, u32[]{:S(2)}, u32[]{:S(2)}) collective-permute-start(f32[7,16,512]{2,1,0:T(8,128)S(1)} %get-tuple-element.25), channel_id=1, source_target_pairs={{0,16},{1,0},{2,1},{3,2},{4,20},{5,4},{6,5},{7,6},{8,24},{9,8},{10... | collective-permute-start | bytes 688136 | tf_op jit(solution)/shard_map/ppermute | solution.py:489
  2.6 0.3 %collective-permute-start.2 = (f32[24,512]{1,0:T(8,128)S(1)}, f32[24,512]{1,0:T(8,128)S(1)}, u32[]{:S(2)}, u32[]{:S(2)}) collective-permute-start(f32[24,512]{1,0:T(8,128)S(1)} %get-tuple-element.26), channel_id=1, source_target_pairs={{4,0},{8,4},{12,8},{0,12},{5,1},{9,5},{13,9},{1,13},{6,2},{10,6},{... | collective-permute-start | bytes 147464 | tf_op jit(solution)/shard_map/ppermute | solution.py:469
  2.9 3.2 %collective-permute-start = (f32[8,512]{1,0:T(8,128)S(1)}, f32[8,512]{1,0:T(8,128)S(1)}, u32[]{:S(2)}, u32[]{:S(2)}) collective-permute-start(f32[8,512]{1,0:T(8,128)S(1)} %get-tuple-element.24), channel_id=1, source_target_pairs={{0,28},{1,12},{2,13},{3,14},{4,16},{5,0},{6,1},{7,2},{8,20},{9,4},... | collective-permute-start | bytes 49160 | tf_op jit(solution)/shard_map/ppermute | solution.py:489
  6.1 2.7 %shard_map.47 = (f32[4,16,512]{2,1,0:T(8,128)S(1)}, f32[2,24,512]{2,1,0:T(8,128)S(1)}, f32[2,9,512]{2,1,0:T(8,128)S(1)}, f32[6,16,512]{2,1,0:T(8,128)S(1)}, f32[...) custom-call(f32[2,3,4,16,512]{4,3,2,1,0:T(8,128)S(1)} %get-tuple-element.27.refs_0_, ...), custom_call_target="tpu_custom_call" | custom-call | tf_op jit(solution)/shard_map/pallas_call | solution.py:457
  8.8 0.0 collective-permute-done.refs_0_
  8.8 0.0 collective-permute-done.2.refs_2_
  8.8 0.0 collective-permute-done.1.refs_1_
  8.8 1.0 %shard_map.48.refs_0_ = f32[88,512]{1,0:T(8,128)S(1)} custom-call(f32[8,512]{1,0:T(8,128)S(1)} %collective-permute-done.refs_0_, f32[7,16,512]{2,1,0:T(8,128)S(1)} %collective-permute-done.1.refs_1_, f32[24,512]{1,0:T(8,128)S(1)} %collective-permute-done.2.refs_2_, f32[4,16,512]{2,1,0:T(8,128)S(1)} %get-tuple-element.31.refs_3_, ...), custom_call_target="tpu_custom_call" | custom-call | tf_op jit(solution)/shard_map/pallas_call | solution.py:457
  9.8 0.4 %collective-permute-start.3 = (f32[88,512]{1,0:T(8,128)S(1)}, f32[88,512]{1,0:T(8,128)S(1)}, u32[]{:S(2)}, u32[]{:S(2)}) collective-permute-start(f32[88,512]{1,0:T(8,128)S(1)} %shard_map.48.refs_0_), channel_id=1, source_target_pairs={{0,16},{16,0},{1,17},{17,1},{2,18},{18,2},{3,19},{19,3},{4,20},{20... | collective-permute-start | bytes 540680 | tf_op jit(solution)/shard_map/ppermute | solution.py:474
  10.2 1.1 %collective-permute-done.3.refs_1_ = f32[88,512]{1,0:T(8,128)S(1)} collective-permute-done((f32[88,512]{1,0:T(8,128)S(1)}, f32[88,512]{1,0:T(8,128)S(1)}, u32[]{:S(2)}, u32[]{:S(2)}) %collective-permute-start.3) | collective-permute-done | bytes 180256 | tf_op jit(solution)/shard_map/ppermute | solution.py:474
  11.3 1.3 %collective-permute-start.4 = (f32[4,16,512]{2,1,0:T(8,128)S(1)}, f32[4,16,512]{2,1,0:T(8,128)S(1)}, u32[]{:S(2)}, u32[]{:S(2)}) collective-permute-start(f32[4,16,512]{2,1,0:T(8,128)S(1)} %get-tuple-element.39), channel_id=1, source_target_pairs={{0,16},{1,0},{2,1},{3,2},{4,20},{5,4},{6,5},{7,6},{8,24},{9,8},{10... | collective-permute-start | bytes 393224 | tf_op jit(solution)/shard_map/ppermute | solution.py:489
  12.6 1.2 %collective-permute-start.5 = (f32[16,512]{1,0:T(8,128)S(1)}, f32[16,512]{1,0:T(8,128)S(1)}, u32[]{:S(2)}, u32[]{:S(2)}) collective-permute-start(f32[16,512]{1,0:T(8,128)S(1)} %get-tuple-element.40), channel_id=1, source_target_pairs={{0,16},{1,17},{2,18},{3,19},{4,0},{5,1},{6,2},{7,3},{8,4},{9,5},{1... | collective-permute-start | bytes 98312 | tf_op jit(solution)/shard_map/ppermute | solution.py:489
  13.8 1.5 %collective-permute-start.6 = (f32[12,512]{1,0:T(8,128)S(1)}, f32[12,512]{1,0:T(8,128)S(1)}, u32[]{:S(2)}, u32[]{:S(2)}) collective-permute-start(f32[12,512]{1,0:T(8,128)S(1)} %get-tuple-element.41), channel_id=1, source_target_pairs={{0,16},{1,17},{2,18},{3,19},{4,20},{5,0},{6,1},{7,2},{8,24},{9,4},... | collective-permute-start | bytes 73736 | tf_op jit(solution)/shard_map/ppermute | solution.py:489
  15.4 0.0 collective-permute-start.7
  15.4 2.4 %collective-permute-done.6.d_in = f32[12,512]{1,0:T(8,128)S(1)} collective-permute-done((f32[12,512]{1,0:T(8,128)S(1)}, f32[12,512]{1,0:T(8,128)S(1)}, u32[]{:S(2)}, u32[]{:S(2)}) %collective-permute-start.6) | collective-permute-done | bytes 24608 | tf_op jit(solution)/shard_map/ppermute | solution.py:489
  17.8 2.1 %collective-permute-done.7.e_in = f32[12,512]{1,0:T(8,128)S(1)} collective-permute-done((f32[12,512]{1,0:T(8,128)S(1)}, f32[12,512]{1,0:T(8,128)S(1)}, u32[]{:S(2)}, u32[]{:S(2)}) %collective-permute-start.7) | collective-permute-done | bytes 24608 | tf_op jit(solution)/shard_map/ppermute | solution.py:489
  19.9 0.0 collective-permute-done.5.y_in
  19.9 0.0 collective-permute-done.4.z_in
  19.9 0.1 shard_map.50.part
  20.1 0.1 collective-permute-start.8
  20.2 1.3 %collective-permute-done.8.other = f32[4,16,512]{2,1,0:T(8,128)S(1)} collective-permute-done((f32[4,16,512]{2,1,0:T(8,128)S(1)}, f32[4,16,512]{2,1,0:T(8,128)S(1)}, u32[]{:S(2)}, u32[]{:S(2)}) %collective-permute-start.8) | collective-permute-done | bytes 131104 | tf_op jit(solution)/shard_map/ppermute | solution.py:474
  21.5 0.7 %shard_map.51 = f32[4,16,512]{2,1,0:T(8,128)} custom-call(f32[4,16,512]{2,1,0:T(8,128)S(1)} %shard_map.50.part, f32[4,16,512]{2,1,0:T(8,128)S(1)} %collective-permute-done.8.other), custom_call_target="tpu_custom_call" | custom-call | tf_op jit(solution)/shard_map/pallas_call | solution.py:457
  (1 shorter events, 0.0 us)
Async XLA Ops:
  1.3 7.5 %collective-permute-start.1 = (f32[7,16,512]{2,1,0:T(8,128)S(1)}, f32[7,16,512]{2,1,0:T(8,128)S(1)}, u32[]{:S(2)}, u32[]{:S(2)}) collective-permute-start(f32[7,16,512]{2,1,0:T(8,128)S(1)} %get-tuple-element.25), channel_id=1, source_target_pairs={{0,16},{1,0},{2,1},{3,2},{4,20},{5,4},{6,5},{7,6},{8,24},{9,8},{10... | collective-permute-start | bytes 688136 | tf_op jit(solution)/shard_map/ppermute | solution.py:489
  2.6 6.1 %collective-permute-start.2 = (f32[24,512]{1,0:T(8,128)S(1)}, f32[24,512]{1,0:T(8,128)S(1)}, u32[]{:S(2)}, u32[]{:S(2)}) collective-permute-start(f32[24,512]{1,0:T(8,128)S(1)} %get-tuple-element.26), channel_id=1, source_target_pairs={{4,0},{8,4},{12,8},{0,12},{5,1},{9,5},{13,9},{1,13},{6,2},{10,6},{... | collective-permute-start | bytes 147464 | tf_op jit(solution)/shard_map/ppermute | solution.py:469
  2.9 5.9 %collective-permute-start = (f32[8,512]{1,0:T(8,128)S(1)}, f32[8,512]{1,0:T(8,128)S(1)}, u32[]{:S(2)}, u32[]{:S(2)}) collective-permute-start(f32[8,512]{1,0:T(8,128)S(1)} %get-tuple-element.24), channel_id=1, source_target_pairs={{0,28},{1,12},{2,13},{3,14},{4,16},{5,0},{6,1},{7,2},{8,20},{9,4},... | collective-permute-start | bytes 49160 | tf_op jit(solution)/shard_map/ppermute | solution.py:489
  9.8 1.5 %collective-permute-start.3 = (f32[88,512]{1,0:T(8,128)S(1)}, f32[88,512]{1,0:T(8,128)S(1)}, u32[]{:S(2)}, u32[]{:S(2)}) collective-permute-start(f32[88,512]{1,0:T(8,128)S(1)} %shard_map.48.refs_0_), channel_id=1, source_target_pairs={{0,16},{16,0},{1,17},{17,1},{2,18},{18,2},{3,19},{19,3},{4,20},{20... | collective-permute-start | bytes 540680 | tf_op jit(solution)/shard_map/ppermute | solution.py:474
  11.3 8.6 %collective-permute-start.4 = (f32[4,16,512]{2,1,0:T(8,128)S(1)}, f32[4,16,512]{2,1,0:T(8,128)S(1)}, u32[]{:S(2)}, u32[]{:S(2)}) collective-permute-start(f32[4,16,512]{2,1,0:T(8,128)S(1)} %get-tuple-element.39), channel_id=1, source_target_pairs={{0,16},{1,0},{2,1},{3,2},{4,20},{5,4},{6,5},{7,6},{8,24},{9,8},{10... | collective-permute-start | bytes 393224 | tf_op jit(solution)/shard_map/ppermute | solution.py:489
  12.6 7.3 %collective-permute-start.5 = (f32[16,512]{1,0:T(8,128)S(1)}, f32[16,512]{1,0:T(8,128)S(1)}, u32[]{:S(2)}, u32[]{:S(2)}) collective-permute-start(f32[16,512]{1,0:T(8,128)S(1)} %get-tuple-element.40), channel_id=1, source_target_pairs={{0,16},{1,17},{2,18},{3,19},{4,0},{5,1},{6,2},{7,3},{8,4},{9,5},{1... | collective-permute-start | bytes 98312 | tf_op jit(solution)/shard_map/ppermute | solution.py:489
  13.8 4.0 %collective-permute-start.6 = (f32[12,512]{1,0:T(8,128)S(1)}, f32[12,512]{1,0:T(8,128)S(1)}, u32[]{:S(2)}, u32[]{:S(2)}) collective-permute-start(f32[12,512]{1,0:T(8,128)S(1)} %get-tuple-element.41), channel_id=1, source_target_pairs={{0,16},{1,17},{2,18},{3,19},{4,20},{5,0},{6,1},{7,2},{8,24},{9,4},... | collective-permute-start | bytes 73736 | tf_op jit(solution)/shard_map/ppermute | solution.py:489
  15.4 4.6 %collective-permute-start.7 = (f32[12,512]{1,0:T(8,128)S(1)}, f32[12,512]{1,0:T(8,128)S(1)}, u32[]{:S(2)}, u32[]{:S(2)}) collective-permute-start(f32[12,512]{1,0:T(8,128)S(1)} %get-tuple-element.42), channel_id=1, source_target_pairs={{0,16},{1,4},{2,5},{3,6},{4,20},{5,8},{6,9},{7,10},{8,24},{9,12},{... | collective-permute-start | bytes 73736 | tf_op jit(solution)/shard_map/ppermute | solution.py:489
  20.1 1.4 %collective-permute-start.8 = (f32[4,16,512]{2,1,0:T(8,128)S(1)}, f32[4,16,512]{2,1,0:T(8,128)S(1)}, u32[]{:S(2)}, u32[]{:S(2)}) collective-permute-start(f32[4,16,512]{2,1,0:T(8,128)S(1)} %shard_map.50.part), channel_id=1, source_target_pairs={{0,16},{16,0},{1,17},{17,1},{2,18},{18,2},{3,19},{19,3},{4,20},{20... | collective-permute-start | bytes 393224 | tf_op jit(solution)/shard_map/ppermute | solution.py:474

commit v17 on v16

--- a/solution.py
+++ b/solution.py
@@ -378,7 +378,7 @@
     share[ylen * zlen :] = jnp.concatenate(ups + [ends[:REACH]] + downs + [ends[REACH : 2 * REACH]], axis=0)
 
 
-def total_kernel(shape, share, other, h_out, z_out, y_out, d_out, e_out):
+def total_kernel(shape, share, other, h_out, d_out, e_out, y_out, *z_outs):
     _, _, zlen, ylen, xlen = shape
     first_core = on_first()
     inner, rows = zlen - 1, ylen * zlen
@@ -394,18 +394,20 @@
     for z in range(inner):
         h_out[z + 1] = middle[ylen * z : ylen * (z + 1)]
     h_out[zlen] = highest
-    z_out[...] = h_out[pl.ds(jnp.where(first_core, 0, 1), zlen)]
+    for k, z_out in enumerate(z_outs):
+        z_out[...] = h_out[jnp.where(first_core, k, k + 1)]
     ups = jnp.concatenate(layers(rows, REACH), axis=0)
     downs = jnp.concatenate(layers(rows + reach, REACH), axis=0)
-    blank = jnp.zeros((y_out.shape[0] - reach - REACH, xlen), jnp.float32)
-    y_out[...] = jnp.concatenate([jnp.where(first_core, downs, ups), blank], axis=0)
-    d_out[...] = jnp.where(first_core, downs[:reach], ups[REACH:])
-    e_out[...] = jnp.where(first_core, ups[:reach], downs[REACH:])
-
-
-def layers_kernel(h, z_in, y_in, d_in, e_in, out):
+    y_out[: reach + REACH] = jnp.where(first_core, downs, ups)
+    for out, used in ((y_out, reach + REACH), (d_out, reach), (e_out, reach)):
+        out[used:] = jnp.zeros((out.shape[0] - used, xlen), jnp.float32)
+    d_out[:reach] = jnp.where(first_core, downs[:reach], ups[REACH:])
+    e_out[:reach] = jnp.where(first_core, ups[:reach], downs[REACH:])
+
+
+def layers_kernel(h, d_in, e_in, y_in, *rest):
+    *z_in, out = rest
     zlen, ylen, xlen = out.shape
-    reach = REACH * zlen
     first_core = on_first()
     z_index, z_last = lax.axis_index("sz"), lax.axis_size("sz") - 1
     y_index, y_last = lax.axis_index("sy"), lax.axis_size("sy") - 1
@@ -437,7 +439,7 @@
     come = []
     for k in range(zlen):
         part = slice(REACH * k, REACH * (k + 1))
-        layer = jnp.where(z_side, z_in[k], 0.0)
+        layer = jnp.where(z_side, z_in[k][...], 0.0)
         straight = ends(d_in[part], z_side & y_side, first_core)
         across = ends(e_in[part], z_side & y_other, jnp.logical_not(first_core))
         come.append(with_ends(layer, straight, across))
@@ -535,22 +537,17 @@
             pltpu.VMEM((ylen, xlen), jnp.float32),
         ],
     )
-    h, z_send, y_send, d_send, e_send = call(
+    sent = (-(-(reach + REACH) // TILE) * TILE, xlen)
+    h, d_send, e_send, y_send, *z_sends = call(
         lambda *refs: total_kernel(displacements.shape, *refs),
-        [
-            (zlen + 1, ylen, xlen),
-            (zlen, ylen, xlen),
-            (-(-(reach + REACH) // TILE) * TILE, xlen),
-            (reach, xlen),
-            (reach, xlen),
-        ],
+        [(zlen + 1, ylen, xlen)] + 3 * [sent] + zlen * [(ylen, xlen)],
         (share, chip_swapped(share)),
     )
     d_in = opposed(d_send, -1, -1)
     e_in = opposed(e_send, -1, 1)
     y_in = opposed(y_send, 0, -1)
-    z_in = opposed(z_send, -1, 0)
-    (part,) = call(layers_kernel, [(zlen, ylen, xlen)], (h, z_in, y_in, d_in, e_in))
+    z_in = [opposed(z_send, -1, 0) for z_send in z_sends]
+    (part,) = call(layers_kernel, [(zlen, ylen, xlen)], (h, d_in, e_in, y_in, *z_in))
     (out,) = call(sum_kernel, [(zlen, ylen, xlen)], (part, chip_swapped(part)))
     return out
 

time: 22.3 us -> 24.9 us (1.12)
  the two profiles are of different devices: /device:TPU:11 before, /device:TPU:0 now
where the time goes in v17:
time: 24.9 us; the launch traced here: 24.7 us
  starting transfers between devices  11.6 us (47%)
  waiting for transfers between devices  7.21 us (29%)
  Pallas kernels  5.84 us (23%)
    ppermute x9, starting transfers between devices, opposed(): return lax.ppermute(value, ('load', 'sy', 'sz'), pairs)  7.87 us
    pallas_call x6, Pallas kernels, call(): pl.pallas_call(kernel, out_shape=shapes, in_specs=[pl.BlockSpec(memory_sp...  5.84 us
    ppermute x9, waiting for transfers between devices, opposed(): return lax.ppermute(value, ('load', 'sy', 'sz'), pairs)  4.58 us
    ppermute x1, starting transfers between devices, ring_moved(): return lax.ppermute(value, axis, [((k + 1) % size, k) for k in range(size)])  3.51 us
    ppermute x2, waiting for transfers between devices, chip_swapped(): lax.ppermute(value, 'load', [(core, cores - 1 - core) for core in range(c...  2.63 us
  transfers between devices with their start and end apart: 12, of which 6 were waited for; matrix products, arithmetic and copies ran while one was open for 0% of the time, Pallas kernels for 11%

profile of v17, /device:TPU:0, one launch (start us, length us, event | category | flops | bytes accessed | tf_op | source)
XLA Modules:
  0.0 24.7 jit_solution(13912651866859705926)
XLA Ops:
  0.0 1.3 %shard_map.46 = (f32[2,3,4,16,512]{4,3,2,1,0:T(8,128)S(1)}, s32[4,16,512]{2,1,0:T(8,128)S(1)}, f32[4,16,512]{2,1,0:T(8,128)S(1)}, s32[4,16,512]{2,1,0:T(8,128)S(...) custom-call(f32[2,3,4,16,512]{4,3,2,1,0:T(8,128)} %refs_0_.1, s32[4,16,512]{2,1,0:T(8,128)} %refs_1_.1, ...), custom_call_target="tpu_custom_call" | custom-call | tf_op jit(solution)/shard_map/pallas_call | solution.py:459
  1.3 0.5 %collective-permute-start.1 = (f32[7,16,512]{2,1,0:T(8,128)S(1)}, f32[7,16,512]{2,1,0:T(8,128)S(1)}, u32[]{:S(2)}, u32[]{:S(2)}) collective-permute-start(f32[7,16,512]{2,1,0:T(8,128)S(1)} %get-tuple-element.28), channel_id=1, source_target_pairs={{0,16},{1,0},{2,1},{3,2},{4,20},{5,4},{6,5},{7,6},{8,24},{9,8},{10... | collective-permute-start | bytes 688136 | tf_op jit(solution)/shard_map/ppermute | solution.py:491
  1.8 3.5 %collective-permute-start.2 = (f32[24,512]{1,0:T(8,128)S(1)}, f32[24,512]{1,0:T(8,128)S(1)}, u32[]{:S(2)}, u32[]{:S(2)}) collective-permute-start(f32[24,512]{1,0:T(8,128)S(1)} %get-tuple-element.29), channel_id=1, source_target_pairs={{4,0},{8,4},{12,8},{0,12},{5,1},{9,5},{13,9},{1,13},{6,2},{10,6},{... | collective-permute-start | bytes 147464 | tf_op jit(solution)/shard_map/ppermute | solution.py:471
  5.3 0.9 %collective-permute-start = (f32[8,512]{1,0:T(8,128)S(1)}, f32[8,512]{1,0:T(8,128)S(1)}, u32[]{:S(2)}, u32[]{:S(2)}) collective-permute-start(f32[8,512]{1,0:T(8,128)S(1)} %get-tuple-element.27), channel_id=1, source_target_pairs={{0,28},{1,12},{2,13},{3,14},{4,16},{5,0},{6,1},{7,2},{8,20},{9,4},... | collective-permute-start | bytes 49160 | tf_op jit(solution)/shard_map/ppermute | solution.py:491
  6.2 2.7 %shard_map.47 = (f32[4,16,512]{2,1,0:T(8,128)S(1)}, f32[2,24,512]{2,1,0:T(8,128)S(1)}, f32[2,9,512]{2,1,0:T(8,128)S(1)}, f32[6,16,512]{2,1,0:T(8,128)S(1)}, f32[...) custom-call(f32[2,3,4,16,512]{4,3,2,1,0:T(8,128)S(1)} %get-tuple-element.30.refs_0_, ...), custom_call_target="tpu_custom_call" | custom-call | tf_op jit(solution)/shard_map/pallas_call | solution.py:459
  8.9 1.0 %collective-permute-done.refs_0_ = f32[8,512]{1,0:T(8,128)S(1)} collective-permute-done((f32[8,512]{1,0:T(8,128)S(1)}, f32[8,512]{1,0:T(8,128)S(1)}, u32[]{:S(2)}, u32[]{:S(2)}) %collective-permute-start) | collective-permute-done | bytes 16416 | tf_op jit(solution)/shard_map/ppermute | solution.py:491
  9.9 0.0 collective-permute-done.2.refs_2_
  9.9 0.0 collective-permute-done.1.refs_1_
  10.0 1.0 %shard_map.48.refs_0_ = f32[88,512]{1,0:T(8,128)S(1)} custom-call(f32[8,512]{1,0:T(8,128)S(1)} %collective-permute-done.refs_0_, f32[7,16,512]{2,1,0:T(8,128)S(1)} %collective-permute-done.1.refs_1_, f32[24,512]{1,0:T(8,128)S(1)} %collective-permute-done.2.refs_2_, f32[4,16,512]{2,1,0:T(8,128)S(1)} %get-tuple-element.34.refs_3_, ...), custom_call_target="tpu_custom_call" | custom-call | tf_op jit(solution)/shard_map/pallas_call | solution.py:459
  11.0 0.2 collective-permute-start.3
  11.1 1.3 %collective-permute-done.3.refs_1_ = f32[88,512]{1,0:T(8,128)S(1)} collective-permute-done((f32[88,512]{1,0:T(8,128)S(1)}, f32[88,512]{1,0:T(8,128)S(1)}, u32[]{:S(2)}, u32[]{:S(2)}) %collective-permute-start.3) | collective-permute-done | bytes 180256 | tf_op jit(solution)/shard_map/ppermute | solution.py:476
  12.5 0.2 collective-permute-start.4
  12.7 2.2 %collective-permute-start.5 = (f32[16,512]{1,0:T(8,128)S(1)}, f32[16,512]{1,0:T(8,128)S(1)}, u32[]{:S(2)}, u32[]{:S(2)}) collective-permute-start(f32[16,512]{1,0:T(8,128)S(1)} %get-tuple-element.43), channel_id=1, source_target_pairs={{0,16},{1,4},{2,5},{3,6},{4,20},{5,8},{6,9},{7,10},{8,24},{9,12},{... | collective-permute-start | bytes 98312 | tf_op jit(solution)/shard_map/ppermute | solution.py:491
  14.9 0.0 collective-permute-start.6
  14.9 2.5 %collective-permute-start.7 = (f32[16,512]{1,0:T(8,128)S(1)}, f32[16,512]{1,0:T(8,128)S(1)}, u32[]{:S(2)}, u32[]{:S(2)}) collective-permute-start(f32[16,512]{1,0:T(8,128)S(1)} %get-tuple-element.45), channel_id=1, source_target_pairs={{0,16},{1,0},{2,1},{3,2},{4,20},{5,4},{6,5},{7,6},{8,24},{9,8},{10... | collective-permute-start | bytes 98312 | tf_op jit(solution)/shard_map/ppermute | solution.py:491
  17.4 0.9 %collective-permute-start.8 = (f32[16,512]{1,0:T(8,128)S(1)}, f32[16,512]{1,0:T(8,128)S(1)}, u32[]{:S(2)}, u32[]{:S(2)}) collective-permute-start(f32[16,512]{1,0:T(8,128)S(1)} %get-tuple-element.46), channel_id=1, source_target_pairs={{0,16},{1,0},{2,1},{3,2},{4,20},{5,4},{6,5},{7,6},{8,24},{9,8},{10... | collective-permute-start | bytes 98312 | tf_op jit(solution)/shard_map/ppermute | solution.py:491
  18.3 0.0 collective-permute-done.4.d_in
  18.3 0.0 collective-permute-start.9
  18.3 0.0 collective-permute-done.5.e_in
  18.3 0.7 %collective-permute-start.10 = (f32[16,512]{1,0:T(8,128)S(1)}, f32[16,512]{1,0:T(8,128)S(1)}, u32[]{:S(2)}, u32[]{:S(2)}) collective-permute-start(f32[16,512]{1,0:T(8,128)S(1)} %get-tuple-element.48), channel_id=1, source_target_pairs={{0,16},{1,0},{2,1},{3,2},{4,20},{5,4},{6,5},{7,6},{8,24},{9,8},{10... | collective-permute-start | bytes 98312 | tf_op jit(solution)/shard_map/ppermute | solution.py:491
  19.0 0.0 collective-permute-done.6.y_in
  19.0 0.0 collective-permute-done.7.rest_0_
  19.0 2.3 %collective-permute-done.8.rest_1_ = f32[16,512]{1,0:T(8,128)S(1)} collective-permute-done((f32[16,512]{1,0:T(8,128)S(1)}, f32[16,512]{1,0:T(8,128)S(1)}, u32[]{:S(2)}, u32[]{:S(2)}) %collective-permute-start.8) | collective-permute-done | bytes 32800 | tf_op jit(solution)/shard_map/ppermute | solution.py:491
  21.3 0.9 %collective-permute-done.9.rest_2_ = f32[16,512]{1,0:T(8,128)S(1)} collective-permute-done((f32[16,512]{1,0:T(8,128)S(1)}, f32[16,512]{1,0:T(8,128)S(1)}, u32[]{:S(2)}, u32[]{:S(2)}) %collective-permute-start.9) | collective-permute-done | bytes 32800 | tf_op jit(solution)/shard_map/ppermute | solution.py:491
  22.2 0.4 %collective-permute-done.10.rest_3_ = f32[16,512]{1,0:T(8,128)S(1)} collective-permute-done((f32[16,512]{1,0:T(8,128)S(1)}, f32[16,512]{1,0:T(8,128)S(1)}, u32[]{:S(2)}, u32[]{:S(2)}) %collective-permute-start.10) | collective-permute-done | bytes 32800 | tf_op jit(solution)/shard_map/ppermute | solution.py:491
  22.5 0.1 shard_map.50.part
  22.7 0.1 collective-permute-start.11
  22.7 1.3 %collective-permute-done.11.other = f32[4,16,512]{2,1,0:T(8,128)S(1)} collective-permute-done((f32[4,16,512]{2,1,0:T(8,128)S(1)}, f32[4,16,512]{2,1,0:T(8,128)S(1)}, u32[]{:S(2)}, u32[]{:S(2)}) %collective-permute-start.11) | collective-permute-done | bytes 131104 | tf_op jit(solution)/shard_map/ppermute | solution.py:476
  24.1 0.7 %shard_map.51 = f32[4,16,512]{2,1,0:T(8,128)} custom-call(f32[4,16,512]{2,1,0:T(8,128)S(1)} %shard_map.50.part, f32[4,16,512]{2,1,0:T(8,128)S(1)} %collective-permute-done.11.other), custom_call_target="tpu_custom_call" | custom-call | tf_op jit(solution)/shard_map/pallas_call | solution.py:459
  (1 shorter events, 0.0 us)
Async XLA Ops:
  1.3 8.6 %collective-permute-start.1 = (f32[7,16,512]{2,1,0:T(8,128)S(1)}, f32[7,16,512]{2,1,0:T(8,128)S(1)}, u32[]{:S(2)}, u32[]{:S(2)}) collective-permute-start(f32[7,16,512]{2,1,0:T(8,128)S(1)} %get-tuple-element.28), channel_id=1, source_target_pairs={{0,16},{1,0},{2,1},{3,2},{4,20},{5,4},{6,5},{7,6},{8,24},{9,8},{10... | collective-permute-start | bytes 688136 | tf_op jit(solution)/shard_map/ppermute | solution.py:491
  1.8 8.1 %collective-permute-start.2 = (f32[24,512]{1,0:T(8,128)S(1)}, f32[24,512]{1,0:T(8,128)S(1)}, u32[]{:S(2)}, u32[]{:S(2)}) collective-permute-start(f32[24,512]{1,0:T(8,128)S(1)} %get-tuple-element.29), channel_id=1, source_target_pairs={{4,0},{8,4},{12,8},{0,12},{5,1},{9,5},{13,9},{1,13},{6,2},{10,6},{... | collective-permute-start | bytes 147464 | tf_op jit(solution)/shard_map/ppermute | solution.py:471
  5.3 4.6 %collective-permute-start = (f32[8,512]{1,0:T(8,128)S(1)}, f32[8,512]{1,0:T(8,128)S(1)}, u32[]{:S(2)}, u32[]{:S(2)}) collective-permute-start(f32[8,512]{1,0:T(8,128)S(1)} %get-tuple-element.27), channel_id=1, source_target_pairs={{0,28},{1,12},{2,13},{3,14},{4,16},{5,0},{6,1},{7,2},{8,20},{9,4},... | collective-permute-start | bytes 49160 | tf_op jit(solution)/shard_map/ppermute | solution.py:491
  11.0 1.5 %collective-permute-start.3 = (f32[88,512]{1,0:T(8,128)S(1)}, f32[88,512]{1,0:T(8,128)S(1)}, u32[]{:S(2)}, u32[]{:S(2)}) collective-permute-start(f32[88,512]{1,0:T(8,128)S(1)} %shard_map.48.refs_0_), channel_id=1, source_target_pairs={{0,16},{16,0},{1,17},{17,1},{2,18},{18,2},{3,19},{19,3},{4,20},{20... | collective-permute-start | bytes 540680 | tf_op jit(solution)/shard_map/ppermute | solution.py:476
  12.5 5.8 %collective-permute-start.4 = (f32[16,512]{1,0:T(8,128)S(1)}, f32[16,512]{1,0:T(8,128)S(1)}, u32[]{:S(2)}, u32[]{:S(2)}) collective-permute-start(f32[16,512]{1,0:T(8,128)S(1)} %get-tuple-element.42), channel_id=1, source_target_pairs={{0,16},{1,17},{2,18},{3,19},{4,20},{5,0},{6,1},{7,2},{8,24},{9,4},... | collective-permute-start | bytes 98312 | tf_op jit(solution)/shard_map/ppermute | solution.py:491
  12.7 5.6 %collective-permute-start.5 = (f32[16,512]{1,0:T(8,128)S(1)}, f32[16,512]{1,0:T(8,128)S(1)}, u32[]{:S(2)}, u32[]{:S(2)}) collective-permute-start(f32[16,512]{1,0:T(8,128)S(1)} %get-tuple-element.43), channel_id=1, source_target_pairs={{0,16},{1,4},{2,5},{3,6},{4,20},{5,8},{6,9},{7,10},{8,24},{9,12},{... | collective-permute-start | bytes 98312 | tf_op jit(solution)/shard_map/ppermute | solution.py:491
  14.9 4.1 %collective-permute-start.6 = (f32[16,512]{1,0:T(8,128)S(1)}, f32[16,512]{1,0:T(8,128)S(1)}, u32[]{:S(2)}, u32[]{:S(2)}) collective-permute-start(f32[16,512]{1,0:T(8,128)S(1)} %get-tuple-element.44), channel_id=1, source_target_pairs={{0,16},{1,17},{2,18},{3,19},{4,0},{5,1},{6,2},{7,3},{8,4},{9,5},{1... | collective-permute-start | bytes 98312 | tf_op jit(solution)/shard_map/ppermute | solution.py:491
  14.9 4.1 %collective-permute-start.7 = (f32[16,512]{1,0:T(8,128)S(1)}, f32[16,512]{1,0:T(8,128)S(1)}, u32[]{:S(2)}, u32[]{:S(2)}) collective-permute-start(f32[16,512]{1,0:T(8,128)S(1)} %get-tuple-element.45), channel_id=1, source_target_pairs={{0,16},{1,0},{2,1},{3,2},{4,20},{5,4},{6,5},{7,6},{8,24},{9,8},{10... | collective-permute-start | bytes 98312 | tf_op jit(solution)/shard_map/ppermute | solution.py:491
  17.4 3.9 %collective-permute-start.8 = (f32[16,512]{1,0:T(8,128)S(1)}, f32[16,512]{1,0:T(8,128)S(1)}, u32[]{:S(2)}, u32[]{:S(2)}) collective-permute-start(f32[16,512]{1,0:T(8,128)S(1)} %get-tuple-element.46), channel_id=1, source_target_pairs={{0,16},{1,0},{2,1},{3,2},{4,20},{5,4},{6,5},{7,6},{8,24},{9,8},{10... | collective-permute-start | bytes 98312 | tf_op jit(solution)/shard_map/ppermute | solution.py:491
  18.3 3.9 %collective-permute-start.9 = (f32[16,512]{1,0:T(8,128)S(1)}, f32[16,512]{1,0:T(8,128)S(1)}, u32[]{:S(2)}, u32[]{:S(2)}) collective-permute-start(f32[16,512]{1,0:T(8,128)S(1)} %get-tuple-element.47), channel_id=1, source_target_pairs={{0,16},{1,0},{2,1},{3,2},{4,20},{5,4},{6,5},{7,6},{8,24},{9,8},{10... | collective-permute-start | bytes 98312 | tf_op jit(solution)/shard_map/ppermute | solution.py:491
  18.3 4.2 %collective-permute-start.10 = (f32[16,512]{1,0:T(8,128)S(1)}, f32[16,512]{1,0:T(8,128)S(1)}, u32[]{:S(2)}, u32[]{:S(2)}) collective-permute-start(f32[16,512]{1,0:T(8,128)S(1)} %get-tuple-element.48), channel_id=1, source_target_pairs={{0,16},{1,0},{2,1},{3,2},{4,20},{5,4},{6,5},{7,6},{8,24},{9,8},{10... | collective-permute-start | bytes 98312 | tf_op jit(solution)/shard_map/ppermute | solution.py:491
  22.7 1.4 %collective-permute-start.11 = (f32[4,16,512]{2,1,0:T(8,128)S(1)}, f32[4,16,512]{2,1,0:T(8,128)S(1)}, u32[]{:S(2)}, u32[]{:S(2)}) collective-permute-start(f32[4,16,512]{2,1,0:T(8,128)S(1)} %shard_map.50.part), channel_id=1, source_target_pairs={{0,16},{16,0},{1,17},{17,1},{2,18},{18,2},{3,19},{19,3},{4,20},{20... | collective-permute-start | bytes 393224 | tf_op jit(solution)/shard_map/ppermute | solution.py:476

commit v18 on v16

--- a/solution.py
+++ b/solution.py
@@ -397,13 +397,14 @@
     z_out[...] = h_out[pl.ds(jnp.where(first_core, 0, 1), zlen)]
     ups = jnp.concatenate(layers(rows, REACH), axis=0)
     downs = jnp.concatenate(layers(rows + reach, REACH), axis=0)
-    blank = jnp.zeros((y_out.shape[0] - reach - REACH, xlen), jnp.float32)
-    y_out[...] = jnp.concatenate([jnp.where(first_core, downs, ups), blank], axis=0)
-    d_out[...] = jnp.where(first_core, downs[:reach], ups[REACH:])
-    e_out[...] = jnp.where(first_core, ups[:reach], downs[REACH:])
-
-
-def layers_kernel(h, z_in, y_in, d_in, e_in, out):
+    y_out[: reach + REACH] = jnp.where(first_core, downs, ups)
+    for out, used in ((y_out, reach + REACH), (d_out, reach), (e_out, reach)):
+        out[used:] = jnp.zeros((out.shape[0] - used, xlen), jnp.float32)
+    d_out[:reach] = jnp.where(first_core, downs[:reach], ups[REACH:])
+    e_out[:reach] = jnp.where(first_core, ups[:reach], downs[REACH:])
+
+
+def layers_kernel(h, d_in, e_in, y_in, z_in, out):
     zlen, ylen, xlen = out.shape
     reach = REACH * zlen
     first_core = on_first()
@@ -535,14 +536,15 @@
             pltpu.VMEM((ylen, xlen), jnp.float32),
         ],
     )
+    sent = (-(-(reach + REACH) // TILE) * TILE, xlen)
     h, z_send, y_send, d_send, e_send = call(
         lambda *refs: total_kernel(displacements.shape, *refs),
         [
             (zlen + 1, ylen, xlen),
             (zlen, ylen, xlen),
-            (-(-(reach + REACH) // TILE) * TILE, xlen),
-            (reach, xlen),
-            (reach, xlen),
+            sent,
+            sent,
+            sent,
         ],
         (share, chip_swapped(share)),
     )
@@ -550,7 +552,7 @@
     e_in = opposed(e_send, -1, 1)
     y_in = opposed(y_send, 0, -1)
     z_in = opposed(z_send, -1, 0)
-    (part,) = call(layers_kernel, [(zlen, ylen, xlen)], (h, z_in, y_in, d_in, e_in))
+    (part,) = call(layers_kernel, [(zlen, ylen, xlen)], (h, d_in, e_in, y_in, z_in))
     (out,) = call(sum_kernel, [(zlen, ylen, xlen)], (part, chip_swapped(part)))
     return out
 

time: 22.3 us -> 22.4 us (level)
  the two profiles are of different devices: /device:TPU:11 before, /device:TPU:0 now
where the time goes in v18:
time: 22.4 us; the launch traced here: 22.3 us
  starting transfers between devices  8.81 us (39%)
  waiting for transfers between devices  7.57 us (34%)
  Pallas kernels  5.84 us (26%)
    pallas_call x6, Pallas kernels, call(): pl.pallas_call(kernel, out_shape=shapes, in_specs=[pl.BlockSpec(memory_sp...  5.84 us
    ppermute x6, starting transfers between devices, opposed(): return lax.ppermute(value, ('load', 'sy', 'sz'), pairs)  5.05 us
    ppermute x6, waiting for transfers between devices, opposed(): return lax.ppermute(value, ('load', 'sy', 'sz'), pairs)  4.94 us
    ppermute x1, starting transfers between devices, ring_moved(): return lax.ppermute(value, axis, [((k + 1) % size, k) for k in range(size)])  3.51 us
    ppermute x2, waiting for transfers between devices, chip_swapped(): lax.ppermute(value, 'load', [(core, cores - 1 - core) for core in range(c...  2.63 us
  transfers between devices with their start and end apart: 9, of which 5 were waited for; matrix products, arithmetic and copies ran while one was open for 0% of the time, Pallas kernels for 12%

profile of v18, /device:TPU:0, one launch (start us, length us, event | category | flops | bytes accessed | tf_op | source)
XLA Modules:
  0.0 22.3 jit_solution(11418394119263674043)
XLA Ops:
  0.0 1.3 %shard_map.46 = (f32[2,3,4,16,512]{4,3,2,1,0:T(8,128)S(1)}, s32[4,16,512]{2,1,0:T(8,128)S(1)}, f32[4,16,512]{2,1,0:T(8,128)S(1)}, s32[4,16,512]{2,1,0:T(8,128)S(...) custom-call(f32[2,3,4,16,512]{4,3,2,1,0:T(8,128)} %refs_0_.1, s32[4,16,512]{2,1,0:T(8,128)} %refs_1_.1, ...), custom_call_target="tpu_custom_call" | custom-call | tf_op jit(solution)/shard_map/pallas_call | solution.py:458
  1.3 0.5 %collective-permute-start.1 = (f32[7,16,512]{2,1,0:T(8,128)S(1)}, f32[7,16,512]{2,1,0:T(8,128)S(1)}, u32[]{:S(2)}, u32[]{:S(2)}) collective-permute-start(f32[7,16,512]{2,1,0:T(8,128)S(1)} %get-tuple-element.25), channel_id=1, source_target_pairs={{0,16},{1,0},{2,1},{3,2},{4,20},{5,4},{6,5},{7,6},{8,24},{9,8},{10... | collective-permute-start | bytes 688136 | tf_op jit(solution)/shard_map/ppermute | solution.py:490
  1.8 3.5 %collective-permute-start.2 = (f32[24,512]{1,0:T(8,128)S(1)}, f32[24,512]{1,0:T(8,128)S(1)}, u32[]{:S(2)}, u32[]{:S(2)}) collective-permute-start(f32[24,512]{1,0:T(8,128)S(1)} %get-tuple-element.26), channel_id=1, source_target_pairs={{4,0},{8,4},{12,8},{0,12},{5,1},{9,5},{13,9},{1,13},{6,2},{10,6},{... | collective-permute-start | bytes 147464 | tf_op jit(solution)/shard_map/ppermute | solution.py:470
  5.3 0.9 %collective-permute-start = (f32[8,512]{1,0:T(8,128)S(1)}, f32[8,512]{1,0:T(8,128)S(1)}, u32[]{:S(2)}, u32[]{:S(2)}) collective-permute-start(f32[8,512]{1,0:T(8,128)S(1)} %get-tuple-element.24), channel_id=1, source_target_pairs={{0,28},{1,12},{2,13},{3,14},{4,16},{5,0},{6,1},{7,2},{8,20},{9,4},... | collective-permute-start | bytes 49160 | tf_op jit(solution)/shard_map/ppermute | solution.py:490
  6.2 2.7 %shard_map.47 = (f32[4,16,512]{2,1,0:T(8,128)S(1)}, f32[2,24,512]{2,1,0:T(8,128)S(1)}, f32[2,9,512]{2,1,0:T(8,128)S(1)}, f32[6,16,512]{2,1,0:T(8,128)S(1)}, f32[...) custom-call(f32[2,3,4,16,512]{4,3,2,1,0:T(8,128)S(1)} %get-tuple-element.27.refs_0_, ...), custom_call_target="tpu_custom_call" | custom-call | tf_op jit(solution)/shard_map/pallas_call | solution.py:458
  8.9 1.0 %collective-permute-done.refs_0_ = f32[8,512]{1,0:T(8,128)S(1)} collective-permute-done((f32[8,512]{1,0:T(8,128)S(1)}, f32[8,512]{1,0:T(8,128)S(1)}, u32[]{:S(2)}, u32[]{:S(2)}) %collective-permute-start) | collective-permute-done | bytes 16416 | tf_op jit(solution)/shard_map/ppermute | solution.py:490
  9.9 0.0 collective-permute-done.2.refs_2_
  9.9 0.0 collective-permute-done.1.refs_1_
  10.0 1.0 %shard_map.48.refs_0_ = f32[88,512]{1,0:T(8,128)S(1)} custom-call(f32[8,512]{1,0:T(8,128)S(1)} %collective-permute-done.refs_0_, f32[7,16,512]{2,1,0:T(8,128)S(1)} %collective-permute-done.1.refs_1_, f32[24,512]{1,0:T(8,128)S(1)} %collective-permute-done.2.refs_2_, f32[4,16,512]{2,1,0:T(8,128)S(1)} %get-tuple-element.31.refs_3_, ...), custom_call_target="tpu_custom_call" | custom-call | tf_op jit(solution)/shard_map/pallas_call | solution.py:458
  11.0 0.2 collective-permute-start.3
  11.1 1.3 %collective-permute-done.3.refs_1_ = f32[88,512]{1,0:T(8,128)S(1)} collective-permute-done((f32[88,512]{1,0:T(8,128)S(1)}, f32[88,512]{1,0:T(8,128)S(1)}, u32[]{:S(2)}, u32[]{:S(2)}) %collective-permute-start.3) | collective-permute-done | bytes 180256 | tf_op jit(solution)/shard_map/ppermute | solution.py:475
  12.5 0.2 collective-permute-start.7
  12.7 1.7 %collective-permute-start.4 = (f32[16,512]{1,0:T(8,128)S(1)}, f32[16,512]{1,0:T(8,128)S(1)}, u32[]{:S(2)}, u32[]{:S(2)}) collective-permute-start(f32[16,512]{1,0:T(8,128)S(1)} %get-tuple-element.39), channel_id=1, source_target_pairs={{0,16},{1,17},{2,18},{3,19},{4,20},{5,0},{6,1},{7,2},{8,24},{9,4},... | collective-permute-start | bytes 98312 | tf_op jit(solution)/shard_map/ppermute | solution.py:490
  14.3 1.8 %collective-permute-start.5 = (f32[16,512]{1,0:T(8,128)S(1)}, f32[16,512]{1,0:T(8,128)S(1)}, u32[]{:S(2)}, u32[]{:S(2)}) collective-permute-start(f32[16,512]{1,0:T(8,128)S(1)} %get-tuple-element.40), channel_id=1, source_target_pairs={{0,16},{1,4},{2,5},{3,6},{4,20},{5,8},{6,9},{7,10},{8,24},{9,12},{... | collective-permute-start | bytes 98312 | tf_op jit(solution)/shard_map/ppermute | solution.py:490
  16.1 0.0 collective-permute-start.6
  16.1 2.6 %collective-permute-done.4.d_in = f32[16,512]{1,0:T(8,128)S(1)} collective-permute-done((f32[16,512]{1,0:T(8,128)S(1)}, f32[16,512]{1,0:T(8,128)S(1)}, u32[]{:S(2)}, u32[]{:S(2)}) %collective-permute-start.4) | collective-permute-done | bytes 32800 | tf_op jit(solution)/shard_map/ppermute | solution.py:490
  18.7 0.0 collective-permute-done.5.e_in
  18.7 1.3 %collective-permute-done.6.y_in = f32[16,512]{1,0:T(8,128)S(1)} collective-permute-done((f32[16,512]{1,0:T(8,128)S(1)}, f32[16,512]{1,0:T(8,128)S(1)}, u32[]{:S(2)}, u32[]{:S(2)}) %collective-permute-start.6) | collective-permute-done | bytes 32800 | tf_op jit(solution)/shard_map/ppermute | solution.py:490
  20.1 0.0 collective-permute-done.7.z_in
  20.1 0.1 shard_map.50.part
  20.2 0.1 collective-permute-start.8
  20.3 1.3 %collective-permute-done.8.other = f32[4,16,512]{2,1,0:T(8,128)S(1)} collective-permute-done((f32[4,16,512]{2,1,0:T(8,128)S(1)}, f32[4,16,512]{2,1,0:T(8,128)S(1)}, u32[]{:S(2)}, u32[]{:S(2)}) %collective-permute-start.8) | collective-permute-done | bytes 131104 | tf_op jit(solution)/shard_map/ppermute | solution.py:475
  21.6 0.7 %shard_map.51 = f32[4,16,512]{2,1,0:T(8,128)} custom-call(f32[4,16,512]{2,1,0:T(8,128)S(1)} %shard_map.50.part, f32[4,16,512]{2,1,0:T(8,128)S(1)} %collective-permute-done.8.other), custom_call_target="tpu_custom_call" | custom-call | tf_op jit(solution)/shard_map/pallas_call | solution.py:458
  (1 shorter events, 0.0 us)
Async XLA Ops:
  1.3 8.6 %collective-permute-start.1 = (f32[7,16,512]{2,1,0:T(8,128)S(1)}, f32[7,16,512]{2,1,0:T(8,128)S(1)}, u32[]{:S(2)}, u32[]{:S(2)}) collective-permute-start(f32[7,16,512]{2,1,0:T(8,128)S(1)} %get-tuple-element.25), channel_id=1, source_target_pairs={{0,16},{1,0},{2,1},{3,2},{4,20},{5,4},{6,5},{7,6},{8,24},{9,8},{10... | collective-permute-start | bytes 688136 | tf_op jit(solution)/shard_map/ppermute | solution.py:490
  1.8 8.1 %collective-permute-start.2 = (f32[24,512]{1,0:T(8,128)S(1)}, f32[24,512]{1,0:T(8,128)S(1)}, u32[]{:S(2)}, u32[]{:S(2)}) collective-permute-start(f32[24,512]{1,0:T(8,128)S(1)} %get-tuple-element.26), channel_id=1, source_target_pairs={{4,0},{8,4},{12,8},{0,12},{5,1},{9,5},{13,9},{1,13},{6,2},{10,6},{... | collective-permute-start | bytes 147464 | tf_op jit(solution)/shard_map/ppermute | solution.py:470
  5.3 4.6 %collective-permute-start = (f32[8,512]{1,0:T(8,128)S(1)}, f32[8,512]{1,0:T(8,128)S(1)}, u32[]{:S(2)}, u32[]{:S(2)}) collective-permute-start(f32[8,512]{1,0:T(8,128)S(1)} %get-tuple-element.24), channel_id=1, source_target_pairs={{0,28},{1,12},{2,13},{3,14},{4,16},{5,0},{6,1},{7,2},{8,20},{9,4},... | collective-permute-start | bytes 49160 | tf_op jit(solution)/shard_map/ppermute | solution.py:490
  11.0 1.5 %collective-permute-start.3 = (f32[88,512]{1,0:T(8,128)S(1)}, f32[88,512]{1,0:T(8,128)S(1)}, u32[]{:S(2)}, u32[]{:S(2)}) collective-permute-start(f32[88,512]{1,0:T(8,128)S(1)} %shard_map.48.refs_0_), channel_id=1, source_target_pairs={{0,16},{16,0},{1,17},{17,1},{2,18},{18,2},{3,19},{19,3},{4,20},{20... | collective-permute-start | bytes 540680 | tf_op jit(solution)/shard_map/ppermute | solution.py:475
  12.5 7.6 %collective-permute-start.7 = (f32[4,16,512]{2,1,0:T(8,128)S(1)}, f32[4,16,512]{2,1,0:T(8,128)S(1)}, u32[]{:S(2)}, u32[]{:S(2)}) collective-permute-start(f32[4,16,512]{2,1,0:T(8,128)S(1)} %get-tuple-element.42), channel_id=1, source_target_pairs={{0,16},{1,0},{2,1},{3,2},{4,20},{5,4},{6,5},{7,6},{8,24},{9,8},{10... | collective-permute-start | bytes 393224 | tf_op jit(solution)/shard_map/ppermute | solution.py:490
  12.7 6.1 %collective-permute-start.4 = (f32[16,512]{1,0:T(8,128)S(1)}, f32[16,512]{1,0:T(8,128)S(1)}, u32[]{:S(2)}, u32[]{:S(2)}) collective-permute-start(f32[16,512]{1,0:T(8,128)S(1)} %get-tuple-element.39), channel_id=1, source_target_pairs={{0,16},{1,17},{2,18},{3,19},{4,20},{5,0},{6,1},{7,2},{8,24},{9,4},... | collective-permute-start | bytes 98312 | tf_op jit(solution)/shard_map/ppermute | solution.py:490
  14.3 4.4 %collective-permute-start.5 = (f32[16,512]{1,0:T(8,128)S(1)}, f32[16,512]{1,0:T(8,128)S(1)}, u32[]{:S(2)}, u32[]{:S(2)}) collective-permute-start(f32[16,512]{1,0:T(8,128)S(1)} %get-tuple-element.40), channel_id=1, source_target_pairs={{0,16},{1,4},{2,5},{3,6},{4,20},{5,8},{6,9},{7,10},{8,24},{9,12},{... | collective-permute-start | bytes 98312 | tf_op jit(solution)/shard_map/ppermute | solution.py:490
  16.1 3.9 %collective-permute-start.6 = (f32[16,512]{1,0:T(8,128)S(1)}, f32[16,512]{1,0:T(8,128)S(1)}, u32[]{:S(2)}, u32[]{:S(2)}) collective-permute-start(f32[16,512]{1,0:T(8,128)S(1)} %get-tuple-element.41), channel_id=1, source_target_pairs={{0,16},{1,17},{2,18},{3,19},{4,0},{5,1},{6,2},{7,3},{8,4},{9,5},{1... | collective-permute-start | bytes 98312 | tf_op jit(solution)/shard_map/ppermute | solution.py:490
  20.2 1.4 %collective-permute-start.8 = (f32[4,16,512]{2,1,0:T(8,128)S(1)}, f32[4,16,512]{2,1,0:T(8,128)S(1)}, u32[]{:S(2)}, u32[]{:S(2)}) collective-permute-start(f32[4,16,512]{2,1,0:T(8,128)S(1)} %shard_map.50.part), channel_id=1, source_target_pairs={{0,16},{16,0},{1,17},{17,1},{2,18},{18,2},{3,19},{19,3},{4,20},{20... | collective-permute-start | bytes 393224 | tf_op jit(solution)/shard_map/ppermute | solution.py:475

commit v19 on v17

--- a/solution.py
+++ b/solution.py
@@ -183,7 +183,7 @@
     return lax.axis_index("load") == 0
 
 
-def lead_kernel(totals, disp_hbm, fixed_hbm, density_hbm, solid_hbm, disp, fixed, density, solid, d_out, z_out, y_out, sems):
+def lead_kernel(totals, disp_hbm, fixed_hbm, density_hbm, solid_hbm, disp, fixed, density, solid, z_out, y_out, sems):
     loads, comps, zlen, ylen, _ = disp.shape
     copies = [
         pltpu.make_async_copy(source, target, sems.at[k])
@@ -198,13 +198,10 @@
     gives = jnp.where(on_first(), 0, zlen - 1)
     plane = lax.axis_index("sz") * zlen + gives
     base_y = lax.axis_index("sy") * ylen
-    d_out[...] = jnp.zeros(d_out.shape, jnp.float32)
     z_out[loads * comps] = voxel_factor(density[gives], solid[gives], plane, base_y, *totals)
     for case in range(loads):
         for comp in range(comps):
-            k = case * comps + comp
-            z_out[k] = held(disp, fixed, case, comp, gives, slice(None))
-            d_out[k : k + 1] = z_out[k, :1]
+            z_out[case * comps + comp] = held(disp, fixed, case, comp, gives, slice(None))
             for z in range(zlen):
                 at = (comp * loads + case) * zlen + z
                 y_out[at : at + 1] = held(disp, fixed, case, comp, z, slice(0, 1))
@@ -291,35 +288,61 @@
         sends[1, REACH * z : REACH * (z + 1)] = ends[REACH : 2 * REACH]
 
 
-def outer_kernel(
-    shape, d_in, z_in, y_in, own_in, line, sends, last_plus, last_diff, last_factor, edge, share, plus, diff, quotient, factor
-):
+def pass_kernel(shape, y_in, d_out):
+    loads, comps, zlen, _, _ = shape
+    first_core = on_first()
+    d_out[...] = jnp.zeros(d_out.shape, jnp.float32)
+    for k in range(loads * comps):
+        at = (k % comps * loads + k // comps) * zlen
+        d_out[k : k + 1] = jnp.where(first_core, y_in[at : at + 1], y_in[at + zlen - 1 : at + zlen])
+
+
+def lines_kernel(shape, y_in, own, line, sends, edge, share):
+    loads, comps, zlen, ylen, xlen = shape
+    inner = zlen - 1
+    more = lax.axis_index("sy") < lax.axis_size("sy") - 1
+    count = loads * zlen
+    low, high = [], []
+    for comp in range(comps):
+        part = slice(comp * count, (comp + 1) * count)
+        whole, change = line[0, part], line[1, part]
+        whole_next, change_next = split_x(jnp.where(more, y_in[part], 0.0))
+        face = (whole + whole_next, change + change_next, whole_next - whole, change_next - change)
+        low.append(face)
+        high.append([pltpu.roll(value, count - 1, 0) for value in face])
+    energy = quadratic(low, high, mode_weights())
+    energy = sum(energy[case * zlen : case * zlen + inner] for case in range(loads)) * edge[:inner]
+    last = spread_x(jnp.concatenate([energy, jnp.zeros((TILE - inner, xlen), jnp.float32)], axis=0))
+
+    row = lax.broadcasted_iota(jnp.int32, (TILE, xlen), 0)
+    rising = jnp.maximum(row - (TILE - 1 - ROWS), 0).astype(jnp.float32)
+    ups, downs = [], []
+    for z in range(inner):
+        share[ylen * z : ylen * (z + 1)] = own[z]
+        share[ylen * (z + 1) - TILE : ylen * (z + 1)] += rising * last[z : z + 1]
+        here = sends[0, REACH * z : REACH * (z + 1)]
+        ups += [here[r : r + 1] + float(REACH - r) * last[z : z + 1] for r in range(REACH)]
+        downs.append(sends[1, REACH * z : REACH * (z + 1)])
+    share[ylen * inner :] = jnp.concatenate(ups + downs, axis=0)
+
+
+def outer_kernel(shape, z_in, last_plus, last_diff, last_factor, own, ends, corner, plus, diff, quotient, factor):
     loads, comps, zlen, ylen, xlen = shape
     planes = loads * comps
-    inner = zlen - 1
     first_core, index = on_first(), lax.axis_index("sz")
     top = first_core & (index == lax.axis_size("sz") - 1)
-    more = lax.axis_index("sy") < lax.axis_size("sy") - 1
     stays, comes = jnp.where(first_core, 0, 1), jnp.where(first_core, jnp.where(top, 2, 1), 0)
-    y_rows = jnp.where(more, y_in[...], 0.0)
-    y_plus, y_diff = split_x(y_rows)
-    d_plus, d_diff = split_x(jnp.where(more, d_in[...], 0.0))
     for k in range(planes):
-        case, comp = k // comps, k % comps
-        at = (comp * loads + case) * zlen
-        beside = jnp.where(first_core, y_plus[at + inner : at + zlen], y_plus[at : at + 1])
-        beside_diff = jnp.where(first_core, y_diff[at + inner : at + zlen], y_diff[at : at + 1])
         plus[k, stays, :ylen] = last_plus[k]
         diff[k, stays, :ylen] = last_diff[k]
-        plus[k, stays, ylen : ylen + 1] = beside
-        diff[k, stays, ylen : ylen + 1] = beside_diff
         whole, change = split_x(z_in[k])
         plus[k, comes, :ylen] = whole
         diff[k, comes, :ylen] = change
-        plus[k, comes, ylen : ylen + 1] = d_plus[k : k + 1]
-        diff[k, comes, ylen : ylen + 1] = d_diff[k : k + 1]
+        for group, value in enumerate((last_plus[k, ylen - 1 :], last_diff[k, ylen - 1 :], whole[ylen - 1 :], change[ylen - 1 :])):
+            corner[group, k : k + 1] = value
     below = jnp.where(index > 0, z_in[planes], 0.0)
     factor[...] = jnp.where(first_core, last_factor[...], below)
+    corner[0, planes : planes + 1] = factor[ylen - 1 :]
 
     @pl.when(top)
     def _():
@@ -338,7 +361,8 @@
         def _(chunk):
             lanes = pl.ds(pl.multiple_of(chunk * LANES, LANES), LANES)
             (energy,) = tile_energies(plus, diff, first, lanes, 1, loads, comps)
-            quotient[first + TILE : first + 2 * TILE, lanes] = energy * factor[first : first + TILE, lanes]
+            here = energy * factor[first : first + TILE, lanes]
+            quotient[first + TILE : first + 2 * TILE, lanes] = blank_last(here, first, ylen)
 
     @pl.when(top)
     def _():
@@ -348,83 +372,98 @@
             def _(chunk):
                 lanes = pl.ds(pl.multiple_of(chunk * LANES, LANES), LANES)
                 (energy,) = tile_energies(plus, diff, first, lanes, 1, loads, comps, base=2)
-                quotient[first + TILE : first + 2 * TILE, lanes] += energy * factor[first : first + TILE, lanes]
-
-    count = loads * zlen
+                here = energy * factor[first : first + TILE, lanes]
+                quotient[first + TILE : first + 2 * TILE, lanes] += blank_last(here, first, ylen)
+
+    own[...] = spread_x(spread_y(quotient, ylen))
+    ahead, back = to_neighbours(quotient, ylen)
+    ends[...] = spread_x(jnp.concatenate(ahead + back + [zeros[: TILE - 2 * REACH]], axis=0))
+
+
+def corner_line(shape, corner, y_in, d_in):
+    loads, comps, zlen, ylen, xlen = shape
+    planes = loads * comps
+    first_core = on_first()
+    top = first_core & (lax.axis_index("sz") == lax.axis_size("sz") - 1)
+    more = lax.axis_index("sy") < lax.axis_size("sy") - 1
+    rows = []
+    for k in range(planes):
+        at = (k % comps * loads + k // comps) * zlen
+        rows.append(jnp.where(first_core, y_in[at + zlen - 1 : at + zlen], y_in[at : at + 1]))
+    rows.append(jnp.zeros((-planes % TILE, xlen), jnp.float32))
+    stays_next = split_x(jnp.where(more, jnp.concatenate(rows, axis=0), 0.0))
+    comes_next = split_x(jnp.where(more, d_in[...], 0.0))
+
+    def faces(stays, comes, comp):
+        zero = jnp.zeros((1, xlen), jnp.float32)
+        under, over = [], []
+        for own, other in zip(stays, comes):
+            own, other = ([value[case * comps + comp : case * comps + comp + 1] for case in range(loads)] for value in (own, other))
+            low = [jnp.where(first_core, a, b) for a, b in zip(own, other)] + [jnp.where(top, b, 0.0) for b in other]
+            high = [jnp.where(first_core, jnp.where(top, 0.0, b), a) for a, b in zip(own, other)] + [zero] * loads
+            under.append(jnp.concatenate(low, axis=0))
+            over.append(jnp.concatenate(high, axis=0))
+        return under, over
+
     low, high = [], []
     for comp in range(comps):
-        part = slice(comp * count, (comp + 1) * count)
-        whole, change = line[0, part], line[1, part]
-        whole_next, change_next = y_plus[part], y_diff[part]
-        face = (whole + whole_next, change + change_next, whole_next - whole, change_next - change)
-        low.append(face)
-        high.append([pltpu.roll(value, count - 1, 0) for value in face])
+        near = faces((corner[0], corner[1]), (corner[2], corner[3]), comp)
+        far = faces(stays_next, comes_next, comp)
+        for (whole, change), (whole_next, change_next), into in zip(near, far, (low, high)):
+            into.append((whole + whole_next, change + change_next, whole_next - whole, change_next - change))
     energy = quadratic(low, high, mode_weights())
-    energy = sum(energy[case * zlen : case * zlen + inner] for case in range(loads)) * edge[:inner]
-    last = spread_x(jnp.concatenate([energy, jnp.zeros((TILE - inner, xlen), jnp.float32)], axis=0))
-
+    line = sum(energy[case : case + 1] for case in range(2 * loads)) * corner[0, planes : planes + 1]
+    return spread_x(jnp.concatenate([line, jnp.zeros((TILE - 1, xlen), jnp.float32)], axis=0))[:1]
+
+
+def total_kernel(shape, share, other, own, ends, corner, y_in, d_in, h_out, d_out, e_out, y_out, z_out, i_out):
+    _, _, zlen, ylen, xlen = shape
+    inner = zlen - 1
+    first_core = on_first()
+    line = corner_line(shape, corner, y_in, d_in)
     row = lax.broadcasted_iota(jnp.int32, (TILE, xlen), 0)
     rising = jnp.maximum(row - (TILE - 1 - ROWS), 0).astype(jnp.float32)
-    ups, downs = [], []
     for z in range(inner):
-        share[ylen * z : ylen * (z + 1)] = own_in[z]
-        share[ylen * (z + 1) - TILE : ylen * (z + 1)] += rising * last[z : z + 1]
-        here = sends[0, REACH * z : REACH * (z + 1)]
-        ups += [here[r : r + 1] + float(REACH - r) * last[z : z + 1] for r in range(REACH)]
-        downs.append(sends[1, REACH * z : REACH * (z + 1)])
-    share[ylen * inner : ylen * zlen] = spread_x(spread_y(quotient, ylen))
-    ahead, back = to_neighbours(quotient, ylen)
-    ends = spread_x(jnp.concatenate(ahead + back + [zeros[:2]], axis=0))
-    share[ylen * zlen :] = jnp.concatenate(ups + [ends[:REACH]] + downs + [ends[REACH : 2 * REACH]], axis=0)
-
-
-def total_kernel(shape, share, other, h_out, d_out, e_out, y_out, *z_outs):
-    _, _, zlen, ylen, xlen = shape
-    first_core = on_first()
-    inner, rows = zlen - 1, ylen * zlen
-    reach = REACH * zlen
-
-    def layers(first, count):
-        mine, theirs = share[first + inner * count : first + zlen * count], other[first + inner * count : first + zlen * count]
-        middle = share[first : first + inner * count] + other[first : first + inner * count]
-        return jnp.where(first_core, theirs, mine), middle, jnp.where(first_core, mine, theirs)
-
-    lowest, middle, highest = layers(0, ylen)
-    h_out[0] = lowest
+        h_out[z] = share[ylen * z : ylen * (z + 1)] + other[ylen * z : ylen * (z + 1)]
+    h_out[inner] = own[...]
+    h_out[inner, ylen - TILE :] += rising * line
+    shift = jnp.where(first_core, 0, 1)
     for z in range(inner):
-        h_out[z + 1] = middle[ylen * z : ylen * (z + 1)]
-    h_out[zlen] = highest
-    for k, z_out in enumerate(z_outs):
-        z_out[...] = h_out[jnp.where(first_core, k, k + 1)]
-    ups = jnp.concatenate(layers(rows, REACH), axis=0)
-    downs = jnp.concatenate(layers(rows + reach, REACH), axis=0)
-    y_out[: reach + REACH] = jnp.where(first_core, downs, ups)
-    for out, used in ((y_out, reach + REACH), (d_out, reach), (e_out, reach)):
+        z_out[z + shift] = h_out[z]
+    z_out[jnp.where(first_core, inner, 0)] = h_out[inner]
+    first, reach = ylen * inner, REACH * inner
+    ups, downs = (share[at : at + reach] + other[at : at + reach] for at in (first, first + reach))
+    weights = jnp.maximum(REACH - lax.broadcasted_iota(jnp.int32, (REACH, xlen), 0), 0).astype(jnp.float32)
+    between_ups, between_downs = ends[:REACH] + weights * line, ends[REACH : 2 * REACH]
+
+    def stacked(rows, between):
+        return jnp.where(first_core, jnp.concatenate([rows, between], axis=0), jnp.concatenate([between, rows], axis=0))
+
+    used = reach + REACH
+    all_ups, all_downs = stacked(ups, between_ups), stacked(downs, between_downs)
+    y_out[:used] = jnp.where(first_core, all_downs, all_ups)
+    d_out[:used] = jnp.where(first_core, all_ups, all_downs)
+    e_out[:used] = jnp.where(first_core, all_downs, all_ups)
+    for out in (y_out, d_out, e_out):
         out[used:] = jnp.zeros((out.shape[0] - used, xlen), jnp.float32)
-    d_out[:reach] = jnp.where(first_core, downs[:reach], ups[REACH:])
-    e_out[:reach] = jnp.where(first_core, ups[:reach], downs[REACH:])
-
-
-def layers_kernel(h, d_in, e_in, y_in, *rest):
-    *z_in, out = rest
+    i_out[:REACH] = jnp.where(first_core, between_ups, between_downs)
+    i_out[REACH:] = jnp.zeros((i_out.shape[0] - REACH, xlen), jnp.float32)
+
+
+def layers_kernel(h, d_in, e_in, y_in, z_in, i_in, out):
     zlen, ylen, xlen = out.shape
+    inner = zlen - 1
     first_core = on_first()
     z_index, z_last = lax.axis_index("sz"), lax.axis_size("sz") - 1
     y_index, y_last = lax.axis_index("sy"), lax.axis_size("sy") - 1
-    z_side = jnp.where(first_core, z_index < z_last, z_index > 0)
-    y_side = jnp.where(first_core, y_index < y_last, y_index > 0)
-    y_other = jnp.where(first_core, y_index > 0, y_index < y_last)
+    not_first, not_last = y_index > 0, y_index < y_last
+    z_side = jnp.where(first_core, z_index > 0, z_index < z_last)
     blank = jnp.zeros((TILE - REACH, xlen), jnp.float32)
-
-    def at_start(rows):
-        return jnp.concatenate([rows, blank], axis=0)
-
-    def at_end(rows):
-        return jnp.concatenate([blank, rows], axis=0)
 
     def ends(rows, keep, at_last):
         rows = jnp.where(keep, rows, 0.0)
-        return at_start(jnp.where(at_last, 0.0, rows)), at_end(jnp.where(at_last, rows, 0.0))
+        at_start, at_end = jnp.where(at_last, 0.0, rows), jnp.where(at_last, rows, 0.0)
+        return jnp.concatenate([at_start, blank], axis=0), jnp.concatenate([blank, at_end], axis=0)
 
     def with_ends(layer, *pairs):
         head, tail = layer[:TILE], layer[ylen - TILE :]
@@ -432,19 +471,27 @@
             head, tail = head + first, tail + last
         return jnp.concatenate([head, layer[TILE : ylen - TILE], tail] if ylen > 2 * TILE else [head, tail], axis=0)
 
-    own = []
-    for k in range(zlen + 1):
-        layer = jnp.where(first_core, h[k], 0.0)
-        own.append(with_ends(layer, ends(y_in[REACH * k : REACH * (k + 1)], y_side, first_core)))
-    come = []
+    second_core = jnp.logical_not(first_core)
+    y_side = jnp.where(first_core, not_last, not_first)
+    y_other = jnp.where(first_core, not_first, not_last)
+    own, come = [], []
     for k in range(zlen):
         part = slice(REACH * k, REACH * (k + 1))
-        layer = jnp.where(z_side, z_in[k][...], 0.0)
-        straight = ends(d_in[part], z_side & y_side, first_core)
-        across = ends(e_in[part], z_side & y_other, jnp.logical_not(first_core))
-        come.append(with_ends(layer, straight, across))
-    below = [jnp.where(first_core, 0.0, layer) for layer in come[zlen - REACH :]]
-    above = [jnp.where(first_core, layer, 0.0) for layer in come]
+        at = jnp.where(first_core, k, k - 1 if k else inner)
+        layer = h[at]
+        keep = first_core | (k == 0)
+        pairs = [ends(y_in[part], y_side, first_core)]
+        if k in (0, inner):
+            between = first_core if k else second_core
+            pairs.append(ends(i_in[:REACH], y_other & between, second_core))
+        own.append(with_ends(jnp.where(keep, layer, 0.0), *pairs))
+        straight = ends(d_in[part], z_side & jnp.where(first_core, not_first, not_last), second_core)
+        across = ends(e_in[part], z_side & jnp.where(first_core, not_last, not_first), first_core)
+        come.append(with_ends(jnp.where(z_side, z_in[k], 0.0), straight, across))
+    zero = jnp.zeros((ylen, xlen), jnp.float32)
+    own = [jnp.where(first_core, a, b) for a, b in zip([zero] + own, own + [zero])]
+    below = [jnp.where(first_core, layer, 0.0) for layer in come[zlen - REACH :]]
+    above = [jnp.where(first_core, 0.0, layer) for layer in come]
     layers = below[:-1] + [below[-1] + own[0]] + own[1:-1] + [own[-1] + above[0]] + above[1:]
     for z, layer in enumerate(spread_layers(layers)):
         out[z] = layer
@@ -476,7 +523,7 @@
     return lax.ppermute(value, "load", [(core, cores - 1 - core) for core in range(cores)])
 
 
-def opposed(value, z_step, y_step, y_shift=0):
+def opposed(value, z_step, y_step):
     cores, rows, size = lax.axis_size("load"), lax.axis_size("sy"), lax.axis_size("sz")
     pairs = []
     for core in range(cores):
@@ -486,7 +533,6 @@
                 to_y, to_z, side = y + sign * y_step, z + sign * z_step, core
                 if not (0 <= to_y < rows and 0 <= to_z < size):
                     to_y, to_z, side = y, z, cores - 1 - core
-                to_y = (to_y + y_shift) % rows
                 pairs.append(((core * rows + y) * size + z, (side * rows + to_y) * size + to_z))
     return lax.ppermute(value, ("load", "sy", "sz"), pairs)
 
@@ -499,15 +545,14 @@
         pltpu.with_memory_space_constraint(arg, pltpu.HBM) for arg in (displacements, fixed, density, solid)
     ]
 
-    disp, fixed, density, solid, d_send, z_send, y_send = call(
+    disp, fixed, density, solid, z_send, y_send = call(
         lambda *refs: lead_kernel(totals, *refs),
         [jax.ShapeDtypeStruct(arg.shape, arg.dtype) for arg in args]
-        + [(-(-planes // TILE) * TILE, xlen), (planes + 1, ylen, xlen), (planes * zlen, xlen)],
+        + [(planes + 1, ylen, xlen), (planes * zlen, xlen)],
         args,
         scratch=[pltpu.SemaphoreType.DMA((len(args),))],
         space=pltpu.HBM,
     )
-    d_in = opposed(d_send, -1, 0, y_shift=-1)
     z_in = opposed(z_send, -1, 0)
     y_in = ring_moved(y_send, "sy")
     nodes = lambda layers: pltpu.VMEM((planes, layers, ylen + TILE, xlen), jnp.float32)
@@ -525,11 +570,20 @@
         (disp, fixed, density, solid),
         scratch=[nodes(zlen), nodes(zlen), pltpu.VMEM((zlen - 1, ylen + 2 * TILE, xlen), jnp.float32)],
     )
-    reach = REACH * zlen
+    own, line, sends, last_plus, last_diff, last_factor, edge = inner
+    shape = displacements.shape
+    padded = -(-(planes + 1) // TILE) * TILE
+    (d_send,) = call(lambda *refs: pass_kernel(shape, *refs), [(-(-planes // TILE) * TILE, xlen)], (y_in,))
+    d_in = opposed(d_send, -1, 0)
     (share,) = call(
-        lambda *refs: outer_kernel(displacements.shape, *refs),
-        [(ylen * zlen + 2 * reach, xlen)],
-        (d_in, z_in, y_in, *inner),
+        lambda *refs: lines_kernel(shape, *refs),
+        [((zlen - 1) * (ylen + 2 * REACH), xlen)],
+        (y_in, own, line, sends, edge),
+    )
+    own, ends, corner = call(
+        lambda *refs: outer_kernel(shape, *refs),
+        [(ylen, xlen), (TILE, xlen), (4, padded, xlen)],
+        (z_in, last_plus, last_diff, last_factor),
         scratch=[
             nodes(4),
             nodes(4),
@@ -537,17 +591,18 @@
             pltpu.VMEM((ylen, xlen), jnp.float32),
         ],
     )
-    sent = (-(-(reach + REACH) // TILE) * TILE, xlen)
-    h, d_send, e_send, y_send, *z_sends = call(
-        lambda *refs: total_kernel(displacements.shape, *refs),
-        [(zlen + 1, ylen, xlen)] + 3 * [sent] + zlen * [(ylen, xlen)],
-        (share, chip_swapped(share)),
-    )
-    d_in = opposed(d_send, -1, -1)
-    e_in = opposed(e_send, -1, 1)
+    sent = (-(-REACH * zlen // TILE) * TILE, xlen)
+    h, d_send, e_send, y_send, z_send, i_send = call(
+        lambda *refs: total_kernel(shape, *refs),
+        [(zlen, ylen, xlen), sent, sent, sent, (zlen, ylen, xlen), (TILE, xlen)],
+        (share, chip_swapped(share), own, ends, corner, y_in, d_in),
+    )
+    d_in = opposed(d_send, 1, 1)
+    e_in = opposed(e_send, 1, -1)
     y_in = opposed(y_send, 0, -1)
-    z_in = [opposed(z_send, -1, 0) for z_send in z_sends]
-    (part,) = call(layers_kernel, [(zlen, ylen, xlen)], (h, d_in, e_in, y_in, *z_in))
+    z_in = opposed(z_send, 1, 0)
+    i_in = opposed(i_send, 0, 1)
+    (part,) = call(layers_kernel, [(zlen, ylen, xlen)], (h, d_in, e_in, y_in, z_in, i_in))
     (out,) = call(sum_kernel, [(zlen, ylen, xlen)], (part, chip_swapped(part)))
     return out
 

time: 24.9 us -> 24.4 us (0.980)
  the two profiles are of different devices: /device:TPU:0 before, /device:TPU:5 now
where the time goes in v19:
time: 24.4 us; the launch traced here: 24.2 us
  starting transfers between devices  15.6 us (64%)
  Pallas kernels  6.27 us (26%)
  waiting for transfers between devices  2.3 us (9%)
    ppermute x7, starting transfers between devices, opposed(): return lax.ppermute(value, ('load', 'sy', 'sz'), pairs)  11.7 us
    pallas_call x8, Pallas kernels, call(): pl.pallas_call(kernel, out_shape=shapes, in_specs=[pl.BlockSpec(memory_sp...  6.27 us
    ppermute x2, starting transfers between devices, chip_swapped(): lax.ppermute(value, 'load', [(core, cores - 1 - core) for core in range(c...  2.72 us
    ppermute x7, waiting for transfers between devices, opposed(): return lax.ppermute(value, ('load', 'sy', 'sz'), pairs)  1.3 us
    ppermute x1, starting transfers between devices, ring_moved(): return lax.ppermute(value, axis, [((k + 1) % size, k) for k in range(size)])  1.15 us
    ppermute x2, waiting for transfers between devices, chip_swapped(): lax.ppermute(value, 'load', [(core, cores - 1 - core) for core in range(c...  0.99 us
  transfers between devices with their start and end apart: 10, of which 3 were waited for; matrix products, arithmetic and copies ran while one was open for 0% of the time, Pallas kernels for 16%

profile of v19, /device:TPU:5, one launch (start us, length us, event | category | flops | bytes accessed | tf_op | source)
XLA Modules:
  0.0 24.2 jit_solution(10589230662784709688)
XLA Ops:
  0.0 1.3 %shard_map.46 = (f32[2,3,4,16,512]{4,3,2,1,0:T(8,128)S(1)}, s32[4,16,512]{2,1,0:T(8,128)S(1)}, f32[4,16,512]{2,1,0:T(8,128)S(1)}, s32[4,16,512]{2,1,0:T(8,128)S(...) custom-call(f32[2,3,4,16,512]{4,3,2,1,0:T(8,128)} %refs_0_.1, s32[4,16,512]{2,1,0:T(8,128)} %refs_1_.1, ...), custom_call_target="tpu_custom_call" | custom-call | tf_op jit(solution)/shard_map/pallas_call | solution.py:506
  1.3 1.3 %collective-permute-start.2 = (f32[7,16,512]{2,1,0:T(8,128)S(1)}, f32[7,16,512]{2,1,0:T(8,128)S(1)}, u32[]{:S(2)}, u32[]{:S(2)}) collective-permute-start(f32[7,16,512]{2,1,0:T(8,128)S(1)} %get-tuple-element.36), channel_id=1, source_target_pairs={{0,16},{1,0},{2,1},{3,2},{4,20},{5,4},{6,5},{7,6},{8,24},{9,8},{10... | collective-permute-start | bytes 688136 | tf_op jit(solution)/shard_map/ppermute | solution.py:537
  2.6 1.2 %collective-permute-start = (f32[24,512]{1,0:T(8,128)S(1)}, f32[24,512]{1,0:T(8,128)S(1)}, u32[]{:S(2)}, u32[]{:S(2)}) collective-permute-start(f32[24,512]{1,0:T(8,128)S(1)} %get-tuple-element.27), channel_id=1, source_target_pairs={{4,0},{8,4},{12,8},{0,12},{5,1},{9,5},{13,9},{1,13},{6,2},{10,6},{... | collective-permute-start | bytes 147464 | tf_op jit(solution)/shard_map/ppermute | solution.py:518
  3.8 2.7 %shard_map.47 = (f32[4,16,512]{2,1,0:T(8,128)S(1)}, f32[2,24,512]{2,1,0:T(8,128)S(1)}, f32[2,9,512]{2,1,0:T(8,128)S(1)}, f32[6,16,512]{2,1,0:T(8,128)S(1)}, f32[...) custom-call(f32[2,3,4,16,512]{4,3,2,1,0:T(8,128)S(1)} %get-tuple-element.28.refs_0_, ...), custom_call_target="tpu_custom_call" | custom-call | tf_op jit(solution)/shard_map/pallas_call | solution.py:506
  6.5 0.0 collective-permute-done.refs_0_.refs_5_
  6.5 0.3 %shard_map.48.refs_0_ = f32[66,512]{1,0:T(8,128)S(1)} custom-call(f32[24,512]{1,0:T(8,128)S(1)} %collective-permute-done.refs_0_.refs_5_, f32[4,16,512]{2,1,0:T(8,128)S(1)} %get-tuple-element.32.refs_1_, f32[2,24,512]{2,1,0:T(8,128)S(1)} %get-tuple-element.33.refs_2_, f32[2,9,512]{2,1,0:T(8,128)S(1)} %get-tuple-element.34.refs_3_, ...), custom_call_target="tpu_custom_call" | custom-call | tf_op jit(solution)/shard_map/pallas_call | solution.py:506
  6.7 0.2 collective-permute-start.1
  6.9 1.5 %collective-permute-start.3 = (f32[8,512]{1,0:T(8,128)S(1)}, f32[8,512]{1,0:T(8,128)S(1)}, u32[]{:S(2)}, u32[]{:S(2)}) collective-permute-start(f32[8,512]{1,0:T(8,128)S(1)} %shard_map.50), channel_id=1, source_target_pairs={{0,16},{1,0},{2,1},{3,2},{4,20},{5,4},{6,5},{7,6},{8,24},{9,8},{10... | collective-permute-start | bytes 49160 | tf_op jit(solution)/shard_map/ppermute | solution.py:537
  8.4 0.0 collective-permute-done.2.refs_0_
  8.4 0.9 %shard_map.49 = (f32[16,512]{1,0:T(8,128)S(1)}, f32[8,512]{1,0:T(8,128)S(1)}, f32[4,8,512]{2,1,0:T(8,128)S(1)}) custom-call(f32[7,16,512]{2,1,0:T(8,128)S(1)} %collective-permute-done.2.refs_0_, f32[6,16,512]{2,1,0:T(8,128)S(1)} %get-tuple-element.37.refs_1_, f32[6,16,512]{2,1,0:T(8,128)S(1)} %get-tuple-element.38.refs_2_, ...), custom_call_target="tpu_custom_call" | custom-call | tf_op jit(solution)/shard_map/pallas_call | solution.py:506
  9.4 0.0 collective-permute-done.3.refs_6_
  9.4 0.0 collective-permute-done.1.refs_1_
  9.4 0.3 %shard_map.51 = (f32[4,16,512]{2,1,0:T(8,128)S(1)}, f32[16,512]{1,0:T(8,128)S(1)}, f32[16,512]{1,0:T(8,128)S(1)}, f32[16,512]{1,0:T(8,128)S(1)}, f32[4,16,512]{2,1,0:T(8,128)S(1)}, /*index=5*/f32[8,512]{1,0:T(8,128)S(1)}) custom-call(f32[66,512]{1,0:T(8,128)S(1)} %shard_map.48.refs_0_, f32[66,512]{1,0:T(8,128)S(1)} %collective-permute-done.1.refs_1_, ...), custom_call_target="tpu_custom_call" | custom-call | tf_op jit(solution)/shard_map/pallas_call | solution.py:506
  9.7 1.7 %collective-permute-start.7 = (f32[4,16,512]{2,1,0:T(8,128)S(1)}, f32[4,16,512]{2,1,0:T(8,128)S(1)}, u32[]{:S(2)}, u32[]{:S(2)}) collective-permute-start(f32[4,16,512]{2,1,0:T(8,128)S(1)} %get-tuple-element.47), channel_id=1, source_target_pairs={{0,1},{1,2},{2,3},{3,19},{4,5},{5,6},{6,7},{7,23},{8,9},{9,10},{10... | collective-permute-start | bytes 393224 | tf_op jit(solution)/shard_map/ppermute | solution.py:537
  11.4 1.6 %collective-permute-start.4 = (f32[16,512]{1,0:T(8,128)S(1)}, f32[16,512]{1,0:T(8,128)S(1)}, u32[]{:S(2)}, u32[]{:S(2)}) collective-permute-start(f32[16,512]{1,0:T(8,128)S(1)} %get-tuple-element.44), channel_id=1, source_target_pairs={{0,5},{1,6},{2,7},{3,19},{4,9},{5,10},{6,11},{7,23},{8,13},{9,14},... | collective-permute-start | bytes 98312 | tf_op jit(solution)/shard_map/ppermute | solution.py:537
  13.0 3.2 %collective-permute-start.5 = (f32[16,512]{1,0:T(8,128)S(1)}, f32[16,512]{1,0:T(8,128)S(1)}, u32[]{:S(2)}, u32[]{:S(2)}) collective-permute-start(f32[16,512]{1,0:T(8,128)S(1)} %get-tuple-element.45), channel_id=1, source_target_pairs={{0,16},{1,17},{2,18},{3,19},{4,1},{5,2},{6,3},{7,23},{8,5},{9,6},{... | collective-permute-start | bytes 98312 | tf_op jit(solution)/shard_map/ppermute | solution.py:537
  16.2 0.0 collective-permute-start.6
  16.2 2.4 %collective-permute-start.8 = (f32[8,512]{1,0:T(8,128)S(1)}, f32[8,512]{1,0:T(8,128)S(1)}, u32[]{:S(2)}, u32[]{:S(2)}) collective-permute-start(f32[8,512]{1,0:T(8,128)S(1)} %get-tuple-element.48), channel_id=1, source_target_pairs={{0,4},{1,5},{2,6},{3,7},{4,8},{5,9},{6,10},{7,11},{8,12},{9,13},{1... | collective-permute-start | bytes 49160 | tf_op jit(solution)/shard_map/ppermute | solution.py:537
  18.6 0.9 %collective-permute-done.8.i_in = f32[8,512]{1,0:T(8,128)S(1)} collective-permute-done((f32[8,512]{1,0:T(8,128)S(1)}, f32[8,512]{1,0:T(8,128)S(1)}, u32[]{:S(2)}, u32[]{:S(2)}) %collective-permute-start.8) | collective-permute-done | bytes 16416 | tf_op jit(solution)/shard_map/ppermute | solution.py:537
  19.4 0.0 collective-permute-done.4.d_in
  19.4 0.0 collective-permute-done.5.e_in
  19.4 0.4 %collective-permute-done.6.y_in = f32[16,512]{1,0:T(8,128)S(1)} collective-permute-done((f32[16,512]{1,0:T(8,128)S(1)}, f32[16,512]{1,0:T(8,128)S(1)}, u32[]{:S(2)}, u32[]{:S(2)}) %collective-permute-start.6) | collective-permute-done | bytes 32800 | tf_op jit(solution)/shard_map/ppermute | solution.py:537
  19.9 0.0 collective-permute-done.7.z_in
  19.9 0.1 shard_map.52.part
  20.0 2.5 %collective-permute-start.9 = (f32[4,16,512]{2,1,0:T(8,128)S(1)}, f32[4,16,512]{2,1,0:T(8,128)S(1)}, u32[]{:S(2)}, u32[]{:S(2)}) collective-permute-start(f32[4,16,512]{2,1,0:T(8,128)S(1)} %shard_map.52.part), channel_id=1, source_target_pairs={{0,16},{16,0},{1,17},{17,1},{2,18},{18,2},{3,19},{19,3},{4,20},{20... | collective-permute-start | bytes 393224 | tf_op jit(solution)/shard_map/ppermute | solution.py:523
  22.6 1.0 %collective-permute-done.9.other = f32[4,16,512]{2,1,0:T(8,128)S(1)} collective-permute-done((f32[4,16,512]{2,1,0:T(8,128)S(1)}, f32[4,16,512]{2,1,0:T(8,128)S(1)}, u32[]{:S(2)}, u32[]{:S(2)}) %collective-permute-start.9) | collective-permute-done | bytes 131104 | tf_op jit(solution)/shard_map/ppermute | solution.py:523
  23.5 0.7 %shard_map.53 = f32[4,16,512]{2,1,0:T(8,128)} custom-call(f32[4,16,512]{2,1,0:T(8,128)S(1)} %shard_map.52.part, f32[4,16,512]{2,1,0:T(8,128)S(1)} %collective-permute-done.9.other), custom_call_target="tpu_custom_call" | custom-call | tf_op jit(solution)/shard_map/pallas_call | solution.py:506
  (1 shorter events, 0.0 us)
Async XLA Ops:
  1.3 7.1 %collective-permute-start.2 = (f32[7,16,512]{2,1,0:T(8,128)S(1)}, f32[7,16,512]{2,1,0:T(8,128)S(1)}, u32[]{:S(2)}, u32[]{:S(2)}) collective-permute-start(f32[7,16,512]{2,1,0:T(8,128)S(1)} %get-tuple-element.36), channel_id=1, source_target_pairs={{0,16},{1,0},{2,1},{3,2},{4,20},{5,4},{6,5},{7,6},{8,24},{9,8},{10... | collective-permute-start | bytes 688136 | tf_op jit(solution)/shard_map/ppermute | solution.py:537
  2.6 3.8 %collective-permute-start = (f32[24,512]{1,0:T(8,128)S(1)}, f32[24,512]{1,0:T(8,128)S(1)}, u32[]{:S(2)}, u32[]{:S(2)}) collective-permute-start(f32[24,512]{1,0:T(8,128)S(1)} %get-tuple-element.27), channel_id=1, source_target_pairs={{4,0},{8,4},{12,8},{0,12},{5,1},{9,5},{13,9},{1,13},{6,2},{10,6},{... | collective-permute-start | bytes 147464 | tf_op jit(solution)/shard_map/ppermute | solution.py:518
  6.7 2.6 %collective-permute-start.1 = (f32[66,512]{1,0:T(8,128)S(1)}, f32[66,512]{1,0:T(8,128)S(1)}, u32[]{:S(2)}, u32[]{:S(2)}) collective-permute-start(f32[66,512]{1,0:T(8,128)S(1)} %shard_map.48.refs_0_), channel_id=1, source_target_pairs={{0,16},{16,0},{1,17},{17,1},{2,18},{18,2},{3,19},{19,3},{4,20},{20... | collective-permute-start | bytes 405512 | tf_op jit(solution)/shard_map/ppermute | solution.py:523
  6.9 2.4 %collective-permute-start.3 = (f32[8,512]{1,0:T(8,128)S(1)}, f32[8,512]{1,0:T(8,128)S(1)}, u32[]{:S(2)}, u32[]{:S(2)}) collective-permute-start(f32[8,512]{1,0:T(8,128)S(1)} %shard_map.50), channel_id=1, source_target_pairs={{0,16},{1,0},{2,1},{3,2},{4,20},{5,4},{6,5},{7,6},{8,24},{9,8},{10... | collective-permute-start | bytes 49160 | tf_op jit(solution)/shard_map/ppermute | solution.py:537
  9.7 10.2 %collective-permute-start.7 = (f32[4,16,512]{2,1,0:T(8,128)S(1)}, f32[4,16,512]{2,1,0:T(8,128)S(1)}, u32[]{:S(2)}, u32[]{:S(2)}) collective-permute-start(f32[4,16,512]{2,1,0:T(8,128)S(1)} %get-tuple-element.47), channel_id=1, source_target_pairs={{0,1},{1,2},{2,3},{3,19},{4,5},{5,6},{6,7},{7,23},{8,9},{9,10},{10... | collective-permute-start | bytes 393224 | tf_op jit(solution)/shard_map/ppermute | solution.py:537
  11.4 8.0 %collective-permute-start.4 = (f32[16,512]{1,0:T(8,128)S(1)}, f32[16,512]{1,0:T(8,128)S(1)}, u32[]{:S(2)}, u32[]{:S(2)}) collective-permute-start(f32[16,512]{1,0:T(8,128)S(1)} %get-tuple-element.44), channel_id=1, source_target_pairs={{0,5},{1,6},{2,7},{3,19},{4,9},{5,10},{6,11},{7,23},{8,13},{9,14},... | collective-permute-start | bytes 98312 | tf_op jit(solution)/shard_map/ppermute | solution.py:537
  13.0 6.5 %collective-permute-start.5 = (f32[16,512]{1,0:T(8,128)S(1)}, f32[16,512]{1,0:T(8,128)S(1)}, u32[]{:S(2)}, u32[]{:S(2)}) collective-permute-start(f32[16,512]{1,0:T(8,128)S(1)} %get-tuple-element.45), channel_id=1, source_target_pairs={{0,16},{1,17},{2,18},{3,19},{4,1},{5,2},{6,3},{7,23},{8,5},{9,6},{... | collective-permute-start | bytes 98312 | tf_op jit(solution)/shard_map/ppermute | solution.py:537
  16.2 3.7 %collective-permute-start.6 = (f32[16,512]{1,0:T(8,128)S(1)}, f32[16,512]{1,0:T(8,128)S(1)}, u32[]{:S(2)}, u32[]{:S(2)}) collective-permute-start(f32[16,512]{1,0:T(8,128)S(1)} %get-tuple-element.46), channel_id=1, source_target_pairs={{0,16},{1,17},{2,18},{3,19},{4,0},{5,1},{6,2},{7,3},{8,4},{9,5},{1... | collective-permute-start | bytes 98312 | tf_op jit(solution)/shard_map/ppermute | solution.py:537
  16.2 3.2 %collective-permute-start.8 = (f32[8,512]{1,0:T(8,128)S(1)}, f32[8,512]{1,0:T(8,128)S(1)}, u32[]{:S(2)}, u32[]{:S(2)}) collective-permute-start(f32[8,512]{1,0:T(8,128)S(1)} %get-tuple-element.48), channel_id=1, source_target_pairs={{0,4},{1,5},{2,6},{3,7},{4,8},{5,9},{6,10},{7,11},{8,12},{9,13},{1... | collective-permute-start | bytes 49160 | tf_op jit(solution)/shard_map/ppermute | solution.py:537
  20.0 3.5 %collective-permute-start.9 = (f32[4,16,512]{2,1,0:T(8,128)S(1)}, f32[4,16,512]{2,1,0:T(8,128)S(1)}, u32[]{:S(2)}, u32[]{:S(2)}) collective-permute-start(f32[4,16,512]{2,1,0:T(8,128)S(1)} %shard_map.52.part), channel_id=1, source_target_pairs={{0,16},{16,0},{1,17},{17,1},{2,18},{18,2},{3,19},{19,3},{4,20},{20... | collective-permute-start | bytes 393224 | tf_op jit(solution)/shard_map/ppermute | solution.py:523

commit v20 on v18

--- a/solution.py
+++ b/solution.py
@@ -244,7 +244,7 @@
     inner = zlen - 1
     keeps = jnp.where(on_first(), inner, 0)
 
-    @pl.loop(0, loads * comps)
+    @pl.loop(0, loads * comps, unroll=True)
     def _(k):
         case, comp = k // comps, k % comps
         for z in range(zlen):
@@ -275,7 +275,7 @@
 
     for first in range(0, ylen, TILE):
 
-        @pl.loop(0, xlen // LANES)
+        @pl.loop(0, xlen // LANES, unroll=True)
         def _(chunk):
             lanes = pl.ds(pl.multiple_of(chunk * LANES, LANES), LANES)
             energy = tile_energies(plus, diff, first, lanes, inner, loads, comps)
@@ -334,7 +334,7 @@
     quotient[TILE + ylen :] = zeros
     for first in range(0, ylen, TILE):
 
-        @pl.loop(0, xlen // LANES)
+        @pl.loop(0, xlen // LANES, unroll=True)
         def _(chunk):
             lanes = pl.ds(pl.multiple_of(chunk * LANES, LANES), LANES)
             (energy,) = tile_energies(plus, diff, first, lanes, 1, loads, comps)
@@ -344,7 +344,7 @@
     def _():
         for first in range(0, ylen, TILE):
 
-            @pl.loop(0, xlen // LANES)
+            @pl.loop(0, xlen // LANES, unroll=True)
             def _(chunk):
                 lanes = pl.ds(pl.multiple_of(chunk * LANES, LANES), LANES)
                 (energy,) = tile_energies(plus, diff, first, lanes, 1, loads, comps, base=2)

time: 22.4 us -> 22.4 us (level)
  waiting for transfers between devices: 7.57 us -> 8.03 us
  Pallas kernels: 5.84 us -> 5.43 us
    pallas_call x6, Pallas kernels: 5.84 us -> 5.43 us  [call(): pl.pallas_call(kernel, out_shape=shapes, in_specs=[pl.BlockSpec(memory_sp...]
    ppermute x6, waiting for transfers between devices: 4.94 us -> 5.29 us  [opposed(): return lax.ppermute(value, ('load', 'sy', 'sz'), pairs)]
  transfers between devices with their start and end apart: 9 -> 9, of which waited for: 5 -> 5; matrix products, arithmetic and copies ran while one was open for 0% -> 0% of each run, Pallas kernels for 12% -> 11%
where the time goes in v20:
time: 22.4 us; the launch traced here: 22.2 us
  starting transfers between devices  8.7 us (39%)
  waiting for transfers between devices  8.03 us (36%)
  Pallas kernels  5.43 us (24%)
    pallas_call x6, Pallas kernels, call(): pl.pallas_call(kernel, out_shape=shapes, in_specs=[pl.BlockSpec(memory_sp...  5.43 us
    ppermute x6, waiting for transfers between devices, opposed(): return lax.ppermute(value, ('load', 'sy', 'sz'), pairs)  5.29 us
    ppermute x6, starting transfers between devices, opposed(): return lax.ppermute(value, ('load', 'sy', 'sz'), pairs)  5.05 us
    ppermute x1, starting transfers between devices, ring_moved(): return lax.ppermute(value, axis, [((k + 1) % size, k) for k in range(size)])  3.51 us
    ppermute x2, waiting for transfers between devices, chip_swapped(): lax.ppermute(value, 'load', [(core, cores - 1 - core) for core in range(c...  2.74 us
  transfers between devices with their start and end apart: 9, of which 5 were waited for; matrix products, arithmetic and copies ran while one was open for 0% of the time, Pallas kernels for 11%

profile of v20, /device:TPU:0, one launch (start us, length us, event | category | flops | bytes accessed | tf_op | source)
XLA Modules:
  0.0 22.2 jit_solution(7347925563266791705)
XLA Ops:
  0.0 1.3 %shard_map.46 = (f32[2,3,4,16,512]{4,3,2,1,0:T(8,128)S(1)}, s32[4,16,512]{2,1,0:T(8,128)S(1)}, f32[4,16,512]{2,1,0:T(8,128)S(1)}, s32[4,16,512]{2,1,0:T(8,128)S(...) custom-call(f32[2,3,4,16,512]{4,3,2,1,0:T(8,128)} %refs_0_.1, s32[4,16,512]{2,1,0:T(8,128)} %refs_1_.1, ...), custom_call_target="tpu_custom_call" | custom-call | tf_op jit(solution)/shard_map/pallas_call | solution.py:458
  1.3 0.5 %collective-permute-start.1 = (f32[7,16,512]{2,1,0:T(8,128)S(1)}, f32[7,16,512]{2,1,0:T(8,128)S(1)}, u32[]{:S(2)}, u32[]{:S(2)}) collective-permute-start(f32[7,16,512]{2,1,0:T(8,128)S(1)} %get-tuple-element.25), channel_id=1, source_target_pairs={{0,16},{1,0},{2,1},{3,2},{4,20},{5,4},{6,5},{7,6},{8,24},{9,8},{10... | collective-permute-start | bytes 688136 | tf_op jit(solution)/shard_map/ppermute | solution.py:490
  1.8 3.5 %collective-permute-start.2 = (f32[24,512]{1,0:T(8,128)S(1)}, f32[24,512]{1,0:T(8,128)S(1)}, u32[]{:S(2)}, u32[]{:S(2)}) collective-permute-start(f32[24,512]{1,0:T(8,128)S(1)} %get-tuple-element.26), channel_id=1, source_target_pairs={{4,0},{8,4},{12,8},{0,12},{5,1},{9,5},{13,9},{1,13},{6,2},{10,6},{... | collective-permute-start | bytes 147464 | tf_op jit(solution)/shard_map/ppermute | solution.py:470
  5.3 0.9 %collective-permute-start = (f32[8,512]{1,0:T(8,128)S(1)}, f32[8,512]{1,0:T(8,128)S(1)}, u32[]{:S(2)}, u32[]{:S(2)}) collective-permute-start(f32[8,512]{1,0:T(8,128)S(1)} %get-tuple-element.24), channel_id=1, source_target_pairs={{0,28},{1,12},{2,13},{3,14},{4,16},{5,0},{6,1},{7,2},{8,20},{9,4},... | collective-permute-start | bytes 49160 | tf_op jit(solution)/shard_map/ppermute | solution.py:490
  6.2 2.3 %shard_map.47 = (f32[4,16,512]{2,1,0:T(8,128)S(1)}, f32[2,24,512]{2,1,0:T(8,128)S(1)}, f32[2,9,512]{2,1,0:T(8,128)S(1)}, f32[6,16,512]{2,1,0:T(8,128)S(1)}, f32[...) custom-call(f32[2,3,4,16,512]{4,3,2,1,0:T(8,128)S(1)} %get-tuple-element.27.refs_0_, ...), custom_call_target="tpu_custom_call" | custom-call | tf_op jit(solution)/shard_map/pallas_call | solution.py:458
  8.6 1.4 %collective-permute-done.refs_0_ = f32[8,512]{1,0:T(8,128)S(1)} collective-permute-done((f32[8,512]{1,0:T(8,128)S(1)}, f32[8,512]{1,0:T(8,128)S(1)}, u32[]{:S(2)}, u32[]{:S(2)}) %collective-permute-start) | collective-permute-done | bytes 16416 | tf_op jit(solution)/shard_map/ppermute | solution.py:490
  9.9 0.0 collective-permute-done.2.refs_2_
  9.9 0.0 collective-permute-done.1.refs_1_
  10.0 0.9 %shard_map.48.refs_0_ = f32[88,512]{1,0:T(8,128)S(1)} custom-call(f32[8,512]{1,0:T(8,128)S(1)} %collective-permute-done.refs_0_, f32[7,16,512]{2,1,0:T(8,128)S(1)} %collective-permute-done.1.refs_1_, f32[24,512]{1,0:T(8,128)S(1)} %collective-permute-done.2.refs_2_, f32[4,16,512]{2,1,0:T(8,128)S(1)} %get-tuple-element.31.refs_3_, ...), custom_call_target="tpu_custom_call" | custom-call | tf_op jit(solution)/shard_map/pallas_call | solution.py:458
  10.9 0.1 collective-permute-start.3
  11.0 1.4 %collective-permute-done.3.refs_1_ = f32[88,512]{1,0:T(8,128)S(1)} collective-permute-done((f32[88,512]{1,0:T(8,128)S(1)}, f32[88,512]{1,0:T(8,128)S(1)}, u32[]{:S(2)}, u32[]{:S(2)}) %collective-permute-start.3) | collective-permute-done | bytes 180256 | tf_op jit(solution)/shard_map/ppermute | solution.py:475
  12.4 0.2 collective-permute-start.7
  12.6 1.7 %collective-permute-start.4 = (f32[16,512]{1,0:T(8,128)S(1)}, f32[16,512]{1,0:T(8,128)S(1)}, u32[]{:S(2)}, u32[]{:S(2)}) collective-permute-start(f32[16,512]{1,0:T(8,128)S(1)} %get-tuple-element.39), channel_id=1, source_target_pairs={{0,16},{1,17},{2,18},{3,19},{4,20},{5,0},{6,1},{7,2},{8,24},{9,4},... | collective-permute-start | bytes 98312 | tf_op jit(solution)/shard_map/ppermute | solution.py:490
  14.3 1.8 %collective-permute-start.5 = (f32[16,512]{1,0:T(8,128)S(1)}, f32[16,512]{1,0:T(8,128)S(1)}, u32[]{:S(2)}, u32[]{:S(2)}) collective-permute-start(f32[16,512]{1,0:T(8,128)S(1)} %get-tuple-element.40), channel_id=1, source_target_pairs={{0,16},{1,4},{2,5},{3,6},{4,20},{5,8},{6,9},{7,10},{8,24},{9,12},{... | collective-permute-start | bytes 98312 | tf_op jit(solution)/shard_map/ppermute | solution.py:490
  16.1 0.0 collective-permute-start.6
  16.1 2.6 %collective-permute-done.4.d_in = f32[16,512]{1,0:T(8,128)S(1)} collective-permute-done((f32[16,512]{1,0:T(8,128)S(1)}, f32[16,512]{1,0:T(8,128)S(1)}, u32[]{:S(2)}, u32[]{:S(2)}) %collective-permute-start.4) | collective-permute-done | bytes 32800 | tf_op jit(solution)/shard_map/ppermute | solution.py:490
  18.7 0.0 collective-permute-done.5.e_in
  18.7 1.3 %collective-permute-done.6.y_in = f32[16,512]{1,0:T(8,128)S(1)} collective-permute-done((f32[16,512]{1,0:T(8,128)S(1)}, f32[16,512]{1,0:T(8,128)S(1)}, u32[]{:S(2)}, u32[]{:S(2)}) %collective-permute-start.6) | collective-permute-done | bytes 32800 | tf_op jit(solution)/shard_map/ppermute | solution.py:490
  20.0 0.0 collective-permute-done.7.z_in
  20.0 0.1 shard_map.50.part
  20.1 0.1 collective-permute-start.8
  20.2 1.3 %collective-permute-done.8.other = f32[4,16,512]{2,1,0:T(8,128)S(1)} collective-permute-done((f32[4,16,512]{2,1,0:T(8,128)S(1)}, f32[4,16,512]{2,1,0:T(8,128)S(1)}, u32[]{:S(2)}, u32[]{:S(2)}) %collective-permute-start.8) | collective-permute-done | bytes 131104 | tf_op jit(solution)/shard_map/ppermute | solution.py:475
  21.5 0.7 %shard_map.51 = f32[4,16,512]{2,1,0:T(8,128)} custom-call(f32[4,16,512]{2,1,0:T(8,128)S(1)} %shard_map.50.part, f32[4,16,512]{2,1,0:T(8,128)S(1)} %collective-permute-done.8.other), custom_call_target="tpu_custom_call" | custom-call | tf_op jit(solution)/shard_map/pallas_call | solution.py:458
  (1 shorter events, 0.0 us)
Async XLA Ops:
  1.3 8.6 %collective-permute-start.1 = (f32[7,16,512]{2,1,0:T(8,128)S(1)}, f32[7,16,512]{2,1,0:T(8,128)S(1)}, u32[]{:S(2)}, u32[]{:S(2)}) collective-permute-start(f32[7,16,512]{2,1,0:T(8,128)S(1)} %get-tuple-element.25), channel_id=1, source_target_pairs={{0,16},{1,0},{2,1},{3,2},{4,20},{5,4},{6,5},{7,6},{8,24},{9,8},{10... | collective-permute-start | bytes 688136 | tf_op jit(solution)/shard_map/ppermute | solution.py:490
  1.8 8.1 %collective-permute-start.2 = (f32[24,512]{1,0:T(8,128)S(1)}, f32[24,512]{1,0:T(8,128)S(1)}, u32[]{:S(2)}, u32[]{:S(2)}) collective-permute-start(f32[24,512]{1,0:T(8,128)S(1)} %get-tuple-element.26), channel_id=1, source_target_pairs={{4,0},{8,4},{12,8},{0,12},{5,1},{9,5},{13,9},{1,13},{6,2},{10,6},{... | collective-permute-start | bytes 147464 | tf_op jit(solution)/shard_map/ppermute | solution.py:470
  5.3 4.6 %collective-permute-start = (f32[8,512]{1,0:T(8,128)S(1)}, f32[8,512]{1,0:T(8,128)S(1)}, u32[]{:S(2)}, u32[]{:S(2)}) collective-permute-start(f32[8,512]{1,0:T(8,128)S(1)} %get-tuple-element.24), channel_id=1, source_target_pairs={{0,28},{1,12},{2,13},{3,14},{4,16},{5,0},{6,1},{7,2},{8,20},{9,4},... | collective-permute-start | bytes 49160 | tf_op jit(solution)/shard_map/ppermute | solution.py:490
  10.9 1.5 %collective-permute-start.3 = (f32[88,512]{1,0:T(8,128)S(1)}, f32[88,512]{1,0:T(8,128)S(1)}, u32[]{:S(2)}, u32[]{:S(2)}) collective-permute-start(f32[88,512]{1,0:T(8,128)S(1)} %shard_map.48.refs_0_), channel_id=1, source_target_pairs={{0,16},{16,0},{1,17},{17,1},{2,18},{18,2},{3,19},{19,3},{4,20},{20... | collective-permute-start | bytes 540680 | tf_op jit(solution)/shard_map/ppermute | solution.py:475
  12.4 7.6 %collective-permute-start.7 = (f32[4,16,512]{2,1,0:T(8,128)S(1)}, f32[4,16,512]{2,1,0:T(8,128)S(1)}, u32[]{:S(2)}, u32[]{:S(2)}) collective-permute-start(f32[4,16,512]{2,1,0:T(8,128)S(1)} %get-tuple-element.42), channel_id=1, source_target_pairs={{0,16},{1,0},{2,1},{3,2},{4,20},{5,4},{6,5},{7,6},{8,24},{9,8},{10... | collective-permute-start | bytes 393224 | tf_op jit(solution)/shard_map/ppermute | solution.py:490
  12.6 6.1 %collective-permute-start.4 = (f32[16,512]{1,0:T(8,128)S(1)}, f32[16,512]{1,0:T(8,128)S(1)}, u32[]{:S(2)}, u32[]{:S(2)}) collective-permute-start(f32[16,512]{1,0:T(8,128)S(1)} %get-tuple-element.39), channel_id=1, source_target_pairs={{0,16},{1,17},{2,18},{3,19},{4,20},{5,0},{6,1},{7,2},{8,24},{9,4},... | collective-permute-start | bytes 98312 | tf_op jit(solution)/shard_map/ppermute | solution.py:490
  14.3 4.4 %collective-permute-start.5 = (f32[16,512]{1,0:T(8,128)S(1)}, f32[16,512]{1,0:T(8,128)S(1)}, u32[]{:S(2)}, u32[]{:S(2)}) collective-permute-start(f32[16,512]{1,0:T(8,128)S(1)} %get-tuple-element.40), channel_id=1, source_target_pairs={{0,16},{1,4},{2,5},{3,6},{4,20},{5,8},{6,9},{7,10},{8,24},{9,12},{... | collective-permute-start | bytes 98312 | tf_op jit(solution)/shard_map/ppermute | solution.py:490
  16.1 3.9 %collective-permute-start.6 = (f32[16,512]{1,0:T(8,128)S(1)}, f32[16,512]{1,0:T(8,128)S(1)}, u32[]{:S(2)}, u32[]{:S(2)}) collective-permute-start(f32[16,512]{1,0:T(8,128)S(1)} %get-tuple-element.41), channel_id=1, source_target_pairs={{0,16},{1,17},{2,18},{3,19},{4,0},{5,1},{6,2},{7,3},{8,4},{9,5},{1... | collective-permute-start | bytes 98312 | tf_op jit(solution)/shard_map/ppermute | solution.py:490
  20.1 1.4 %collective-permute-start.8 = (f32[4,16,512]{2,1,0:T(8,128)S(1)}, f32[4,16,512]{2,1,0:T(8,128)S(1)}, u32[]{:S(2)}, u32[]{:S(2)}) collective-permute-start(f32[4,16,512]{2,1,0:T(8,128)S(1)} %shard_map.50.part), channel_id=1, source_target_pairs={{0,16},{16,0},{1,17},{17,1},{2,18},{18,2},{3,19},{19,3},{4,20},{20... | collective-permute-start | bytes 393224 | tf_op jit(solution)/shard_map/ppermute | solution.py:475

commit v21 on v20

--- a/solution.py
+++ b/solution.py
@@ -183,31 +183,46 @@
     return lax.axis_index("load") == 0
 
 
-def lead_kernel(totals, disp_hbm, fixed_hbm, density_hbm, solid_hbm, disp, fixed, density, solid, d_out, z_out, y_out, sems):
-    loads, comps, zlen, ylen, _ = disp.shape
+def lead_kernel(totals, disp_hbm, fixed_hbm, density_hbm, solid_hbm, d_out, z_out, y_out, layer, layer_fixed, density, solid, rows, rows_fixed, sems):
+    loads, comps, zlen, ylen, _ = disp_hbm.shape
+    gives = jnp.where(on_first(), 0, zlen - 1)
     copies = [
         pltpu.make_async_copy(source, target, sems.at[k])
         for k, (source, target) in enumerate(
-            ((disp_hbm, disp), (fixed_hbm, fixed), (density_hbm, density), (solid_hbm, solid))
+            (
+                (density_hbm.at[gives], density),
+                (solid_hbm.at[gives], solid),
+                (fixed_hbm.at[gives], layer_fixed),
+                (disp_hbm.at[:, :, gives], layer),
+                (fixed_hbm.at[:, :TILE], rows_fixed),
+                (disp_hbm.at[:, :, :, :TILE], rows),
+            )
         )
     ]
     for copy in copies:
         copy.start()
-    for copy in copies:
+    for copy in copies[:2]:
         copy.wait()
-    gives = jnp.where(on_first(), 0, zlen - 1)
     plane = lax.axis_index("sz") * zlen + gives
     base_y = lax.axis_index("sy") * ylen
     d_out[...] = jnp.zeros(d_out.shape, jnp.float32)
-    z_out[loads * comps] = voxel_factor(density[gives], solid[gives], plane, base_y, *totals)
+    z_out[loads * comps] = voxel_factor(density[...], solid[...], plane, base_y, *totals)
+    for copy in copies[2:4]:
+        copy.wait()
+    free = 1.0 - layer_fixed[...].astype(jnp.float32)
     for case in range(loads):
         for comp in range(comps):
             k = case * comps + comp
-            z_out[k] = held(disp, fixed, case, comp, gives, slice(None))
+            z_out[k] = layer[case, comp] * free
             d_out[k : k + 1] = z_out[k, :1]
-            for z in range(zlen):
+    for copy in copies[4:]:
+        copy.wait()
+    for z in range(zlen):
+        free = 1.0 - rows_fixed[z, :1].astype(jnp.float32)
+        for case in range(loads):
+            for comp in range(comps):
                 at = (comp * loads + case) * zlen + z
-                y_out[at : at + 1] = held(disp, fixed, case, comp, z, slice(0, 1))
+                y_out[at : at + 1] = rows[case, comp, z, :1] * free
 
 
 def tile_energies(plus, diff, first, lanes, layers, loads, comps, base=0):
@@ -292,7 +307,7 @@
 
 
 def outer_kernel(
-    shape, d_in, z_in, y_in, own_in, line, sends, last_plus, last_diff, last_factor, edge, share, plus, diff, quotient, factor
+    shape, z_in, y_in, own_in, line, sends, last_plus, last_diff, last_factor, edge, share, corner, plus, diff, quotient, factor
 ):
     loads, comps, zlen, ylen, xlen = shape
     planes = loads * comps
@@ -301,25 +316,18 @@
     top = first_core & (index == lax.axis_size("sz") - 1)
     more = lax.axis_index("sy") < lax.axis_size("sy") - 1
     stays, comes = jnp.where(first_core, 0, 1), jnp.where(first_core, jnp.where(top, 2, 1), 0)
-    y_rows = jnp.where(more, y_in[...], 0.0)
-    y_plus, y_diff = split_x(y_rows)
-    d_plus, d_diff = split_x(jnp.where(more, d_in[...], 0.0))
+    y_plus, y_diff = split_x(jnp.where(more, y_in[...], 0.0))
     for k in range(planes):
-        case, comp = k // comps, k % comps
-        at = (comp * loads + case) * zlen
-        beside = jnp.where(first_core, y_plus[at + inner : at + zlen], y_plus[at : at + 1])
-        beside_diff = jnp.where(first_core, y_diff[at + inner : at + zlen], y_diff[at : at + 1])
         plus[k, stays, :ylen] = last_plus[k]
         diff[k, stays, :ylen] = last_diff[k]
-        plus[k, stays, ylen : ylen + 1] = beside
-        diff[k, stays, ylen : ylen + 1] = beside_diff
         whole, change = split_x(z_in[k])
         plus[k, comes, :ylen] = whole
         diff[k, comes, :ylen] = change
-        plus[k, comes, ylen : ylen + 1] = d_plus[k : k + 1]
-        diff[k, comes, ylen : ylen + 1] = d_diff[k : k + 1]
+        for group, value in enumerate((last_plus[k, ylen - 1 :], last_diff[k, ylen - 1 :], whole[ylen - 1 :], change[ylen - 1 :])):
+            corner[group, k : k + 1] = value
     below = jnp.where(index > 0, z_in[planes], 0.0)
     factor[...] = jnp.where(first_core, last_factor[...], below)
+    corner[0, planes : planes + 1] = factor[ylen - 1 :]
 
     @pl.when(top)
     def _():
@@ -338,7 +346,8 @@
         def _(chunk):
             lanes = pl.ds(pl.multiple_of(chunk * LANES, LANES), LANES)
             (energy,) = tile_energies(plus, diff, first, lanes, 1, loads, comps)
-            quotient[first + TILE : first + 2 * TILE, lanes] = energy * factor[first : first + TILE, lanes]
+            here = energy * factor[first : first + TILE, lanes]
+            quotient[first + TILE : first + 2 * TILE, lanes] = blank_last(here, first, ylen)
 
     @pl.when(top)
     def _():
@@ -348,7 +357,8 @@
             def _(chunk):
                 lanes = pl.ds(pl.multiple_of(chunk * LANES, LANES), LANES)
                 (energy,) = tile_energies(plus, diff, first, lanes, 1, loads, comps, base=2)
-                quotient[first + TILE : first + 2 * TILE, lanes] += energy * factor[first : first + TILE, lanes]
+                here = energy * factor[first : first + TILE, lanes]
+                quotient[first + TILE : first + 2 * TILE, lanes] += blank_last(here, first, ylen)
 
     count = loads * zlen
     low, high = [], []
@@ -376,6 +386,52 @@
     ahead, back = to_neighbours(quotient, ylen)
     ends = spread_x(jnp.concatenate(ahead + back + [zeros[:2]], axis=0))
     share[ylen * zlen :] = jnp.concatenate(ups + [ends[:REACH]] + downs + [ends[REACH : 2 * REACH]], axis=0)
+
+
+def corner_line(shape, corner, y_in, d_in):
+    loads, comps, zlen, ylen, xlen = shape
+    planes = loads * comps
+    first_core = on_first()
+    top = first_core & (lax.axis_index("sz") == lax.axis_size("sz") - 1)
+    more = lax.axis_index("sy") < lax.axis_size("sy") - 1
+    rows = []
+    for k in range(planes):
+        at = (k % comps * loads + k // comps) * zlen
+        rows.append(jnp.where(first_core, y_in[at + zlen - 1 : at + zlen], y_in[at : at + 1]))
+    rows.append(jnp.zeros((-planes % TILE, xlen), jnp.float32))
+    stays_next = split_x(jnp.where(more, jnp.concatenate(rows, axis=0), 0.0))
+    comes_next = split_x(jnp.where(more, d_in[...], 0.0))
+
+    def faces(stays, comes, comp):
+        zero = jnp.zeros((1, xlen), jnp.float32)
+        under, over = [], []
+        for own, other in zip(stays, comes):
+            own, other = ([value[case * comps + comp : case * comps + comp + 1] for case in range(loads)] for value in (own, other))
+            low = [jnp.where(first_core, a, b) for a, b in zip(own, other)] + [jnp.where(top, b, 0.0) for b in other]
+            high = [jnp.where(first_core, jnp.where(top, 0.0, b), a) for a, b in zip(own, other)] + [zero] * loads
+            under.append(jnp.concatenate(low, axis=0))
+            over.append(jnp.concatenate(high, axis=0))
+        return under, over
+
+    low, high = [], []
+    for comp in range(comps):
+        near = faces((corner[0], corner[1]), (corner[2], corner[3]), comp)
+        far = faces(stays_next, comes_next, comp)
+        for (whole, change), (whole_next, change_next), into in zip(near, far, (low, high)):
+            into.append((whole + whole_next, change + change_next, whole_next - whole, change_next - change))
+    energy = quadratic(low, high, mode_weights())
+    line = sum(energy[case : case + 1] for case in range(2 * loads)) * corner[0, planes : planes + 1]
+    return spread_x(jnp.concatenate([line, jnp.zeros((TILE - 1, xlen), jnp.float32)], axis=0))[:1]
+
+
+def corner_kernel(shape, share_in, corner, y_in, d_in, share):
+    _, _, zlen, ylen, xlen = shape
+    line = corner_line(shape, corner, y_in, d_in)
+    rising = jnp.maximum(lax.broadcasted_iota(jnp.int32, (TILE, xlen), 0) - (TILE - 1 - ROWS), 0).astype(jnp.float32)
+    falling = (REACH - lax.broadcasted_iota(jnp.int32, (REACH, xlen), 0)).astype(jnp.float32)
+    share[...] = share_in[...]
+    share[ylen * zlen - TILE : ylen * zlen] += rising * line
+    share[ylen * zlen + REACH * (zlen - 1) : ylen * zlen + REACH * zlen] += falling * line
 
 
 def total_kernel(shape, share, other, h_out, z_out, y_out, d_out, e_out):
@@ -498,12 +554,19 @@
         pltpu.with_memory_space_constraint(arg, pltpu.HBM) for arg in (displacements, fixed, density, solid)
     ]
 
-    disp, fixed, density, solid, d_send, z_send, y_send = call(
+    d_send, z_send, y_send = call(
         lambda *refs: lead_kernel(totals, *refs),
-        [jax.ShapeDtypeStruct(arg.shape, arg.dtype) for arg in args]
-        + [(-(-planes // TILE) * TILE, xlen), (planes + 1, ylen, xlen), (planes * zlen, xlen)],
+        [(-(-planes // TILE) * TILE, xlen), (planes + 1, ylen, xlen), (planes * zlen, xlen)],
         args,
-        scratch=[pltpu.SemaphoreType.DMA((len(args),))],
+        scratch=[
+            pltpu.VMEM((loads, comps, ylen, xlen), jnp.float32),
+            pltpu.VMEM((ylen, xlen), jnp.int32),
+            pltpu.VMEM((ylen, xlen), jnp.float32),
+            pltpu.VMEM((ylen, xlen), jnp.int32),
+            pltpu.VMEM((loads, comps, zlen, TILE, xlen), jnp.float32),
+            pltpu.VMEM((zlen, TILE, xlen), jnp.int32),
+            pltpu.SemaphoreType.DMA((6,)),
+        ],
         space=pltpu.HBM,
     )
     d_in = opposed(d_send, -1, 0, y_shift=-1)
@@ -521,20 +584,24 @@
             (ylen, xlen),
             (TILE, xlen),
         ],
-        (disp, fixed, density, solid),
+        (displacements, fixed, density, solid),
         scratch=[nodes(zlen), nodes(zlen), pltpu.VMEM((zlen - 1, ylen + 2 * TILE, xlen), jnp.float32)],
     )
     reach = REACH * zlen
-    (share,) = call(
-        lambda *refs: outer_kernel(displacements.shape, *refs),
-        [(ylen * zlen + 2 * reach, xlen)],
-        (d_in, z_in, y_in, *inner),
+    shape = displacements.shape
+    share, corner = call(
+        lambda *refs: outer_kernel(shape, *refs),
+        [(ylen * zlen + 2 * reach, xlen), (4, -(-(planes + 1) // TILE) * TILE, xlen)],
+        (z_in, y_in, *inner),
         scratch=[
             nodes(4),
             nodes(4),
             pltpu.VMEM((ylen + 2 * TILE, xlen), jnp.float32),
             pltpu.VMEM((ylen, xlen), jnp.float32),
         ],
+    )
+    (share,) = call(
+        lambda *refs: corner_kernel(shape, *refs), [(ylen * zlen + 2 * reach, xlen)], (share, corner, y_in, d_in)
     )
     sent = (-(-(reach + REACH) // TILE) * TILE, xlen)
     h, z_send, y_send, d_send, e_send = call(

time: 22.4 us -> 21.7 us (0.969)
  waiting for transfers between devices: 8.03 us -> 6.7 us
  starting transfers between devices: 8.7 us -> 9.08 us
  Pallas kernels: 5.43 us -> 5.74 us
    ppermute x6, waiting for transfers between devices: 5.29 us -> 4.31 us  [opposed(): return lax.ppermute(value, ('load', 'sy', 'sz'), pairs)]
    ppermute x2, starting transfers between devices: 0.14 us -> 0.87 us  [chip_swapped(): lax.ppermute(value, 'load', [(core, cores - 1 - core) for core in range(c...]
    ppermute x2, waiting for transfers between devices: 2.74 us -> 2.38 us  [chip_swapped(): lax.ppermute(value, 'load', [(core, cores - 1 - core) for core in range(c...]
    ppermute x6, starting transfers between devices: 5.05 us -> 4.7 us  [opposed(): return lax.ppermute(value, ('load', 'sy', 'sz'), pairs)]
    pallas_call x6 -> x7, Pallas kernels: 5.43 us -> 5.74 us  [call(): pl.pallas_call(kernel, out_shape=shapes, in_specs=[pl.BlockSpec(memory_sp...]
  transfers between devices with their start and end apart: 9 -> 9, of which waited for: 5 -> 5; matrix products, arithmetic and copies ran while one was open for 0% -> 0% of each run, Pallas kernels for 11% -> 15%
where the time goes in v21:
time: 21.7 us; the launch traced here: 21.6 us
  starting transfers between devices  9.08 us (42%)
  waiting for transfers between devices  6.7 us (31%)
  Pallas kernels  5.74 us (26%)
    pallas_call x7, Pallas kernels, call(): pl.pallas_call(kernel, out_shape=shapes, in_specs=[pl.BlockSpec(memory_sp...  5.74 us
    ppermute x6, starting transfers between devices, opposed(): return lax.ppermute(value, ('load', 'sy', 'sz'), pairs)  4.7 us
    ppermute x6, waiting for transfers between devices, opposed(): return lax.ppermute(value, ('load', 'sy', 'sz'), pairs)  4.31 us
    ppermute x1, starting transfers between devices, ring_moved(): return lax.ppermute(value, axis, [((k + 1) % size, k) for k in range(size)])  3.51 us
    ppermute x2, waiting for transfers between devices, chip_swapped(): lax.ppermute(value, 'load', [(core, cores - 1 - core) for core in range(c...  2.38 us
    ppermute x2, starting transfers between devices, chip_swapped(): lax.ppermute(value, 'load', [(core, cores - 1 - core) for core in range(c...  0.87 us
  transfers between devices with their start and end apart: 9, of which 5 were waited for; matrix products, arithmetic and copies ran while one was open for 0% of the time, Pallas kernels for 15%

profile of v21, /device:TPU:0, one launch (start us, length us, event | category | flops | bytes accessed | tf_op | source)
XLA Modules:
  0.0 21.6 jit_solution(18287605817804193981)
XLA Ops:
  0.0 0.0 copy-start.1
  0.0 0.0 copy-start.3
  0.0 0.0 copy-start.2
  0.0 0.0 copy-start
  0.0 1.4 %shard_map.46 = (f32[8,512]{1,0:T(8,128)S(1)}, f32[7,16,512]{2,1,0:T(8,128)S(1)}, f32[24,512]{1,0:T(8,128)S(1)}) custom-call(f32[2,3,4,16,512]{4,3,2,1,0:T(8,128)} %refs_0_.3, s32[4,16,512]{2,1,0:T(8,128)} %refs_1_.3, f32[4,16,512]{2,1,0:T(8,128)} %refs_2_.3, s32[4,16,512]{2,1,0:T(8,128)} %refs_3_.3), custom_call_target="tpu_custom_call" | custom-call | tf_op jit(solution)/shard_map/pallas_call | solution.py:514
  1.4 0.5 %collective-permute-start = (f32[7,16,512]{2,1,0:T(8,128)S(1)}, f32[7,16,512]{2,1,0:T(8,128)S(1)}, u32[]{:S(2)}, u32[]{:S(2)}) collective-permute-start(f32[7,16,512]{2,1,0:T(8,128)S(1)} %get-tuple-element.22), channel_id=1, source_target_pairs={{0,16},{1,0},{2,1},{3,2},{4,20},{5,4},{6,5},{7,6},{8,24},{9,8},{10... | collective-permute-start | bytes 688136 | tf_op jit(solution)/shard_map/ppermute | solution.py:546
  1.9 3.5 %collective-permute-start.1 = (f32[24,512]{1,0:T(8,128)S(1)}, f32[24,512]{1,0:T(8,128)S(1)}, u32[]{:S(2)}, u32[]{:S(2)}) collective-permute-start(f32[24,512]{1,0:T(8,128)S(1)} %get-tuple-element.23), channel_id=1, source_target_pairs={{4,0},{8,4},{12,8},{0,12},{5,1},{9,5},{13,9},{1,13},{6,2},{10,6},{... | collective-permute-start | bytes 147464 | tf_op jit(solution)/shard_map/ppermute | solution.py:526
  5.4 0.9 %collective-permute-start.2 = (f32[8,512]{1,0:T(8,128)S(1)}, f32[8,512]{1,0:T(8,128)S(1)}, u32[]{:S(2)}, u32[]{:S(2)}) collective-permute-start(f32[8,512]{1,0:T(8,128)S(1)} %get-tuple-element.33), channel_id=1, source_target_pairs={{0,28},{1,12},{2,13},{3,14},{4,16},{5,0},{6,1},{7,2},{8,20},{9,4},... | collective-permute-start | bytes 49160 | tf_op jit(solution)/shard_map/ppermute | solution.py:546
  6.3 0.0 copy-done.1
  6.3 0.0 copy-done.3
  6.3 0.0 copy-done.2
  6.3 0.0 copy-done
  6.3 2.3 %shard_map.47 = (f32[4,16,512]{2,1,0:T(8,128)S(1)}, f32[2,24,512]{2,1,0:T(8,128)S(1)}, f32[2,9,512]{2,1,0:T(8,128)S(1)}, f32[6,16,512]{2,1,0:T(8,128)S(1)}, f32[...) custom-call(f32[2,3,4,16,512]{4,3,2,1,0:T(8,128)S(1)} %copy-done, s32[4,16,512]{2,1,0:T(8,128)S(1)} %copy-done.1, ...), custom_call_target="tpu_custom_call" | custom-call | tf_op jit(solution)/shard_map/pallas_call | solution.py:514
  8.6 0.0 collective-permute-done.1.refs_1_.refs_2_
  8.7 0.0 collective-permute-done.refs_0_
  8.7 0.9 %shard_map.48 = (f32[88,512]{1,0:T(8,128)S(1)}, f32[4,8,512]{2,1,0:T(8,128)S(1)}) custom-call(f32[7,16,512]{2,1,0:T(8,128)S(1)} %collective-permute-done.refs_0_, f32[24,512]{1,0:T(8,128)S(1)} %collective-permute-done.1.refs_1_.refs_2_, f32[4,16,512]{2,1,0:T(8,128)S(1)} %get-tuple-element.24.refs_2_, f32[2,24,512]{2,1,0:T(8,128)S(1)} %get-tuple-element.25.refs_3_, ...), custom_call_target="tpu_custom_call" | custom-call | tf_op jit(solution)/shard_map/pallas_call | solution.py:514
  9.6 0.4 %collective-permute-done.2.refs_3_ = f32[8,512]{1,0:T(8,128)S(1)} collective-permute-done((f32[8,512]{1,0:T(8,128)S(1)}, f32[8,512]{1,0:T(8,128)S(1)}, u32[]{:S(2)}, u32[]{:S(2)}) %collective-permute-start.2) | collective-permute-done | bytes 16416 | tf_op jit(solution)/shard_map/ppermute | solution.py:546
  10.0 0.3 %shard_map.49.refs_0_ = f32[88,512]{1,0:T(8,128)S(1)} custom-call(f32[88,512]{1,0:T(8,128)S(1)} %get-tuple-element.31.refs_0_, f32[4,8,512]{2,1,0:T(8,128)S(1)} %get-tuple-element.32.refs_1_, f32[24,512]{1,0:T(8,128)S(1)} %collective-permute-done.1.refs_1_.refs_2_, f32[8,512]{1,0:T(8,128)S(1)} %collective-permute-done.2.refs_3_), custom_call_target="tpu_custom_call" | custom-call | tf_op jit(solution)/shard_map/pallas_call | solution.py:514
  10.3 0.8 %collective-permute-start.3 = (f32[88,512]{1,0:T(8,128)S(1)}, f32[88,512]{1,0:T(8,128)S(1)}, u32[]{:S(2)}, u32[]{:S(2)}) collective-permute-start(f32[88,512]{1,0:T(8,128)S(1)} %shard_map.49.refs_0_), channel_id=1, source_target_pairs={{0,16},{16,0},{1,17},{17,1},{2,18},{18,2},{3,19},{19,3},{4,20},{20... | collective-permute-start | bytes 540680 | tf_op jit(solution)/shard_map/ppermute | solution.py:531
  11.1 1.0 %collective-permute-done.3.refs_1_ = f32[88,512]{1,0:T(8,128)S(1)} collective-permute-done((f32[88,512]{1,0:T(8,128)S(1)}, f32[88,512]{1,0:T(8,128)S(1)}, u32[]{:S(2)}, u32[]{:S(2)}) %collective-permute-start.3) | collective-permute-done | bytes 180256 | tf_op jit(solution)/shard_map/ppermute | solution.py:531
  12.2 0.4 %collective-permute-start.7 = (f32[4,16,512]{2,1,0:T(8,128)S(1)}, f32[4,16,512]{2,1,0:T(8,128)S(1)}, u32[]{:S(2)}, u32[]{:S(2)}) collective-permute-start(f32[4,16,512]{2,1,0:T(8,128)S(1)} %get-tuple-element.38), channel_id=1, source_target_pairs={{0,16},{1,0},{2,1},{3,2},{4,20},{5,4},{6,5},{7,6},{8,24},{9,8},{10... | collective-permute-start | bytes 393224 | tf_op jit(solution)/shard_map/ppermute | solution.py:546
  12.6 1.3 %collective-permute-start.4 = (f32[16,512]{1,0:T(8,128)S(1)}, f32[16,512]{1,0:T(8,128)S(1)}, u32[]{:S(2)}, u32[]{:S(2)}) collective-permute-start(f32[16,512]{1,0:T(8,128)S(1)} %get-tuple-element.35), channel_id=1, source_target_pairs={{0,16},{1,17},{2,18},{3,19},{4,20},{5,0},{6,1},{7,2},{8,24},{9,4},... | collective-permute-start | bytes 98312 | tf_op jit(solution)/shard_map/ppermute | solution.py:546
  13.9 1.6 %collective-permute-start.5 = (f32[16,512]{1,0:T(8,128)S(1)}, f32[16,512]{1,0:T(8,128)S(1)}, u32[]{:S(2)}, u32[]{:S(2)}) collective-permute-start(f32[16,512]{1,0:T(8,128)S(1)} %get-tuple-element.36), channel_id=1, source_target_pairs={{0,16},{1,4},{2,5},{3,6},{4,20},{5,8},{6,9},{7,10},{8,24},{9,12},{... | collective-permute-start | bytes 98312 | tf_op jit(solution)/shard_map/ppermute | solution.py:546
  15.5 0.0 collective-permute-start.6
  15.5 3.0 %collective-permute-done.4.d_in = f32[16,512]{1,0:T(8,128)S(1)} collective-permute-done((f32[16,512]{1,0:T(8,128)S(1)}, f32[16,512]{1,0:T(8,128)S(1)}, u32[]{:S(2)}, u32[]{:S(2)}) %collective-permute-start.4) | collective-permute-done | bytes 32800 | tf_op jit(solution)/shard_map/ppermute | solution.py:546
  18.5 0.0 collective-permute-done.5.e_in
  18.5 0.9 %collective-permute-done.6.y_in = f32[16,512]{1,0:T(8,128)S(1)} collective-permute-done((f32[16,512]{1,0:T(8,128)S(1)}, f32[16,512]{1,0:T(8,128)S(1)}, u32[]{:S(2)}, u32[]{:S(2)}) %collective-permute-start.6) | collective-permute-done | bytes 32800 | tf_op jit(solution)/shard_map/ppermute | solution.py:546
  19.4 0.0 collective-permute-done.7.z_in
  19.4 0.1 shard_map.51.part
  19.5 0.1 collective-permute-start.8
  19.6 1.3 %collective-permute-done.8.other = f32[4,16,512]{2,1,0:T(8,128)S(1)} collective-permute-done((f32[4,16,512]{2,1,0:T(8,128)S(1)}, f32[4,16,512]{2,1,0:T(8,128)S(1)}, u32[]{:S(2)}, u32[]{:S(2)}) %collective-permute-start.8) | collective-permute-done | bytes 131104 | tf_op jit(solution)/shard_map/ppermute | solution.py:531
  20.9 0.7 %shard_map.52 = f32[4,16,512]{2,1,0:T(8,128)} custom-call(f32[4,16,512]{2,1,0:T(8,128)S(1)} %shard_map.51.part, f32[4,16,512]{2,1,0:T(8,128)S(1)} %collective-permute-done.8.other), custom_call_target="tpu_custom_call" | custom-call | tf_op jit(solution)/shard_map/pallas_call | solution.py:514
  (1 shorter events, 0.0 us)
Async XLA Ops:
  0.0 6.3 %copy-start.1 = (s32[4,16,512]{2,1,0:T(8,128)S(1)}, s32[4,16,512]{2,1,0:T(8,128)}, u32[]{:S(2)}) copy-start(s32[4,16,512]{2,1,0:T(8,128)} %refs_1_.3) | copy-start | bytes 393220
  0.0 6.3 %copy-start.3 = (s32[4,16,512]{2,1,0:T(8,128)S(1)}, s32[4,16,512]{2,1,0:T(8,128)}, u32[]{:S(2)}) copy-start(s32[4,16,512]{2,1,0:T(8,128)} %refs_3_.3) | copy-start | bytes 393220
  0.0 6.3 %copy-start.2 = (f32[4,16,512]{2,1,0:T(8,128)S(1)}, f32[4,16,512]{2,1,0:T(8,128)}, u32[]{:S(2)}) copy-start(f32[4,16,512]{2,1,0:T(8,128)} %refs_2_.3) | copy-start | bytes 393220
  0.0 6.3 %copy-start = (f32[2,3,4,16,512]{4,3,2,1,0:T(8,128)S(1)}, f32[2,3,4,16,512]{4,3,2,1,0:T(8,128)}, u32[]{:S(2)}) copy-start(f32[2,3,4,16,512]{4,3,2,1,0:T(8,128)} %refs_0_.3) | copy-start | bytes 2359300
  1.4 7.3 %collective-permute-start = (f32[7,16,512]{2,1,0:T(8,128)S(1)}, f32[7,16,512]{2,1,0:T(8,128)S(1)}, u32[]{:S(2)}, u32[]{:S(2)}) collective-permute-start(f32[7,16,512]{2,1,0:T(8,128)S(1)} %get-tuple-element.22), channel_id=1, source_target_pairs={{0,16},{1,0},{2,1},{3,2},{4,20},{5,4},{6,5},{7,6},{8,24},{9,8},{10... | collective-permute-start | bytes 688136 | tf_op jit(solution)/shard_map/ppermute | solution.py:546
  1.9 6.8 %collective-permute-start.1 = (f32[24,512]{1,0:T(8,128)S(1)}, f32[24,512]{1,0:T(8,128)S(1)}, u32[]{:S(2)}, u32[]{:S(2)}) collective-permute-start(f32[24,512]{1,0:T(8,128)S(1)} %get-tuple-element.23), channel_id=1, source_target_pairs={{4,0},{8,4},{12,8},{0,12},{5,1},{9,5},{13,9},{1,13},{6,2},{10,6},{... | collective-permute-start | bytes 147464 | tf_op jit(solution)/shard_map/ppermute | solution.py:526
  5.4 4.6 %collective-permute-start.2 = (f32[8,512]{1,0:T(8,128)S(1)}, f32[8,512]{1,0:T(8,128)S(1)}, u32[]{:S(2)}, u32[]{:S(2)}) collective-permute-start(f32[8,512]{1,0:T(8,128)S(1)} %get-tuple-element.33), channel_id=1, source_target_pairs={{0,28},{1,12},{2,13},{3,14},{4,16},{5,0},{6,1},{7,2},{8,20},{9,4},... | collective-permute-start | bytes 49160 | tf_op jit(solution)/shard_map/ppermute | solution.py:546
  10.3 1.9 %collective-permute-start.3 = (f32[88,512]{1,0:T(8,128)S(1)}, f32[88,512]{1,0:T(8,128)S(1)}, u32[]{:S(2)}, u32[]{:S(2)}) collective-permute-start(f32[88,512]{1,0:T(8,128)S(1)} %shard_map.49.refs_0_), channel_id=1, source_target_pairs={{0,16},{16,0},{1,17},{17,1},{2,18},{18,2},{3,19},{19,3},{4,20},{20... | collective-permute-start | bytes 540680 | tf_op jit(solution)/shard_map/ppermute | solution.py:531
  12.2 7.2 %collective-permute-start.7 = (f32[4,16,512]{2,1,0:T(8,128)S(1)}, f32[4,16,512]{2,1,0:T(8,128)S(1)}, u32[]{:S(2)}, u32[]{:S(2)}) collective-permute-start(f32[4,16,512]{2,1,0:T(8,128)S(1)} %get-tuple-element.38), channel_id=1, source_target_pairs={{0,16},{1,0},{2,1},{3,2},{4,20},{5,4},{6,5},{7,6},{8,24},{9,8},{10... | collective-permute-start | bytes 393224 | tf_op jit(solution)/shard_map/ppermute | solution.py:546
  12.6 5.9 %collective-permute-start.4 = (f32[16,512]{1,0:T(8,128)S(1)}, f32[16,512]{1,0:T(8,128)S(1)}, u32[]{:S(2)}, u32[]{:S(2)}) collective-permute-start(f32[16,512]{1,0:T(8,128)S(1)} %get-tuple-element.35), channel_id=1, source_target_pairs={{0,16},{1,17},{2,18},{3,19},{4,20},{5,0},{6,1},{7,2},{8,24},{9,4},... | collective-permute-start | bytes 98312 | tf_op jit(solution)/shard_map/ppermute | solution.py:546
  13.9 4.6 %collective-permute-start.5 = (f32[16,512]{1,0:T(8,128)S(1)}, f32[16,512]{1,0:T(8,128)S(1)}, u32[]{:S(2)}, u32[]{:S(2)}) collective-permute-start(f32[16,512]{1,0:T(8,128)S(1)} %get-tuple-element.36), channel_id=1, source_target_pairs={{0,16},{1,4},{2,5},{3,6},{4,20},{5,8},{6,9},{7,10},{8,24},{9,12},{... | collective-permute-start | bytes 98312 | tf_op jit(solution)/shard_map/ppermute | solution.py:546
  15.5 3.9 %collective-permute-start.6 = (f32[16,512]{1,0:T(8,128)S(1)}, f32[16,512]{1,0:T(8,128)S(1)}, u32[]{:S(2)}, u32[]{:S(2)}) collective-permute-start(f32[16,512]{1,0:T(8,128)S(1)} %get-tuple-element.37), channel_id=1, source_target_pairs={{0,16},{1,17},{2,18},{3,19},{4,0},{5,1},{6,2},{7,3},{8,4},{9,5},{1... | collective-permute-start | bytes 98312 | tf_op jit(solution)/shard_map/ppermute | solution.py:546
  19.5 1.4 %collective-permute-start.8 = (f32[4,16,512]{2,1,0:T(8,128)S(1)}, f32[4,16,512]{2,1,0:T(8,128)S(1)}, u32[]{:S(2)}, u32[]{:S(2)}) collective-permute-start(f32[4,16,512]{2,1,0:T(8,128)S(1)} %shard_map.51.part), channel_id=1, source_target_pairs={{0,16},{16,0},{1,17},{17,1},{2,18},{18,2},{3,19},{19,3},{4,20},{20... | collective-permute-start | bytes 393224 | tf_op jit(solution)/shard_map/ppermute | solution.py:531

commit v22 on v21

--- a/solution.py
+++ b/solution.py
@@ -400,7 +400,7 @@
         rows.append(jnp.where(first_core, y_in[at + zlen - 1 : at + zlen], y_in[at : at + 1]))
     rows.append(jnp.zeros((-planes % TILE, xlen), jnp.float32))
     stays_next = split_x(jnp.where(more, jnp.concatenate(rows, axis=0), 0.0))
-    comes_next = split_x(jnp.where(more, d_in[...], 0.0))
+    comes_next = split_x(jnp.where(more, d_in[: -(-planes // TILE) * TILE], 0.0))
 
     def faces(stays, comes, comp):
         zero = jnp.zeros((1, xlen), jnp.float32)
@@ -556,7 +556,7 @@
 
     d_send, z_send, y_send = call(
         lambda *refs: lead_kernel(totals, *refs),
-        [(-(-planes // TILE) * TILE, xlen), (planes + 1, ylen, xlen), (planes * zlen, xlen)],
+        [(planes * zlen + TILE, xlen), (planes + 1, ylen, xlen), (planes * zlen, xlen)],
         args,
         scratch=[
             pltpu.VMEM((loads, comps, ylen, xlen), jnp.float32),

time: 21.7 us -> 23.4 us (1.078); the launches traced: 21.6 us -> 23 us
  waiting for transfers between devices: 6.7 us -> 9.69 us
  starting transfers between devices: 9.08 us -> 7.47 us
    ppermute x1, starting transfers between devices: 3.51 us -> 0.53 us  [ring_moved(): return lax.ppermute(value, axis, [((k + 1) % size, k) for k in range(size)])]
    ppermute x1, waiting for transfers between devices: 0.01 us -> 2.27 us  [ring_moved(): return lax.ppermute(value, axis, [((k + 1) % size, k) for k in range(size)])]
    ppermute x6, starting transfers between devices: 4.7 us -> 6.68 us  [opposed(): return lax.ppermute(value, ('load', 'sy', 'sz'), pairs)]
    ppermute x2, starting transfers between devices: 0.87 us -> 0.25 us  [chip_swapped(): lax.ppermute(value, 'load', [(core, cores - 1 - core) for core in range(c...]
    ppermute x6, waiting for transfers between devices: 4.31 us -> 4.78 us  [opposed(): return lax.ppermute(value, ('load', 'sy', 'sz'), pairs)]
    ppermute x2, waiting for transfers between devices: 2.38 us -> 2.64 us  [chip_swapped(): lax.ppermute(value, 'load', [(core, cores - 1 - core) for core in range(c...]
  transfers between devices with their start and end apart: 9 -> 9, of which waited for: 5 -> 5; matrix products, arithmetic and copies ran while one was open for 0% -> 0% of each run, Pallas kernels for 15% -> 14%
where the time goes in v22:
time: 23.4 us; the launch traced here: 23 us
  waiting for transfers between devices  9.69 us (41%)
  starting transfers between devices  7.47 us (32%)
  Pallas kernels  5.75 us (25%)
    ppermute x6, starting transfers between devices, opposed(): return lax.ppermute(value, ('load', 'sy', 'sz'), pairs)  6.68 us
    pallas_call x7, Pallas kernels, call(): pl.pallas_call(kernel, out_shape=shapes, in_specs=[pl.BlockSpec(memory_sp...  5.75 us
    ppermute x6, waiting for transfers between devices, opposed(): return lax.ppermute(value, ('load', 'sy', 'sz'), pairs)  4.78 us
    ppermute x2, waiting for transfers between devices, chip_swapped(): lax.ppermute(value, 'load', [(core, cores - 1 - core) for core in range(c...  2.64 us
    ppermute x1, waiting for transfers between devices, ring_moved(): return lax.ppermute(value, axis, [((k + 1) % size, k) for k in range(size)])  2.27 us
    ppermute x1, starting transfers between devices, ring_moved(): return lax.ppermute(value, axis, [((k + 1) % size, k) for k in range(size)])  0.53 us
  transfers between devices with their start and end apart: 9, of which 5 were waited for; matrix products, arithmetic and copies ran while one was open for 0% of the time, Pallas kernels for 14%

profile of v22, /device:TPU:0, one launch (start us, length us, event | category | flops | bytes accessed | tf_op | source)
XLA Modules:
  0.0 23.0 jit_solution(2796201021138098236)
XLA Ops:
  0.0 0.0 copy-start.1
  0.0 0.0 copy-start.3
  0.0 0.0 copy-start.2
  0.0 0.0 copy-start
  0.0 1.4 %shard_map.46 = (f32[32,512]{1,0:T(8,128)S(1)}, f32[7,16,512]{2,1,0:T(8,128)S(1)}, f32[24,512]{1,0:T(8,128)S(1)}) custom-call(f32[2,3,4,16,512]{4,3,2,1,0:T(8,128)} %refs_0_.3, s32[4,16,512]{2,1,0:T(8,128)} %refs_1_.3, f32[4,16,512]{2,1,0:T(8,128)} %refs_2_.3, s32[4,16,512]{2,1,0:T(8,128)} %refs_3_.3), custom_call_target="tpu_custom_call" | custom-call | tf_op jit(solution)/shard_map/pallas_call | solution.py:514
  1.4 0.5 %collective-permute-start = (f32[7,16,512]{2,1,0:T(8,128)S(1)}, f32[7,16,512]{2,1,0:T(8,128)S(1)}, u32[]{:S(2)}, u32[]{:S(2)}) collective-permute-start(f32[7,16,512]{2,1,0:T(8,128)S(1)} %get-tuple-element.22), channel_id=1, source_target_pairs={{0,16},{1,0},{2,1},{3,2},{4,20},{5,4},{6,5},{7,6},{8,24},{9,8},{10... | collective-permute-start | bytes 688136 | tf_op jit(solution)/shard_map/ppermute | solution.py:546
  1.9 4.2 %collective-permute-start.2 = (f32[32,512]{1,0:T(8,128)S(1)}, f32[32,512]{1,0:T(8,128)S(1)}, u32[]{:S(2)}, u32[]{:S(2)}) collective-permute-start(f32[32,512]{1,0:T(8,128)S(1)} %get-tuple-element.33), channel_id=1, source_target_pairs={{0,28},{1,12},{2,13},{3,14},{4,16},{5,0},{6,1},{7,2},{8,20},{9,4},... | collective-permute-start | bytes 196616 | tf_op jit(solution)/shard_map/ppermute | solution.py:546
  6.0 0.5 %collective-permute-start.1 = (f32[24,512]{1,0:T(8,128)S(1)}, f32[24,512]{1,0:T(8,128)S(1)}, u32[]{:S(2)}, u32[]{:S(2)}) collective-permute-start(f32[24,512]{1,0:T(8,128)S(1)} %get-tuple-element.23), channel_id=1, source_target_pairs={{4,0},{8,4},{12,8},{0,12},{5,1},{9,5},{13,9},{1,13},{6,2},{10,6},{... | collective-permute-start | bytes 147464 | tf_op jit(solution)/shard_map/ppermute | solution.py:526
  6.6 0.0 copy-done.1
  6.6 0.0 copy-done.3
  6.6 0.0 copy-done.2
  6.6 0.0 copy-done
  6.6 2.3 %shard_map.47 = (f32[4,16,512]{2,1,0:T(8,128)S(1)}, f32[2,24,512]{2,1,0:T(8,128)S(1)}, f32[2,9,512]{2,1,0:T(8,128)S(1)}, f32[6,16,512]{2,1,0:T(8,128)S(1)}, f32[...) custom-call(f32[2,3,4,16,512]{4,3,2,1,0:T(8,128)S(1)} %copy-done, s32[4,16,512]{2,1,0:T(8,128)S(1)} %copy-done.1, ...), custom_call_target="tpu_custom_call" | custom-call | tf_op jit(solution)/shard_map/pallas_call | solution.py:514
  8.9 2.3 %collective-permute-done.1.refs_1_.refs_2_ = f32[24,512]{1,0:T(8,128)S(1)} collective-permute-done((f32[24,512]{1,0:T(8,128)S(1)}, f32[24,512]{1,0:T(8,128)S(1)}, u32[]{:S(2)}, u32[]{:S(2)}) %collective-permute-start.1) | collective-permute-done | bytes 49184 | tf_op jit(solution)/shard_map/ppermute | solution.py:526
  11.2 0.0 collective-permute-done.refs_0_
  11.2 0.9 %shard_map.48 = (f32[88,512]{1,0:T(8,128)S(1)}, f32[4,8,512]{2,1,0:T(8,128)S(1)}) custom-call(f32[7,16,512]{2,1,0:T(8,128)S(1)} %collective-permute-done.refs_0_, f32[24,512]{1,0:T(8,128)S(1)} %collective-permute-done.1.refs_1_.refs_2_, f32[4,16,512]{2,1,0:T(8,128)S(1)} %get-tuple-element.24.refs_2_, f32[2,24,512]{2,1,0:T(8,128)S(1)} %get-tuple-element.25.refs_3_, ...), custom_call_target="tpu_custom_call" | custom-call | tf_op jit(solution)/shard_map/pallas_call | solution.py:514
  12.1 0.0 collective-permute-done.2.refs_3_
  12.1 0.3 %shard_map.49.refs_0_ = f32[88,512]{1,0:T(8,128)S(1)} custom-call(f32[88,512]{1,0:T(8,128)S(1)} %get-tuple-element.31.refs_0_, f32[4,8,512]{2,1,0:T(8,128)S(1)} %get-tuple-element.32.refs_1_, f32[24,512]{1,0:T(8,128)S(1)} %collective-permute-done.1.refs_1_.refs_2_, f32[32,512]{1,0:T(8,128)S(1)} %collective-permute-done.2.refs_3_), custom_call_target="tpu_custom_call" | custom-call | tf_op jit(solution)/shard_map/pallas_call | solution.py:514
  12.4 0.2 collective-permute-start.3
  12.6 1.3 %collective-permute-done.3.refs_1_ = f32[88,512]{1,0:T(8,128)S(1)} collective-permute-done((f32[88,512]{1,0:T(8,128)S(1)}, f32[88,512]{1,0:T(8,128)S(1)}, u32[]{:S(2)}, u32[]{:S(2)}) %collective-permute-start.3) | collective-permute-done | bytes 180256 | tf_op jit(solution)/shard_map/ppermute | solution.py:531
  14.0 0.2 collective-permute-start.7
  14.1 0.9 %collective-permute-start.4 = (f32[16,512]{1,0:T(8,128)S(1)}, f32[16,512]{1,0:T(8,128)S(1)}, u32[]{:S(2)}, u32[]{:S(2)}) collective-permute-start(f32[16,512]{1,0:T(8,128)S(1)} %get-tuple-element.35), channel_id=1, source_target_pairs={{0,16},{1,17},{2,18},{3,19},{4,20},{5,0},{6,1},{7,2},{8,24},{9,4},... | collective-permute-start | bytes 98312 | tf_op jit(solution)/shard_map/ppermute | solution.py:546
  15.0 1.0 %collective-permute-start.5 = (f32[16,512]{1,0:T(8,128)S(1)}, f32[16,512]{1,0:T(8,128)S(1)}, u32[]{:S(2)}, u32[]{:S(2)}) collective-permute-start(f32[16,512]{1,0:T(8,128)S(1)} %get-tuple-element.36), channel_id=1, source_target_pairs={{0,16},{1,4},{2,5},{3,6},{4,20},{5,8},{6,9},{7,10},{8,24},{9,12},{... | collective-permute-start | bytes 98312 | tf_op jit(solution)/shard_map/ppermute | solution.py:546
  16.0 0.0 collective-permute-start.6
  16.0 2.9 %collective-permute-done.4.d_in = f32[16,512]{1,0:T(8,128)S(1)} collective-permute-done((f32[16,512]{1,0:T(8,128)S(1)}, f32[16,512]{1,0:T(8,128)S(1)}, u32[]{:S(2)}, u32[]{:S(2)}) %collective-permute-start.4) | collective-permute-done | bytes 32800 | tf_op jit(solution)/shard_map/ppermute | solution.py:546
  18.9 0.0 collective-permute-done.5.e_in
  19.0 1.8 %collective-permute-done.6.y_in = f32[16,512]{1,0:T(8,128)S(1)} collective-permute-done((f32[16,512]{1,0:T(8,128)S(1)}, f32[16,512]{1,0:T(8,128)S(1)}, u32[]{:S(2)}, u32[]{:S(2)}) %collective-permute-start.6) | collective-permute-done | bytes 32800 | tf_op jit(solution)/shard_map/ppermute | solution.py:546
  20.8 0.0 collective-permute-done.7.z_in
  20.8 0.1 shard_map.51.part
  20.9 0.1 collective-permute-start.8
  21.0 1.3 %collective-permute-done.8.other = f32[4,16,512]{2,1,0:T(8,128)S(1)} collective-permute-done((f32[4,16,512]{2,1,0:T(8,128)S(1)}, f32[4,16,512]{2,1,0:T(8,128)S(1)}, u32[]{:S(2)}, u32[]{:S(2)}) %collective-permute-start.8) | collective-permute-done | bytes 131104 | tf_op jit(solution)/shard_map/ppermute | solution.py:531
  22.3 0.7 %shard_map.52 = f32[4,16,512]{2,1,0:T(8,128)} custom-call(f32[4,16,512]{2,1,0:T(8,128)S(1)} %shard_map.51.part, f32[4,16,512]{2,1,0:T(8,128)S(1)} %collective-permute-done.8.other), custom_call_target="tpu_custom_call" | custom-call | tf_op jit(solution)/shard_map/pallas_call | solution.py:514
  (1 shorter events, 0.0 us)
Async XLA Ops:
  0.0 6.6 %copy-start.1 = (s32[4,16,512]{2,1,0:T(8,128)S(1)}, s32[4,16,512]{2,1,0:T(8,128)}, u32[]{:S(2)}) copy-start(s32[4,16,512]{2,1,0:T(8,128)} %refs_1_.3) | copy-start | bytes 393220
  0.0 6.6 %copy-start.3 = (s32[4,16,512]{2,1,0:T(8,128)S(1)}, s32[4,16,512]{2,1,0:T(8,128)}, u32[]{:S(2)}) copy-start(s32[4,16,512]{2,1,0:T(8,128)} %refs_3_.3) | copy-start | bytes 393220
  0.0 6.6 %copy-start.2 = (f32[4,16,512]{2,1,0:T(8,128)S(1)}, f32[4,16,512]{2,1,0:T(8,128)}, u32[]{:S(2)}) copy-start(f32[4,16,512]{2,1,0:T(8,128)} %refs_2_.3) | copy-start | bytes 393220
  0.0 6.6 %copy-start = (f32[2,3,4,16,512]{4,3,2,1,0:T(8,128)S(1)}, f32[2,3,4,16,512]{4,3,2,1,0:T(8,128)}, u32[]{:S(2)}) copy-start(f32[2,3,4,16,512]{4,3,2,1,0:T(8,128)} %refs_0_.3) | copy-start | bytes 2359300
  1.4 9.8 %collective-permute-start = (f32[7,16,512]{2,1,0:T(8,128)S(1)}, f32[7,16,512]{2,1,0:T(8,128)S(1)}, u32[]{:S(2)}, u32[]{:S(2)}) collective-permute-start(f32[7,16,512]{2,1,0:T(8,128)S(1)} %get-tuple-element.22), channel_id=1, source_target_pairs={{0,16},{1,0},{2,1},{3,2},{4,20},{5,4},{6,5},{7,6},{8,24},{9,8},{10... | collective-permute-start | bytes 688136 | tf_op jit(solution)/shard_map/ppermute | solution.py:546
  1.9 10.3 %collective-permute-start.2 = (f32[32,512]{1,0:T(8,128)S(1)}, f32[32,512]{1,0:T(8,128)S(1)}, u32[]{:S(2)}, u32[]{:S(2)}) collective-permute-start(f32[32,512]{1,0:T(8,128)S(1)} %get-tuple-element.33), channel_id=1, source_target_pairs={{0,28},{1,12},{2,13},{3,14},{4,16},{5,0},{6,1},{7,2},{8,20},{9,4},... | collective-permute-start | bytes 196616 | tf_op jit(solution)/shard_map/ppermute | solution.py:546
  6.0 5.2 %collective-permute-start.1 = (f32[24,512]{1,0:T(8,128)S(1)}, f32[24,512]{1,0:T(8,128)S(1)}, u32[]{:S(2)}, u32[]{:S(2)}) collective-permute-start(f32[24,512]{1,0:T(8,128)S(1)} %get-tuple-element.23), channel_id=1, source_target_pairs={{4,0},{8,4},{12,8},{0,12},{5,1},{9,5},{13,9},{1,13},{6,2},{10,6},{... | collective-permute-start | bytes 147464 | tf_op jit(solution)/shard_map/ppermute | solution.py:526
  12.4 1.5 %collective-permute-start.3 = (f32[88,512]{1,0:T(8,128)S(1)}, f32[88,512]{1,0:T(8,128)S(1)}, u32[]{:S(2)}, u32[]{:S(2)}) collective-permute-start(f32[88,512]{1,0:T(8,128)S(1)} %shard_map.49.refs_0_), channel_id=1, source_target_pairs={{0,16},{16,0},{1,17},{17,1},{2,18},{18,2},{3,19},{19,3},{4,20},{20... | collective-permute-start | bytes 540680 | tf_op jit(solution)/shard_map/ppermute | solution.py:531
  14.0 6.8 %collective-permute-start.7 = (f32[4,16,512]{2,1,0:T(8,128)S(1)}, f32[4,16,512]{2,1,0:T(8,128)S(1)}, u32[]{:S(2)}, u32[]{:S(2)}) collective-permute-start(f32[4,16,512]{2,1,0:T(8,128)S(1)} %get-tuple-element.38), channel_id=1, source_target_pairs={{0,16},{1,0},{2,1},{3,2},{4,20},{5,4},{6,5},{7,6},{8,24},{9,8},{10... | collective-permute-start | bytes 393224 | tf_op jit(solution)/shard_map/ppermute | solution.py:546
  14.1 4.8 %collective-permute-start.4 = (f32[16,512]{1,0:T(8,128)S(1)}, f32[16,512]{1,0:T(8,128)S(1)}, u32[]{:S(2)}, u32[]{:S(2)}) collective-permute-start(f32[16,512]{1,0:T(8,128)S(1)} %get-tuple-element.35), channel_id=1, source_target_pairs={{0,16},{1,17},{2,18},{3,19},{4,20},{5,0},{6,1},{7,2},{8,24},{9,4},... | collective-permute-start | bytes 98312 | tf_op jit(solution)/shard_map/ppermute | solution.py:546
  15.0 3.9 %collective-permute-start.5 = (f32[16,512]{1,0:T(8,128)S(1)}, f32[16,512]{1,0:T(8,128)S(1)}, u32[]{:S(2)}, u32[]{:S(2)}) collective-permute-start(f32[16,512]{1,0:T(8,128)S(1)} %get-tuple-element.36), channel_id=1, source_target_pairs={{0,16},{1,4},{2,5},{3,6},{4,20},{5,8},{6,9},{7,10},{8,24},{9,12},{... | collective-permute-start | bytes 98312 | tf_op jit(solution)/shard_map/ppermute | solution.py:546
  16.0 4.8 %collective-permute-start.6 = (f32[16,512]{1,0:T(8,128)S(1)}, f32[16,512]{1,0:T(8,128)S(1)}, u32[]{:S(2)}, u32[]{:S(2)}) collective-permute-start(f32[16,512]{1,0:T(8,128)S(1)} %get-tuple-element.37), channel_id=1, source_target_pairs={{0,16},{1,17},{2,18},{3,19},{4,0},{5,1},{6,2},{7,3},{8,4},{9,5},{1... | collective-permute-start | bytes 98312 | tf_op jit(solution)/shard_map/ppermute | solution.py:546
  20.9 1.4 %collective-permute-start.8 = (f32[4,16,512]{2,1,0:T(8,128)S(1)}, f32[4,16,512]{2,1,0:T(8,128)S(1)}, u32[]{:S(2)}, u32[]{:S(2)}) collective-permute-start(f32[4,16,512]{2,1,0:T(8,128)S(1)} %shard_map.51.part), channel_id=1, source_target_pairs={{0,16},{16,0},{1,17},{17,1},{2,18},{18,2},{3,19},{19,3},{4,20},{20... | collective-permute-start | bytes 393224 | tf_op jit(solution)/shard_map/ppermute | solution.py:531

commit v23 on v21

--- a/solution.py
+++ b/solution.py
@@ -177,6 +177,10 @@
         ahead.append(sum(float(REACH - row - k) * top[TILE - 1 - k : TILE - k] for k in range(REACH - row)))
         back.append(sum(float(row + 1 - k) * base[k : k + 1] for k in range(row + 1)))
     return ahead, back
+
+
+def upward(axis):
+    return (lax.axis_index(axis) + lax.axis_index("load")) % 2 == 0
 
 
 def on_first():
@@ -450,56 +454,47 @@
     for z in range(inner):
         h_out[z + 1] = middle[ylen * z : ylen * (z + 1)]
     h_out[zlen] = highest
-    z_out[...] = h_out[pl.ds(jnp.where(first_core, 0, 1), zlen)]
+    up_z, up_y = upward("sz"), upward("sy")
+    z_out[...] = h_out[pl.ds(jnp.where(up_z, 1, 0), zlen)]
     ups = jnp.concatenate(layers(rows, REACH), axis=0)
     downs = jnp.concatenate(layers(rows + reach, REACH), axis=0)
-    y_out[: reach + REACH] = jnp.where(first_core, downs, ups)
+    ends = jnp.where(up_y, ups, downs)
+    y_out[: reach + REACH] = ends
     for out, used in ((y_out, reach + REACH), (d_out, reach), (e_out, reach)):
         out[used:] = jnp.zeros((out.shape[0] - used, xlen), jnp.float32)
-    d_out[:reach] = jnp.where(first_core, downs[:reach], ups[REACH:])
-    e_out[:reach] = jnp.where(first_core, ups[:reach], downs[REACH:])
+    d_out[:reach] = jnp.where(up_z, ends[REACH:], ends[:reach])
+    e_out[:reach] = jnp.where(up_z, ends[:reach], ends[REACH:])
 
 
 def layers_kernel(h, d_in, e_in, y_in, z_in, out):
     zlen, ylen, xlen = out.shape
-    reach = REACH * zlen
     first_core = on_first()
+    up_z, up_y = upward("sz"), upward("sy")
     z_index, z_last = lax.axis_index("sz"), lax.axis_size("sz") - 1
     y_index, y_last = lax.axis_index("sy"), lax.axis_size("sy") - 1
-    z_side = jnp.where(first_core, z_index < z_last, z_index > 0)
-    y_side = jnp.where(first_core, y_index < y_last, y_index > 0)
-    y_other = jnp.where(first_core, y_index > 0, y_index < y_last)
+    near = jnp.where(up_z, z_index < z_last, z_index > 0)
+    far = jnp.where(up_z, z_index > 0, z_index < z_last)
+    beside = jnp.where(up_y, y_index < y_last, y_index > 0)
     blank = jnp.zeros((TILE - REACH, xlen), jnp.float32)
 
-    def at_start(rows):
-        return jnp.concatenate([rows, blank], axis=0)
-
-    def at_end(rows):
-        return jnp.concatenate([blank, rows], axis=0)
-
-    def ends(rows, keep, at_last):
+    def with_ends(layer, rows, keep):
         rows = jnp.where(keep, rows, 0.0)
-        return at_start(jnp.where(at_last, 0.0, rows)), at_end(jnp.where(at_last, rows, 0.0))
-
-    def with_ends(layer, *pairs):
-        head, tail = layer[:TILE], layer[ylen - TILE :]
-        for first, last in pairs:
-            head, tail = head + first, tail + last
+        head = layer[:TILE] + jnp.concatenate([jnp.where(up_y, 0.0, rows), blank], axis=0)
+        tail = layer[ylen - TILE :] + jnp.concatenate([blank, jnp.where(up_y, rows, 0.0)], axis=0)
         return jnp.concatenate([head, layer[TILE : ylen - TILE], tail] if ylen > 2 * TILE else [head, tail], axis=0)
 
     own = []
     for k in range(zlen + 1):
-        layer = jnp.where(first_core, h[k], 0.0)
-        own.append(with_ends(layer, ends(y_in[REACH * k : REACH * (k + 1)], y_side, first_core)))
-    come = []
+        own.append(with_ends(jnp.where(first_core, h[k], 0.0), y_in[REACH * k : REACH * (k + 1)], beside))
+    zero = jnp.zeros((ylen, xlen), jnp.float32)
+    below, above = [], []
     for k in range(zlen):
         part = slice(REACH * k, REACH * (k + 1))
-        layer = jnp.where(z_side, z_in[k], 0.0)
-        straight = ends(d_in[part], z_side & y_side, first_core)
-        across = ends(e_in[part], z_side & y_other, jnp.logical_not(first_core))
-        come.append(with_ends(layer, straight, across))
-    below = [jnp.where(first_core, 0.0, layer) for layer in come[zlen - REACH :]]
-    above = [jnp.where(first_core, layer, 0.0) for layer in come]
+        from_near = with_ends(jnp.where(near, z_in[k], 0.0), d_in[part], near & beside)
+        from_far = with_ends(zero, e_in[part], far & beside)
+        below.append(jnp.where(up_z, from_far, from_near))
+        above.append(jnp.where(up_z, from_near, from_far))
+    below = below[zlen - REACH :]
     layers = below[:-1] + [below[-1] + own[0]] + own[1:-1] + [own[-1] + above[0]] + above[1:]
     for z, layer in enumerate(spread_layers(layers)):
         out[z] = layer
@@ -543,6 +538,23 @@
                     to_y, to_z, side = y, z, cores - 1 - core
                 to_y = (to_y + y_shift) % rows
                 pairs.append(((core * rows + y) * size + z, (side * rows + to_y) * size + to_z))
+    return lax.ppermute(value, ("load", "sy", "sz"), pairs)
+
+
+def partnered(value, z_way, y_way):
+    cores, rows, size = lax.axis_size("load"), lax.axis_size("sy"), lax.axis_size("sz")
+    pairs = []
+    for core in range(cores):
+        for y in range(rows):
+            for z in range(size):
+                to_z = z + z_way * (1 if (z + core) % 2 == 0 else -1)
+                to_y = y + y_way * (1 if (y + core) % 2 == 0 else -1)
+                if not 0 <= to_z < size:
+                    to_y, to_z = y ^ 1, z
+                elif not 0 <= to_y < rows:
+                    to_y, to_z = y, z + z_way * (1 if (z + core) % 2 == 0 else -1) if z_way else z ^ 1
+                pairs.append(((core * rows + y) * size + z, (core * rows + to_y) * size + to_z))
+    assert sorted(target for _, target in pairs) == list(range(len(pairs)))
     return lax.ppermute(value, ("load", "sy", "sz"), pairs)
 
 
@@ -615,10 +627,10 @@
         ],
         (share, chip_swapped(share)),
     )
-    d_in = opposed(d_send, -1, -1)
-    e_in = opposed(e_send, -1, 1)
-    y_in = opposed(y_send, 0, -1)
-    z_in = opposed(z_send, -1, 0)
+    d_in = partnered(d_send, 1, 1)
+    e_in = partnered(e_send, -1, 1)
+    y_in = partnered(y_send, 0, 1)
+    z_in = partnered(z_send, 1, 0)
     (part,) = call(layers_kernel, [(zlen, ylen, xlen)], (h, d_in, e_in, y_in, z_in))
     (out,) = call(sum_kernel, [(zlen, ylen, xlen)], (part, chip_swapped(part)))
     return out

time: 21.7 us -> 22 us (1.014)
  starting transfers between devices: 9.08 us -> 10.8 us
  waiting for transfers between devices: 6.7 us -> 5.21 us
    ppermute x0 -> x4, starting transfers between devices: none -> 5.04 us  [partnered(): return lax.ppermute(value, ('load', 'sy', 'sz'), pairs)]
    ppermute x6 -> x2, waiting for transfers between devices: 4.31 us -> 0.4 us  [opposed(): return lax.ppermute(value, ('load', 'sy', 'sz'), pairs)]
    ppermute x6 -> x2, starting transfers between devices: 4.7 us -> 1.41 us  [opposed(): return lax.ppermute(value, ('load', 'sy', 'sz'), pairs)]
    ppermute x0 -> x4, waiting for transfers between devices: none -> 2.42 us  [partnered(): return lax.ppermute(value, ('load', 'sy', 'sz'), pairs)]
  transfers between devices with their start and end apart: 9 -> 9, of which waited for: 5 -> 6; matrix products, arithmetic and copies ran while one was open for 0% -> 0% of each run, Pallas kernels for 15% -> 15%
where the time goes in v23:
time: 22 us; the launch traced here: 21.9 us
  starting transfers between devices  10.8 us (49%)
  Pallas kernels  5.73 us (26%)
  waiting for transfers between devices  5.21 us (24%)
    pallas_call x7, Pallas kernels, call(): pl.pallas_call(kernel, out_shape=shapes, in_specs=[pl.BlockSpec(memory_sp...  5.73 us
    ppermute x4, starting transfers between devices, partnered(): return lax.ppermute(value, ('load', 'sy', 'sz'), pairs)  5.04 us
    ppermute x1, starting transfers between devices, ring_moved(): return lax.ppermute(value, axis, [((k + 1) % size, k) for k in range(size)])  3.51 us
    ppermute x4, waiting for transfers between devices, partnered(): return lax.ppermute(value, ('load', 'sy', 'sz'), pairs)  2.42 us
    ppermute x2, waiting for transfers between devices, chip_swapped(): lax.ppermute(value, 'load', [(core, cores - 1 - core) for core in range(c...  2.38 us
    ppermute x2, starting transfers between devices, opposed(): return lax.ppermute(value, ('load', 'sy', 'sz'), pairs)  1.41 us
    ppermute x2, starting transfers between devices, chip_swapped(): lax.ppermute(value, 'load', [(core, cores - 1 - core) for core in range(c...  0.87 us
  transfers between devices with their start and end apart: 9, of which 6 were waited for; matrix products, arithmetic and copies ran while one was open for 0% of the time, Pallas kernels for 15%

profile of v23, /device:TPU:0, one launch (start us, length us, event | category | flops | bytes accessed | tf_op | source)
XLA Modules:
  0.0 21.9 jit_solution(12149180672049180071)
XLA Ops:
  0.0 0.0 copy-start.1
  0.0 0.0 copy-start.3
  0.0 0.0 copy-start.2
  0.0 0.0 copy-start
  0.0 1.4 %shard_map.46 = (f32[8,512]{1,0:T(8,128)S(1)}, f32[7,16,512]{2,1,0:T(8,128)S(1)}, f32[24,512]{1,0:T(8,128)S(1)}) custom-call(f32[2,3,4,16,512]{4,3,2,1,0:T(8,128)} %refs_0_.3, s32[4,16,512]{2,1,0:T(8,128)} %refs_1_.3, f32[4,16,512]{2,1,0:T(8,128)} %refs_2_.3, s32[4,16,512]{2,1,0:T(8,128)} %refs_3_.3), custom_call_target="tpu_custom_call" | custom-call | tf_op jit(solution)/shard_map/pallas_call | solution.py:509
  1.4 0.5 %collective-permute-start = (f32[7,16,512]{2,1,0:T(8,128)S(1)}, f32[7,16,512]{2,1,0:T(8,128)S(1)}, u32[]{:S(2)}, u32[]{:S(2)}) collective-permute-start(f32[7,16,512]{2,1,0:T(8,128)S(1)} %get-tuple-element.22), channel_id=1, source_target_pairs={{0,16},{1,0},{2,1},{3,2},{4,20},{5,4},{6,5},{7,6},{8,24},{9,8},{10... | collective-permute-start | bytes 688136 | tf_op jit(solution)/shard_map/ppermute | solution.py:541
  1.9 3.5 %collective-permute-start.1 = (f32[24,512]{1,0:T(8,128)S(1)}, f32[24,512]{1,0:T(8,128)S(1)}, u32[]{:S(2)}, u32[]{:S(2)}) collective-permute-start(f32[24,512]{1,0:T(8,128)S(1)} %get-tuple-element.23), channel_id=1, source_target_pairs={{4,0},{8,4},{12,8},{0,12},{5,1},{9,5},{13,9},{1,13},{6,2},{10,6},{... | collective-permute-start | bytes 147464 | tf_op jit(solution)/shard_map/ppermute | solution.py:521
  5.4 0.9 %collective-permute-start.2 = (f32[8,512]{1,0:T(8,128)S(1)}, f32[8,512]{1,0:T(8,128)S(1)}, u32[]{:S(2)}, u32[]{:S(2)}) collective-permute-start(f32[8,512]{1,0:T(8,128)S(1)} %get-tuple-element.33), channel_id=1, source_target_pairs={{0,28},{1,12},{2,13},{3,14},{4,16},{5,0},{6,1},{7,2},{8,20},{9,4},... | collective-permute-start | bytes 49160 | tf_op jit(solution)/shard_map/ppermute | solution.py:541
  6.3 0.0 copy-done.1
  6.3 0.0 copy-done.3
  6.3 0.0 copy-done.2
  6.3 0.0 copy-done
  6.3 2.3 %shard_map.47 = (f32[4,16,512]{2,1,0:T(8,128)S(1)}, f32[2,24,512]{2,1,0:T(8,128)S(1)}, f32[2,9,512]{2,1,0:T(8,128)S(1)}, f32[6,16,512]{2,1,0:T(8,128)S(1)}, f32[...) custom-call(f32[2,3,4,16,512]{4,3,2,1,0:T(8,128)S(1)} %copy-done, s32[4,16,512]{2,1,0:T(8,128)S(1)} %copy-done.1, ...), custom_call_target="tpu_custom_call" | custom-call | tf_op jit(solution)/shard_map/pallas_call | solution.py:509
  8.6 0.0 collective-permute-done.1.refs_1_.refs_2_
  8.7 0.0 collective-permute-done.refs_0_
  8.7 0.9 %shard_map.48 = (f32[88,512]{1,0:T(8,128)S(1)}, f32[4,8,512]{2,1,0:T(8,128)S(1)}) custom-call(f32[7,16,512]{2,1,0:T(8,128)S(1)} %collective-permute-done.refs_0_, f32[24,512]{1,0:T(8,128)S(1)} %collective-permute-done.1.refs_1_.refs_2_, f32[4,16,512]{2,1,0:T(8,128)S(1)} %get-tuple-element.24.refs_2_, f32[2,24,512]{2,1,0:T(8,128)S(1)} %get-tuple-element.25.refs_3_, ...), custom_call_target="tpu_custom_call" | custom-call | tf_op jit(solution)/shard_map/pallas_call | solution.py:509
  9.6 0.4 %collective-permute-done.2.refs_3_ = f32[8,512]{1,0:T(8,128)S(1)} collective-permute-done((f32[8,512]{1,0:T(8,128)S(1)}, f32[8,512]{1,0:T(8,128)S(1)}, u32[]{:S(2)}, u32[]{:S(2)}) %collective-permute-start.2) | collective-permute-done | bytes 16416 | tf_op jit(solution)/shard_map/ppermute | solution.py:541
  10.0 0.3 %shard_map.49.refs_0_ = f32[88,512]{1,0:T(8,128)S(1)} custom-call(f32[88,512]{1,0:T(8,128)S(1)} %get-tuple-element.31.refs_0_, f32[4,8,512]{2,1,0:T(8,128)S(1)} %get-tuple-element.32.refs_1_, f32[24,512]{1,0:T(8,128)S(1)} %collective-permute-done.1.refs_1_.refs_2_, f32[8,512]{1,0:T(8,128)S(1)} %collective-permute-done.2.refs_3_), custom_call_target="tpu_custom_call" | custom-call | tf_op jit(solution)/shard_map/pallas_call | solution.py:509
  10.3 0.8 %collective-permute-start.3 = (f32[88,512]{1,0:T(8,128)S(1)}, f32[88,512]{1,0:T(8,128)S(1)}, u32[]{:S(2)}, u32[]{:S(2)}) collective-permute-start(f32[88,512]{1,0:T(8,128)S(1)} %shard_map.49.refs_0_), channel_id=1, source_target_pairs={{0,16},{16,0},{1,17},{17,1},{2,18},{18,2},{3,19},{19,3},{4,20},{20... | collective-permute-start | bytes 540680 | tf_op jit(solution)/shard_map/ppermute | solution.py:526
  11.1 1.0 %collective-permute-done.3.refs_1_ = f32[88,512]{1,0:T(8,128)S(1)} collective-permute-done((f32[88,512]{1,0:T(8,128)S(1)}, f32[88,512]{1,0:T(8,128)S(1)}, u32[]{:S(2)}, u32[]{:S(2)}) %collective-permute-start.3) | collective-permute-done | bytes 180256 | tf_op jit(solution)/shard_map/ppermute | solution.py:526
  12.2 1.7 %collective-permute-start.7 = (f32[4,16,512]{2,1,0:T(8,128)S(1)}, f32[4,16,512]{2,1,0:T(8,128)S(1)}, u32[]{:S(2)}, u32[]{:S(2)}) collective-permute-start(f32[4,16,512]{2,1,0:T(8,128)S(1)} %get-tuple-element.38), channel_id=1, source_target_pairs={{0,1},{1,0},{2,3},{3,2},{4,5},{5,4},{6,7},{7,6},{8,9},{9,8},{10,11... | collective-permute-start | bytes 393224 | tf_op jit(solution)/shard_map/ppermute | solution.py:558
  13.8 1.4 %collective-permute-start.4 = (f32[16,512]{1,0:T(8,128)S(1)}, f32[16,512]{1,0:T(8,128)S(1)}, u32[]{:S(2)}, u32[]{:S(2)}) collective-permute-start(f32[16,512]{1,0:T(8,128)S(1)} %get-tuple-element.35), channel_id=1, source_target_pairs={{0,5},{1,4},{2,7},{3,6},{4,1},{5,0},{6,3},{7,2},{8,13},{9,12},{10,... | collective-permute-start | bytes 98312 | tf_op jit(solution)/shard_map/ppermute | solution.py:558
  15.2 0.5 %collective-permute-start.5 = (f32[16,512]{1,0:T(8,128)S(1)}, f32[16,512]{1,0:T(8,128)S(1)}, u32[]{:S(2)}, u32[]{:S(2)}) collective-permute-start(f32[16,512]{1,0:T(8,128)S(1)} %get-tuple-element.36), channel_id=1, source_target_pairs={{0,4},{1,6},{2,5},{3,7},{4,0},{5,2},{6,1},{7,3},{8,12},{9,14},{10,... | collective-permute-start | bytes 98312 | tf_op jit(solution)/shard_map/ppermute | solution.py:558
  15.7 1.5 %collective-permute-start.6 = (f32[16,512]{1,0:T(8,128)S(1)}, f32[16,512]{1,0:T(8,128)S(1)}, u32[]{:S(2)}, u32[]{:S(2)}) collective-permute-start(f32[16,512]{1,0:T(8,128)S(1)} %get-tuple-element.37), channel_id=1, source_target_pairs={{0,4},{1,5},{2,6},{3,7},{4,0},{5,1},{6,2},{7,3},{8,12},{9,13},{10,... | collective-permute-start | bytes 98312 | tf_op jit(solution)/shard_map/ppermute | solution.py:558
  17.2 1.6 %collective-permute-done.4.d_in = f32[16,512]{1,0:T(8,128)S(1)} collective-permute-done((f32[16,512]{1,0:T(8,128)S(1)}, f32[16,512]{1,0:T(8,128)S(1)}, u32[]{:S(2)}, u32[]{:S(2)}) %collective-permute-start.4) | collective-permute-done | bytes 32800 | tf_op jit(solution)/shard_map/ppermute | solution.py:558
  18.9 0.3 %collective-permute-done.5.e_in = f32[16,512]{1,0:T(8,128)S(1)} collective-permute-done((f32[16,512]{1,0:T(8,128)S(1)}, f32[16,512]{1,0:T(8,128)S(1)}, u32[]{:S(2)}, u32[]{:S(2)}) %collective-permute-start.5) | collective-permute-done | bytes 32800 | tf_op jit(solution)/shard_map/ppermute | solution.py:558
  19.2 0.5 %collective-permute-done.6.y_in = f32[16,512]{1,0:T(8,128)S(1)} collective-permute-done((f32[16,512]{1,0:T(8,128)S(1)}, f32[16,512]{1,0:T(8,128)S(1)}, u32[]{:S(2)}, u32[]{:S(2)}) %collective-permute-start.6) | collective-permute-done | bytes 32800 | tf_op jit(solution)/shard_map/ppermute | solution.py:558
  19.7 0.0 collective-permute-done.7.z_in
  19.7 0.1 shard_map.51.part
  19.8 0.1 collective-permute-start.8
  19.9 1.3 %collective-permute-done.8.other = f32[4,16,512]{2,1,0:T(8,128)S(1)} collective-permute-done((f32[4,16,512]{2,1,0:T(8,128)S(1)}, f32[4,16,512]{2,1,0:T(8,128)S(1)}, u32[]{:S(2)}, u32[]{:S(2)}) %collective-permute-start.8) | collective-permute-done | bytes 131104 | tf_op jit(solution)/shard_map/ppermute | solution.py:526
  21.2 0.7 %shard_map.52 = f32[4,16,512]{2,1,0:T(8,128)} custom-call(f32[4,16,512]{2,1,0:T(8,128)S(1)} %shard_map.51.part, f32[4,16,512]{2,1,0:T(8,128)S(1)} %collective-permute-done.8.other), custom_call_target="tpu_custom_call" | custom-call | tf_op jit(solution)/shard_map/pallas_call | solution.py:509
  (1 shorter events, 0.0 us)
Async XLA Ops:
  0.0 6.3 %copy-start.1 = (s32[4,16,512]{2,1,0:T(8,128)S(1)}, s32[4,16,512]{2,1,0:T(8,128)}, u32[]{:S(2)}) copy-start(s32[4,16,512]{2,1,0:T(8,128)} %refs_1_.3) | copy-start | bytes 393220
  0.0 6.3 %copy-start.3 = (s32[4,16,512]{2,1,0:T(8,128)S(1)}, s32[4,16,512]{2,1,0:T(8,128)}, u32[]{:S(2)}) copy-start(s32[4,16,512]{2,1,0:T(8,128)} %refs_3_.3) | copy-start | bytes 393220
  0.0 6.3 %copy-start.2 = (f32[4,16,512]{2,1,0:T(8,128)S(1)}, f32[4,16,512]{2,1,0:T(8,128)}, u32[]{:S(2)}) copy-start(f32[4,16,512]{2,1,0:T(8,128)} %refs_2_.3) | copy-start | bytes 393220
  0.0 6.3 %copy-start = (f32[2,3,4,16,512]{4,3,2,1,0:T(8,128)S(1)}, f32[2,3,4,16,512]{4,3,2,1,0:T(8,128)}, u32[]{:S(2)}) copy-start(f32[2,3,4,16,512]{4,3,2,1,0:T(8,128)} %refs_0_.3) | copy-start | bytes 2359300
  1.4 7.3 %collective-permute-start = (f32[7,16,512]{2,1,0:T(8,128)S(1)}, f32[7,16,512]{2,1,0:T(8,128)S(1)}, u32[]{:S(2)}, u32[]{:S(2)}) collective-permute-start(f32[7,16,512]{2,1,0:T(8,128)S(1)} %get-tuple-element.22), channel_id=1, source_target_pairs={{0,16},{1,0},{2,1},{3,2},{4,20},{5,4},{6,5},{7,6},{8,24},{9,8},{10... | collective-permute-start | bytes 688136 | tf_op jit(solution)/shard_map/ppermute | solution.py:541
  1.9 6.8 %collective-permute-start.1 = (f32[24,512]{1,0:T(8,128)S(1)}, f32[24,512]{1,0:T(8,128)S(1)}, u32[]{:S(2)}, u32[]{:S(2)}) collective-permute-start(f32[24,512]{1,0:T(8,128)S(1)} %get-tuple-element.23), channel_id=1, source_target_pairs={{4,0},{8,4},{12,8},{0,12},{5,1},{9,5},{13,9},{1,13},{6,2},{10,6},{... | collective-permute-start | bytes 147464 | tf_op jit(solution)/shard_map/ppermute | solution.py:521
  5.4 4.6 %collective-permute-start.2 = (f32[8,512]{1,0:T(8,128)S(1)}, f32[8,512]{1,0:T(8,128)S(1)}, u32[]{:S(2)}, u32[]{:S(2)}) collective-permute-start(f32[8,512]{1,0:T(8,128)S(1)} %get-tuple-element.33), channel_id=1, source_target_pairs={{0,28},{1,12},{2,13},{3,14},{4,16},{5,0},{6,1},{7,2},{8,20},{9,4},... | collective-permute-start | bytes 49160 | tf_op jit(solution)/shard_map/ppermute | solution.py:541
  10.3 1.9 %collective-permute-start.3 = (f32[88,512]{1,0:T(8,128)S(1)}, f32[88,512]{1,0:T(8,128)S(1)}, u32[]{:S(2)}, u32[]{:S(2)}) collective-permute-start(f32[88,512]{1,0:T(8,128)S(1)} %shard_map.49.refs_0_), channel_id=1, source_target_pairs={{0,16},{16,0},{1,17},{17,1},{2,18},{18,2},{3,19},{19,3},{4,20},{20... | collective-permute-start | bytes 540680 | tf_op jit(solution)/shard_map/ppermute | solution.py:526
  12.2 7.5 %collective-permute-start.7 = (f32[4,16,512]{2,1,0:T(8,128)S(1)}, f32[4,16,512]{2,1,0:T(8,128)S(1)}, u32[]{:S(2)}, u32[]{:S(2)}) collective-permute-start(f32[4,16,512]{2,1,0:T(8,128)S(1)} %get-tuple-element.38), channel_id=1, source_target_pairs={{0,1},{1,0},{2,3},{3,2},{4,5},{5,4},{6,7},{7,6},{8,9},{9,8},{10,11... | collective-permute-start | bytes 393224 | tf_op jit(solution)/shard_map/ppermute | solution.py:558
  13.8 5.0 %collective-permute-start.4 = (f32[16,512]{1,0:T(8,128)S(1)}, f32[16,512]{1,0:T(8,128)S(1)}, u32[]{:S(2)}, u32[]{:S(2)}) collective-permute-start(f32[16,512]{1,0:T(8,128)S(1)} %get-tuple-element.35), channel_id=1, source_target_pairs={{0,5},{1,4},{2,7},{3,6},{4,1},{5,0},{6,3},{7,2},{8,13},{9,12},{10,... | collective-permute-start | bytes 98312 | tf_op jit(solution)/shard_map/ppermute | solution.py:558
  15.2 4.0 %collective-permute-start.5 = (f32[16,512]{1,0:T(8,128)S(1)}, f32[16,512]{1,0:T(8,128)S(1)}, u32[]{:S(2)}, u32[]{:S(2)}) collective-permute-start(f32[16,512]{1,0:T(8,128)S(1)} %get-tuple-element.36), channel_id=1, source_target_pairs={{0,4},{1,6},{2,5},{3,7},{4,0},{5,2},{6,1},{7,3},{8,12},{9,14},{10,... | collective-permute-start | bytes 98312 | tf_op jit(solution)/shard_map/ppermute | solution.py:558
  15.7 3.9 %collective-permute-start.6 = (f32[16,512]{1,0:T(8,128)S(1)}, f32[16,512]{1,0:T(8,128)S(1)}, u32[]{:S(2)}, u32[]{:S(2)}) collective-permute-start(f32[16,512]{1,0:T(8,128)S(1)} %get-tuple-element.37), channel_id=1, source_target_pairs={{0,4},{1,5},{2,6},{3,7},{4,0},{5,1},{6,2},{7,3},{8,12},{9,13},{10,... | collective-permute-start | bytes 98312 | tf_op jit(solution)/shard_map/ppermute | solution.py:558
  19.8 1.4 %collective-permute-start.8 = (f32[4,16,512]{2,1,0:T(8,128)S(1)}, f32[4,16,512]{2,1,0:T(8,128)S(1)}, u32[]{:S(2)}, u32[]{:S(2)}) collective-permute-start(f32[4,16,512]{2,1,0:T(8,128)S(1)} %shard_map.51.part), channel_id=1, source_target_pairs={{0,16},{16,0},{1,17},{17,1},{2,18},{18,2},{3,19},{19,3},{4,20},{20... | collective-permute-start | bytes 393224 | tf_op jit(solution)/shard_map/ppermute | solution.py:526

commit v24 on v21

--- a/solution.py
+++ b/solution.py
@@ -183,7 +183,10 @@
     return lax.axis_index("load") == 0
 
 
-def lead_kernel(totals, disp_hbm, fixed_hbm, density_hbm, solid_hbm, d_out, z_out, y_out, layer, layer_fixed, density, solid, rows, rows_fixed, sems):
+def lead_kernel(
+    totals, disp_hbm, fixed_hbm, density_hbm, solid_hbm, d_out, z_out, y_out, *rest
+):
+    *kept, layer, layer_fixed, density, solid, rows, rows_fixed, sems = rest
     loads, comps, zlen, ylen, _ = disp_hbm.shape
     gives = jnp.where(on_first(), 0, zlen - 1)
     copies = [
@@ -196,6 +199,7 @@
                 (disp_hbm.at[:, :, gives], layer),
                 (fixed_hbm.at[:, :TILE], rows_fixed),
                 (disp_hbm.at[:, :, :, :TILE], rows),
+                *zip((disp_hbm, fixed_hbm, density_hbm, solid_hbm), kept),
             )
         )
     ]
@@ -215,7 +219,7 @@
             k = case * comps + comp
             z_out[k] = layer[case, comp] * free
             d_out[k : k + 1] = z_out[k, :1]
-    for copy in copies[4:]:
+    for copy in copies[4:6]:
         copy.wait()
     for z in range(zlen):
         free = 1.0 - rows_fixed[z, :1].astype(jnp.float32)
@@ -223,6 +227,8 @@
             for comp in range(comps):
                 at = (comp * loads + case) * zlen + z
                 y_out[at : at + 1] = rows[case, comp, z, :1] * free
+    for copy in copies[6:]:
+        copy.wait()
 
 
 def tile_energies(plus, diff, first, lanes, layers, loads, comps, base=0):
@@ -258,12 +264,13 @@
     base_y = lax.axis_index("sy") * ylen
     inner = zlen - 1
     keeps = jnp.where(on_first(), inner, 0)
+    free = [1.0 - fixed[z].astype(jnp.float32) for z in range(zlen)]
 
     @pl.loop(0, loads * comps, unroll=True)
     def _(k):
         case, comp = k // comps, k % comps
         for z in range(zlen):
-            whole, change = split_x(held(disp, fixed, case, comp, z, slice(None)))
+            whole, change = split_x(disp[case, comp, z] * free[z])
             plus[k, z, :ylen] = whole
             diff[k, z, :ylen] = change
         last_plus[k] = plus[k, keeps, :ylen]
@@ -554,9 +561,10 @@
         pltpu.with_memory_space_constraint(arg, pltpu.HBM) for arg in (displacements, fixed, density, solid)
     ]
 
-    d_send, z_send, y_send = call(
+    d_send, z_send, y_send, *kept = call(
         lambda *refs: lead_kernel(totals, *refs),
-        [(-(-planes // TILE) * TILE, xlen), (planes + 1, ylen, xlen), (planes * zlen, xlen)],
+        [(-(-planes // TILE) * TILE, xlen), (planes + 1, ylen, xlen), (planes * zlen, xlen)]
+        + [jax.ShapeDtypeStruct(arg.shape, arg.dtype) for arg in args],
         args,
         scratch=[
             pltpu.VMEM((loads, comps, ylen, xlen), jnp.float32),
@@ -565,7 +573,7 @@
             pltpu.VMEM((ylen, xlen), jnp.int32),
             pltpu.VMEM((loads, comps, zlen, TILE, xlen), jnp.float32),
             pltpu.VMEM((zlen, TILE, xlen), jnp.int32),
-            pltpu.SemaphoreType.DMA((6,)),
+            pltpu.SemaphoreType.DMA((6 + len(args),)),
         ],
         space=pltpu.HBM,
     )
@@ -584,7 +592,7 @@
             (ylen, xlen),
             (TILE, xlen),
         ],
-        (displacements, fixed, density, solid),
+        kept,
         scratch=[nodes(zlen), nodes(zlen), pltpu.VMEM((zlen - 1, ylen + 2 * TILE, xlen), jnp.float32)],
     )
     reach = REACH * zlen

time: 21.7 us -> 22 us (1.014)
  Pallas kernels: 5.74 us -> 5.99 us
    pallas_call x7, Pallas kernels: 5.74 us -> 5.99 us  [call(): pl.pallas_call(kernel, out_shape=shapes, in_specs=[pl.BlockSpec(memory_sp...]
where the time goes in v24:
time: 22 us; the launch traced here: 21.8 us
  starting transfers between devices  9.06 us (41%)
  waiting for transfers between devices  6.72 us (31%)
  Pallas kernels  5.99 us (27%)
    pallas_call x7, Pallas kernels, call(): pl.pallas_call(kernel, out_shape=shapes, in_specs=[pl.BlockSpec(memory_sp...  5.99 us
    ppermute x6, starting transfers between devices, opposed(): return lax.ppermute(value, ('load', 'sy', 'sz'), pairs)  4.69 us
    ppermute x6, waiting for transfers between devices, opposed(): return lax.ppermute(value, ('load', 'sy', 'sz'), pairs)  4.33 us
    ppermute x1, starting transfers between devices, ring_moved(): return lax.ppermute(value, axis, [((k + 1) % size, k) for k in range(size)])  3.51 us
    ppermute x2, waiting for transfers between devices, chip_swapped(): lax.ppermute(value, 'load', [(core, cores - 1 - core) for core in range(c...  2.38 us
    ppermute x2, starting transfers between devices, chip_swapped(): lax.ppermute(value, 'load', [(core, cores - 1 - core) for core in range(c...  0.86 us
  transfers between devices with their start and end apart: 9, of which 5 were waited for; matrix products, arithmetic and copies ran while one was open for 0% of the time, Pallas kernels for 15%

profile of v24, /device:TPU:0, one launch (start us, length us, event | category | flops | bytes accessed | tf_op | source)
XLA Modules:
  0.0 21.8 jit_solution(5669321537282273674)
XLA Ops:
  0.0 1.6 %shard_map.46 = (f32[8,512]{1,0:T(8,128)S(1)}, f32[7,16,512]{2,1,0:T(8,128)S(1)}, f32[24,512]{1,0:T(8,128)S(1)}, f32[2,3,4,16,512]{4,3,2,1,0:T(8,128)S(1)}, s32[...) custom-call(f32[2,3,4,16,512]{4,3,2,1,0:T(8,128)} %refs_0_.1, s32[4,16,512]{2,1,0:T(8,128)} %refs_1_.1, ...), custom_call_target="tpu_custom_call" | custom-call | tf_op jit(solution)/shard_map/pallas_call | solution.py:521
  1.6 0.5 %collective-permute-start = (f32[7,16,512]{2,1,0:T(8,128)S(1)}, f32[7,16,512]{2,1,0:T(8,128)S(1)}, u32[]{:S(2)}, u32[]{:S(2)}) collective-permute-start(f32[7,16,512]{2,1,0:T(8,128)S(1)} %get-tuple-element.26), channel_id=1, source_target_pairs={{0,16},{1,0},{2,1},{3,2},{4,20},{5,4},{6,5},{7,6},{8,24},{9,8},{10... | collective-permute-start | bytes 688136 | tf_op jit(solution)/shard_map/ppermute | solution.py:553
  2.1 3.5 %collective-permute-start.1 = (f32[24,512]{1,0:T(8,128)S(1)}, f32[24,512]{1,0:T(8,128)S(1)}, u32[]{:S(2)}, u32[]{:S(2)}) collective-permute-start(f32[24,512]{1,0:T(8,128)S(1)} %get-tuple-element.27), channel_id=1, source_target_pairs={{4,0},{8,4},{12,8},{0,12},{5,1},{9,5},{13,9},{1,13},{6,2},{10,6},{... | collective-permute-start | bytes 147464 | tf_op jit(solution)/shard_map/ppermute | solution.py:533
  5.6 0.9 %collective-permute-start.2 = (f32[8,512]{1,0:T(8,128)S(1)}, f32[8,512]{1,0:T(8,128)S(1)}, u32[]{:S(2)}, u32[]{:S(2)}) collective-permute-start(f32[8,512]{1,0:T(8,128)S(1)} %get-tuple-element.41), channel_id=1, source_target_pairs={{0,28},{1,12},{2,13},{3,14},{4,16},{5,0},{6,1},{7,2},{8,20},{9,4},... | collective-permute-start | bytes 49160 | tf_op jit(solution)/shard_map/ppermute | solution.py:553
  6.5 2.3 %shard_map.47 = (f32[4,16,512]{2,1,0:T(8,128)S(1)}, f32[2,24,512]{2,1,0:T(8,128)S(1)}, f32[2,9,512]{2,1,0:T(8,128)S(1)}, f32[6,16,512]{2,1,0:T(8,128)S(1)}, f32[...) custom-call(f32[2,3,4,16,512]{4,3,2,1,0:T(8,128)S(1)} %get-tuple-element.28.refs_0_, ...), custom_call_target="tpu_custom_call" | custom-call | tf_op jit(solution)/shard_map/pallas_call | solution.py:521
  8.9 0.0 collective-permute-done.1.refs_1_.refs_2_
  8.9 0.0 collective-permute-done.refs_0_
  8.9 0.9 %shard_map.48 = (f32[88,512]{1,0:T(8,128)S(1)}, f32[4,8,512]{2,1,0:T(8,128)S(1)}) custom-call(f32[7,16,512]{2,1,0:T(8,128)S(1)} %collective-permute-done.refs_0_, f32[24,512]{1,0:T(8,128)S(1)} %collective-permute-done.1.refs_1_.refs_2_, f32[4,16,512]{2,1,0:T(8,128)S(1)} %get-tuple-element.32.refs_2_, f32[2,24,512]{2,1,0:T(8,128)S(1)} %get-tuple-element.33.refs_3_, ...), custom_call_target="tpu_custom_call" | custom-call | tf_op jit(solution)/shard_map/pallas_call | solution.py:521
  9.8 0.4 %collective-permute-done.2.refs_3_ = f32[8,512]{1,0:T(8,128)S(1)} collective-permute-done((f32[8,512]{1,0:T(8,128)S(1)}, f32[8,512]{1,0:T(8,128)S(1)}, u32[]{:S(2)}, u32[]{:S(2)}) %collective-permute-start.2) | collective-permute-done | bytes 16416 | tf_op jit(solution)/shard_map/ppermute | solution.py:553
  10.2 0.3 %shard_map.49.refs_0_ = f32[88,512]{1,0:T(8,128)S(1)} custom-call(f32[88,512]{1,0:T(8,128)S(1)} %get-tuple-element.39.refs_0_, f32[4,8,512]{2,1,0:T(8,128)S(1)} %get-tuple-element.40.refs_1_, f32[24,512]{1,0:T(8,128)S(1)} %collective-permute-done.1.refs_1_.refs_2_, f32[8,512]{1,0:T(8,128)S(1)} %collective-permute-done.2.refs_3_), custom_call_target="tpu_custom_call" | custom-call | tf_op jit(solution)/shard_map/pallas_call | solution.py:521
  10.5 0.8 %collective-permute-start.3 = (f32[88,512]{1,0:T(8,128)S(1)}, f32[88,512]{1,0:T(8,128)S(1)}, u32[]{:S(2)}, u32[]{:S(2)}) collective-permute-start(f32[88,512]{1,0:T(8,128)S(1)} %shard_map.49.refs_0_), channel_id=1, source_target_pairs={{0,16},{16,0},{1,17},{17,1},{2,18},{18,2},{3,19},{19,3},{4,20},{20... | collective-permute-start | bytes 540680 | tf_op jit(solution)/shard_map/ppermute | solution.py:538
  11.3 1.0 %collective-permute-done.3.refs_1_ = f32[88,512]{1,0:T(8,128)S(1)} collective-permute-done((f32[88,512]{1,0:T(8,128)S(1)}, f32[88,512]{1,0:T(8,128)S(1)}, u32[]{:S(2)}, u32[]{:S(2)}) %collective-permute-start.3) | collective-permute-done | bytes 180256 | tf_op jit(solution)/shard_map/ppermute | solution.py:538
  12.4 0.4 %collective-permute-start.7 = (f32[4,16,512]{2,1,0:T(8,128)S(1)}, f32[4,16,512]{2,1,0:T(8,128)S(1)}, u32[]{:S(2)}, u32[]{:S(2)}) collective-permute-start(f32[4,16,512]{2,1,0:T(8,128)S(1)} %get-tuple-element.46), channel_id=1, source_target_pairs={{0,16},{1,0},{2,1},{3,2},{4,20},{5,4},{6,5},{7,6},{8,24},{9,8},{10... | collective-permute-start | bytes 393224 | tf_op jit(solution)/shard_map/ppermute | solution.py:553
  12.8 1.3 %collective-permute-start.4 = (f32[16,512]{1,0:T(8,128)S(1)}, f32[16,512]{1,0:T(8,128)S(1)}, u32[]{:S(2)}, u32[]{:S(2)}) collective-permute-start(f32[16,512]{1,0:T(8,128)S(1)} %get-tuple-element.43), channel_id=1, source_target_pairs={{0,16},{1,17},{2,18},{3,19},{4,20},{5,0},{6,1},{7,2},{8,24},{9,4},... | collective-permute-start | bytes 98312 | tf_op jit(solution)/shard_map/ppermute | solution.py:553
  14.1 1.6 %collective-permute-start.5 = (f32[16,512]{1,0:T(8,128)S(1)}, f32[16,512]{1,0:T(8,128)S(1)}, u32[]{:S(2)}, u32[]{:S(2)}) collective-permute-start(f32[16,512]{1,0:T(8,128)S(1)} %get-tuple-element.44), channel_id=1, source_target_pairs={{0,16},{1,4},{2,5},{3,6},{4,20},{5,8},{6,9},{7,10},{8,24},{9,12},{... | collective-permute-start | bytes 98312 | tf_op jit(solution)/shard_map/ppermute | solution.py:553
  15.7 0.0 collective-permute-start.6
  15.7 3.0 %collective-permute-done.4.d_in = f32[16,512]{1,0:T(8,128)S(1)} collective-permute-done((f32[16,512]{1,0:T(8,128)S(1)}, f32[16,512]{1,0:T(8,128)S(1)}, u32[]{:S(2)}, u32[]{:S(2)}) %collective-permute-start.4) | collective-permute-done | bytes 32800 | tf_op jit(solution)/shard_map/ppermute | solution.py:553
  18.7 0.0 collective-permute-done.5.e_in
  18.7 0.9 %collective-permute-done.6.y_in = f32[16,512]{1,0:T(8,128)S(1)} collective-permute-done((f32[16,512]{1,0:T(8,128)S(1)}, f32[16,512]{1,0:T(8,128)S(1)}, u32[]{:S(2)}, u32[]{:S(2)}) %collective-permute-start.6) | collective-permute-done | bytes 32800 | tf_op jit(solution)/shard_map/ppermute | solution.py:553
  19.6 0.0 collective-permute-done.7.z_in
  19.6 0.1 shard_map.51.part
  19.7 0.1 collective-permute-start.8
  19.8 1.3 %collective-permute-done.8.other = f32[4,16,512]{2,1,0:T(8,128)S(1)} collective-permute-done((f32[4,16,512]{2,1,0:T(8,128)S(1)}, f32[4,16,512]{2,1,0:T(8,128)S(1)}, u32[]{:S(2)}, u32[]{:S(2)}) %collective-permute-start.8) | collective-permute-done | bytes 131104 | tf_op jit(solution)/shard_map/ppermute | solution.py:538
  21.2 0.7 %shard_map.52 = f32[4,16,512]{2,1,0:T(8,128)} custom-call(f32[4,16,512]{2,1,0:T(8,128)S(1)} %shard_map.51.part, f32[4,16,512]{2,1,0:T(8,128)S(1)} %collective-permute-done.8.other), custom_call_target="tpu_custom_call" | custom-call | tf_op jit(solution)/shard_map/pallas_call | solution.py:521
  (1 shorter events, 0.0 us)
Async XLA Ops:
  1.6 7.3 %collective-permute-start = (f32[7,16,512]{2,1,0:T(8,128)S(1)}, f32[7,16,512]{2,1,0:T(8,128)S(1)}, u32[]{:S(2)}, u32[]{:S(2)}) collective-permute-start(f32[7,16,512]{2,1,0:T(8,128)S(1)} %get-tuple-element.26), channel_id=1, source_target_pairs={{0,16},{1,0},{2,1},{3,2},{4,20},{5,4},{6,5},{7,6},{8,24},{9,8},{10... | collective-permute-start | bytes 688136 | tf_op jit(solution)/shard_map/ppermute | solution.py:553
  2.1 6.8 %collective-permute-start.1 = (f32[24,512]{1,0:T(8,128)S(1)}, f32[24,512]{1,0:T(8,128)S(1)}, u32[]{:S(2)}, u32[]{:S(2)}) collective-permute-start(f32[24,512]{1,0:T(8,128)S(1)} %get-tuple-element.27), channel_id=1, source_target_pairs={{4,0},{8,4},{12,8},{0,12},{5,1},{9,5},{13,9},{1,13},{6,2},{10,6},{... | collective-permute-start | bytes 147464 | tf_op jit(solution)/shard_map/ppermute | solution.py:533
  5.6 4.6 %collective-permute-start.2 = (f32[8,512]{1,0:T(8,128)S(1)}, f32[8,512]{1,0:T(8,128)S(1)}, u32[]{:S(2)}, u32[]{:S(2)}) collective-permute-start(f32[8,512]{1,0:T(8,128)S(1)} %get-tuple-element.41), channel_id=1, source_target_pairs={{0,28},{1,12},{2,13},{3,14},{4,16},{5,0},{6,1},{7,2},{8,20},{9,4},... | collective-permute-start | bytes 49160 | tf_op jit(solution)/shard_map/ppermute | solution.py:553
  10.5 1.8 %collective-permute-start.3 = (f32[88,512]{1,0:T(8,128)S(1)}, f32[88,512]{1,0:T(8,128)S(1)}, u32[]{:S(2)}, u32[]{:S(2)}) collective-permute-start(f32[88,512]{1,0:T(8,128)S(1)} %shard_map.49.refs_0_), channel_id=1, source_target_pairs={{0,16},{16,0},{1,17},{17,1},{2,18},{18,2},{3,19},{19,3},{4,20},{20... | collective-permute-start | bytes 540680 | tf_op jit(solution)/shard_map/ppermute | solution.py:538
  12.4 7.2 %collective-permute-start.7 = (f32[4,16,512]{2,1,0:T(8,128)S(1)}, f32[4,16,512]{2,1,0:T(8,128)S(1)}, u32[]{:S(2)}, u32[]{:S(2)}) collective-permute-start(f32[4,16,512]{2,1,0:T(8,128)S(1)} %get-tuple-element.46), channel_id=1, source_target_pairs={{0,16},{1,0},{2,1},{3,2},{4,20},{5,4},{6,5},{7,6},{8,24},{9,8},{10... | collective-permute-start | bytes 393224 | tf_op jit(solution)/shard_map/ppermute | solution.py:553
  12.8 5.9 %collective-permute-start.4 = (f32[16,512]{1,0:T(8,128)S(1)}, f32[16,512]{1,0:T(8,128)S(1)}, u32[]{:S(2)}, u32[]{:S(2)}) collective-permute-start(f32[16,512]{1,0:T(8,128)S(1)} %get-tuple-element.43), channel_id=1, source_target_pairs={{0,16},{1,17},{2,18},{3,19},{4,20},{5,0},{6,1},{7,2},{8,24},{9,4},... | collective-permute-start | bytes 98312 | tf_op jit(solution)/shard_map/ppermute | solution.py:553
  14.1 4.6 %collective-permute-start.5 = (f32[16,512]{1,0:T(8,128)S(1)}, f32[16,512]{1,0:T(8,128)S(1)}, u32[]{:S(2)}, u32[]{:S(2)}) collective-permute-start(f32[16,512]{1,0:T(8,128)S(1)} %get-tuple-element.44), channel_id=1, source_target_pairs={{0,16},{1,4},{2,5},{3,6},{4,20},{5,8},{6,9},{7,10},{8,24},{9,12},{... | collective-permute-start | bytes 98312 | tf_op jit(solution)/shard_map/ppermute | solution.py:553
  15.7 3.9 %collective-permute-start.6 = (f32[16,512]{1,0:T(8,128)S(1)}, f32[16,512]{1,0:T(8,128)S(1)}, u32[]{:S(2)}, u32[]{:S(2)}) collective-permute-start(f32[16,512]{1,0:T(8,128)S(1)} %get-tuple-element.45), channel_id=1, source_target_pairs={{0,16},{1,17},{2,18},{3,19},{4,0},{5,1},{6,2},{7,3},{8,4},{9,5},{1... | collective-permute-start | bytes 98312 | tf_op jit(solution)/shard_map/ppermute | solution.py:553
  19.7 1.4 %collective-permute-start.8 = (f32[4,16,512]{2,1,0:T(8,128)S(1)}, f32[4,16,512]{2,1,0:T(8,128)S(1)}, u32[]{:S(2)}, u32[]{:S(2)}) collective-permute-start(f32[4,16,512]{2,1,0:T(8,128)S(1)} %shard_map.51.part), channel_id=1, source_target_pairs={{0,16},{16,0},{1,17},{17,1},{2,18},{18,2},{3,19},{19,3},{4,20},{20... | collective-permute-start | bytes 393224 | tf_op jit(solution)/shard_map/ppermute | solution.py:538

commit v25 on v21

--- a/solution.py
+++ b/solution.py
@@ -194,8 +194,8 @@
                 (solid_hbm.at[gives], solid),
                 (fixed_hbm.at[gives], layer_fixed),
                 (disp_hbm.at[:, :, gives], layer),
-                (fixed_hbm.at[:, :TILE], rows_fixed),
-                (disp_hbm.at[:, :, :, :TILE], rows),
+                (fixed_hbm.at[:, :1], rows_fixed),
+                (disp_hbm.at[:, :, :, :1], rows),
             )
         )
     ]
@@ -258,12 +258,13 @@
     base_y = lax.axis_index("sy") * ylen
     inner = zlen - 1
     keeps = jnp.where(on_first(), inner, 0)
+    free = [1.0 - fixed[z].astype(jnp.float32) for z in range(zlen)]
 
     @pl.loop(0, loads * comps, unroll=True)
     def _(k):
         case, comp = k // comps, k % comps
         for z in range(zlen):
-            whole, change = split_x(held(disp, fixed, case, comp, z, slice(None)))
+            whole, change = split_x(disp[case, comp, z] * free[z])
             plus[k, z, :ylen] = whole
             diff[k, z, :ylen] = change
         last_plus[k] = plus[k, keeps, :ylen]
@@ -563,8 +564,8 @@
             pltpu.VMEM((ylen, xlen), jnp.int32),
             pltpu.VMEM((ylen, xlen), jnp.float32),
             pltpu.VMEM((ylen, xlen), jnp.int32),
-            pltpu.VMEM((loads, comps, zlen, TILE, xlen), jnp.float32),
-            pltpu.VMEM((zlen, TILE, xlen), jnp.int32),
+            pltpu.VMEM((loads, comps, zlen, 1, xlen), jnp.float32),
+            pltpu.VMEM((zlen, 1, xlen), jnp.int32),
             pltpu.SemaphoreType.DMA((6,)),
         ],
         space=pltpu.HBM,

time: 21.7 us -> 21.6 us (level)
  no operation moved by 1% of the time
where the time goes in v25:
time: 21.6 us; the launch traced here: 21.4 us
  starting transfers between devices  9.08 us (42%)
  waiting for transfers between devices  6.7 us (31%)
  Pallas kernels  5.56 us (26%)
    pallas_call x7, Pallas kernels, call(): pl.pallas_call(kernel, out_shape=shapes, in_specs=[pl.BlockSpec(memory_sp...  5.56 us
    ppermute x6, starting transfers between devices, opposed(): return lax.ppermute(value, ('load', 'sy', 'sz'), pairs)  4.7 us
    ppermute x6, waiting for transfers between devices, opposed(): return lax.ppermute(value, ('load', 'sy', 'sz'), pairs)  4.31 us
    ppermute x1, starting transfers between devices, ring_moved(): return lax.ppermute(value, axis, [((k + 1) % size, k) for k in range(size)])  3.51 us
    ppermute x2, waiting for transfers between devices, chip_swapped(): lax.ppermute(value, 'load', [(core, cores - 1 - core) for core in range(c...  2.38 us
    ppermute x2, starting transfers between devices, chip_swapped(): lax.ppermute(value, 'load', [(core, cores - 1 - core) for core in range(c...  0.88 us
  transfers between devices with their start and end apart: 9, of which 5 were waited for; matrix products, arithmetic and copies ran while one was open for 0% of the time, Pallas kernels for 15%

profile of v25, /device:TPU:0, one launch (start us, length us, event | category | flops | bytes accessed | tf_op | source)
XLA Modules:
  0.0 21.4 jit_solution(16825222169635855297)
XLA Ops:
  0.0 0.0 copy-start.1
  0.0 0.0 copy-start.3
  0.0 0.0 copy-start.2
  0.0 0.0 copy-start
  0.0 1.2 %shard_map.46 = (f32[8,512]{1,0:T(8,128)S(1)}, f32[7,16,512]{2,1,0:T(8,128)S(1)}, f32[24,512]{1,0:T(8,128)S(1)}) custom-call(f32[2,3,4,16,512]{4,3,2,1,0:T(8,128)} %refs_0_.3, s32[4,16,512]{2,1,0:T(8,128)} %refs_1_.3, f32[4,16,512]{2,1,0:T(8,128)} %refs_2_.3, s32[4,16,512]{2,1,0:T(8,128)} %refs_3_.3), custom_call_target="tpu_custom_call" | custom-call | tf_op jit(solution)/shard_map/pallas_call | solution.py:515
  1.2 0.5 %collective-permute-start = (f32[7,16,512]{2,1,0:T(8,128)S(1)}, f32[7,16,512]{2,1,0:T(8,128)S(1)}, u32[]{:S(2)}, u32[]{:S(2)}) collective-permute-start(f32[7,16,512]{2,1,0:T(8,128)S(1)} %get-tuple-element.22), channel_id=1, source_target_pairs={{0,16},{1,0},{2,1},{3,2},{4,20},{5,4},{6,5},{7,6},{8,24},{9,8},{10... | collective-permute-start | bytes 688136 | tf_op jit(solution)/shard_map/ppermute | solution.py:547
  1.7 3.5 %collective-permute-start.1 = (f32[24,512]{1,0:T(8,128)S(1)}, f32[24,512]{1,0:T(8,128)S(1)}, u32[]{:S(2)}, u32[]{:S(2)}) collective-permute-start(f32[24,512]{1,0:T(8,128)S(1)} %get-tuple-element.23), channel_id=1, source_target_pairs={{4,0},{8,4},{12,8},{0,12},{5,1},{9,5},{13,9},{1,13},{6,2},{10,6},{... | collective-permute-start | bytes 147464 | tf_op jit(solution)/shard_map/ppermute | solution.py:527
  5.2 0.9 %collective-permute-start.2 = (f32[8,512]{1,0:T(8,128)S(1)}, f32[8,512]{1,0:T(8,128)S(1)}, u32[]{:S(2)}, u32[]{:S(2)}) collective-permute-start(f32[8,512]{1,0:T(8,128)S(1)} %get-tuple-element.33), channel_id=1, source_target_pairs={{0,28},{1,12},{2,13},{3,14},{4,16},{5,0},{6,1},{7,2},{8,20},{9,4},... | collective-permute-start | bytes 49160 | tf_op jit(solution)/shard_map/ppermute | solution.py:547
  6.1 0.0 copy-done.1
  6.1 0.0 copy-done.3
  6.1 0.0 copy-done.2
  6.1 0.0 copy-done
  6.1 2.3 %shard_map.47 = (f32[4,16,512]{2,1,0:T(8,128)S(1)}, f32[2,24,512]{2,1,0:T(8,128)S(1)}, f32[2,9,512]{2,1,0:T(8,128)S(1)}, f32[6,16,512]{2,1,0:T(8,128)S(1)}, f32[...) custom-call(f32[2,3,4,16,512]{4,3,2,1,0:T(8,128)S(1)} %copy-done, s32[4,16,512]{2,1,0:T(8,128)S(1)} %copy-done.1, ...), custom_call_target="tpu_custom_call" | custom-call | tf_op jit(solution)/shard_map/pallas_call | solution.py:515
  8.5 0.0 collective-permute-done.1.refs_1_.refs_2_
  8.5 0.0 collective-permute-done.refs_0_
  8.5 0.9 %shard_map.48 = (f32[88,512]{1,0:T(8,128)S(1)}, f32[4,8,512]{2,1,0:T(8,128)S(1)}) custom-call(f32[7,16,512]{2,1,0:T(8,128)S(1)} %collective-permute-done.refs_0_, f32[24,512]{1,0:T(8,128)S(1)} %collective-permute-done.1.refs_1_.refs_2_, f32[4,16,512]{2,1,0:T(8,128)S(1)} %get-tuple-element.24.refs_2_, f32[2,24,512]{2,1,0:T(8,128)S(1)} %get-tuple-element.25.refs_3_, ...), custom_call_target="tpu_custom_call" | custom-call | tf_op jit(solution)/shard_map/pallas_call | solution.py:515
  9.4 0.4 %collective-permute-done.2.refs_3_ = f32[8,512]{1,0:T(8,128)S(1)} collective-permute-done((f32[8,512]{1,0:T(8,128)S(1)}, f32[8,512]{1,0:T(8,128)S(1)}, u32[]{:S(2)}, u32[]{:S(2)}) %collective-permute-start.2) | collective-permute-done | bytes 16416 | tf_op jit(solution)/shard_map/ppermute | solution.py:547
  9.8 0.3 %shard_map.49.refs_0_ = f32[88,512]{1,0:T(8,128)S(1)} custom-call(f32[88,512]{1,0:T(8,128)S(1)} %get-tuple-element.31.refs_0_, f32[4,8,512]{2,1,0:T(8,128)S(1)} %get-tuple-element.32.refs_1_, f32[24,512]{1,0:T(8,128)S(1)} %collective-permute-done.1.refs_1_.refs_2_, f32[8,512]{1,0:T(8,128)S(1)} %collective-permute-done.2.refs_3_), custom_call_target="tpu_custom_call" | custom-call | tf_op jit(solution)/shard_map/pallas_call | solution.py:515
  10.1 0.8 %collective-permute-start.3 = (f32[88,512]{1,0:T(8,128)S(1)}, f32[88,512]{1,0:T(8,128)S(1)}, u32[]{:S(2)}, u32[]{:S(2)}) collective-permute-start(f32[88,512]{1,0:T(8,128)S(1)} %shard_map.49.refs_0_), channel_id=1, source_target_pairs={{0,16},{16,0},{1,17},{17,1},{2,18},{18,2},{3,19},{19,3},{4,20},{20... | collective-permute-start | bytes 540680 | tf_op jit(solution)/shard_map/ppermute | solution.py:532
  10.9 1.0 %collective-permute-done.3.refs_1_ = f32[88,512]{1,0:T(8,128)S(1)} collective-permute-done((f32[88,512]{1,0:T(8,128)S(1)}, f32[88,512]{1,0:T(8,128)S(1)}, u32[]{:S(2)}, u32[]{:S(2)}) %collective-permute-start.3) | collective-permute-done | bytes 180256 | tf_op jit(solution)/shard_map/ppermute | solution.py:532
  12.0 0.4 %collective-permute-start.7 = (f32[4,16,512]{2,1,0:T(8,128)S(1)}, f32[4,16,512]{2,1,0:T(8,128)S(1)}, u32[]{:S(2)}, u32[]{:S(2)}) collective-permute-start(f32[4,16,512]{2,1,0:T(8,128)S(1)} %get-tuple-element.38), channel_id=1, source_target_pairs={{0,16},{1,0},{2,1},{3,2},{4,20},{5,4},{6,5},{7,6},{8,24},{9,8},{10... | collective-permute-start | bytes 393224 | tf_op jit(solution)/shard_map/ppermute | solution.py:547
  12.4 1.3 %collective-permute-start.4 = (f32[16,512]{1,0:T(8,128)S(1)}, f32[16,512]{1,0:T(8,128)S(1)}, u32[]{:S(2)}, u32[]{:S(2)}) collective-permute-start(f32[16,512]{1,0:T(8,128)S(1)} %get-tuple-element.35), channel_id=1, source_target_pairs={{0,16},{1,17},{2,18},{3,19},{4,20},{5,0},{6,1},{7,2},{8,24},{9,4},... | collective-permute-start | bytes 98312 | tf_op jit(solution)/shard_map/ppermute | solution.py:547
  13.7 1.6 %collective-permute-start.5 = (f32[16,512]{1,0:T(8,128)S(1)}, f32[16,512]{1,0:T(8,128)S(1)}, u32[]{:S(2)}, u32[]{:S(2)}) collective-permute-start(f32[16,512]{1,0:T(8,128)S(1)} %get-tuple-element.36), channel_id=1, source_target_pairs={{0,16},{1,4},{2,5},{3,6},{4,20},{5,8},{6,9},{7,10},{8,24},{9,12},{... | collective-permute-start | bytes 98312 | tf_op jit(solution)/shard_map/ppermute | solution.py:547
  15.3 0.0 collective-permute-start.6
  15.3 3.0 %collective-permute-done.4.d_in = f32[16,512]{1,0:T(8,128)S(1)} collective-permute-done((f32[16,512]{1,0:T(8,128)S(1)}, f32[16,512]{1,0:T(8,128)S(1)}, u32[]{:S(2)}, u32[]{:S(2)}) %collective-permute-start.4) | collective-permute-done | bytes 32800 | tf_op jit(solution)/shard_map/ppermute | solution.py:547
  18.3 0.0 collective-permute-done.5.e_in
  18.3 0.9 %collective-permute-done.6.y_in = f32[16,512]{1,0:T(8,128)S(1)} collective-permute-done((f32[16,512]{1,0:T(8,128)S(1)}, f32[16,512]{1,0:T(8,128)S(1)}, u32[]{:S(2)}, u32[]{:S(2)}) %collective-permute-start.6) | collective-permute-done | bytes 32800 | tf_op jit(solution)/shard_map/ppermute | solution.py:547
  19.2 0.0 collective-permute-done.7.z_in
  19.2 0.1 shard_map.51.part
  19.3 0.1 collective-permute-start.8
  19.4 1.3 %collective-permute-done.8.other = f32[4,16,512]{2,1,0:T(8,128)S(1)} collective-permute-done((f32[4,16,512]{2,1,0:T(8,128)S(1)}, f32[4,16,512]{2,1,0:T(8,128)S(1)}, u32[]{:S(2)}, u32[]{:S(2)}) %collective-permute-start.8) | collective-permute-done | bytes 131104 | tf_op jit(solution)/shard_map/ppermute | solution.py:532
  20.8 0.7 %shard_map.52 = f32[4,16,512]{2,1,0:T(8,128)} custom-call(f32[4,16,512]{2,1,0:T(8,128)S(1)} %shard_map.51.part, f32[4,16,512]{2,1,0:T(8,128)S(1)} %collective-permute-done.8.other), custom_call_target="tpu_custom_call" | custom-call | tf_op jit(solution)/shard_map/pallas_call | solution.py:515
  (1 shorter events, 0.0 us)
Async XLA Ops:
  0.0 6.1 %copy-start.1 = (s32[4,16,512]{2,1,0:T(8,128)S(1)}, s32[4,16,512]{2,1,0:T(8,128)}, u32[]{:S(2)}) copy-start(s32[4,16,512]{2,1,0:T(8,128)} %refs_1_.3) | copy-start | bytes 393220
  0.0 6.1 %copy-start.3 = (s32[4,16,512]{2,1,0:T(8,128)S(1)}, s32[4,16,512]{2,1,0:T(8,128)}, u32[]{:S(2)}) copy-start(s32[4,16,512]{2,1,0:T(8,128)} %refs_3_.3) | copy-start | bytes 393220
  0.0 6.1 %copy-start.2 = (f32[4,16,512]{2,1,0:T(8,128)S(1)}, f32[4,16,512]{2,1,0:T(8,128)}, u32[]{:S(2)}) copy-start(f32[4,16,512]{2,1,0:T(8,128)} %refs_2_.3) | copy-start | bytes 393220
  0.0 6.1 %copy-start = (f32[2,3,4,16,512]{4,3,2,1,0:T(8,128)S(1)}, f32[2,3,4,16,512]{4,3,2,1,0:T(8,128)}, u32[]{:S(2)}) copy-start(f32[2,3,4,16,512]{4,3,2,1,0:T(8,128)} %refs_0_.3) | copy-start | bytes 2359300
  1.2 7.3 %collective-permute-start = (f32[7,16,512]{2,1,0:T(8,128)S(1)}, f32[7,16,512]{2,1,0:T(8,128)S(1)}, u32[]{:S(2)}, u32[]{:S(2)}) collective-permute-start(f32[7,16,512]{2,1,0:T(8,128)S(1)} %get-tuple-element.22), channel_id=1, source_target_pairs={{0,16},{1,0},{2,1},{3,2},{4,20},{5,4},{6,5},{7,6},{8,24},{9,8},{10... | collective-permute-start | bytes 688136 | tf_op jit(solution)/shard_map/ppermute | solution.py:547
  1.7 6.8 %collective-permute-start.1 = (f32[24,512]{1,0:T(8,128)S(1)}, f32[24,512]{1,0:T(8,128)S(1)}, u32[]{:S(2)}, u32[]{:S(2)}) collective-permute-start(f32[24,512]{1,0:T(8,128)S(1)} %get-tuple-element.23), channel_id=1, source_target_pairs={{4,0},{8,4},{12,8},{0,12},{5,1},{9,5},{13,9},{1,13},{6,2},{10,6},{... | collective-permute-start | bytes 147464 | tf_op jit(solution)/shard_map/ppermute | solution.py:527
  5.2 4.6 %collective-permute-start.2 = (f32[8,512]{1,0:T(8,128)S(1)}, f32[8,512]{1,0:T(8,128)S(1)}, u32[]{:S(2)}, u32[]{:S(2)}) collective-permute-start(f32[8,512]{1,0:T(8,128)S(1)} %get-tuple-element.33), channel_id=1, source_target_pairs={{0,28},{1,12},{2,13},{3,14},{4,16},{5,0},{6,1},{7,2},{8,20},{9,4},... | collective-permute-start | bytes 49160 | tf_op jit(solution)/shard_map/ppermute | solution.py:547
  10.1 1.9 %collective-permute-start.3 = (f32[88,512]{1,0:T(8,128)S(1)}, f32[88,512]{1,0:T(8,128)S(1)}, u32[]{:S(2)}, u32[]{:S(2)}) collective-permute-start(f32[88,512]{1,0:T(8,128)S(1)} %shard_map.49.refs_0_), channel_id=1, source_target_pairs={{0,16},{16,0},{1,17},{17,1},{2,18},{18,2},{3,19},{19,3},{4,20},{20... | collective-permute-start | bytes 540680 | tf_op jit(solution)/shard_map/ppermute | solution.py:532
  12.0 7.2 %collective-permute-start.7 = (f32[4,16,512]{2,1,0:T(8,128)S(1)}, f32[4,16,512]{2,1,0:T(8,128)S(1)}, u32[]{:S(2)}, u32[]{:S(2)}) collective-permute-start(f32[4,16,512]{2,1,0:T(8,128)S(1)} %get-tuple-element.38), channel_id=1, source_target_pairs={{0,16},{1,0},{2,1},{3,2},{4,20},{5,4},{6,5},{7,6},{8,24},{9,8},{10... | collective-permute-start | bytes 393224 | tf_op jit(solution)/shard_map/ppermute | solution.py:547
  12.4 5.9 %collective-permute-start.4 = (f32[16,512]{1,0:T(8,128)S(1)}, f32[16,512]{1,0:T(8,128)S(1)}, u32[]{:S(2)}, u32[]{:S(2)}) collective-permute-start(f32[16,512]{1,0:T(8,128)S(1)} %get-tuple-element.35), channel_id=1, source_target_pairs={{0,16},{1,17},{2,18},{3,19},{4,20},{5,0},{6,1},{7,2},{8,24},{9,4},... | collective-permute-start | bytes 98312 | tf_op jit(solution)/shard_map/ppermute | solution.py:547
  13.7 4.6 %collective-permute-start.5 = (f32[16,512]{1,0:T(8,128)S(1)}, f32[16,512]{1,0:T(8,128)S(1)}, u32[]{:S(2)}, u32[]{:S(2)}) collective-permute-start(f32[16,512]{1,0:T(8,128)S(1)} %get-tuple-element.36), channel_id=1, source_target_pairs={{0,16},{1,4},{2,5},{3,6},{4,20},{5,8},{6,9},{7,10},{8,24},{9,12},{... | collective-permute-start | bytes 98312 | tf_op jit(solution)/shard_map/ppermute | solution.py:547
  15.3 3.9 %collective-permute-start.6 = (f32[16,512]{1,0:T(8,128)S(1)}, f32[16,512]{1,0:T(8,128)S(1)}, u32[]{:S(2)}, u32[]{:S(2)}) collective-permute-start(f32[16,512]{1,0:T(8,128)S(1)} %get-tuple-element.37), channel_id=1, source_target_pairs={{0,16},{1,17},{2,18},{3,19},{4,0},{5,1},{6,2},{7,3},{8,4},{9,5},{1... | collective-permute-start | bytes 98312 | tf_op jit(solution)/shard_map/ppermute | solution.py:547
  19.3 1.4 %collective-permute-start.8 = (f32[4,16,512]{2,1,0:T(8,128)S(1)}, f32[4,16,512]{2,1,0:T(8,128)S(1)}, u32[]{:S(2)}, u32[]{:S(2)}) collective-permute-start(f32[4,16,512]{2,1,0:T(8,128)S(1)} %shard_map.51.part), channel_id=1, source_target_pairs={{0,16},{16,0},{1,17},{17,1},{2,18},{18,2},{3,19},{19,3},{4,20},{20... | collective-permute-start | bytes 393224 | tf_op jit(solution)/shard_map/ppermute | solution.py:532

commit v26 on v25

--- a/solution.py
+++ b/solution.py
@@ -177,6 +177,10 @@
         ahead.append(sum(float(REACH - row - k) * top[TILE - 1 - k : TILE - k] for k in range(REACH - row)))
         back.append(sum(float(row + 1 - k) * base[k : k + 1] for k in range(row + 1)))
     return ahead, back
+
+
+def next_is_partner(start):
+    return (lax.axis_index("sy") - start) % 2 == 0
 
 
 def on_first():
@@ -457,8 +461,9 @@
     y_out[: reach + REACH] = jnp.where(first_core, downs, ups)
     for out, used in ((y_out, reach + REACH), (d_out, reach), (e_out, reach)):
         out[used:] = jnp.zeros((out.shape[0] - used, xlen), jnp.float32)
-    d_out[:reach] = jnp.where(first_core, downs[:reach], ups[REACH:])
-    e_out[:reach] = jnp.where(first_core, ups[:reach], downs[REACH:])
+    for out, start in ((d_out, 1), (e_out, 0)):
+        rows = jnp.where(next_is_partner(start), ups, downs)
+        out[:reach] = jnp.where(first_core, rows[:reach], rows[REACH:])
 
 
 def layers_kernel(h, d_in, e_in, y_in, z_in, out):
@@ -469,7 +474,8 @@
     y_index, y_last = lax.axis_index("sy"), lax.axis_size("sy") - 1
     z_side = jnp.where(first_core, z_index < z_last, z_index > 0)
     y_side = jnp.where(first_core, y_index < y_last, y_index > 0)
-    y_other = jnp.where(first_core, y_index > 0, y_index < y_last)
+    d_next, e_next = next_is_partner(1), next_is_partner(0)
+    d_side, e_side = (jnp.where(up, y_index < y_last, y_index > 0) for up in (d_next, e_next))
     blank = jnp.zeros((TILE - REACH, xlen), jnp.float32)
 
     def at_start(rows):
@@ -496,9 +502,7 @@
     for k in range(zlen):
         part = slice(REACH * k, REACH * (k + 1))
         layer = jnp.where(z_side, z_in[k], 0.0)
-        straight = ends(d_in[part], z_side & y_side, first_core)
-        across = ends(e_in[part], z_side & y_other, jnp.logical_not(first_core))
-        come.append(with_ends(layer, straight, across))
+        come.append(with_ends(layer, ends(d_in[part], z_side & d_side, d_next), ends(e_in[part], z_side & e_side, e_next)))
     below = [jnp.where(first_core, 0.0, layer) for layer in come[zlen - REACH :]]
     above = [jnp.where(first_core, layer, 0.0) for layer in come]
     layers = below[:-1] + [below[-1] + own[0]] + own[1:-1] + [own[-1] + above[0]] + above[1:]
@@ -532,7 +536,7 @@
     return lax.ppermute(value, "load", [(core, cores - 1 - core) for core in range(cores)])
 
 
-def opposed(value, z_step, y_step, y_shift=0):
+def opposed(value, z_step, y_step, y_shift=0, start=None):
     cores, rows, size = lax.axis_size("load"), lax.axis_size("sy"), lax.axis_size("sz")
     pairs = []
     for core in range(cores):
@@ -540,6 +544,8 @@
         for y in range(rows):
             for z in range(size):
                 to_y, to_z, side = y + sign * y_step, z + sign * z_step, core
+                if start is not None:
+                    to_y = y + 1 if (y - start) % 2 == 0 else y - 1
                 if not (0 <= to_y < rows and 0 <= to_z < size):
                     to_y, to_z, side = y, z, cores - 1 - core
                 to_y = (to_y + y_shift) % rows
@@ -616,8 +622,8 @@
         ],
         (share, chip_swapped(share)),
     )
-    d_in = opposed(d_send, -1, -1)
-    e_in = opposed(e_send, -1, 1)
+    d_in = opposed(d_send, -1, 0, start=1)
+    e_in = opposed(e_send, -1, 0, start=0)
     y_in = opposed(y_send, 0, -1)
     z_in = opposed(z_send, -1, 0)
     (part,) = call(layers_kernel, [(zlen, ylen, xlen)], (h, d_in, e_in, y_in, z_in))

time: 21.6 us -> 21.5 us (level)
  waiting for transfers between devices: 6.7 us -> 5.3 us
  starting transfers between devices: 9.08 us -> 10.4 us
    ppermute x6, waiting for transfers between devices: 4.31 us -> 2.92 us  [opposed(): return lax.ppermute(value, ('load', 'sy', 'sz'), pairs)]
    ppermute x6, starting transfers between devices: 4.7 us -> 6.04 us  [opposed(): return lax.ppermute(value, ('load', 'sy', 'sz'), pairs)]
where the time goes in v26:
time: 21.5 us; the launch traced here: 21.4 us
  starting transfers between devices  10.4 us (48%)
  Pallas kernels  5.56 us (26%)
  waiting for transfers between devices  5.3 us (25%)
    ppermute x6, starting transfers between devices, opposed(): return lax.ppermute(value, ('load', 'sy', 'sz'), pairs)  6.04 us
    pallas_call x7, Pallas kernels, call(): pl.pallas_call(kernel, out_shape=shapes, in_specs=[pl.BlockSpec(memory_sp...  5.56 us
    ppermute x1, starting transfers between devices, ring_moved(): return lax.ppermute(value, axis, [((k + 1) % size, k) for k in range(size)])  3.51 us
    ppermute x6, waiting for transfers between devices, opposed(): return lax.ppermute(value, ('load', 'sy', 'sz'), pairs)  2.92 us
    ppermute x2, waiting for transfers between devices, chip_swapped(): lax.ppermute(value, 'load', [(core, cores - 1 - core) for core in range(c...  2.38 us
    ppermute x2, starting transfers between devices, chip_swapped(): lax.ppermute(value, 'load', [(core, cores - 1 - core) for core in range(c...  0.88 us
  transfers between devices with their start and end apart: 9, of which 5 were waited for; matrix products, arithmetic and copies ran while one was open for 0% of the time, Pallas kernels for 15%

profile of v26, /device:TPU:0, one launch (start us, length us, event | category | flops | bytes accessed | tf_op | source)
XLA Modules:
  0.0 21.4 jit_solution(10946429640991046800)
XLA Ops:
  0.0 0.0 copy-start.1
  0.0 0.0 copy-start.3
  0.0 0.0 copy-start.2
  0.0 1.2 %shard_map.46 = (f32[8,512]{1,0:T(8,128)S(1)}, f32[7,16,512]{2,1,0:T(8,128)S(1)}, f32[24,512]{1,0:T(8,128)S(1)}) custom-call(f32[2,3,4,16,512]{4,3,2,1,0:T(8,128)} %refs_0_.3, s32[4,16,512]{2,1,0:T(8,128)} %refs_1_.3, f32[4,16,512]{2,1,0:T(8,128)} %refs_2_.3, s32[4,16,512]{2,1,0:T(8,128)} %refs_3_.3), custom_call_target="tpu_custom_call" | custom-call | tf_op jit(solution)/shard_map/pallas_call | solution.py:519
  1.2 0.5 %collective-permute-start = (f32[7,16,512]{2,1,0:T(8,128)S(1)}, f32[7,16,512]{2,1,0:T(8,128)S(1)}, u32[]{:S(2)}, u32[]{:S(2)}) collective-permute-start(f32[7,16,512]{2,1,0:T(8,128)S(1)} %get-tuple-element.22), channel_id=1, source_target_pairs={{0,16},{1,0},{2,1},{3,2},{4,20},{5,4},{6,5},{7,6},{8,24},{9,8},{10... | collective-permute-start | bytes 688136 | tf_op jit(solution)/shard_map/ppermute | solution.py:553
  1.7 3.5 %collective-permute-start.1 = (f32[24,512]{1,0:T(8,128)S(1)}, f32[24,512]{1,0:T(8,128)S(1)}, u32[]{:S(2)}, u32[]{:S(2)}) collective-permute-start(f32[24,512]{1,0:T(8,128)S(1)} %get-tuple-element.23), channel_id=1, source_target_pairs={{4,0},{8,4},{12,8},{0,12},{5,1},{9,5},{13,9},{1,13},{6,2},{10,6},{... | collective-permute-start | bytes 147464 | tf_op jit(solution)/shard_map/ppermute | solution.py:531
  5.2 0.9 %collective-permute-start.2 = (f32[8,512]{1,0:T(8,128)S(1)}, f32[8,512]{1,0:T(8,128)S(1)}, u32[]{:S(2)}, u32[]{:S(2)}) collective-permute-start(f32[8,512]{1,0:T(8,128)S(1)} %get-tuple-element.33), channel_id=1, source_target_pairs={{0,28},{1,12},{2,13},{3,14},{4,16},{5,0},{6,1},{7,2},{8,20},{9,4},... | collective-permute-start | bytes 49160 | tf_op jit(solution)/shard_map/ppermute | solution.py:553
  6.1 0.0 copy-done.1
  6.1 0.0 copy-done.3
  6.1 0.0 copy-done.2
  6.1 0.0 copy-done
  6.1 2.3 %shard_map.47 = (f32[4,16,512]{2,1,0:T(8,128)S(1)}, f32[2,24,512]{2,1,0:T(8,128)S(1)}, f32[2,9,512]{2,1,0:T(8,128)S(1)}, f32[6,16,512]{2,1,0:T(8,128)S(1)}, f32[...) custom-call(f32[2,3,4,16,512]{4,3,2,1,0:T(8,128)S(1)} %copy-done, s32[4,16,512]{2,1,0:T(8,128)S(1)} %copy-done.1, ...), custom_call_target="tpu_custom_call" | custom-call | tf_op jit(solution)/shard_map/pallas_call | solution.py:519
  8.5 0.0 collective-permute-done.1.refs_1_.refs_2_
  8.5 0.0 collective-permute-done.refs_0_
  8.5 0.9 %shard_map.48 = (f32[88,512]{1,0:T(8,128)S(1)}, f32[4,8,512]{2,1,0:T(8,128)S(1)}) custom-call(f32[7,16,512]{2,1,0:T(8,128)S(1)} %collective-permute-done.refs_0_, f32[24,512]{1,0:T(8,128)S(1)} %collective-permute-done.1.refs_1_.refs_2_, f32[4,16,512]{2,1,0:T(8,128)S(1)} %get-tuple-element.24.refs_2_, f32[2,24,512]{2,1,0:T(8,128)S(1)} %get-tuple-element.25.refs_3_, ...), custom_call_target="tpu_custom_call" | custom-call | tf_op jit(solution)/shard_map/pallas_call | solution.py:519
  9.4 0.4 %collective-permute-done.2.refs_3_ = f32[8,512]{1,0:T(8,128)S(1)} collective-permute-done((f32[8,512]{1,0:T(8,128)S(1)}, f32[8,512]{1,0:T(8,128)S(1)}, u32[]{:S(2)}, u32[]{:S(2)}) %collective-permute-start.2) | collective-permute-done | bytes 16416 | tf_op jit(solution)/shard_map/ppermute | solution.py:553
  9.8 0.3 %shard_map.49.refs_0_ = f32[88,512]{1,0:T(8,128)S(1)} custom-call(f32[88,512]{1,0:T(8,128)S(1)} %get-tuple-element.31.refs_0_, f32[4,8,512]{2,1,0:T(8,128)S(1)} %get-tuple-element.32.refs_1_, f32[24,512]{1,0:T(8,128)S(1)} %collective-permute-done.1.refs_1_.refs_2_, f32[8,512]{1,0:T(8,128)S(1)} %collective-permute-done.2.refs_3_), custom_call_target="tpu_custom_call" | custom-call | tf_op jit(solution)/shard_map/pallas_call | solution.py:519
  10.1 0.8 %collective-permute-start.3 = (f32[88,512]{1,0:T(8,128)S(1)}, f32[88,512]{1,0:T(8,128)S(1)}, u32[]{:S(2)}, u32[]{:S(2)}) collective-permute-start(f32[88,512]{1,0:T(8,128)S(1)} %shard_map.49.refs_0_), channel_id=1, source_target_pairs={{0,16},{16,0},{1,17},{17,1},{2,18},{18,2},{3,19},{19,3},{4,20},{20... | collective-permute-start | bytes 540680 | tf_op jit(solution)/shard_map/ppermute | solution.py:536
  10.9 1.0 %collective-permute-done.3.refs_1_ = f32[88,512]{1,0:T(8,128)S(1)} collective-permute-done((f32[88,512]{1,0:T(8,128)S(1)}, f32[88,512]{1,0:T(8,128)S(1)}, u32[]{:S(2)}, u32[]{:S(2)}) %collective-permute-start.3) | collective-permute-done | bytes 180256 | tf_op jit(solution)/shard_map/ppermute | solution.py:536
  12.0 0.1 shard_map.50
  12.0 0.4 %collective-permute-start.7 = (f32[4,16,512]{2,1,0:T(8,128)S(1)}, f32[4,16,512]{2,1,0:T(8,128)S(1)}, u32[]{:S(2)}, u32[]{:S(2)}) collective-permute-start(f32[4,16,512]{2,1,0:T(8,128)S(1)} %get-tuple-element.38), channel_id=1, source_target_pairs={{0,16},{1,0},{2,1},{3,2},{4,20},{5,4},{6,5},{7,6},{8,24},{9,8},{10... | collective-permute-start | bytes 393224 | tf_op jit(solution)/shard_map/ppermute | solution.py:553
  12.4 1.3 %collective-permute-start.4 = (f32[16,512]{1,0:T(8,128)S(1)}, f32[16,512]{1,0:T(8,128)S(1)}, u32[]{:S(2)}, u32[]{:S(2)}) collective-permute-start(f32[16,512]{1,0:T(8,128)S(1)} %get-tuple-element.35), channel_id=1, source_target_pairs={{0,16},{1,17},{2,18},{3,19},{4,20},{5,8},{6,9},{7,10},{8,24},{9,4}... | collective-permute-start | bytes 98312 | tf_op jit(solution)/shard_map/ppermute | solution.py:553
  13.7 0.0 collective-permute-start.5
  13.7 2.9 %collective-permute-start.6 = (f32[16,512]{1,0:T(8,128)S(1)}, f32[16,512]{1,0:T(8,128)S(1)}, u32[]{:S(2)}, u32[]{:S(2)}) collective-permute-start(f32[16,512]{1,0:T(8,128)S(1)} %get-tuple-element.37), channel_id=1, source_target_pairs={{0,16},{1,17},{2,18},{3,19},{4,0},{5,1},{6,2},{7,3},{8,4},{9,5},{1... | collective-permute-start | bytes 98312 | tf_op jit(solution)/shard_map/ppermute | solution.py:553
  16.6 0.0 collective-permute-done.4.d_in
  16.6 2.0 %collective-permute-done.5.e_in = f32[16,512]{1,0:T(8,128)S(1)} collective-permute-done((f32[16,512]{1,0:T(8,128)S(1)}, f32[16,512]{1,0:T(8,128)S(1)}, u32[]{:S(2)}, u32[]{:S(2)}) %collective-permute-start.5) | collective-permute-done | bytes 32800 | tf_op jit(solution)/shard_map/ppermute | solution.py:553
  18.7 0.5 %collective-permute-done.6.y_in = f32[16,512]{1,0:T(8,128)S(1)} collective-permute-done((f32[16,512]{1,0:T(8,128)S(1)}, f32[16,512]{1,0:T(8,128)S(1)}, u32[]{:S(2)}, u32[]{:S(2)}) %collective-permute-start.6) | collective-permute-done | bytes 32800 | tf_op jit(solution)/shard_map/ppermute | solution.py:553
  19.2 0.0 collective-permute-done.7.z_in
  19.2 0.1 shard_map.51.part
  19.3 0.1 collective-permute-start.8
  19.4 1.3 %collective-permute-done.8.other = f32[4,16,512]{2,1,0:T(8,128)S(1)} collective-permute-done((f32[4,16,512]{2,1,0:T(8,128)S(1)}, f32[4,16,512]{2,1,0:T(8,128)S(1)}, u32[]{:S(2)}, u32[]{:S(2)}) %collective-permute-start.8) | collective-permute-done | bytes 131104 | tf_op jit(solution)/shard_map/ppermute | solution.py:536
  20.7 0.7 %shard_map.52 = f32[4,16,512]{2,1,0:T(8,128)} custom-call(f32[4,16,512]{2,1,0:T(8,128)S(1)} %shard_map.51.part, f32[4,16,512]{2,1,0:T(8,128)S(1)} %collective-permute-done.8.other), custom_call_target="tpu_custom_call" | custom-call | tf_op jit(solution)/shard_map/pallas_call | solution.py:519
  (1 shorter events, 0.0 us)
Async XLA Ops:
  0.0 6.1 %copy-start.1 = (s32[4,16,512]{2,1,0:T(8,128)S(1)}, s32[4,16,512]{2,1,0:T(8,128)}, u32[]{:S(2)}) copy-start(s32[4,16,512]{2,1,0:T(8,128)} %refs_1_.3) | copy-start | bytes 393220
  0.0 6.1 %copy-start.3 = (s32[4,16,512]{2,1,0:T(8,128)S(1)}, s32[4,16,512]{2,1,0:T(8,128)}, u32[]{:S(2)}) copy-start(s32[4,16,512]{2,1,0:T(8,128)} %refs_3_.3) | copy-start | bytes 393220
  0.0 6.1 %copy-start.2 = (f32[4,16,512]{2,1,0:T(8,128)S(1)}, f32[4,16,512]{2,1,0:T(8,128)}, u32[]{:S(2)}) copy-start(f32[4,16,512]{2,1,0:T(8,128)} %refs_2_.3) | copy-start | bytes 393220
  0.0 6.1 %copy-start = (f32[2,3,4,16,512]{4,3,2,1,0:T(8,128)S(1)}, f32[2,3,4,16,512]{4,3,2,1,0:T(8,128)}, u32[]{:S(2)}) copy-start(f32[2,3,4,16,512]{4,3,2,1,0:T(8,128)} %refs_0_.3) | copy-start | bytes 2359300
  1.2 7.3 %collective-permute-start = (f32[7,16,512]{2,1,0:T(8,128)S(1)}, f32[7,16,512]{2,1,0:T(8,128)S(1)}, u32[]{:S(2)}, u32[]{:S(2)}) collective-permute-start(f32[7,16,512]{2,1,0:T(8,128)S(1)} %get-tuple-element.22), channel_id=1, source_target_pairs={{0,16},{1,0},{2,1},{3,2},{4,20},{5,4},{6,5},{7,6},{8,24},{9,8},{10... | collective-permute-start | bytes 688136 | tf_op jit(solution)/shard_map/ppermute | solution.py:553
  1.7 6.8 %collective-permute-start.1 = (f32[24,512]{1,0:T(8,128)S(1)}, f32[24,512]{1,0:T(8,128)S(1)}, u32[]{:S(2)}, u32[]{:S(2)}) collective-permute-start(f32[24,512]{1,0:T(8,128)S(1)} %get-tuple-element.23), channel_id=1, source_target_pairs={{4,0},{8,4},{12,8},{0,12},{5,1},{9,5},{13,9},{1,13},{6,2},{10,6},{... | collective-permute-start | bytes 147464 | tf_op jit(solution)/shard_map/ppermute | solution.py:531
  5.2 4.6 %collective-permute-start.2 = (f32[8,512]{1,0:T(8,128)S(1)}, f32[8,512]{1,0:T(8,128)S(1)}, u32[]{:S(2)}, u32[]{:S(2)}) collective-permute-start(f32[8,512]{1,0:T(8,128)S(1)} %get-tuple-element.33), channel_id=1, source_target_pairs={{0,28},{1,12},{2,13},{3,14},{4,16},{5,0},{6,1},{7,2},{8,20},{9,4},... | collective-permute-start | bytes 49160 | tf_op jit(solution)/shard_map/ppermute | solution.py:553
  10.1 1.9 %collective-permute-start.3 = (f32[88,512]{1,0:T(8,128)S(1)}, f32[88,512]{1,0:T(8,128)S(1)}, u32[]{:S(2)}, u32[]{:S(2)}) collective-permute-start(f32[88,512]{1,0:T(8,128)S(1)} %shard_map.49.refs_0_), channel_id=1, source_target_pairs={{0,16},{16,0},{1,17},{17,1},{2,18},{18,2},{3,19},{19,3},{4,20},{20... | collective-permute-start | bytes 540680 | tf_op jit(solution)/shard_map/ppermute | solution.py:536
  12.0 7.1 %collective-permute-start.7 = (f32[4,16,512]{2,1,0:T(8,128)S(1)}, f32[4,16,512]{2,1,0:T(8,128)S(1)}, u32[]{:S(2)}, u32[]{:S(2)}) collective-permute-start(f32[4,16,512]{2,1,0:T(8,128)S(1)} %get-tuple-element.38), channel_id=1, source_target_pairs={{0,16},{1,0},{2,1},{3,2},{4,20},{5,4},{6,5},{7,6},{8,24},{9,8},{10... | collective-permute-start | bytes 393224 | tf_op jit(solution)/shard_map/ppermute | solution.py:553
  12.4 4.2 %collective-permute-start.4 = (f32[16,512]{1,0:T(8,128)S(1)}, f32[16,512]{1,0:T(8,128)S(1)}, u32[]{:S(2)}, u32[]{:S(2)}) collective-permute-start(f32[16,512]{1,0:T(8,128)S(1)} %get-tuple-element.35), channel_id=1, source_target_pairs={{0,16},{1,17},{2,18},{3,19},{4,20},{5,8},{6,9},{7,10},{8,24},{9,4}... | collective-permute-start | bytes 98312 | tf_op jit(solution)/shard_map/ppermute | solution.py:553
  13.7 5.0 %collective-permute-start.5 = (f32[16,512]{1,0:T(8,128)S(1)}, f32[16,512]{1,0:T(8,128)S(1)}, u32[]{:S(2)}, u32[]{:S(2)}) collective-permute-start(f32[16,512]{1,0:T(8,128)S(1)} %get-tuple-element.36), channel_id=1, source_target_pairs={{0,16},{1,4},{2,5},{3,6},{4,20},{5,0},{6,1},{7,2},{8,24},{9,12},{1... | collective-permute-start | bytes 98312 | tf_op jit(solution)/shard_map/ppermute | solution.py:553
  13.7 5.5 %collective-permute-start.6 = (f32[16,512]{1,0:T(8,128)S(1)}, f32[16,512]{1,0:T(8,128)S(1)}, u32[]{:S(2)}, u32[]{:S(2)}) collective-permute-start(f32[16,512]{1,0:T(8,128)S(1)} %get-tuple-element.37), channel_id=1, source_target_pairs={{0,16},{1,17},{2,18},{3,19},{4,0},{5,1},{6,2},{7,3},{8,4},{9,5},{1... | collective-permute-start | bytes 98312 | tf_op jit(solution)/shard_map/ppermute | solution.py:553
  19.3 1.4 %collective-permute-start.8 = (f32[4,16,512]{2,1,0:T(8,128)S(1)}, f32[4,16,512]{2,1,0:T(8,128)S(1)}, u32[]{:S(2)}, u32[]{:S(2)}) collective-permute-start(f32[4,16,512]{2,1,0:T(8,128)S(1)} %shard_map.51.part), channel_id=1, source_target_pairs={{0,16},{16,0},{1,17},{17,1},{2,18},{18,2},{3,19},{19,3},{4,20},{20... | collective-permute-start | bytes 393224 | tf_op jit(solution)/shard_map/ppermute | solution.py:536

commit v27 on v26

--- a/solution.py
+++ b/solution.py
@@ -466,7 +466,7 @@
         out[:reach] = jnp.where(first_core, rows[:reach], rows[REACH:])
 
 
-def layers_kernel(h, d_in, e_in, y_in, z_in, out):
+def layers_kernel(h, d_in, y_in, e_in, z_in, out):
     zlen, ylen, xlen = out.shape
     reach = REACH * zlen
     first_core = on_first()
@@ -626,7 +626,7 @@
     e_in = opposed(e_send, -1, 0, start=0)
     y_in = opposed(y_send, 0, -1)
     z_in = opposed(z_send, -1, 0)
-    (part,) = call(layers_kernel, [(zlen, ylen, xlen)], (h, d_in, e_in, y_in, z_in))
+    (part,) = call(layers_kernel, [(zlen, ylen, xlen)], (h, d_in, y_in, e_in, z_in))
     (out,) = call(sum_kernel, [(zlen, ylen, xlen)], (part, chip_swapped(part)))
     return out
 

time: 21.5 us -> 21.8 us (1.014)
  starting transfers between devices: 10.4 us -> 11.5 us
  waiting for transfers between devices: 5.3 us -> 4.56 us
    ppermute x2, starting transfers between devices: 0.88 us -> 2.08 us  [chip_swapped(): lax.ppermute(value, 'load', [(core, cores - 1 - core) for core in range(c...]
    ppermute x6, waiting for transfers between devices: 2.92 us -> 2.52 us  [opposed(): return lax.ppermute(value, ('load', 'sy', 'sz'), pairs)]
    ppermute x2, waiting for transfers between devices: 2.38 us -> 2.04 us  [chip_swapped(): lax.ppermute(value, 'load', [(core, cores - 1 - core) for core in range(c...]
where the time goes in v27:
time: 21.8 us; the launch traced here: 21.7 us
  starting transfers between devices  11.5 us (53%)
  Pallas kernels  5.56 us (26%)
  waiting for transfers between devices  4.56 us (21%)
    ppermute x6, starting transfers between devices, opposed(): return lax.ppermute(value, ('load', 'sy', 'sz'), pairs)  5.9 us
    pallas_call x7, Pallas kernels, call(): pl.pallas_call(kernel, out_shape=shapes, in_specs=[pl.BlockSpec(memory_sp...  5.56 us
    ppermute x1, starting transfers between devices, ring_moved(): return lax.ppermute(value, axis, [((k + 1) % size, k) for k in range(size)])  3.51 us
    ppermute x6, waiting for transfers between devices, opposed(): return lax.ppermute(value, ('load', 'sy', 'sz'), pairs)  2.52 us
    ppermute x2, starting transfers between devices, chip_swapped(): lax.ppermute(value, 'load', [(core, cores - 1 - core) for core in range(c...  2.08 us
    ppermute x2, waiting for transfers between devices, chip_swapped(): lax.ppermute(value, 'load', [(core, cores - 1 - core) for core in range(c...  2.04 us
  transfers between devices with their start and end apart: 9, of which 5 were waited for; matrix products, arithmetic and copies ran while one was open for 0% of the time, Pallas kernels for 15%

profile of v27, /device:TPU:0, one launch (start us, length us, event | category | flops | bytes accessed | tf_op | source)
XLA Modules:
  0.0 21.7 jit_solution(7073951822022387335)
XLA Ops:
  0.0 0.0 copy-start.1
  0.0 0.0 copy-start.3
  0.0 0.0 copy-start.2
  0.0 1.2 %shard_map.46 = (f32[8,512]{1,0:T(8,128)S(1)}, f32[7,16,512]{2,1,0:T(8,128)S(1)}, f32[24,512]{1,0:T(8,128)S(1)}) custom-call(f32[2,3,4,16,512]{4,3,2,1,0:T(8,128)} %refs_0_.3, s32[4,16,512]{2,1,0:T(8,128)} %refs_1_.3, f32[4,16,512]{2,1,0:T(8,128)} %refs_2_.3, s32[4,16,512]{2,1,0:T(8,128)} %refs_3_.3), custom_call_target="tpu_custom_call" | custom-call | tf_op jit(solution)/shard_map/pallas_call | solution.py:519
  1.2 0.5 %collective-permute-start = (f32[7,16,512]{2,1,0:T(8,128)S(1)}, f32[7,16,512]{2,1,0:T(8,128)S(1)}, u32[]{:S(2)}, u32[]{:S(2)}) collective-permute-start(f32[7,16,512]{2,1,0:T(8,128)S(1)} %get-tuple-element.22), channel_id=1, source_target_pairs={{0,16},{1,0},{2,1},{3,2},{4,20},{5,4},{6,5},{7,6},{8,24},{9,8},{10... | collective-permute-start | bytes 688136 | tf_op jit(solution)/shard_map/ppermute | solution.py:553
  1.7 3.5 %collective-permute-start.1 = (f32[24,512]{1,0:T(8,128)S(1)}, f32[24,512]{1,0:T(8,128)S(1)}, u32[]{:S(2)}, u32[]{:S(2)}) collective-permute-start(f32[24,512]{1,0:T(8,128)S(1)} %get-tuple-element.23), channel_id=1, source_target_pairs={{4,0},{8,4},{12,8},{0,12},{5,1},{9,5},{13,9},{1,13},{6,2},{10,6},{... | collective-permute-start | bytes 147464 | tf_op jit(solution)/shard_map/ppermute | solution.py:531
  5.2 0.9 %collective-permute-start.2 = (f32[8,512]{1,0:T(8,128)S(1)}, f32[8,512]{1,0:T(8,128)S(1)}, u32[]{:S(2)}, u32[]{:S(2)}) collective-permute-start(f32[8,512]{1,0:T(8,128)S(1)} %get-tuple-element.33), channel_id=1, source_target_pairs={{0,28},{1,12},{2,13},{3,14},{4,16},{5,0},{6,1},{7,2},{8,20},{9,4},... | collective-permute-start | bytes 49160 | tf_op jit(solution)/shard_map/ppermute | solution.py:553
  6.1 0.0 copy-done.1
  6.1 0.0 copy-done.3
  6.1 0.0 copy-done.2
  6.1 0.0 copy-done
  6.1 2.3 %shard_map.47 = (f32[4,16,512]{2,1,0:T(8,128)S(1)}, f32[2,24,512]{2,1,0:T(8,128)S(1)}, f32[2,9,512]{2,1,0:T(8,128)S(1)}, f32[6,16,512]{2,1,0:T(8,128)S(1)}, f32[...) custom-call(f32[2,3,4,16,512]{4,3,2,1,0:T(8,128)S(1)} %copy-done, s32[4,16,512]{2,1,0:T(8,128)S(1)} %copy-done.1, ...), custom_call_target="tpu_custom_call" | custom-call | tf_op jit(solution)/shard_map/pallas_call | solution.py:519
  8.5 0.0 collective-permute-done.1.refs_1_.refs_2_
  8.5 0.0 collective-permute-done.refs_0_
  8.5 0.9 %shard_map.48 = (f32[88,512]{1,0:T(8,128)S(1)}, f32[4,8,512]{2,1,0:T(8,128)S(1)}) custom-call(f32[7,16,512]{2,1,0:T(8,128)S(1)} %collective-permute-done.refs_0_, f32[24,512]{1,0:T(8,128)S(1)} %collective-permute-done.1.refs_1_.refs_2_, f32[4,16,512]{2,1,0:T(8,128)S(1)} %get-tuple-element.24.refs_2_, f32[2,24,512]{2,1,0:T(8,128)S(1)} %get-tuple-element.25.refs_3_, ...), custom_call_target="tpu_custom_call" | custom-call | tf_op jit(solution)/shard_map/pallas_call | solution.py:519
  9.4 0.4 %collective-permute-done.2.refs_3_ = f32[8,512]{1,0:T(8,128)S(1)} collective-permute-done((f32[8,512]{1,0:T(8,128)S(1)}, f32[8,512]{1,0:T(8,128)S(1)}, u32[]{:S(2)}, u32[]{:S(2)}) %collective-permute-start.2) | collective-permute-done | bytes 16416 | tf_op jit(solution)/shard_map/ppermute | solution.py:553
  9.8 0.3 %shard_map.49.refs_0_ = f32[88,512]{1,0:T(8,128)S(1)} custom-call(f32[88,512]{1,0:T(8,128)S(1)} %get-tuple-element.31.refs_0_, f32[4,8,512]{2,1,0:T(8,128)S(1)} %get-tuple-element.32.refs_1_, f32[24,512]{1,0:T(8,128)S(1)} %collective-permute-done.1.refs_1_.refs_2_, f32[8,512]{1,0:T(8,128)S(1)} %collective-permute-done.2.refs_3_), custom_call_target="tpu_custom_call" | custom-call | tf_op jit(solution)/shard_map/pallas_call | solution.py:519
  10.1 0.8 %collective-permute-start.3 = (f32[88,512]{1,0:T(8,128)S(1)}, f32[88,512]{1,0:T(8,128)S(1)}, u32[]{:S(2)}, u32[]{:S(2)}) collective-permute-start(f32[88,512]{1,0:T(8,128)S(1)} %shard_map.49.refs_0_), channel_id=1, source_target_pairs={{0,16},{16,0},{1,17},{17,1},{2,18},{18,2},{3,19},{19,3},{4,20},{20... | collective-permute-start | bytes 540680 | tf_op jit(solution)/shard_map/ppermute | solution.py:536
  10.9 1.0 %collective-permute-done.3.refs_1_ = f32[88,512]{1,0:T(8,128)S(1)} collective-permute-done((f32[88,512]{1,0:T(8,128)S(1)}, f32[88,512]{1,0:T(8,128)S(1)}, u32[]{:S(2)}, u32[]{:S(2)}) %collective-permute-start.3) | collective-permute-done | bytes 180256 | tf_op jit(solution)/shard_map/ppermute | solution.py:536
  12.0 0.1 shard_map.50
  12.0 0.4 %collective-permute-start.7 = (f32[4,16,512]{2,1,0:T(8,128)S(1)}, f32[4,16,512]{2,1,0:T(8,128)S(1)}, u32[]{:S(2)}, u32[]{:S(2)}) collective-permute-start(f32[4,16,512]{2,1,0:T(8,128)S(1)} %get-tuple-element.38), channel_id=1, source_target_pairs={{0,16},{1,0},{2,1},{3,2},{4,20},{5,4},{6,5},{7,6},{8,24},{9,8},{10... | collective-permute-start | bytes 393224 | tf_op jit(solution)/shard_map/ppermute | solution.py:553
  12.4 1.3 %collective-permute-start.4 = (f32[16,512]{1,0:T(8,128)S(1)}, f32[16,512]{1,0:T(8,128)S(1)}, u32[]{:S(2)}, u32[]{:S(2)}) collective-permute-start(f32[16,512]{1,0:T(8,128)S(1)} %get-tuple-element.35), channel_id=1, source_target_pairs={{0,16},{1,17},{2,18},{3,19},{4,20},{5,8},{6,9},{7,10},{8,24},{9,4}... | collective-permute-start | bytes 98312 | tf_op jit(solution)/shard_map/ppermute | solution.py:553
  13.7 0.0 collective-permute-start.5
  13.7 2.8 %collective-permute-start.6 = (f32[16,512]{1,0:T(8,128)S(1)}, f32[16,512]{1,0:T(8,128)S(1)}, u32[]{:S(2)}, u32[]{:S(2)}) collective-permute-start(f32[16,512]{1,0:T(8,128)S(1)} %get-tuple-element.37), channel_id=1, source_target_pairs={{0,16},{1,4},{2,5},{3,6},{4,20},{5,0},{6,1},{7,2},{8,24},{9,12},{1... | collective-permute-start | bytes 98312 | tf_op jit(solution)/shard_map/ppermute | solution.py:553
  16.5 0.0 collective-permute-done.4.d_in
  16.5 1.1 %collective-permute-done.5.y_in = f32[16,512]{1,0:T(8,128)S(1)} collective-permute-done((f32[16,512]{1,0:T(8,128)S(1)}, f32[16,512]{1,0:T(8,128)S(1)}, u32[]{:S(2)}, u32[]{:S(2)}) %collective-permute-start.5) | collective-permute-done | bytes 32800 | tf_op jit(solution)/shard_map/ppermute | solution.py:553
  17.6 1.0 %collective-permute-done.6.e_in = f32[16,512]{1,0:T(8,128)S(1)} collective-permute-done((f32[16,512]{1,0:T(8,128)S(1)}, f32[16,512]{1,0:T(8,128)S(1)}, u32[]{:S(2)}, u32[]{:S(2)}) %collective-permute-start.6) | collective-permute-done | bytes 32800 | tf_op jit(solution)/shard_map/ppermute | solution.py:553
  18.6 0.0 collective-permute-done.7.z_in
  18.6 0.1 shard_map.51.part
  18.8 1.3 %collective-permute-start.8 = (f32[4,16,512]{2,1,0:T(8,128)S(1)}, f32[4,16,512]{2,1,0:T(8,128)S(1)}, u32[]{:S(2)}, u32[]{:S(2)}) collective-permute-start(f32[4,16,512]{2,1,0:T(8,128)S(1)} %shard_map.51.part), channel_id=1, source_target_pairs={{0,16},{16,0},{1,17},{17,1},{2,18},{18,2},{3,19},{19,3},{4,20},{20... | collective-permute-start | bytes 393224 | tf_op jit(solution)/shard_map/ppermute | solution.py:536
  20.0 1.0 %collective-permute-done.8.other = f32[4,16,512]{2,1,0:T(8,128)S(1)} collective-permute-done((f32[4,16,512]{2,1,0:T(8,128)S(1)}, f32[4,16,512]{2,1,0:T(8,128)S(1)}, u32[]{:S(2)}, u32[]{:S(2)}) %collective-permute-start.8) | collective-permute-done | bytes 131104 | tf_op jit(solution)/shard_map/ppermute | solution.py:536
  21.0 0.7 %shard_map.52 = f32[4,16,512]{2,1,0:T(8,128)} custom-call(f32[4,16,512]{2,1,0:T(8,128)S(1)} %shard_map.51.part, f32[4,16,512]{2,1,0:T(8,128)S(1)} %collective-permute-done.8.other), custom_call_target="tpu_custom_call" | custom-call | tf_op jit(solution)/shard_map/pallas_call | solution.py:519
  (1 shorter events, 0.0 us)
Async XLA Ops:
  0.0 6.1 %copy-start.1 = (s32[4,16,512]{2,1,0:T(8,128)S(1)}, s32[4,16,512]{2,1,0:T(8,128)}, u32[]{:S(2)}) copy-start(s32[4,16,512]{2,1,0:T(8,128)} %refs_1_.3) | copy-start | bytes 393220
  0.0 6.1 %copy-start.3 = (s32[4,16,512]{2,1,0:T(8,128)S(1)}, s32[4,16,512]{2,1,0:T(8,128)}, u32[]{:S(2)}) copy-start(s32[4,16,512]{2,1,0:T(8,128)} %refs_3_.3) | copy-start | bytes 393220
  0.0 6.1 %copy-start.2 = (f32[4,16,512]{2,1,0:T(8,128)S(1)}, f32[4,16,512]{2,1,0:T(8,128)}, u32[]{:S(2)}) copy-start(f32[4,16,512]{2,1,0:T(8,128)} %refs_2_.3) | copy-start | bytes 393220
  0.0 6.1 %copy-start = (f32[2,3,4,16,512]{4,3,2,1,0:T(8,128)S(1)}, f32[2,3,4,16,512]{4,3,2,1,0:T(8,128)}, u32[]{:S(2)}) copy-start(f32[2,3,4,16,512]{4,3,2,1,0:T(8,128)} %refs_0_.3) | copy-start | bytes 2359300
  1.2 7.3 %collective-permute-start = (f32[7,16,512]{2,1,0:T(8,128)S(1)}, f32[7,16,512]{2,1,0:T(8,128)S(1)}, u32[]{:S(2)}, u32[]{:S(2)}) collective-permute-start(f32[7,16,512]{2,1,0:T(8,128)S(1)} %get-tuple-element.22), channel_id=1, source_target_pairs={{0,16},{1,0},{2,1},{3,2},{4,20},{5,4},{6,5},{7,6},{8,24},{9,8},{10... | collective-permute-start | bytes 688136 | tf_op jit(solution)/shard_map/ppermute | solution.py:553
  1.7 6.8 %collective-permute-start.1 = (f32[24,512]{1,0:T(8,128)S(1)}, f32[24,512]{1,0:T(8,128)S(1)}, u32[]{:S(2)}, u32[]{:S(2)}) collective-permute-start(f32[24,512]{1,0:T(8,128)S(1)} %get-tuple-element.23), channel_id=1, source_target_pairs={{4,0},{8,4},{12,8},{0,12},{5,1},{9,5},{13,9},{1,13},{6,2},{10,6},{... | collective-permute-start | bytes 147464 | tf_op jit(solution)/shard_map/ppermute | solution.py:531
  5.2 4.6 %collective-permute-start.2 = (f32[8,512]{1,0:T(8,128)S(1)}, f32[8,512]{1,0:T(8,128)S(1)}, u32[]{:S(2)}, u32[]{:S(2)}) collective-permute-start(f32[8,512]{1,0:T(8,128)S(1)} %get-tuple-element.33), channel_id=1, source_target_pairs={{0,28},{1,12},{2,13},{3,14},{4,16},{5,0},{6,1},{7,2},{8,20},{9,4},... | collective-permute-start | bytes 49160 | tf_op jit(solution)/shard_map/ppermute | solution.py:553
  10.1 1.9 %collective-permute-start.3 = (f32[88,512]{1,0:T(8,128)S(1)}, f32[88,512]{1,0:T(8,128)S(1)}, u32[]{:S(2)}, u32[]{:S(2)}) collective-permute-start(f32[88,512]{1,0:T(8,128)S(1)} %shard_map.49.refs_0_), channel_id=1, source_target_pairs={{0,16},{16,0},{1,17},{17,1},{2,18},{18,2},{3,19},{19,3},{4,20},{20... | collective-permute-start | bytes 540680 | tf_op jit(solution)/shard_map/ppermute | solution.py:536
  12.0 6.6 %collective-permute-start.7 = (f32[4,16,512]{2,1,0:T(8,128)S(1)}, f32[4,16,512]{2,1,0:T(8,128)S(1)}, u32[]{:S(2)}, u32[]{:S(2)}) collective-permute-start(f32[4,16,512]{2,1,0:T(8,128)S(1)} %get-tuple-element.38), channel_id=1, source_target_pairs={{0,16},{1,0},{2,1},{3,2},{4,20},{5,4},{6,5},{7,6},{8,24},{9,8},{10... | collective-permute-start | bytes 393224 | tf_op jit(solution)/shard_map/ppermute | solution.py:553
  12.4 4.1 %collective-permute-start.4 = (f32[16,512]{1,0:T(8,128)S(1)}, f32[16,512]{1,0:T(8,128)S(1)}, u32[]{:S(2)}, u32[]{:S(2)}) collective-permute-start(f32[16,512]{1,0:T(8,128)S(1)} %get-tuple-element.35), channel_id=1, source_target_pairs={{0,16},{1,17},{2,18},{3,19},{4,20},{5,8},{6,9},{7,10},{8,24},{9,4}... | collective-permute-start | bytes 98312 | tf_op jit(solution)/shard_map/ppermute | solution.py:553
  13.7 3.9 %collective-permute-start.5 = (f32[16,512]{1,0:T(8,128)S(1)}, f32[16,512]{1,0:T(8,128)S(1)}, u32[]{:S(2)}, u32[]{:S(2)}) collective-permute-start(f32[16,512]{1,0:T(8,128)S(1)} %get-tuple-element.36), channel_id=1, source_target_pairs={{0,16},{1,17},{2,18},{3,19},{4,0},{5,1},{6,2},{7,3},{8,4},{9,5},{1... | collective-permute-start | bytes 98312 | tf_op jit(solution)/shard_map/ppermute | solution.py:553
  13.7 4.9 %collective-permute-start.6 = (f32[16,512]{1,0:T(8,128)S(1)}, f32[16,512]{1,0:T(8,128)S(1)}, u32[]{:S(2)}, u32[]{:S(2)}) collective-permute-start(f32[16,512]{1,0:T(8,128)S(1)} %get-tuple-element.37), channel_id=1, source_target_pairs={{0,16},{1,4},{2,5},{3,6},{4,20},{5,0},{6,1},{7,2},{8,24},{9,12},{1... | collective-permute-start | bytes 98312 | tf_op jit(solution)/shard_map/ppermute | solution.py:553
  18.8 2.3 %collective-permute-start.8 = (f32[4,16,512]{2,1,0:T(8,128)S(1)}, f32[4,16,512]{2,1,0:T(8,128)S(1)}, u32[]{:S(2)}, u32[]{:S(2)}) collective-permute-start(f32[4,16,512]{2,1,0:T(8,128)S(1)} %shard_map.51.part), channel_id=1, source_target_pairs={{0,16},{16,0},{1,17},{17,1},{2,18},{18,2},{3,19},{19,3},{4,20},{20... | collective-permute-start | bytes 393224 | tf_op jit(solution)/shard_map/ppermute | solution.py:536

commit v28 on v26

--- a/solution.py
+++ b/solution.py
@@ -162,6 +162,13 @@
     column = lax.broadcasted_iota(jnp.int32, value.shape, 1)
     ahead = jnp.where(column == length - 1, 0.0, pltpu.roll(value, length - 1, 1))
     return value + ahead, ahead - value
+
+
+def face_sums(value):
+    following = pltpu.roll(value, value.shape[0] - 1, 0)
+    both, along_x = split_x(value + following)
+    along_y, mixed = split_x(following - value)
+    return both, along_x, along_y, mixed
 
 
 def spread_y(quotient, ylen):
@@ -229,20 +236,14 @@
                 y_out[at : at + 1] = rows[case, comp, z, :1] * free
 
 
-def tile_energies(plus, diff, first, lanes, layers, loads, comps, base=0):
+def tile_energies(faces, first, lanes, layers, loads, comps, base=0):
     weights = mode_weights()
-
-    def faces(k, z):
-        near, far = slice(first, first + TILE), slice(first + 1, first + TILE + 1)
-        whole, whole_next = plus[k, z, near, lanes], plus[k, z, far, lanes]
-        change, change_next = diff[k, z, near, lanes], diff[k, z, far, lanes]
-        return whole + whole_next, change + change_next, whole_next - whole, change_next - change
-
     energy = [None] * layers
     for case in range(loads):
         low = None
         for z in range(layers + 1):
-            high = [faces(case * comps + comp, base + z) for comp in range(comps)]
+            planes = [case * comps + comp for comp in range(comps)]
+            high = [[faces[kind, k, base + z, first : first + TILE, lanes] for kind in range(4)] for k in planes]
             if low is not None:
                 part = quadratic(low, high, weights)
                 energy[z - 1] = part if energy[z - 1] is None else energy[z - 1] + part
@@ -255,7 +256,7 @@
     return jnp.where(row == ylen - 1, 0.0, value)
 
 
-def inner_kernel(totals, disp, fixed, density, solid, own, line, sends, last_plus, last_diff, last_factor, edge, plus, diff, quotient):
+def inner_kernel(totals, disp, fixed, density, solid, own, line, sends, last_faces, last_factor, edge, faces, quotient):
     loads, comps, zlen, ylen, xlen = disp.shape
     total_z, total_y = totals
     base_z = lax.axis_index("sz") * zlen
@@ -264,22 +265,18 @@
     keeps = jnp.where(on_first(), inner, 0)
     free = [1.0 - fixed[z].astype(jnp.float32) for z in range(zlen)]
 
-    @pl.loop(0, loads * comps, unroll=True)
-    def _(k):
+    for k in range(loads * comps):
         case, comp = k // comps, k % comps
         for z in range(zlen):
-            whole, change = split_x(disp[case, comp, z] * free[z])
-            plus[k, z, :ylen] = whole
-            diff[k, z, :ylen] = change
-        last_plus[k] = plus[k, keeps, :ylen]
-        last_diff[k] = diff[k, keeps, :ylen]
-
-    for comp in range(comps):
-        for case in range(loads):
-            for z in range(zlen):
-                at = (comp * loads + case) * zlen + z
-                line[0, at : at + 1] = plus[case * comps + comp, z, ylen - 1 : ylen]
-                line[1, at : at + 1] = diff[case * comps + comp, z, ylen - 1 : ylen]
+            plane = disp[case, comp, z] * free[z]
+            for kind, value in enumerate(face_sums(plane)):
+                faces[kind, k, z] = value
+            at = (comp * loads + case) * zlen + z
+            line[0, at : at + 1] = plane[ylen - 1 :]
+        for kind in range(4):
+            last_faces[kind, k] = faces[kind, k, keeps]
+
+    line[0], line[1] = split_x(line[0])
 
     zeros = jnp.zeros((TILE, xlen), jnp.float32)
     edge[...] = jnp.zeros(edge.shape, jnp.float32)
@@ -298,7 +295,7 @@
         @pl.loop(0, xlen // LANES, unroll=True)
         def _(chunk):
             lanes = pl.ds(pl.multiple_of(chunk * LANES, LANES), LANES)
-            energy = tile_energies(plus, diff, first, lanes, inner, loads, comps)
+            energy = tile_energies(faces, first, lanes, inner, loads, comps)
             for z in range(inner):
                 here = quotient[z, first + TILE : first + 2 * TILE, lanes]
                 quotient[z, first + TILE : first + 2 * TILE, lanes] = blank_last(energy[z] * here, first, ylen)
@@ -312,7 +309,7 @@
 
 
 def outer_kernel(
-    shape, z_in, y_in, own_in, line, sends, last_plus, last_diff, last_factor, edge, share, corner, plus, diff, quotient, factor
+    shape, z_in, y_in, own_in, line, sends, last_faces, last_factor, edge, share, corner, faces, quotient, factor
 ):
     loads, comps, zlen, ylen, xlen = shape
     planes = loads * comps
@@ -322,25 +319,29 @@
     more = lax.axis_index("sy") < lax.axis_size("sy") - 1
     stays, comes = jnp.where(first_core, 0, 1), jnp.where(first_core, jnp.where(top, 2, 1), 0)
     y_plus, y_diff = split_x(jnp.where(more, y_in[...], 0.0))
+    come_rows = []
     for k in range(planes):
-        plus[k, stays, :ylen] = last_plus[k]
-        diff[k, stays, :ylen] = last_diff[k]
-        whole, change = split_x(z_in[k])
-        plus[k, comes, :ylen] = whole
-        diff[k, comes, :ylen] = change
-        for group, value in enumerate((last_plus[k, ylen - 1 :], last_diff[k, ylen - 1 :], whole[ylen - 1 :], change[ylen - 1 :])):
-            corner[group, k : k + 1] = value
+        for kind, value in enumerate(face_sums(z_in[k])):
+            faces[kind, k, stays] = last_faces[kind, k]
+            faces[kind, k, comes] = value
+        come_rows.append(z_in[k, ylen - 1 :])
+        at = (k % comps * loads + k // comps) * zlen
+        for group in range(2):
+            corner[group, k : k + 1] = jnp.where(first_core, line[group, at + inner : at + zlen], line[group, at : at + 1])
+    come_rows.append(jnp.zeros((-planes % TILE, xlen), jnp.float32))
+    for group, value in enumerate(split_x(jnp.concatenate(come_rows, axis=0))):
+        corner[2 + group, :planes] = value[:planes]
     below = jnp.where(index > 0, z_in[planes], 0.0)
     factor[...] = jnp.where(first_core, last_factor[...], below)
     corner[0, planes : planes + 1] = factor[ylen - 1 :]
 
     @pl.when(top)
     def _():
-        clamped = jnp.zeros((ylen + TILE, xlen), jnp.float32)
+        clamped = jnp.zeros((ylen, xlen), jnp.float32)
         for k in range(planes):
             for slot in (1, 3):
-                plus[k, slot] = clamped
-                diff[k, slot] = clamped
+                for kind in range(4):
+                    faces[kind, k, slot] = clamped
 
     zeros = jnp.zeros((TILE, xlen), jnp.float32)
     quotient[:TILE] = zeros
@@ -350,7 +351,7 @@
         @pl.loop(0, xlen // LANES, unroll=True)
         def _(chunk):
             lanes = pl.ds(pl.multiple_of(chunk * LANES, LANES), LANES)
-            (energy,) = tile_energies(plus, diff, first, lanes, 1, loads, comps)
+            (energy,) = tile_energies(faces, first, lanes, 1, loads, comps)
             here = energy * factor[first : first + TILE, lanes]
             quotient[first + TILE : first + 2 * TILE, lanes] = blank_last(here, first, ylen)
 
@@ -361,7 +362,7 @@
             @pl.loop(0, xlen // LANES, unroll=True)
             def _(chunk):
                 lanes = pl.ds(pl.multiple_of(chunk * LANES, LANES), LANES)
-                (energy,) = tile_energies(plus, diff, first, lanes, 1, loads, comps, base=2)
+                (energy,) = tile_energies(faces, first, lanes, 1, loads, comps, base=2)
                 here = energy * factor[first : first + TILE, lanes]
                 quotient[first + TILE : first + 2 * TILE, lanes] += blank_last(here, first, ylen)
 
@@ -579,20 +580,19 @@
     d_in = opposed(d_send, -1, 0, y_shift=-1)
     z_in = opposed(z_send, -1, 0)
     y_in = ring_moved(y_send, "sy")
-    nodes = lambda layers: pltpu.VMEM((planes, layers, ylen + TILE, xlen), jnp.float32)
+    faces = lambda layers: pltpu.VMEM((4, planes, layers, ylen, xlen), jnp.float32)
     inner = call(
         lambda *refs: inner_kernel(totals, *refs),
         [
             (zlen, ylen, xlen),
             (2, planes * zlen, xlen),
             (2, REACH * (zlen - 1), xlen),
-            (planes, ylen, xlen),
-            (planes, ylen, xlen),
+            (4, planes, ylen, xlen),
             (ylen, xlen),
             (TILE, xlen),
         ],
         (displacements, fixed, density, solid),
-        scratch=[nodes(zlen), nodes(zlen), pltpu.VMEM((zlen - 1, ylen + 2 * TILE, xlen), jnp.float32)],
+        scratch=[faces(zlen), pltpu.VMEM((zlen - 1, ylen + 2 * TILE, xlen), jnp.float32)],
     )
     reach = REACH * zlen
     shape = displacements.shape
@@ -601,8 +601,7 @@
         [(ylen * zlen + 2 * reach, xlen), (4, -(-(planes + 1) // TILE) * TILE, xlen)],
         (z_in, y_in, *inner),
         scratch=[
-            nodes(4),
-            nodes(4),
+            faces(4),
             pltpu.VMEM((ylen + 2 * TILE, xlen), jnp.float32),
             pltpu.VMEM((ylen, xlen), jnp.float32),
         ],

time: 21.5 us -> 21.4 us (level)
  the two profiles are of different devices: /device:TPU:0 before, /device:TPU:3 now
where the time goes in v28:
time: 21.4 us; the launch traced here: 21.3 us
  starting transfers between devices  13 us (61%)
  Pallas kernels  4.51 us (21%)
  waiting for transfers between devices  3.66 us (17%)
    ppermute x6, starting transfers between devices, opposed(): return lax.ppermute(value, ('load', 'sy', 'sz'), pairs)  9.19 us
    pallas_call x7, Pallas kernels, call(): pl.pallas_call(kernel, out_shape=shapes, in_specs=[pl.BlockSpec(memory_sp...  4.51 us
    ppermute x2, starting transfers between devices, chip_swapped(): lax.ppermute(value, 'load', [(core, cores - 1 - core) for core in range(c...  3.55 us
    ppermute x2, waiting for transfers between devices, chip_swapped(): lax.ppermute(value, 'load', [(core, cores - 1 - core) for core in range(c...  2.04 us
    ppermute x6, waiting for transfers between devices, opposed(): return lax.ppermute(value, ('load', 'sy', 'sz'), pairs)  1.62 us
  transfers between devices with their start and end apart: 9, of which 4 were waited for; matrix products, arithmetic and copies ran while one was open for 0% of the time, Pallas kernels for 10%

profile of v28, /device:TPU:3, one launch (start us, length us, event | category | flops | bytes accessed | tf_op | source)
XLA Modules:
  0.0 21.3 jit_solution(13424489946080694898)
XLA Ops:
  0.0 0.0 copy-start.1
  0.0 0.0 copy-start.3
  0.0 0.0 copy-start
  0.0 1.2 %shard_map.46 = (f32[8,512]{1,0:T(8,128)S(1)}, f32[7,16,512]{2,1,0:T(8,128)S(1)}, f32[24,512]{1,0:T(8,128)S(1)}) custom-call(f32[2,3,4,16,512]{4,3,2,1,0:T(8,128)} %refs_0_.3, s32[4,16,512]{2,1,0:T(8,128)} %refs_1_.3, f32[4,16,512]{2,1,0:T(8,128)} %refs_2_.3, s32[4,16,512]{2,1,0:T(8,128)} %refs_3_.3), custom_call_target="tpu_custom_call" | custom-call | tf_op jit(solution)/shard_map/pallas_call | solution.py:520
  1.2 1.3 %collective-permute-start = (f32[7,16,512]{2,1,0:T(8,128)S(1)}, f32[7,16,512]{2,1,0:T(8,128)S(1)}, u32[]{:S(2)}, u32[]{:S(2)}) collective-permute-start(f32[7,16,512]{2,1,0:T(8,128)S(1)} %get-tuple-element.21), channel_id=1, source_target_pairs={{0,16},{1,0},{2,1},{3,2},{4,20},{5,4},{6,5},{7,6},{8,24},{9,8},{10... | collective-permute-start | bytes 688136 | tf_op jit(solution)/shard_map/ppermute | solution.py:554
  2.5 0.3 %collective-permute-start.1 = (f32[24,512]{1,0:T(8,128)S(1)}, f32[24,512]{1,0:T(8,128)S(1)}, u32[]{:S(2)}, u32[]{:S(2)}) collective-permute-start(f32[24,512]{1,0:T(8,128)S(1)} %get-tuple-element.22), channel_id=1, source_target_pairs={{4,0},{8,4},{12,8},{0,12},{5,1},{9,5},{13,9},{1,13},{6,2},{10,6},{... | collective-permute-start | bytes 147464 | tf_op jit(solution)/shard_map/ppermute | solution.py:532
  2.8 3.2 %collective-permute-start.2 = (f32[8,512]{1,0:T(8,128)S(1)}, f32[8,512]{1,0:T(8,128)S(1)}, u32[]{:S(2)}, u32[]{:S(2)}) collective-permute-start(f32[8,512]{1,0:T(8,128)S(1)} %get-tuple-element.31), channel_id=1, source_target_pairs={{0,28},{1,12},{2,13},{3,14},{4,16},{5,0},{6,1},{7,2},{8,20},{9,4},... | collective-permute-start | bytes 49160 | tf_op jit(solution)/shard_map/ppermute | solution.py:554
  5.9 0.0 copy-done.1
  6.0 0.0 copy-done.3
  6.0 0.0 copy-done.2
  6.0 0.0 copy-done
  6.0 1.6 %shard_map.47 = (f32[4,16,512]{2,1,0:T(8,128)S(1)}, f32[2,24,512]{2,1,0:T(8,128)S(1)}, f32[2,9,512]{2,1,0:T(8,128)S(1)}, f32[4,6,16,512]{3,2,1,0:T(8,128)S(1)}, ...) custom-call(f32[2,3,4,16,512]{4,3,2,1,0:T(8,128)S(1)} %copy-done, s32[4,16,512]{2,1,0:T(8,128)S(1)} %copy-done.1, ...), custom_call_target="tpu_custom_call" | custom-call | tf_op jit(solution)/shard_map/pallas_call | solution.py:520
  7.5 0.0 collective-permute-done.1.refs_1_.refs_2_
  7.5 0.0 collective-permute-done.refs_0_
  7.5 0.7 %shard_map.48 = (f32[88,512]{1,0:T(8,128)S(1)}, f32[4,8,512]{2,1,0:T(8,128)S(1)}) custom-call(f32[7,16,512]{2,1,0:T(8,128)S(1)} %collective-permute-done.refs_0_, f32[24,512]{1,0:T(8,128)S(1)} %collective-permute-done.1.refs_1_.refs_2_, f32[4,16,512]{2,1,0:T(8,128)S(1)} %get-tuple-element.23.refs_2_, f32[2,24,512]{2,1,0:T(8,128)S(1)} %get-tuple-element.24.refs_3_, ...), custom_call_target="tpu_custom_call" | custom-call | tf_op jit(solution)/shard_map/pallas_call | solution.py:520
  8.2 0.0 collective-permute-done.2.refs_3_
  8.2 0.3 %shard_map.49.refs_0_ = f32[88,512]{1,0:T(8,128)S(1)} custom-call(f32[88,512]{1,0:T(8,128)S(1)} %get-tuple-element.29.refs_0_, f32[4,8,512]{2,1,0:T(8,128)S(1)} %get-tuple-element.30.refs_1_, f32[24,512]{1,0:T(8,128)S(1)} %collective-permute-done.1.refs_1_.refs_2_, f32[8,512]{1,0:T(8,128)S(1)} %collective-permute-done.2.refs_3_), custom_call_target="tpu_custom_call" | custom-call | tf_op jit(solution)/shard_map/pallas_call | solution.py:520
  8.5 0.9 %collective-permute-start.3 = (f32[88,512]{1,0:T(8,128)S(1)}, f32[88,512]{1,0:T(8,128)S(1)}, u32[]{:S(2)}, u32[]{:S(2)}) collective-permute-start(f32[88,512]{1,0:T(8,128)S(1)} %shard_map.49.refs_0_), channel_id=1, source_target_pairs={{0,16},{16,0},{1,17},{17,1},{2,18},{18,2},{3,19},{19,3},{4,20},{20... | collective-permute-start | bytes 540680 | tf_op jit(solution)/shard_map/ppermute | solution.py:537
  9.4 1.0 %collective-permute-done.3.refs_1_ = f32[88,512]{1,0:T(8,128)S(1)} collective-permute-done((f32[88,512]{1,0:T(8,128)S(1)}, f32[88,512]{1,0:T(8,128)S(1)}, u32[]{:S(2)}, u32[]{:S(2)}) %collective-permute-start.3) | collective-permute-done | bytes 180256 | tf_op jit(solution)/shard_map/ppermute | solution.py:537
  10.4 0.1 shard_map.50
  10.5 1.3 %collective-permute-start.7 = (f32[4,16,512]{2,1,0:T(8,128)S(1)}, f32[4,16,512]{2,1,0:T(8,128)S(1)}, u32[]{:S(2)}, u32[]{:S(2)}) collective-permute-start(f32[4,16,512]{2,1,0:T(8,128)S(1)} %get-tuple-element.36), channel_id=1, source_target_pairs={{0,16},{1,0},{2,1},{3,2},{4,20},{5,4},{6,5},{7,6},{8,24},{9,8},{10... | collective-permute-start | bytes 393224 | tf_op jit(solution)/shard_map/ppermute | solution.py:554
  11.8 2.2 %collective-permute-start.4 = (f32[16,512]{1,0:T(8,128)S(1)}, f32[16,512]{1,0:T(8,128)S(1)}, u32[]{:S(2)}, u32[]{:S(2)}) collective-permute-start(f32[16,512]{1,0:T(8,128)S(1)} %get-tuple-element.33), channel_id=1, source_target_pairs={{0,16},{1,17},{2,18},{3,19},{4,20},{5,8},{6,9},{7,10},{8,24},{9,4}... | collective-permute-start | bytes 98312 | tf_op jit(solution)/shard_map/ppermute | solution.py:554
  14.0 0.0 collective-permute-start.5
  14.0 1.2 %collective-permute-start.6 = (f32[16,512]{1,0:T(8,128)S(1)}, f32[16,512]{1,0:T(8,128)S(1)}, u32[]{:S(2)}, u32[]{:S(2)}) collective-permute-start(f32[16,512]{1,0:T(8,128)S(1)} %get-tuple-element.35), channel_id=1, source_target_pairs={{0,16},{1,17},{2,18},{3,19},{4,0},{5,1},{6,2},{7,3},{8,4},{9,5},{1... | collective-permute-start | bytes 98312 | tf_op jit(solution)/shard_map/ppermute | solution.py:554
  15.2 0.0 collective-permute-done.4.d_in
  15.2 0.2 collective-permute-done.5.e_in
  15.3 1.4 %collective-permute-done.6.y_in = f32[16,512]{1,0:T(8,128)S(1)} collective-permute-done((f32[16,512]{1,0:T(8,128)S(1)}, f32[16,512]{1,0:T(8,128)S(1)}, u32[]{:S(2)}, u32[]{:S(2)}) %collective-permute-start.6) | collective-permute-done | bytes 32800 | tf_op jit(solution)/shard_map/ppermute | solution.py:554
  16.8 0.0 collective-permute-done.7.z_in
  16.8 0.1 shard_map.51.part
  16.9 2.7 %collective-permute-start.8 = (f32[4,16,512]{2,1,0:T(8,128)S(1)}, f32[4,16,512]{2,1,0:T(8,128)S(1)}, u32[]{:S(2)}, u32[]{:S(2)}) collective-permute-start(f32[4,16,512]{2,1,0:T(8,128)S(1)} %shard_map.51.part), channel_id=1, source_target_pairs={{0,16},{16,0},{1,17},{17,1},{2,18},{18,2},{3,19},{19,3},{4,20},{20... | collective-permute-start | bytes 393224 | tf_op jit(solution)/shard_map/ppermute | solution.py:537
  19.6 1.0 %collective-permute-done.8.other = f32[4,16,512]{2,1,0:T(8,128)S(1)} collective-permute-done((f32[4,16,512]{2,1,0:T(8,128)S(1)}, f32[4,16,512]{2,1,0:T(8,128)S(1)}, u32[]{:S(2)}, u32[]{:S(2)}) %collective-permute-start.8) | collective-permute-done | bytes 131104 | tf_op jit(solution)/shard_map/ppermute | solution.py:537
  20.6 0.7 %shard_map.52 = f32[4,16,512]{2,1,0:T(8,128)} custom-call(f32[4,16,512]{2,1,0:T(8,128)S(1)} %shard_map.51.part, f32[4,16,512]{2,1,0:T(8,128)S(1)} %collective-permute-done.8.other), custom_call_target="tpu_custom_call" | custom-call | tf_op jit(solution)/shard_map/pallas_call | solution.py:520
  (1 shorter events, 0.0 us)
Async XLA Ops:
  0.0 6.0 %copy-start.1 = (s32[4,16,512]{2,1,0:T(8,128)S(1)}, s32[4,16,512]{2,1,0:T(8,128)}, u32[]{:S(2)}) copy-start(s32[4,16,512]{2,1,0:T(8,128)} %refs_1_.3) | copy-start | bytes 393220
  0.0 6.0 %copy-start.3 = (s32[4,16,512]{2,1,0:T(8,128)S(1)}, s32[4,16,512]{2,1,0:T(8,128)}, u32[]{:S(2)}) copy-start(s32[4,16,512]{2,1,0:T(8,128)} %refs_3_.3) | copy-start | bytes 393220
  0.0 6.0 %copy-start.2 = (f32[4,16,512]{2,1,0:T(8,128)S(1)}, f32[4,16,512]{2,1,0:T(8,128)}, u32[]{:S(2)}) copy-start(f32[4,16,512]{2,1,0:T(8,128)} %refs_2_.3) | copy-start | bytes 393220
  0.0 5.9 %copy-start = (f32[2,3,4,16,512]{4,3,2,1,0:T(8,128)S(1)}, f32[2,3,4,16,512]{4,3,2,1,0:T(8,128)}, u32[]{:S(2)}) copy-start(f32[2,3,4,16,512]{4,3,2,1,0:T(8,128)} %refs_0_.3) | copy-start | bytes 2359300
  1.2 6.3 %collective-permute-start = (f32[7,16,512]{2,1,0:T(8,128)S(1)}, f32[7,16,512]{2,1,0:T(8,128)S(1)}, u32[]{:S(2)}, u32[]{:S(2)}) collective-permute-start(f32[7,16,512]{2,1,0:T(8,128)S(1)} %get-tuple-element.21), channel_id=1, source_target_pairs={{0,16},{1,0},{2,1},{3,2},{4,20},{5,4},{6,5},{7,6},{8,24},{9,8},{10... | collective-permute-start | bytes 688136 | tf_op jit(solution)/shard_map/ppermute | solution.py:554
  2.5 5.0 %collective-permute-start.1 = (f32[24,512]{1,0:T(8,128)S(1)}, f32[24,512]{1,0:T(8,128)S(1)}, u32[]{:S(2)}, u32[]{:S(2)}) collective-permute-start(f32[24,512]{1,0:T(8,128)S(1)} %get-tuple-element.22), channel_id=1, source_target_pairs={{4,0},{8,4},{12,8},{0,12},{5,1},{9,5},{13,9},{1,13},{6,2},{10,6},{... | collective-permute-start | bytes 147464 | tf_op jit(solution)/shard_map/ppermute | solution.py:532
  2.8 5.4 %collective-permute-start.2 = (f32[8,512]{1,0:T(8,128)S(1)}, f32[8,512]{1,0:T(8,128)S(1)}, u32[]{:S(2)}, u32[]{:S(2)}) collective-permute-start(f32[8,512]{1,0:T(8,128)S(1)} %get-tuple-element.31), channel_id=1, source_target_pairs={{0,28},{1,12},{2,13},{3,14},{4,16},{5,0},{6,1},{7,2},{8,20},{9,4},... | collective-permute-start | bytes 49160 | tf_op jit(solution)/shard_map/ppermute | solution.py:554
  8.5 1.9 %collective-permute-start.3 = (f32[88,512]{1,0:T(8,128)S(1)}, f32[88,512]{1,0:T(8,128)S(1)}, u32[]{:S(2)}, u32[]{:S(2)}) collective-permute-start(f32[88,512]{1,0:T(8,128)S(1)} %shard_map.49.refs_0_), channel_id=1, source_target_pairs={{0,16},{16,0},{1,17},{17,1},{2,18},{18,2},{3,19},{19,3},{4,20},{20... | collective-permute-start | bytes 540680 | tf_op jit(solution)/shard_map/ppermute | solution.py:537
  10.5 6.3 %collective-permute-start.7 = (f32[4,16,512]{2,1,0:T(8,128)S(1)}, f32[4,16,512]{2,1,0:T(8,128)S(1)}, u32[]{:S(2)}, u32[]{:S(2)}) collective-permute-start(f32[4,16,512]{2,1,0:T(8,128)S(1)} %get-tuple-element.36), channel_id=1, source_target_pairs={{0,16},{1,0},{2,1},{3,2},{4,20},{5,4},{6,5},{7,6},{8,24},{9,8},{10... | collective-permute-start | bytes 393224 | tf_op jit(solution)/shard_map/ppermute | solution.py:554
  11.8 3.4 %collective-permute-start.4 = (f32[16,512]{1,0:T(8,128)S(1)}, f32[16,512]{1,0:T(8,128)S(1)}, u32[]{:S(2)}, u32[]{:S(2)}) collective-permute-start(f32[16,512]{1,0:T(8,128)S(1)} %get-tuple-element.33), channel_id=1, source_target_pairs={{0,16},{1,17},{2,18},{3,19},{4,20},{5,8},{6,9},{7,10},{8,24},{9,4}... | collective-permute-start | bytes 98312 | tf_op jit(solution)/shard_map/ppermute | solution.py:554
  14.0 1.3 %collective-permute-start.5 = (f32[16,512]{1,0:T(8,128)S(1)}, f32[16,512]{1,0:T(8,128)S(1)}, u32[]{:S(2)}, u32[]{:S(2)}) collective-permute-start(f32[16,512]{1,0:T(8,128)S(1)} %get-tuple-element.34), channel_id=1, source_target_pairs={{0,16},{1,4},{2,5},{3,6},{4,20},{5,0},{6,1},{7,2},{8,24},{9,12},{1... | collective-permute-start | bytes 98312 | tf_op jit(solution)/shard_map/ppermute | solution.py:554
  14.0 2.8 %collective-permute-start.6 = (f32[16,512]{1,0:T(8,128)S(1)}, f32[16,512]{1,0:T(8,128)S(1)}, u32[]{:S(2)}, u32[]{:S(2)}) collective-permute-start(f32[16,512]{1,0:T(8,128)S(1)} %get-tuple-element.35), channel_id=1, source_target_pairs={{0,16},{1,17},{2,18},{3,19},{4,0},{5,1},{6,2},{7,3},{8,4},{9,5},{1... | collective-permute-start | bytes 98312 | tf_op jit(solution)/shard_map/ppermute | solution.py:554
  16.9 3.7 %collective-permute-start.8 = (f32[4,16,512]{2,1,0:T(8,128)S(1)}, f32[4,16,512]{2,1,0:T(8,128)S(1)}, u32[]{:S(2)}, u32[]{:S(2)}) collective-permute-start(f32[4,16,512]{2,1,0:T(8,128)S(1)} %shard_map.51.part), channel_id=1, source_target_pairs={{0,16},{16,0},{1,17},{17,1},{2,18},{18,2},{3,19},{19,3},{4,20},{20... | collective-permute-start | bytes 393224 | tf_op jit(solution)/shard_map/ppermute | solution.py:537

commit v29 on v28

--- a/solution.py
+++ b/solution.py
@@ -459,7 +459,7 @@
     z_out[...] = h_out[pl.ds(jnp.where(first_core, 0, 1), zlen)]
     ups = jnp.concatenate(layers(rows, REACH), axis=0)
     downs = jnp.concatenate(layers(rows + reach, REACH), axis=0)
-    y_out[: reach + REACH] = jnp.where(first_core, downs, ups)
+    y_out[: reach + REACH] = jnp.where(next_is_partner(lax.axis_index("load")), ups, downs)
     for out, used in ((y_out, reach + REACH), (d_out, reach), (e_out, reach)):
         out[used:] = jnp.zeros((out.shape[0] - used, xlen), jnp.float32)
     for out, start in ((d_out, 1), (e_out, 0)):
@@ -474,7 +474,8 @@
     z_index, z_last = lax.axis_index("sz"), lax.axis_size("sz") - 1
     y_index, y_last = lax.axis_index("sy"), lax.axis_size("sy") - 1
     z_side = jnp.where(first_core, z_index < z_last, z_index > 0)
-    y_side = jnp.where(first_core, y_index < y_last, y_index > 0)
+    y_next = next_is_partner(lax.axis_index("load"))
+    y_side = jnp.where(y_next, y_index < y_last, y_index > 0)
     d_next, e_next = next_is_partner(1), next_is_partner(0)
     d_side, e_side = (jnp.where(up, y_index < y_last, y_index > 0) for up in (d_next, e_next))
     blank = jnp.zeros((TILE - REACH, xlen), jnp.float32)
@@ -498,7 +499,7 @@
     own = []
     for k in range(zlen + 1):
         layer = jnp.where(first_core, h[k], 0.0)
-        own.append(with_ends(layer, ends(y_in[REACH * k : REACH * (k + 1)], y_side, first_core)))
+        own.append(with_ends(layer, ends(y_in[REACH * k : REACH * (k + 1)], y_side, y_next)))
     come = []
     for k in range(zlen):
         part = slice(REACH * k, REACH * (k + 1))
@@ -551,6 +552,18 @@
                     to_y, to_z, side = y, z, cores - 1 - core
                 to_y = (to_y + y_shift) % rows
                 pairs.append(((core * rows + y) * size + z, (side * rows + to_y) * size + to_z))
+    return lax.ppermute(value, ("load", "sy", "sz"), pairs)
+
+
+def beside(value):
+    cores, rows, size = lax.axis_size("load"), lax.axis_size("sy"), lax.axis_size("sz")
+    pairs = []
+    for core in range(cores):
+        for y in range(rows):
+            to_y = y + 1 if (y - core) % 2 == 0 else y - 1
+            for z in range(size):
+                target = (to_y, z) if 0 <= to_y < rows else (y, z ^ 1)
+                pairs.append(((core * rows + y) * size + z, (core * rows + target[0]) * size + target[1]))
     return lax.ppermute(value, ("load", "sy", "sz"), pairs)
 
 
@@ -623,7 +636,7 @@
     )
     d_in = opposed(d_send, -1, 0, start=1)
     e_in = opposed(e_send, -1, 0, start=0)
-    y_in = opposed(y_send, 0, -1)
+    y_in = beside(y_send)
     z_in = opposed(z_send, -1, 0)
     (part,) = call(layers_kernel, [(zlen, ylen, xlen)], (h, d_in, e_in, y_in, z_in))
     (out,) = call(sum_kernel, [(zlen, ylen, xlen)], (part, chip_swapped(part)))

time: 21.4 us -> 21 us (0.981)
  the two profiles are of different devices: /device:TPU:3 before, /device:TPU:0 now
where the time goes in v29:
time: 21 us; the launch traced here: 20.9 us
  starting transfers between devices  10.6 us (50%)
  waiting for transfers between devices  5.73 us (27%)
  Pallas kernels  4.52 us (22%)
    pallas_call x7, Pallas kernels, call(): pl.pallas_call(kernel, out_shape=shapes, in_specs=[pl.BlockSpec(memory_sp...  4.52 us
    ppermute x1, starting transfers between devices, ring_moved(): return lax.ppermute(value, axis, [((k + 1) % size, k) for k in range(size)])  3.51 us
    ppermute x1, starting transfers between devices, beside(): return lax.ppermute(value, ('load', 'sy', 'sz'), pairs)  3.3 us
    ppermute x5, starting transfers between devices, opposed(): return lax.ppermute(value, ('load', 'sy', 'sz'), pairs)  3.25 us
    ppermute x5, waiting for transfers between devices, opposed(): return lax.ppermute(value, ('load', 'sy', 'sz'), pairs)  2.96 us
    ppermute x2, waiting for transfers between devices, chip_swapped(): lax.ppermute(value, 'load', [(core, cores - 1 - core) for core in range(c...  2.39 us
    ppermute x2, starting transfers between devices, chip_swapped(): lax.ppermute(value, 'load', [(core, cores - 1 - core) for core in range(c...  0.51 us
  transfers between devices with their start and end apart: 9, of which 6 were waited for; matrix products, arithmetic and copies ran while one was open for 0% of the time, Pallas kernels for 11%

profile of v29, /device:TPU:0, one launch (start us, length us, event | category | flops | bytes accessed | tf_op | source)
XLA Modules:
  0.0 20.9 jit_solution(4230865489783706251)
XLA Ops:
  0.0 0.0 copy-start.1
  0.0 0.0 copy-start.3
  0.0 0.0 copy-start.2
  0.0 1.2 %shard_map.46 = (f32[8,512]{1,0:T(8,128)S(1)}, f32[7,16,512]{2,1,0:T(8,128)S(1)}, f32[24,512]{1,0:T(8,128)S(1)}) custom-call(f32[2,3,4,16,512]{4,3,2,1,0:T(8,128)} %refs_0_.3, s32[4,16,512]{2,1,0:T(8,128)} %refs_1_.3, f32[4,16,512]{2,1,0:T(8,128)} %refs_2_.3, s32[4,16,512]{2,1,0:T(8,128)} %refs_3_.3), custom_call_target="tpu_custom_call" | custom-call | tf_op jit(solution)/shard_map/pallas_call | solution.py:521
  1.2 0.5 %collective-permute-start = (f32[7,16,512]{2,1,0:T(8,128)S(1)}, f32[7,16,512]{2,1,0:T(8,128)S(1)}, u32[]{:S(2)}, u32[]{:S(2)}) collective-permute-start(f32[7,16,512]{2,1,0:T(8,128)S(1)} %get-tuple-element.21), channel_id=1, source_target_pairs={{0,16},{1,0},{2,1},{3,2},{4,20},{5,4},{6,5},{7,6},{8,24},{9,8},{10... | collective-permute-start | bytes 688136 | tf_op jit(solution)/shard_map/ppermute | solution.py:555
  1.7 3.5 %collective-permute-start.1 = (f32[24,512]{1,0:T(8,128)S(1)}, f32[24,512]{1,0:T(8,128)S(1)}, u32[]{:S(2)}, u32[]{:S(2)}) collective-permute-start(f32[24,512]{1,0:T(8,128)S(1)} %get-tuple-element.22), channel_id=1, source_target_pairs={{4,0},{8,4},{12,8},{0,12},{5,1},{9,5},{13,9},{1,13},{6,2},{10,6},{... | collective-permute-start | bytes 147464 | tf_op jit(solution)/shard_map/ppermute | solution.py:533
  5.2 0.9 %collective-permute-start.2 = (f32[8,512]{1,0:T(8,128)S(1)}, f32[8,512]{1,0:T(8,128)S(1)}, u32[]{:S(2)}, u32[]{:S(2)}) collective-permute-start(f32[8,512]{1,0:T(8,128)S(1)} %get-tuple-element.31), channel_id=1, source_target_pairs={{0,28},{1,12},{2,13},{3,14},{4,16},{5,0},{6,1},{7,2},{8,20},{9,4},... | collective-permute-start | bytes 49160 | tf_op jit(solution)/shard_map/ppermute | solution.py:555
  6.1 0.0 copy-done.1
  6.1 0.0 copy-done.3
  6.1 0.0 copy-done.2
  6.1 0.0 copy-done
  6.1 1.6 %shard_map.47 = (f32[4,16,512]{2,1,0:T(8,128)S(1)}, f32[2,24,512]{2,1,0:T(8,128)S(1)}, f32[2,9,512]{2,1,0:T(8,128)S(1)}, f32[4,6,16,512]{3,2,1,0:T(8,128)S(1)}, ...) custom-call(f32[2,3,4,16,512]{4,3,2,1,0:T(8,128)S(1)} %copy-done, s32[4,16,512]{2,1,0:T(8,128)S(1)} %copy-done.1, ...), custom_call_target="tpu_custom_call" | custom-call | tf_op jit(solution)/shard_map/pallas_call | solution.py:521
  7.7 0.0 collective-permute-done.1.refs_1_.refs_2_
  7.7 0.5 %collective-permute-done.refs_0_ = f32[7,16,512]{2,1,0:T(8,128)S(1)} collective-permute-done((f32[7,16,512]{2,1,0:T(8,128)S(1)}, f32[7,16,512]{2,1,0:T(8,128)S(1)}, u32[]{:S(2)}, u32[]{:S(2)}) %collective-permute-start) | collective-permute-done | bytes 229408 | tf_op jit(solution)/shard_map/ppermute | solution.py:555
  8.2 0.6 %shard_map.48 = (f32[88,512]{1,0:T(8,128)S(1)}, f32[4,8,512]{2,1,0:T(8,128)S(1)}) custom-call(f32[7,16,512]{2,1,0:T(8,128)S(1)} %collective-permute-done.refs_0_, f32[24,512]{1,0:T(8,128)S(1)} %collective-permute-done.1.refs_1_.refs_2_, f32[4,16,512]{2,1,0:T(8,128)S(1)} %get-tuple-element.23.refs_2_, f32[2,24,512]{2,1,0:T(8,128)S(1)} %get-tuple-element.24.refs_3_, ...), custom_call_target="tpu_custom_call" | custom-call | tf_op jit(solution)/shard_map/pallas_call | solution.py:521
  8.9 0.9 %collective-permute-done.2.refs_3_ = f32[8,512]{1,0:T(8,128)S(1)} collective-permute-done((f32[8,512]{1,0:T(8,128)S(1)}, f32[8,512]{1,0:T(8,128)S(1)}, u32[]{:S(2)}, u32[]{:S(2)}) %collective-permute-start.2) | collective-permute-done | bytes 16416 | tf_op jit(solution)/shard_map/ppermute | solution.py:555
  9.8 0.3 %shard_map.49.refs_0_ = f32[88,512]{1,0:T(8,128)S(1)} custom-call(f32[88,512]{1,0:T(8,128)S(1)} %get-tuple-element.29.refs_0_, f32[4,8,512]{2,1,0:T(8,128)S(1)} %get-tuple-element.30.refs_1_, f32[24,512]{1,0:T(8,128)S(1)} %collective-permute-done.1.refs_1_.refs_2_, f32[8,512]{1,0:T(8,128)S(1)} %collective-permute-done.2.refs_3_), custom_call_target="tpu_custom_call" | custom-call | tf_op jit(solution)/shard_map/pallas_call | solution.py:521
  10.1 0.1 collective-permute-start.3
  10.2 1.4 %collective-permute-done.3.refs_1_ = f32[88,512]{1,0:T(8,128)S(1)} collective-permute-done((f32[88,512]{1,0:T(8,128)S(1)}, f32[88,512]{1,0:T(8,128)S(1)}, u32[]{:S(2)}, u32[]{:S(2)}) %collective-permute-start.3) | collective-permute-done | bytes 180256 | tf_op jit(solution)/shard_map/ppermute | solution.py:538
  11.6 0.1 shard_map.50
  11.6 0.2 collective-permute-start.7
  11.8 1.7 %collective-permute-start.4 = (f32[16,512]{1,0:T(8,128)S(1)}, f32[16,512]{1,0:T(8,128)S(1)}, u32[]{:S(2)}, u32[]{:S(2)}) collective-permute-start(f32[16,512]{1,0:T(8,128)S(1)} %get-tuple-element.33), channel_id=1, source_target_pairs={{0,16},{1,17},{2,18},{3,19},{4,20},{5,8},{6,9},{7,10},{8,24},{9,4}... | collective-permute-start | bytes 98312 | tf_op jit(solution)/shard_map/ppermute | solution.py:555
  13.5 0.0 collective-permute-start.5
  13.5 3.3 %collective-permute-start.6 = (f32[16,512]{1,0:T(8,128)S(1)}, f32[16,512]{1,0:T(8,128)S(1)}, u32[]{:S(2)}, u32[]{:S(2)}) collective-permute-start(f32[16,512]{1,0:T(8,128)S(1)} %get-tuple-element.35), channel_id=1, source_target_pairs={{0,4},{1,5},{2,6},{3,7},{4,0},{5,1},{6,2},{7,3},{8,12},{9,13},{10,... | collective-permute-start | bytes 98312 | tf_op jit(solution)/shard_map/ppermute | solution.py:567
  16.8 0.0 collective-permute-done.4.d_in
  16.8 1.5 %collective-permute-done.5.e_in = f32[16,512]{1,0:T(8,128)S(1)} collective-permute-done((f32[16,512]{1,0:T(8,128)S(1)}, f32[16,512]{1,0:T(8,128)S(1)}, u32[]{:S(2)}, u32[]{:S(2)}) %collective-permute-start.5) | collective-permute-done | bytes 32800 | tf_op jit(solution)/shard_map/ppermute | solution.py:555
  18.3 0.4 %collective-permute-done.6.y_in = f32[16,512]{1,0:T(8,128)S(1)} collective-permute-done((f32[16,512]{1,0:T(8,128)S(1)}, f32[16,512]{1,0:T(8,128)S(1)}, u32[]{:S(2)}, u32[]{:S(2)}) %collective-permute-start.6) | collective-permute-done | bytes 32800 | tf_op jit(solution)/shard_map/ppermute | solution.py:567
  18.7 0.0 collective-permute-done.7.z_in
  18.7 0.1 shard_map.51.part
  18.8 0.4 %collective-permute-start.8 = (f32[4,16,512]{2,1,0:T(8,128)S(1)}, f32[4,16,512]{2,1,0:T(8,128)S(1)}, u32[]{:S(2)}, u32[]{:S(2)}) collective-permute-start(f32[4,16,512]{2,1,0:T(8,128)S(1)} %shard_map.51.part), channel_id=1, source_target_pairs={{0,16},{16,0},{1,17},{17,1},{2,18},{18,2},{3,19},{19,3},{4,20},{20... | collective-permute-start | bytes 393224 | tf_op jit(solution)/shard_map/ppermute | solution.py:538
  19.2 1.0 %collective-permute-done.8.other = f32[4,16,512]{2,1,0:T(8,128)S(1)} collective-permute-done((f32[4,16,512]{2,1,0:T(8,128)S(1)}, f32[4,16,512]{2,1,0:T(8,128)S(1)}, u32[]{:S(2)}, u32[]{:S(2)}) %collective-permute-start.8) | collective-permute-done | bytes 131104 | tf_op jit(solution)/shard_map/ppermute | solution.py:538
  20.2 0.7 %shard_map.52 = f32[4,16,512]{2,1,0:T(8,128)} custom-call(f32[4,16,512]{2,1,0:T(8,128)S(1)} %shard_map.51.part, f32[4,16,512]{2,1,0:T(8,128)S(1)} %collective-permute-done.8.other), custom_call_target="tpu_custom_call" | custom-call | tf_op jit(solution)/shard_map/pallas_call | solution.py:521
  (1 shorter events, 0.0 us)
Async XLA Ops:
  0.0 6.1 %copy-start.1 = (s32[4,16,512]{2,1,0:T(8,128)S(1)}, s32[4,16,512]{2,1,0:T(8,128)}, u32[]{:S(2)}) copy-start(s32[4,16,512]{2,1,0:T(8,128)} %refs_1_.3) | copy-start | bytes 393220
  0.0 6.1 %copy-start.3 = (s32[4,16,512]{2,1,0:T(8,128)S(1)}, s32[4,16,512]{2,1,0:T(8,128)}, u32[]{:S(2)}) copy-start(s32[4,16,512]{2,1,0:T(8,128)} %refs_3_.3) | copy-start | bytes 393220
  0.0 6.1 %copy-start.2 = (f32[4,16,512]{2,1,0:T(8,128)S(1)}, f32[4,16,512]{2,1,0:T(8,128)}, u32[]{:S(2)}) copy-start(f32[4,16,512]{2,1,0:T(8,128)} %refs_2_.3) | copy-start | bytes 393220
  0.0 6.1 %copy-start = (f32[2,3,4,16,512]{4,3,2,1,0:T(8,128)S(1)}, f32[2,3,4,16,512]{4,3,2,1,0:T(8,128)}, u32[]{:S(2)}) copy-start(f32[2,3,4,16,512]{4,3,2,1,0:T(8,128)} %refs_0_.3) | copy-start | bytes 2359300
  1.2 7.1 %collective-permute-start = (f32[7,16,512]{2,1,0:T(8,128)S(1)}, f32[7,16,512]{2,1,0:T(8,128)S(1)}, u32[]{:S(2)}, u32[]{:S(2)}) collective-permute-start(f32[7,16,512]{2,1,0:T(8,128)S(1)} %get-tuple-element.21), channel_id=1, source_target_pairs={{0,16},{1,0},{2,1},{3,2},{4,20},{5,4},{6,5},{7,6},{8,24},{9,8},{10... | collective-permute-start | bytes 688136 | tf_op jit(solution)/shard_map/ppermute | solution.py:555
  1.7 6.0 %collective-permute-start.1 = (f32[24,512]{1,0:T(8,128)S(1)}, f32[24,512]{1,0:T(8,128)S(1)}, u32[]{:S(2)}, u32[]{:S(2)}) collective-permute-start(f32[24,512]{1,0:T(8,128)S(1)} %get-tuple-element.22), channel_id=1, source_target_pairs={{4,0},{8,4},{12,8},{0,12},{5,1},{9,5},{13,9},{1,13},{6,2},{10,6},{... | collective-permute-start | bytes 147464 | tf_op jit(solution)/shard_map/ppermute | solution.py:533
  5.2 4.6 %collective-permute-start.2 = (f32[8,512]{1,0:T(8,128)S(1)}, f32[8,512]{1,0:T(8,128)S(1)}, u32[]{:S(2)}, u32[]{:S(2)}) collective-permute-start(f32[8,512]{1,0:T(8,128)S(1)} %get-tuple-element.31), channel_id=1, source_target_pairs={{0,28},{1,12},{2,13},{3,14},{4,16},{5,0},{6,1},{7,2},{8,20},{9,4},... | collective-permute-start | bytes 49160 | tf_op jit(solution)/shard_map/ppermute | solution.py:555
  10.1 1.5 %collective-permute-start.3 = (f32[88,512]{1,0:T(8,128)S(1)}, f32[88,512]{1,0:T(8,128)S(1)}, u32[]{:S(2)}, u32[]{:S(2)}) collective-permute-start(f32[88,512]{1,0:T(8,128)S(1)} %shard_map.49.refs_0_), channel_id=1, source_target_pairs={{0,16},{16,0},{1,17},{17,1},{2,18},{18,2},{3,19},{19,3},{4,20},{20... | collective-permute-start | bytes 540680 | tf_op jit(solution)/shard_map/ppermute | solution.py:538
  11.6 7.0 %collective-permute-start.7 = (f32[4,16,512]{2,1,0:T(8,128)S(1)}, f32[4,16,512]{2,1,0:T(8,128)S(1)}, u32[]{:S(2)}, u32[]{:S(2)}) collective-permute-start(f32[4,16,512]{2,1,0:T(8,128)S(1)} %get-tuple-element.36), channel_id=1, source_target_pairs={{0,16},{1,0},{2,1},{3,2},{4,20},{5,4},{6,5},{7,6},{8,24},{9,8},{10... | collective-permute-start | bytes 393224 | tf_op jit(solution)/shard_map/ppermute | solution.py:555
  11.8 5.0 %collective-permute-start.4 = (f32[16,512]{1,0:T(8,128)S(1)}, f32[16,512]{1,0:T(8,128)S(1)}, u32[]{:S(2)}, u32[]{:S(2)}) collective-permute-start(f32[16,512]{1,0:T(8,128)S(1)} %get-tuple-element.33), channel_id=1, source_target_pairs={{0,16},{1,17},{2,18},{3,19},{4,20},{5,8},{6,9},{7,10},{8,24},{9,4}... | collective-permute-start | bytes 98312 | tf_op jit(solution)/shard_map/ppermute | solution.py:555
  13.5 4.8 %collective-permute-start.5 = (f32[16,512]{1,0:T(8,128)S(1)}, f32[16,512]{1,0:T(8,128)S(1)}, u32[]{:S(2)}, u32[]{:S(2)}) collective-permute-start(f32[16,512]{1,0:T(8,128)S(1)} %get-tuple-element.34), channel_id=1, source_target_pairs={{0,16},{1,4},{2,5},{3,6},{4,20},{5,0},{6,1},{7,2},{8,24},{9,12},{1... | collective-permute-start | bytes 98312 | tf_op jit(solution)/shard_map/ppermute | solution.py:555
  13.5 5.2 %collective-permute-start.6 = (f32[16,512]{1,0:T(8,128)S(1)}, f32[16,512]{1,0:T(8,128)S(1)}, u32[]{:S(2)}, u32[]{:S(2)}) collective-permute-start(f32[16,512]{1,0:T(8,128)S(1)} %get-tuple-element.35), channel_id=1, source_target_pairs={{0,4},{1,5},{2,6},{3,7},{4,0},{5,1},{6,2},{7,3},{8,12},{9,13},{10,... | collective-permute-start | bytes 98312 | tf_op jit(solution)/shard_map/ppermute | solution.py:567
  18.8 1.4 %collective-permute-start.8 = (f32[4,16,512]{2,1,0:T(8,128)S(1)}, f32[4,16,512]{2,1,0:T(8,128)S(1)}, u32[]{:S(2)}, u32[]{:S(2)}) collective-permute-start(f32[4,16,512]{2,1,0:T(8,128)S(1)} %shard_map.51.part), channel_id=1, source_target_pairs={{0,16},{16,0},{1,17},{17,1},{2,18},{18,2},{3,19},{19,3},{4,20},{20... | collective-permute-start | bytes 393224 | tf_op jit(solution)/shard_map/ppermute | solution.py:538

commit v30 on v29

--- a/solution.py
+++ b/solution.py
@@ -467,7 +467,7 @@
         out[:reach] = jnp.where(first_core, rows[:reach], rows[REACH:])
 
 
-def layers_kernel(h, d_in, e_in, y_in, z_in, out):
+def layers_kernel(h, d_in, y_in, e_in, z_in, out):
     zlen, ylen, xlen = out.shape
     reach = REACH * zlen
     first_core = on_first()
@@ -638,7 +638,7 @@
     e_in = opposed(e_send, -1, 0, start=0)
     y_in = beside(y_send)
     z_in = opposed(z_send, -1, 0)
-    (part,) = call(layers_kernel, [(zlen, ylen, xlen)], (h, d_in, e_in, y_in, z_in))
+    (part,) = call(layers_kernel, [(zlen, ylen, xlen)], (h, d_in, y_in, e_in, z_in))
     (out,) = call(sum_kernel, [(zlen, ylen, xlen)], (part, chip_swapped(part)))
     return out
 

time: 21 us -> 21.8 us (1.038)
  waiting for transfers between devices: 5.73 us -> 8.89 us
  starting transfers between devices: 10.6 us -> 8.19 us
    ppermute x1, waiting for transfers between devices: 0.38 us -> 2.61 us  [beside(): return lax.ppermute(value, ('load', 'sy', 'sz'), pairs)]
    ppermute x1, starting transfers between devices: 3.3 us -> 1.08 us  [beside(): return lax.ppermute(value, ('load', 'sy', 'sz'), pairs)]
    ppermute x5, waiting for transfers between devices: 2.96 us -> 3.53 us  [opposed(): return lax.ppermute(value, ('load', 'sy', 'sz'), pairs)]
    ppermute x2, starting transfers between devices: 0.51 us -> 0.14 us  [chip_swapped(): lax.ppermute(value, 'load', [(core, cores - 1 - core) for core in range(c...]
    ppermute x2, waiting for transfers between devices: 2.39 us -> 2.74 us  [chip_swapped(): lax.ppermute(value, 'load', [(core, cores - 1 - core) for core in range(c...]
  transfers between devices with their start and end apart: 9 -> 9, of which waited for: 6 -> 6; matrix products, arithmetic and copies ran while one was open for 0% -> 0% of each run, Pallas kernels for 11% -> 10%
where the time goes in v30:
time: 21.8 us; the launch traced here: 21.7 us
  waiting for transfers between devices  8.89 us (41%)
  starting transfers between devices  8.19 us (38%)
  Pallas kernels  4.52 us (21%)
    pallas_call x7, Pallas kernels, call(): pl.pallas_call(kernel, out_shape=shapes, in_specs=[pl.BlockSpec(memory_sp...  4.52 us
    ppermute x5, waiting for transfers between devices, opposed(): return lax.ppermute(value, ('load', 'sy', 'sz'), pairs)  3.53 us
    ppermute x1, starting transfers between devices, ring_moved(): return lax.ppermute(value, axis, [((k + 1) % size, k) for k in range(size)])  3.51 us
    ppermute x5, starting transfers between devices, opposed(): return lax.ppermute(value, ('load', 'sy', 'sz'), pairs)  3.46 us
    ppermute x2, waiting for transfers between devices, chip_swapped(): lax.ppermute(value, 'load', [(core, cores - 1 - core) for core in range(c...  2.74 us
    ppermute x1, waiting for transfers between devices, beside(): return lax.ppermute(value, ('load', 'sy', 'sz'), pairs)  2.61 us
    ppermute x1, starting transfers between devices, beside(): return lax.ppermute(value, ('load', 'sy', 'sz'), pairs)  1.08 us
  transfers between devices with their start and end apart: 9, of which 6 were waited for; matrix products, arithmetic and copies ran while one was open for 0% of the time, Pallas kernels for 10%

profile of v30, /device:TPU:0, one launch (start us, length us, event | category | flops | bytes accessed | tf_op | source)
XLA Modules:
  0.0 21.7 jit_solution(13965113628534538217)
XLA Ops:
  0.0 0.0 copy-start.1
  0.0 0.0 copy-start.3
  0.0 0.0 copy-start.2
  0.0 1.2 %shard_map.46 = (f32[8,512]{1,0:T(8,128)S(1)}, f32[7,16,512]{2,1,0:T(8,128)S(1)}, f32[24,512]{1,0:T(8,128)S(1)}) custom-call(f32[2,3,4,16,512]{4,3,2,1,0:T(8,128)} %refs_0_.3, s32[4,16,512]{2,1,0:T(8,128)} %refs_1_.3, f32[4,16,512]{2,1,0:T(8,128)} %refs_2_.3, s32[4,16,512]{2,1,0:T(8,128)} %refs_3_.3), custom_call_target="tpu_custom_call" | custom-call | tf_op jit(solution)/shard_map/pallas_call | solution.py:521
  1.2 0.5 %collective-permute-start = (f32[7,16,512]{2,1,0:T(8,128)S(1)}, f32[7,16,512]{2,1,0:T(8,128)S(1)}, u32[]{:S(2)}, u32[]{:S(2)}) collective-permute-start(f32[7,16,512]{2,1,0:T(8,128)S(1)} %get-tuple-element.21), channel_id=1, source_target_pairs={{0,16},{1,0},{2,1},{3,2},{4,20},{5,4},{6,5},{7,6},{8,24},{9,8},{10... | collective-permute-start | bytes 688136 | tf_op jit(solution)/shard_map/ppermute | solution.py:555
  1.7 3.5 %collective-permute-start.1 = (f32[24,512]{1,0:T(8,128)S(1)}, f32[24,512]{1,0:T(8,128)S(1)}, u32[]{:S(2)}, u32[]{:S(2)}) collective-permute-start(f32[24,512]{1,0:T(8,128)S(1)} %get-tuple-element.22), channel_id=1, source_target_pairs={{4,0},{8,4},{12,8},{0,12},{5,1},{9,5},{13,9},{1,13},{6,2},{10,6},{... | collective-permute-start | bytes 147464 | tf_op jit(solution)/shard_map/ppermute | solution.py:533
  5.2 0.9 %collective-permute-start.2 = (f32[8,512]{1,0:T(8,128)S(1)}, f32[8,512]{1,0:T(8,128)S(1)}, u32[]{:S(2)}, u32[]{:S(2)}) collective-permute-start(f32[8,512]{1,0:T(8,128)S(1)} %get-tuple-element.31), channel_id=1, source_target_pairs={{0,28},{1,12},{2,13},{3,14},{4,16},{5,0},{6,1},{7,2},{8,20},{9,4},... | collective-permute-start | bytes 49160 | tf_op jit(solution)/shard_map/ppermute | solution.py:555
  6.1 0.0 copy-done.1
  6.1 0.0 copy-done.3
  6.1 0.0 copy-done.2
  6.1 0.0 copy-done
  6.1 1.6 %shard_map.47 = (f32[4,16,512]{2,1,0:T(8,128)S(1)}, f32[2,24,512]{2,1,0:T(8,128)S(1)}, f32[2,9,512]{2,1,0:T(8,128)S(1)}, f32[4,6,16,512]{3,2,1,0:T(8,128)S(1)}, ...) custom-call(f32[2,3,4,16,512]{4,3,2,1,0:T(8,128)S(1)} %copy-done, s32[4,16,512]{2,1,0:T(8,128)S(1)} %copy-done.1, ...), custom_call_target="tpu_custom_call" | custom-call | tf_op jit(solution)/shard_map/pallas_call | solution.py:521
  7.7 0.0 collective-permute-done.1.refs_1_.refs_2_
  7.7 0.5 %collective-permute-done.refs_0_ = f32[7,16,512]{2,1,0:T(8,128)S(1)} collective-permute-done((f32[7,16,512]{2,1,0:T(8,128)S(1)}, f32[7,16,512]{2,1,0:T(8,128)S(1)}, u32[]{:S(2)}, u32[]{:S(2)}) %collective-permute-start) | collective-permute-done | bytes 229408 | tf_op jit(solution)/shard_map/ppermute | solution.py:555
  8.2 0.6 %shard_map.48 = (f32[88,512]{1,0:T(8,128)S(1)}, f32[4,8,512]{2,1,0:T(8,128)S(1)}) custom-call(f32[7,16,512]{2,1,0:T(8,128)S(1)} %collective-permute-done.refs_0_, f32[24,512]{1,0:T(8,128)S(1)} %collective-permute-done.1.refs_1_.refs_2_, f32[4,16,512]{2,1,0:T(8,128)S(1)} %get-tuple-element.23.refs_2_, f32[2,24,512]{2,1,0:T(8,128)S(1)} %get-tuple-element.24.refs_3_, ...), custom_call_target="tpu_custom_call" | custom-call | tf_op jit(solution)/shard_map/pallas_call | solution.py:521
  8.9 0.9 %collective-permute-done.2.refs_3_ = f32[8,512]{1,0:T(8,128)S(1)} collective-permute-done((f32[8,512]{1,0:T(8,128)S(1)}, f32[8,512]{1,0:T(8,128)S(1)}, u32[]{:S(2)}, u32[]{:S(2)}) %collective-permute-start.2) | collective-permute-done | bytes 16416 | tf_op jit(solution)/shard_map/ppermute | solution.py:555
  9.8 0.3 %shard_map.49.refs_0_ = f32[88,512]{1,0:T(8,128)S(1)} custom-call(f32[88,512]{1,0:T(8,128)S(1)} %get-tuple-element.29.refs_0_, f32[4,8,512]{2,1,0:T(8,128)S(1)} %get-tuple-element.30.refs_1_, f32[24,512]{1,0:T(8,128)S(1)} %collective-permute-done.1.refs_1_.refs_2_, f32[8,512]{1,0:T(8,128)S(1)} %collective-permute-done.2.refs_3_), custom_call_target="tpu_custom_call" | custom-call | tf_op jit(solution)/shard_map/pallas_call | solution.py:521
  10.1 0.1 collective-permute-start.3
  10.2 1.4 %collective-permute-done.3.refs_1_ = f32[88,512]{1,0:T(8,128)S(1)} collective-permute-done((f32[88,512]{1,0:T(8,128)S(1)}, f32[88,512]{1,0:T(8,128)S(1)}, u32[]{:S(2)}, u32[]{:S(2)}) %collective-permute-start.3) | collective-permute-done | bytes 180256 | tf_op jit(solution)/shard_map/ppermute | solution.py:538
  11.6 0.1 shard_map.50
  11.6 0.2 collective-permute-start.7
  11.8 1.7 %collective-permute-start.4 = (f32[16,512]{1,0:T(8,128)S(1)}, f32[16,512]{1,0:T(8,128)S(1)}, u32[]{:S(2)}, u32[]{:S(2)}) collective-permute-start(f32[16,512]{1,0:T(8,128)S(1)} %get-tuple-element.33), channel_id=1, source_target_pairs={{0,16},{1,17},{2,18},{3,19},{4,20},{5,8},{6,9},{7,10},{8,24},{9,4}... | collective-permute-start | bytes 98312 | tf_op jit(solution)/shard_map/ppermute | solution.py:555
  13.5 1.1 %collective-permute-start.5 = (f32[16,512]{1,0:T(8,128)S(1)}, f32[16,512]{1,0:T(8,128)S(1)}, u32[]{:S(2)}, u32[]{:S(2)}) collective-permute-start(f32[16,512]{1,0:T(8,128)S(1)} %get-tuple-element.34), channel_id=1, source_target_pairs={{0,4},{1,5},{2,6},{3,7},{4,0},{5,1},{6,2},{7,3},{8,12},{9,13},{10,... | collective-permute-start | bytes 98312 | tf_op jit(solution)/shard_map/ppermute | solution.py:567
  14.6 0.2 %collective-permute-start.6 = (f32[16,512]{1,0:T(8,128)S(1)}, f32[16,512]{1,0:T(8,128)S(1)}, u32[]{:S(2)}, u32[]{:S(2)}) collective-permute-start(f32[16,512]{1,0:T(8,128)S(1)} %get-tuple-element.35), channel_id=1, source_target_pairs={{0,16},{1,4},{2,5},{3,6},{4,20},{5,0},{6,1},{7,2},{8,24},{9,12},{1... | collective-permute-start | bytes 98312 | tf_op jit(solution)/shard_map/ppermute | solution.py:555
  14.8 0.0 collective-permute-done.4.d_in
  14.8 2.6 %collective-permute-done.5.y_in = f32[16,512]{1,0:T(8,128)S(1)} collective-permute-done((f32[16,512]{1,0:T(8,128)S(1)}, f32[16,512]{1,0:T(8,128)S(1)}, u32[]{:S(2)}, u32[]{:S(2)}) %collective-permute-start.5) | collective-permute-done | bytes 32800 | tf_op jit(solution)/shard_map/ppermute | solution.py:567
  17.4 2.1 %collective-permute-done.6.e_in = f32[16,512]{1,0:T(8,128)S(1)} collective-permute-done((f32[16,512]{1,0:T(8,128)S(1)}, f32[16,512]{1,0:T(8,128)S(1)}, u32[]{:S(2)}, u32[]{:S(2)}) %collective-permute-start.6) | collective-permute-done | bytes 32800 | tf_op jit(solution)/shard_map/ppermute | solution.py:555
  19.5 0.0 collective-permute-done.7.z_in
  19.5 0.1 shard_map.51.part
  19.6 0.1 collective-permute-start.8
  19.7 1.3 %collective-permute-done.8.other = f32[4,16,512]{2,1,0:T(8,128)S(1)} collective-permute-done((f32[4,16,512]{2,1,0:T(8,128)S(1)}, f32[4,16,512]{2,1,0:T(8,128)S(1)}, u32[]{:S(2)}, u32[]{:S(2)}) %collective-permute-start.8) | collective-permute-done | bytes 131104 | tf_op jit(solution)/shard_map/ppermute | solution.py:538
  21.0 0.7 %shard_map.52 = f32[4,16,512]{2,1,0:T(8,128)} custom-call(f32[4,16,512]{2,1,0:T(8,128)S(1)} %shard_map.51.part, f32[4,16,512]{2,1,0:T(8,128)S(1)} %collective-permute-done.8.other), custom_call_target="tpu_custom_call" | custom-call | tf_op jit(solution)/shard_map/pallas_call | solution.py:521
  (1 shorter events, 0.0 us)
Async XLA Ops:
  0.0 6.1 %copy-start.1 = (s32[4,16,512]{2,1,0:T(8,128)S(1)}, s32[4,16,512]{2,1,0:T(8,128)}, u32[]{:S(2)}) copy-start(s32[4,16,512]{2,1,0:T(8,128)} %refs_1_.3) | copy-start | bytes 393220
  0.0 6.1 %copy-start.3 = (s32[4,16,512]{2,1,0:T(8,128)S(1)}, s32[4,16,512]{2,1,0:T(8,128)}, u32[]{:S(2)}) copy-start(s32[4,16,512]{2,1,0:T(8,128)} %refs_3_.3) | copy-start | bytes 393220
  0.0 6.1 %copy-start.2 = (f32[4,16,512]{2,1,0:T(8,128)S(1)}, f32[4,16,512]{2,1,0:T(8,128)}, u32[]{:S(2)}) copy-start(f32[4,16,512]{2,1,0:T(8,128)} %refs_2_.3) | copy-start | bytes 393220
  0.0 6.1 %copy-start = (f32[2,3,4,16,512]{4,3,2,1,0:T(8,128)S(1)}, f32[2,3,4,16,512]{4,3,2,1,0:T(8,128)}, u32[]{:S(2)}) copy-start(f32[2,3,4,16,512]{4,3,2,1,0:T(8,128)} %refs_0_.3) | copy-start | bytes 2359300
  1.2 7.1 %collective-permute-start = (f32[7,16,512]{2,1,0:T(8,128)S(1)}, f32[7,16,512]{2,1,0:T(8,128)S(1)}, u32[]{:S(2)}, u32[]{:S(2)}) collective-permute-start(f32[7,16,512]{2,1,0:T(8,128)S(1)} %get-tuple-element.21), channel_id=1, source_target_pairs={{0,16},{1,0},{2,1},{3,2},{4,20},{5,4},{6,5},{7,6},{8,24},{9,8},{10... | collective-permute-start | bytes 688136 | tf_op jit(solution)/shard_map/ppermute | solution.py:555
  1.7 6.0 %collective-permute-start.1 = (f32[24,512]{1,0:T(8,128)S(1)}, f32[24,512]{1,0:T(8,128)S(1)}, u32[]{:S(2)}, u32[]{:S(2)}) collective-permute-start(f32[24,512]{1,0:T(8,128)S(1)} %get-tuple-element.22), channel_id=1, source_target_pairs={{4,0},{8,4},{12,8},{0,12},{5,1},{9,5},{13,9},{1,13},{6,2},{10,6},{... | collective-permute-start | bytes 147464 | tf_op jit(solution)/shard_map/ppermute | solution.py:533
  5.2 4.6 %collective-permute-start.2 = (f32[8,512]{1,0:T(8,128)S(1)}, f32[8,512]{1,0:T(8,128)S(1)}, u32[]{:S(2)}, u32[]{:S(2)}) collective-permute-start(f32[8,512]{1,0:T(8,128)S(1)} %get-tuple-element.31), channel_id=1, source_target_pairs={{0,28},{1,12},{2,13},{3,14},{4,16},{5,0},{6,1},{7,2},{8,20},{9,4},... | collective-permute-start | bytes 49160 | tf_op jit(solution)/shard_map/ppermute | solution.py:555
  10.1 1.5 %collective-permute-start.3 = (f32[88,512]{1,0:T(8,128)S(1)}, f32[88,512]{1,0:T(8,128)S(1)}, u32[]{:S(2)}, u32[]{:S(2)}) collective-permute-start(f32[88,512]{1,0:T(8,128)S(1)} %shard_map.49.refs_0_), channel_id=1, source_target_pairs={{0,16},{16,0},{1,17},{17,1},{2,18},{18,2},{3,19},{19,3},{4,20},{20... | collective-permute-start | bytes 540680 | tf_op jit(solution)/shard_map/ppermute | solution.py:538
  11.6 7.8 %collective-permute-start.7 = (f32[4,16,512]{2,1,0:T(8,128)S(1)}, f32[4,16,512]{2,1,0:T(8,128)S(1)}, u32[]{:S(2)}, u32[]{:S(2)}) collective-permute-start(f32[4,16,512]{2,1,0:T(8,128)S(1)} %get-tuple-element.36), channel_id=1, source_target_pairs={{0,16},{1,0},{2,1},{3,2},{4,20},{5,4},{6,5},{7,6},{8,24},{9,8},{10... | collective-permute-start | bytes 393224 | tf_op jit(solution)/shard_map/ppermute | solution.py:555
  11.8 3.0 %collective-permute-start.4 = (f32[16,512]{1,0:T(8,128)S(1)}, f32[16,512]{1,0:T(8,128)S(1)}, u32[]{:S(2)}, u32[]{:S(2)}) collective-permute-start(f32[16,512]{1,0:T(8,128)S(1)} %get-tuple-element.33), channel_id=1, source_target_pairs={{0,16},{1,17},{2,18},{3,19},{4,20},{5,8},{6,9},{7,10},{8,24},{9,4}... | collective-permute-start | bytes 98312 | tf_op jit(solution)/shard_map/ppermute | solution.py:555
  13.5 3.9 %collective-permute-start.5 = (f32[16,512]{1,0:T(8,128)S(1)}, f32[16,512]{1,0:T(8,128)S(1)}, u32[]{:S(2)}, u32[]{:S(2)}) collective-permute-start(f32[16,512]{1,0:T(8,128)S(1)} %get-tuple-element.34), channel_id=1, source_target_pairs={{0,4},{1,5},{2,6},{3,7},{4,0},{5,1},{6,2},{7,3},{8,12},{9,13},{10,... | collective-permute-start | bytes 98312 | tf_op jit(solution)/shard_map/ppermute | solution.py:567
  14.6 4.9 %collective-permute-start.6 = (f32[16,512]{1,0:T(8,128)S(1)}, f32[16,512]{1,0:T(8,128)S(1)}, u32[]{:S(2)}, u32[]{:S(2)}) collective-permute-start(f32[16,512]{1,0:T(8,128)S(1)} %get-tuple-element.35), channel_id=1, source_target_pairs={{0,16},{1,4},{2,5},{3,6},{4,20},{5,0},{6,1},{7,2},{8,24},{9,12},{1... | collective-permute-start | bytes 98312 | tf_op jit(solution)/shard_map/ppermute | solution.py:555
  19.6 1.4 %collective-permute-start.8 = (f32[4,16,512]{2,1,0:T(8,128)S(1)}, f32[4,16,512]{2,1,0:T(8,128)S(1)}, u32[]{:S(2)}, u32[]{:S(2)}) collective-permute-start(f32[4,16,512]{2,1,0:T(8,128)S(1)} %shard_map.51.part), channel_id=1, source_target_pairs={{0,16},{16,0},{1,17},{17,1},{2,18},{18,2},{3,19},{19,3},{4,20},{20... | collective-permute-start | bytes 393224 | tf_op jit(solution)/shard_map/ppermute | solution.py:538

commit v31 on v29

--- a/solution.py
+++ b/solution.py
@@ -225,7 +225,8 @@
         for comp in range(comps):
             k = case * comps + comp
             z_out[k] = layer[case, comp] * free
-            d_out[k : k + 1] = z_out[k, :1]
+            at = comp * loads + case
+            d_out[at : at + 1] = z_out[k, :1]
     for copy in copies[4:]:
         copy.wait()
     for z in range(zlen):
@@ -324,10 +325,10 @@
         for kind, value in enumerate(face_sums(z_in[k])):
             faces[kind, k, stays] = last_faces[kind, k]
             faces[kind, k, comes] = value
-        come_rows.append(z_in[k, ylen - 1 :])
-        at = (k % comps * loads + k // comps) * zlen
+        come_rows.append(z_in[k % loads * comps + k // loads, ylen - 1 :])
         for group in range(2):
-            corner[group, k : k + 1] = jnp.where(first_core, line[group, at + inner : at + zlen], line[group, at : at + 1])
+            rows = line[group, k * zlen + inner : (k + 1) * zlen], line[group, k * zlen : k * zlen + 1]
+            corner[group, k : k + 1] = jnp.where(first_core, *rows)
     come_rows.append(jnp.zeros((-planes % TILE, xlen), jnp.float32))
     for group, value in enumerate(split_x(jnp.concatenate(come_rows, axis=0))):
         corner[2 + group, :planes] = value[:planes]
@@ -400,31 +401,31 @@
     first_core = on_first()
     top = first_core & (lax.axis_index("sz") == lax.axis_size("sz") - 1)
     more = lax.axis_index("sy") < lax.axis_size("sy") - 1
-    rows = []
-    for k in range(planes):
-        at = (k % comps * loads + k // comps) * zlen
-        rows.append(jnp.where(first_core, y_in[at + zlen - 1 : at + zlen], y_in[at : at + 1]))
+    rows = [jnp.where(first_core, y_in[(k + 1) * zlen - 1 : (k + 1) * zlen], y_in[k * zlen : k * zlen + 1]) for k in range(planes)]
     rows.append(jnp.zeros((-planes % TILE, xlen), jnp.float32))
     stays_next = split_x(jnp.where(more, jnp.concatenate(rows, axis=0), 0.0))
     comes_next = split_x(jnp.where(more, d_in[...], 0.0))
-
-    def faces(stays, comes, comp):
-        zero = jnp.zeros((1, xlen), jnp.float32)
-        under, over = [], []
-        for own, other in zip(stays, comes):
-            own, other = ([value[case * comps + comp : case * comps + comp + 1] for case in range(loads)] for value in (own, other))
-            low = [jnp.where(first_core, a, b) for a, b in zip(own, other)] + [jnp.where(top, b, 0.0) for b in other]
-            high = [jnp.where(first_core, jnp.where(top, 0.0, b), a) for a, b in zip(own, other)] + [zero] * loads
-            under.append(jnp.concatenate(low, axis=0))
-            over.append(jnp.concatenate(high, axis=0))
-        return under, over
-
+    zero = jnp.zeros((loads, xlen), jnp.float32)
+
+    def face(near, far, comp, more_near, more_far):
+        part = slice(comp * loads, (comp + 1) * loads)
+        (whole, change), (whole_next, change_next) = (
+            [jnp.concatenate([value[part], zero if extra is None else extra[part]], axis=0) for value, extra in zip(values, extras)]
+            for values, extras in ((near, more_near), (far, more_far))
+        )
+        return whole + whole_next, change + change_next, whole_next - whole, change_next - change
+
+    def under(stays, comes):
+        return [jnp.where(first_core, a, b) for a, b in zip(stays, comes)], [jnp.where(top, b, 0.0) for b in comes]
+
+    def over(stays, comes):
+        return [jnp.where(first_core, jnp.where(top, 0.0, b), a) for a, b in zip(stays, comes)], (None, None)
+
+    near, far = ((corner[0], corner[1]), (corner[2], corner[3])), (stays_next, comes_next)
     low, high = [], []
-    for comp in range(comps):
-        near = faces((corner[0], corner[1]), (corner[2], corner[3]), comp)
-        far = faces(stays_next, comes_next, comp)
-        for (whole, change), (whole_next, change_next), into in zip(near, far, (low, high)):
-            into.append((whole + whole_next, change + change_next, whole_next - whole, change_next - change))
+    for side, into in ((under, low), (over, high)):
+        (near_own, near_more), (far_own, far_more) = side(*near), side(*far)
+        into += [face(near_own, far_own, comp, near_more, far_more) for comp in range(comps)]
     energy = quadratic(low, high, mode_weights())
     line = sum(energy[case : case + 1] for case in range(2 * loads)) * corner[0, planes : planes + 1]
     return spread_x(jnp.concatenate([line, jnp.zeros((TILE - 1, xlen), jnp.float32)], axis=0))[:1]

time: 21 us -> 21 us (level)
  no operation moved by 1% of the time
where the time goes in v31:
time: 21 us; the launch traced here: 20.9 us
  starting transfers between devices  10.6 us (50%)
  waiting for transfers between devices  5.73 us (27%)
  Pallas kernels  4.5 us (21%)
    pallas_call x7, Pallas kernels, call(): pl.pallas_call(kernel, out_shape=shapes, in_specs=[pl.BlockSpec(memory_sp...  4.5 us
    ppermute x1, starting transfers between devices, ring_moved(): return lax.ppermute(value, axis, [((k + 1) % size, k) for k in range(size)])  3.51 us
    ppermute x1, starting transfers between devices, beside(): return lax.ppermute(value, ('load', 'sy', 'sz'), pairs)  3.3 us
    ppermute x5, starting transfers between devices, opposed(): return lax.ppermute(value, ('load', 'sy', 'sz'), pairs)  3.25 us
    ppermute x5, waiting for transfers between devices, opposed(): return lax.ppermute(value, ('load', 'sy', 'sz'), pairs)  2.96 us
    ppermute x2, waiting for transfers between devices, chip_swapped(): lax.ppermute(value, 'load', [(core, cores - 1 - core) for core in range(c...  2.39 us
    ppermute x2, starting transfers between devices, chip_swapped(): lax.ppermute(value, 'load', [(core, cores - 1 - core) for core in range(c...  0.51 us
  transfers between devices with their start and end apart: 9, of which 6 were waited for; matrix products, arithmetic and copies ran while one was open for 0% of the time, Pallas kernels for 11%

profile of v31, /device:TPU:0, one launch (start us, length us, event | category | flops | bytes accessed | tf_op | source)
XLA Modules:
  0.0 20.9 jit_solution(10056802552479643076)
XLA Ops:
  0.0 0.0 copy-start.1
  0.0 0.0 copy-start.3
  0.0 0.0 copy-start.2
  0.0 1.2 %shard_map.46 = (f32[8,512]{1,0:T(8,128)S(1)}, f32[7,16,512]{2,1,0:T(8,128)S(1)}, f32[24,512]{1,0:T(8,128)S(1)}) custom-call(f32[2,3,4,16,512]{4,3,2,1,0:T(8,128)} %refs_0_.3, s32[4,16,512]{2,1,0:T(8,128)} %refs_1_.3, f32[4,16,512]{2,1,0:T(8,128)} %refs_2_.3, s32[4,16,512]{2,1,0:T(8,128)} %refs_3_.3), custom_call_target="tpu_custom_call" | custom-call | tf_op jit(solution)/shard_map/pallas_call | solution.py:522
  1.2 0.5 %collective-permute-start = (f32[7,16,512]{2,1,0:T(8,128)S(1)}, f32[7,16,512]{2,1,0:T(8,128)S(1)}, u32[]{:S(2)}, u32[]{:S(2)}) collective-permute-start(f32[7,16,512]{2,1,0:T(8,128)S(1)} %get-tuple-element.21), channel_id=1, source_target_pairs={{0,16},{1,0},{2,1},{3,2},{4,20},{5,4},{6,5},{7,6},{8,24},{9,8},{10... | collective-permute-start | bytes 688136 | tf_op jit(solution)/shard_map/ppermute | solution.py:556
  1.7 3.5 %collective-permute-start.1 = (f32[24,512]{1,0:T(8,128)S(1)}, f32[24,512]{1,0:T(8,128)S(1)}, u32[]{:S(2)}, u32[]{:S(2)}) collective-permute-start(f32[24,512]{1,0:T(8,128)S(1)} %get-tuple-element.22), channel_id=1, source_target_pairs={{4,0},{8,4},{12,8},{0,12},{5,1},{9,5},{13,9},{1,13},{6,2},{10,6},{... | collective-permute-start | bytes 147464 | tf_op jit(solution)/shard_map/ppermute | solution.py:534
  5.2 0.9 %collective-permute-start.2 = (f32[8,512]{1,0:T(8,128)S(1)}, f32[8,512]{1,0:T(8,128)S(1)}, u32[]{:S(2)}, u32[]{:S(2)}) collective-permute-start(f32[8,512]{1,0:T(8,128)S(1)} %get-tuple-element.31), channel_id=1, source_target_pairs={{0,28},{1,12},{2,13},{3,14},{4,16},{5,0},{6,1},{7,2},{8,20},{9,4},... | collective-permute-start | bytes 49160 | tf_op jit(solution)/shard_map/ppermute | solution.py:556
  6.1 0.0 copy-done.1
  6.1 0.0 copy-done.3
  6.1 0.0 copy-done.2
  6.1 0.0 copy-done
  6.1 1.6 %shard_map.47 = (f32[4,16,512]{2,1,0:T(8,128)S(1)}, f32[2,24,512]{2,1,0:T(8,128)S(1)}, f32[2,9,512]{2,1,0:T(8,128)S(1)}, f32[4,6,16,512]{3,2,1,0:T(8,128)S(1)}, ...) custom-call(f32[2,3,4,16,512]{4,3,2,1,0:T(8,128)S(1)} %copy-done, s32[4,16,512]{2,1,0:T(8,128)S(1)} %copy-done.1, ...), custom_call_target="tpu_custom_call" | custom-call | tf_op jit(solution)/shard_map/pallas_call | solution.py:522
  7.7 0.0 collective-permute-done.1.refs_1_.refs_2_
  7.7 0.5 %collective-permute-done.refs_0_ = f32[7,16,512]{2,1,0:T(8,128)S(1)} collective-permute-done((f32[7,16,512]{2,1,0:T(8,128)S(1)}, f32[7,16,512]{2,1,0:T(8,128)S(1)}, u32[]{:S(2)}, u32[]{:S(2)}) %collective-permute-start) | collective-permute-done | bytes 229408 | tf_op jit(solution)/shard_map/ppermute | solution.py:556
  8.2 0.6 %shard_map.48 = (f32[88,512]{1,0:T(8,128)S(1)}, f32[4,8,512]{2,1,0:T(8,128)S(1)}) custom-call(f32[7,16,512]{2,1,0:T(8,128)S(1)} %collective-permute-done.refs_0_, f32[24,512]{1,0:T(8,128)S(1)} %collective-permute-done.1.refs_1_.refs_2_, f32[4,16,512]{2,1,0:T(8,128)S(1)} %get-tuple-element.23.refs_2_, f32[2,24,512]{2,1,0:T(8,128)S(1)} %get-tuple-element.24.refs_3_, ...), custom_call_target="tpu_custom_call" | custom-call | tf_op jit(solution)/shard_map/pallas_call | solution.py:522
  8.9 0.9 %collective-permute-done.2.refs_3_ = f32[8,512]{1,0:T(8,128)S(1)} collective-permute-done((f32[8,512]{1,0:T(8,128)S(1)}, f32[8,512]{1,0:T(8,128)S(1)}, u32[]{:S(2)}, u32[]{:S(2)}) %collective-permute-start.2) | collective-permute-done | bytes 16416 | tf_op jit(solution)/shard_map/ppermute | solution.py:556
  9.8 0.3 %shard_map.49.refs_0_ = f32[88,512]{1,0:T(8,128)S(1)} custom-call(f32[88,512]{1,0:T(8,128)S(1)} %get-tuple-element.29.refs_0_, f32[4,8,512]{2,1,0:T(8,128)S(1)} %get-tuple-element.30.refs_1_, f32[24,512]{1,0:T(8,128)S(1)} %collective-permute-done.1.refs_1_.refs_2_, f32[8,512]{1,0:T(8,128)S(1)} %collective-permute-done.2.refs_3_), custom_call_target="tpu_custom_call" | custom-call | tf_op jit(solution)/shard_map/pallas_call | solution.py:522
  10.1 0.1 collective-permute-start.3
  10.2 1.4 %collective-permute-done.3.refs_1_ = f32[88,512]{1,0:T(8,128)S(1)} collective-permute-done((f32[88,512]{1,0:T(8,128)S(1)}, f32[88,512]{1,0:T(8,128)S(1)}, u32[]{:S(2)}, u32[]{:S(2)}) %collective-permute-start.3) | collective-permute-done | bytes 180256 | tf_op jit(solution)/shard_map/ppermute | solution.py:539
  11.6 0.1 shard_map.50
  11.6 0.2 collective-permute-start.7
  11.8 1.7 %collective-permute-start.4 = (f32[16,512]{1,0:T(8,128)S(1)}, f32[16,512]{1,0:T(8,128)S(1)}, u32[]{:S(2)}, u32[]{:S(2)}) collective-permute-start(f32[16,512]{1,0:T(8,128)S(1)} %get-tuple-element.33), channel_id=1, source_target_pairs={{0,16},{1,17},{2,18},{3,19},{4,20},{5,8},{6,9},{7,10},{8,24},{9,4}... | collective-permute-start | bytes 98312 | tf_op jit(solution)/shard_map/ppermute | solution.py:556
  13.5 0.0 collective-permute-start.5
  13.5 3.3 %collective-permute-start.6 = (f32[16,512]{1,0:T(8,128)S(1)}, f32[16,512]{1,0:T(8,128)S(1)}, u32[]{:S(2)}, u32[]{:S(2)}) collective-permute-start(f32[16,512]{1,0:T(8,128)S(1)} %get-tuple-element.35), channel_id=1, source_target_pairs={{0,4},{1,5},{2,6},{3,7},{4,0},{5,1},{6,2},{7,3},{8,12},{9,13},{10,... | collective-permute-start | bytes 98312 | tf_op jit(solution)/shard_map/ppermute | solution.py:568
  16.8 0.0 collective-permute-done.4.d_in
  16.8 1.5 %collective-permute-done.5.e_in = f32[16,512]{1,0:T(8,128)S(1)} collective-permute-done((f32[16,512]{1,0:T(8,128)S(1)}, f32[16,512]{1,0:T(8,128)S(1)}, u32[]{:S(2)}, u32[]{:S(2)}) %collective-permute-start.5) | collective-permute-done | bytes 32800 | tf_op jit(solution)/shard_map/ppermute | solution.py:556
  18.3 0.4 %collective-permute-done.6.y_in = f32[16,512]{1,0:T(8,128)S(1)} collective-permute-done((f32[16,512]{1,0:T(8,128)S(1)}, f32[16,512]{1,0:T(8,128)S(1)}, u32[]{:S(2)}, u32[]{:S(2)}) %collective-permute-start.6) | collective-permute-done | bytes 32800 | tf_op jit(solution)/shard_map/ppermute | solution.py:568
  18.7 0.0 collective-permute-done.7.z_in
  18.7 0.1 shard_map.51.part
  18.8 0.4 %collective-permute-start.8 = (f32[4,16,512]{2,1,0:T(8,128)S(1)}, f32[4,16,512]{2,1,0:T(8,128)S(1)}, u32[]{:S(2)}, u32[]{:S(2)}) collective-permute-start(f32[4,16,512]{2,1,0:T(8,128)S(1)} %shard_map.51.part), channel_id=1, source_target_pairs={{0,16},{16,0},{1,17},{17,1},{2,18},{18,2},{3,19},{19,3},{4,20},{20... | collective-permute-start | bytes 393224 | tf_op jit(solution)/shard_map/ppermute | solution.py:539
  19.2 1.0 %collective-permute-done.8.other = f32[4,16,512]{2,1,0:T(8,128)S(1)} collective-permute-done((f32[4,16,512]{2,1,0:T(8,128)S(1)}, f32[4,16,512]{2,1,0:T(8,128)S(1)}, u32[]{:S(2)}, u32[]{:S(2)}) %collective-permute-start.8) | collective-permute-done | bytes 131104 | tf_op jit(solution)/shard_map/ppermute | solution.py:539
  20.2 0.7 %shard_map.52 = f32[4,16,512]{2,1,0:T(8,128)} custom-call(f32[4,16,512]{2,1,0:T(8,128)S(1)} %shard_map.51.part, f32[4,16,512]{2,1,0:T(8,128)S(1)} %collective-permute-done.8.other), custom_call_target="tpu_custom_call" | custom-call | tf_op jit(solution)/shard_map/pallas_call | solution.py:522
  (1 shorter events, 0.0 us)
Async XLA Ops:
  0.0 6.1 %copy-start.1 = (s32[4,16,512]{2,1,0:T(8,128)S(1)}, s32[4,16,512]{2,1,0:T(8,128)}, u32[]{:S(2)}) copy-start(s32[4,16,512]{2,1,0:T(8,128)} %refs_1_.3) | copy-start | bytes 393220
  0.0 6.1 %copy-start.3 = (s32[4,16,512]{2,1,0:T(8,128)S(1)}, s32[4,16,512]{2,1,0:T(8,128)}, u32[]{:S(2)}) copy-start(s32[4,16,512]{2,1,0:T(8,128)} %refs_3_.3) | copy-start | bytes 393220
  0.0 6.1 %copy-start.2 = (f32[4,16,512]{2,1,0:T(8,128)S(1)}, f32[4,16,512]{2,1,0:T(8,128)}, u32[]{:S(2)}) copy-start(f32[4,16,512]{2,1,0:T(8,128)} %refs_2_.3) | copy-start | bytes 393220
  0.0 6.1 %copy-start = (f32[2,3,4,16,512]{4,3,2,1,0:T(8,128)S(1)}, f32[2,3,4,16,512]{4,3,2,1,0:T(8,128)}, u32[]{:S(2)}) copy-start(f32[2,3,4,16,512]{4,3,2,1,0:T(8,128)} %refs_0_.3) | copy-start | bytes 2359300
  1.2 7.1 %collective-permute-start = (f32[7,16,512]{2,1,0:T(8,128)S(1)}, f32[7,16,512]{2,1,0:T(8,128)S(1)}, u32[]{:S(2)}, u32[]{:S(2)}) collective-permute-start(f32[7,16,512]{2,1,0:T(8,128)S(1)} %get-tuple-element.21), channel_id=1, source_target_pairs={{0,16},{1,0},{2,1},{3,2},{4,20},{5,4},{6,5},{7,6},{8,24},{9,8},{10... | collective-permute-start | bytes 688136 | tf_op jit(solution)/shard_map/ppermute | solution.py:556
  1.7 6.0 %collective-permute-start.1 = (f32[24,512]{1,0:T(8,128)S(1)}, f32[24,512]{1,0:T(8,128)S(1)}, u32[]{:S(2)}, u32[]{:S(2)}) collective-permute-start(f32[24,512]{1,0:T(8,128)S(1)} %get-tuple-element.22), channel_id=1, source_target_pairs={{4,0},{8,4},{12,8},{0,12},{5,1},{9,5},{13,9},{1,13},{6,2},{10,6},{... | collective-permute-start | bytes 147464 | tf_op jit(solution)/shard_map/ppermute | solution.py:534
  5.2 4.6 %collective-permute-start.2 = (f32[8,512]{1,0:T(8,128)S(1)}, f32[8,512]{1,0:T(8,128)S(1)}, u32[]{:S(2)}, u32[]{:S(2)}) collective-permute-start(f32[8,512]{1,0:T(8,128)S(1)} %get-tuple-element.31), channel_id=1, source_target_pairs={{0,28},{1,12},{2,13},{3,14},{4,16},{5,0},{6,1},{7,2},{8,20},{9,4},... | collective-permute-start | bytes 49160 | tf_op jit(solution)/shard_map/ppermute | solution.py:556
  10.1 1.5 %collective-permute-start.3 = (f32[88,512]{1,0:T(8,128)S(1)}, f32[88,512]{1,0:T(8,128)S(1)}, u32[]{:S(2)}, u32[]{:S(2)}) collective-permute-start(f32[88,512]{1,0:T(8,128)S(1)} %shard_map.49.refs_0_), channel_id=1, source_target_pairs={{0,16},{16,0},{1,17},{17,1},{2,18},{18,2},{3,19},{19,3},{4,20},{20... | collective-permute-start | bytes 540680 | tf_op jit(solution)/shard_map/ppermute | solution.py:539
  11.6 7.0 %collective-permute-start.7 = (f32[4,16,512]{2,1,0:T(8,128)S(1)}, f32[4,16,512]{2,1,0:T(8,128)S(1)}, u32[]{:S(2)}, u32[]{:S(2)}) collective-permute-start(f32[4,16,512]{2,1,0:T(8,128)S(1)} %get-tuple-element.36), channel_id=1, source_target_pairs={{0,16},{1,0},{2,1},{3,2},{4,20},{5,4},{6,5},{7,6},{8,24},{9,8},{10... | collective-permute-start | bytes 393224 | tf_op jit(solution)/shard_map/ppermute | solution.py:556
  11.8 5.0 %collective-permute-start.4 = (f32[16,512]{1,0:T(8,128)S(1)}, f32[16,512]{1,0:T(8,128)S(1)}, u32[]{:S(2)}, u32[]{:S(2)}) collective-permute-start(f32[16,512]{1,0:T(8,128)S(1)} %get-tuple-element.33), channel_id=1, source_target_pairs={{0,16},{1,17},{2,18},{3,19},{4,20},{5,8},{6,9},{7,10},{8,24},{9,4}... | collective-permute-start | bytes 98312 | tf_op jit(solution)/shard_map/ppermute | solution.py:556
  13.5 4.8 %collective-permute-start.5 = (f32[16,512]{1,0:T(8,128)S(1)}, f32[16,512]{1,0:T(8,128)S(1)}, u32[]{:S(2)}, u32[]{:S(2)}) collective-permute-start(f32[16,512]{1,0:T(8,128)S(1)} %get-tuple-element.34), channel_id=1, source_target_pairs={{0,16},{1,4},{2,5},{3,6},{4,20},{5,0},{6,1},{7,2},{8,24},{9,12},{1... | collective-permute-start | bytes 98312 | tf_op jit(solution)/shard_map/ppermute | solution.py:556
  13.5 5.2 %collective-permute-start.6 = (f32[16,512]{1,0:T(8,128)S(1)}, f32[16,512]{1,0:T(8,128)S(1)}, u32[]{:S(2)}, u32[]{:S(2)}) collective-permute-start(f32[16,512]{1,0:T(8,128)S(1)} %get-tuple-element.35), channel_id=1, source_target_pairs={{0,4},{1,5},{2,6},{3,7},{4,0},{5,1},{6,2},{7,3},{8,12},{9,13},{10,... | collective-permute-start | bytes 98312 | tf_op jit(solution)/shard_map/ppermute | solution.py:568
  18.8 1.4 %collective-permute-start.8 = (f32[4,16,512]{2,1,0:T(8,128)S(1)}, f32[4,16,512]{2,1,0:T(8,128)S(1)}, u32[]{:S(2)}, u32[]{:S(2)}) collective-permute-start(f32[4,16,512]{2,1,0:T(8,128)S(1)} %shard_map.51.part), channel_id=1, source_target_pairs={{0,16},{16,0},{1,17},{17,1},{2,18},{18,2},{3,19},{19,3},{4,20},{20... | collective-permute-start | bytes 393224 | tf_op jit(solution)/shard_map/ppermute | solution.py:539

commit v32 on v31

--- a/solution.py
+++ b/solution.py
@@ -468,7 +468,7 @@
         out[:reach] = jnp.where(first_core, rows[:reach], rows[REACH:])
 
 
-def layers_kernel(h, d_in, e_in, y_in, z_in, out):
+def layers_kernel(h, y_in, d_in, e_in, z_in, out):
     zlen, ylen, xlen = out.shape
     reach = REACH * zlen
     first_core = on_first()
@@ -639,7 +639,7 @@
     e_in = opposed(e_send, -1, 0, start=0)
     y_in = beside(y_send)
     z_in = opposed(z_send, -1, 0)
-    (part,) = call(layers_kernel, [(zlen, ylen, xlen)], (h, d_in, e_in, y_in, z_in))
+    (part,) = call(layers_kernel, [(zlen, ylen, xlen)], (h, y_in, d_in, e_in, z_in))
     (out,) = call(sum_kernel, [(zlen, ylen, xlen)], (part, chip_swapped(part)))
     return out
 

time: 21 us -> 21.9 us (1.043)
  waiting for transfers between devices: 5.73 us -> 9 us
  starting transfers between devices: 10.6 us -> 8.19 us
    ppermute x5, waiting for transfers between devices: 2.96 us -> 5.32 us  [opposed(): return lax.ppermute(value, ('load', 'sy', 'sz'), pairs)]
    ppermute x1, starting transfers between devices: 3.3 us -> 1.46 us  [beside(): return lax.ppermute(value, ('load', 'sy', 'sz'), pairs)]
    ppermute x1, waiting for transfers between devices: 0.38 us -> 0.93 us  [beside(): return lax.ppermute(value, ('load', 'sy', 'sz'), pairs)]
    ppermute x2, starting transfers between devices: 0.51 us -> 0.14 us  [chip_swapped(): lax.ppermute(value, 'load', [(core, cores - 1 - core) for core in range(c...]
    ppermute x2, waiting for transfers between devices: 2.39 us -> 2.74 us  [chip_swapped(): lax.ppermute(value, 'load', [(core, cores - 1 - core) for core in range(c...]
  transfers between devices with their start and end apart: 9 -> 9, of which waited for: 6 -> 6; matrix products, arithmetic and copies ran while one was open for 0% -> 0% of each run, Pallas kernels for 11% -> 10%
where the time goes in v32:
time: 21.9 us; the launch traced here: 21.8 us
  waiting for transfers between devices  9 us (41%)
  starting transfers between devices  8.19 us (37%)
  Pallas kernels  4.5 us (21%)
    ppermute x5, waiting for transfers between devices, opposed(): return lax.ppermute(value, ('load', 'sy', 'sz'), pairs)  5.32 us
    pallas_call x7, Pallas kernels, call(): pl.pallas_call(kernel, out_shape=shapes, in_specs=[pl.BlockSpec(memory_sp...  4.5 us
    ppermute x1, starting transfers between devices, ring_moved(): return lax.ppermute(value, axis, [((k + 1) % size, k) for k in range(size)])  3.51 us
    ppermute x5, starting transfers between devices, opposed(): return lax.ppermute(value, ('load', 'sy', 'sz'), pairs)  3.08 us
    ppermute x2, waiting for transfers between devices, chip_swapped(): lax.ppermute(value, 'load', [(core, cores - 1 - core) for core in range(c...  2.74 us
    ppermute x1, starting transfers between devices, beside(): return lax.ppermute(value, ('load', 'sy', 'sz'), pairs)  1.46 us
    ppermute x1, waiting for transfers between devices, beside(): return lax.ppermute(value, ('load', 'sy', 'sz'), pairs)  0.93 us
  transfers between devices with their start and end apart: 9, of which 6 were waited for; matrix products, arithmetic and copies ran while one was open for 0% of the time, Pallas kernels for 10%

profile of v32, /device:TPU:0, one launch (start us, length us, event | category | flops | bytes accessed | tf_op | source)
XLA Modules:
  0.0 21.8 jit_solution(4857015155044177873)
XLA Ops:
  0.0 0.0 copy-start.3
  0.0 0.0 copy-start.2
  0.0 0.0 copy-start
  0.0 1.2 %shard_map.46 = (f32[8,512]{1,0:T(8,128)S(1)}, f32[7,16,512]{2,1,0:T(8,128)S(1)}, f32[24,512]{1,0:T(8,128)S(1)}) custom-call(f32[2,3,4,16,512]{4,3,2,1,0:T(8,128)} %refs_0_.3, s32[4,16,512]{2,1,0:T(8,128)} %refs_1_.3, f32[4,16,512]{2,1,0:T(8,128)} %refs_2_.3, s32[4,16,512]{2,1,0:T(8,128)} %refs_3_.3), custom_call_target="tpu_custom_call" | custom-call | tf_op jit(solution)/shard_map/pallas_call | solution.py:522
  1.2 0.5 %collective-permute-start = (f32[7,16,512]{2,1,0:T(8,128)S(1)}, f32[7,16,512]{2,1,0:T(8,128)S(1)}, u32[]{:S(2)}, u32[]{:S(2)}) collective-permute-start(f32[7,16,512]{2,1,0:T(8,128)S(1)} %get-tuple-element.21), channel_id=1, source_target_pairs={{0,16},{1,0},{2,1},{3,2},{4,20},{5,4},{6,5},{7,6},{8,24},{9,8},{10... | collective-permute-start | bytes 688136 | tf_op jit(solution)/shard_map/ppermute | solution.py:556
  1.7 3.5 %collective-permute-start.1 = (f32[24,512]{1,0:T(8,128)S(1)}, f32[24,512]{1,0:T(8,128)S(1)}, u32[]{:S(2)}, u32[]{:S(2)}) collective-permute-start(f32[24,512]{1,0:T(8,128)S(1)} %get-tuple-element.22), channel_id=1, source_target_pairs={{4,0},{8,4},{12,8},{0,12},{5,1},{9,5},{13,9},{1,13},{6,2},{10,6},{... | collective-permute-start | bytes 147464 | tf_op jit(solution)/shard_map/ppermute | solution.py:534
  5.2 0.9 %collective-permute-start.2 = (f32[8,512]{1,0:T(8,128)S(1)}, f32[8,512]{1,0:T(8,128)S(1)}, u32[]{:S(2)}, u32[]{:S(2)}) collective-permute-start(f32[8,512]{1,0:T(8,128)S(1)} %get-tuple-element.31), channel_id=1, source_target_pairs={{0,28},{1,12},{2,13},{3,14},{4,16},{5,0},{6,1},{7,2},{8,20},{9,4},... | collective-permute-start | bytes 49160 | tf_op jit(solution)/shard_map/ppermute | solution.py:556
  6.1 0.0 copy-done.1
  6.1 0.0 copy-done.3
  6.1 0.0 copy-done.2
  6.1 0.0 copy-done
  6.1 1.6 %shard_map.47 = (f32[4,16,512]{2,1,0:T(8,128)S(1)}, f32[2,24,512]{2,1,0:T(8,128)S(1)}, f32[2,9,512]{2,1,0:T(8,128)S(1)}, f32[4,6,16,512]{3,2,1,0:T(8,128)S(1)}, ...) custom-call(f32[2,3,4,16,512]{4,3,2,1,0:T(8,128)S(1)} %copy-done, s32[4,16,512]{2,1,0:T(8,128)S(1)} %copy-done.1, ...), custom_call_target="tpu_custom_call" | custom-call | tf_op jit(solution)/shard_map/pallas_call | solution.py:522
  7.7 0.0 collective-permute-done.1.refs_1_.refs_2_
  7.7 0.5 %collective-permute-done.refs_0_ = f32[7,16,512]{2,1,0:T(8,128)S(1)} collective-permute-done((f32[7,16,512]{2,1,0:T(8,128)S(1)}, f32[7,16,512]{2,1,0:T(8,128)S(1)}, u32[]{:S(2)}, u32[]{:S(2)}) %collective-permute-start) | collective-permute-done | bytes 229408 | tf_op jit(solution)/shard_map/ppermute | solution.py:556
  8.2 0.6 %shard_map.48 = (f32[88,512]{1,0:T(8,128)S(1)}, f32[4,8,512]{2,1,0:T(8,128)S(1)}) custom-call(f32[7,16,512]{2,1,0:T(8,128)S(1)} %collective-permute-done.refs_0_, f32[24,512]{1,0:T(8,128)S(1)} %collective-permute-done.1.refs_1_.refs_2_, f32[4,16,512]{2,1,0:T(8,128)S(1)} %get-tuple-element.23.refs_2_, f32[2,24,512]{2,1,0:T(8,128)S(1)} %get-tuple-element.24.refs_3_, ...), custom_call_target="tpu_custom_call" | custom-call | tf_op jit(solution)/shard_map/pallas_call | solution.py:522
  8.9 0.9 %collective-permute-done.2.refs_3_ = f32[8,512]{1,0:T(8,128)S(1)} collective-permute-done((f32[8,512]{1,0:T(8,128)S(1)}, f32[8,512]{1,0:T(8,128)S(1)}, u32[]{:S(2)}, u32[]{:S(2)}) %collective-permute-start.2) | collective-permute-done | bytes 16416 | tf_op jit(solution)/shard_map/ppermute | solution.py:556
  9.8 0.3 %shard_map.49.refs_0_ = f32[88,512]{1,0:T(8,128)S(1)} custom-call(f32[88,512]{1,0:T(8,128)S(1)} %get-tuple-element.29.refs_0_, f32[4,8,512]{2,1,0:T(8,128)S(1)} %get-tuple-element.30.refs_1_, f32[24,512]{1,0:T(8,128)S(1)} %collective-permute-done.1.refs_1_.refs_2_, f32[8,512]{1,0:T(8,128)S(1)} %collective-permute-done.2.refs_3_), custom_call_target="tpu_custom_call" | custom-call | tf_op jit(solution)/shard_map/pallas_call | solution.py:522
  10.1 0.1 collective-permute-start.3
  10.2 1.4 %collective-permute-done.3.refs_1_ = f32[88,512]{1,0:T(8,128)S(1)} collective-permute-done((f32[88,512]{1,0:T(8,128)S(1)}, f32[88,512]{1,0:T(8,128)S(1)}, u32[]{:S(2)}, u32[]{:S(2)}) %collective-permute-start.3) | collective-permute-done | bytes 180256 | tf_op jit(solution)/shard_map/ppermute | solution.py:539
  11.6 0.1 shard_map.50
  11.6 0.2 collective-permute-start.7
  11.8 1.5 %collective-permute-start.4 = (f32[16,512]{1,0:T(8,128)S(1)}, f32[16,512]{1,0:T(8,128)S(1)}, u32[]{:S(2)}, u32[]{:S(2)}) collective-permute-start(f32[16,512]{1,0:T(8,128)S(1)} %get-tuple-element.33), channel_id=1, source_target_pairs={{0,4},{1,5},{2,6},{3,7},{4,0},{5,1},{6,2},{7,3},{8,12},{9,13},{10,... | collective-permute-start | bytes 98312 | tf_op jit(solution)/shard_map/ppermute | solution.py:568
  13.2 1.5 %collective-permute-start.5 = (f32[16,512]{1,0:T(8,128)S(1)}, f32[16,512]{1,0:T(8,128)S(1)}, u32[]{:S(2)}, u32[]{:S(2)}) collective-permute-start(f32[16,512]{1,0:T(8,128)S(1)} %get-tuple-element.34), channel_id=1, source_target_pairs={{0,16},{1,17},{2,18},{3,19},{4,20},{5,8},{6,9},{7,10},{8,24},{9,4}... | collective-permute-start | bytes 98312 | tf_op jit(solution)/shard_map/ppermute | solution.py:556
  14.8 0.0 collective-permute-start.6
  14.8 0.9 %collective-permute-done.4.y_in = f32[16,512]{1,0:T(8,128)S(1)} collective-permute-done((f32[16,512]{1,0:T(8,128)S(1)}, f32[16,512]{1,0:T(8,128)S(1)}, u32[]{:S(2)}, u32[]{:S(2)}) %collective-permute-start.4) | collective-permute-done | bytes 32800 | tf_op jit(solution)/shard_map/ppermute | solution.py:568
  15.7 0.0 collective-permute-done.5.d_in
  15.7 3.9 %collective-permute-done.6.e_in = f32[16,512]{1,0:T(8,128)S(1)} collective-permute-done((f32[16,512]{1,0:T(8,128)S(1)}, f32[16,512]{1,0:T(8,128)S(1)}, u32[]{:S(2)}, u32[]{:S(2)}) %collective-permute-start.6) | collective-permute-done | bytes 32800 | tf_op jit(solution)/shard_map/ppermute | solution.py:556
  19.6 0.0 collective-permute-done.7.z_in
  19.6 0.1 shard_map.51.part
  19.7 0.1 collective-permute-start.8
  19.8 1.3 %collective-permute-done.8.other = f32[4,16,512]{2,1,0:T(8,128)S(1)} collective-permute-done((f32[4,16,512]{2,1,0:T(8,128)S(1)}, f32[4,16,512]{2,1,0:T(8,128)S(1)}, u32[]{:S(2)}, u32[]{:S(2)}) %collective-permute-start.8) | collective-permute-done | bytes 131104 | tf_op jit(solution)/shard_map/ppermute | solution.py:539
  21.1 0.7 %shard_map.52 = f32[4,16,512]{2,1,0:T(8,128)} custom-call(f32[4,16,512]{2,1,0:T(8,128)S(1)} %shard_map.51.part, f32[4,16,512]{2,1,0:T(8,128)S(1)} %collective-permute-done.8.other), custom_call_target="tpu_custom_call" | custom-call | tf_op jit(solution)/shard_map/pallas_call | solution.py:522
  (1 shorter events, 0.0 us)
Async XLA Ops:
  0.0 6.1 %copy-start.1 = (s32[4,16,512]{2,1,0:T(8,128)S(1)}, s32[4,16,512]{2,1,0:T(8,128)}, u32[]{:S(2)}) copy-start(s32[4,16,512]{2,1,0:T(8,128)} %refs_1_.3) | copy-start | bytes 393220
  0.0 6.1 %copy-start.3 = (s32[4,16,512]{2,1,0:T(8,128)S(1)}, s32[4,16,512]{2,1,0:T(8,128)}, u32[]{:S(2)}) copy-start(s32[4,16,512]{2,1,0:T(8,128)} %refs_3_.3) | copy-start | bytes 393220
  0.0 6.1 %copy-start.2 = (f32[4,16,512]{2,1,0:T(8,128)S(1)}, f32[4,16,512]{2,1,0:T(8,128)}, u32[]{:S(2)}) copy-start(f32[4,16,512]{2,1,0:T(8,128)} %refs_2_.3) | copy-start | bytes 393220
  0.0 6.1 %copy-start = (f32[2,3,4,16,512]{4,3,2,1,0:T(8,128)S(1)}, f32[2,3,4,16,512]{4,3,2,1,0:T(8,128)}, u32[]{:S(2)}) copy-start(f32[2,3,4,16,512]{4,3,2,1,0:T(8,128)} %refs_0_.3) | copy-start | bytes 2359300
  1.2 7.1 %collective-permute-start = (f32[7,16,512]{2,1,0:T(8,128)S(1)}, f32[7,16,512]{2,1,0:T(8,128)S(1)}, u32[]{:S(2)}, u32[]{:S(2)}) collective-permute-start(f32[7,16,512]{2,1,0:T(8,128)S(1)} %get-tuple-element.21), channel_id=1, source_target_pairs={{0,16},{1,0},{2,1},{3,2},{4,20},{5,4},{6,5},{7,6},{8,24},{9,8},{10... | collective-permute-start | bytes 688136 | tf_op jit(solution)/shard_map/ppermute | solution.py:556
  1.7 6.0 %collective-permute-start.1 = (f32[24,512]{1,0:T(8,128)S(1)}, f32[24,512]{1,0:T(8,128)S(1)}, u32[]{:S(2)}, u32[]{:S(2)}) collective-permute-start(f32[24,512]{1,0:T(8,128)S(1)} %get-tuple-element.22), channel_id=1, source_target_pairs={{4,0},{8,4},{12,8},{0,12},{5,1},{9,5},{13,9},{1,13},{6,2},{10,6},{... | collective-permute-start | bytes 147464 | tf_op jit(solution)/shard_map/ppermute | solution.py:534
  5.2 4.6 %collective-permute-start.2 = (f32[8,512]{1,0:T(8,128)S(1)}, f32[8,512]{1,0:T(8,128)S(1)}, u32[]{:S(2)}, u32[]{:S(2)}) collective-permute-start(f32[8,512]{1,0:T(8,128)S(1)} %get-tuple-element.31), channel_id=1, source_target_pairs={{0,28},{1,12},{2,13},{3,14},{4,16},{5,0},{6,1},{7,2},{8,20},{9,4},... | collective-permute-start | bytes 49160 | tf_op jit(solution)/shard_map/ppermute | solution.py:556
  10.1 1.5 %collective-permute-start.3 = (f32[88,512]{1,0:T(8,128)S(1)}, f32[88,512]{1,0:T(8,128)S(1)}, u32[]{:S(2)}, u32[]{:S(2)}) collective-permute-start(f32[88,512]{1,0:T(8,128)S(1)} %shard_map.49.refs_0_), channel_id=1, source_target_pairs={{0,16},{16,0},{1,17},{17,1},{2,18},{18,2},{3,19},{19,3},{4,20},{20... | collective-permute-start | bytes 540680 | tf_op jit(solution)/shard_map/ppermute | solution.py:539
  11.6 8.0 %collective-permute-start.7 = (f32[4,16,512]{2,1,0:T(8,128)S(1)}, f32[4,16,512]{2,1,0:T(8,128)S(1)}, u32[]{:S(2)}, u32[]{:S(2)}) collective-permute-start(f32[4,16,512]{2,1,0:T(8,128)S(1)} %get-tuple-element.36), channel_id=1, source_target_pairs={{0,16},{1,0},{2,1},{3,2},{4,20},{5,4},{6,5},{7,6},{8,24},{9,8},{10... | collective-permute-start | bytes 393224 | tf_op jit(solution)/shard_map/ppermute | solution.py:556
  11.8 3.9 %collective-permute-start.4 = (f32[16,512]{1,0:T(8,128)S(1)}, f32[16,512]{1,0:T(8,128)S(1)}, u32[]{:S(2)}, u32[]{:S(2)}) collective-permute-start(f32[16,512]{1,0:T(8,128)S(1)} %get-tuple-element.33), channel_id=1, source_target_pairs={{0,4},{1,5},{2,6},{3,7},{4,0},{5,1},{6,2},{7,3},{8,12},{9,13},{10,... | collective-permute-start | bytes 98312 | tf_op jit(solution)/shard_map/ppermute | solution.py:568
  13.2 2.5 %collective-permute-start.5 = (f32[16,512]{1,0:T(8,128)S(1)}, f32[16,512]{1,0:T(8,128)S(1)}, u32[]{:S(2)}, u32[]{:S(2)}) collective-permute-start(f32[16,512]{1,0:T(8,128)S(1)} %get-tuple-element.34), channel_id=1, source_target_pairs={{0,16},{1,17},{2,18},{3,19},{4,20},{5,8},{6,9},{7,10},{8,24},{9,4}... | collective-permute-start | bytes 98312 | tf_op jit(solution)/shard_map/ppermute | solution.py:556
  14.8 4.8 %collective-permute-start.6 = (f32[16,512]{1,0:T(8,128)S(1)}, f32[16,512]{1,0:T(8,128)S(1)}, u32[]{:S(2)}, u32[]{:S(2)}) collective-permute-start(f32[16,512]{1,0:T(8,128)S(1)} %get-tuple-element.35), channel_id=1, source_target_pairs={{0,16},{1,4},{2,5},{3,6},{4,20},{5,0},{6,1},{7,2},{8,24},{9,12},{1... | collective-permute-start | bytes 98312 | tf_op jit(solution)/shard_map/ppermute | solution.py:556
  19.7 1.4 %collective-permute-start.8 = (f32[4,16,512]{2,1,0:T(8,128)S(1)}, f32[4,16,512]{2,1,0:T(8,128)S(1)}, u32[]{:S(2)}, u32[]{:S(2)}) collective-permute-start(f32[4,16,512]{2,1,0:T(8,128)S(1)} %shard_map.51.part), channel_id=1, source_target_pairs={{0,16},{16,0},{1,17},{17,1},{2,18},{18,2},{3,19},{19,3},{4,20},{20... | collective-permute-start | bytes 393224 | tf_op jit(solution)/shard_map/ppermute | solution.py:539

commit v33 on v31

--- a/solution.py
+++ b/solution.py
@@ -210,7 +210,7 @@
             )
         )
     ]
-    for copy in copies:
+    for copy in reversed(copies):
         copy.start()
     for copy in copies[:2]:
         copy.wait()

time: 21 us -> 21 us (level)
  no operation moved by 1% of the time
where the time goes in v33:
time: 21 us; the launch traced here: 20.9 us
  starting transfers between devices  10.6 us (50%)
  waiting for transfers between devices  5.73 us (27%)
  Pallas kernels  4.49 us (21%)
    pallas_call x7, Pallas kernels, call(): pl.pallas_call(kernel, out_shape=shapes, in_specs=[pl.BlockSpec(memory_sp...  4.49 us
    ppermute x1, starting transfers between devices, ring_moved(): return lax.ppermute(value, axis, [((k + 1) % size, k) for k in range(size)])  3.51 us
    ppermute x1, starting transfers between devices, beside(): return lax.ppermute(value, ('load', 'sy', 'sz'), pairs)  3.3 us
    ppermute x5, starting transfers between devices, opposed(): return lax.ppermute(value, ('load', 'sy', 'sz'), pairs)  3.25 us
    ppermute x5, waiting for transfers between devices, opposed(): return lax.ppermute(value, ('load', 'sy', 'sz'), pairs)  2.96 us
    ppermute x2, waiting for transfers between devices, chip_swapped(): lax.ppermute(value, 'load', [(core, cores - 1 - core) for core in range(c...  2.39 us
    ppermute x2, starting transfers between devices, chip_swapped(): lax.ppermute(value, 'load', [(core, cores - 1 - core) for core in range(c...  0.51 us
  transfers between devices with their start and end apart: 9, of which 6 were waited for; matrix products, arithmetic and copies ran while one was open for 0% of the time, Pallas kernels for 11%

profile of v33, /device:TPU:0, one launch (start us, length us, event | category | flops | bytes accessed | tf_op | source)
XLA Modules:
  0.0 20.9 jit_solution(11460733160817062383)
XLA Ops:
  0.0 0.0 copy-start.1
  0.0 0.0 copy-start.3
  0.0 0.0 copy-start.2
  0.0 1.2 %shard_map.46 = (f32[8,512]{1,0:T(8,128)S(1)}, f32[7,16,512]{2,1,0:T(8,128)S(1)}, f32[24,512]{1,0:T(8,128)S(1)}) custom-call(f32[2,3,4,16,512]{4,3,2,1,0:T(8,128)} %refs_0_.3, s32[4,16,512]{2,1,0:T(8,128)} %refs_1_.3, f32[4,16,512]{2,1,0:T(8,128)} %refs_2_.3, s32[4,16,512]{2,1,0:T(8,128)} %refs_3_.3), custom_call_target="tpu_custom_call" | custom-call | tf_op jit(solution)/shard_map/pallas_call | solution.py:522
  1.2 0.5 %collective-permute-start = (f32[7,16,512]{2,1,0:T(8,128)S(1)}, f32[7,16,512]{2,1,0:T(8,128)S(1)}, u32[]{:S(2)}, u32[]{:S(2)}) collective-permute-start(f32[7,16,512]{2,1,0:T(8,128)S(1)} %get-tuple-element.21), channel_id=1, source_target_pairs={{0,16},{1,0},{2,1},{3,2},{4,20},{5,4},{6,5},{7,6},{8,24},{9,8},{10... | collective-permute-start | bytes 688136 | tf_op jit(solution)/shard_map/ppermute | solution.py:556
  1.7 3.5 %collective-permute-start.1 = (f32[24,512]{1,0:T(8,128)S(1)}, f32[24,512]{1,0:T(8,128)S(1)}, u32[]{:S(2)}, u32[]{:S(2)}) collective-permute-start(f32[24,512]{1,0:T(8,128)S(1)} %get-tuple-element.22), channel_id=1, source_target_pairs={{4,0},{8,4},{12,8},{0,12},{5,1},{9,5},{13,9},{1,13},{6,2},{10,6},{... | collective-permute-start | bytes 147464 | tf_op jit(solution)/shard_map/ppermute | solution.py:534
  5.2 0.9 %collective-permute-start.2 = (f32[8,512]{1,0:T(8,128)S(1)}, f32[8,512]{1,0:T(8,128)S(1)}, u32[]{:S(2)}, u32[]{:S(2)}) collective-permute-start(f32[8,512]{1,0:T(8,128)S(1)} %get-tuple-element.31), channel_id=1, source_target_pairs={{0,28},{1,12},{2,13},{3,14},{4,16},{5,0},{6,1},{7,2},{8,20},{9,4},... | collective-permute-start | bytes 49160 | tf_op jit(solution)/shard_map/ppermute | solution.py:556
  6.1 0.0 copy-done.1
  6.1 0.0 copy-done.3
  6.1 0.0 copy-done.2
  6.1 0.0 copy-done
  6.1 1.6 %shard_map.47 = (f32[4,16,512]{2,1,0:T(8,128)S(1)}, f32[2,24,512]{2,1,0:T(8,128)S(1)}, f32[2,9,512]{2,1,0:T(8,128)S(1)}, f32[4,6,16,512]{3,2,1,0:T(8,128)S(1)}, ...) custom-call(f32[2,3,4,16,512]{4,3,2,1,0:T(8,128)S(1)} %copy-done, s32[4,16,512]{2,1,0:T(8,128)S(1)} %copy-done.1, ...), custom_call_target="tpu_custom_call" | custom-call | tf_op jit(solution)/shard_map/pallas_call | solution.py:522
  7.7 0.0 collective-permute-done.1.refs_1_.refs_2_
  7.7 0.5 %collective-permute-done.refs_0_ = f32[7,16,512]{2,1,0:T(8,128)S(1)} collective-permute-done((f32[7,16,512]{2,1,0:T(8,128)S(1)}, f32[7,16,512]{2,1,0:T(8,128)S(1)}, u32[]{:S(2)}, u32[]{:S(2)}) %collective-permute-start) | collective-permute-done | bytes 229408 | tf_op jit(solution)/shard_map/ppermute | solution.py:556
  8.2 0.6 %shard_map.48 = (f32[88,512]{1,0:T(8,128)S(1)}, f32[4,8,512]{2,1,0:T(8,128)S(1)}) custom-call(f32[7,16,512]{2,1,0:T(8,128)S(1)} %collective-permute-done.refs_0_, f32[24,512]{1,0:T(8,128)S(1)} %collective-permute-done.1.refs_1_.refs_2_, f32[4,16,512]{2,1,0:T(8,128)S(1)} %get-tuple-element.23.refs_2_, f32[2,24,512]{2,1,0:T(8,128)S(1)} %get-tuple-element.24.refs_3_, ...), custom_call_target="tpu_custom_call" | custom-call | tf_op jit(solution)/shard_map/pallas_call | solution.py:522
  8.9 0.9 %collective-permute-done.2.refs_3_ = f32[8,512]{1,0:T(8,128)S(1)} collective-permute-done((f32[8,512]{1,0:T(8,128)S(1)}, f32[8,512]{1,0:T(8,128)S(1)}, u32[]{:S(2)}, u32[]{:S(2)}) %collective-permute-start.2) | collective-permute-done | bytes 16416 | tf_op jit(solution)/shard_map/ppermute | solution.py:556
  9.8 0.3 %shard_map.49.refs_0_ = f32[88,512]{1,0:T(8,128)S(1)} custom-call(f32[88,512]{1,0:T(8,128)S(1)} %get-tuple-element.29.refs_0_, f32[4,8,512]{2,1,0:T(8,128)S(1)} %get-tuple-element.30.refs_1_, f32[24,512]{1,0:T(8,128)S(1)} %collective-permute-done.1.refs_1_.refs_2_, f32[8,512]{1,0:T(8,128)S(1)} %collective-permute-done.2.refs_3_), custom_call_target="tpu_custom_call" | custom-call | tf_op jit(solution)/shard_map/pallas_call | solution.py:522
  10.1 0.1 collective-permute-start.3
  10.2 1.4 %collective-permute-done.3.refs_1_ = f32[88,512]{1,0:T(8,128)S(1)} collective-permute-done((f32[88,512]{1,0:T(8,128)S(1)}, f32[88,512]{1,0:T(8,128)S(1)}, u32[]{:S(2)}, u32[]{:S(2)}) %collective-permute-start.3) | collective-permute-done | bytes 180256 | tf_op jit(solution)/shard_map/ppermute | solution.py:539
  11.6 0.1 shard_map.50
  11.6 0.2 collective-permute-start.7
  11.8 1.7 %collective-permute-start.4 = (f32[16,512]{1,0:T(8,128)S(1)}, f32[16,512]{1,0:T(8,128)S(1)}, u32[]{:S(2)}, u32[]{:S(2)}) collective-permute-start(f32[16,512]{1,0:T(8,128)S(1)} %get-tuple-element.33), channel_id=1, source_target_pairs={{0,16},{1,17},{2,18},{3,19},{4,20},{5,8},{6,9},{7,10},{8,24},{9,4}... | collective-permute-start | bytes 98312 | tf_op jit(solution)/shard_map/ppermute | solution.py:556
  13.5 0.0 collective-permute-start.5
  13.5 3.3 %collective-permute-start.6 = (f32[16,512]{1,0:T(8,128)S(1)}, f32[16,512]{1,0:T(8,128)S(1)}, u32[]{:S(2)}, u32[]{:S(2)}) collective-permute-start(f32[16,512]{1,0:T(8,128)S(1)} %get-tuple-element.35), channel_id=1, source_target_pairs={{0,4},{1,5},{2,6},{3,7},{4,0},{5,1},{6,2},{7,3},{8,12},{9,13},{10,... | collective-permute-start | bytes 98312 | tf_op jit(solution)/shard_map/ppermute | solution.py:568
  16.8 0.0 collective-permute-done.4.d_in
  16.8 1.5 %collective-permute-done.5.e_in = f32[16,512]{1,0:T(8,128)S(1)} collective-permute-done((f32[16,512]{1,0:T(8,128)S(1)}, f32[16,512]{1,0:T(8,128)S(1)}, u32[]{:S(2)}, u32[]{:S(2)}) %collective-permute-start.5) | collective-permute-done | bytes 32800 | tf_op jit(solution)/shard_map/ppermute | solution.py:556
  18.3 0.4 %collective-permute-done.6.y_in = f32[16,512]{1,0:T(8,128)S(1)} collective-permute-done((f32[16,512]{1,0:T(8,128)S(1)}, f32[16,512]{1,0:T(8,128)S(1)}, u32[]{:S(2)}, u32[]{:S(2)}) %collective-permute-start.6) | collective-permute-done | bytes 32800 | tf_op jit(solution)/shard_map/ppermute | solution.py:568
  18.7 0.0 collective-permute-done.7.z_in
  18.7 0.1 shard_map.51.part
  18.8 0.4 %collective-permute-start.8 = (f32[4,16,512]{2,1,0:T(8,128)S(1)}, f32[4,16,512]{2,1,0:T(8,128)S(1)}, u32[]{:S(2)}, u32[]{:S(2)}) collective-permute-start(f32[4,16,512]{2,1,0:T(8,128)S(1)} %shard_map.51.part), channel_id=1, source_target_pairs={{0,16},{16,0},{1,17},{17,1},{2,18},{18,2},{3,19},{19,3},{4,20},{20... | collective-permute-start | bytes 393224 | tf_op jit(solution)/shard_map/ppermute | solution.py:539
  19.2 1.0 %collective-permute-done.8.other = f32[4,16,512]{2,1,0:T(8,128)S(1)} collective-permute-done((f32[4,16,512]{2,1,0:T(8,128)S(1)}, f32[4,16,512]{2,1,0:T(8,128)S(1)}, u32[]{:S(2)}, u32[]{:S(2)}) %collective-permute-start.8) | collective-permute-done | bytes 131104 | tf_op jit(solution)/shard_map/ppermute | solution.py:539
  20.2 0.7 %shard_map.52 = f32[4,16,512]{2,1,0:T(8,128)} custom-call(f32[4,16,512]{2,1,0:T(8,128)S(1)} %shard_map.51.part, f32[4,16,512]{2,1,0:T(8,128)S(1)} %collective-permute-done.8.other), custom_call_target="tpu_custom_call" | custom-call | tf_op jit(solution)/shard_map/pallas_call | solution.py:522
  (1 shorter events, 0.0 us)
Async XLA Ops:
  0.0 6.1 %copy-start.1 = (s32[4,16,512]{2,1,0:T(8,128)S(1)}, s32[4,16,512]{2,1,0:T(8,128)}, u32[]{:S(2)}) copy-start(s32[4,16,512]{2,1,0:T(8,128)} %refs_1_.3) | copy-start | bytes 393220
  0.0 6.1 %copy-start.3 = (s32[4,16,512]{2,1,0:T(8,128)S(1)}, s32[4,16,512]{2,1,0:T(8,128)}, u32[]{:S(2)}) copy-start(s32[4,16,512]{2,1,0:T(8,128)} %refs_3_.3) | copy-start | bytes 393220
  0.0 6.1 %copy-start.2 = (f32[4,16,512]{2,1,0:T(8,128)S(1)}, f32[4,16,512]{2,1,0:T(8,128)}, u32[]{:S(2)}) copy-start(f32[4,16,512]{2,1,0:T(8,128)} %refs_2_.3) | copy-start | bytes 393220
  0.0 6.1 %copy-start = (f32[2,3,4,16,512]{4,3,2,1,0:T(8,128)S(1)}, f32[2,3,4,16,512]{4,3,2,1,0:T(8,128)}, u32[]{:S(2)}) copy-start(f32[2,3,4,16,512]{4,3,2,1,0:T(8,128)} %refs_0_.3) | copy-start | bytes 2359300
  1.2 7.1 %collective-permute-start = (f32[7,16,512]{2,1,0:T(8,128)S(1)}, f32[7,16,512]{2,1,0:T(8,128)S(1)}, u32[]{:S(2)}, u32[]{:S(2)}) collective-permute-start(f32[7,16,512]{2,1,0:T(8,128)S(1)} %get-tuple-element.21), channel_id=1, source_target_pairs={{0,16},{1,0},{2,1},{3,2},{4,20},{5,4},{6,5},{7,6},{8,24},{9,8},{10... | collective-permute-start | bytes 688136 | tf_op jit(solution)/shard_map/ppermute | solution.py:556
  1.7 6.0 %collective-permute-start.1 = (f32[24,512]{1,0:T(8,128)S(1)}, f32[24,512]{1,0:T(8,128)S(1)}, u32[]{:S(2)}, u32[]{:S(2)}) collective-permute-start(f32[24,512]{1,0:T(8,128)S(1)} %get-tuple-element.22), channel_id=1, source_target_pairs={{4,0},{8,4},{12,8},{0,12},{5,1},{9,5},{13,9},{1,13},{6,2},{10,6},{... | collective-permute-start | bytes 147464 | tf_op jit(solution)/shard_map/ppermute | solution.py:534
  5.2 4.6 %collective-permute-start.2 = (f32[8,512]{1,0:T(8,128)S(1)}, f32[8,512]{1,0:T(8,128)S(1)}, u32[]{:S(2)}, u32[]{:S(2)}) collective-permute-start(f32[8,512]{1,0:T(8,128)S(1)} %get-tuple-element.31), channel_id=1, source_target_pairs={{0,28},{1,12},{2,13},{3,14},{4,16},{5,0},{6,1},{7,2},{8,20},{9,4},... | collective-permute-start | bytes 49160 | tf_op jit(solution)/shard_map/ppermute | solution.py:556
  10.1 1.5 %collective-permute-start.3 = (f32[88,512]{1,0:T(8,128)S(1)}, f32[88,512]{1,0:T(8,128)S(1)}, u32[]{:S(2)}, u32[]{:S(2)}) collective-permute-start(f32[88,512]{1,0:T(8,128)S(1)} %shard_map.49.refs_0_), channel_id=1, source_target_pairs={{0,16},{16,0},{1,17},{17,1},{2,18},{18,2},{3,19},{19,3},{4,20},{20... | collective-permute-start | bytes 540680 | tf_op jit(solution)/shard_map/ppermute | solution.py:539
  11.6 7.0 %collective-permute-start.7 = (f32[4,16,512]{2,1,0:T(8,128)S(1)}, f32[4,16,512]{2,1,0:T(8,128)S(1)}, u32[]{:S(2)}, u32[]{:S(2)}) collective-permute-start(f32[4,16,512]{2,1,0:T(8,128)S(1)} %get-tuple-element.36), channel_id=1, source_target_pairs={{0,16},{1,0},{2,1},{3,2},{4,20},{5,4},{6,5},{7,6},{8,24},{9,8},{10... | collective-permute-start | bytes 393224 | tf_op jit(solution)/shard_map/ppermute | solution.py:556
  11.8 5.0 %collective-permute-start.4 = (f32[16,512]{1,0:T(8,128)S(1)}, f32[16,512]{1,0:T(8,128)S(1)}, u32[]{:S(2)}, u32[]{:S(2)}) collective-permute-start(f32[16,512]{1,0:T(8,128)S(1)} %get-tuple-element.33), channel_id=1, source_target_pairs={{0,16},{1,17},{2,18},{3,19},{4,20},{5,8},{6,9},{7,10},{8,24},{9,4}... | collective-permute-start | bytes 98312 | tf_op jit(solution)/shard_map/ppermute | solution.py:556
  13.5 4.8 %collective-permute-start.5 = (f32[16,512]{1,0:T(8,128)S(1)}, f32[16,512]{1,0:T(8,128)S(1)}, u32[]{:S(2)}, u32[]{:S(2)}) collective-permute-start(f32[16,512]{1,0:T(8,128)S(1)} %get-tuple-element.34), channel_id=1, source_target_pairs={{0,16},{1,4},{2,5},{3,6},{4,20},{5,0},{6,1},{7,2},{8,24},{9,12},{1... | collective-permute-start | bytes 98312 | tf_op jit(solution)/shard_map/ppermute | solution.py:556
  13.5 5.2 %collective-permute-start.6 = (f32[16,512]{1,0:T(8,128)S(1)}, f32[16,512]{1,0:T(8,128)S(1)}, u32[]{:S(2)}, u32[]{:S(2)}) collective-permute-start(f32[16,512]{1,0:T(8,128)S(1)} %get-tuple-element.35), channel_id=1, source_target_pairs={{0,4},{1,5},{2,6},{3,7},{4,0},{5,1},{6,2},{7,3},{8,12},{9,13},{10,... | collective-permute-start | bytes 98312 | tf_op jit(solution)/shard_map/ppermute | solution.py:568
  18.8 1.4 %collective-permute-start.8 = (f32[4,16,512]{2,1,0:T(8,128)S(1)}, f32[4,16,512]{2,1,0:T(8,128)S(1)}, u32[]{:S(2)}, u32[]{:S(2)}) collective-permute-start(f32[4,16,512]{2,1,0:T(8,128)S(1)} %shard_map.51.part), channel_id=1, source_target_pairs={{0,16},{16,0},{1,17},{17,1},{2,18},{18,2},{3,19},{19,3},{4,20},{20... | collective-permute-start | bytes 393224 | tf_op jit(solution)/shard_map/ppermute | solution.py:539

commit v34 on v33

--- a/solution.py
+++ b/solution.py
@@ -210,7 +210,7 @@
             )
         )
     ]
-    for copy in reversed(copies):
+    for copy in copies[3:4] + copies[:3] + copies[4:]:
         copy.start()
     for copy in copies[:2]:
         copy.wait()

time: 21 us -> 21 us (level)
  no operation moved by 1% of the time
where the time goes in v34:
time: 21 us; the launch traced here: 20.8 us
  starting transfers between devices  10.6 us (50%)
  waiting for transfers between devices  5.73 us (27%)
  Pallas kernels  4.45 us (21%)
    pallas_call x7, Pallas kernels, call(): pl.pallas_call(kernel, out_shape=shapes, in_specs=[pl.BlockSpec(memory_sp...  4.45 us
    ppermute x1, starting transfers between devices, ring_moved(): return lax.ppermute(value, axis, [((k + 1) % size, k) for k in range(size)])  3.51 us
    ppermute x1, starting transfers between devices, beside(): return lax.ppermute(value, ('load', 'sy', 'sz'), pairs)  3.3 us
    ppermute x5, starting transfers between devices, opposed(): return lax.ppermute(value, ('load', 'sy', 'sz'), pairs)  3.25 us
    ppermute x5, waiting for transfers between devices, opposed(): return lax.ppermute(value, ('load', 'sy', 'sz'), pairs)  2.96 us
    ppermute x2, waiting for transfers between devices, chip_swapped(): lax.ppermute(value, 'load', [(core, cores - 1 - core) for core in range(c...  2.39 us
    ppermute x2, starting transfers between devices, chip_swapped(): lax.ppermute(value, 'load', [(core, cores - 1 - core) for core in range(c...  0.51 us
  transfers between devices with their start and end apart: 9, of which 6 were waited for; matrix products, arithmetic and copies ran while one was open for 0% of the time, Pallas kernels for 11%

profile of v34, /device:TPU:0, one launch (start us, length us, event | category | flops | bytes accessed | tf_op | source)
XLA Modules:
  0.0 20.8 jit_solution(17226608329146718975)
XLA Ops:
  0.0 0.0 copy-start.1
  0.0 0.0 copy-start.3
  0.0 0.0 copy-start.2
  0.0 1.1 %shard_map.46 = (f32[8,512]{1,0:T(8,128)S(1)}, f32[7,16,512]{2,1,0:T(8,128)S(1)}, f32[24,512]{1,0:T(8,128)S(1)}) custom-call(f32[2,3,4,16,512]{4,3,2,1,0:T(8,128)} %refs_0_.3, s32[4,16,512]{2,1,0:T(8,128)} %refs_1_.3, f32[4,16,512]{2,1,0:T(8,128)} %refs_2_.3, s32[4,16,512]{2,1,0:T(8,128)} %refs_3_.3), custom_call_target="tpu_custom_call" | custom-call | tf_op jit(solution)/shard_map/pallas_call | solution.py:522
  1.1 0.5 %collective-permute-start = (f32[7,16,512]{2,1,0:T(8,128)S(1)}, f32[7,16,512]{2,1,0:T(8,128)S(1)}, u32[]{:S(2)}, u32[]{:S(2)}) collective-permute-start(f32[7,16,512]{2,1,0:T(8,128)S(1)} %get-tuple-element.21), channel_id=1, source_target_pairs={{0,16},{1,0},{2,1},{3,2},{4,20},{5,4},{6,5},{7,6},{8,24},{9,8},{10... | collective-permute-start | bytes 688136 | tf_op jit(solution)/shard_map/ppermute | solution.py:556
  1.6 3.5 %collective-permute-start.1 = (f32[24,512]{1,0:T(8,128)S(1)}, f32[24,512]{1,0:T(8,128)S(1)}, u32[]{:S(2)}, u32[]{:S(2)}) collective-permute-start(f32[24,512]{1,0:T(8,128)S(1)} %get-tuple-element.22), channel_id=1, source_target_pairs={{4,0},{8,4},{12,8},{0,12},{5,1},{9,5},{13,9},{1,13},{6,2},{10,6},{... | collective-permute-start | bytes 147464 | tf_op jit(solution)/shard_map/ppermute | solution.py:534
  5.1 0.9 %collective-permute-start.2 = (f32[8,512]{1,0:T(8,128)S(1)}, f32[8,512]{1,0:T(8,128)S(1)}, u32[]{:S(2)}, u32[]{:S(2)}) collective-permute-start(f32[8,512]{1,0:T(8,128)S(1)} %get-tuple-element.31), channel_id=1, source_target_pairs={{0,28},{1,12},{2,13},{3,14},{4,16},{5,0},{6,1},{7,2},{8,20},{9,4},... | collective-permute-start | bytes 49160 | tf_op jit(solution)/shard_map/ppermute | solution.py:556
  6.1 0.0 copy-done.1
  6.1 0.0 copy-done.3
  6.1 0.0 copy-done.2
  6.1 0.0 copy-done
  6.1 1.6 %shard_map.47 = (f32[4,16,512]{2,1,0:T(8,128)S(1)}, f32[2,24,512]{2,1,0:T(8,128)S(1)}, f32[2,9,512]{2,1,0:T(8,128)S(1)}, f32[4,6,16,512]{3,2,1,0:T(8,128)S(1)}, ...) custom-call(f32[2,3,4,16,512]{4,3,2,1,0:T(8,128)S(1)} %copy-done, s32[4,16,512]{2,1,0:T(8,128)S(1)} %copy-done.1, ...), custom_call_target="tpu_custom_call" | custom-call | tf_op jit(solution)/shard_map/pallas_call | solution.py:522
  7.7 0.0 collective-permute-done.1.refs_1_.refs_2_
  7.7 0.5 %collective-permute-done.refs_0_ = f32[7,16,512]{2,1,0:T(8,128)S(1)} collective-permute-done((f32[7,16,512]{2,1,0:T(8,128)S(1)}, f32[7,16,512]{2,1,0:T(8,128)S(1)}, u32[]{:S(2)}, u32[]{:S(2)}) %collective-permute-start) | collective-permute-done | bytes 229408 | tf_op jit(solution)/shard_map/ppermute | solution.py:556
  8.2 0.6 %shard_map.48 = (f32[88,512]{1,0:T(8,128)S(1)}, f32[4,8,512]{2,1,0:T(8,128)S(1)}) custom-call(f32[7,16,512]{2,1,0:T(8,128)S(1)} %collective-permute-done.refs_0_, f32[24,512]{1,0:T(8,128)S(1)} %collective-permute-done.1.refs_1_.refs_2_, f32[4,16,512]{2,1,0:T(8,128)S(1)} %get-tuple-element.23.refs_2_, f32[2,24,512]{2,1,0:T(8,128)S(1)} %get-tuple-element.24.refs_3_, ...), custom_call_target="tpu_custom_call" | custom-call | tf_op jit(solution)/shard_map/pallas_call | solution.py:522
  8.8 0.9 %collective-permute-done.2.refs_3_ = f32[8,512]{1,0:T(8,128)S(1)} collective-permute-done((f32[8,512]{1,0:T(8,128)S(1)}, f32[8,512]{1,0:T(8,128)S(1)}, u32[]{:S(2)}, u32[]{:S(2)}) %collective-permute-start.2) | collective-permute-done | bytes 16416 | tf_op jit(solution)/shard_map/ppermute | solution.py:556
  9.8 0.3 %shard_map.49.refs_0_ = f32[88,512]{1,0:T(8,128)S(1)} custom-call(f32[88,512]{1,0:T(8,128)S(1)} %get-tuple-element.29.refs_0_, f32[4,8,512]{2,1,0:T(8,128)S(1)} %get-tuple-element.30.refs_1_, f32[24,512]{1,0:T(8,128)S(1)} %collective-permute-done.1.refs_1_.refs_2_, f32[8,512]{1,0:T(8,128)S(1)} %collective-permute-done.2.refs_3_), custom_call_target="tpu_custom_call" | custom-call | tf_op jit(solution)/shard_map/pallas_call | solution.py:522
  10.0 0.1 collective-permute-start.3
  10.1 1.4 %collective-permute-done.3.refs_1_ = f32[88,512]{1,0:T(8,128)S(1)} collective-permute-done((f32[88,512]{1,0:T(8,128)S(1)}, f32[88,512]{1,0:T(8,128)S(1)}, u32[]{:S(2)}, u32[]{:S(2)}) %collective-permute-start.3) | collective-permute-done | bytes 180256 | tf_op jit(solution)/shard_map/ppermute | solution.py:539
  11.5 0.1 shard_map.50
  11.6 0.2 collective-permute-start.7
  11.7 1.7 %collective-permute-start.4 = (f32[16,512]{1,0:T(8,128)S(1)}, f32[16,512]{1,0:T(8,128)S(1)}, u32[]{:S(2)}, u32[]{:S(2)}) collective-permute-start(f32[16,512]{1,0:T(8,128)S(1)} %get-tuple-element.33), channel_id=1, source_target_pairs={{0,16},{1,17},{2,18},{3,19},{4,20},{5,8},{6,9},{7,10},{8,24},{9,4}... | collective-permute-start | bytes 98312 | tf_op jit(solution)/shard_map/ppermute | solution.py:556
  13.4 0.0 collective-permute-start.5
  13.4 3.3 %collective-permute-start.6 = (f32[16,512]{1,0:T(8,128)S(1)}, f32[16,512]{1,0:T(8,128)S(1)}, u32[]{:S(2)}, u32[]{:S(2)}) collective-permute-start(f32[16,512]{1,0:T(8,128)S(1)} %get-tuple-element.35), channel_id=1, source_target_pairs={{0,4},{1,5},{2,6},{3,7},{4,0},{5,1},{6,2},{7,3},{8,12},{9,13},{10,... | collective-permute-start | bytes 98312 | tf_op jit(solution)/shard_map/ppermute | solution.py:568
  16.7 0.0 collective-permute-done.4.d_in
  16.7 1.5 %collective-permute-done.5.e_in = f32[16,512]{1,0:T(8,128)S(1)} collective-permute-done((f32[16,512]{1,0:T(8,128)S(1)}, f32[16,512]{1,0:T(8,128)S(1)}, u32[]{:S(2)}, u32[]{:S(2)}) %collective-permute-start.5) | collective-permute-done | bytes 32800 | tf_op jit(solution)/shard_map/ppermute | solution.py:556
  18.2 0.4 %collective-permute-done.6.y_in = f32[16,512]{1,0:T(8,128)S(1)} collective-permute-done((f32[16,512]{1,0:T(8,128)S(1)}, f32[16,512]{1,0:T(8,128)S(1)}, u32[]{:S(2)}, u32[]{:S(2)}) %collective-permute-start.6) | collective-permute-done | bytes 32800 | tf_op jit(solution)/shard_map/ppermute | solution.py:568
  18.6 0.0 collective-permute-done.7.z_in
  18.6 0.1 shard_map.51.part
  18.7 0.4 %collective-permute-start.8 = (f32[4,16,512]{2,1,0:T(8,128)S(1)}, f32[4,16,512]{2,1,0:T(8,128)S(1)}, u32[]{:S(2)}, u32[]{:S(2)}) collective-permute-start(f32[4,16,512]{2,1,0:T(8,128)S(1)} %shard_map.51.part), channel_id=1, source_target_pairs={{0,16},{16,0},{1,17},{17,1},{2,18},{18,2},{3,19},{19,3},{4,20},{20... | collective-permute-start | bytes 393224 | tf_op jit(solution)/shard_map/ppermute | solution.py:539
  19.2 1.0 %collective-permute-done.8.other = f32[4,16,512]{2,1,0:T(8,128)S(1)} collective-permute-done((f32[4,16,512]{2,1,0:T(8,128)S(1)}, f32[4,16,512]{2,1,0:T(8,128)S(1)}, u32[]{:S(2)}, u32[]{:S(2)}) %collective-permute-start.8) | collective-permute-done | bytes 131104 | tf_op jit(solution)/shard_map/ppermute | solution.py:539
  20.2 0.7 %shard_map.52 = f32[4,16,512]{2,1,0:T(8,128)} custom-call(f32[4,16,512]{2,1,0:T(8,128)S(1)} %shard_map.51.part, f32[4,16,512]{2,1,0:T(8,128)S(1)} %collective-permute-done.8.other), custom_call_target="tpu_custom_call" | custom-call | tf_op jit(solution)/shard_map/pallas_call | solution.py:522
  (1 shorter events, 0.0 us)
Async XLA Ops:
  0.0 6.1 %copy-start.1 = (s32[4,16,512]{2,1,0:T(8,128)S(1)}, s32[4,16,512]{2,1,0:T(8,128)}, u32[]{:S(2)}) copy-start(s32[4,16,512]{2,1,0:T(8,128)} %refs_1_.3) | copy-start | bytes 393220
  0.0 6.1 %copy-start.3 = (s32[4,16,512]{2,1,0:T(8,128)S(1)}, s32[4,16,512]{2,1,0:T(8,128)}, u32[]{:S(2)}) copy-start(s32[4,16,512]{2,1,0:T(8,128)} %refs_3_.3) | copy-start | bytes 393220
  0.0 6.1 %copy-start.2 = (f32[4,16,512]{2,1,0:T(8,128)S(1)}, f32[4,16,512]{2,1,0:T(8,128)}, u32[]{:S(2)}) copy-start(f32[4,16,512]{2,1,0:T(8,128)} %refs_2_.3) | copy-start | bytes 393220
  0.0 6.1 %copy-start = (f32[2,3,4,16,512]{4,3,2,1,0:T(8,128)S(1)}, f32[2,3,4,16,512]{4,3,2,1,0:T(8,128)}, u32[]{:S(2)}) copy-start(f32[2,3,4,16,512]{4,3,2,1,0:T(8,128)} %refs_0_.3) | copy-start | bytes 2359300
  1.1 7.1 %collective-permute-start = (f32[7,16,512]{2,1,0:T(8,128)S(1)}, f32[7,16,512]{2,1,0:T(8,128)S(1)}, u32[]{:S(2)}, u32[]{:S(2)}) collective-permute-start(f32[7,16,512]{2,1,0:T(8,128)S(1)} %get-tuple-element.21), channel_id=1, source_target_pairs={{0,16},{1,0},{2,1},{3,2},{4,20},{5,4},{6,5},{7,6},{8,24},{9,8},{10... | collective-permute-start | bytes 688136 | tf_op jit(solution)/shard_map/ppermute | solution.py:556
  1.6 6.0 %collective-permute-start.1 = (f32[24,512]{1,0:T(8,128)S(1)}, f32[24,512]{1,0:T(8,128)S(1)}, u32[]{:S(2)}, u32[]{:S(2)}) collective-permute-start(f32[24,512]{1,0:T(8,128)S(1)} %get-tuple-element.22), channel_id=1, source_target_pairs={{4,0},{8,4},{12,8},{0,12},{5,1},{9,5},{13,9},{1,13},{6,2},{10,6},{... | collective-permute-start | bytes 147464 | tf_op jit(solution)/shard_map/ppermute | solution.py:534
  5.1 4.6 %collective-permute-start.2 = (f32[8,512]{1,0:T(8,128)S(1)}, f32[8,512]{1,0:T(8,128)S(1)}, u32[]{:S(2)}, u32[]{:S(2)}) collective-permute-start(f32[8,512]{1,0:T(8,128)S(1)} %get-tuple-element.31), channel_id=1, source_target_pairs={{0,28},{1,12},{2,13},{3,14},{4,16},{5,0},{6,1},{7,2},{8,20},{9,4},... | collective-permute-start | bytes 49160 | tf_op jit(solution)/shard_map/ppermute | solution.py:556
  10.0 1.5 %collective-permute-start.3 = (f32[88,512]{1,0:T(8,128)S(1)}, f32[88,512]{1,0:T(8,128)S(1)}, u32[]{:S(2)}, u32[]{:S(2)}) collective-permute-start(f32[88,512]{1,0:T(8,128)S(1)} %shard_map.49.refs_0_), channel_id=1, source_target_pairs={{0,16},{16,0},{1,17},{17,1},{2,18},{18,2},{3,19},{19,3},{4,20},{20... | collective-permute-start | bytes 540680 | tf_op jit(solution)/shard_map/ppermute | solution.py:539
  11.6 7.0 %collective-permute-start.7 = (f32[4,16,512]{2,1,0:T(8,128)S(1)}, f32[4,16,512]{2,1,0:T(8,128)S(1)}, u32[]{:S(2)}, u32[]{:S(2)}) collective-permute-start(f32[4,16,512]{2,1,0:T(8,128)S(1)} %get-tuple-element.36), channel_id=1, source_target_pairs={{0,16},{1,0},{2,1},{3,2},{4,20},{5,4},{6,5},{7,6},{8,24},{9,8},{10... | collective-permute-start | bytes 393224 | tf_op jit(solution)/shard_map/ppermute | solution.py:556
  11.7 5.0 %collective-permute-start.4 = (f32[16,512]{1,0:T(8,128)S(1)}, f32[16,512]{1,0:T(8,128)S(1)}, u32[]{:S(2)}, u32[]{:S(2)}) collective-permute-start(f32[16,512]{1,0:T(8,128)S(1)} %get-tuple-element.33), channel_id=1, source_target_pairs={{0,16},{1,17},{2,18},{3,19},{4,20},{5,8},{6,9},{7,10},{8,24},{9,4}... | collective-permute-start | bytes 98312 | tf_op jit(solution)/shard_map/ppermute | solution.py:556
  13.4 4.8 %collective-permute-start.5 = (f32[16,512]{1,0:T(8,128)S(1)}, f32[16,512]{1,0:T(8,128)S(1)}, u32[]{:S(2)}, u32[]{:S(2)}) collective-permute-start(f32[16,512]{1,0:T(8,128)S(1)} %get-tuple-element.34), channel_id=1, source_target_pairs={{0,16},{1,4},{2,5},{3,6},{4,20},{5,0},{6,1},{7,2},{8,24},{9,12},{1... | collective-permute-start | bytes 98312 | tf_op jit(solution)/shard_map/ppermute | solution.py:556
  13.4 5.2 %collective-permute-start.6 = (f32[16,512]{1,0:T(8,128)S(1)}, f32[16,512]{1,0:T(8,128)S(1)}, u32[]{:S(2)}, u32[]{:S(2)}) collective-permute-start(f32[16,512]{1,0:T(8,128)S(1)} %get-tuple-element.35), channel_id=1, source_target_pairs={{0,4},{1,5},{2,6},{3,7},{4,0},{5,1},{6,2},{7,3},{8,12},{9,13},{10,... | collective-permute-start | bytes 98312 | tf_op jit(solution)/shard_map/ppermute | solution.py:568
  18.7 1.4 %collective-permute-start.8 = (f32[4,16,512]{2,1,0:T(8,128)S(1)}, f32[4,16,512]{2,1,0:T(8,128)S(1)}, u32[]{:S(2)}, u32[]{:S(2)}) collective-permute-start(f32[4,16,512]{2,1,0:T(8,128)S(1)} %shard_map.51.part), channel_id=1, source_target_pairs={{0,16},{16,0},{1,17},{17,1},{2,18},{18,2},{3,19},{19,3},{4,20},{20... | collective-permute-start | bytes 393224 | tf_op jit(solution)/shard_map/ppermute | solution.py:539

commit v35 on v34

--- a/solution.py
+++ b/solution.py
@@ -210,7 +210,7 @@
             )
         )
     ]
-    for copy in copies[3:4] + copies[:3] + copies[4:]:
+    for copy in copies[3:4] + copies[5:] + copies[:3] + copies[4:5]:
         copy.start()
     for copy in copies[:2]:
         copy.wait()

time: 21 us -> 21 us (level)
  no operation moved by 1% of the time
where the time goes in v35:
time: 21 us; the launch traced here: 20.9 us
  starting transfers between devices  10.6 us (50%)
  waiting for transfers between devices  5.73 us (27%)
  Pallas kernels  4.47 us (21%)
    pallas_call x7, Pallas kernels, call(): pl.pallas_call(kernel, out_shape=shapes, in_specs=[pl.BlockSpec(memory_sp...  4.47 us
    ppermute x1, starting transfers between devices, ring_moved(): return lax.ppermute(value, axis, [((k + 1) % size, k) for k in range(size)])  3.51 us
    ppermute x1, starting transfers between devices, beside(): return lax.ppermute(value, ('load', 'sy', 'sz'), pairs)  3.3 us
    ppermute x5, starting transfers between devices, opposed(): return lax.ppermute(value, ('load', 'sy', 'sz'), pairs)  3.25 us
    ppermute x5, waiting for transfers between devices, opposed(): return lax.ppermute(value, ('load', 'sy', 'sz'), pairs)  2.96 us
    ppermute x2, waiting for transfers between devices, chip_swapped(): lax.ppermute(value, 'load', [(core, cores - 1 - core) for core in range(c...  2.39 us
    ppermute x2, starting transfers between devices, chip_swapped(): lax.ppermute(value, 'load', [(core, cores - 1 - core) for core in range(c...  0.51 us
  transfers between devices with their start and end apart: 9, of which 6 were waited for; matrix products, arithmetic and copies ran while one was open for 0% of the time, Pallas kernels for 11%

profile of v35, /device:TPU:0, one launch (start us, length us, event | category | flops | bytes accessed | tf_op | source)
XLA Modules:
  0.0 20.9 jit_solution(7985855623950336891)
XLA Ops:
  0.0 0.0 copy-start.1
  0.0 0.0 copy-start.3
  0.0 0.0 copy-start.2
  0.0 1.1 %shard_map.46 = (f32[8,512]{1,0:T(8,128)S(1)}, f32[7,16,512]{2,1,0:T(8,128)S(1)}, f32[24,512]{1,0:T(8,128)S(1)}) custom-call(f32[2,3,4,16,512]{4,3,2,1,0:T(8,128)} %refs_0_.3, s32[4,16,512]{2,1,0:T(8,128)} %refs_1_.3, f32[4,16,512]{2,1,0:T(8,128)} %refs_2_.3, s32[4,16,512]{2,1,0:T(8,128)} %refs_3_.3), custom_call_target="tpu_custom_call" | custom-call | tf_op jit(solution)/shard_map/pallas_call | solution.py:522
  1.2 0.5 %collective-permute-start = (f32[7,16,512]{2,1,0:T(8,128)S(1)}, f32[7,16,512]{2,1,0:T(8,128)S(1)}, u32[]{:S(2)}, u32[]{:S(2)}) collective-permute-start(f32[7,16,512]{2,1,0:T(8,128)S(1)} %get-tuple-element.21), channel_id=1, source_target_pairs={{0,16},{1,0},{2,1},{3,2},{4,20},{5,4},{6,5},{7,6},{8,24},{9,8},{10... | collective-permute-start | bytes 688136 | tf_op jit(solution)/shard_map/ppermute | solution.py:556
  1.6 3.5 %collective-permute-start.1 = (f32[24,512]{1,0:T(8,128)S(1)}, f32[24,512]{1,0:T(8,128)S(1)}, u32[]{:S(2)}, u32[]{:S(2)}) collective-permute-start(f32[24,512]{1,0:T(8,128)S(1)} %get-tuple-element.22), channel_id=1, source_target_pairs={{4,0},{8,4},{12,8},{0,12},{5,1},{9,5},{13,9},{1,13},{6,2},{10,6},{... | collective-permute-start | bytes 147464 | tf_op jit(solution)/shard_map/ppermute | solution.py:534
  5.1 0.9 %collective-permute-start.2 = (f32[8,512]{1,0:T(8,128)S(1)}, f32[8,512]{1,0:T(8,128)S(1)}, u32[]{:S(2)}, u32[]{:S(2)}) collective-permute-start(f32[8,512]{1,0:T(8,128)S(1)} %get-tuple-element.31), channel_id=1, source_target_pairs={{0,28},{1,12},{2,13},{3,14},{4,16},{5,0},{6,1},{7,2},{8,20},{9,4},... | collective-permute-start | bytes 49160 | tf_op jit(solution)/shard_map/ppermute | solution.py:556
  6.1 0.0 copy-done.1
  6.1 0.0 copy-done.3
  6.1 0.0 copy-done.2
  6.1 0.0 copy-done
  6.1 1.6 %shard_map.47 = (f32[4,16,512]{2,1,0:T(8,128)S(1)}, f32[2,24,512]{2,1,0:T(8,128)S(1)}, f32[2,9,512]{2,1,0:T(8,128)S(1)}, f32[4,6,16,512]{3,2,1,0:T(8,128)S(1)}, ...) custom-call(f32[2,3,4,16,512]{4,3,2,1,0:T(8,128)S(1)} %copy-done, s32[4,16,512]{2,1,0:T(8,128)S(1)} %copy-done.1, ...), custom_call_target="tpu_custom_call" | custom-call | tf_op jit(solution)/shard_map/pallas_call | solution.py:522
  7.7 0.0 collective-permute-done.1.refs_1_.refs_2_
  7.7 0.5 %collective-permute-done.refs_0_ = f32[7,16,512]{2,1,0:T(8,128)S(1)} collective-permute-done((f32[7,16,512]{2,1,0:T(8,128)S(1)}, f32[7,16,512]{2,1,0:T(8,128)S(1)}, u32[]{:S(2)}, u32[]{:S(2)}) %collective-permute-start) | collective-permute-done | bytes 229408 | tf_op jit(solution)/shard_map/ppermute | solution.py:556
  8.2 0.6 %shard_map.48 = (f32[88,512]{1,0:T(8,128)S(1)}, f32[4,8,512]{2,1,0:T(8,128)S(1)}) custom-call(f32[7,16,512]{2,1,0:T(8,128)S(1)} %collective-permute-done.refs_0_, f32[24,512]{1,0:T(8,128)S(1)} %collective-permute-done.1.refs_1_.refs_2_, f32[4,16,512]{2,1,0:T(8,128)S(1)} %get-tuple-element.23.refs_2_, f32[2,24,512]{2,1,0:T(8,128)S(1)} %get-tuple-element.24.refs_3_, ...), custom_call_target="tpu_custom_call" | custom-call | tf_op jit(solution)/shard_map/pallas_call | solution.py:522
  8.9 0.9 %collective-permute-done.2.refs_3_ = f32[8,512]{1,0:T(8,128)S(1)} collective-permute-done((f32[8,512]{1,0:T(8,128)S(1)}, f32[8,512]{1,0:T(8,128)S(1)}, u32[]{:S(2)}, u32[]{:S(2)}) %collective-permute-start.2) | collective-permute-done | bytes 16416 | tf_op jit(solution)/shard_map/ppermute | solution.py:556
  9.8 0.3 %shard_map.49.refs_0_ = f32[88,512]{1,0:T(8,128)S(1)} custom-call(f32[88,512]{1,0:T(8,128)S(1)} %get-tuple-element.29.refs_0_, f32[4,8,512]{2,1,0:T(8,128)S(1)} %get-tuple-element.30.refs_1_, f32[24,512]{1,0:T(8,128)S(1)} %collective-permute-done.1.refs_1_.refs_2_, f32[8,512]{1,0:T(8,128)S(1)} %collective-permute-done.2.refs_3_), custom_call_target="tpu_custom_call" | custom-call | tf_op jit(solution)/shard_map/pallas_call | solution.py:522
  10.0 0.1 collective-permute-start.3
  10.1 1.4 %collective-permute-done.3.refs_1_ = f32[88,512]{1,0:T(8,128)S(1)} collective-permute-done((f32[88,512]{1,0:T(8,128)S(1)}, f32[88,512]{1,0:T(8,128)S(1)}, u32[]{:S(2)}, u32[]{:S(2)}) %collective-permute-start.3) | collective-permute-done | bytes 180256 | tf_op jit(solution)/shard_map/ppermute | solution.py:539
  11.5 0.1 shard_map.50
  11.6 0.2 collective-permute-start.7
  11.7 1.7 %collective-permute-start.4 = (f32[16,512]{1,0:T(8,128)S(1)}, f32[16,512]{1,0:T(8,128)S(1)}, u32[]{:S(2)}, u32[]{:S(2)}) collective-permute-start(f32[16,512]{1,0:T(8,128)S(1)} %get-tuple-element.33), channel_id=1, source_target_pairs={{0,16},{1,17},{2,18},{3,19},{4,20},{5,8},{6,9},{7,10},{8,24},{9,4}... | collective-permute-start | bytes 98312 | tf_op jit(solution)/shard_map/ppermute | solution.py:556
  13.4 0.0 collective-permute-start.5
  13.4 3.3 %collective-permute-start.6 = (f32[16,512]{1,0:T(8,128)S(1)}, f32[16,512]{1,0:T(8,128)S(1)}, u32[]{:S(2)}, u32[]{:S(2)}) collective-permute-start(f32[16,512]{1,0:T(8,128)S(1)} %get-tuple-element.35), channel_id=1, source_target_pairs={{0,4},{1,5},{2,6},{3,7},{4,0},{5,1},{6,2},{7,3},{8,12},{9,13},{10,... | collective-permute-start | bytes 98312 | tf_op jit(solution)/shard_map/ppermute | solution.py:568
  16.7 0.0 collective-permute-done.4.d_in
  16.7 1.5 %collective-permute-done.5.e_in = f32[16,512]{1,0:T(8,128)S(1)} collective-permute-done((f32[16,512]{1,0:T(8,128)S(1)}, f32[16,512]{1,0:T(8,128)S(1)}, u32[]{:S(2)}, u32[]{:S(2)}) %collective-permute-start.5) | collective-permute-done | bytes 32800 | tf_op jit(solution)/shard_map/ppermute | solution.py:556
  18.2 0.4 %collective-permute-done.6.y_in = f32[16,512]{1,0:T(8,128)S(1)} collective-permute-done((f32[16,512]{1,0:T(8,128)S(1)}, f32[16,512]{1,0:T(8,128)S(1)}, u32[]{:S(2)}, u32[]{:S(2)}) %collective-permute-start.6) | collective-permute-done | bytes 32800 | tf_op jit(solution)/shard_map/ppermute | solution.py:568
  18.6 0.0 collective-permute-done.7.z_in
  18.6 0.1 shard_map.51.part
  18.8 0.4 %collective-permute-start.8 = (f32[4,16,512]{2,1,0:T(8,128)S(1)}, f32[4,16,512]{2,1,0:T(8,128)S(1)}, u32[]{:S(2)}, u32[]{:S(2)}) collective-permute-start(f32[4,16,512]{2,1,0:T(8,128)S(1)} %shard_map.51.part), channel_id=1, source_target_pairs={{0,16},{16,0},{1,17},{17,1},{2,18},{18,2},{3,19},{19,3},{4,20},{20... | collective-permute-start | bytes 393224 | tf_op jit(solution)/shard_map/ppermute | solution.py:539
  19.2 1.0 %collective-permute-done.8.other = f32[4,16,512]{2,1,0:T(8,128)S(1)} collective-permute-done((f32[4,16,512]{2,1,0:T(8,128)S(1)}, f32[4,16,512]{2,1,0:T(8,128)S(1)}, u32[]{:S(2)}, u32[]{:S(2)}) %collective-permute-start.8) | collective-permute-done | bytes 131104 | tf_op jit(solution)/shard_map/ppermute | solution.py:539
  20.2 0.7 %shard_map.52 = f32[4,16,512]{2,1,0:T(8,128)} custom-call(f32[4,16,512]{2,1,0:T(8,128)S(1)} %shard_map.51.part, f32[4,16,512]{2,1,0:T(8,128)S(1)} %collective-permute-done.8.other), custom_call_target="tpu_custom_call" | custom-call | tf_op jit(solution)/shard_map/pallas_call | solution.py:522
  (1 shorter events, 0.0 us)
Async XLA Ops:
  0.0 6.1 %copy-start.1 = (s32[4,16,512]{2,1,0:T(8,128)S(1)}, s32[4,16,512]{2,1,0:T(8,128)}, u32[]{:S(2)}) copy-start(s32[4,16,512]{2,1,0:T(8,128)} %refs_1_.3) | copy-start | bytes 393220
  0.0 6.1 %copy-start.3 = (s32[4,16,512]{2,1,0:T(8,128)S(1)}, s32[4,16,512]{2,1,0:T(8,128)}, u32[]{:S(2)}) copy-start(s32[4,16,512]{2,1,0:T(8,128)} %refs_3_.3) | copy-start | bytes 393220
  0.0 6.1 %copy-start.2 = (f32[4,16,512]{2,1,0:T(8,128)S(1)}, f32[4,16,512]{2,1,0:T(8,128)}, u32[]{:S(2)}) copy-start(f32[4,16,512]{2,1,0:T(8,128)} %refs_2_.3) | copy-start | bytes 393220
  0.0 6.1 %copy-start = (f32[2,3,4,16,512]{4,3,2,1,0:T(8,128)S(1)}, f32[2,3,4,16,512]{4,3,2,1,0:T(8,128)}, u32[]{:S(2)}) copy-start(f32[2,3,4,16,512]{4,3,2,1,0:T(8,128)} %refs_0_.3) | copy-start | bytes 2359300
  1.2 7.1 %collective-permute-start = (f32[7,16,512]{2,1,0:T(8,128)S(1)}, f32[7,16,512]{2,1,0:T(8,128)S(1)}, u32[]{:S(2)}, u32[]{:S(2)}) collective-permute-start(f32[7,16,512]{2,1,0:T(8,128)S(1)} %get-tuple-element.21), channel_id=1, source_target_pairs={{0,16},{1,0},{2,1},{3,2},{4,20},{5,4},{6,5},{7,6},{8,24},{9,8},{10... | collective-permute-start | bytes 688136 | tf_op jit(solution)/shard_map/ppermute | solution.py:556
  1.6 6.0 %collective-permute-start.1 = (f32[24,512]{1,0:T(8,128)S(1)}, f32[24,512]{1,0:T(8,128)S(1)}, u32[]{:S(2)}, u32[]{:S(2)}) collective-permute-start(f32[24,512]{1,0:T(8,128)S(1)} %get-tuple-element.22), channel_id=1, source_target_pairs={{4,0},{8,4},{12,8},{0,12},{5,1},{9,5},{13,9},{1,13},{6,2},{10,6},{... | collective-permute-start | bytes 147464 | tf_op jit(solution)/shard_map/ppermute | solution.py:534
  5.1 4.6 %collective-permute-start.2 = (f32[8,512]{1,0:T(8,128)S(1)}, f32[8,512]{1,0:T(8,128)S(1)}, u32[]{:S(2)}, u32[]{:S(2)}) collective-permute-start(f32[8,512]{1,0:T(8,128)S(1)} %get-tuple-element.31), channel_id=1, source_target_pairs={{0,28},{1,12},{2,13},{3,14},{4,16},{5,0},{6,1},{7,2},{8,20},{9,4},... | collective-permute-start | bytes 49160 | tf_op jit(solution)/shard_map/ppermute | solution.py:556
  10.0 1.5 %collective-permute-start.3 = (f32[88,512]{1,0:T(8,128)S(1)}, f32[88,512]{1,0:T(8,128)S(1)}, u32[]{:S(2)}, u32[]{:S(2)}) collective-permute-start(f32[88,512]{1,0:T(8,128)S(1)} %shard_map.49.refs_0_), channel_id=1, source_target_pairs={{0,16},{16,0},{1,17},{17,1},{2,18},{18,2},{3,19},{19,3},{4,20},{20... | collective-permute-start | bytes 540680 | tf_op jit(solution)/shard_map/ppermute | solution.py:539
  11.6 7.0 %collective-permute-start.7 = (f32[4,16,512]{2,1,0:T(8,128)S(1)}, f32[4,16,512]{2,1,0:T(8,128)S(1)}, u32[]{:S(2)}, u32[]{:S(2)}) collective-permute-start(f32[4,16,512]{2,1,0:T(8,128)S(1)} %get-tuple-element.36), channel_id=1, source_target_pairs={{0,16},{1,0},{2,1},{3,2},{4,20},{5,4},{6,5},{7,6},{8,24},{9,8},{10... | collective-permute-start | bytes 393224 | tf_op jit(solution)/shard_map/ppermute | solution.py:556
  11.7 5.0 %collective-permute-start.4 = (f32[16,512]{1,0:T(8,128)S(1)}, f32[16,512]{1,0:T(8,128)S(1)}, u32[]{:S(2)}, u32[]{:S(2)}) collective-permute-start(f32[16,512]{1,0:T(8,128)S(1)} %get-tuple-element.33), channel_id=1, source_target_pairs={{0,16},{1,17},{2,18},{3,19},{4,20},{5,8},{6,9},{7,10},{8,24},{9,4}... | collective-permute-start | bytes 98312 | tf_op jit(solution)/shard_map/ppermute | solution.py:556
  13.4 4.8 %collective-permute-start.5 = (f32[16,512]{1,0:T(8,128)S(1)}, f32[16,512]{1,0:T(8,128)S(1)}, u32[]{:S(2)}, u32[]{:S(2)}) collective-permute-start(f32[16,512]{1,0:T(8,128)S(1)} %get-tuple-element.34), channel_id=1, source_target_pairs={{0,16},{1,4},{2,5},{3,6},{4,20},{5,0},{6,1},{7,2},{8,24},{9,12},{1... | collective-permute-start | bytes 98312 | tf_op jit(solution)/shard_map/ppermute | solution.py:556
  13.4 5.2 %collective-permute-start.6 = (f32[16,512]{1,0:T(8,128)S(1)}, f32[16,512]{1,0:T(8,128)S(1)}, u32[]{:S(2)}, u32[]{:S(2)}) collective-permute-start(f32[16,512]{1,0:T(8,128)S(1)} %get-tuple-element.35), channel_id=1, source_target_pairs={{0,4},{1,5},{2,6},{3,7},{4,0},{5,1},{6,2},{7,3},{8,12},{9,13},{10,... | collective-permute-start | bytes 98312 | tf_op jit(solution)/shard_map/ppermute | solution.py:568
  18.8 1.4 %collective-permute-start.8 = (f32[4,16,512]{2,1,0:T(8,128)S(1)}, f32[4,16,512]{2,1,0:T(8,128)S(1)}, u32[]{:S(2)}, u32[]{:S(2)}) collective-permute-start(f32[4,16,512]{2,1,0:T(8,128)S(1)} %shard_map.51.part), channel_id=1, source_target_pairs={{0,16},{16,0},{1,17},{17,1},{2,18},{18,2},{3,19},{19,3},{4,20},{20... | collective-permute-start | bytes 393224 | tf_op jit(solution)/shard_map/ppermute | solution.py:539
